TPU v7x, 32 devices: a whole 2x2x4 slice. The times are simulated.
32 devices in a mesh: grp: 4 (over y, core), tok: 8 (over z, x).
Axes of the slice: x: 2, y: 2, z: 4, core: 2. Of those that a mesh axis runs over, the one named last changes fastest.
Arguments:
- probe_states: bfloat16 [256, 2048], P('tok'), may hold values from -40 to 40
- norm_gain: float32 [2048], replicated, may hold values from 0.1 to 1.9
- gate_weight: bfloat16 [6144, 2048], P(('grp', 'tok')), may hold values from -1 to 1
- up_weight: bfloat16 [6144, 2048], P(('grp', 'tok')), may hold values from -1 to 1
- down_weight: bfloat16 [6144, 2048], P(('grp', 'tok')), may hold values from -1 to 1
- route_weight: float32 [32, 64], P(('grp', 'tok')), may hold values from 0.02 to 1
Outputs:
- features: bfloat16 [2048, 2048], P(('grp', 'tok'))
- cka: float32 [8, 8], replicated
All inputs are finite; a program needn't handle non-finite values.
Results may differ from a plain program's by a relative error of at most 0.0015.
The roundings to bfloat16 on the way count: a program that leaves them out, or rounds other values in their place, can miss the bound.
Values may be sent and summed in bfloat16 or wider, within the bound.
No kernel may reach another device: no remote copies, remote signals or barrier semaphores. Data moves between devices by JAX's collectives and lax.ppermute only.
A program may use at most 64 MiB of HBM per device.

v0:
```python
import jax
import jax.numpy as jnp
from jax import lax
from jax.sharding import PartitionSpec as P


def swapped(array, axis, bit):
    return lax.ppermute(array, axis, [(i, i ^ 1 << bit) for i in range(lax.axis_size(axis))])


def shards(probe_states, norm_gain, gate_weight, up_weight, down_weight, route_weight):
    contract = (((1,), (1,)), ((), ()))
    states = probe_states.astype(jnp.float32)
    scaled = (
        states * lax.rsqrt(jnp.mean(states * states, axis=1, keepdims=True) + 1e-06) * norm_gain
    )
    normed = scaled.astype(jnp.bfloat16)
    position = lax.axis_index("tok")
    route_column = route_weight[0][:, None]
    piece = lax.all_gather(normed, "tok", axis=0, tiled=True)
    gate = lax.dot_general(piece, gate_weight, contract, preferred_element_type=jnp.float32)
    upward = lax.dot_general(piece, up_weight, contract, preferred_element_type=jnp.float32)
    gathered = (jax.nn.silu(gate) * upward).astype(jnp.bfloat16)
    hidden = gathered
    weights_now = down_weight
    for bit_number in (1, 0):
        bit_value = position >> bit_number & 1
        half_rows = hidden.shape[0] // 2
        kept_part = lax.dynamic_slice_in_dim(hidden, bit_value * half_rows, half_rows, 0)
        sent_part = lax.dynamic_slice_in_dim(hidden, (1 - bit_value) * half_rows, half_rows, 0)
        got_hidden, got_weights = swapped((sent_part, weights_now), "tok", bit_number)
        lower_first = bit_value == 0
        hidden = jnp.where(
            lower_first,
            jnp.concatenate([kept_part, got_hidden], 1),
            jnp.concatenate([got_hidden, kept_part], 1),
        )
        weights_now = jnp.where(
            lower_first,
            jnp.concatenate([weights_now, got_weights], 0),
            jnp.concatenate([got_weights, weights_now], 0),
        )
    output = jnp.dot(hidden, weights_now, preferred_element_type=jnp.float32)
    features = (output * route_column).astype(jnp.bfloat16)
    every_row = features
    for bit_number in (0, 1):
        bit_value = position >> bit_number & 1
        got_rows = swapped(every_row, "tok", bit_number)
        every_row = jnp.where(
            bit_value == 0,
            jnp.concatenate([every_row, got_rows], 0),
            jnp.concatenate([got_rows, every_row], 0),
        )
    token_count = every_row.shape[0]
    column_mean = jnp.sum(every_row, axis=0, dtype=jnp.float32) / token_count
    projection_all = jnp.sum(every_row.astype(jnp.float32) * column_mean, axis=1)
    projection_own = jnp.sum(features.astype(jnp.float32) * column_mean, axis=1)
    mean_square = jnp.sum(column_mean * column_mean)
    gram = lax.dot_general(features, every_row, contract, preferred_element_type=jnp.float32)
    centered = (gram - projection_own[:, None] - projection_all[None, :] + mean_square).astype(
        jnp.bfloat16
    )
    group_count = lax.axis_size("grp")
    token_devices = lax.axis_size("tok")
    blocks = centered.reshape(group_count, token_devices, -1)
    arrived = lax.all_to_all(
        lax.all_to_all(blocks, "grp", split_axis=0, concat_axis=0, tiled=True),
        "tok",
        split_axis=1,
        concat_axis=1,
        tiled=True,
    )
    flat = arrived.reshape(group_count * token_devices // 4, -1)
    partial_value = lax.dot_general(flat, flat, contract, preferred_element_type=jnp.float32)
    pair_totals = lax.psum(partial_value, ("grp", "tok"))
    diagonal = jnp.diagonal(pair_totals)
    cka = pair_totals / jnp.sqrt(diagonal[:, None] * diagonal[None, :])
    return (features, cka)


def solution(mesh):
    return jax.shard_map(
        shards,
        mesh=mesh,
        in_specs=(
            P("tok", None),
            P(),
            P(("grp", "tok"), None),
            P(("grp", "tok"), None),
            P(("grp", "tok"), None),
            P(("grp", "tok"), None),
        ),
        out_specs=(P(("grp", "tok"), None), P()),
        check_vma=False,
    )
```

profile of v0, /device:TPU:0, one launch (start us, length us, event | category | flops | bytes accessed | tf_op | source)
XLA Modules:
  0.0 169.9 jit_solution(17102717230161573206)
XLA Ops:
  7.2 0.0 copy-start
  7.2 0.0 all-gather.2.cloned.1.call-start
  7.2 1.1 fusion.14
  8.3 1.7 fusion.16
  10.0 0.0 all-gather.2.cloned.1.call-update
  10.0 3.1 %collective-permute-start.2 = (bf16[192,2048]{1,0:T(8,128)(2,1)}, bf16[192,2048]{1,0:T(8,128)(2,1)S(1)}, u32[]{:S(2)}, u32[]{:S(2)}) collective-permute-start(bf16[192,2048]{1,0:T(8,128)(2,1)} %param.10), channel_id=1, source_target_pairs={{0,2},{1,3},{2,0},{3,1},{4,6},{5,7},{6,4},{7,5},{8,10},{9,11},{10,... | collective-permute-start | bytes 2359304 | tf_op jit(solution)/shard_map/ppermute | solution.py:8
  13.1 22.0 %collective-permute-done.2 = bf16[192,2048]{1,0:T(8,128)(2,1)S(1)} collective-permute-done((bf16[192,2048]{1,0:T(8,128)(2,1)}, bf16[192,2048]{1,0:T(8,128)(2,1)S(1)}, u32[]{:S(2)}, u32[]{:S(2)}) %collective-permute-start.2) | collective-permute-done | bytes 786464 | tf_op jit(solution)/shard_map/ppermute | solution.py:8
  35.1 2.0 %maximum_select_fusion.6 = bf16[384,2048]{1,0:T(8,128)(2,1)S(1)} fusion(bf16[192,2048]{1,0:T(8,128)(2,1)S(1)} %collective-permute-done.2, bf16[192,2048]{1,0:T(8,128)(2,1)} %param.10, pred[]{:T(512)S(6)} %eq.9), kind=kLoop, calls=%fused_computation.14 | loop fusion | flops 7077888 | bytes 3145729 | tf_op jit(solution)/shard_map/jit(_where)/select_n | solution.py:38
  37.1 0.0 copy-start.3
  37.1 1.7 %collective-permute-start.3 = (bf16[384,2048]{1,0:T(8,128)(2,1)S(1)}, bf16[384,2048]{1,0:T(8,128)(2,1)}, u32[]{:S(2)}, u32[]{:S(2)}) collective-permute-start(bf16[384,2048]{1,0:T(8,128)(2,1)S(1)} %maximum_select_fusion.6), channel_id=1, source_target_pairs={{0,1},{1,0},{2,3},{3,2},{4,5},{5,4},{6,7},{7,6},{8,9},{9,8},{10,11... | collective-permute-start | bytes 4718600 | tf_op jit(solution)/shard_map/ppermute | solution.py:8
  38.8 20.9 %all-gather.2.cloned.1.call-done = bf16[256,2048]{1,0:T(8,128)(2,1)} async-done(((bf16[32,2048]{1,0:T(8,128)(2,1)}), bf16[256,2048]{1,0:T(8,128)(2,1)}) %all-gather.2.cloned.1.call-update) | async-done | bytes 1048592 | tf_op jit(solution)/shard_map/all_gather | solution.py:20
  59.8 0.0 copy-done
  59.8 0.0 copy-start.1
  59.8 1.8 %fusion.24 = f32[256,192]{0,1:T(8,128)S(1)} fusion(bf16[256,2048]{1,0:T(8,128)(2,1)} %all-gather.2.cloned.1.call-done, bf16[192,2048]{1,0:T(8,128)(2,1)S(1)} %copy-done), kind=kOutput, calls=%fused_computation.47 | convolution fusion | flops 201326592 | bytes 2031616 | tf_op jit(solution)/shard_map/dot_general | solution.py:21
  61.6 0.0 copy-done.3
  61.6 0.0 copy-done.1
  61.6 0.0 copy-start.4
  61.6 0.5 fusion.10
  62.2 1.9 %collective-permute-start = (bf16[128,192]{0,1:T(8,128)(2,1)S(1)}, bf16[128,192]{0,1:T(8,128)(2,1)S(1)}, u32[]{:S(2)}, u32[]{:S(2)}) collective-permute-start(bf16[128,192]{0,1:T(8,128)(2,1)S(1)} %get-tuple-element.5), channel_id=1, source_target_pairs={{0,2},{1,3},{2,0},{3,1},{4,6},{5,7},{6,4},{7,5},{8,10},{9,11},{10,... | collective-permute-start | bytes 147464 | tf_op jit(solution)/shard_map/ppermute | solution.py:8
  64.0 2.3 %collective-permute-done = bf16[128,192]{0,1:T(8,128)(2,1)S(1)} collective-permute-done((bf16[128,192]{0,1:T(8,128)(2,1)S(1)}, bf16[128,192]{0,1:T(8,128)(2,1)S(1)}, u32[]{:S(2)}, u32[]{:S(2)}) %collective-permute-start) | collective-permute-done | bytes 49184 | tf_op jit(solution)/shard_map/ppermute | solution.py:8
  66.3 0.1 constant_dynamic-slice_fusion.1
  66.5 0.5 collective-permute-start.1
  67.0 13.4 %collective-permute-done.1 = bf16[64,384]{0,1:T(8,128)(2,1)S(1)} collective-permute-done((bf16[64,384]{0,1:T(8,128)(2,1)S(1)}, bf16[64,384]{0,1:T(8,128)(2,1)S(1)}, u32[]{:S(2)}, u32[]{:S(2)}) %collective-permute-start.1) | collective-permute-done | bytes 49184 | tf_op jit(solution)/shard_map/ppermute | solution.py:8
  80.4 0.0 collective-permute-done.3
  80.4 0.0 copy-done.4
  80.4 3.0 %fusion.8 = bf16[64,2048]{1,0:T(8,128)(2,1)S(1)} fusion(bf16[384,2048]{1,0:T(8,128)(2,1)} %collective-permute-done.3, bf16[384,2048]{1,0:T(8,128)(2,1)S(1)} %maximum_select_fusion.6, pred[]{:T(512)S(6)} %eq.8, f32[64]{0:T(128)S(1)} %bitcast.10, bf16[64,384]{0,1:T(8,128)(2,1)S(1)} %collective-permute-done.1, bf16[64,384]{0,1:T(8,128)(2,1)S(1)} %get-tuple-element.2), kind=kOutput, calls=%fused_computation.12 | convolution fusion | flops 216186880 | bytes 3506433 | tf_op jit(solution)/shard_map/dot_general | solution.py:43
  83.4 0.0 copy-start.2
  83.4 1.6 collective-permute-start.4
  84.9 5.1 %collective-permute-done.4 = bf16[64,2048]{1,0:T(8,128)(2,1)S(1)} collective-permute-done((bf16[64,2048]{1,0:T(8,128)(2,1)S(1)}, bf16[64,2048]{1,0:T(8,128)(2,1)S(1)}, u32[]{:S(2)}, u32[]{:S(2)}) %collective-permute-start.4) | collective-permute-done | bytes 262176 | tf_op jit(solution)/shard_map/ppermute | solution.py:8
  90.0 0.1 maximum_select_fusion.8
  90.2 1.3 collective-permute-start.5
  91.4 10.1 %collective-permute-done.5 = bf16[128,2048]{1,0:T(8,128)(2,1)S(1)} collective-permute-done((bf16[128,2048]{1,0:T(8,128)(2,1)S(1)}, bf16[128,2048]{1,0:T(8,128)(2,1)S(1)}, u32[]{:S(2)}, u32[]{:S(2)}) %collective-permute-start.5) | collective-permute-done | bytes 524320 | tf_op jit(solution)/shard_map/ppermute | solution.py:8
  101.5 0.3 convert_reduce_fusion
  101.8 0.6 broadcast_multiply_fusion
  102.4 0.2 multiply_reduce_fusion
  102.6 0.4 fusion.9
  102.9 0.0 copy-done.2
  102.9 1.2 fusion.13
  104.2 6.3 %all_to_all.10 = bf16[4,8,512]{2,1,0:T(8,128)(2,1)S(1)} all-to-all(bf16[4,8,512]{2,1,0:T(8,128)(2,1)S(1)} %reshape.27), channel_id=1, replica_groups=mesh['grp'=4,'tok'=8] {'grp'}, dimensions={0} | all-to-all | bytes 65536 | tf_op jit(solution)/shard_map/all_to_all | solution.py:67
  110.5 0.6 copy.11
  111.1 5.7 %all-to-all-start.1 = ((bf16[4,8,512]{2,0,1:T(4,128)(2,1)}), bf16[4,8,512]{2,0,1:T(4,128)(2,1)S(1)}, u32[]{:S(2)}, u32[]{:S(2)}) async-start(bf16[4,8,512]{2,0,1:T(4,128)(2,1)} %copy.11), calls=%async_computation.1 | async-start | bytes 65536 | tf_op jit(solution)/shard_map/all_to_all | solution.py:66
  116.8 6.7 %all-to-all-done.1 = bf16[4,8,512]{2,0,1:T(4,128)(2,1)S(1)} async-done(((bf16[4,8,512]{2,0,1:T(4,128)(2,1)}), bf16[4,8,512]{2,0,1:T(4,128)(2,1)S(1)}, u32[]{:S(2)}, u32[]{:S(2)}) %all-to-all-start.1) | async-done | bytes 32800 | tf_op jit(solution)/shard_map/all_to_all | solution.py:66
  123.5 0.1 fusion.25
  123.7 38.1 %psum.7 = f32[8,8]{1,0:T(8,128)S(1)} all-reduce(f32[8,8]{1,0:T(8,128)S(1)} %fusion.25), channel_id=1, replica_groups=mesh['grp'=4,'tok'=8] {'grp','tok'}, use_global_device_ids=true, to_apply=%region_5.6 | all-reduce | flops 64 | bytes 512 | tf_op jit(solution)/shard_map/psum | solution.py:75
  161.8 0.6 gather_fusion
  162.4 0.7 rsqrt_multiply_fusion
  (7 shorter events, 0.1 us)
Async XLA Ops:
  7.2 52.6 %copy-start = (bf16[192,2048]{1,0:T(8,128)(2,1)S(1)}, bf16[192,2048]{1,0:T(8,128)(2,1)}, u32[]{:S(2)}) copy-start(bf16[192,2048]{1,0:T(8,128)(2,1)} %param.8) | copy-start | bytes 2359300
  7.2 52.6 %all-gather.2.cloned.1.call-start = ((), (), s32[]{:S(2)}) async-start(), calls=%async_computation.2 | async-start | bytes 1179648 | tf_op jit(solution)/shard_map/all_gather | solution.py:20
  10.0 25.1 %collective-permute-start.2 = (bf16[192,2048]{1,0:T(8,128)(2,1)}, bf16[192,2048]{1,0:T(8,128)(2,1)S(1)}, u32[]{:S(2)}, u32[]{:S(2)}) collective-permute-start(bf16[192,2048]{1,0:T(8,128)(2,1)} %param.10), channel_id=1, source_target_pairs={{0,2},{1,3},{2,0},{3,1},{4,6},{5,7},{6,4},{7,5},{8,10},{9,11},{10,... | collective-permute-start | bytes 2359304 | tf_op jit(solution)/shard_map/ppermute | solution.py:8
  37.1 24.5 %copy-start.3 = (bf16[192,2048]{1,0:T(8,128)(2,1)S(1)}, bf16[192,2048]{1,0:T(8,128)(2,1)}, u32[]{:S(2)}) copy-start(bf16[192,2048]{1,0:T(8,128)(2,1)} %param.9) | copy-start | bytes 2359300
  37.1 43.3 %collective-permute-start.3 = (bf16[384,2048]{1,0:T(8,128)(2,1)S(1)}, bf16[384,2048]{1,0:T(8,128)(2,1)}, u32[]{:S(2)}, u32[]{:S(2)}) collective-permute-start(bf16[384,2048]{1,0:T(8,128)(2,1)S(1)} %maximum_select_fusion.6), channel_id=1, source_target_pairs={{0,1},{1,0},{2,3},{3,2},{4,5},{5,4},{6,7},{7,6},{8,9},{9,8},{10,11... | collective-permute-start | bytes 4718600 | tf_op jit(solution)/shard_map/ppermute | solution.py:8
  59.8 1.8 %copy-start.1 = (bf16[256,2048]{1,0:T(8,128)(2,1)S(1)}, bf16[256,2048]{1,0:T(8,128)(2,1)}, u32[]{:S(2)}) copy-start(bf16[256,2048]{1,0:T(8,128)(2,1)} %all-gather.2.cloned.1.call-done) | copy-start | bytes 3145732
  61.6 18.8 %copy-start.4 = (f32[1,64]{1,0:T(1,128)S(1)}, f32[1,64]{1,0:T(1,128)}, u32[]{:S(2)}) copy-start(f32[1,64]{1,0:T(1,128)} %param.11) | copy-start | bytes 772
  62.2 4.2 %collective-permute-start = (bf16[128,192]{0,1:T(8,128)(2,1)S(1)}, bf16[128,192]{0,1:T(8,128)(2,1)S(1)}, u32[]{:S(2)}, u32[]{:S(2)}) collective-permute-start(bf16[128,192]{0,1:T(8,128)(2,1)S(1)} %get-tuple-element.5), channel_id=1, source_target_pairs={{0,2},{1,3},{2,0},{3,1},{4,6},{5,7},{6,4},{7,5},{8,10},{9,11},{10,... | collective-permute-start | bytes 147464 | tf_op jit(solution)/shard_map/ppermute | solution.py:8
  66.5 13.9 %collective-permute-start.1 = (bf16[64,384]{0,1:T(8,128)(2,1)S(1)}, bf16[64,384]{0,1:T(8,128)(2,1)S(1)}, u32[]{:S(2)}, u32[]{:S(2)}) collective-permute-start(bf16[64,384]{0,1:T(8,128)(2,1)S(1)} %get-tuple-element.3), channel_id=1, source_target_pairs={{0,1},{1,0},{2,3},{3,2},{4,5},{5,4},{6,7},{7,6},{8,9},{9,8},{10,11... | collective-permute-start | bytes 147464 | tf_op jit(solution)/shard_map/ppermute | solution.py:8
  83.4 19.6 %copy-start.2 = (bf16[64,2048]{1,0:T(8,128)(2,1)}, bf16[64,2048]{1,0:T(8,128)(2,1)S(1)}, u32[]{:S(2)}) copy-start(bf16[64,2048]{1,0:T(8,128)(2,1)S(1)} %fusion.8) | copy-start | bytes 786436
  83.4 6.7 %collective-permute-start.4 = (bf16[64,2048]{1,0:T(8,128)(2,1)S(1)}, bf16[64,2048]{1,0:T(8,128)(2,1)S(1)}, u32[]{:S(2)}, u32[]{:S(2)}) collective-permute-start(bf16[64,2048]{1,0:T(8,128)(2,1)S(1)} %fusion.8), channel_id=1, source_target_pairs={{0,1},{1,0},{2,3},{3,2},{4,5},{5,4},{6,7},{7,6},{8,9},{9,8},{10,11... | collective-permute-start | bytes 786440 | tf_op jit(solution)/shard_map/ppermute | solution.py:8
  90.2 11.4 %collective-permute-start.5 = (bf16[128,2048]{1,0:T(8,128)(2,1)S(1)}, bf16[128,2048]{1,0:T(8,128)(2,1)S(1)}, u32[]{:S(2)}, u32[]{:S(2)}) collective-permute-start(bf16[128,2048]{1,0:T(8,128)(2,1)S(1)} %maximum_select_fusion.8), channel_id=1, source_target_pairs={{0,2},{1,3},{2,0},{3,1},{4,6},{5,7},{6,4},{7,5},{8,10},{9,11},{10,... | collective-permute-start | bytes 1572872 | tf_op jit(solution)/shard_map/ppermute | solution.py:8
  111.1 12.4 %all-to-all-start.1 = ((bf16[4,8,512]{2,0,1:T(4,128)(2,1)}), bf16[4,8,512]{2,0,1:T(4,128)(2,1)S(1)}, u32[]{:S(2)}, u32[]{:S(2)}) async-start(bf16[4,8,512]{2,0,1:T(4,128)(2,1)} %copy.11), calls=%async_computation.1 | async-start | bytes 65536 | tf_op jit(solution)/shard_map/all_to_all | solution.py:66
Sparse Core Ops, SparseCore 0:
  10.7 48.9 all-gather.1
where the time goes:
time: 170 us
  waiting for transfers between devices  80.4 us (47%)
  blocking collectives  44.4 us (26%)
  starting transfers between devices  15.8 us (9%)
  between operations  14.2 us (8%)
  other arithmetic  7 us (4%)
  matrix products  6.59 us (4%)
    ppermute x6, waiting for transfers between devices, swapped(): lax.ppermute(array, axis, [(i, i ^ 1 << bit) for i in range(lax.axis_size...  52.8 us
    psum x1, blocking collectives, shards(): pair_totals = lax.psum(partial_value, ('grp', 'tok'))  38.1 us
    all_gather x1, waiting for transfers between devices, shards(): piece = lax.all_gather(normed, 'tok', axis=0, tiled=True)  20.9 us
    ppermute x6, starting transfers between devices, swapped(): lax.ppermute(array, axis, [(i, i ^ 1 << bit) for i in range(lax.axis_size...  10.1 us
    all_to_all x1, waiting for transfers between devices, shards(): lax.all_to_all(lax.all_to_all(blocks, 'grp', split_axis=0, concat_axis=0,...  6.68 us
    all_to_all x1, blocking collectives, shards(): lax.all_to_all(blocks, 'grp', split_axis=0, concat_axis=0, tiled=True)  6.3 us
    all_to_all x1, starting transfers between devices, shards(): lax.all_to_all(lax.all_to_all(blocks, 'grp', split_axis=0, concat_axis=0,...  5.74 us
  transfers between devices with their start and end apart: 8, of which 7 were waited for; matrix products, arithmetic and copies ran while one was open for 3% of the time, Pallas kernels for 0%

commit v1 on v0

v1 whole, which is shorter than its diff:
```python
import functools

import jax
import jax.numpy as jnp
from jax import lax
from jax.experimental import pallas as pl
from jax.experimental.pallas import tpu as pltpu
from jax.sharding import PartitionSpec as P

HOLDERS = 4
LANES = 128
TRANSPOSED = (((1,), (1,)), ((), ()))
VMEM = pl.BlockSpec(memory_space=pltpu.VMEM)
SMEM = pl.BlockSpec(memory_space=pltpu.SMEM)


def swapped(array, axis, mask):
    return lax.ppermute(array, axis, [(i, i ^ mask) for i in range(lax.axis_size(axis))])


def dot_f32(a, b, dims):
    return lax.dot_general(a, b, dims, preferred_element_type=jnp.float32)


def call(body, outs, vmem_bytes, *operands, scalars=0):
    return pl.pallas_call(
        body,
        out_shape=outs,
        in_specs=[SMEM] * scalars + [VMEM] * (len(operands) - scalars),
        out_specs=jax.tree.map(lambda _: VMEM, outs),
        compiler_params=pltpu.CompilerParams(vmem_limit_bytes=vmem_bytes),
    )(*operands)


def norm_kernel(states_ref, gain_ref, out_ref):
    states = states_ref[...].astype(jnp.float32)
    scale = lax.rsqrt(jnp.mean(states * states, axis=1, keepdims=True) + 1e-06)
    out_ref[...] = (states * scale * gain_ref[...]).astype(jnp.bfloat16)


def hidden_kernel(half_ref, mine_ref, other_ref, gate_ref, up_ref, out_ref):
    width = mine_ref.shape[1]
    own = pl.ds(pl.multiple_of(half_ref[0] * width, width), width)
    far = pl.ds(pl.multiple_of((1 - half_ref[0]) * width, width), width)
    mine, other = mine_ref[...], other_ref[...]
    gate = dot_f32(mine, gate_ref[:, own], TRANSPOSED) + dot_f32(other, gate_ref[:, far], TRANSPOSED)
    upward = dot_f32(mine, up_ref[:, own], TRANSPOSED) + dot_f32(other, up_ref[:, far], TRANSPOSED)
    out_ref[...] = (gate / (1.0 + jnp.exp(-gate)) * upward).astype(jnp.bfloat16)


def features_kernel(*refs):
    hidden_refs, down_refs = refs[:HOLDERS], refs[HOLDERS : 2 * HOLDERS]
    route_ref, features_ref, centered_ref = refs[2 * HOLDERS :]
    plain = (((1,), (0,)), ((), ()))
    output = dot_f32(hidden_refs[0][...], down_refs[0][...], plain)
    for h, w in zip(hidden_refs[1:], down_refs[1:]):
        output = output + dot_f32(h[...], w[...], plain)
    features = (output * route_ref[...]).astype(jnp.bfloat16)
    features_ref[...] = features
    tokens = features.shape[0]
    wide = features.astype(jnp.float32)
    mean = jnp.sum(wide, axis=0, keepdims=True) / tokens
    column = jnp.sum(wide * mean, axis=1, keepdims=True)
    row = jnp.transpose(jnp.broadcast_to(column, (tokens, LANES)))[:1]
    gram = dot_f32(features, features, TRANSPOSED)
    centered = (gram - column - row + jnp.sum(mean * mean)).astype(jnp.bfloat16)
    depth = 16
    at = 0
    for i in range(tokens // depth):
        for j in range(tokens // LANES):
            centered_ref[at * depth : (at + 1) * depth] = centered[
                i * depth : (i + 1) * depth, j * LANES : (j + 1) * LANES
            ]
            at += 1


def pair_kernel(parts_ref, out_ref):
    experts, holders, depth, lanes = parts_ref.shape
    flat = jnp.sum(parts_ref[...].astype(jnp.float32), axis=1).astype(jnp.bfloat16)
    flat = flat.reshape(experts, depth * lanes)
    out_ref[...] = dot_f32(flat, flat, TRANSPOSED)


def cka_of(totals):
    diagonal = jnp.diagonal(totals)
    return totals / jnp.sqrt(diagonal[:, None] * diagonal[None, :])


def shards(probe_states, norm_gain, gate_weight, up_weight, down_weight, route_weight):
    group, position = lax.axis_index("grp"), lax.axis_index("tok")
    groups, members = lax.axis_size("grp"), lax.axis_size("tok")
    devices = groups * members
    rows, model = probe_states.shape
    tokens = rows * members
    hidden_rows = gate_weight.shape[0]
    holder = position % HOLDERS
    big = 48 * 1024 * 1024

    normed = call(
        norm_kernel,
        jax.ShapeDtypeStruct((rows, model), jnp.bfloat16),
        big,
        probe_states,
        norm_gain[None, :],
    )
    half_width = model // 2
    half = group % 2
    own_half = lax.dynamic_slice_in_dim(normed, half * half_width, half_width, 1)
    spread = jnp.broadcast_to(own_half[None], (members, rows, half_width))
    mine = lax.all_to_all(spread, "tok", split_axis=0, concat_axis=0, tiled=True)
    mine = mine.reshape(tokens, half_width)
    down_weight, mine = lax.optimization_barrier((down_weight, mine))
    other = swapped(mine, "grp", 1)

    part = model // HOLDERS
    column = route_weight.reshape(-1, 1)
    downs, routes = [], []
    for mask in range(HOLDERS):
        block = lax.dynamic_slice_in_dim(down_weight, (holder ^ mask) * part, part, 1)
        downs.append(swapped(block, "tok", mask) if mask else block)
        routes.append(swapped(route_weight, "tok", mask) if mask else route_weight)
    every_route = jnp.stack(routes)[:, 0]
    every_route = jnp.stack([every_route[0], every_route[1], every_route[2], every_route[3]])
    swap_low = jnp.where(holder & 1, every_route[jnp.array([1, 0, 3, 2])], every_route)
    ordered = jnp.where(holder & 2, swap_low[jnp.array([2, 3, 0, 1])], swap_low)
    route_column = ordered.reshape(tokens, 1)

    hidden = call(
        hidden_kernel,
        jax.ShapeDtypeStruct((tokens, hidden_rows), jnp.bfloat16),
        big,
        half[None].astype(jnp.int32),
        mine,
        other,
        gate_weight,
        up_weight,
        scalars=1,
    )
    hiddens = [hidden] + [swapped(hidden, "tok", mask) for mask in range(1, HOLDERS)]
    depth = tokens * tokens // LANES // devices
    features_part, centered = call(
        features_kernel,
        (
            jax.ShapeDtypeStruct((tokens, part), jnp.bfloat16),
            jax.ShapeDtypeStruct((devices * depth, LANES), jnp.bfloat16),
        ),
        big,
        *hiddens,
        *downs,
        route_column,
    )
    arrived = lax.all_to_all(centered, ("grp", "tok"), split_axis=0, concat_axis=0, tiled=True)
    arrived = arrived.reshape(devices // HOLDERS, HOLDERS, depth, LANES)
    experts = devices // HOLDERS
    flat = jnp.sum(arrived.astype(jnp.float32), axis=1).astype(jnp.bfloat16).reshape(experts, -1)
    partial_value = dot_f32(flat, flat, TRANSPOSED)
    if devices * partial_value.size <= 1 << 16:
        copies = jnp.broadcast_to(partial_value[None], (devices, experts, experts))
        totals = jnp.sum(
            lax.all_to_all(copies, ("grp", "tok"), split_axis=0, concat_axis=0, tiled=True), axis=0
        )
    else:
        totals = lax.psum(partial_value, ("grp", "tok"))

    token_part = tokens // HOLDERS
    features = jnp.zeros((token_part, model), jnp.bfloat16)
    for mask in range(HOLDERS):
        block = lax.dynamic_slice_in_dim(features_part, (holder ^ mask) * token_part, token_part, 0)
        got = swapped(block, "tok", mask) if mask else block
        features = lax.dynamic_update_slice_in_dim(features, got, (holder ^ mask) * part, 1)
    return (features, cka_of(totals))


def solution(mesh):
    return jax.shard_map(
        shards,
        mesh=mesh,
        in_specs=(
            P("tok", None),
            P(),
            P(("grp", "tok"), None),
            P(("grp", "tok"), None),
            P(("grp", "tok"), None),
            P(("grp", "tok"), None),
        ),
        out_specs=(P(("grp", "tok"), None), P()),
        check_vma=False,
    )
```

time: 170 us -> 74.8 us (0.44)
  waiting for transfers between devices: 80.4 us -> 34.8 us
  blocking collectives: 44.4 us -> 0 us
  between operations: 14.2 us -> 0.95 us
  starting transfers between devices: 15.8 us -> 28.2 us
  matrix products: 6.59 us -> 0.13 us
  other arithmetic: 7 us -> 0.78 us
  local copies, waits for them, and re-layouts: 1.48 us -> 7.33 us
  Pallas kernels: 0 us -> 2.24 us
    psum x1 -> x0, blocking collectives: 38.1 us -> none  [shards(): pair_totals = lax.psum(partial_value, ('grp', 'tok'))]
    ppermute x6 -> x13, waiting for transfers between devices: 52.8 us -> 15.1 us  [swapped(): lax.ppermute(array, axis, [(i, i ^ mask) for i in range(lax.axis_size(axi...]
    all_gather x1 -> x0, waiting for transfers between devices: 20.9 us -> none  [shards(): piece = lax.all_gather(normed, 'tok', axis=0, tiled=True)]
    all_to_all x1 -> x3, waiting for transfers between devices: 6.68 us -> 19.7 us  [the longest x1 10.9 us: shards(): lax.all_to_all(spread, 'tok', split_axis=0, concat_axis=0, tiled=True)]
    all_to_all x1 -> x3, starting transfers between devices: 5.74 us -> 13.9 us  [the longest x1 7.38 us: shards(): lax.all_to_all(spread, 'tok', split_axis=0, concat_axis=0, tiled=True)]
    dot_general x5 -> x1, matrix products: 6.59 us -> 0.13 us  [dot_f32(): return lax.dot_general(a, b, dims, preferred_element_type=jnp.float32)]
    all_to_all x1 -> x0, blocking collectives: 6.3 us -> none  [shards(): lax.all_to_all(blocks, 'grp', split_axis=0, concat_axis=0, tiled=True)]
    ppermute x6 -> x13, starting transfers between devices: 10.1 us -> 14.3 us  [swapped(): lax.ppermute(array, axis, [(i, i ^ mask) for i in range(lax.axis_size(axi...]
  transfers between devices with their start and end apart: 8 -> 16, of which waited for: 7 -> 10; matrix products, arithmetic and copies ran while one was open for 3% -> 6% of each run, Pallas kernels for 0% -> 1%
where the time goes in v1:
time: 74.8 us; the launch traced here: 74.4 us
  waiting for transfers between devices  34.8 us (47%)
  starting transfers between devices  28.2 us (38%)
  local copies, waits for them, and re-layouts  7.33 us (10%)
  Pallas kernels  2.24 us (3%)
  between operations  0.95 us (1%)
  other arithmetic  0.78 us (1%)
    ppermute x13, waiting for transfers between devices, swapped(): lax.ppermute(array, axis, [(i, i ^ mask) for i in range(lax.axis_size(axi...  15.1 us
    ppermute x13, starting transfers between devices, swapped(): lax.ppermute(array, axis, [(i, i ^ mask) for i in range(lax.axis_size(axi...  14.3 us
    all_to_all x1, waiting for transfers between devices, shards(): lax.all_to_all(spread, 'tok', split_axis=0, concat_axis=0, tiled=True)  10.9 us
    all_to_all x1, waiting for transfers between devices, shards(): lax.all_to_all(copies, ('grp', 'tok'), split_axis=0, concat_axis=0, tiled...  7.7 us
    all_to_all x1, starting transfers between devices, shards(): lax.all_to_all(spread, 'tok', split_axis=0, concat_axis=0, tiled=True)  7.38 us
    all_to_all x1, starting transfers between devices, shards(): lax.all_to_all(copies, ('grp', 'tok'), split_axis=0, concat_axis=0, tiled...  3.76 us
    all_to_all x1, starting transfers between devices, shards(): lax.all_to_all(centered, ('grp', 'tok'), split_axis=0, concat_axis=0, til...  2.78 us
    pallas_call x3, Pallas kernels, call(): pl.pallas_call(body, out_shape=outs, in_specs=[SMEM] * scalars + [VMEM] *...  2.24 us
  transfers between devices with their start and end apart: 16, of which 10 were waited for; matrix products, arithmetic and copies ran while one was open for 6% of the time, Pallas kernels for 1%

profile of v1, /device:TPU:0, one launch (start us, length us, event | category | flops | bytes accessed | tf_op | source)
XLA Modules:
  0.0 74.4 jit_solution(8935185095236072956)
XLA Ops:
  0.6 0.0 copy-start.3
  0.7 0.7 copy-done.3
  1.3 0.9 %copy-done.2 = bf16[32,2048]{1,0:T(8,128)(2,1)S(1)} copy-done((bf16[32,2048]{1,0:T(8,128)(2,1)S(1)}, bf16[32,2048]{1,0:T(8,128)(2,1)}, u32[]{:S(2)}) %copy-start.2) | copy-done | bytes 131096
  2.2 0.1 shard_map.95
  2.4 0.9 %broadcast_in_dim.36 = bf16[8,32,1024]{2,1,0:T(8,128)(2,1)} broadcast(bf16[32,1024]{1,0:T(8,128)(2,1)S(1)} %constant_dynamic-slice_fusion.7), dimensions={1,2} | broadcast | bytes 589824 | tf_op jit(solution)/shard_map/broadcast_in_dim | solution.py:109
  3.3 7.4 %all-to-all-start = ((bf16[8,32,1024]{2,1,0:T(8,128)(2,1)}), bf16[8,32,1024]{2,1,0:T(8,128)(2,1)S(1)}, u32[]{:S(2)}, u32[]{:S(2)}) async-start(bf16[8,32,1024]{2,1,0:T(8,128)(2,1)} %broadcast_in_dim.36), calls=%async_computation | async-start | bytes 1048576 | tf_op jit(solution)/shard_map/all_to_all | solution.py:110
  10.7 0.0 copy-done.5
  10.7 2.9 %collective-permute-start.9 = (f32[1,64]{1,0:T(1,128)S(1)}, f32[1,64]{1,0:T(1,128)S(1)}, u32[]{:S(2)}, u32[]{:S(2)}) collective-permute-start(f32[1,64]{1,0:T(1,128)S(1)} %copy-done.5), channel_id=1, source_target_pairs={{0,3},{1,2},{2,1},{3,0},{4,7},{5,6},{6,5},{7,4},{8,11},{9,10},{10,... | collective-permute-start | bytes 776 | tf_op jit(solution)/shard_map/ppermute | solution.py:18
  13.6 0.6 collective-permute-start.8
  14.1 0.1 collective-permute-start.7
  14.2 0.0 copy-done.11
  14.2 0.0 copy-start.10
  14.2 10.9 %all-to-all-done = bf16[8,32,1024]{2,1,0:T(8,128)(2,1)S(1)} async-done(((bf16[8,32,1024]{2,1,0:T(8,128)(2,1)}), bf16[8,32,1024]{2,1,0:T(8,128)(2,1)S(1)}, u32[]{:S(2)}, u32[]{:S(2)}) %all-to-all-start) | async-done | bytes 524320 | tf_op jit(solution)/shard_map/all_to_all | solution.py:110
  25.1 0.0 collective-permute-start
  25.2 0.0 copy-done.10
  25.2 0.0 collective-permute-done.9
  25.2 0.0 collective-permute-done.8
  25.2 0.0 copy-start.6
  25.3 0.0 collective-permute-done.7
  25.3 0.0 copy-start.8
  25.3 0.6 gather_fusion
  25.9 0.0 copy-start
  25.9 0.0 copy-start.1
  25.9 2.2 %constant_dynamic-slice_fusion.3 = (bf16[192,512]{1,0:T(8,128)(2,1)}, bf16[192,512]{1,0:T(8,128)(2,1)}, bf16[192,512]{1,0:T(8,128)(2,1)}, bf16[192,512]{1,0:T(8,128)(2,1)S(1)}) fusion(bf16[192,2048]{1,0:T(8,128)(2,1)} %param.12, s32[]{:T(128)S(6)} %select_n.90, s32[]{:T(128)S(6)} %select_n.89, s32[]{:T(128)S(6)} %select_n.88, s32[]{:T(128)S(6)} %select_n.87), kind=kLoop, calls=%fused_computation.16 | loop fusion | bytes 1572880 | tf_op jit(solution)/shard_map/dynamic_slice | solution.py:119
  28.0 1.5 %collective-permute-start.4 = (bf16[192,512]{1,0:T(8,128)(2,1)}, bf16[192,512]{1,0:T(8,128)(2,1)S(1)}, u32[]{:S(2)}, u32[]{:S(2)}) collective-permute-start(bf16[192,512]{1,0:T(8,128)(2,1)} %get-tuple-element.12), channel_id=1, source_target_pairs={{0,1},{1,0},{2,3},{3,2},{4,5},{5,4},{6,7},{7,6},{8,9},{9,8},{10,11... | collective-permute-start | bytes 589832 | tf_op jit(solution)/shard_map/ppermute | solution.py:18
  29.5 0.0 copy-done.6
  29.5 0.0 copy-done.8
  29.5 0.6 gather_fusion.1
  30.1 0.1 collective-permute-start.5
  30.2 2.0 %collective-permute-start.6 = (bf16[192,512]{1,0:T(8,128)(2,1)}, bf16[192,512]{1,0:T(8,128)(2,1)S(1)}, u32[]{:S(2)}, u32[]{:S(2)}) collective-permute-start(bf16[192,512]{1,0:T(8,128)(2,1)} %get-tuple-element.10), channel_id=1, source_target_pairs={{0,3},{1,2},{2,1},{3,0},{4,7},{5,6},{6,5},{7,4},{8,11},{9,10},{10,... | collective-permute-start | bytes 589832 | tf_op jit(solution)/shard_map/ppermute | solution.py:18
  32.2 0.0 collective-permute-done.other_ref
  32.2 0.0 copy-done
  32.2 0.0 copy-done.1
  32.2 0.0 copy-start.7
  32.2 0.0 copy-start.9
  32.2 0.7 %shard_map.96.refs_0_ = bf16[256,192]{1,0:T(8,128)(2,1)S(1)} custom-call(s32[1]{0:T(128)} %bitcast.half_ref, bf16[256,1024]{1,0:T(8,128)(2,1)S(1)} %bitcast.11, bf16[256,1024]{1,0:T(8,128)(2,1)S(1)} %collective-permute-done.other_ref, bf16[192,2048]{1,0:T(8,128)(2,1)S(1)} %copy-done, bf16[192,2048]{1,0:T(8,128)(2,1)S(1)} %copy-done.1), custom_call_target="tpu_custom_call" | custom-call | tf_op jit(solution)/shard_map/pallas_call | solution.py:26
  33.0 1.5 %collective-permute-start.1 = (bf16[256,192]{1,0:T(8,128)(2,1)S(1)}, bf16[256,192]{1,0:T(8,128)(2,1)S(1)}, u32[]{:S(2)}, u32[]{:S(2)}) collective-permute-start(bf16[256,192]{1,0:T(8,128)(2,1)S(1)} %shard_map.96.refs_0_), channel_id=1, source_target_pairs={{0,1},{1,0},{2,3},{3,2},{4,5},{5,4},{6,7},{7,6},{8,9},{9,8},{10,11... | collective-permute-start | bytes 294920 | tf_op jit(solution)/shard_map/ppermute | solution.py:18
  34.5 0.1 collective-permute-start.2
  34.6 1.2 %collective-permute-done.4.refs_5_ = bf16[192,512]{1,0:T(8,128)(2,1)S(1)} collective-permute-done((bf16[192,512]{1,0:T(8,128)(2,1)}, bf16[192,512]{1,0:T(8,128)(2,1)S(1)}, u32[]{:S(2)}, u32[]{:S(2)}) %collective-permute-start.4) | collective-permute-done | bytes 196640 | tf_op jit(solution)/shard_map/ppermute | solution.py:18
  35.8 0.7 collective-permute-start.3
  36.5 0.0 copy-done.7
  36.5 0.0 copy-done.9
  36.5 0.1 select_n.102.refs_8_
  36.7 1.4 %collective-permute-done.5.refs_6_ = bf16[192,512]{1,0:T(8,128)(2,1)S(1)} collective-permute-done((bf16[192,512]{1,0:T(8,128)(2,1)}, bf16[192,512]{1,0:T(8,128)(2,1)S(1)}, u32[]{:S(2)}, u32[]{:S(2)}) %collective-permute-start.5) | collective-permute-done | bytes 196640 | tf_op jit(solution)/shard_map/ppermute | solution.py:18
  38.1 4.3 %collective-permute-done.6.refs_7_ = bf16[192,512]{1,0:T(8,128)(2,1)S(1)} collective-permute-done((bf16[192,512]{1,0:T(8,128)(2,1)}, bf16[192,512]{1,0:T(8,128)(2,1)S(1)}, u32[]{:S(2)}, u32[]{:S(2)}) %collective-permute-start.6) | collective-permute-done | bytes 196640 | tf_op jit(solution)/shard_map/ppermute | solution.py:18
  42.3 0.2 collective-permute-done.1.refs_1_
  42.6 2.6 %collective-permute-done.2.refs_2_ = bf16[256,192]{1,0:T(8,128)(2,1)S(1)} collective-permute-done((bf16[256,192]{1,0:T(8,128)(2,1)S(1)}, bf16[256,192]{1,0:T(8,128)(2,1)S(1)}, u32[]{:S(2)}, u32[]{:S(2)}) %collective-permute-start.2) | collective-permute-done | bytes 98336 | tf_op jit(solution)/shard_map/ppermute | solution.py:18
  45.2 2.1 %collective-permute-done.3.refs_3_ = bf16[256,192]{1,0:T(8,128)(2,1)S(1)} collective-permute-done((bf16[256,192]{1,0:T(8,128)(2,1)S(1)}, bf16[256,192]{1,0:T(8,128)(2,1)S(1)}, u32[]{:S(2)}, u32[]{:S(2)}) %collective-permute-start.3) | collective-permute-done | bytes 98336 | tf_op jit(solution)/shard_map/ppermute | solution.py:18
  47.3 1.4 %shard_map.97 = (bf16[256,512]{1,0:T(8,128)(2,1)S(1)}, bf16[512,128]{1,0:T(8,128)(2,1)}) custom-call(bf16[256,192]{1,0:T(8,128)(2,1)S(1)} %shard_map.96.refs_0_, bf16[256,192]{1,0:T(8,128)(2,1)S(1)} %collective-permute-done.1.refs_1_, bf16[256,192]{1,0:T(8,128)(2,1)S(1)} %collective-permute-done.2.refs_2_, ...), custom_call_target="tpu_custom_call" | custom-call | tf_op jit(solution)/shard_map/pallas_call | solution.py:26
  48.7 1.5 %collective-permute-start.10 = (bf16[64,512]{1,0:T(8,128)(2,1)S(1)}, bf16[64,512]{1,0:T(8,128)(2,1)S(1)}, u32[]{:S(2)}, u32[]{:S(2)}) collective-permute-start(bf16[64,512]{1,0:T(8,128)(2,1)S(1)} %get-tuple-element.16), channel_id=1, source_target_pairs={{0,1},{1,0},{2,3},{3,2},{4,5},{5,4},{6,7},{7,6},{8,9},{9,8},{10,11... | collective-permute-start | bytes 196616 | tf_op jit(solution)/shard_map/ppermute | solution.py:18
  50.2 2.8 %all-to-all-start.1 = ((bf16[32,16,128]{2,1,0:T(8,128)(2,1)}), bf16[32,16,128]{2,1,0:T(8,128)(2,1)S(1)}, u32[]{:S(2)}, u32[]{:S(2)}) async-start(bf16[32,16,128]{2,1,0:T(8,128)(2,1)} %bitcast.3), calls=%async_computation.1 | async-start | bytes 262144 | tf_op jit(solution)/shard_map/all_to_all | solution.py:152
  53.0 1.8 %collective-permute-start.11 = (bf16[64,512]{1,0:T(8,128)(2,1)S(1)}, bf16[64,512]{1,0:T(8,128)(2,1)S(1)}, u32[]{:S(2)}, u32[]{:S(2)}) collective-permute-start(bf16[64,512]{1,0:T(8,128)(2,1)S(1)} %get-tuple-element.15), channel_id=1, source_target_pairs={{0,2},{1,3},{2,0},{3,1},{4,6},{5,7},{6,4},{7,5},{8,10},{9,11},{10,... | collective-permute-start | bytes 196616 | tf_op jit(solution)/shard_map/ppermute | solution.py:18
  54.9 1.5 %collective-permute-start.12 = (bf16[64,512]{1,0:T(8,128)(2,1)S(1)}, bf16[64,512]{1,0:T(8,128)(2,1)S(1)}, u32[]{:S(2)}, u32[]{:S(2)}) collective-permute-start(bf16[64,512]{1,0:T(8,128)(2,1)S(1)} %get-tuple-element.14), channel_id=1, source_target_pairs={{0,3},{1,2},{2,1},{3,0},{4,7},{5,6},{6,5},{7,4},{8,11},{9,10},{10,... | collective-permute-start | bytes 196616 | tf_op jit(solution)/shard_map/ppermute | solution.py:18
  56.3 0.0 collective-permute-done.10
  56.3 3.3 %collective-permute-done.11 = bf16[64,512]{1,0:T(8,128)(2,1)S(1)} collective-permute-done((bf16[64,512]{1,0:T(8,128)(2,1)S(1)}, bf16[64,512]{1,0:T(8,128)(2,1)S(1)}, u32[]{:S(2)}, u32[]{:S(2)}) %collective-permute-start.11) | collective-permute-done | bytes 65568 | tf_op jit(solution)/shard_map/ppermute | solution.py:18
  59.6 1.1 %all-to-all-done.1 = bf16[32,16,128]{2,1,0:T(8,128)(2,1)S(1)} async-done(((bf16[32,16,128]{2,1,0:T(8,128)(2,1)}), bf16[32,16,128]{2,1,0:T(8,128)(2,1)S(1)}, u32[]{:S(2)}, u32[]{:S(2)}) %all-to-all-start.1) | async-done | bytes 131104 | tf_op jit(solution)/shard_map/all_to_all | solution.py:152
  60.8 0.1 convolution_bitcast_fusion
  60.9 0.7 broadcast_in_dim.39
  61.6 3.8 %all-to-all-start.2 = ((f32[32,8,8]{2,1,0:T(8,128)}), f32[32,8,8]{2,1,0:T(8,128)S(1)}, u32[]{:S(2)}, u32[]{:S(2)}) async-start(f32[32,8,8]{2,1,0:T(8,128)} %broadcast_in_dim.39), calls=%async_computation.2 | async-start | bytes 262144 | tf_op jit(solution)/shard_map/all_to_all | solution.py:160
  65.3 0.0 collective-permute-done.12
  65.4 0.0 copy-start.4
  65.4 7.7 %all-to-all-done.2 = f32[32,8,8]{2,1,0:T(8,128)S(1)} async-done(((f32[32,8,8]{2,1,0:T(8,128)}), f32[32,8,8]{2,1,0:T(8,128)S(1)}, u32[]{:S(2)}, u32[]{:S(2)}) %all-to-all-start.2) | async-done | bytes 8224 | tf_op jit(solution)/shard_map/all_to_all | solution.py:160
  73.1 0.6 gather_fusion.2
  73.8 0.7 rsqrt_multiply_fusion
  (18 shorter events, 0.2 us)
Async XLA Ops:
  0.6 0.7 copy-start.3
  1.3 0.9 %copy-start.2 = (bf16[32,2048]{1,0:T(8,128)(2,1)S(1)}, bf16[32,2048]{1,0:T(8,128)(2,1)}, u32[]{:S(2)}) copy-start(bf16[32,2048]{1,0:T(8,128)(2,1)} %states_ref.1) | copy-start | bytes 393220
  3.3 7.4 %copy-start.5 = (f32[1,64]{1,0:T(1,128)S(1)}, f32[1,64]{1,0:T(1,128)}, u32[]{:S(2)}) copy-start(f32[1,64]{1,0:T(1,128)} %param.13) | copy-start | bytes 772
  3.3 10.9 %copy-start.11 = (s32[4]{0:T(128)S(1)}, s32[4]{0:T(128)}, u32[]{:S(2)}) copy-start(s32[4]{0:T(128)} %constant.87) | copy-start | bytes 52
  3.3 21.9 %all-to-all-start = ((bf16[8,32,1024]{2,1,0:T(8,128)(2,1)}), bf16[8,32,1024]{2,1,0:T(8,128)(2,1)S(1)}, u32[]{:S(2)}, u32[]{:S(2)}) async-start(bf16[8,32,1024]{2,1,0:T(8,128)(2,1)} %broadcast_in_dim.36), calls=%async_computation | async-start | bytes 1048576 | tf_op jit(solution)/shard_map/all_to_all | solution.py:110
  10.7 14.6 %collective-permute-start.9 = (f32[1,64]{1,0:T(1,128)S(1)}, f32[1,64]{1,0:T(1,128)S(1)}, u32[]{:S(2)}, u32[]{:S(2)}) collective-permute-start(f32[1,64]{1,0:T(1,128)S(1)} %copy-done.5), channel_id=1, source_target_pairs={{0,3},{1,2},{2,1},{3,0},{4,7},{5,6},{6,5},{7,4},{8,11},{9,10},{10,... | collective-permute-start | bytes 776 | tf_op jit(solution)/shard_map/ppermute | solution.py:18
  13.6 11.7 %collective-permute-start.8 = (f32[1,64]{1,0:T(1,128)S(1)}, f32[1,64]{1,0:T(1,128)S(1)}, u32[]{:S(2)}, u32[]{:S(2)}) collective-permute-start(f32[1,64]{1,0:T(1,128)S(1)} %copy-done.5), channel_id=1, source_target_pairs={{0,2},{1,3},{2,0},{3,1},{4,6},{5,7},{6,4},{7,5},{8,10},{9,11},{10,... | collective-permute-start | bytes 776 | tf_op jit(solution)/shard_map/ppermute | solution.py:18
  14.1 11.1 %collective-permute-start.7 = (f32[1,64]{1,0:T(1,128)S(1)}, f32[1,64]{1,0:T(1,128)S(1)}, u32[]{:S(2)}, u32[]{:S(2)}) collective-permute-start(f32[1,64]{1,0:T(1,128)S(1)} %copy-done.5), channel_id=1, source_target_pairs={{0,1},{1,0},{2,3},{3,2},{4,5},{5,4},{6,7},{7,6},{8,9},{9,8},{10,11... | collective-permute-start | bytes 776 | tf_op jit(solution)/shard_map/ppermute | solution.py:18
  14.2 10.9 %copy-start.10 = (s32[4]{0:T(128)S(1)}, s32[4]{0:T(128)}, u32[]{:S(2)}) copy-start(s32[4]{0:T(128)} %constant.88) | copy-start | bytes 52
  25.1 7.0 %collective-permute-start = (bf16[256,1024]{1,0:T(8,128)(2,1)S(1)}, bf16[256,1024]{1,0:T(8,128)(2,1)S(1)}, u32[]{:S(2)}, u32[]{:S(2)}) collective-permute-start(bf16[256,1024]{1,0:T(8,128)(2,1)S(1)} %bitcast.10), channel_id=1, source_target_pairs={{0,8},{8,0},{16,24},{24,16},{1,9},{9,1},{17,25},{25,17},{2,10},{10... | collective-permute-start | bytes 1572872 | tf_op jit(solution)/shard_map/ppermute | solution.py:18
  25.2 4.3 %copy-start.6 = (f32[1,64]{1,0:T(1,128)}, f32[1,64]{1,0:T(1,128)S(1)}, u32[]{:S(2)}) copy-start(f32[1,64]{1,0:T(1,128)S(1)} %collective-permute-done.8) | copy-start | bytes 772
  25.3 4.2 %copy-start.8 = (f32[1,64]{1,0:T(1,128)}, f32[1,64]{1,0:T(1,128)S(1)}, u32[]{:S(2)}) copy-start(f32[1,64]{1,0:T(1,128)S(1)} %collective-permute-done.7) | copy-start | bytes 772
  25.9 6.3 %copy-start = (bf16[192,2048]{1,0:T(8,128)(2,1)S(1)}, bf16[192,2048]{1,0:T(8,128)(2,1)}, u32[]{:S(2)}) copy-start(bf16[192,2048]{1,0:T(8,128)(2,1)} %gate_ref.1) | copy-start | bytes 2359300
  25.9 6.3 %copy-start.1 = (bf16[192,2048]{1,0:T(8,128)(2,1)S(1)}, bf16[192,2048]{1,0:T(8,128)(2,1)}, u32[]{:S(2)}) copy-start(bf16[192,2048]{1,0:T(8,128)(2,1)} %up_ref.1) | copy-start | bytes 2359300
  28.0 7.7 %collective-permute-start.4 = (bf16[192,512]{1,0:T(8,128)(2,1)}, bf16[192,512]{1,0:T(8,128)(2,1)S(1)}, u32[]{:S(2)}, u32[]{:S(2)}) collective-permute-start(bf16[192,512]{1,0:T(8,128)(2,1)} %get-tuple-element.12), channel_id=1, source_target_pairs={{0,1},{1,0},{2,3},{3,2},{4,5},{5,4},{6,7},{7,6},{8,9},{9,8},{10,11... | collective-permute-start | bytes 589832 | tf_op jit(solution)/shard_map/ppermute | solution.py:18
  30.1 8.0 %collective-permute-start.5 = (bf16[192,512]{1,0:T(8,128)(2,1)}, bf16[192,512]{1,0:T(8,128)(2,1)S(1)}, u32[]{:S(2)}, u32[]{:S(2)}) collective-permute-start(bf16[192,512]{1,0:T(8,128)(2,1)} %get-tuple-element.11), channel_id=1, source_target_pairs={{0,2},{1,3},{2,0},{3,1},{4,6},{5,7},{6,4},{7,5},{8,10},{9,11},{10,... | collective-permute-start | bytes 589832 | tf_op jit(solution)/shard_map/ppermute | solution.py:18
  30.2 12.2 %collective-permute-start.6 = (bf16[192,512]{1,0:T(8,128)(2,1)}, bf16[192,512]{1,0:T(8,128)(2,1)S(1)}, u32[]{:S(2)}, u32[]{:S(2)}) collective-permute-start(bf16[192,512]{1,0:T(8,128)(2,1)} %get-tuple-element.10), channel_id=1, source_target_pairs={{0,3},{1,2},{2,1},{3,0},{4,7},{5,6},{6,5},{7,4},{8,11},{9,10},{10,... | collective-permute-start | bytes 589832 | tf_op jit(solution)/shard_map/ppermute | solution.py:18
  32.2 4.3 %copy-start.7 = (f32[1,64]{1,0:T(1,128)S(1)}, f32[1,64]{1,0:T(1,128)}, u32[]{:S(2)}) copy-start(f32[1,64]{1,0:T(1,128)} %copy-done.6) | copy-start | bytes 772
  32.2 4.3 %copy-start.9 = (f32[1,64]{1,0:T(1,128)S(1)}, f32[1,64]{1,0:T(1,128)}, u32[]{:S(2)}) copy-start(f32[1,64]{1,0:T(1,128)} %copy-done.8) | copy-start | bytes 772
  33.0 9.6 %collective-permute-start.1 = (bf16[256,192]{1,0:T(8,128)(2,1)S(1)}, bf16[256,192]{1,0:T(8,128)(2,1)S(1)}, u32[]{:S(2)}, u32[]{:S(2)}) collective-permute-start(bf16[256,192]{1,0:T(8,128)(2,1)S(1)} %shard_map.96.refs_0_), channel_id=1, source_target_pairs={{0,1},{1,0},{2,3},{3,2},{4,5},{5,4},{6,7},{7,6},{8,9},{9,8},{10,11... | collective-permute-start | bytes 294920 | tf_op jit(solution)/shard_map/ppermute | solution.py:18
  34.5 10.7 %collective-permute-start.2 = (bf16[256,192]{1,0:T(8,128)(2,1)S(1)}, bf16[256,192]{1,0:T(8,128)(2,1)S(1)}, u32[]{:S(2)}, u32[]{:S(2)}) collective-permute-start(bf16[256,192]{1,0:T(8,128)(2,1)S(1)} %shard_map.96.refs_0_), channel_id=1, source_target_pairs={{0,2},{1,3},{2,0},{3,1},{4,6},{5,7},{6,4},{7,5},{8,10},{9,11},{10,... | collective-permute-start | bytes 294920 | tf_op jit(solution)/shard_map/ppermute | solution.py:18
  35.8 11.5 %collective-permute-start.3 = (bf16[256,192]{1,0:T(8,128)(2,1)S(1)}, bf16[256,192]{1,0:T(8,128)(2,1)S(1)}, u32[]{:S(2)}, u32[]{:S(2)}) collective-permute-start(bf16[256,192]{1,0:T(8,128)(2,1)S(1)} %shard_map.96.refs_0_), channel_id=1, source_target_pairs={{0,3},{1,2},{2,1},{3,0},{4,7},{5,6},{6,5},{7,4},{8,11},{9,10},{10,... | collective-permute-start | bytes 294920 | tf_op jit(solution)/shard_map/ppermute | solution.py:18
  48.7 7.6 %collective-permute-start.10 = (bf16[64,512]{1,0:T(8,128)(2,1)S(1)}, bf16[64,512]{1,0:T(8,128)(2,1)S(1)}, u32[]{:S(2)}, u32[]{:S(2)}) collective-permute-start(bf16[64,512]{1,0:T(8,128)(2,1)S(1)} %get-tuple-element.16), channel_id=1, source_target_pairs={{0,1},{1,0},{2,3},{3,2},{4,5},{5,4},{6,7},{7,6},{8,9},{9,8},{10,11... | collective-permute-start | bytes 196616 | tf_op jit(solution)/shard_map/ppermute | solution.py:18
  50.2 10.5 %all-to-all-start.1 = ((bf16[32,16,128]{2,1,0:T(8,128)(2,1)}), bf16[32,16,128]{2,1,0:T(8,128)(2,1)S(1)}, u32[]{:S(2)}, u32[]{:S(2)}) async-start(bf16[32,16,128]{2,1,0:T(8,128)(2,1)} %bitcast.3), calls=%async_computation.1 | async-start | bytes 262144 | tf_op jit(solution)/shard_map/all_to_all | solution.py:152
  53.0 6.6 %collective-permute-start.11 = (bf16[64,512]{1,0:T(8,128)(2,1)S(1)}, bf16[64,512]{1,0:T(8,128)(2,1)S(1)}, u32[]{:S(2)}, u32[]{:S(2)}) collective-permute-start(bf16[64,512]{1,0:T(8,128)(2,1)S(1)} %get-tuple-element.15), channel_id=1, source_target_pairs={{0,2},{1,3},{2,0},{3,1},{4,6},{5,7},{6,4},{7,5},{8,10},{9,11},{10,... | collective-permute-start | bytes 196616 | tf_op jit(solution)/shard_map/ppermute | solution.py:18
  54.9 10.5 %collective-permute-start.12 = (bf16[64,512]{1,0:T(8,128)(2,1)S(1)}, bf16[64,512]{1,0:T(8,128)(2,1)S(1)}, u32[]{:S(2)}, u32[]{:S(2)}) collective-permute-start(bf16[64,512]{1,0:T(8,128)(2,1)S(1)} %get-tuple-element.14), channel_id=1, source_target_pairs={{0,3},{1,2},{2,1},{3,0},{4,7},{5,6},{6,5},{7,4},{8,11},{9,10},{10,... | collective-permute-start | bytes 196616 | tf_op jit(solution)/shard_map/ppermute | solution.py:18
  61.6 11.5 %all-to-all-start.2 = ((f32[32,8,8]{2,1,0:T(8,128)}), f32[32,8,8]{2,1,0:T(8,128)S(1)}, u32[]{:S(2)}, u32[]{:S(2)}) async-start(f32[32,8,8]{2,1,0:T(8,128)} %broadcast_in_dim.39), calls=%async_computation.2 | async-start | bytes 262144 | tf_op jit(solution)/shard_map/all_to_all | solution.py:160
  65.4 8.4 %copy-start.4 = (bf16[64,2048]{1,0:T(8,128)(2,1)}, bf16[64,2048]{1,0:T(8,128)(2,1)S(1)}, u32[]{:S(2)}) copy-start(bf16[64,2048]{1,0:T(8,128)(2,1)S(1)} %constant_dynamic-update-slice_fusion.2) | copy-start | bytes 786436

commit v2 on v0

v2 whole, which is shorter than its diff:
```python
import jax
import jax.numpy as jnp
from jax import lax
from jax.experimental import pallas as pl
from jax.experimental.pallas import tpu as pltpu
from jax.sharding import PartitionSpec as P

HOLDERS = 4
LANES = 128
TILE = 16
BIG = 48 * 1024 * 1024
TRANSPOSED = (((1,), (1,)), ((), ()))
VMEM = pl.BlockSpec(memory_space=pltpu.VMEM)
SMEM = pl.BlockSpec(memory_space=pltpu.SMEM)
ANY = pl.BlockSpec(memory_space=pl.ANY)
bf16 = jnp.bfloat16
f32 = jnp.float32


def swapped(array, axis, mask):
    return lax.ppermute(array, axis, [(i, i ^ mask) for i in range(lax.axis_size(axis))])


def dot_f32(a, b, dims):
    return lax.dot_general(a, b, dims, preferred_element_type=f32)


def call(body, outs, in_specs, operands, out_specs=None, scratch=()):
    return pl.pallas_call(
        body,
        out_shape=outs,
        in_specs=in_specs,
        out_specs=jax.tree.map(lambda _: VMEM, outs) if out_specs is None else out_specs,
        scratch_shapes=list(scratch),
        compiler_params=pltpu.CompilerParams(vmem_limit_bytes=BIG),
    )(*operands)


def norm_kernel(place_ref, states_ref, gain_ref, out_ref):
    states = states_ref[...].astype(f32)
    scale = lax.rsqrt(jnp.mean(states * states, axis=1, keepdims=True) + 1e-06)
    width = out_ref.shape[1]
    own = pl.ds(pl.multiple_of(place_ref[0] * width, width), width)
    out_ref[...] = (states_ref[:, own].astype(f32) * scale * gain_ref[:, own]).astype(bf16)


def stack_kernel(place_ref, *refs):
    pieces, out_ref = refs[:-1], refs[-1]
    rows = pieces[0].shape[0]
    for m, piece in enumerate(pieces):
        place = (place_ref[1] >> 1) ^ m
        out_ref[pl.ds(pl.multiple_of(place * rows, rows), rows)] = piece[...]


def stacked(place, pieces):
    rows, width = pieces[0].shape
    out = jax.ShapeDtypeStruct((rows * len(pieces), width), bf16)
    return call(stack_kernel, out, [SMEM] + [VMEM] * len(pieces), (place, *pieces))


def cut_kernel(place_ref, route_ref, after_ref, down_ref, *refs):
    outs, sems = refs[:-1], refs[-1]
    rows, width = down_ref.shape[0], outs[0].shape[1]
    holder = place_ref[1] & (HOLDERS - 1)
    copies = []
    for m, out_ref in enumerate(outs):
        columns = pl.ds(pl.multiple_of((holder ^ m) * width, width), width)
        copies.append(
            pltpu.make_async_copy(
                down_ref.at[:, columns], out_ref.at[pl.ds(0, rows)], sems.at[m]
            )
        )
        copies[-1].start()
    route = route_ref[...]
    high = route.astype(bf16)
    middle = (route - high.astype(f32)).astype(bf16)
    low = (route - high.astype(f32) - middle.astype(f32)).astype(bf16)
    count = route.shape[1]
    row = lax.broadcasted_iota(jnp.int32, (TILE, count), 0)
    terms = jnp.where(
        row == 0,
        high.astype(f32),
        jnp.where(row == 1, middle.astype(f32), jnp.where(row == 2, low.astype(f32), 0.0)),
    )
    terms = jnp.concatenate([terms, jnp.zeros((TILE, width - count), f32)], 1).astype(bf16)
    for out_ref in outs:
        out_ref[rows : rows + TILE] = terms
    for copy in copies:
        copy.wait()


def hidden_kernel(count, place_ref, near_ref, far_ref, near2_ref, far2_ref, gate_ref, up_ref, out_ref, tokens_ref):
    width = near_ref.shape[1]
    rows = near_ref.shape[0] // count
    x = place_ref[1] & 1
    for half, near, far in ((place_ref[0], near_ref, far_ref), (1 - place_ref[0], near2_ref, far2_ref)):
        columns = pl.ds(pl.multiple_of(half * width, width), width)
        for at, block in ((x, near), (1 - x, far)):
            for z in range(count):
                place = pl.multiple_of((2 * z + at) * rows, rows)
                tokens_ref[pl.ds(place, rows), columns] = block[z * rows : (z + 1) * rows]
    tokens = tokens_ref[...]
    gate = dot_f32(gate_ref[...], tokens, TRANSPOSED)
    upward = dot_f32(up_ref[...], tokens, TRANSPOSED)
    out_ref[...] = (gate / (1.0 + jnp.exp(-gate)) * upward).astype(bf16)


def features_kernel(place_ref, *refs):
    hidden_refs, down_refs = refs[:HOLDERS], refs[HOLDERS : 2 * HOLDERS]
    block_refs, centered_ref = refs[2 * HOLDERS : 3 * HOLDERS], refs[3 * HOLDERS]
    route_ref, features_ref = refs[3 * HOLDERS + 1 :]
    holder = place_ref[1] & (HOLDERS - 1)
    depth, tokens = hidden_refs[0].shape
    part = tokens // HOLDERS
    eye = lax.broadcasted_iota(jnp.int32, (part, part), 0) == lax.broadcasted_iota(
        jnp.int32, (part, part), 1
    )
    output = None
    for m, (hidden_ref, down_ref) in enumerate(zip(hidden_refs, down_refs)):
        product = dot_f32(hidden_ref[...], down_ref[:depth], (((0,), (0,)), ((), ())))
        output = product if output is None else output + product
        terms = down_ref[depth:, :part].astype(f32)
        route = jnp.sum(terms[:HOLDERS], axis=0, keepdims=True)
        column = jnp.sum(jnp.where(eye, route, 0.0), axis=1, keepdims=True)
        place = pl.multiple_of((holder ^ m) * part, part)
        route_ref[pl.ds(place, part)] = jnp.broadcast_to(column, (part, LANES))
    features = (output * route_ref[:, :1]).astype(bf16)
    features_ref[...] = features
    wide = features.astype(f32)
    mean = jnp.sum(wide, axis=0, keepdims=True) / tokens
    column = jnp.sum(wide * mean, axis=1, keepdims=True)
    row = jnp.transpose(jnp.broadcast_to(column, (tokens, LANES)))[:1]
    gram = dot_f32(features, features, TRANSPOSED)
    centered = (gram - column - row + jnp.sum(mean * mean)).astype(bf16)
    at = 0
    for i in range(tokens // TILE):
        for j in range(tokens // LANES):
            centered_ref[at * TILE : (at + 1) * TILE] = centered[
                i * TILE : (i + 1) * TILE, j * LANES : (j + 1) * LANES
            ]
            at += 1
    for m, block_ref in enumerate(block_refs):
        block_ref[...] = features_ref[pl.ds(pl.multiple_of((holder ^ m) * part, part), part)]


def place_kernel(place_ref, *refs):
    blocks, out_ref, sems = refs[:HOLDERS], refs[HOLDERS], refs[HOLDERS + 1]
    width = blocks[0].shape[1]
    holder = place_ref[1] & (HOLDERS - 1)
    copies = []
    for m, block in enumerate(blocks):
        columns = pl.ds(pl.multiple_of((holder ^ m) * width, width), width)
        copies.append(pltpu.make_async_copy(block, out_ref.at[:, columns], sems.at[m]))
        copies[-1].start()
    for copy in copies:
        copy.wait()


def pair_kernel(parts_ref, out_ref, flat_ref):
    copies, experts, _ = out_ref.shape
    parts = parts_ref[...].astype(f32)
    total = parts[:, 0]
    for holder in range(1, parts.shape[1]):
        total = total + parts[:, holder]
    flat_ref[...] = total.astype(bf16).astype(f32)
    lane = lax.broadcasted_iota(jnp.int32, (experts, experts), 1)

    def one(expert, table):
        products = jnp.sum(flat_ref[...] * flat_ref[pl.ds(expert, 1)], axis=1)
        return jnp.where(lane == expert, jnp.sum(products, axis=1, keepdims=True), table)

    table = lax.fori_loop(0, experts, one, jnp.zeros((experts, experts), f32), unroll=experts <= 8)
    for copy in range(copies):
        out_ref[copy] = table


def cka_kernel(tables_ref, out_ref):
    totals = jnp.sum(tables_ref[...], axis=0)
    shape = totals.shape
    eye = lax.broadcasted_iota(jnp.int32, shape, 0) == lax.broadcasted_iota(jnp.int32, shape, 1)
    kept = jnp.where(eye, totals, 0.0)
    down = jnp.sum(kept, axis=1, keepdims=True)
    across = jnp.sum(kept, axis=0, keepdims=True)
    out_ref[...] = totals / jnp.sqrt(down * across)


def shards(probe_states, norm_gain, gate_weight, up_weight, down_weight, route_weight):
    groups, members = lax.axis_size("grp"), lax.axis_size("tok")
    devices = groups * members
    experts = devices // HOLDERS
    rows, model = probe_states.shape
    tokens = rows * members
    depth = gate_weight.shape[0]
    part, token_part = model // HOLDERS, tokens // HOLDERS
    place = jnp.stack([lax.axis_index("grp") & 1, lax.axis_index("tok")]).astype(jnp.int32)

    own = call(
        norm_kernel,
        jax.ShapeDtypeStruct((rows, model // 2), bf16),
        [SMEM, VMEM, VMEM],
        (place, probe_states, norm_gain[None, :]),
    )
    count = members // 2
    near = {0: own}
    for m in range(count - 1, 0, -1):
        near[m] = swapped(own, "tok", 2 * m)
    far = {m: swapped(near[m], "tok", 1) for m in range(count)}
    near = stacked(place, [near[m] for m in range(count)])
    near2 = swapped(near, "grp", 1)
    far = stacked(place, [far[m] for m in range(count)])
    far2 = swapped(far, "grp", 1)

    blocks = call(
        cut_kernel,
        [jax.ShapeDtypeStruct((depth + TILE, part), bf16)] * HOLDERS,
        [SMEM, VMEM, ANY, ANY],
        (place, route_weight, own, down_weight),
        scratch=[pltpu.SemaphoreType.DMA((HOLDERS,))],
    )
    downs = [swapped(b, "tok", m) if m else b for m, b in enumerate(blocks)]

    hidden = call(
        lambda *refs: hidden_kernel(count, *refs),
        jax.ShapeDtypeStruct((depth, tokens), bf16),
        [SMEM] + [VMEM] * 6,
        (place, near, far, near2, far2, gate_weight, up_weight),
        scratch=[pltpu.VMEM((tokens, model), bf16)],
    )
    hiddens = [swapped(hidden, "tok", m) if m else hidden for m in range(HOLDERS)]
    entries = tokens * tokens // LANES
    *blocks, centered = call(
        features_kernel,
        [jax.ShapeDtypeStruct((token_part, part), bf16)] * HOLDERS
        + [jax.ShapeDtypeStruct((entries, LANES), bf16)],
        [SMEM] + [VMEM] * (2 * HOLDERS),
        (place, *hiddens, *downs),
        scratch=[pltpu.VMEM((tokens, LANES), f32), pltpu.VMEM((tokens, part), bf16)],
    )
    arrived = lax.all_to_all(centered, ("grp", "tok"), split_axis=0, concat_axis=0, tiled=True)
    arrived = arrived.reshape(experts, HOLDERS, entries // devices, LANES)
    direct = devices * experts * experts <= 1 << 16
    tables = call(
        pair_kernel,
        jax.ShapeDtypeStruct((devices if direct else 1, experts, experts), f32),
        [VMEM],
        (arrived,),
        scratch=[pltpu.VMEM((experts, entries // devices, LANES), f32)],
    )
    if direct:
        tables = lax.all_to_all(tables, ("grp", "tok"), split_axis=0, concat_axis=0, tiled=True)
    else:
        tables = lax.psum(tables, ("grp", "tok"))
    cka = call(cka_kernel, jax.ShapeDtypeStruct((experts, experts), f32), [VMEM], (tables,))

    blocks = [swapped(b, "tok", m) if m else b for m, b in enumerate(blocks)]
    features = call(
        place_kernel,
        jax.ShapeDtypeStruct((token_part, model), bf16),
        [SMEM] + [VMEM] * HOLDERS,
        (place, *blocks),
        out_specs=ANY,
        scratch=[pltpu.SemaphoreType.DMA((HOLDERS,))],
    )
    return (features, cka)


def solution(mesh):
    return jax.shard_map(
        shards,
        mesh=mesh,
        in_specs=(
            P("tok", None),
            P(),
            P(("grp", "tok"), None),
            P(("grp", "tok"), None),
            P(("grp", "tok"), None),
            P(("grp", "tok"), None),
        ),
        out_specs=(P(("grp", "tok"), None), P()),
        check_vma=False,
    )
```

time: 170 us -> 64.6 us (0.38)
  waiting for transfers between devices: 80.4 us -> 23.1 us
  blocking collectives: 44.4 us -> 0 us
  between operations: 14.2 us -> 0.81 us
  starting transfers between devices: 15.8 us -> 28.8 us
  Pallas kernels: 0 us -> 8.77 us
  other arithmetic: 7 us -> 0.08 us
  matrix products: 6.59 us -> 0 us
    ppermute x6 -> x18, waiting for transfers between devices: 52.8 us -> 12.5 us  [swapped(): lax.ppermute(array, axis, [(i, i ^ mask) for i in range(lax.axis_size(axi...]
    psum x1 -> x0, blocking collectives: 38.1 us -> none  [shards(): pair_totals = lax.psum(partial_value, ('grp', 'tok'))]
    all_gather x1 -> x0, waiting for transfers between devices: 20.9 us -> none  [shards(): piece = lax.all_gather(normed, 'tok', axis=0, tiled=True)]
    ppermute x6 -> x18, starting transfers between devices: 10.1 us -> 22.1 us  [swapped(): lax.ppermute(array, axis, [(i, i ^ mask) for i in range(lax.axis_size(axi...]
    pallas_call x0 -> x9, Pallas kernels: none -> 8.77 us  [call(): pl.pallas_call(body, out_shape=outs, in_specs=in_specs, out_specs=jax.tre...]
    dot_general x5 -> x0, matrix products: 6.59 us -> none  [the longest x1 2.96 us: shards(): output = jnp.dot(hidden, weights_now, preferred_element_type=jnp.float32)]
    all_to_all x1 -> x0, blocking collectives: 6.3 us -> none  [shards(): lax.all_to_all(blocks, 'grp', split_axis=0, concat_axis=0, tiled=True)]
    all_to_all x1 -> x2, waiting for transfers between devices: 6.68 us -> 10.6 us  [the longest x1 6.43 us: shards(): lax.all_to_all(tables, ('grp', 'tok'), split_axis=0, concat_axis=0, tiled...]
  transfers between devices with their start and end apart: 8 -> 20, of which waited for: 7 -> 10; matrix products, arithmetic and copies ran while one was open for 3% -> 0% of each run, Pallas kernels for 0% -> 8%
where the time goes in v2:
time: 64.6 us; the launch traced here: 64.3 us
  starting transfers between devices  28.8 us (45%)
  waiting for transfers between devices  23.1 us (36%)
  Pallas kernels  8.77 us (14%)
  local copies, waits for them, and re-layouts  2.8 us (4%)
  between operations  0.81 us (1%)
    ppermute x18, starting transfers between devices, swapped(): lax.ppermute(array, axis, [(i, i ^ mask) for i in range(lax.axis_size(axi...  22.1 us
    ppermute x18, waiting for transfers between devices, swapped(): lax.ppermute(array, axis, [(i, i ^ mask) for i in range(lax.axis_size(axi...  12.5 us
    pallas_call x9, Pallas kernels, call(): pl.pallas_call(body, out_shape=outs, in_specs=in_specs, out_specs=jax.tre...  8.77 us
    all_to_all x1, waiting for transfers between devices, shards(): lax.all_to_all(tables, ('grp', 'tok'), split_axis=0, concat_axis=0, tiled...  6.43 us
    all_to_all x1, waiting for transfers between devices, shards(): lax.all_to_all(centered, ('grp', 'tok'), split_axis=0, concat_axis=0, til...  4.19 us
    all_to_all x1, starting transfers between devices, shards(): lax.all_to_all(centered, ('grp', 'tok'), split_axis=0, concat_axis=0, til...  4.17 us
    unnamed x12, local copies, waits for them, and re-layouts  2.8 us
    all_to_all x1, starting transfers between devices, shards(): lax.all_to_all(tables, ('grp', 'tok'), split_axis=0, concat_axis=0, tiled...  2.57 us
  transfers between devices with their start and end apart: 20, of which 10 were waited for; matrix products, arithmetic and copies ran while one was open for 0% of the time, Pallas kernels for 8%

profile of v2, /device:TPU:0, one launch (start us, length us, event | category | flops | bytes accessed | tf_op | source)
XLA Modules:
  0.0 64.3 jit_solution(4549930196517625115)
XLA Ops:
  0.6 0.0 copy-start
  0.6 0.1 pad_add_fusion.place_ref.refs_0_
  0.7 0.0 copy-start.3
  0.7 1.0 %copy-done.3 = bf16[32,2048]{1,0:T(8,128)(2,1)S(1)} copy-done((bf16[32,2048]{1,0:T(8,128)(2,1)S(1)}, bf16[32,2048]{1,0:T(8,128)(2,1)}, u32[]{:S(2)}) %copy-start.3) | copy-done | bytes 131096
  1.7 0.0 copy-start.4
  1.7 0.7 %copy-done.4 = f32[2048]{0:T(1024)S(1)} copy-done((f32[2048]{0:T(1024)S(1)}, f32[2048]{0:T(1024)}, u32[]{:S(2)}) %copy-start.4) | copy-done | bytes 8216
  2.4 0.7 %shard_map.77.refs_0_.after_ref = bf16[32,1024]{1,0:T(8,128)(2,1)S(1)} custom-call(s32[2]{0:T(128)S(1)} %pad_add_fusion.place_ref.refs_0_, bf16[32,2048]{1,0:T(8,128)(2,1)S(1)} %copy-done.3, f32[1,2048]{1,0:T(1,128)S(1)} %bitcast.6), custom_call_target="tpu_custom_call" | custom-call | tf_op jit(solution)/shard_map/pallas_call | solution.py:29
  3.0 5.1 %collective-permute-start.2 = (bf16[32,1024]{1,0:T(8,128)(2,1)S(1)}, bf16[32,1024]{1,0:T(8,128)(2,1)S(1)}, u32[]{:S(2)}, u32[]{:S(2)}) collective-permute-start(bf16[32,1024]{1,0:T(8,128)(2,1)S(1)} %shard_map.77.refs_0_.after_ref), channel_id=1, source_target_pairs={{0,6},{1,7},{2,4},{3,5},{4,2},{5,3},{6,0},{7,1},{8,14},{9,15},{10,... | collective-permute-start | bytes 196616 | tf_op jit(solution)/shard_map/ppermute | solution.py:21
  8.2 0.0 collective-permute-start.1
  8.2 0.6 collective-permute-start
  8.8 1.6 %collective-permute-start.3 = (bf16[32,1024]{1,0:T(8,128)(2,1)S(1)}, bf16[32,1024]{1,0:T(8,128)(2,1)S(1)}, u32[]{:S(2)}, u32[]{:S(2)}) collective-permute-start(bf16[32,1024]{1,0:T(8,128)(2,1)S(1)} %shard_map.77.refs_0_.after_ref), channel_id=1, source_target_pairs={{0,1},{1,0},{2,3},{3,2},{4,5},{5,4},{6,7},{7,6},{8,9},{9,8},{10,11... | collective-permute-start | bytes 196616 | tf_op jit(solution)/shard_map/ppermute | solution.py:21
  10.4 0.3 collective-permute-done.2.refs_3_
  10.7 1.9 %collective-permute-start.6 = (bf16[32,1024]{1,0:T(8,128)(2,1)S(1)}, bf16[32,1024]{1,0:T(8,128)(2,1)S(1)}, u32[]{:S(2)}, u32[]{:S(2)}) collective-permute-start(bf16[32,1024]{1,0:T(8,128)(2,1)S(1)} %collective-permute-done.2.refs_3_), channel_id=1, source_target_pairs={{0,1},{1,0},{2,3},{3,2},{4,5},{5,4},{6,7},{7,6},{8,9},{9,8},{10,11... | collective-permute-start | bytes 196616 | tf_op jit(solution)/shard_map/ppermute | solution.py:21
  12.6 1.2 %collective-permute-done.1.refs_2_ = bf16[32,1024]{1,0:T(8,128)(2,1)S(1)} collective-permute-done((bf16[32,1024]{1,0:T(8,128)(2,1)S(1)}, bf16[32,1024]{1,0:T(8,128)(2,1)S(1)}, u32[]{:S(2)}, u32[]{:S(2)}) %collective-permute-start.1) | collective-permute-done | bytes 65568 | tf_op jit(solution)/shard_map/ppermute | solution.py:21
  13.8 1.5 %collective-permute-start.5 = (bf16[32,1024]{1,0:T(8,128)(2,1)S(1)}, bf16[32,1024]{1,0:T(8,128)(2,1)S(1)}, u32[]{:S(2)}, u32[]{:S(2)}) collective-permute-start(bf16[32,1024]{1,0:T(8,128)(2,1)S(1)} %collective-permute-done.1.refs_2_), channel_id=1, source_target_pairs={{0,1},{1,0},{2,3},{3,2},{4,5},{5,4},{6,7},{7,6},{8,9},{9,8},{10,11... | collective-permute-start | bytes 196616 | tf_op jit(solution)/shard_map/ppermute | solution.py:21
  15.3 0.0 collective-permute-done.refs_1_
  15.3 0.5 collective-permute-start.4
  15.8 0.0 copy-start.5
  15.8 0.6 shard_map.78.refs_1_
  16.4 0.0 copy-start.1
  16.4 0.1 collective-permute-start.7
  16.5 0.0 collective-permute-done.3.refs_0_
  16.5 0.0 collective-permute-done.6.refs_3_
  16.5 2.2 %collective-permute-done.5.refs_2_ = bf16[32,1024]{1,0:T(8,128)(2,1)S(1)} collective-permute-done((bf16[32,1024]{1,0:T(8,128)(2,1)S(1)}, bf16[32,1024]{1,0:T(8,128)(2,1)S(1)}, u32[]{:S(2)}, u32[]{:S(2)}) %collective-permute-start.5) | collective-permute-done | bytes 65568 | tf_op jit(solution)/shard_map/ppermute | solution.py:21
  18.6 0.9 %collective-permute-done.4.refs_1_ = bf16[32,1024]{1,0:T(8,128)(2,1)S(1)} collective-permute-done((bf16[32,1024]{1,0:T(8,128)(2,1)S(1)}, bf16[32,1024]{1,0:T(8,128)(2,1)S(1)}, u32[]{:S(2)}, u32[]{:S(2)}) %collective-permute-start.4) | collective-permute-done | bytes 65568 | tf_op jit(solution)/shard_map/ppermute | solution.py:21
  19.5 0.6 shard_map.79.refs_2_
  20.1 0.1 collective-permute-start.8
  20.2 0.0 copy-done
  20.2 0.0 copy-done.5
  20.2 0.7 %shard_map.81 = (bf16[208,512]{1,0:T(8,128)(2,1)S(1)}, bf16[208,512]{1,0:T(8,128)(2,1)S(1)}, bf16[208,512]{1,0:T(8,128)(2,1)S(1)}, bf16[208,512]{1,0:T(8,128)(2,1)S(1)}) custom-call(s32[2]{0:T(128)S(1)} %pad_add_fusion.place_ref.refs_0_, f32[1,64]{1,0:T(1,128)S(1)} %copy-done.5, bf16[32,1024]{1,0:T(8,128)(2,1)S(1)} %shard_map.77.refs_0_.after_ref, ...), custom_call_target="tpu_custom_call" | custom-call | tf_op jit(solution)/shard_map/pallas_call | solution.py:29
  20.9 1.0 %collective-permute-start.12 = (bf16[208,512]{1,0:T(8,128)(2,1)S(1)}, bf16[208,512]{1,0:T(8,128)(2,1)S(1)}, u32[]{:S(2)}, u32[]{:S(2)}) collective-permute-start(bf16[208,512]{1,0:T(8,128)(2,1)S(1)} %get-tuple-element.12), channel_id=1, source_target_pairs={{0,1},{1,0},{2,3},{3,2},{4,5},{5,4},{6,7},{7,6},{8,9},{9,8},{10,11... | collective-permute-start | bytes 638984 | tf_op jit(solution)/shard_map/ppermute | solution.py:21
  22.0 0.4 collective-permute-start.13
  22.4 2.1 %collective-permute-start.14 = (bf16[208,512]{1,0:T(8,128)(2,1)S(1)}, bf16[208,512]{1,0:T(8,128)(2,1)S(1)}, u32[]{:S(2)}, u32[]{:S(2)}) collective-permute-start(bf16[208,512]{1,0:T(8,128)(2,1)S(1)} %get-tuple-element.14), channel_id=1, source_target_pairs={{0,3},{1,2},{2,1},{3,0},{4,7},{5,6},{6,5},{7,4},{8,11},{9,10},{10,... | collective-permute-start | bytes 638984 | tf_op jit(solution)/shard_map/ppermute | solution.py:21
  24.5 0.0 collective-permute-done.7.refs_3_
  24.5 0.0 collective-permute-done.8.refs_4_
  24.5 0.0 copy-done.1
  24.5 0.0 copy-start.2
  24.5 1.1 %copy-done.2 = bf16[192,2048]{1,0:T(8,128)(2,1)S(1)} copy-done((bf16[192,2048]{1,0:T(8,128)(2,1)S(1)}, bf16[192,2048]{1,0:T(8,128)(2,1)}, u32[]{:S(2)}) %copy-start.2) | copy-done | bytes 786456
  25.6 1.5 %shard_map.80.refs_0_ = bf16[192,256]{1,0:T(8,128)(2,1)S(1)} custom-call(s32[2]{0:T(128)S(1)} %pad_add_fusion.place_ref.refs_0_, bf16[128,1024]{1,0:T(8,128)(2,1)S(1)} %shard_map.78.refs_1_, bf16[128,1024]{1,0:T(8,128)(2,1)S(1)} %shard_map.79.refs_2_, bf16[128,1024]{1,0:T(8,128)(2,1)S(1)} %collective-permute-done.7.refs_3_, ...), custom_call_target="tpu_custom_call" | custom-call | tf_op jit(solution)/shard_map/pallas_call | solution.py:29
  27.1 0.9 %collective-permute-start.11 = (bf16[192,256]{1,0:T(8,128)(2,1)S(1)}, bf16[192,256]{1,0:T(8,128)(2,1)S(1)}, u32[]{:S(2)}, u32[]{:S(2)}) collective-permute-start(bf16[192,256]{1,0:T(8,128)(2,1)S(1)} %shard_map.80.refs_0_), channel_id=1, source_target_pairs={{0,3},{1,2},{2,1},{3,0},{4,7},{5,6},{6,5},{7,4},{8,11},{9,10},{10,... | collective-permute-start | bytes 294920 | tf_op jit(solution)/shard_map/ppermute | solution.py:21
  28.0 1.6 %collective-permute-start.10 = (bf16[192,256]{1,0:T(8,128)(2,1)S(1)}, bf16[192,256]{1,0:T(8,128)(2,1)S(1)}, u32[]{:S(2)}, u32[]{:S(2)}) collective-permute-start(bf16[192,256]{1,0:T(8,128)(2,1)S(1)} %shard_map.80.refs_0_), channel_id=1, source_target_pairs={{0,2},{1,3},{2,0},{3,1},{4,6},{5,7},{6,4},{7,5},{8,10},{9,11},{10,... | collective-permute-start | bytes 294920 | tf_op jit(solution)/shard_map/ppermute | solution.py:21
  29.6 0.0 collective-permute-done.12.refs_5_
  29.6 1.1 %collective-permute-start.9 = (bf16[192,256]{1,0:T(8,128)(2,1)S(1)}, bf16[192,256]{1,0:T(8,128)(2,1)S(1)}, u32[]{:S(2)}, u32[]{:S(2)}) collective-permute-start(bf16[192,256]{1,0:T(8,128)(2,1)S(1)} %shard_map.80.refs_0_), channel_id=1, source_target_pairs={{0,1},{1,0},{2,3},{3,2},{4,5},{5,4},{6,7},{7,6},{8,9},{9,8},{10,11... | collective-permute-start | bytes 294920 | tf_op jit(solution)/shard_map/ppermute | solution.py:21
  30.7 0.0 collective-permute-done.13.refs_6_
  30.7 4.5 %collective-permute-done.14.refs_7_ = bf16[208,512]{1,0:T(8,128)(2,1)S(1)} collective-permute-done((bf16[208,512]{1,0:T(8,128)(2,1)S(1)}, bf16[208,512]{1,0:T(8,128)(2,1)S(1)}, u32[]{:S(2)}, u32[]{:S(2)}) %collective-permute-start.14) | collective-permute-done | bytes 213024 | tf_op jit(solution)/shard_map/ppermute | solution.py:21
  35.2 2.1 %collective-permute-done.11.refs_3_ = bf16[192,256]{1,0:T(8,128)(2,1)S(1)} collective-permute-done((bf16[192,256]{1,0:T(8,128)(2,1)S(1)}, bf16[192,256]{1,0:T(8,128)(2,1)S(1)}, u32[]{:S(2)}, u32[]{:S(2)}) %collective-permute-start.11) | collective-permute-done | bytes 98336 | tf_op jit(solution)/shard_map/ppermute | solution.py:21
  37.3 0.9 %collective-permute-done.10.refs_2_ = bf16[192,256]{1,0:T(8,128)(2,1)S(1)} collective-permute-done((bf16[192,256]{1,0:T(8,128)(2,1)S(1)}, bf16[192,256]{1,0:T(8,128)(2,1)S(1)}, u32[]{:S(2)}, u32[]{:S(2)}) %collective-permute-start.10) | collective-permute-done | bytes 98336 | tf_op jit(solution)/shard_map/ppermute | solution.py:21
  38.1 0.4 collective-permute-done.9.refs_1_
  38.6 2.0 %shard_map.82 = (bf16[64,512]{1,0:T(8,128)(2,1)S(1)}, bf16[64,512]{1,0:T(8,128)(2,1)S(1)}, bf16[64,512]{1,0:T(8,128)(2,1)S(1)}, bf16[64,512]{1,0:T(8,128)(2,1)S(1)}, bf16[512,128]{1,0:T(8,128)(2,1)}) custom-call(s32[2]{0:T(128)S(1)} %pad_add_fusion.place_ref.refs_0_, bf16[192,256]{1,0:T(8,128)(2,1)S(1)} %shard_map.80.refs_0_, ...), custom_call_target="tpu_custom_call" | custom-call | tf_op jit(solution)/shard_map/pallas_call | solution.py:29
  40.6 4.2 %all-to-all-start = ((bf16[32,16,128]{2,1,0:T(8,128)(2,1)}), bf16[32,16,128]{2,1,0:T(8,128)(2,1)S(1)}, u32[]{:S(2)}, u32[]{:S(2)}) async-start(bf16[32,16,128]{2,1,0:T(8,128)(2,1)} %bitcast.3), calls=%async_computation | async-start | bytes 262144 | tf_op jit(solution)/shard_map/all_to_all | solution.py:239
  44.7 1.8 %collective-permute-start.15 = (bf16[64,512]{1,0:T(8,128)(2,1)S(1)}, bf16[64,512]{1,0:T(8,128)(2,1)S(1)}, u32[]{:S(2)}, u32[]{:S(2)}) collective-permute-start(bf16[64,512]{1,0:T(8,128)(2,1)S(1)} %get-tuple-element.16), channel_id=1, source_target_pairs={{0,1},{1,0},{2,3},{3,2},{4,5},{5,4},{6,7},{7,6},{8,9},{9,8},{10,11... | collective-permute-start | bytes 196616 | tf_op jit(solution)/shard_map/ppermute | solution.py:21
  46.6 1.5 %collective-permute-start.16 = (bf16[64,512]{1,0:T(8,128)(2,1)S(1)}, bf16[64,512]{1,0:T(8,128)(2,1)S(1)}, u32[]{:S(2)}, u32[]{:S(2)}) collective-permute-start(bf16[64,512]{1,0:T(8,128)(2,1)S(1)} %get-tuple-element.17), channel_id=1, source_target_pairs={{0,2},{1,3},{2,0},{3,1},{4,6},{5,7},{6,4},{7,5},{8,10},{9,11},{10,... | collective-permute-start | bytes 196616 | tf_op jit(solution)/shard_map/ppermute | solution.py:21
  48.0 0.3 collective-permute-start.17
  48.3 4.2 %all-to-all-done = bf16[32,16,128]{2,1,0:T(8,128)(2,1)S(1)} async-done(((bf16[32,16,128]{2,1,0:T(8,128)(2,1)}), bf16[32,16,128]{2,1,0:T(8,128)(2,1)S(1)}, u32[]{:S(2)}, u32[]{:S(2)}) %all-to-all-start) | async-done | bytes 131104 | tf_op jit(solution)/shard_map/all_to_all | solution.py:239
  52.5 0.8 %shard_map.84 = f32[32,8,8]{2,1,0:T(8,128)} custom-call(bf16[8,4,16,128]{3,2,1,0:T(8,128)(2,1)S(1)} %bitcast.5), custom_call_target="tpu_custom_call" | custom-call | tf_op jit(solution)/shard_map/pallas_call | solution.py:29
  53.3 2.6 %all-to-all-start.1 = ((f32[32,8,8]{2,1,0:T(8,128)}), f32[32,8,8]{2,1,0:T(8,128)S(1)}, u32[]{:S(2)}, u32[]{:S(2)}) async-start(f32[32,8,8]{2,1,0:T(8,128)} %shard_map.84), calls=%async_computation.1 | async-start | bytes 262144 | tf_op jit(solution)/shard_map/all_to_all | solution.py:250
  55.9 0.0 collective-permute-done.15.refs_1_
  55.9 0.0 collective-permute-done.16.refs_2_
  55.9 0.0 collective-permute-done.17.refs_3_
  55.9 1.3 %shard_map.83 = bf16[64,2048]{1,0:T(8,128)(2,1)} custom-call(s32[2]{0:T(128)S(1)} %pad_add_fusion.place_ref.refs_0_, bf16[64,512]{1,0:T(8,128)(2,1)S(1)} %get-tuple-element.15.refs_0_, bf16[64,512]{1,0:T(8,128)(2,1)S(1)} %collective-permute-done.15.refs_1_, bf16[64,512]{1,0:T(8,128)(2,1)S(1)} %collective-permute-done.16.refs_2_, ...), custom_call_target="tpu_custom_call" | custom-call | tf_op jit(solution)/shard_map/pallas_call | solution.py:29
  57.2 6.4 %all-to-all-done.1.tables_ref = f32[32,8,8]{2,1,0:T(8,128)S(1)} async-done(((f32[32,8,8]{2,1,0:T(8,128)}), f32[32,8,8]{2,1,0:T(8,128)S(1)}, u32[]{:S(2)}, u32[]{:S(2)}) %all-to-all-start.1) | async-done | bytes 8224 | tf_op jit(solution)/shard_map/all_to_all | solution.py:250
  63.6 0.7 %shard_map.85 = f32[8,8]{1,0:T(8,128)} custom-call(f32[32,8,8]{2,1,0:T(8,128)S(1)} %all-to-all-done.1.tables_ref), custom_call_target="tpu_custom_call" | custom-call | tf_op jit(solution)/shard_map/pallas_call | solution.py:29
Async XLA Ops:
  0.6 19.5 %copy-start = (bf16[192,2048]{1,0:T(8,128)(2,1)S(1)}, bf16[192,2048]{1,0:T(8,128)(2,1)}, u32[]{:S(2)}) copy-start(bf16[192,2048]{1,0:T(8,128)(2,1)} %down_ref.1) | copy-start | bytes 2359300
  0.7 1.0 %copy-start.3 = (bf16[32,2048]{1,0:T(8,128)(2,1)S(1)}, bf16[32,2048]{1,0:T(8,128)(2,1)}, u32[]{:S(2)}) copy-start(bf16[32,2048]{1,0:T(8,128)(2,1)} %states_ref.1) | copy-start | bytes 393220
  1.7 0.7 %copy-start.4 = (f32[2048]{0:T(1024)S(1)}, f32[2048]{0:T(1024)}, u32[]{:S(2)}) copy-start(f32[2048]{0:T(1024)} %param.7) | copy-start | bytes 24580
  3.0 7.7 %collective-permute-start.2 = (bf16[32,1024]{1,0:T(8,128)(2,1)S(1)}, bf16[32,1024]{1,0:T(8,128)(2,1)S(1)}, u32[]{:S(2)}, u32[]{:S(2)}) collective-permute-start(bf16[32,1024]{1,0:T(8,128)(2,1)S(1)} %shard_map.77.refs_0_.after_ref), channel_id=1, source_target_pairs={{0,6},{1,7},{2,4},{3,5},{4,2},{5,3},{6,0},{7,1},{8,14},{9,15},{10,... | collective-permute-start | bytes 196616 | tf_op jit(solution)/shard_map/ppermute | solution.py:21
  8.2 5.6 %collective-permute-start.1 = (bf16[32,1024]{1,0:T(8,128)(2,1)S(1)}, bf16[32,1024]{1,0:T(8,128)(2,1)S(1)}, u32[]{:S(2)}, u32[]{:S(2)}) collective-permute-start(bf16[32,1024]{1,0:T(8,128)(2,1)S(1)} %shard_map.77.refs_0_.after_ref), channel_id=1, source_target_pairs={{0,4},{1,5},{2,6},{3,7},{4,0},{5,1},{6,2},{7,3},{8,12},{9,13},{10,... | collective-permute-start | bytes 196616 | tf_op jit(solution)/shard_map/ppermute | solution.py:21
  8.2 7.1 %collective-permute-start = (bf16[32,1024]{1,0:T(8,128)(2,1)S(1)}, bf16[32,1024]{1,0:T(8,128)(2,1)S(1)}, u32[]{:S(2)}, u32[]{:S(2)}) collective-permute-start(bf16[32,1024]{1,0:T(8,128)(2,1)S(1)} %shard_map.77.refs_0_.after_ref), channel_id=1, source_target_pairs={{0,2},{1,3},{2,0},{3,1},{4,6},{5,7},{6,4},{7,5},{8,10},{9,11},{10,... | collective-permute-start | bytes 196616 | tf_op jit(solution)/shard_map/ppermute | solution.py:21
  8.8 7.7 %collective-permute-start.3 = (bf16[32,1024]{1,0:T(8,128)(2,1)S(1)}, bf16[32,1024]{1,0:T(8,128)(2,1)S(1)}, u32[]{:S(2)}, u32[]{:S(2)}) collective-permute-start(bf16[32,1024]{1,0:T(8,128)(2,1)S(1)} %shard_map.77.refs_0_.after_ref), channel_id=1, source_target_pairs={{0,1},{1,0},{2,3},{3,2},{4,5},{5,4},{6,7},{7,6},{8,9},{9,8},{10,11... | collective-permute-start | bytes 196616 | tf_op jit(solution)/shard_map/ppermute | solution.py:21
  10.7 5.7 %collective-permute-start.6 = (bf16[32,1024]{1,0:T(8,128)(2,1)S(1)}, bf16[32,1024]{1,0:T(8,128)(2,1)S(1)}, u32[]{:S(2)}, u32[]{:S(2)}) collective-permute-start(bf16[32,1024]{1,0:T(8,128)(2,1)S(1)} %collective-permute-done.2.refs_3_), channel_id=1, source_target_pairs={{0,1},{1,0},{2,3},{3,2},{4,5},{5,4},{6,7},{7,6},{8,9},{9,8},{10,11... | collective-permute-start | bytes 196616 | tf_op jit(solution)/shard_map/ppermute | solution.py:21
  13.8 4.9 %collective-permute-start.5 = (bf16[32,1024]{1,0:T(8,128)(2,1)S(1)}, bf16[32,1024]{1,0:T(8,128)(2,1)S(1)}, u32[]{:S(2)}, u32[]{:S(2)}) collective-permute-start(bf16[32,1024]{1,0:T(8,128)(2,1)S(1)} %collective-permute-done.1.refs_2_), channel_id=1, source_target_pairs={{0,1},{1,0},{2,3},{3,2},{4,5},{5,4},{6,7},{7,6},{8,9},{9,8},{10,11... | collective-permute-start | bytes 196616 | tf_op jit(solution)/shard_map/ppermute | solution.py:21
  15.3 4.3 %collective-permute-start.4 = (bf16[32,1024]{1,0:T(8,128)(2,1)S(1)}, bf16[32,1024]{1,0:T(8,128)(2,1)S(1)}, u32[]{:S(2)}, u32[]{:S(2)}) collective-permute-start(bf16[32,1024]{1,0:T(8,128)(2,1)S(1)} %collective-permute-done.refs_1_), channel_id=1, source_target_pairs={{0,1},{1,0},{2,3},{3,2},{4,5},{5,4},{6,7},{7,6},{8,9},{9,8},{10,11... | collective-permute-start | bytes 196616 | tf_op jit(solution)/shard_map/ppermute | solution.py:21
  15.8 4.4 %copy-start.5 = (f32[1,64]{1,0:T(1,128)S(1)}, f32[1,64]{1,0:T(1,128)}, u32[]{:S(2)}) copy-start(f32[1,64]{1,0:T(1,128)} %route_ref.1) | copy-start | bytes 772
  16.4 8.1 %copy-start.1 = (bf16[192,2048]{1,0:T(8,128)(2,1)S(1)}, bf16[192,2048]{1,0:T(8,128)(2,1)}, u32[]{:S(2)}) copy-start(bf16[192,2048]{1,0:T(8,128)(2,1)} %refs_5_.1) | copy-start | bytes 2359300
  16.4 8.1 %collective-permute-start.7 = (bf16[128,1024]{1,0:T(8,128)(2,1)S(1)}, bf16[128,1024]{1,0:T(8,128)(2,1)S(1)}, u32[]{:S(2)}, u32[]{:S(2)}) collective-permute-start(bf16[128,1024]{1,0:T(8,128)(2,1)S(1)} %shard_map.78.refs_1_), channel_id=1, source_target_pairs={{0,8},{8,0},{16,24},{24,16},{1,9},{9,1},{17,25},{25,17},{2,10},{10... | collective-permute-start | bytes 786440 | tf_op jit(solution)/shard_map/ppermute | solution.py:21
  20.1 4.4 %collective-permute-start.8 = (bf16[128,1024]{1,0:T(8,128)(2,1)S(1)}, bf16[128,1024]{1,0:T(8,128)(2,1)S(1)}, u32[]{:S(2)}, u32[]{:S(2)}) collective-permute-start(bf16[128,1024]{1,0:T(8,128)(2,1)S(1)} %shard_map.79.refs_2_), channel_id=1, source_target_pairs={{0,8},{8,0},{16,24},{24,16},{1,9},{9,1},{17,25},{25,17},{2,10},{10... | collective-permute-start | bytes 786440 | tf_op jit(solution)/shard_map/ppermute | solution.py:21
  20.9 8.7 %collective-permute-start.12 = (bf16[208,512]{1,0:T(8,128)(2,1)S(1)}, bf16[208,512]{1,0:T(8,128)(2,1)S(1)}, u32[]{:S(2)}, u32[]{:S(2)}) collective-permute-start(bf16[208,512]{1,0:T(8,128)(2,1)S(1)} %get-tuple-element.12), channel_id=1, source_target_pairs={{0,1},{1,0},{2,3},{3,2},{4,5},{5,4},{6,7},{7,6},{8,9},{9,8},{10,11... | collective-permute-start | bytes 638984 | tf_op jit(solution)/shard_map/ppermute | solution.py:21
  22.0 8.7 %collective-permute-start.13 = (bf16[208,512]{1,0:T(8,128)(2,1)S(1)}, bf16[208,512]{1,0:T(8,128)(2,1)S(1)}, u32[]{:S(2)}, u32[]{:S(2)}) collective-permute-start(bf16[208,512]{1,0:T(8,128)(2,1)S(1)} %get-tuple-element.13), channel_id=1, source_target_pairs={{0,2},{1,3},{2,0},{3,1},{4,6},{5,7},{6,4},{7,5},{8,10},{9,11},{10,... | collective-permute-start | bytes 638984 | tf_op jit(solution)/shard_map/ppermute | solution.py:21
  22.4 12.8 %collective-permute-start.14 = (bf16[208,512]{1,0:T(8,128)(2,1)S(1)}, bf16[208,512]{1,0:T(8,128)(2,1)S(1)}, u32[]{:S(2)}, u32[]{:S(2)}) collective-permute-start(bf16[208,512]{1,0:T(8,128)(2,1)S(1)} %get-tuple-element.14), channel_id=1, source_target_pairs={{0,3},{1,2},{2,1},{3,0},{4,7},{5,6},{6,5},{7,4},{8,11},{9,10},{10,... | collective-permute-start | bytes 638984 | tf_op jit(solution)/shard_map/ppermute | solution.py:21
  24.5 1.1 %copy-start.2 = (bf16[192,2048]{1,0:T(8,128)(2,1)S(1)}, bf16[192,2048]{1,0:T(8,128)(2,1)}, u32[]{:S(2)}) copy-start(bf16[192,2048]{1,0:T(8,128)(2,1)} %refs_6_.1) | copy-start | bytes 2359300
  27.1 10.1 %collective-permute-start.11 = (bf16[192,256]{1,0:T(8,128)(2,1)S(1)}, bf16[192,256]{1,0:T(8,128)(2,1)S(1)}, u32[]{:S(2)}, u32[]{:S(2)}) collective-permute-start(bf16[192,256]{1,0:T(8,128)(2,1)S(1)} %shard_map.80.refs_0_), channel_id=1, source_target_pairs={{0,3},{1,2},{2,1},{3,0},{4,7},{5,6},{6,5},{7,4},{8,11},{9,10},{10,... | collective-permute-start | bytes 294920 | tf_op jit(solution)/shard_map/ppermute | solution.py:21
  28.0 10.1 %collective-permute-start.10 = (bf16[192,256]{1,0:T(8,128)(2,1)S(1)}, bf16[192,256]{1,0:T(8,128)(2,1)S(1)}, u32[]{:S(2)}, u32[]{:S(2)}) collective-permute-start(bf16[192,256]{1,0:T(8,128)(2,1)S(1)} %shard_map.80.refs_0_), channel_id=1, source_target_pairs={{0,2},{1,3},{2,0},{3,1},{4,6},{5,7},{6,4},{7,5},{8,10},{9,11},{10,... | collective-permute-start | bytes 294920 | tf_op jit(solution)/shard_map/ppermute | solution.py:21
  29.6 9.0 %collective-permute-start.9 = (bf16[192,256]{1,0:T(8,128)(2,1)S(1)}, bf16[192,256]{1,0:T(8,128)(2,1)S(1)}, u32[]{:S(2)}, u32[]{:S(2)}) collective-permute-start(bf16[192,256]{1,0:T(8,128)(2,1)S(1)} %shard_map.80.refs_0_), channel_id=1, source_target_pairs={{0,1},{1,0},{2,3},{3,2},{4,5},{5,4},{6,7},{7,6},{8,9},{9,8},{10,11... | collective-permute-start | bytes 294920 | tf_op jit(solution)/shard_map/ppermute | solution.py:21
  40.6 11.9 %all-to-all-start = ((bf16[32,16,128]{2,1,0:T(8,128)(2,1)}), bf16[32,16,128]{2,1,0:T(8,128)(2,1)S(1)}, u32[]{:S(2)}, u32[]{:S(2)}) async-start(bf16[32,16,128]{2,1,0:T(8,128)(2,1)} %bitcast.3), calls=%async_computation | async-start | bytes 262144 | tf_op jit(solution)/shard_map/all_to_all | solution.py:239
  44.7 11.1 %collective-permute-start.15 = (bf16[64,512]{1,0:T(8,128)(2,1)S(1)}, bf16[64,512]{1,0:T(8,128)(2,1)S(1)}, u32[]{:S(2)}, u32[]{:S(2)}) collective-permute-start(bf16[64,512]{1,0:T(8,128)(2,1)S(1)} %get-tuple-element.16), channel_id=1, source_target_pairs={{0,1},{1,0},{2,3},{3,2},{4,5},{5,4},{6,7},{7,6},{8,9},{9,8},{10,11... | collective-permute-start | bytes 196616 | tf_op jit(solution)/shard_map/ppermute | solution.py:21
  46.6 9.3 %collective-permute-start.16 = (bf16[64,512]{1,0:T(8,128)(2,1)S(1)}, bf16[64,512]{1,0:T(8,128)(2,1)S(1)}, u32[]{:S(2)}, u32[]{:S(2)}) collective-permute-start(bf16[64,512]{1,0:T(8,128)(2,1)S(1)} %get-tuple-element.17), channel_id=1, source_target_pairs={{0,2},{1,3},{2,0},{3,1},{4,6},{5,7},{6,4},{7,5},{8,10},{9,11},{10,... | collective-permute-start | bytes 196616 | tf_op jit(solution)/shard_map/ppermute | solution.py:21
  48.0 7.8 %collective-permute-start.17 = (bf16[64,512]{1,0:T(8,128)(2,1)S(1)}, bf16[64,512]{1,0:T(8,128)(2,1)S(1)}, u32[]{:S(2)}, u32[]{:S(2)}) collective-permute-start(bf16[64,512]{1,0:T(8,128)(2,1)S(1)} %get-tuple-element.18), channel_id=1, source_target_pairs={{0,3},{1,2},{2,1},{3,0},{4,7},{5,6},{6,5},{7,4},{8,11},{9,10},{10,... | collective-permute-start | bytes 196616 | tf_op jit(solution)/shard_map/ppermute | solution.py:21
  53.3 10.3 %all-to-all-start.1 = ((f32[32,8,8]{2,1,0:T(8,128)}), f32[32,8,8]{2,1,0:T(8,128)S(1)}, u32[]{:S(2)}, u32[]{:S(2)}) async-start(f32[32,8,8]{2,1,0:T(8,128)} %shard_map.84), calls=%async_computation.1 | async-start | bytes 262144 | tf_op jit(solution)/shard_map/all_to_all | solution.py:250

commit v3 on v2

v3 whole, which is shorter than its diff:
```python
import jax
import jax.numpy as jnp
from jax import lax
from jax.experimental import pallas as pl
from jax.experimental.pallas import tpu as pltpu
from jax.sharding import PartitionSpec as P

HOLDERS = 4
LANES = 128
TILE = 16
BIG = 24 * 1024 * 1024
TRANSPOSED = (((1,), (1,)), ((), ()))
VMEM = pl.BlockSpec(memory_space=pltpu.VMEM)
ANY = pl.BlockSpec(memory_space=pl.ANY)
HBM = pl.BlockSpec(memory_space=pltpu.HBM)
bf16 = jnp.bfloat16
f32 = jnp.float32


def swapped(array, axis, mask):
    return lax.ppermute(array, axis, [(i, i ^ mask) for i in range(lax.axis_size(axis))])


def dot_f32(a, b, dims):
    return lax.dot_general(a, b, dims, preferred_element_type=f32)


def call(body, outs, in_specs, operands, out_specs=None, scratch=(), aliases={}):
    return pl.pallas_call(
        body,
        out_shape=outs,
        in_specs=in_specs,
        out_specs=jax.tree.map(lambda _: VMEM, outs) if out_specs is None else out_specs,
        scratch_shapes=list(scratch),
        compiler_params=pltpu.CompilerParams(vmem_limit_bytes=BIG),
        input_output_aliases=aliases,
    )(*operands)


def core():
    return lax.axis_index("grp") & 1


def holder():
    return lax.axis_index("tok") & (HOLDERS - 1)


def first_kernel(states_hbm, gain_hbm, down_hbm, *refs):
    out_ref, downs = refs[0], refs[1 : 1 + HOLDERS]
    states_ref, gain_ref, sems = refs[1 + HOLDERS :]
    copies = [
        pltpu.make_async_copy(states_hbm, states_ref, sems.at[0]),
        pltpu.make_async_copy(gain_hbm, gain_ref, sems.at[1]),
    ]
    width = downs[0].shape[1]
    for m, down_ref in enumerate(downs):
        columns = pl.ds(pl.multiple_of((holder() ^ m) * width, width), width)
        copies.append(pltpu.make_async_copy(down_hbm.at[:, columns], down_ref, sems.at[2 + m]))
    for copy in copies:
        copy.start()
    for copy in copies[:2]:
        copy.wait()
    states = states_ref[...].astype(f32)
    scale = lax.rsqrt(jnp.mean(states * states, axis=1, keepdims=True) + 1e-06)
    width = out_ref.shape[1]
    own = pl.ds(pl.multiple_of(core() * width, width), width)
    out_ref[...] = (states_ref[:, own].astype(f32) * scale * gain_ref[:, own]).astype(bf16)
    for copy in copies[2:]:
        copy.wait()


def hold_kernel(*refs):
    pass


def held(arrays, after):
    return call(
        hold_kernel,
        [jax.ShapeDtypeStruct(a.shape, a.dtype) for a in arrays],
        [ANY] * (len(arrays) + 1),
        (*arrays, after),
        out_specs=[ANY] * len(arrays),
        aliases={i: i for i in range(len(arrays))},
    )


def stack_kernel(*refs):
    pieces, out_ref = refs[1:-1], refs[-1]
    rows = pieces[0].shape[0]
    for m, piece in enumerate(pieces):
        place = lax.axis_index("tok") ^ m
        out_ref[pl.ds(pl.multiple_of(place * rows, rows), rows)] = piece[...]


def hidden_kernel(mine_ref, other_ref, gate_ref, up_ref, route_ref, out_ref):
    tokens, width = mine_ref.shape
    gate, upward = [
        sum(
            dot_f32(ref[:, pl.ds(pl.multiple_of(half * width, width), width)], block[...], TRANSPOSED)
            for half, block in ((core(), mine_ref), (1 - core(), other_ref))
        )
        for ref in (gate_ref, up_ref)
    ]
    depth = gate.shape[0]
    out_ref[:depth] = (gate / (1.0 + jnp.exp(-gate)) * upward).astype(bf16)
    route = route_ref[...]
    high = route.astype(bf16).astype(f32)
    middle = (route - high).astype(bf16).astype(f32)
    low = route - high - middle
    part = route.shape[1]
    row = lax.broadcasted_iota(jnp.int32, (TILE, part), 0)
    terms = jnp.where(row == 0, high, jnp.where(row == 1, middle, jnp.where(row == 2, low, 0.0)))
    terms = jnp.concatenate([terms, jnp.zeros((TILE, tokens - part), f32)], 1)
    out_ref[depth:] = terms.astype(bf16)


def features_kernel(*refs):
    hidden_refs, down_refs = refs[:HOLDERS], refs[HOLDERS : 2 * HOLDERS]
    block_refs, centered_ref = refs[2 * HOLDERS : 3 * HOLDERS], refs[3 * HOLDERS]
    route_ref, features_ref = refs[3 * HOLDERS + 1 :]
    depth, tokens = down_refs[0].shape[0], hidden_refs[0].shape[1]
    part = tokens // HOLDERS
    eye = lax.broadcasted_iota(jnp.int32, (part, part), 0) == lax.broadcasted_iota(
        jnp.int32, (part, part), 1
    )
    output = None
    for m, (hidden_ref, down_ref) in enumerate(zip(hidden_refs, down_refs)):
        product = dot_f32(hidden_ref[:depth], down_ref[...], (((0,), (0,)), ((), ())))
        output = product if output is None else output + product
        terms = hidden_ref[depth:, :part].astype(f32)
        route = jnp.sum(terms[:HOLDERS], axis=0, keepdims=True)
        column = jnp.sum(jnp.where(eye, route, 0.0), axis=1, keepdims=True)
        place = pl.multiple_of((holder() ^ m) * part, part)
        route_ref[pl.ds(place, part)] = jnp.broadcast_to(column, (part, LANES))
    features = (output * route_ref[:, :1]).astype(bf16)
    features_ref[...] = features
    wide = features.astype(f32)
    mean = jnp.sum(wide, axis=0, keepdims=True) / tokens
    column = jnp.sum(wide * mean, axis=1, keepdims=True)
    row = jnp.transpose(jnp.broadcast_to(column, (tokens, LANES)))[:1]
    gram = dot_f32(features, features, TRANSPOSED)
    centered = (gram - column - row + jnp.sum(mean * mean)).astype(bf16)
    at = 0
    for i in range(tokens // TILE):
        for j in range(tokens // LANES):
            centered_ref[at * TILE : (at + 1) * TILE] = centered[
                i * TILE : (i + 1) * TILE, j * LANES : (j + 1) * LANES
            ]
            at += 1
    for m, block_ref in enumerate(block_refs):
        block_ref[...] = features_ref[pl.ds(pl.multiple_of((holder() ^ m) * part, part), part)]


def place_kernel(*refs):
    blocks, out_ref, sems = refs[:HOLDERS], refs[HOLDERS], refs[HOLDERS + 1]
    width = blocks[0].shape[1]
    copies = []
    for m, block in enumerate(blocks):
        columns = pl.ds(pl.multiple_of((holder() ^ m) * width, width), width)
        copies.append(pltpu.make_async_copy(block, out_ref.at[:, columns], sems.at[m]))
        copies[-1].start()
    for copy in copies:
        copy.wait()


def pair_kernel(parts_ref, out_ref, flat_ref):
    copies, experts, _ = out_ref.shape
    parts = parts_ref[...].astype(f32)
    total = parts[:, 0]
    for holder in range(1, parts.shape[1]):
        total = total + parts[:, holder]
    flat_ref[...] = total.astype(bf16).astype(f32)
    lane = lax.broadcasted_iota(jnp.int32, (experts, experts), 1)

    def one(expert, table):
        products = jnp.sum(flat_ref[...] * flat_ref[pl.ds(expert, 1)], axis=1)
        return jnp.where(lane == expert, jnp.sum(products, axis=1, keepdims=True), table)

    table = lax.fori_loop(0, experts, one, jnp.zeros((experts, experts), f32), unroll=experts <= 8)
    for copy in range(copies):
        out_ref[copy] = table


def cka_kernel(tables_ref, out_ref):
    totals = jnp.sum(tables_ref[...], axis=0)
    shape = totals.shape
    eye = lax.broadcasted_iota(jnp.int32, shape, 0) == lax.broadcasted_iota(jnp.int32, shape, 1)
    kept = jnp.where(eye, totals, 0.0)
    down = jnp.sum(kept, axis=1, keepdims=True)
    across = jnp.sum(kept, axis=0, keepdims=True)
    out_ref[...] = totals / jnp.sqrt(down * across)


def shards(probe_states, norm_gain, gate_weight, up_weight, down_weight, route_weight):
    groups, members = lax.axis_size("grp"), lax.axis_size("tok")
    devices = groups * members
    experts = devices // HOLDERS
    rows, model = probe_states.shape
    tokens = rows * members
    depth = gate_weight.shape[0]
    part, token_part = model // HOLDERS, tokens // HOLDERS

    own, down_own, down_x, down_z, down_xz = call(
        first_kernel,
        [jax.ShapeDtypeStruct((rows, model // 2), bf16)]
        + [jax.ShapeDtypeStruct((depth, part), bf16)] * HOLDERS,
        [HBM] * 3,
        [
            pltpu.with_memory_space_constraint(a, pltpu.HBM)
            for a in (probe_states, norm_gain[None, :], down_weight)
        ],
        scratch=[
            pltpu.VMEM((rows, model), bf16),
            pltpu.VMEM((1, model), f32),
            pltpu.SemaphoreType.DMA((2 + HOLDERS,)),
        ],
    )
    pieces = {0: own}
    for m in range(members - 2, 0, -2):
        pieces[m] = swapped(own, "tok", m)
    for m in range(0, members, 2):
        pieces[m + 1] = swapped(pieces[m], "tok", 1)
    down_x = swapped(down_x, "tok", 1)
    mine = call(
        stack_kernel,
        jax.ShapeDtypeStruct((tokens, model // 2), bf16),
        [ANY] + [VMEM] * members,
        (down_x, *[pieces[m] for m in range(members)]),
    )
    other = swapped(mine, "grp", 1)
    (down_z,) = held((down_z,), pieces[2])
    (down_xz,) = held((down_xz,), mine)
    downs = [down_own, down_x, swapped(down_z, "tok", 2), swapped(down_xz, "tok", 3)]

    hidden = call(
        hidden_kernel,
        jax.ShapeDtypeStruct((depth + TILE, tokens), bf16),
        [VMEM] * 5,
        (mine, other, gate_weight, up_weight, route_weight),
    )
    hiddens = [swapped(hidden, "tok", m) if m else hidden for m in range(HOLDERS)]
    entries = tokens * tokens // LANES
    *blocks, centered = call(
        features_kernel,
        [jax.ShapeDtypeStruct((token_part, part), bf16)] * HOLDERS
        + [jax.ShapeDtypeStruct((entries, LANES), bf16)],
        [VMEM] * (2 * HOLDERS),
        (*hiddens, *downs),
        scratch=[pltpu.VMEM((tokens, LANES), f32), pltpu.VMEM((tokens, part), bf16)],
    )
    arrived = lax.all_to_all(centered, ("grp", "tok"), split_axis=0, concat_axis=0, tiled=True)
    arrived = arrived.reshape(experts, HOLDERS, entries // devices, LANES)
    direct = devices * experts * experts <= 1 << 16
    tables = call(
        pair_kernel,
        jax.ShapeDtypeStruct((devices if direct else 1, experts, experts), f32),
        [VMEM],
        (arrived,),
        scratch=[pltpu.VMEM((experts, entries // devices, LANES), f32)],
    )
    if direct:
        tables = lax.all_to_all(tables, ("grp", "tok"), split_axis=0, concat_axis=0, tiled=True)
    else:
        tables = lax.psum(tables, ("grp", "tok"))
    cka = call(cka_kernel, jax.ShapeDtypeStruct((experts, experts), f32), [VMEM], (tables,))

    blocks = [swapped(b, "tok", m) if m else b for m, b in enumerate(blocks)]
    features = call(
        place_kernel,
        jax.ShapeDtypeStruct((token_part, model), bf16),
        [VMEM] * HOLDERS,
        blocks,
        out_specs=ANY,
        scratch=[pltpu.SemaphoreType.DMA((HOLDERS,))],
    )
    return (features, cka)


def solution(mesh):
    return jax.shard_map(
        shards,
        mesh=mesh,
        in_specs=(
            P("tok", None),
            P(),
            P(("grp", "tok"), None),
            P(("grp", "tok"), None),
            P(("grp", "tok"), None),
            P(("grp", "tok"), None),
        ),
        out_specs=(P(("grp", "tok"), None), P()),
        check_vma=False,
    )
```

time: 64.6 us -> 61.4 us (0.950)
  waiting for transfers between devices: 23.1 us -> 27.5 us
  Pallas kernels: 8.77 us -> 5.94 us
  local copies, waits for them, and re-layouts: 2.8 us -> 0.01 us
  starting transfers between devices: 28.8 us -> 26.9 us
    ppermute x18 -> x17, waiting for transfers between devices: 12.5 us -> 16.4 us  [swapped(): lax.ppermute(array, axis, [(i, i ^ mask) for i in range(lax.axis_size(axi...]
    pallas_call x9, Pallas kernels: 8.77 us -> 5.94 us  [call(): pl.pallas_call(body, out_shape=outs, in_specs=in_specs, out_specs=jax.tre...]
    unnamed x12 -> x6, local copies, waits for them, and re-layouts: 2.8 us -> 0.01 us
    ppermute x18 -> x17, starting transfers between devices: 22.1 us -> 19.8 us  [swapped(): lax.ppermute(array, axis, [(i, i ^ mask) for i in range(lax.axis_size(axi...]
  transfers between devices with their start and end apart: 20 -> 19, of which waited for: 10 -> 12; matrix products, arithmetic and copies ran while one was open for 0% -> 0% of each run, Pallas kernels for 8% -> 4%
where the time goes in v3:
time: 61.4 us; the launch traced here: 61.1 us
  waiting for transfers between devices  27.5 us (45%)
  starting transfers between devices  26.9 us (44%)
  Pallas kernels  5.94 us (10%)
  between operations  0.75 us (1%)
    ppermute x17, starting transfers between devices, swapped(): lax.ppermute(array, axis, [(i, i ^ mask) for i in range(lax.axis_size(axi...  19.8 us
    ppermute x17, waiting for transfers between devices, swapped(): lax.ppermute(array, axis, [(i, i ^ mask) for i in range(lax.axis_size(axi...  16.4 us
    all_to_all x1, waiting for transfers between devices, shards(): lax.all_to_all(tables, ('grp', 'tok'), split_axis=0, concat_axis=0, tiled...  6.96 us
    pallas_call x9, Pallas kernels, call(): pl.pallas_call(body, out_shape=outs, in_specs=in_specs, out_specs=jax.tre...  5.94 us
    all_to_all x1, starting transfers between devices, shards(): lax.all_to_all(centered, ('grp', 'tok'), split_axis=0, concat_axis=0, til...  4.49 us
    all_to_all x1, waiting for transfers between devices, shards(): lax.all_to_all(centered, ('grp', 'tok'), split_axis=0, concat_axis=0, til...  4.19 us
    all_to_all x1, starting transfers between devices, shards(): lax.all_to_all(tables, ('grp', 'tok'), split_axis=0, concat_axis=0, tiled...  2.57 us
  transfers between devices with their start and end apart: 19, of which 12 were waited for; matrix products, arithmetic and copies ran while one was open for 0% of the time, Pallas kernels for 4%

profile of v3, /device:TPU:0, one launch (start us, length us, event | category | flops | bytes accessed | tf_op | source)
XLA Modules:
  0.0 61.1 jit_solution(16956951167559469337)
XLA Ops:
  0.6 1.3 %shard_map.77 = (bf16[32,1024]{1,0:T(8,128)(2,1)S(1)}, bf16[192,512]{1,0:T(8,128)(2,1)S(1)}, bf16[192,512]{1,0:T(8,128)(2,1)S(1)}, bf16[192,512]{1,0:T(8,128)(2,1)S(1)}, bf16[192,512]{1,0:T(8,128)(2,1)S(1)}) custom-call(bf16[32,2048]{1,0:T(8,128)(2,1)} %states_hbm.1, f32[1,2048]{1,0:T(1,128)} %bitcast.4, bf16[192,2048]{1,0:T(8,128)(2,1)} %down_hbm.1), custom_call_target="tpu_custom_call" | custom-call | tf_op jit(solution)/shard_map/pallas_call | solution.py:29
  2.0 3.0 %collective-permute-start = (bf16[192,512]{1,0:T(8,128)(2,1)S(1)}, bf16[192,512]{1,0:T(8,128)(2,1)S(1)}, u32[]{:S(2)}, u32[]{:S(2)}) collective-permute-start(bf16[192,512]{1,0:T(8,128)(2,1)S(1)} %get-tuple-element.12), channel_id=1, source_target_pairs={{0,1},{1,0},{2,3},{3,2},{4,5},{5,4},{6,7},{7,6},{8,9},{9,8},{10,11... | collective-permute-start | bytes 589832 | tf_op jit(solution)/shard_map/ppermute | solution.py:21
  5.0 3.6 %collective-permute-start.6 = (bf16[32,1024]{1,0:T(8,128)(2,1)S(1)}, bf16[32,1024]{1,0:T(8,128)(2,1)S(1)}, u32[]{:S(2)}, u32[]{:S(2)}) collective-permute-start(bf16[32,1024]{1,0:T(8,128)(2,1)S(1)} %get-tuple-element.13.refs_1_), channel_id=1, source_target_pairs={{0,6},{1,7},{2,4},{3,5},{4,2},{5,3},{6,0},{7,1},{8,14},{9,15},{10,... | collective-permute-start | bytes 196616 | tf_op jit(solution)/shard_map/ppermute | solution.py:21
  8.6 0.0 collective-permute-start.4
  8.6 0.8 %collective-permute-start.2 = (bf16[32,1024]{1,0:T(8,128)(2,1)S(1)}, bf16[32,1024]{1,0:T(8,128)(2,1)S(1)}, u32[]{:S(2)}, u32[]{:S(2)}) collective-permute-start(bf16[32,1024]{1,0:T(8,128)(2,1)S(1)} %get-tuple-element.13.refs_1_), channel_id=1, source_target_pairs={{0,2},{1,3},{2,0},{3,1},{4,6},{5,7},{6,4},{7,5},{8,10},{9,11},{10,... | collective-permute-start | bytes 196616 | tf_op jit(solution)/shard_map/ppermute | solution.py:21
  9.4 0.3 collective-permute-start.1
  9.7 2.1 %collective-permute-done.6.refs_7_ = bf16[32,1024]{1,0:T(8,128)(2,1)S(1)} collective-permute-done((bf16[32,1024]{1,0:T(8,128)(2,1)S(1)}, bf16[32,1024]{1,0:T(8,128)(2,1)S(1)}, u32[]{:S(2)}, u32[]{:S(2)}) %collective-permute-start.6) | collective-permute-done | bytes 65568 | tf_op jit(solution)/shard_map/ppermute | solution.py:21
  11.8 0.0 collective-permute-start.7
  11.9 2.1 %collective-permute-done.4.refs_5_ = bf16[32,1024]{1,0:T(8,128)(2,1)S(1)} collective-permute-done((bf16[32,1024]{1,0:T(8,128)(2,1)S(1)}, bf16[32,1024]{1,0:T(8,128)(2,1)S(1)}, u32[]{:S(2)}, u32[]{:S(2)}) %collective-permute-start.4) | collective-permute-done | bytes 65568 | tf_op jit(solution)/shard_map/ppermute | solution.py:21
  13.9 0.5 collective-permute-start.5
  14.4 0.0 collective-permute-done.2.refs_3_.refs_1_
  14.4 1.5 %collective-permute-start.3 = (bf16[32,1024]{1,0:T(8,128)(2,1)S(1)}, bf16[32,1024]{1,0:T(8,128)(2,1)S(1)}, u32[]{:S(2)}, u32[]{:S(2)}) collective-permute-start(bf16[32,1024]{1,0:T(8,128)(2,1)S(1)} %collective-permute-done.2.refs_3_.refs_1_), channel_id=1, source_target_pairs={{0,1},{1,0},{2,3},{3,2},{4,5},{5,4},{6,7},{7,6},{8,9},{9,8},{10,11... | collective-permute-start | bytes 196616 | tf_op jit(solution)/shard_map/ppermute | solution.py:21
  16.0 0.0 collective-permute-done.1.refs_2_
  16.0 0.3 collective-permute-done.7.refs_8_
  16.3 1.9 %collective-permute-done.5.refs_6_ = bf16[32,1024]{1,0:T(8,128)(2,1)S(1)} collective-permute-done((bf16[32,1024]{1,0:T(8,128)(2,1)S(1)}, bf16[32,1024]{1,0:T(8,128)(2,1)S(1)}, u32[]{:S(2)}, u32[]{:S(2)}) %collective-permute-start.5) | collective-permute-done | bytes 65568 | tf_op jit(solution)/shard_map/ppermute | solution.py:21
  18.2 0.7 %collective-permute-done.3.refs_4_ = bf16[32,1024]{1,0:T(8,128)(2,1)S(1)} collective-permute-done((bf16[32,1024]{1,0:T(8,128)(2,1)S(1)}, bf16[32,1024]{1,0:T(8,128)(2,1)S(1)}, u32[]{:S(2)}, u32[]{:S(2)}) %collective-permute-start.3) | collective-permute-done | bytes 65568 | tf_op jit(solution)/shard_map/ppermute | solution.py:21
  18.9 0.0 collective-permute-done.refs_0_.refs_5_
  18.9 0.0 copy-start.1
  19.0 0.0 copy-start
  19.0 0.1 collective-permute-start.8
  19.1 0.4 collective-permute-start.12
  19.5 0.0 copy-start.2
  19.5 2.5 %collective-permute-start.13 = (bf16[192,512]{1,0:T(8,128)(2,1)S(1)}, bf16[192,512]{1,0:T(8,128)(2,1)S(1)}, u32[]{:S(2)}, u32[]{:S(2)}) collective-permute-start(bf16[192,512]{1,0:T(8,128)(2,1)S(1)} %shard_map.81), channel_id=1, source_target_pairs={{0,3},{1,2},{2,1},{3,0},{4,7},{5,6},{6,5},{7,4},{8,11},{9,10},{10,... | collective-permute-start | bytes 589832 | tf_op jit(solution)/shard_map/ppermute | solution.py:21
  21.9 0.0 collective-permute-done.8.other_ref
  21.9 0.0 copy-done.1
  21.9 0.0 copy-done
  21.9 0.0 copy-done.2
  22.0 0.9 %shard_map.79.refs_0_ = bf16[208,256]{1,0:T(8,128)(2,1)S(1)} custom-call(bf16[256,1024]{1,0:T(8,128)(2,1)S(1)} %shard_map.78.mine_ref.refs_1_, bf16[256,1024]{1,0:T(8,128)(2,1)S(1)} %collective-permute-done.8.other_ref, bf16[192,2048]{1,0:T(8,128)(2,1)S(1)} %copy-done, bf16[192,2048]{1,0:T(8,128)(2,1)S(1)} %copy-done.1, f32[1,64]{1,0:T(1,128)S(1)} %copy-done.2), custom_call_target="tpu_custom_call" | custom-call | tf_op jit(solution)/shard_map/pallas_call | solution.py:29
  22.8 0.7 %collective-permute-start.11 = (bf16[208,256]{1,0:T(8,128)(2,1)S(1)}, bf16[208,256]{1,0:T(8,128)(2,1)S(1)}, u32[]{:S(2)}, u32[]{:S(2)}) collective-permute-start(bf16[208,256]{1,0:T(8,128)(2,1)S(1)} %shard_map.79.refs_0_), channel_id=1, source_target_pairs={{0,3},{1,2},{2,1},{3,0},{4,7},{5,6},{6,5},{7,4},{8,11},{9,10},{10,... | collective-permute-start | bytes 319496 | tf_op jit(solution)/shard_map/ppermute | solution.py:21
  23.5 1.5 %collective-permute-start.10 = (bf16[208,256]{1,0:T(8,128)(2,1)S(1)}, bf16[208,256]{1,0:T(8,128)(2,1)S(1)}, u32[]{:S(2)}, u32[]{:S(2)}) collective-permute-start(bf16[208,256]{1,0:T(8,128)(2,1)S(1)} %shard_map.79.refs_0_), channel_id=1, source_target_pairs={{0,2},{1,3},{2,0},{3,1},{4,6},{5,7},{6,4},{7,5},{8,10},{9,11},{10,... | collective-permute-start | bytes 319496 | tf_op jit(solution)/shard_map/ppermute | solution.py:21
  25.1 1.3 %collective-permute-start.9 = (bf16[208,256]{1,0:T(8,128)(2,1)S(1)}, bf16[208,256]{1,0:T(8,128)(2,1)S(1)}, u32[]{:S(2)}, u32[]{:S(2)}) collective-permute-start(bf16[208,256]{1,0:T(8,128)(2,1)S(1)} %shard_map.79.refs_0_), channel_id=1, source_target_pairs={{0,1},{1,0},{2,3},{3,2},{4,5},{5,4},{6,7},{7,6},{8,9},{9,8},{10,11... | collective-permute-start | bytes 319496 | tf_op jit(solution)/shard_map/ppermute | solution.py:21
  26.4 0.5 collective-permute-done.12.refs_6_
  26.8 5.1 %collective-permute-done.13.refs_7_ = bf16[192,512]{1,0:T(8,128)(2,1)S(1)} collective-permute-done((bf16[192,512]{1,0:T(8,128)(2,1)S(1)}, bf16[192,512]{1,0:T(8,128)(2,1)S(1)}, u32[]{:S(2)}, u32[]{:S(2)}) %collective-permute-start.13) | collective-permute-done | bytes 196640 | tf_op jit(solution)/shard_map/ppermute | solution.py:21
  31.9 2.2 %collective-permute-done.11.refs_3_ = bf16[208,256]{1,0:T(8,128)(2,1)S(1)} collective-permute-done((bf16[208,256]{1,0:T(8,128)(2,1)S(1)}, bf16[208,256]{1,0:T(8,128)(2,1)S(1)}, u32[]{:S(2)}, u32[]{:S(2)}) %collective-permute-start.11) | collective-permute-done | bytes 106528 | tf_op jit(solution)/shard_map/ppermute | solution.py:21
  34.2 1.0 %collective-permute-done.10.refs_2_ = bf16[208,256]{1,0:T(8,128)(2,1)S(1)} collective-permute-done((bf16[208,256]{1,0:T(8,128)(2,1)S(1)}, bf16[208,256]{1,0:T(8,128)(2,1)S(1)}, u32[]{:S(2)}, u32[]{:S(2)}) %collective-permute-start.10) | collective-permute-done | bytes 106528 | tf_op jit(solution)/shard_map/ppermute | solution.py:21
  35.2 0.4 collective-permute-done.9.refs_1_
  35.6 1.4 %shard_map.82 = (bf16[64,512]{1,0:T(8,128)(2,1)S(1)}, bf16[64,512]{1,0:T(8,128)(2,1)S(1)}, bf16[64,512]{1,0:T(8,128)(2,1)S(1)}, bf16[64,512]{1,0:T(8,128)(2,1)S(1)}, bf16[512,128]{1,0:T(8,128)(2,1)}) custom-call(bf16[208,256]{1,0:T(8,128)(2,1)S(1)} %shard_map.79.refs_0_, bf16[208,256]{1,0:T(8,128)(2,1)S(1)} %collective-permute-done.9.refs_1_, ...), custom_call_target="tpu_custom_call" | custom-call | tf_op jit(solution)/shard_map/pallas_call | solution.py:29
  37.0 4.5 %all-to-all-start = ((bf16[32,16,128]{2,1,0:T(8,128)(2,1)}), bf16[32,16,128]{2,1,0:T(8,128)(2,1)S(1)}, u32[]{:S(2)}, u32[]{:S(2)}) async-start(bf16[32,16,128]{2,1,0:T(8,128)(2,1)} %bitcast.1), calls=%async_computation | async-start | bytes 262144 | tf_op jit(solution)/shard_map/all_to_all | solution.py:251
  41.5 1.8 %collective-permute-start.14 = (bf16[64,512]{1,0:T(8,128)(2,1)S(1)}, bf16[64,512]{1,0:T(8,128)(2,1)S(1)}, u32[]{:S(2)}, u32[]{:S(2)}) collective-permute-start(bf16[64,512]{1,0:T(8,128)(2,1)S(1)} %get-tuple-element.18), channel_id=1, source_target_pairs={{0,1},{1,0},{2,3},{3,2},{4,5},{5,4},{6,7},{7,6},{8,9},{9,8},{10,11... | collective-permute-start | bytes 196616 | tf_op jit(solution)/shard_map/ppermute | solution.py:21
  43.4 1.5 %collective-permute-start.15 = (bf16[64,512]{1,0:T(8,128)(2,1)S(1)}, bf16[64,512]{1,0:T(8,128)(2,1)S(1)}, u32[]{:S(2)}, u32[]{:S(2)}) collective-permute-start(bf16[64,512]{1,0:T(8,128)(2,1)S(1)} %get-tuple-element.19), channel_id=1, source_target_pairs={{0,2},{1,3},{2,0},{3,1},{4,6},{5,7},{6,4},{7,5},{8,10},{9,11},{10,... | collective-permute-start | bytes 196616 | tf_op jit(solution)/shard_map/ppermute | solution.py:21
  44.8 0.3 collective-permute-start.16
  45.1 4.2 %all-to-all-done = bf16[32,16,128]{2,1,0:T(8,128)(2,1)S(1)} async-done(((bf16[32,16,128]{2,1,0:T(8,128)(2,1)}), bf16[32,16,128]{2,1,0:T(8,128)(2,1)S(1)}, u32[]{:S(2)}, u32[]{:S(2)}) %all-to-all-start) | async-done | bytes 131104 | tf_op jit(solution)/shard_map/all_to_all | solution.py:251
  49.3 0.8 %shard_map.84 = f32[32,8,8]{2,1,0:T(8,128)} custom-call(bf16[8,4,16,128]{3,2,1,0:T(8,128)(2,1)S(1)} %bitcast.3), custom_call_target="tpu_custom_call" | custom-call | tf_op jit(solution)/shard_map/pallas_call | solution.py:29
  50.1 2.6 %all-to-all-start.1 = ((f32[32,8,8]{2,1,0:T(8,128)}), f32[32,8,8]{2,1,0:T(8,128)S(1)}, u32[]{:S(2)}, u32[]{:S(2)}) async-start(f32[32,8,8]{2,1,0:T(8,128)} %shard_map.84), calls=%async_computation.1 | async-start | bytes 262144 | tf_op jit(solution)/shard_map/all_to_all | solution.py:262
  52.7 0.0 collective-permute-done.14.refs_1_
  52.7 0.0 collective-permute-done.15.refs_2_
  52.7 0.0 collective-permute-done.16.refs_3_
  52.7 0.7 %shard_map.83 = bf16[64,2048]{1,0:T(8,128)(2,1)} custom-call(bf16[64,512]{1,0:T(8,128)(2,1)S(1)} %get-tuple-element.17.refs_0_, bf16[64,512]{1,0:T(8,128)(2,1)S(1)} %collective-permute-done.14.refs_1_, bf16[64,512]{1,0:T(8,128)(2,1)S(1)} %collective-permute-done.15.refs_2_, bf16[64,512]{1,0:T(8,128)(2,1)S(1)} %collective-permute-done.16.refs_3_), custom_call_target="tpu_custom_call" | custom-call | tf_op jit(solution)/shard_map/pallas_call | solution.py:29
  53.4 7.0 %all-to-all-done.1.tables_ref = f32[32,8,8]{2,1,0:T(8,128)S(1)} async-done(((f32[32,8,8]{2,1,0:T(8,128)}), f32[32,8,8]{2,1,0:T(8,128)S(1)}, u32[]{:S(2)}, u32[]{:S(2)}) %all-to-all-start.1) | async-done | bytes 8224 | tf_op jit(solution)/shard_map/all_to_all | solution.py:262
  60.4 0.7 %shard_map.85 = f32[8,8]{1,0:T(8,128)} custom-call(f32[32,8,8]{2,1,0:T(8,128)S(1)} %all-to-all-done.1.tables_ref), custom_call_target="tpu_custom_call" | custom-call | tf_op jit(solution)/shard_map/pallas_call | solution.py:29
  (3 shorter events, 0.1 us)
Async XLA Ops:
  2.0 17.0 %collective-permute-start = (bf16[192,512]{1,0:T(8,128)(2,1)S(1)}, bf16[192,512]{1,0:T(8,128)(2,1)S(1)}, u32[]{:S(2)}, u32[]{:S(2)}) collective-permute-start(bf16[192,512]{1,0:T(8,128)(2,1)S(1)} %get-tuple-element.12), channel_id=1, source_target_pairs={{0,1},{1,0},{2,3},{3,2},{4,5},{5,4},{6,7},{7,6},{8,9},{9,8},{10,11... | collective-permute-start | bytes 589832 | tf_op jit(solution)/shard_map/ppermute | solution.py:21
  5.0 6.9 %collective-permute-start.6 = (bf16[32,1024]{1,0:T(8,128)(2,1)S(1)}, bf16[32,1024]{1,0:T(8,128)(2,1)S(1)}, u32[]{:S(2)}, u32[]{:S(2)}) collective-permute-start(bf16[32,1024]{1,0:T(8,128)(2,1)S(1)} %get-tuple-element.13.refs_1_), channel_id=1, source_target_pairs={{0,6},{1,7},{2,4},{3,5},{4,2},{5,3},{6,0},{7,1},{8,14},{9,15},{10,... | collective-permute-start | bytes 196616 | tf_op jit(solution)/shard_map/ppermute | solution.py:21
  8.6 5.4 %collective-permute-start.4 = (bf16[32,1024]{1,0:T(8,128)(2,1)S(1)}, bf16[32,1024]{1,0:T(8,128)(2,1)S(1)}, u32[]{:S(2)}, u32[]{:S(2)}) collective-permute-start(bf16[32,1024]{1,0:T(8,128)(2,1)S(1)} %get-tuple-element.13.refs_1_), channel_id=1, source_target_pairs={{0,4},{1,5},{2,6},{3,7},{4,0},{5,1},{6,2},{7,3},{8,12},{9,13},{10,... | collective-permute-start | bytes 196616 | tf_op jit(solution)/shard_map/ppermute | solution.py:21
  8.6 5.9 %collective-permute-start.2 = (bf16[32,1024]{1,0:T(8,128)(2,1)S(1)}, bf16[32,1024]{1,0:T(8,128)(2,1)S(1)}, u32[]{:S(2)}, u32[]{:S(2)}) collective-permute-start(bf16[32,1024]{1,0:T(8,128)(2,1)S(1)} %get-tuple-element.13.refs_1_), channel_id=1, source_target_pairs={{0,2},{1,3},{2,0},{3,1},{4,6},{5,7},{6,4},{7,5},{8,10},{9,11},{10,... | collective-permute-start | bytes 196616 | tf_op jit(solution)/shard_map/ppermute | solution.py:21
  9.4 6.6 %collective-permute-start.1 = (bf16[32,1024]{1,0:T(8,128)(2,1)S(1)}, bf16[32,1024]{1,0:T(8,128)(2,1)S(1)}, u32[]{:S(2)}, u32[]{:S(2)}) collective-permute-start(bf16[32,1024]{1,0:T(8,128)(2,1)S(1)} %get-tuple-element.13.refs_1_), channel_id=1, source_target_pairs={{0,1},{1,0},{2,3},{3,2},{4,5},{5,4},{6,7},{7,6},{8,9},{9,8},{10,11... | collective-permute-start | bytes 196616 | tf_op jit(solution)/shard_map/ppermute | solution.py:21
  11.8 4.4 %collective-permute-start.7 = (bf16[32,1024]{1,0:T(8,128)(2,1)S(1)}, bf16[32,1024]{1,0:T(8,128)(2,1)S(1)}, u32[]{:S(2)}, u32[]{:S(2)}) collective-permute-start(bf16[32,1024]{1,0:T(8,128)(2,1)S(1)} %collective-permute-done.6.refs_7_), channel_id=1, source_target_pairs={{0,1},{1,0},{2,3},{3,2},{4,5},{5,4},{6,7},{7,6},{8,9},{9,8},{10,11... | collective-permute-start | bytes 196616 | tf_op jit(solution)/shard_map/ppermute | solution.py:21
  13.9 4.3 %collective-permute-start.5 = (bf16[32,1024]{1,0:T(8,128)(2,1)S(1)}, bf16[32,1024]{1,0:T(8,128)(2,1)S(1)}, u32[]{:S(2)}, u32[]{:S(2)}) collective-permute-start(bf16[32,1024]{1,0:T(8,128)(2,1)S(1)} %collective-permute-done.4.refs_5_), channel_id=1, source_target_pairs={{0,1},{1,0},{2,3},{3,2},{4,5},{5,4},{6,7},{7,6},{8,9},{9,8},{10,11... | collective-permute-start | bytes 196616 | tf_op jit(solution)/shard_map/ppermute | solution.py:21
  14.4 4.5 %collective-permute-start.3 = (bf16[32,1024]{1,0:T(8,128)(2,1)S(1)}, bf16[32,1024]{1,0:T(8,128)(2,1)S(1)}, u32[]{:S(2)}, u32[]{:S(2)}) collective-permute-start(bf16[32,1024]{1,0:T(8,128)(2,1)S(1)} %collective-permute-done.2.refs_3_.refs_1_), channel_id=1, source_target_pairs={{0,1},{1,0},{2,3},{3,2},{4,5},{5,4},{6,7},{7,6},{8,9},{9,8},{10,11... | collective-permute-start | bytes 196616 | tf_op jit(solution)/shard_map/ppermute | solution.py:21
  18.9 3.0 %copy-start.1 = (bf16[192,2048]{1,0:T(8,128)(2,1)S(1)}, bf16[192,2048]{1,0:T(8,128)(2,1)}, u32[]{:S(2)}) copy-start(bf16[192,2048]{1,0:T(8,128)(2,1)} %up_ref.1) | copy-start | bytes 2359300
  19.0 3.0 %copy-start = (bf16[192,2048]{1,0:T(8,128)(2,1)S(1)}, bf16[192,2048]{1,0:T(8,128)(2,1)}, u32[]{:S(2)}) copy-start(bf16[192,2048]{1,0:T(8,128)(2,1)} %gate_ref.1) | copy-start | bytes 2359300
  19.0 3.0 %collective-permute-start.8 = (bf16[256,1024]{1,0:T(8,128)(2,1)S(1)}, bf16[256,1024]{1,0:T(8,128)(2,1)S(1)}, u32[]{:S(2)}, u32[]{:S(2)}) collective-permute-start(bf16[256,1024]{1,0:T(8,128)(2,1)S(1)} %shard_map.78.mine_ref.refs_1_), channel_id=1, source_target_pairs={{0,8},{8,0},{16,24},{24,16},{1,9},{9,1},{17,25},{25,17},{2,10},{10... | collective-permute-start | bytes 1572872 | tf_op jit(solution)/shard_map/ppermute | solution.py:21
  19.1 7.8 %collective-permute-start.12 = (bf16[192,512]{1,0:T(8,128)(2,1)S(1)}, bf16[192,512]{1,0:T(8,128)(2,1)S(1)}, u32[]{:S(2)}, u32[]{:S(2)}) collective-permute-start(bf16[192,512]{1,0:T(8,128)(2,1)S(1)} %shard_map.80), channel_id=1, source_target_pairs={{0,2},{1,3},{2,0},{3,1},{4,6},{5,7},{6,4},{7,5},{8,10},{9,11},{10,... | collective-permute-start | bytes 589832 | tf_op jit(solution)/shard_map/ppermute | solution.py:21
  19.5 2.5 %copy-start.2 = (f32[1,64]{1,0:T(1,128)S(1)}, f32[1,64]{1,0:T(1,128)}, u32[]{:S(2)}) copy-start(f32[1,64]{1,0:T(1,128)} %route_ref.1) | copy-start | bytes 772
  19.5 12.5 %collective-permute-start.13 = (bf16[192,512]{1,0:T(8,128)(2,1)S(1)}, bf16[192,512]{1,0:T(8,128)(2,1)S(1)}, u32[]{:S(2)}, u32[]{:S(2)}) collective-permute-start(bf16[192,512]{1,0:T(8,128)(2,1)S(1)} %shard_map.81), channel_id=1, source_target_pairs={{0,3},{1,2},{2,1},{3,0},{4,7},{5,6},{6,5},{7,4},{8,11},{9,10},{10,... | collective-permute-start | bytes 589832 | tf_op jit(solution)/shard_map/ppermute | solution.py:21
  22.8 11.3 %collective-permute-start.11 = (bf16[208,256]{1,0:T(8,128)(2,1)S(1)}, bf16[208,256]{1,0:T(8,128)(2,1)S(1)}, u32[]{:S(2)}, u32[]{:S(2)}) collective-permute-start(bf16[208,256]{1,0:T(8,128)(2,1)S(1)} %shard_map.79.refs_0_), channel_id=1, source_target_pairs={{0,3},{1,2},{2,1},{3,0},{4,7},{5,6},{6,5},{7,4},{8,11},{9,10},{10,... | collective-permute-start | bytes 319496 | tf_op jit(solution)/shard_map/ppermute | solution.py:21
  23.5 11.7 %collective-permute-start.10 = (bf16[208,256]{1,0:T(8,128)(2,1)S(1)}, bf16[208,256]{1,0:T(8,128)(2,1)S(1)}, u32[]{:S(2)}, u32[]{:S(2)}) collective-permute-start(bf16[208,256]{1,0:T(8,128)(2,1)S(1)} %shard_map.79.refs_0_), channel_id=1, source_target_pairs={{0,2},{1,3},{2,0},{3,1},{4,6},{5,7},{6,4},{7,5},{8,10},{9,11},{10,... | collective-permute-start | bytes 319496 | tf_op jit(solution)/shard_map/ppermute | solution.py:21
  25.1 10.5 %collective-permute-start.9 = (bf16[208,256]{1,0:T(8,128)(2,1)S(1)}, bf16[208,256]{1,0:T(8,128)(2,1)S(1)}, u32[]{:S(2)}, u32[]{:S(2)}) collective-permute-start(bf16[208,256]{1,0:T(8,128)(2,1)S(1)} %shard_map.79.refs_0_), channel_id=1, source_target_pairs={{0,1},{1,0},{2,3},{3,2},{4,5},{5,4},{6,7},{7,6},{8,9},{9,8},{10,11... | collective-permute-start | bytes 319496 | tf_op jit(solution)/shard_map/ppermute | solution.py:21
  37.0 12.2 %all-to-all-start = ((bf16[32,16,128]{2,1,0:T(8,128)(2,1)}), bf16[32,16,128]{2,1,0:T(8,128)(2,1)S(1)}, u32[]{:S(2)}, u32[]{:S(2)}) async-start(bf16[32,16,128]{2,1,0:T(8,128)(2,1)} %bitcast.1), calls=%async_computation | async-start | bytes 262144 | tf_op jit(solution)/shard_map/all_to_all | solution.py:251
  41.5 11.1 %collective-permute-start.14 = (bf16[64,512]{1,0:T(8,128)(2,1)S(1)}, bf16[64,512]{1,0:T(8,128)(2,1)S(1)}, u32[]{:S(2)}, u32[]{:S(2)}) collective-permute-start(bf16[64,512]{1,0:T(8,128)(2,1)S(1)} %get-tuple-element.18), channel_id=1, source_target_pairs={{0,1},{1,0},{2,3},{3,2},{4,5},{5,4},{6,7},{7,6},{8,9},{9,8},{10,11... | collective-permute-start | bytes 196616 | tf_op jit(solution)/shard_map/ppermute | solution.py:21
  43.4 9.3 %collective-permute-start.15 = (bf16[64,512]{1,0:T(8,128)(2,1)S(1)}, bf16[64,512]{1,0:T(8,128)(2,1)S(1)}, u32[]{:S(2)}, u32[]{:S(2)}) collective-permute-start(bf16[64,512]{1,0:T(8,128)(2,1)S(1)} %get-tuple-element.19), channel_id=1, source_target_pairs={{0,2},{1,3},{2,0},{3,1},{4,6},{5,7},{6,4},{7,5},{8,10},{9,11},{10,... | collective-permute-start | bytes 196616 | tf_op jit(solution)/shard_map/ppermute | solution.py:21
  44.8 7.8 %collective-permute-start.16 = (bf16[64,512]{1,0:T(8,128)(2,1)S(1)}, bf16[64,512]{1,0:T(8,128)(2,1)S(1)}, u32[]{:S(2)}, u32[]{:S(2)}) collective-permute-start(bf16[64,512]{1,0:T(8,128)(2,1)S(1)} %get-tuple-element.20), channel_id=1, source_target_pairs={{0,3},{1,2},{2,1},{3,0},{4,7},{5,6},{6,5},{7,4},{8,11},{9,10},{10,... | collective-permute-start | bytes 196616 | tf_op jit(solution)/shard_map/ppermute | solution.py:21
  50.1 10.3 %all-to-all-start.1 = ((f32[32,8,8]{2,1,0:T(8,128)}), f32[32,8,8]{2,1,0:T(8,128)S(1)}, u32[]{:S(2)}, u32[]{:S(2)}) async-start(f32[32,8,8]{2,1,0:T(8,128)} %shard_map.84), calls=%async_computation.1 | async-start | bytes 262144 | tf_op jit(solution)/shard_map/all_to_all | solution.py:262

commit v4 on v3

--- a/solution.py
+++ b/solution.py
@@ -73,19 +73,19 @@
     pass
 
 
-def held(arrays, after):
+def held(array, after):
     return call(
         hold_kernel,
-        [jax.ShapeDtypeStruct(a.shape, a.dtype) for a in arrays],
-        [ANY] * (len(arrays) + 1),
-        (*arrays, after),
-        out_specs=[ANY] * len(arrays),
-        aliases={i: i for i in range(len(arrays))},
+        jax.ShapeDtypeStruct(array.shape, array.dtype),
+        [ANY] * 2,
+        (array, after),
+        out_specs=ANY,
+        aliases={0: 0},
     )
 
 
 def stack_kernel(*refs):
-    pieces, out_ref = refs[1:-1], refs[-1]
+    pieces, out_ref = refs[2:-1], refs[-1]
     rows = pieces[0].shape[0]
     for m, piece in enumerate(pieces):
         place = lax.axis_index("tok") ^ m
@@ -200,7 +200,7 @@
     depth = gate_weight.shape[0]
     part, token_part = model // HOLDERS, tokens // HOLDERS
 
-    own, down_own, down_x, down_z, down_xz = call(
+    own, *downs = call(
         first_kernel,
         [jax.ShapeDtypeStruct((rows, model // 2), bf16)]
         + [jax.ShapeDtypeStruct((depth, part), bf16)] * HOLDERS,
@@ -220,18 +220,16 @@
         pieces[m] = swapped(own, "tok", m)
     for m in range(0, members, 2):
         pieces[m + 1] = swapped(pieces[m], "tok", 1)
-    down_x = swapped(down_x, "tok", 1)
+    down_x, down_z = swapped(downs[1], "tok", 1), swapped(downs[2], "tok", 2)
     mine = call(
         stack_kernel,
         jax.ShapeDtypeStruct((tokens, model // 2), bf16),
-        [ANY] + [VMEM] * members,
-        (down_x, *[pieces[m] for m in range(members)]),
+        [ANY] * 2 + [VMEM] * members,
+        (down_x, down_z, *[pieces[m] for m in range(members)]),
     )
     other = swapped(mine, "grp", 1)
-    (down_z,) = held((down_z,), pieces[2])
-    (down_xz,) = held((down_xz,), mine)
-    downs = [down_own, down_x, swapped(down_z, "tok", 2), swapped(down_xz, "tok", 3)]
-
+
+    downs = [downs[0], down_x, down_z, swapped(held(downs[3], mine), "tok", 3)]
     hidden = call(
         hidden_kernel,
         jax.ShapeDtypeStruct((depth + TILE, tokens), bf16),

time: 61.4 us -> 60.9 us (level)
  waiting for transfers between devices: 27.5 us -> 25.8 us
  starting transfers between devices: 26.9 us -> 28.1 us
    ppermute x17, waiting for transfers between devices: 16.4 us -> 14.6 us  [swapped(): lax.ppermute(array, axis, [(i, i ^ mask) for i in range(lax.axis_size(axi...]
    ppermute x17, starting transfers between devices: 19.8 us -> 21.5 us  [swapped(): lax.ppermute(array, axis, [(i, i ^ mask) for i in range(lax.axis_size(axi...]
    pallas_call x9 -> x8, Pallas kernels: 5.94 us -> 5.94 us  [call(): pl.pallas_call(body, out_shape=outs, in_specs=in_specs, out_specs=jax.tre...]
where the time goes in v4:
time: 60.9 us; the launch traced here: 60.6 us
  starting transfers between devices  28.1 us (46%)
  waiting for transfers between devices  25.8 us (42%)
  Pallas kernels  5.94 us (10%)
  between operations  0.76 us (1%)
    ppermute x17, starting transfers between devices, swapped(): lax.ppermute(array, axis, [(i, i ^ mask) for i in range(lax.axis_size(axi...  21.5 us
    ppermute x17, waiting for transfers between devices, swapped(): lax.ppermute(array, axis, [(i, i ^ mask) for i in range(lax.axis_size(axi...  14.6 us
    all_to_all x1, waiting for transfers between devices, shards(): lax.all_to_all(tables, ('grp', 'tok'), split_axis=0, concat_axis=0, tiled...  6.96 us
    pallas_call x8, Pallas kernels, call(): pl.pallas_call(body, out_shape=outs, in_specs=in_specs, out_specs=jax.tre...  5.94 us
    all_to_all x1, waiting for transfers between devices, shards(): lax.all_to_all(centered, ('grp', 'tok'), split_axis=0, concat_axis=0, til...  4.19 us
    all_to_all x1, starting transfers between devices, shards(): lax.all_to_all(centered, ('grp', 'tok'), split_axis=0, concat_axis=0, til...  4.03 us
    all_to_all x1, starting transfers between devices, shards(): lax.all_to_all(tables, ('grp', 'tok'), split_axis=0, concat_axis=0, tiled...  2.57 us
  transfers between devices with their start and end apart: 19, of which 12 were waited for; matrix products, arithmetic and copies ran while one was open for 0% of the time, Pallas kernels for 4%

profile of v4, /device:TPU:0, one launch (start us, length us, event | category | flops | bytes accessed | tf_op | source)
XLA Modules:
  0.0 60.6 jit_solution(13725345277450757849)
XLA Ops:
  0.6 1.3 %shard_map.77 = (bf16[32,1024]{1,0:T(8,128)(2,1)S(1)}, bf16[192,512]{1,0:T(8,128)(2,1)S(1)}, bf16[192,512]{1,0:T(8,128)(2,1)S(1)}, bf16[192,512]{1,0:T(8,128)(2,1)S(1)}, bf16[192,512]{1,0:T(8,128)(2,1)S(1)}) custom-call(bf16[32,2048]{1,0:T(8,128)(2,1)} %states_hbm.1, f32[1,2048]{1,0:T(1,128)} %bitcast.4, bf16[192,2048]{1,0:T(8,128)(2,1)} %down_hbm.1), custom_call_target="tpu_custom_call" | custom-call | tf_op jit(solution)/shard_map/pallas_call | solution.py:29
  2.0 5.1 %collective-permute-start.7 = (bf16[32,1024]{1,0:T(8,128)(2,1)S(1)}, bf16[32,1024]{1,0:T(8,128)(2,1)S(1)}, u32[]{:S(2)}, u32[]{:S(2)}) collective-permute-start(bf16[32,1024]{1,0:T(8,128)(2,1)S(1)} %get-tuple-element.14.refs_2_), channel_id=1, source_target_pairs={{0,6},{1,7},{2,4},{3,5},{4,2},{5,3},{6,0},{7,1},{8,14},{9,15},{10,... | collective-permute-start | bytes 196616 | tf_op jit(solution)/shard_map/ppermute | solution.py:21
  7.1 1.5 %collective-permute-start = (bf16[192,512]{1,0:T(8,128)(2,1)S(1)}, bf16[192,512]{1,0:T(8,128)(2,1)S(1)}, u32[]{:S(2)}, u32[]{:S(2)}) collective-permute-start(bf16[192,512]{1,0:T(8,128)(2,1)S(1)} %get-tuple-element.12), channel_id=1, source_target_pairs={{0,1},{1,0},{2,3},{3,2},{4,5},{5,4},{6,7},{7,6},{8,9},{9,8},{10,11... | collective-permute-start | bytes 589832 | tf_op jit(solution)/shard_map/ppermute | solution.py:21
  8.6 0.0 collective-permute-start.1
  8.6 0.8 %collective-permute-start.5 = (bf16[32,1024]{1,0:T(8,128)(2,1)S(1)}, bf16[32,1024]{1,0:T(8,128)(2,1)S(1)}, u32[]{:S(2)}, u32[]{:S(2)}) collective-permute-start(bf16[32,1024]{1,0:T(8,128)(2,1)S(1)} %get-tuple-element.14.refs_2_), channel_id=1, source_target_pairs={{0,4},{1,5},{2,6},{3,7},{4,0},{5,1},{6,2},{7,3},{8,12},{9,13},{10,... | collective-permute-start | bytes 196616 | tf_op jit(solution)/shard_map/ppermute | solution.py:21
  9.4 1.2 %collective-permute-start.3 = (bf16[32,1024]{1,0:T(8,128)(2,1)S(1)}, bf16[32,1024]{1,0:T(8,128)(2,1)S(1)}, u32[]{:S(2)}, u32[]{:S(2)}) collective-permute-start(bf16[32,1024]{1,0:T(8,128)(2,1)S(1)} %get-tuple-element.14.refs_2_), channel_id=1, source_target_pairs={{0,2},{1,3},{2,0},{3,1},{4,6},{5,7},{6,4},{7,5},{8,10},{9,11},{10,... | collective-permute-start | bytes 196616 | tf_op jit(solution)/shard_map/ppermute | solution.py:21
  10.6 0.0 collective-permute-done.7.refs_8_
  10.6 1.1 %collective-permute-start.2 = (bf16[32,1024]{1,0:T(8,128)(2,1)S(1)}, bf16[32,1024]{1,0:T(8,128)(2,1)S(1)}, u32[]{:S(2)}, u32[]{:S(2)}) collective-permute-start(bf16[32,1024]{1,0:T(8,128)(2,1)S(1)} %get-tuple-element.14.refs_2_), channel_id=1, source_target_pairs={{0,1},{1,0},{2,3},{3,2},{4,5},{5,4},{6,7},{7,6},{8,9},{9,8},{10,11... | collective-permute-start | bytes 196616 | tf_op jit(solution)/shard_map/ppermute | solution.py:21
  11.7 3.4 %collective-permute-done.5.refs_6_ = bf16[32,1024]{1,0:T(8,128)(2,1)S(1)} collective-permute-done((bf16[32,1024]{1,0:T(8,128)(2,1)S(1)}, bf16[32,1024]{1,0:T(8,128)(2,1)S(1)}, u32[]{:S(2)}, u32[]{:S(2)}) %collective-permute-start.5) | collective-permute-done | bytes 65568 | tf_op jit(solution)/shard_map/ppermute | solution.py:21
  15.2 1.1 %collective-permute-start.8 = (bf16[32,1024]{1,0:T(8,128)(2,1)S(1)}, bf16[32,1024]{1,0:T(8,128)(2,1)S(1)}, u32[]{:S(2)}, u32[]{:S(2)}) collective-permute-start(bf16[32,1024]{1,0:T(8,128)(2,1)S(1)} %collective-permute-done.7.refs_8_), channel_id=1, source_target_pairs={{0,1},{1,0},{2,3},{3,2},{4,5},{5,4},{6,7},{7,6},{8,9},{9,8},{10,11... | collective-permute-start | bytes 196616 | tf_op jit(solution)/shard_map/ppermute | solution.py:21
  16.2 1.2 %collective-permute-done.3.refs_4_ = bf16[32,1024]{1,0:T(8,128)(2,1)S(1)} collective-permute-done((bf16[32,1024]{1,0:T(8,128)(2,1)S(1)}, bf16[32,1024]{1,0:T(8,128)(2,1)S(1)}, u32[]{:S(2)}, u32[]{:S(2)}) %collective-permute-start.3) | collective-permute-done | bytes 65568 | tf_op jit(solution)/shard_map/ppermute | solution.py:21
  17.5 0.9 %collective-permute-start.6 = (bf16[32,1024]{1,0:T(8,128)(2,1)S(1)}, bf16[32,1024]{1,0:T(8,128)(2,1)S(1)}, u32[]{:S(2)}, u32[]{:S(2)}) collective-permute-start(bf16[32,1024]{1,0:T(8,128)(2,1)S(1)} %collective-permute-done.5.refs_6_), channel_id=1, source_target_pairs={{0,1},{1,0},{2,3},{3,2},{4,5},{5,4},{6,7},{7,6},{8,9},{9,8},{10,11... | collective-permute-start | bytes 196616 | tf_op jit(solution)/shard_map/ppermute | solution.py:21
  18.4 0.0 collective-permute-done.2.refs_3_
  18.4 1.1 %collective-permute-start.4 = (bf16[32,1024]{1,0:T(8,128)(2,1)S(1)}, bf16[32,1024]{1,0:T(8,128)(2,1)S(1)}, u32[]{:S(2)}, u32[]{:S(2)}) collective-permute-start(bf16[32,1024]{1,0:T(8,128)(2,1)S(1)} %collective-permute-done.3.refs_4_), channel_id=1, source_target_pairs={{0,1},{1,0},{2,3},{3,2},{4,5},{5,4},{6,7},{7,6},{8,9},{9,8},{10,11... | collective-permute-start | bytes 196616 | tf_op jit(solution)/shard_map/ppermute | solution.py:21
  19.5 0.4 collective-permute-done.8.refs_9_
  19.9 1.8 %collective-permute-done.6.refs_7_ = bf16[32,1024]{1,0:T(8,128)(2,1)S(1)} collective-permute-done((bf16[32,1024]{1,0:T(8,128)(2,1)S(1)}, bf16[32,1024]{1,0:T(8,128)(2,1)S(1)}, u32[]{:S(2)}, u32[]{:S(2)}) %collective-permute-start.6) | collective-permute-done | bytes 65568 | tf_op jit(solution)/shard_map/ppermute | solution.py:21
  21.7 0.9 %collective-permute-done.4.refs_5_ = bf16[32,1024]{1,0:T(8,128)(2,1)S(1)} collective-permute-done((bf16[32,1024]{1,0:T(8,128)(2,1)S(1)}, bf16[32,1024]{1,0:T(8,128)(2,1)S(1)}, u32[]{:S(2)}, u32[]{:S(2)}) %collective-permute-start.4) | collective-permute-done | bytes 65568 | tf_op jit(solution)/shard_map/ppermute | solution.py:21
  22.6 0.0 collective-permute-done.refs_0_.refs_5_
  22.6 0.0 collective-permute-done.1.refs_1_.refs_6_
  22.7 0.0 copy-start.1
  22.7 0.1 shard_map.78.mine_ref.refs_1_
  22.7 0.0 copy-start
  22.7 0.1 collective-permute-start.9
  22.8 0.0 copy-start.2
  22.8 1.5 %collective-permute-start.13 = (bf16[192,512]{1,0:T(8,128)(2,1)S(1)}, bf16[192,512]{1,0:T(8,128)(2,1)S(1)}, u32[]{:S(2)}, u32[]{:S(2)}) collective-permute-start(bf16[192,512]{1,0:T(8,128)(2,1)S(1)} %shard_map.80), channel_id=1, source_target_pairs={{0,3},{1,2},{2,1},{3,0},{4,7},{5,6},{6,5},{7,4},{8,11},{9,10},{10,... | collective-permute-start | bytes 589832 | tf_op jit(solution)/shard_map/ppermute | solution.py:21
  24.3 0.4 collective-permute-done.9.other_ref
  24.7 0.0 copy-done.1
  24.7 0.0 copy-done
  24.7 0.0 copy-done.2
  24.7 0.9 %shard_map.79.refs_0_ = bf16[208,256]{1,0:T(8,128)(2,1)S(1)} custom-call(bf16[256,1024]{1,0:T(8,128)(2,1)S(1)} %shard_map.78.mine_ref.refs_1_, bf16[256,1024]{1,0:T(8,128)(2,1)S(1)} %collective-permute-done.9.other_ref, bf16[192,2048]{1,0:T(8,128)(2,1)S(1)} %copy-done, bf16[192,2048]{1,0:T(8,128)(2,1)S(1)} %copy-done.1, f32[1,64]{1,0:T(1,128)S(1)} %copy-done.2), custom_call_target="tpu_custom_call" | custom-call | tf_op jit(solution)/shard_map/pallas_call | solution.py:29
  25.6 1.5 %collective-permute-start.12 = (bf16[208,256]{1,0:T(8,128)(2,1)S(1)}, bf16[208,256]{1,0:T(8,128)(2,1)S(1)}, u32[]{:S(2)}, u32[]{:S(2)}) collective-permute-start(bf16[208,256]{1,0:T(8,128)(2,1)S(1)} %shard_map.79.refs_0_), channel_id=1, source_target_pairs={{0,3},{1,2},{2,1},{3,0},{4,7},{5,6},{6,5},{7,4},{8,11},{9,10},{10,... | collective-permute-start | bytes 319496 | tf_op jit(solution)/shard_map/ppermute | solution.py:21
  27.1 1.1 %collective-permute-start.11 = (bf16[208,256]{1,0:T(8,128)(2,1)S(1)}, bf16[208,256]{1,0:T(8,128)(2,1)S(1)}, u32[]{:S(2)}, u32[]{:S(2)}) collective-permute-start(bf16[208,256]{1,0:T(8,128)(2,1)S(1)} %shard_map.79.refs_0_), channel_id=1, source_target_pairs={{0,2},{1,3},{2,0},{3,1},{4,6},{5,7},{6,4},{7,5},{8,10},{9,11},{10,... | collective-permute-start | bytes 319496 | tf_op jit(solution)/shard_map/ppermute | solution.py:21
  28.2 0.9 %collective-permute-start.10 = (bf16[208,256]{1,0:T(8,128)(2,1)S(1)}, bf16[208,256]{1,0:T(8,128)(2,1)S(1)}, u32[]{:S(2)}, u32[]{:S(2)}) collective-permute-start(bf16[208,256]{1,0:T(8,128)(2,1)S(1)} %shard_map.79.refs_0_), channel_id=1, source_target_pairs={{0,1},{1,0},{2,3},{3,2},{4,5},{5,4},{6,7},{7,6},{8,9},{9,8},{10,11... | collective-permute-start | bytes 319496 | tf_op jit(solution)/shard_map/ppermute | solution.py:21
  29.2 2.5 %collective-permute-done.13.refs_7_ = bf16[192,512]{1,0:T(8,128)(2,1)S(1)} collective-permute-done((bf16[192,512]{1,0:T(8,128)(2,1)S(1)}, bf16[192,512]{1,0:T(8,128)(2,1)S(1)}, u32[]{:S(2)}, u32[]{:S(2)}) %collective-permute-start.13) | collective-permute-done | bytes 196640 | tf_op jit(solution)/shard_map/ppermute | solution.py:21
  31.6 2.2 %collective-permute-done.12.refs_3_ = bf16[208,256]{1,0:T(8,128)(2,1)S(1)} collective-permute-done((bf16[208,256]{1,0:T(8,128)(2,1)S(1)}, bf16[208,256]{1,0:T(8,128)(2,1)S(1)}, u32[]{:S(2)}, u32[]{:S(2)}) %collective-permute-start.12) | collective-permute-done | bytes 106528 | tf_op jit(solution)/shard_map/ppermute | solution.py:21
  33.8 1.5 %collective-permute-done.11.refs_2_ = bf16[208,256]{1,0:T(8,128)(2,1)S(1)} collective-permute-done((bf16[208,256]{1,0:T(8,128)(2,1)S(1)}, bf16[208,256]{1,0:T(8,128)(2,1)S(1)}, u32[]{:S(2)}, u32[]{:S(2)}) %collective-permute-start.11) | collective-permute-done | bytes 106528 | tf_op jit(solution)/shard_map/ppermute | solution.py:21
  35.3 0.3 collective-permute-done.10.refs_1_
  35.6 1.4 %shard_map.81 = (bf16[64,512]{1,0:T(8,128)(2,1)S(1)}, bf16[64,512]{1,0:T(8,128)(2,1)S(1)}, bf16[64,512]{1,0:T(8,128)(2,1)S(1)}, bf16[64,512]{1,0:T(8,128)(2,1)S(1)}, bf16[512,128]{1,0:T(8,128)(2,1)}) custom-call(bf16[208,256]{1,0:T(8,128)(2,1)S(1)} %shard_map.79.refs_0_, bf16[208,256]{1,0:T(8,128)(2,1)S(1)} %collective-permute-done.10.refs_1_, ...), custom_call_target="tpu_custom_call" | custom-call | tf_op jit(solution)/shard_map/pallas_call | solution.py:29
  37.0 4.0 %all-to-all-start = ((bf16[32,16,128]{2,1,0:T(8,128)(2,1)}), bf16[32,16,128]{2,1,0:T(8,128)(2,1)S(1)}, u32[]{:S(2)}, u32[]{:S(2)}) async-start(bf16[32,16,128]{2,1,0:T(8,128)(2,1)} %bitcast.1), calls=%async_computation | async-start | bytes 262144 | tf_op jit(solution)/shard_map/all_to_all | solution.py:249
  41.1 1.8 %collective-permute-start.14 = (bf16[64,512]{1,0:T(8,128)(2,1)S(1)}, bf16[64,512]{1,0:T(8,128)(2,1)S(1)}, u32[]{:S(2)}, u32[]{:S(2)}) collective-permute-start(bf16[64,512]{1,0:T(8,128)(2,1)S(1)} %get-tuple-element.18), channel_id=1, source_target_pairs={{0,1},{1,0},{2,3},{3,2},{4,5},{5,4},{6,7},{7,6},{8,9},{9,8},{10,11... | collective-permute-start | bytes 196616 | tf_op jit(solution)/shard_map/ppermute | solution.py:21
  42.9 1.5 %collective-permute-start.15 = (bf16[64,512]{1,0:T(8,128)(2,1)S(1)}, bf16[64,512]{1,0:T(8,128)(2,1)S(1)}, u32[]{:S(2)}, u32[]{:S(2)}) collective-permute-start(bf16[64,512]{1,0:T(8,128)(2,1)S(1)} %get-tuple-element.19), channel_id=1, source_target_pairs={{0,2},{1,3},{2,0},{3,1},{4,6},{5,7},{6,4},{7,5},{8,10},{9,11},{10,... | collective-permute-start | bytes 196616 | tf_op jit(solution)/shard_map/ppermute | solution.py:21
  44.4 0.3 collective-permute-start.16
  44.6 4.2 %all-to-all-done = bf16[32,16,128]{2,1,0:T(8,128)(2,1)S(1)} async-done(((bf16[32,16,128]{2,1,0:T(8,128)(2,1)}), bf16[32,16,128]{2,1,0:T(8,128)(2,1)S(1)}, u32[]{:S(2)}, u32[]{:S(2)}) %all-to-all-start) | async-done | bytes 131104 | tf_op jit(solution)/shard_map/all_to_all | solution.py:249
  48.8 0.8 %shard_map.83 = f32[32,8,8]{2,1,0:T(8,128)} custom-call(bf16[8,4,16,128]{3,2,1,0:T(8,128)(2,1)S(1)} %bitcast.3), custom_call_target="tpu_custom_call" | custom-call | tf_op jit(solution)/shard_map/pallas_call | solution.py:29
  49.6 2.6 %all-to-all-start.1 = ((f32[32,8,8]{2,1,0:T(8,128)}), f32[32,8,8]{2,1,0:T(8,128)S(1)}, u32[]{:S(2)}, u32[]{:S(2)}) async-start(f32[32,8,8]{2,1,0:T(8,128)} %shard_map.83), calls=%async_computation.1 | async-start | bytes 262144 | tf_op jit(solution)/shard_map/all_to_all | solution.py:260
  52.2 0.0 collective-permute-done.14.refs_1_
  52.2 0.0 collective-permute-done.15.refs_2_
  52.2 0.0 collective-permute-done.16.refs_3_
  52.2 0.7 %shard_map.82 = bf16[64,2048]{1,0:T(8,128)(2,1)} custom-call(bf16[64,512]{1,0:T(8,128)(2,1)S(1)} %get-tuple-element.17.refs_0_, bf16[64,512]{1,0:T(8,128)(2,1)S(1)} %collective-permute-done.14.refs_1_, bf16[64,512]{1,0:T(8,128)(2,1)S(1)} %collective-permute-done.15.refs_2_, bf16[64,512]{1,0:T(8,128)(2,1)S(1)} %collective-permute-done.16.refs_3_), custom_call_target="tpu_custom_call" | custom-call | tf_op jit(solution)/shard_map/pallas_call | solution.py:29
  53.0 7.0 %all-to-all-done.1.tables_ref = f32[32,8,8]{2,1,0:T(8,128)S(1)} async-done(((f32[32,8,8]{2,1,0:T(8,128)}), f32[32,8,8]{2,1,0:T(8,128)S(1)}, u32[]{:S(2)}, u32[]{:S(2)}) %all-to-all-start.1) | async-done | bytes 8224 | tf_op jit(solution)/shard_map/all_to_all | solution.py:260
  59.9 0.7 %shard_map.84 = f32[8,8]{1,0:T(8,128)} custom-call(f32[32,8,8]{2,1,0:T(8,128)S(1)} %all-to-all-done.1.tables_ref), custom_call_target="tpu_custom_call" | custom-call | tf_op jit(solution)/shard_map/pallas_call | solution.py:29
  (1 shorter events, 0.0 us)
Async XLA Ops:
  2.0 8.6 %collective-permute-start.7 = (bf16[32,1024]{1,0:T(8,128)(2,1)S(1)}, bf16[32,1024]{1,0:T(8,128)(2,1)S(1)}, u32[]{:S(2)}, u32[]{:S(2)}) collective-permute-start(bf16[32,1024]{1,0:T(8,128)(2,1)S(1)} %get-tuple-element.14.refs_2_), channel_id=1, source_target_pairs={{0,6},{1,7},{2,4},{3,5},{4,2},{5,3},{6,0},{7,1},{8,14},{9,15},{10,... | collective-permute-start | bytes 196616 | tf_op jit(solution)/shard_map/ppermute | solution.py:21
  7.1 15.6 %collective-permute-start = (bf16[192,512]{1,0:T(8,128)(2,1)S(1)}, bf16[192,512]{1,0:T(8,128)(2,1)S(1)}, u32[]{:S(2)}, u32[]{:S(2)}) collective-permute-start(bf16[192,512]{1,0:T(8,128)(2,1)S(1)} %get-tuple-element.12), channel_id=1, source_target_pairs={{0,1},{1,0},{2,3},{3,2},{4,5},{5,4},{6,7},{7,6},{8,9},{9,8},{10,11... | collective-permute-start | bytes 589832 | tf_op jit(solution)/shard_map/ppermute | solution.py:21
  8.6 14.1 %collective-permute-start.1 = (bf16[192,512]{1,0:T(8,128)(2,1)S(1)}, bf16[192,512]{1,0:T(8,128)(2,1)S(1)}, u32[]{:S(2)}, u32[]{:S(2)}) collective-permute-start(bf16[192,512]{1,0:T(8,128)(2,1)S(1)} %get-tuple-element.13), channel_id=1, source_target_pairs={{0,2},{1,3},{2,0},{3,1},{4,6},{5,7},{6,4},{7,5},{8,10},{9,11},{10,... | collective-permute-start | bytes 589832 | tf_op jit(solution)/shard_map/ppermute | solution.py:21
  8.6 6.6 %collective-permute-start.5 = (bf16[32,1024]{1,0:T(8,128)(2,1)S(1)}, bf16[32,1024]{1,0:T(8,128)(2,1)S(1)}, u32[]{:S(2)}, u32[]{:S(2)}) collective-permute-start(bf16[32,1024]{1,0:T(8,128)(2,1)S(1)} %get-tuple-element.14.refs_2_), channel_id=1, source_target_pairs={{0,4},{1,5},{2,6},{3,7},{4,0},{5,1},{6,2},{7,3},{8,12},{9,13},{10,... | collective-permute-start | bytes 196616 | tf_op jit(solution)/shard_map/ppermute | solution.py:21
  9.4 8.1 %collective-permute-start.3 = (bf16[32,1024]{1,0:T(8,128)(2,1)S(1)}, bf16[32,1024]{1,0:T(8,128)(2,1)S(1)}, u32[]{:S(2)}, u32[]{:S(2)}) collective-permute-start(bf16[32,1024]{1,0:T(8,128)(2,1)S(1)} %get-tuple-element.14.refs_2_), channel_id=1, source_target_pairs={{0,2},{1,3},{2,0},{3,1},{4,6},{5,7},{6,4},{7,5},{8,10},{9,11},{10,... | collective-permute-start | bytes 196616 | tf_op jit(solution)/shard_map/ppermute | solution.py:21
  10.6 7.8 %collective-permute-start.2 = (bf16[32,1024]{1,0:T(8,128)(2,1)S(1)}, bf16[32,1024]{1,0:T(8,128)(2,1)S(1)}, u32[]{:S(2)}, u32[]{:S(2)}) collective-permute-start(bf16[32,1024]{1,0:T(8,128)(2,1)S(1)} %get-tuple-element.14.refs_2_), channel_id=1, source_target_pairs={{0,1},{1,0},{2,3},{3,2},{4,5},{5,4},{6,7},{7,6},{8,9},{9,8},{10,11... | collective-permute-start | bytes 196616 | tf_op jit(solution)/shard_map/ppermute | solution.py:21
  15.2 4.7 %collective-permute-start.8 = (bf16[32,1024]{1,0:T(8,128)(2,1)S(1)}, bf16[32,1024]{1,0:T(8,128)(2,1)S(1)}, u32[]{:S(2)}, u32[]{:S(2)}) collective-permute-start(bf16[32,1024]{1,0:T(8,128)(2,1)S(1)} %collective-permute-done.7.refs_8_), channel_id=1, source_target_pairs={{0,1},{1,0},{2,3},{3,2},{4,5},{5,4},{6,7},{7,6},{8,9},{9,8},{10,11... | collective-permute-start | bytes 196616 | tf_op jit(solution)/shard_map/ppermute | solution.py:21
  17.5 4.3 %collective-permute-start.6 = (bf16[32,1024]{1,0:T(8,128)(2,1)S(1)}, bf16[32,1024]{1,0:T(8,128)(2,1)S(1)}, u32[]{:S(2)}, u32[]{:S(2)}) collective-permute-start(bf16[32,1024]{1,0:T(8,128)(2,1)S(1)} %collective-permute-done.5.refs_6_), channel_id=1, source_target_pairs={{0,1},{1,0},{2,3},{3,2},{4,5},{5,4},{6,7},{7,6},{8,9},{9,8},{10,11... | collective-permute-start | bytes 196616 | tf_op jit(solution)/shard_map/ppermute | solution.py:21
  18.4 4.3 %collective-permute-start.4 = (bf16[32,1024]{1,0:T(8,128)(2,1)S(1)}, bf16[32,1024]{1,0:T(8,128)(2,1)S(1)}, u32[]{:S(2)}, u32[]{:S(2)}) collective-permute-start(bf16[32,1024]{1,0:T(8,128)(2,1)S(1)} %collective-permute-done.3.refs_4_), channel_id=1, source_target_pairs={{0,1},{1,0},{2,3},{3,2},{4,5},{5,4},{6,7},{7,6},{8,9},{9,8},{10,11... | collective-permute-start | bytes 196616 | tf_op jit(solution)/shard_map/ppermute | solution.py:21
  22.7 2.1 %copy-start.1 = (bf16[192,2048]{1,0:T(8,128)(2,1)S(1)}, bf16[192,2048]{1,0:T(8,128)(2,1)}, u32[]{:S(2)}) copy-start(bf16[192,2048]{1,0:T(8,128)(2,1)} %up_ref.1) | copy-start | bytes 2359300
  22.7 2.0 %copy-start = (bf16[192,2048]{1,0:T(8,128)(2,1)S(1)}, bf16[192,2048]{1,0:T(8,128)(2,1)}, u32[]{:S(2)}) copy-start(bf16[192,2048]{1,0:T(8,128)(2,1)} %gate_ref.1) | copy-start | bytes 2359300
  22.7 2.0 %collective-permute-start.9 = (bf16[256,1024]{1,0:T(8,128)(2,1)S(1)}, bf16[256,1024]{1,0:T(8,128)(2,1)S(1)}, u32[]{:S(2)}, u32[]{:S(2)}) collective-permute-start(bf16[256,1024]{1,0:T(8,128)(2,1)S(1)} %shard_map.78.mine_ref.refs_1_), channel_id=1, source_target_pairs={{0,8},{8,0},{16,24},{24,16},{1,9},{9,1},{17,25},{25,17},{2,10},{10... | collective-permute-start | bytes 1572872 | tf_op jit(solution)/shard_map/ppermute | solution.py:21
  22.8 1.9 %copy-start.2 = (f32[1,64]{1,0:T(1,128)S(1)}, f32[1,64]{1,0:T(1,128)}, u32[]{:S(2)}) copy-start(f32[1,64]{1,0:T(1,128)} %route_ref.1) | copy-start | bytes 772
  22.8 8.8 %collective-permute-start.13 = (bf16[192,512]{1,0:T(8,128)(2,1)S(1)}, bf16[192,512]{1,0:T(8,128)(2,1)S(1)}, u32[]{:S(2)}, u32[]{:S(2)}) collective-permute-start(bf16[192,512]{1,0:T(8,128)(2,1)S(1)} %shard_map.80), channel_id=1, source_target_pairs={{0,3},{1,2},{2,1},{3,0},{4,7},{5,6},{6,5},{7,4},{8,11},{9,10},{10,... | collective-permute-start | bytes 589832 | tf_op jit(solution)/shard_map/ppermute | solution.py:21
  25.6 8.2 %collective-permute-start.12 = (bf16[208,256]{1,0:T(8,128)(2,1)S(1)}, bf16[208,256]{1,0:T(8,128)(2,1)S(1)}, u32[]{:S(2)}, u32[]{:S(2)}) collective-permute-start(bf16[208,256]{1,0:T(8,128)(2,1)S(1)} %shard_map.79.refs_0_), channel_id=1, source_target_pairs={{0,3},{1,2},{2,1},{3,0},{4,7},{5,6},{6,5},{7,4},{8,11},{9,10},{10,... | collective-permute-start | bytes 319496 | tf_op jit(solution)/shard_map/ppermute | solution.py:21
  27.1 8.2 %collective-permute-start.11 = (bf16[208,256]{1,0:T(8,128)(2,1)S(1)}, bf16[208,256]{1,0:T(8,128)(2,1)S(1)}, u32[]{:S(2)}, u32[]{:S(2)}) collective-permute-start(bf16[208,256]{1,0:T(8,128)(2,1)S(1)} %shard_map.79.refs_0_), channel_id=1, source_target_pairs={{0,2},{1,3},{2,0},{3,1},{4,6},{5,7},{6,4},{7,5},{8,10},{9,11},{10,... | collective-permute-start | bytes 319496 | tf_op jit(solution)/shard_map/ppermute | solution.py:21
  28.2 7.4 %collective-permute-start.10 = (bf16[208,256]{1,0:T(8,128)(2,1)S(1)}, bf16[208,256]{1,0:T(8,128)(2,1)S(1)}, u32[]{:S(2)}, u32[]{:S(2)}) collective-permute-start(bf16[208,256]{1,0:T(8,128)(2,1)S(1)} %shard_map.79.refs_0_), channel_id=1, source_target_pairs={{0,1},{1,0},{2,3},{3,2},{4,5},{5,4},{6,7},{7,6},{8,9},{9,8},{10,11... | collective-permute-start | bytes 319496 | tf_op jit(solution)/shard_map/ppermute | solution.py:21
  37.0 11.8 %all-to-all-start = ((bf16[32,16,128]{2,1,0:T(8,128)(2,1)}), bf16[32,16,128]{2,1,0:T(8,128)(2,1)S(1)}, u32[]{:S(2)}, u32[]{:S(2)}) async-start(bf16[32,16,128]{2,1,0:T(8,128)(2,1)} %bitcast.1), calls=%async_computation | async-start | bytes 262144 | tf_op jit(solution)/shard_map/all_to_all | solution.py:249
  41.1 11.1 %collective-permute-start.14 = (bf16[64,512]{1,0:T(8,128)(2,1)S(1)}, bf16[64,512]{1,0:T(8,128)(2,1)S(1)}, u32[]{:S(2)}, u32[]{:S(2)}) collective-permute-start(bf16[64,512]{1,0:T(8,128)(2,1)S(1)} %get-tuple-element.18), channel_id=1, source_target_pairs={{0,1},{1,0},{2,3},{3,2},{4,5},{5,4},{6,7},{7,6},{8,9},{9,8},{10,11... | collective-permute-start | bytes 196616 | tf_op jit(solution)/shard_map/ppermute | solution.py:21
  42.9 9.3 %collective-permute-start.15 = (bf16[64,512]{1,0:T(8,128)(2,1)S(1)}, bf16[64,512]{1,0:T(8,128)(2,1)S(1)}, u32[]{:S(2)}, u32[]{:S(2)}) collective-permute-start(bf16[64,512]{1,0:T(8,128)(2,1)S(1)} %get-tuple-element.19), channel_id=1, source_target_pairs={{0,2},{1,3},{2,0},{3,1},{4,6},{5,7},{6,4},{7,5},{8,10},{9,11},{10,... | collective-permute-start | bytes 196616 | tf_op jit(solution)/shard_map/ppermute | solution.py:21
  44.4 7.8 %collective-permute-start.16 = (bf16[64,512]{1,0:T(8,128)(2,1)S(1)}, bf16[64,512]{1,0:T(8,128)(2,1)S(1)}, u32[]{:S(2)}, u32[]{:S(2)}) collective-permute-start(bf16[64,512]{1,0:T(8,128)(2,1)S(1)} %get-tuple-element.20), channel_id=1, source_target_pairs={{0,3},{1,2},{2,1},{3,0},{4,7},{5,6},{6,5},{7,4},{8,11},{9,10},{10,... | collective-permute-start | bytes 196616 | tf_op jit(solution)/shard_map/ppermute | solution.py:21
  49.6 10.3 %all-to-all-start.1 = ((f32[32,8,8]{2,1,0:T(8,128)}), f32[32,8,8]{2,1,0:T(8,128)S(1)}, u32[]{:S(2)}, u32[]{:S(2)}) async-start(f32[32,8,8]{2,1,0:T(8,128)} %shard_map.83), calls=%async_computation.1 | async-start | bytes 262144 | tf_op jit(solution)/shard_map/all_to_all | solution.py:260

commit v5 on v4

--- a/solution.py
+++ b/solution.py
@@ -1,3 +1,5 @@
+import functools
+
 import jax
 import jax.numpy as jnp
 from jax import lax
@@ -84,15 +86,32 @@
     )
 
 
-def stack_kernel(*refs):
-    pieces, out_ref = refs[2:-1], refs[-1]
-    rows = pieces[0].shape[0]
-    for m, piece in enumerate(pieces):
-        place = lax.axis_index("tok") ^ m
-        out_ref[pl.ds(pl.multiple_of(place * rows, rows), rows)] = piece[...]
-
-
-def hidden_kernel(mine_ref, other_ref, gate_ref, up_ref, route_ref, out_ref):
+def stack_kernel(order, *refs):
+    pieces, out_ref = refs[1:-1], refs[-1]
+    rows = out_ref.shape[0] // lax.axis_size("tok")
+    count = 0
+    for piece in pieces:
+        for at in range(piece.shape[0] // rows):
+            place = lax.axis_index("tok") ^ order[count]
+            out_ref[pl.ds(pl.multiple_of(place * rows, rows), rows)] = piece[
+                at * rows : (at + 1) * rows
+            ]
+            count += 1
+
+
+def pair_up_kernel(after_ref, *refs):
+    rows = refs[0].shape[0]
+    for at, ref in enumerate(refs[:-1]):
+        refs[-1][at * rows : (at + 1) * rows] = ref[...]
+
+
+def together(pieces, after):
+    rows, width = pieces[0].shape
+    out = jax.ShapeDtypeStruct((rows * len(pieces), width), bf16)
+    return call(pair_up_kernel, out, [ANY] + [VMEM] * len(pieces), (after, *pieces))
+
+
+def hidden_kernel(after_ref, mine_ref, other_ref, gate_ref, up_ref, route_ref, out_ref):
     tokens, width = mine_ref.shape
     gate, upward = [
         sum(
@@ -215,26 +234,29 @@
             pltpu.SemaphoreType.DMA((2 + HOLDERS,)),
         ],
     )
-    pieces = {0: own}
-    for m in range(members - 2, 0, -2):
-        pieces[m] = swapped(own, "tok", m)
-    for m in range(0, members, 2):
-        pieces[m + 1] = swapped(pieces[m], "tok", 1)
+    far = range(members - 2, 0, -2)
+    along = {m: swapped(own, "tok", m) for m in far}
+    first, second = (0, *far[: len(far) // 2]), far[len(far) // 2 :]
     down_x, down_z = swapped(downs[1], "tok", 1), swapped(downs[2], "tok", 2)
+    along[0] = own
+    parts = [together([along[m] for m in half], down_x) for half in (first, second)]
+    crossed = [swapped(half, "tok", 1) for half in parts]
+    down_xz = swapped(held(downs[3], crossed[0]), "tok", 3)
+    order = (*first, *second, *(m + 1 for m in (*first, *second)))
     mine = call(
-        stack_kernel,
+        functools.partial(stack_kernel, order),
         jax.ShapeDtypeStruct((tokens, model // 2), bf16),
-        [ANY] * 2 + [VMEM] * members,
-        (down_x, down_z, *[pieces[m] for m in range(members)]),
-    )
+        [ANY] + [VMEM] * (members // 2 + 2),
+        (down_z, *[along[m] for m in (*first, *second)], *crossed),
+    )
+    downs = [downs[0], down_x, down_z, down_xz]
     other = swapped(mine, "grp", 1)
 
-    downs = [downs[0], down_x, down_z, swapped(held(downs[3], mine), "tok", 3)]
     hidden = call(
         hidden_kernel,
         jax.ShapeDtypeStruct((depth + TILE, tokens), bf16),
-        [VMEM] * 5,
-        (mine, other, gate_weight, up_weight, route_weight),
+        [ANY] + [VMEM] * 5,
+        (down_xz, mine, other, gate_weight, up_weight, route_weight),
     )
     hiddens = [swapped(hidden, "tok", m) if m else hidden for m in range(HOLDERS)]
     entries = tokens * tokens // LANES

time: 60.9 us -> 62.5 us (1.026)
  waiting for transfers between devices: 25.8 us -> 28.7 us
  starting transfers between devices: 28.1 us -> 26.8 us
    ppermute x17 -> x15, waiting for transfers between devices: 14.6 us -> 17.5 us  [swapped(): lax.ppermute(array, axis, [(i, i ^ mask) for i in range(lax.axis_size(axi...]
    ppermute x17 -> x15, starting transfers between devices: 21.5 us -> 19.5 us  [swapped(): lax.ppermute(array, axis, [(i, i ^ mask) for i in range(lax.axis_size(axi...]
    all_to_all x1, starting transfers between devices: 4.03 us -> 4.72 us  [shards(): lax.all_to_all(centered, ('grp', 'tok'), split_axis=0, concat_axis=0, til...]
    pallas_call x8 -> x10, Pallas kernels: 5.94 us -> 5.97 us  [call(): pl.pallas_call(body, out_shape=outs, in_specs=in_specs, out_specs=jax.tre...]
  transfers between devices with their start and end apart: 19 -> 17, of which waited for: 12 -> 10; matrix products, arithmetic and copies ran while one was open for 0% -> 0% of each run, Pallas kernels for 4% -> 3%
where the time goes in v5:
time: 62.5 us; the launch traced here: 62.2 us
  waiting for transfers between devices  28.7 us (46%)
  starting transfers between devices  26.8 us (43%)
  Pallas kernels  5.97 us (10%)
  between operations  0.77 us (1%)
    ppermute x15, starting transfers between devices, swapped(): lax.ppermute(array, axis, [(i, i ^ mask) for i in range(lax.axis_size(axi...  19.5 us
    ppermute x15, waiting for transfers between devices, swapped(): lax.ppermute(array, axis, [(i, i ^ mask) for i in range(lax.axis_size(axi...  17.5 us
    all_to_all x1, waiting for transfers between devices, shards(): lax.all_to_all(tables, ('grp', 'tok'), split_axis=0, concat_axis=0, tiled...  6.96 us
    pallas_call x10, Pallas kernels, call(): pl.pallas_call(body, out_shape=outs, in_specs=in_specs, out_specs=jax.tre...  5.97 us
    all_to_all x1, starting transfers between devices, shards(): lax.all_to_all(centered, ('grp', 'tok'), split_axis=0, concat_axis=0, til...  4.72 us
    all_to_all x1, waiting for transfers between devices, shards(): lax.all_to_all(centered, ('grp', 'tok'), split_axis=0, concat_axis=0, til...  4.19 us
    all_to_all x1, starting transfers between devices, shards(): lax.all_to_all(tables, ('grp', 'tok'), split_axis=0, concat_axis=0, tiled...  2.56 us
  transfers between devices with their start and end apart: 17, of which 10 were waited for; matrix products, arithmetic and copies ran while one was open for 0% of the time, Pallas kernels for 3%

profile of v5, /device:TPU:0, one launch (start us, length us, event | category | flops | bytes accessed | tf_op | source)
XLA Modules:
  0.0 62.2 jit_solution(2313574216828570656)
XLA Ops:
  0.6 1.3 %shard_map.77 = (bf16[32,1024]{1,0:T(8,128)(2,1)S(1)}, bf16[192,512]{1,0:T(8,128)(2,1)S(1)}, bf16[192,512]{1,0:T(8,128)(2,1)S(1)}, bf16[192,512]{1,0:T(8,128)(2,1)S(1)}, bf16[192,512]{1,0:T(8,128)(2,1)S(1)}) custom-call(bf16[32,2048]{1,0:T(8,128)(2,1)} %states_hbm.1, f32[1,2048]{1,0:T(1,128)} %bitcast.4, bf16[192,2048]{1,0:T(8,128)(2,1)} %down_hbm.1), custom_call_target="tpu_custom_call" | custom-call | tf_op jit(solution)/shard_map/pallas_call | solution.py:31
  2.0 3.0 %collective-permute-start = (bf16[192,512]{1,0:T(8,128)(2,1)S(1)}, bf16[192,512]{1,0:T(8,128)(2,1)S(1)}, u32[]{:S(2)}, u32[]{:S(2)}) collective-permute-start(bf16[192,512]{1,0:T(8,128)(2,1)S(1)} %get-tuple-element.13), channel_id=1, source_target_pairs={{0,1},{1,0},{2,3},{3,2},{4,5},{5,4},{6,7},{7,6},{8,9},{9,8},{10,11... | collective-permute-start | bytes 589832 | tf_op jit(solution)/shard_map/ppermute | solution.py:23
  5.0 3.6 %collective-permute-start.1 = (bf16[32,1024]{1,0:T(8,128)(2,1)S(1)}, bf16[32,1024]{1,0:T(8,128)(2,1)S(1)}, u32[]{:S(2)}, u32[]{:S(2)}) collective-permute-start(bf16[32,1024]{1,0:T(8,128)(2,1)S(1)} %get-tuple-element.14.refs_0_.refs_1_), channel_id=1, source_target_pairs={{0,6},{1,7},{2,4},{3,5},{4,2},{5,3},{6,0},{7,1},{8,14},{9,15},{10,... | collective-permute-start | bytes 196616 | tf_op jit(solution)/shard_map/ppermute | solution.py:23
  8.6 0.0 collective-permute-start.6
  8.6 0.8 %collective-permute-start.5 = (bf16[32,1024]{1,0:T(8,128)(2,1)S(1)}, bf16[32,1024]{1,0:T(8,128)(2,1)S(1)}, u32[]{:S(2)}, u32[]{:S(2)}) collective-permute-start(bf16[32,1024]{1,0:T(8,128)(2,1)S(1)} %get-tuple-element.14.refs_0_.refs_1_), channel_id=1, source_target_pairs={{0,4},{1,5},{2,6},{3,7},{4,0},{5,1},{6,2},{7,3},{8,12},{9,13},{10,... | collective-permute-start | bytes 196616 | tf_op jit(solution)/shard_map/ppermute | solution.py:23
  9.4 1.2 %collective-permute-start.4 = (bf16[192,512]{1,0:T(8,128)(2,1)S(1)}, bf16[192,512]{1,0:T(8,128)(2,1)S(1)}, u32[]{:S(2)}, u32[]{:S(2)}) collective-permute-start(bf16[192,512]{1,0:T(8,128)(2,1)S(1)} %get-tuple-element.15), channel_id=1, source_target_pairs={{0,2},{1,3},{2,0},{3,1},{4,6},{5,7},{6,4},{7,5},{8,10},{9,11},{10,... | collective-permute-start | bytes 589832 | tf_op jit(solution)/shard_map/ppermute | solution.py:23
  10.6 0.6 collective-permute-done.1.refs_1_.refs_2_
  11.1 0.0 collective-permute-done.after_ref.refs_5_
  11.2 0.6 %collective-permute-start.2 = (bf16[64,1024]{1,0:T(8,128)(2,1)S(1)}, bf16[64,1024]{1,0:T(8,128)(2,1)S(1)}, u32[]{:S(2)}, u32[]{:S(2)}) collective-permute-start(bf16[64,1024]{1,0:T(8,128)(2,1)S(1)} %shard_map.78), channel_id=1, source_target_pairs={{0,1},{1,0},{2,3},{3,2},{4,5},{5,4},{6,7},{7,6},{8,9},{9,8},{10,11... | collective-permute-start | bytes 393224 | tf_op jit(solution)/shard_map/ppermute | solution.py:23
  11.8 2.5 %collective-permute-done.6.refs_1_.refs_4_ = bf16[32,1024]{1,0:T(8,128)(2,1)S(1)} collective-permute-done((bf16[32,1024]{1,0:T(8,128)(2,1)S(1)}, bf16[32,1024]{1,0:T(8,128)(2,1)S(1)}, u32[]{:S(2)}, u32[]{:S(2)}) %collective-permute-start.6) | collective-permute-done | bytes 65568 | tf_op jit(solution)/shard_map/ppermute | solution.py:23
  14.3 0.0 collective-permute-done.5.refs_0_.refs_3_
  14.3 0.0 copy-start
  14.3 0.0 copy-start.1
  14.3 0.6 collective-permute-start.7
  14.9 3.2 %collective-permute-done.4.refs_0_.refs_6_ = bf16[192,512]{1,0:T(8,128)(2,1)S(1)} collective-permute-done((bf16[192,512]{1,0:T(8,128)(2,1)S(1)}, bf16[192,512]{1,0:T(8,128)(2,1)S(1)}, u32[]{:S(2)}, u32[]{:S(2)}) %collective-permute-start.4) | collective-permute-done | bytes 196640 | tf_op jit(solution)/shard_map/ppermute | solution.py:23
  18.1 0.0 collective-permute-done.2.refs_1_.refs_5_
  18.1 1.3 %collective-permute-done.7.refs_6_ = bf16[64,1024]{1,0:T(8,128)(2,1)S(1)} collective-permute-done((bf16[64,1024]{1,0:T(8,128)(2,1)S(1)}, bf16[64,1024]{1,0:T(8,128)(2,1)S(1)}, u32[]{:S(2)}, u32[]{:S(2)}) %collective-permute-start.7) | collective-permute-done | bytes 131104 | tf_op jit(solution)/shard_map/ppermute | solution.py:23
  19.4 0.1 collective-permute-start.8
  19.5 0.0 copy-start.2
  19.5 2.3 %collective-permute-start.3 = (bf16[192,512]{1,0:T(8,128)(2,1)S(1)}, bf16[192,512]{1,0:T(8,128)(2,1)S(1)}, u32[]{:S(2)}, u32[]{:S(2)}) collective-permute-start(bf16[192,512]{1,0:T(8,128)(2,1)S(1)} %shard_map.79), channel_id=1, source_target_pairs={{0,3},{1,2},{2,1},{3,0},{4,7},{5,6},{6,5},{7,4},{8,11},{9,10},{10,... | collective-permute-start | bytes 589832 | tf_op jit(solution)/shard_map/ppermute | solution.py:23
  21.8 5.9 %collective-permute-done.3.after_ref.refs_7_ = bf16[192,512]{1,0:T(8,128)(2,1)S(1)} collective-permute-done((bf16[192,512]{1,0:T(8,128)(2,1)S(1)}, bf16[192,512]{1,0:T(8,128)(2,1)S(1)}, u32[]{:S(2)}, u32[]{:S(2)}) %collective-permute-start.3) | collective-permute-done | bytes 196640 | tf_op jit(solution)/shard_map/ppermute | solution.py:23
  27.7 0.0 collective-permute-done.8.other_ref
  27.7 0.0 copy-done
  27.7 0.0 copy-done.1
  27.7 0.0 copy-done.2
  27.7 0.9 %shard_map.82.refs_0_ = bf16[208,256]{1,0:T(8,128)(2,1)S(1)} custom-call(bf16[192,512]{1,0:T(8,128)(2,1)S(1)} %collective-permute-done.3.after_ref.refs_7_, bf16[256,1024]{1,0:T(8,128)(2,1)S(1)} %shard_map.81.mine_ref, bf16[256,1024]{1,0:T(8,128)(2,1)S(1)} %collective-permute-done.8.other_ref, bf16[192,2048]{1,0:T(8,128)(2,1)S(1)} %copy-done, ...), custom_call_target="tpu_custom_call" | custom-call | tf_op jit(solution)/shard_map/pallas_call | solution.py:31
  28.6 2.3 %collective-permute-start.11 = (bf16[208,256]{1,0:T(8,128)(2,1)S(1)}, bf16[208,256]{1,0:T(8,128)(2,1)S(1)}, u32[]{:S(2)}, u32[]{:S(2)}) collective-permute-start(bf16[208,256]{1,0:T(8,128)(2,1)S(1)} %shard_map.82.refs_0_), channel_id=1, source_target_pairs={{0,3},{1,2},{2,1},{3,0},{4,7},{5,6},{6,5},{7,4},{8,11},{9,10},{10,... | collective-permute-start | bytes 319496 | tf_op jit(solution)/shard_map/ppermute | solution.py:23
  30.9 0.3 collective-permute-start.10
  31.2 1.2 %collective-permute-start.9 = (bf16[208,256]{1,0:T(8,128)(2,1)S(1)}, bf16[208,256]{1,0:T(8,128)(2,1)S(1)}, u32[]{:S(2)}, u32[]{:S(2)}) collective-permute-start(bf16[208,256]{1,0:T(8,128)(2,1)S(1)} %shard_map.82.refs_0_), channel_id=1, source_target_pairs={{0,1},{1,0},{2,3},{3,2},{4,5},{5,4},{6,7},{7,6},{8,9},{9,8},{10,11... | collective-permute-start | bytes 319496 | tf_op jit(solution)/shard_map/ppermute | solution.py:23
  32.4 2.5 %collective-permute-done.11.refs_3_ = bf16[208,256]{1,0:T(8,128)(2,1)S(1)} collective-permute-done((bf16[208,256]{1,0:T(8,128)(2,1)S(1)}, bf16[208,256]{1,0:T(8,128)(2,1)S(1)}, u32[]{:S(2)}, u32[]{:S(2)}) %collective-permute-start.11) | collective-permute-done | bytes 106528 | tf_op jit(solution)/shard_map/ppermute | solution.py:23
  34.9 1.3 %collective-permute-done.10.refs_2_ = bf16[208,256]{1,0:T(8,128)(2,1)S(1)} collective-permute-done((bf16[208,256]{1,0:T(8,128)(2,1)S(1)}, bf16[208,256]{1,0:T(8,128)(2,1)S(1)}, u32[]{:S(2)}, u32[]{:S(2)}) %collective-permute-start.10) | collective-permute-done | bytes 106528 | tf_op jit(solution)/shard_map/ppermute | solution.py:23
  36.2 0.3 collective-permute-done.9.refs_1_
  36.5 1.4 %shard_map.83 = (bf16[64,512]{1,0:T(8,128)(2,1)S(1)}, bf16[64,512]{1,0:T(8,128)(2,1)S(1)}, bf16[64,512]{1,0:T(8,128)(2,1)S(1)}, bf16[64,512]{1,0:T(8,128)(2,1)S(1)}, bf16[512,128]{1,0:T(8,128)(2,1)}) custom-call(bf16[208,256]{1,0:T(8,128)(2,1)S(1)} %shard_map.82.refs_0_, bf16[208,256]{1,0:T(8,128)(2,1)S(1)} %collective-permute-done.9.refs_1_, ...), custom_call_target="tpu_custom_call" | custom-call | tf_op jit(solution)/shard_map/pallas_call | solution.py:31
  37.9 4.7 %all-to-all-start = ((bf16[32,16,128]{2,1,0:T(8,128)(2,1)}), bf16[32,16,128]{2,1,0:T(8,128)(2,1)S(1)}, u32[]{:S(2)}, u32[]{:S(2)}) async-start(bf16[32,16,128]{2,1,0:T(8,128)(2,1)} %bitcast.1), calls=%async_computation | async-start | bytes 262144 | tf_op jit(solution)/shard_map/all_to_all | solution.py:271
  42.6 1.8 %collective-permute-start.12 = (bf16[64,512]{1,0:T(8,128)(2,1)S(1)}, bf16[64,512]{1,0:T(8,128)(2,1)S(1)}, u32[]{:S(2)}, u32[]{:S(2)}) collective-permute-start(bf16[64,512]{1,0:T(8,128)(2,1)S(1)} %get-tuple-element.18), channel_id=1, source_target_pairs={{0,1},{1,0},{2,3},{3,2},{4,5},{5,4},{6,7},{7,6},{8,9},{9,8},{10,11... | collective-permute-start | bytes 196616 | tf_op jit(solution)/shard_map/ppermute | solution.py:23
  44.5 1.5 %collective-permute-start.13 = (bf16[64,512]{1,0:T(8,128)(2,1)S(1)}, bf16[64,512]{1,0:T(8,128)(2,1)S(1)}, u32[]{:S(2)}, u32[]{:S(2)}) collective-permute-start(bf16[64,512]{1,0:T(8,128)(2,1)S(1)} %get-tuple-element.19), channel_id=1, source_target_pairs={{0,2},{1,3},{2,0},{3,1},{4,6},{5,7},{6,4},{7,5},{8,10},{9,11},{10,... | collective-permute-start | bytes 196616 | tf_op jit(solution)/shard_map/ppermute | solution.py:23
  45.9 0.3 collective-permute-start.14
  46.2 4.2 %all-to-all-done = bf16[32,16,128]{2,1,0:T(8,128)(2,1)S(1)} async-done(((bf16[32,16,128]{2,1,0:T(8,128)(2,1)}), bf16[32,16,128]{2,1,0:T(8,128)(2,1)S(1)}, u32[]{:S(2)}, u32[]{:S(2)}) %all-to-all-start) | async-done | bytes 131104 | tf_op jit(solution)/shard_map/all_to_all | solution.py:271
  50.4 0.8 %shard_map.85 = f32[32,8,8]{2,1,0:T(8,128)} custom-call(bf16[8,4,16,128]{3,2,1,0:T(8,128)(2,1)S(1)} %bitcast.3), custom_call_target="tpu_custom_call" | custom-call | tf_op jit(solution)/shard_map/pallas_call | solution.py:31
  51.2 2.6 %all-to-all-start.1 = ((f32[32,8,8]{2,1,0:T(8,128)}), f32[32,8,8]{2,1,0:T(8,128)S(1)}, u32[]{:S(2)}, u32[]{:S(2)}) async-start(f32[32,8,8]{2,1,0:T(8,128)} %shard_map.85), calls=%async_computation.1 | async-start | bytes 262144 | tf_op jit(solution)/shard_map/all_to_all | solution.py:282
  53.8 0.0 collective-permute-done.12.refs_1_
  53.8 0.0 collective-permute-done.13.refs_2_
  53.8 0.0 collective-permute-done.14.refs_3_
  53.8 0.7 %shard_map.84 = bf16[64,2048]{1,0:T(8,128)(2,1)} custom-call(bf16[64,512]{1,0:T(8,128)(2,1)S(1)} %get-tuple-element.17.refs_0_, bf16[64,512]{1,0:T(8,128)(2,1)S(1)} %collective-permute-done.12.refs_1_, bf16[64,512]{1,0:T(8,128)(2,1)S(1)} %collective-permute-done.13.refs_2_, bf16[64,512]{1,0:T(8,128)(2,1)S(1)} %collective-permute-done.14.refs_3_), custom_call_target="tpu_custom_call" | custom-call | tf_op jit(solution)/shard_map/pallas_call | solution.py:31
  54.5 7.0 %all-to-all-done.1.tables_ref = f32[32,8,8]{2,1,0:T(8,128)S(1)} async-done(((f32[32,8,8]{2,1,0:T(8,128)}), f32[32,8,8]{2,1,0:T(8,128)S(1)}, u32[]{:S(2)}, u32[]{:S(2)}) %all-to-all-start.1) | async-done | bytes 8224 | tf_op jit(solution)/shard_map/all_to_all | solution.py:282
  61.5 0.7 %shard_map.86 = f32[8,8]{1,0:T(8,128)} custom-call(f32[32,8,8]{2,1,0:T(8,128)S(1)} %all-to-all-done.1.tables_ref), custom_call_target="tpu_custom_call" | custom-call | tf_op jit(solution)/shard_map/pallas_call | solution.py:31
  (4 shorter events, 0.1 us)
Async XLA Ops:
  2.0 9.2 %collective-permute-start = (bf16[192,512]{1,0:T(8,128)(2,1)S(1)}, bf16[192,512]{1,0:T(8,128)(2,1)S(1)}, u32[]{:S(2)}, u32[]{:S(2)}) collective-permute-start(bf16[192,512]{1,0:T(8,128)(2,1)S(1)} %get-tuple-element.13), channel_id=1, source_target_pairs={{0,1},{1,0},{2,3},{3,2},{4,5},{5,4},{6,7},{7,6},{8,9},{9,8},{10,11... | collective-permute-start | bytes 589832 | tf_op jit(solution)/shard_map/ppermute | solution.py:23
  5.0 6.2 %collective-permute-start.1 = (bf16[32,1024]{1,0:T(8,128)(2,1)S(1)}, bf16[32,1024]{1,0:T(8,128)(2,1)S(1)}, u32[]{:S(2)}, u32[]{:S(2)}) collective-permute-start(bf16[32,1024]{1,0:T(8,128)(2,1)S(1)} %get-tuple-element.14.refs_0_.refs_1_), channel_id=1, source_target_pairs={{0,6},{1,7},{2,4},{3,5},{4,2},{5,3},{6,0},{7,1},{8,14},{9,15},{10,... | collective-permute-start | bytes 196616 | tf_op jit(solution)/shard_map/ppermute | solution.py:23
  8.6 5.7 %collective-permute-start.6 = (bf16[32,1024]{1,0:T(8,128)(2,1)S(1)}, bf16[32,1024]{1,0:T(8,128)(2,1)S(1)}, u32[]{:S(2)}, u32[]{:S(2)}) collective-permute-start(bf16[32,1024]{1,0:T(8,128)(2,1)S(1)} %get-tuple-element.14.refs_0_.refs_1_), channel_id=1, source_target_pairs={{0,2},{1,3},{2,0},{3,1},{4,6},{5,7},{6,4},{7,5},{8,10},{9,11},{10,... | collective-permute-start | bytes 196616 | tf_op jit(solution)/shard_map/ppermute | solution.py:23
  8.6 5.7 %collective-permute-start.5 = (bf16[32,1024]{1,0:T(8,128)(2,1)S(1)}, bf16[32,1024]{1,0:T(8,128)(2,1)S(1)}, u32[]{:S(2)}, u32[]{:S(2)}) collective-permute-start(bf16[32,1024]{1,0:T(8,128)(2,1)S(1)} %get-tuple-element.14.refs_0_.refs_1_), channel_id=1, source_target_pairs={{0,4},{1,5},{2,6},{3,7},{4,0},{5,1},{6,2},{7,3},{8,12},{9,13},{10,... | collective-permute-start | bytes 196616 | tf_op jit(solution)/shard_map/ppermute | solution.py:23
  9.4 8.7 %collective-permute-start.4 = (bf16[192,512]{1,0:T(8,128)(2,1)S(1)}, bf16[192,512]{1,0:T(8,128)(2,1)S(1)}, u32[]{:S(2)}, u32[]{:S(2)}) collective-permute-start(bf16[192,512]{1,0:T(8,128)(2,1)S(1)} %get-tuple-element.15), channel_id=1, source_target_pairs={{0,2},{1,3},{2,0},{3,1},{4,6},{5,7},{6,4},{7,5},{8,10},{9,11},{10,... | collective-permute-start | bytes 589832 | tf_op jit(solution)/shard_map/ppermute | solution.py:23
  11.2 6.9 %collective-permute-start.2 = (bf16[64,1024]{1,0:T(8,128)(2,1)S(1)}, bf16[64,1024]{1,0:T(8,128)(2,1)S(1)}, u32[]{:S(2)}, u32[]{:S(2)}) collective-permute-start(bf16[64,1024]{1,0:T(8,128)(2,1)S(1)} %shard_map.78), channel_id=1, source_target_pairs={{0,1},{1,0},{2,3},{3,2},{4,5},{5,4},{6,7},{7,6},{8,9},{9,8},{10,11... | collective-permute-start | bytes 393224 | tf_op jit(solution)/shard_map/ppermute | solution.py:23
  14.3 13.4 %copy-start = (bf16[192,2048]{1,0:T(8,128)(2,1)S(1)}, bf16[192,2048]{1,0:T(8,128)(2,1)}, u32[]{:S(2)}) copy-start(bf16[192,2048]{1,0:T(8,128)(2,1)} %gate_ref.1) | copy-start | bytes 2359300
  14.3 13.4 %copy-start.1 = (bf16[192,2048]{1,0:T(8,128)(2,1)S(1)}, bf16[192,2048]{1,0:T(8,128)(2,1)}, u32[]{:S(2)}) copy-start(bf16[192,2048]{1,0:T(8,128)(2,1)} %up_ref.1) | copy-start | bytes 2359300
  14.3 5.0 %collective-permute-start.7 = (bf16[64,1024]{1,0:T(8,128)(2,1)S(1)}, bf16[64,1024]{1,0:T(8,128)(2,1)S(1)}, u32[]{:S(2)}, u32[]{:S(2)}) collective-permute-start(bf16[64,1024]{1,0:T(8,128)(2,1)S(1)} %shard_map.80), channel_id=1, source_target_pairs={{0,1},{1,0},{2,3},{3,2},{4,5},{5,4},{6,7},{7,6},{8,9},{9,8},{10,11... | collective-permute-start | bytes 393224 | tf_op jit(solution)/shard_map/ppermute | solution.py:23
  19.4 8.3 %collective-permute-start.8 = (bf16[256,1024]{1,0:T(8,128)(2,1)S(1)}, bf16[256,1024]{1,0:T(8,128)(2,1)S(1)}, u32[]{:S(2)}, u32[]{:S(2)}) collective-permute-start(bf16[256,1024]{1,0:T(8,128)(2,1)S(1)} %shard_map.81.mine_ref), channel_id=1, source_target_pairs={{0,8},{8,0},{16,24},{24,16},{1,9},{9,1},{17,25},{25,17},{2,10},{10... | collective-permute-start | bytes 1572872 | tf_op jit(solution)/shard_map/ppermute | solution.py:23
  19.5 8.2 %copy-start.2 = (f32[1,64]{1,0:T(1,128)S(1)}, f32[1,64]{1,0:T(1,128)}, u32[]{:S(2)}) copy-start(f32[1,64]{1,0:T(1,128)} %route_ref.1) | copy-start | bytes 772
  19.5 8.2 %collective-permute-start.3 = (bf16[192,512]{1,0:T(8,128)(2,1)S(1)}, bf16[192,512]{1,0:T(8,128)(2,1)S(1)}, u32[]{:S(2)}, u32[]{:S(2)}) collective-permute-start(bf16[192,512]{1,0:T(8,128)(2,1)S(1)} %shard_map.79), channel_id=1, source_target_pairs={{0,3},{1,2},{2,1},{3,0},{4,7},{5,6},{6,5},{7,4},{8,11},{9,10},{10,... | collective-permute-start | bytes 589832 | tf_op jit(solution)/shard_map/ppermute | solution.py:23
  28.6 6.3 %collective-permute-start.11 = (bf16[208,256]{1,0:T(8,128)(2,1)S(1)}, bf16[208,256]{1,0:T(8,128)(2,1)S(1)}, u32[]{:S(2)}, u32[]{:S(2)}) collective-permute-start(bf16[208,256]{1,0:T(8,128)(2,1)S(1)} %shard_map.82.refs_0_), channel_id=1, source_target_pairs={{0,3},{1,2},{2,1},{3,0},{4,7},{5,6},{6,5},{7,4},{8,11},{9,10},{10,... | collective-permute-start | bytes 319496 | tf_op jit(solution)/shard_map/ppermute | solution.py:23
  30.9 5.3 %collective-permute-start.10 = (bf16[208,256]{1,0:T(8,128)(2,1)S(1)}, bf16[208,256]{1,0:T(8,128)(2,1)S(1)}, u32[]{:S(2)}, u32[]{:S(2)}) collective-permute-start(bf16[208,256]{1,0:T(8,128)(2,1)S(1)} %shard_map.82.refs_0_), channel_id=1, source_target_pairs={{0,2},{1,3},{2,0},{3,1},{4,6},{5,7},{6,4},{7,5},{8,10},{9,11},{10,... | collective-permute-start | bytes 319496 | tf_op jit(solution)/shard_map/ppermute | solution.py:23
  31.2 5.3 %collective-permute-start.9 = (bf16[208,256]{1,0:T(8,128)(2,1)S(1)}, bf16[208,256]{1,0:T(8,128)(2,1)S(1)}, u32[]{:S(2)}, u32[]{:S(2)}) collective-permute-start(bf16[208,256]{1,0:T(8,128)(2,1)S(1)} %shard_map.82.refs_0_), channel_id=1, source_target_pairs={{0,1},{1,0},{2,3},{3,2},{4,5},{5,4},{6,7},{7,6},{8,9},{9,8},{10,11... | collective-permute-start | bytes 319496 | tf_op jit(solution)/shard_map/ppermute | solution.py:23
  37.9 12.5 %all-to-all-start = ((bf16[32,16,128]{2,1,0:T(8,128)(2,1)}), bf16[32,16,128]{2,1,0:T(8,128)(2,1)S(1)}, u32[]{:S(2)}, u32[]{:S(2)}) async-start(bf16[32,16,128]{2,1,0:T(8,128)(2,1)} %bitcast.1), calls=%async_computation | async-start | bytes 262144 | tf_op jit(solution)/shard_map/all_to_all | solution.py:271
  42.6 11.1 %collective-permute-start.12 = (bf16[64,512]{1,0:T(8,128)(2,1)S(1)}, bf16[64,512]{1,0:T(8,128)(2,1)S(1)}, u32[]{:S(2)}, u32[]{:S(2)}) collective-permute-start(bf16[64,512]{1,0:T(8,128)(2,1)S(1)} %get-tuple-element.18), channel_id=1, source_target_pairs={{0,1},{1,0},{2,3},{3,2},{4,5},{5,4},{6,7},{7,6},{8,9},{9,8},{10,11... | collective-permute-start | bytes 196616 | tf_op jit(solution)/shard_map/ppermute | solution.py:23
  44.5 9.3 %collective-permute-start.13 = (bf16[64,512]{1,0:T(8,128)(2,1)S(1)}, bf16[64,512]{1,0:T(8,128)(2,1)S(1)}, u32[]{:S(2)}, u32[]{:S(2)}) collective-permute-start(bf16[64,512]{1,0:T(8,128)(2,1)S(1)} %get-tuple-element.19), channel_id=1, source_target_pairs={{0,2},{1,3},{2,0},{3,1},{4,6},{5,7},{6,4},{7,5},{8,10},{9,11},{10,... | collective-permute-start | bytes 196616 | tf_op jit(solution)/shard_map/ppermute | solution.py:23
  45.9 7.8 %collective-permute-start.14 = (bf16[64,512]{1,0:T(8,128)(2,1)S(1)}, bf16[64,512]{1,0:T(8,128)(2,1)S(1)}, u32[]{:S(2)}, u32[]{:S(2)}) collective-permute-start(bf16[64,512]{1,0:T(8,128)(2,1)S(1)} %get-tuple-element.20), channel_id=1, source_target_pairs={{0,3},{1,2},{2,1},{3,0},{4,7},{5,6},{6,5},{7,4},{8,11},{9,10},{10,... | collective-permute-start | bytes 196616 | tf_op jit(solution)/shard_map/ppermute | solution.py:23
  51.2 10.3 %all-to-all-start.1 = ((f32[32,8,8]{2,1,0:T(8,128)}), f32[32,8,8]{2,1,0:T(8,128)S(1)}, u32[]{:S(2)}, u32[]{:S(2)}) async-start(f32[32,8,8]{2,1,0:T(8,128)} %shard_map.85), calls=%async_computation.1 | async-start | bytes 262144 | tf_op jit(solution)/shard_map/all_to_all | solution.py:282

commit v6 on v5

--- a/solution.py
+++ b/solution.py
@@ -47,17 +47,16 @@
     return lax.axis_index("tok") & (HOLDERS - 1)
 
 
-def first_kernel(states_hbm, gain_hbm, down_hbm, *refs):
-    out_ref, downs = refs[0], refs[1 : 1 + HOLDERS]
-    states_ref, gain_ref, sems = refs[1 + HOLDERS :]
+def first_kernel(states_hbm, gain_hbm, down_hbm, out_ref, own_ref, z_ref, x_ref, states_ref, gain_ref, sems):
+    depth, width = own_ref.shape
+    blocks = (own_ref, x_ref.at[pl.ds(0, depth)], z_ref, x_ref.at[pl.ds(depth, depth)])
     copies = [
         pltpu.make_async_copy(states_hbm, states_ref, sems.at[0]),
         pltpu.make_async_copy(gain_hbm, gain_ref, sems.at[1]),
     ]
-    width = downs[0].shape[1]
-    for m, down_ref in enumerate(downs):
+    for m, block in enumerate(blocks):
         columns = pl.ds(pl.multiple_of((holder() ^ m) * width, width), width)
-        copies.append(pltpu.make_async_copy(down_hbm.at[:, columns], down_ref, sems.at[2 + m]))
+        copies.append(pltpu.make_async_copy(down_hbm.at[:, columns], block, sems.at[2 + m]))
     for copy in copies:
         copy.start()
     for copy in copies[:2]:
@@ -71,19 +70,10 @@
         copy.wait()
 
 
-def hold_kernel(*refs):
-    pass
-
-
-def held(array, after):
-    return call(
-        hold_kernel,
-        jax.ShapeDtypeStruct(array.shape, array.dtype),
-        [ANY] * 2,
-        (array, after),
-        out_specs=ANY,
-        aliases={0: 0},
-    )
+def onward_kernel(after_ref, own_ref, got_ref, out_ref):
+    depth = own_ref.shape[0]
+    out_ref[:depth] = own_ref[...]
+    out_ref[depth:] = got_ref[depth:]
 
 
 def stack_kernel(order, *refs):
@@ -111,7 +101,7 @@
     return call(pair_up_kernel, out, [ANY] + [VMEM] * len(pieces), (after, *pieces))
 
 
-def hidden_kernel(after_ref, mine_ref, other_ref, gate_ref, up_ref, route_ref, out_ref):
+def hidden_kernel(mine_ref, other_ref, gate_ref, up_ref, route_ref, out_ref):
     tokens, width = mine_ref.shape
     gate, upward = [
         sum(
@@ -134,17 +124,18 @@
 
 
 def features_kernel(*refs):
-    hidden_refs, down_refs = refs[:HOLDERS], refs[HOLDERS : 2 * HOLDERS]
-    block_refs, centered_ref = refs[2 * HOLDERS : 3 * HOLDERS], refs[3 * HOLDERS]
-    route_ref, features_ref = refs[3 * HOLDERS + 1 :]
-    depth, tokens = down_refs[0].shape[0], hidden_refs[0].shape[1]
+    hidden_refs, (own_ref, x_ref, z_ref) = refs[:HOLDERS], refs[HOLDERS : HOLDERS + 3]
+    block_refs, centered_ref = refs[HOLDERS + 3 : 2 * HOLDERS + 3], refs[2 * HOLDERS + 3]
+    route_ref, features_ref = refs[2 * HOLDERS + 4 :]
+    depth, tokens = own_ref.shape[0], hidden_refs[0].shape[1]
+    downs = (own_ref[...], x_ref[:depth], z_ref[:depth], z_ref[depth:])
     part = tokens // HOLDERS
     eye = lax.broadcasted_iota(jnp.int32, (part, part), 0) == lax.broadcasted_iota(
         jnp.int32, (part, part), 1
     )
     output = None
-    for m, (hidden_ref, down_ref) in enumerate(zip(hidden_refs, down_refs)):
-        product = dot_f32(hidden_ref[:depth], down_ref[...], (((0,), (0,)), ((), ())))
+    for m, (hidden_ref, down) in enumerate(zip(hidden_refs, downs)):
+        product = dot_f32(hidden_ref[:depth], down, (((0,), (0,)), ((), ())))
         output = product if output is None else output + product
         terms = hidden_ref[depth:, :part].astype(f32)
         route = jnp.sum(terms[:HOLDERS], axis=0, keepdims=True)
@@ -219,10 +210,10 @@
     depth = gate_weight.shape[0]
     part, token_part = model // HOLDERS, tokens // HOLDERS
 
-    own, *downs = call(
+    own, down_own, down_z, down_x = call(
         first_kernel,
         [jax.ShapeDtypeStruct((rows, model // 2), bf16)]
-        + [jax.ShapeDtypeStruct((depth, part), bf16)] * HOLDERS,
+        + [jax.ShapeDtypeStruct((depth * n, part), bf16) for n in (1, 1, 2)],
         [HBM] * 3,
         [
             pltpu.with_memory_space_constraint(a, pltpu.HBM)
@@ -234,29 +225,31 @@
             pltpu.SemaphoreType.DMA((2 + HOLDERS,)),
         ],
     )
-    far = range(members - 2, 0, -2)
-    along = {m: swapped(own, "tok", m) for m in far}
-    first, second = (0, *far[: len(far) // 2]), far[len(far) // 2 :]
-    down_x, down_z = swapped(downs[1], "tok", 1), swapped(downs[2], "tok", 2)
-    along[0] = own
-    parts = [together([along[m] for m in half], down_x) for half in (first, second)]
-    crossed = [swapped(half, "tok", 1) for half in parts]
-    down_xz = swapped(held(downs[3], crossed[0]), "tok", 3)
-    order = (*first, *second, *(m + 1 for m in (*first, *second)))
+    down_x = swapped(down_x, "tok", 1)
+    order = (0, *range(members - 2, 0, -2))
+    along = [swapped(own, "tok", m) if m else own for m in order]
+    along = together(along, down_x)
+    down_z = call(
+        onward_kernel,
+        jax.ShapeDtypeStruct(down_x.shape, bf16),
+        [ANY, VMEM, VMEM],
+        (along, down_z, down_x),
+    )
+    down_z = swapped(down_z, "tok", 2)
+    across = swapped(along, "tok", 1)
     mine = call(
-        functools.partial(stack_kernel, order),
+        functools.partial(stack_kernel, (*order, *(m + 1 for m in order))),
         jax.ShapeDtypeStruct((tokens, model // 2), bf16),
-        [ANY] + [VMEM] * (members // 2 + 2),
-        (down_z, *[along[m] for m in (*first, *second)], *crossed),
-    )
-    downs = [downs[0], down_x, down_z, down_xz]
+        [ANY, VMEM, VMEM],
+        (down_z, along, across),
+    )
     other = swapped(mine, "grp", 1)
 
     hidden = call(
         hidden_kernel,
         jax.ShapeDtypeStruct((depth + TILE, tokens), bf16),
-        [ANY] + [VMEM] * 5,
-        (down_xz, mine, other, gate_weight, up_weight, route_weight),
+        [VMEM] * 5,
+        (mine, other, gate_weight, up_weight, route_weight),
     )
     hiddens = [swapped(hidden, "tok", m) if m else hidden for m in range(HOLDERS)]
     entries = tokens * tokens // LANES
@@ -264,8 +257,8 @@
         features_kernel,
         [jax.ShapeDtypeStruct((token_part, part), bf16)] * HOLDERS
         + [jax.ShapeDtypeStruct((entries, LANES), bf16)],
-        [VMEM] * (2 * HOLDERS),
-        (*hiddens, *downs),
+        [VMEM] * (HOLDERS + 3),
+        (*hiddens, down_own, down_x, down_z),
         scratch=[pltpu.VMEM((tokens, LANES), f32), pltpu.VMEM((tokens, part), bf16)],
     )
     arrived = lax.all_to_all(centered, ("grp", "tok"), split_axis=0, concat_axis=0, tiled=True)

time: 62.5 us -> 62.8 us (level)
  waiting for transfers between devices: 28.7 us -> 30.6 us
  starting transfers between devices: 26.8 us -> 25.2 us
    ppermute x15 -> x13, starting transfers between devices: 19.5 us -> 16.8 us  [swapped(): lax.ppermute(array, axis, [(i, i ^ mask) for i in range(lax.axis_size(axi...]
    ppermute x15 -> x13, waiting for transfers between devices: 17.5 us -> 19.4 us  [swapped(): lax.ppermute(array, axis, [(i, i ^ mask) for i in range(lax.axis_size(axi...]
    all_to_all x1, starting transfers between devices: 4.72 us -> 5.78 us  [shards(): lax.all_to_all(centered, ('grp', 'tok'), split_axis=0, concat_axis=0, til...]
    pallas_call x10 -> x9, Pallas kernels: 5.97 us -> 5.98 us  [call(): pl.pallas_call(body, out_shape=outs, in_specs=in_specs, out_specs=jax.tre...]
  transfers between devices with their start and end apart: 17 -> 15, of which waited for: 10 -> 9; matrix products, arithmetic and copies ran while one was open for 0% -> 0% of each run, Pallas kernels for 3% -> 2%
where the time goes in v6:
time: 62.8 us; the launch traced here: 62.5 us
  waiting for transfers between devices  30.6 us (49%)
  starting transfers between devices  25.2 us (40%)
  Pallas kernels  5.98 us (10%)
  between operations  0.76 us (1%)
    ppermute x13, waiting for transfers between devices, swapped(): lax.ppermute(array, axis, [(i, i ^ mask) for i in range(lax.axis_size(axi...  19.4 us
    ppermute x13, starting transfers between devices, swapped(): lax.ppermute(array, axis, [(i, i ^ mask) for i in range(lax.axis_size(axi...  16.8 us
    all_to_all x1, waiting for transfers between devices, shards(): lax.all_to_all(tables, ('grp', 'tok'), split_axis=0, concat_axis=0, tiled...  6.96 us
    pallas_call x9, Pallas kernels, call(): pl.pallas_call(body, out_shape=outs, in_specs=in_specs, out_specs=jax.tre...  5.98 us
    all_to_all x1, starting transfers between devices, shards(): lax.all_to_all(centered, ('grp', 'tok'), split_axis=0, concat_axis=0, til...  5.78 us
    all_to_all x1, waiting for transfers between devices, shards(): lax.all_to_all(centered, ('grp', 'tok'), split_axis=0, concat_axis=0, til...  4.19 us
    all_to_all x1, starting transfers between devices, shards(): lax.all_to_all(tables, ('grp', 'tok'), split_axis=0, concat_axis=0, tiled...  2.56 us
  transfers between devices with their start and end apart: 15, of which 9 were waited for; matrix products, arithmetic and copies ran while one was open for 0% of the time, Pallas kernels for 2%

profile of v6, /device:TPU:0, one launch (start us, length us, event | category | flops | bytes accessed | tf_op | source)
XLA Modules:
  0.0 62.5 jit_solution(6838157816610769949)
XLA Ops:
  0.6 1.3 %shard_map.77 = (bf16[32,1024]{1,0:T(8,128)(2,1)S(1)}, bf16[192,512]{1,0:T(8,128)(2,1)S(1)}, bf16[192,512]{1,0:T(8,128)(2,1)S(1)}, bf16[384,512]{1,0:T(8,128)(2,1)S(1)}) custom-call(bf16[32,2048]{1,0:T(8,128)(2,1)} %states_hbm.1, f32[1,2048]{1,0:T(1,128)} %bitcast.4, bf16[192,2048]{1,0:T(8,128)(2,1)} %down_hbm.1), custom_call_target="tpu_custom_call" | custom-call | tf_op jit(solution)/shard_map/pallas_call | solution.py:31
  2.0 3.0 %collective-permute-start = (bf16[384,512]{1,0:T(8,128)(2,1)S(1)}, bf16[384,512]{1,0:T(8,128)(2,1)S(1)}, u32[]{:S(2)}, u32[]{:S(2)}) collective-permute-start(bf16[384,512]{1,0:T(8,128)(2,1)S(1)} %get-tuple-element.11), channel_id=1, source_target_pairs={{0,1},{1,0},{2,3},{3,2},{4,5},{5,4},{6,7},{7,6},{8,9},{9,8},{10,11... | collective-permute-start | bytes 1179656 | tf_op jit(solution)/shard_map/ppermute | solution.py:23
  5.0 1.6 %collective-permute-start.3 = (bf16[32,1024]{1,0:T(8,128)(2,1)S(1)}, bf16[32,1024]{1,0:T(8,128)(2,1)S(1)}, u32[]{:S(2)}, u32[]{:S(2)}) collective-permute-start(bf16[32,1024]{1,0:T(8,128)(2,1)S(1)} %get-tuple-element.12.refs_0_), channel_id=1, source_target_pairs={{0,2},{1,3},{2,0},{3,1},{4,6},{5,7},{6,4},{7,5},{8,10},{9,11},{10,... | collective-permute-start | bytes 196616 | tf_op jit(solution)/shard_map/ppermute | solution.py:23
  6.5 2.6 %collective-permute-start.2 = (bf16[32,1024]{1,0:T(8,128)(2,1)S(1)}, bf16[32,1024]{1,0:T(8,128)(2,1)S(1)}, u32[]{:S(2)}, u32[]{:S(2)}) collective-permute-start(bf16[32,1024]{1,0:T(8,128)(2,1)S(1)} %get-tuple-element.12.refs_0_), channel_id=1, source_target_pairs={{0,4},{1,5},{2,6},{3,7},{4,0},{5,1},{6,2},{7,3},{8,12},{9,13},{10,... | collective-permute-start | bytes 196616 | tf_op jit(solution)/shard_map/ppermute | solution.py:23
  9.1 0.2 collective-permute-start.1
  9.4 0.0 collective-permute-done.3.refs_3_
  9.4 4.2 %collective-permute-done.2.refs_2_ = bf16[32,1024]{1,0:T(8,128)(2,1)S(1)} collective-permute-done((bf16[32,1024]{1,0:T(8,128)(2,1)S(1)}, bf16[32,1024]{1,0:T(8,128)(2,1)S(1)}, u32[]{:S(2)}, u32[]{:S(2)}) %collective-permute-start.2) | collective-permute-done | bytes 65568 | tf_op jit(solution)/shard_map/ppermute | solution.py:23
  13.5 1.7 %collective-permute-done.1.refs_1_ = bf16[32,1024]{1,0:T(8,128)(2,1)S(1)} collective-permute-done((bf16[32,1024]{1,0:T(8,128)(2,1)S(1)}, bf16[32,1024]{1,0:T(8,128)(2,1)S(1)}, u32[]{:S(2)}, u32[]{:S(2)}) %collective-permute-start.1) | collective-permute-done | bytes 65568 | tf_op jit(solution)/shard_map/ppermute | solution.py:23
  15.2 0.0 collective-permute-done.after_ref.got_ref.refs_5_
  15.2 0.0 copy-start.1
  15.3 0.0 copy-start
  15.3 0.0 copy-start.2
  15.3 0.8 %collective-permute-start.4 = (bf16[384,512]{1,0:T(8,128)(2,1)S(1)}, bf16[384,512]{1,0:T(8,128)(2,1)S(1)}, u32[]{:S(2)}, u32[]{:S(2)}) collective-permute-start(bf16[384,512]{1,0:T(8,128)(2,1)S(1)} %shard_map.79), channel_id=1, source_target_pairs={{0,2},{1,3},{2,0},{3,1},{4,6},{5,7},{6,4},{7,5},{8,10},{9,11},{10,... | collective-permute-start | bytes 1179656 | tf_op jit(solution)/shard_map/ppermute | solution.py:23
  16.1 1.5 %collective-permute-start.5 = (bf16[128,1024]{1,0:T(8,128)(2,1)S(1)}, bf16[128,1024]{1,0:T(8,128)(2,1)S(1)}, u32[]{:S(2)}, u32[]{:S(2)}) collective-permute-start(bf16[128,1024]{1,0:T(8,128)(2,1)S(1)} %shard_map.78.after_ref.refs_1_), channel_id=1, source_target_pairs={{0,1},{1,0},{2,3},{3,2},{4,5},{5,4},{6,7},{7,6},{8,9},{9,8},{10,11... | collective-permute-start | bytes 786440 | tf_op jit(solution)/shard_map/ppermute | solution.py:23
  17.6 5.4 %collective-permute-done.5.refs_2_ = bf16[128,1024]{1,0:T(8,128)(2,1)S(1)} collective-permute-done((bf16[128,1024]{1,0:T(8,128)(2,1)S(1)}, bf16[128,1024]{1,0:T(8,128)(2,1)S(1)}, u32[]{:S(2)}, u32[]{:S(2)}) %collective-permute-start.5) | collective-permute-done | bytes 262176 | tf_op jit(solution)/shard_map/ppermute | solution.py:23
  23.0 1.6 %collective-permute-done.4.refs_0_.refs_6_ = bf16[384,512]{1,0:T(8,128)(2,1)S(1)} collective-permute-done((bf16[384,512]{1,0:T(8,128)(2,1)S(1)}, bf16[384,512]{1,0:T(8,128)(2,1)S(1)}, u32[]{:S(2)}, u32[]{:S(2)}) %collective-permute-start.4) | collective-permute-done | bytes 393248 | tf_op jit(solution)/shard_map/ppermute | solution.py:23
  24.6 0.1 collective-permute-start.6
  24.7 1.9 %collective-permute-done.6.other_ref = bf16[256,1024]{1,0:T(8,128)(2,1)S(1)} collective-permute-done((bf16[256,1024]{1,0:T(8,128)(2,1)S(1)}, bf16[256,1024]{1,0:T(8,128)(2,1)S(1)}, u32[]{:S(2)}, u32[]{:S(2)}) %collective-permute-start.6) | collective-permute-done | bytes 524320 | tf_op jit(solution)/shard_map/ppermute | solution.py:23
  26.6 0.0 copy-done.1
  26.6 0.0 copy-done
  26.6 0.0 copy-done.2
  26.6 0.9 %shard_map.81.refs_0_ = bf16[208,256]{1,0:T(8,128)(2,1)S(1)} custom-call(bf16[256,1024]{1,0:T(8,128)(2,1)S(1)} %shard_map.80.mine_ref, bf16[256,1024]{1,0:T(8,128)(2,1)S(1)} %collective-permute-done.6.other_ref, bf16[192,2048]{1,0:T(8,128)(2,1)S(1)} %copy-done, bf16[192,2048]{1,0:T(8,128)(2,1)S(1)} %copy-done.1, f32[1,64]{1,0:T(1,128)S(1)} %copy-done.2), custom_call_target="tpu_custom_call" | custom-call | tf_op jit(solution)/shard_map/pallas_call | solution.py:31
  27.5 2.5 %collective-permute-start.9 = (bf16[208,256]{1,0:T(8,128)(2,1)S(1)}, bf16[208,256]{1,0:T(8,128)(2,1)S(1)}, u32[]{:S(2)}, u32[]{:S(2)}) collective-permute-start(bf16[208,256]{1,0:T(8,128)(2,1)S(1)} %shard_map.81.refs_0_), channel_id=1, source_target_pairs={{0,3},{1,2},{2,1},{3,0},{4,7},{5,6},{6,5},{7,4},{8,11},{9,10},{10,... | collective-permute-start | bytes 319496 | tf_op jit(solution)/shard_map/ppermute | solution.py:23
  30.0 0.4 collective-permute-start.8
  30.4 0.6 collective-permute-start.7
  31.0 3.2 %collective-permute-done.9.refs_3_ = bf16[208,256]{1,0:T(8,128)(2,1)S(1)} collective-permute-done((bf16[208,256]{1,0:T(8,128)(2,1)S(1)}, bf16[208,256]{1,0:T(8,128)(2,1)S(1)}, u32[]{:S(2)}, u32[]{:S(2)}) %collective-permute-start.9) | collective-permute-done | bytes 106528 | tf_op jit(solution)/shard_map/ppermute | solution.py:23
  34.2 1.4 %collective-permute-done.8.refs_2_ = bf16[208,256]{1,0:T(8,128)(2,1)S(1)} collective-permute-done((bf16[208,256]{1,0:T(8,128)(2,1)S(1)}, bf16[208,256]{1,0:T(8,128)(2,1)S(1)}, u32[]{:S(2)}, u32[]{:S(2)}) %collective-permute-start.8) | collective-permute-done | bytes 106528 | tf_op jit(solution)/shard_map/ppermute | solution.py:23
  35.7 0.0 collective-permute-done.7.refs_1_
  35.7 1.4 %shard_map.82 = (bf16[64,512]{1,0:T(8,128)(2,1)S(1)}, bf16[64,512]{1,0:T(8,128)(2,1)S(1)}, bf16[64,512]{1,0:T(8,128)(2,1)S(1)}, bf16[64,512]{1,0:T(8,128)(2,1)S(1)}, bf16[512,128]{1,0:T(8,128)(2,1)}) custom-call(bf16[208,256]{1,0:T(8,128)(2,1)S(1)} %shard_map.81.refs_0_, bf16[208,256]{1,0:T(8,128)(2,1)S(1)} %collective-permute-done.7.refs_1_, ...), custom_call_target="tpu_custom_call" | custom-call | tf_op jit(solution)/shard_map/pallas_call | solution.py:31
  37.2 5.8 %all-to-all-start = ((bf16[32,16,128]{2,1,0:T(8,128)(2,1)}), bf16[32,16,128]{2,1,0:T(8,128)(2,1)S(1)}, u32[]{:S(2)}, u32[]{:S(2)}) async-start(bf16[32,16,128]{2,1,0:T(8,128)(2,1)} %bitcast.1), calls=%async_computation | async-start | bytes 262144 | tf_op jit(solution)/shard_map/all_to_all | solution.py:264
  42.9 1.8 %collective-permute-start.10 = (bf16[64,512]{1,0:T(8,128)(2,1)S(1)}, bf16[64,512]{1,0:T(8,128)(2,1)S(1)}, u32[]{:S(2)}, u32[]{:S(2)}) collective-permute-start(bf16[64,512]{1,0:T(8,128)(2,1)S(1)} %get-tuple-element.16), channel_id=1, source_target_pairs={{0,1},{1,0},{2,3},{3,2},{4,5},{5,4},{6,7},{7,6},{8,9},{9,8},{10,11... | collective-permute-start | bytes 196616 | tf_op jit(solution)/shard_map/ppermute | solution.py:23
  44.8 1.5 %collective-permute-start.11 = (bf16[64,512]{1,0:T(8,128)(2,1)S(1)}, bf16[64,512]{1,0:T(8,128)(2,1)S(1)}, u32[]{:S(2)}, u32[]{:S(2)}) collective-permute-start(bf16[64,512]{1,0:T(8,128)(2,1)S(1)} %get-tuple-element.17), channel_id=1, source_target_pairs={{0,2},{1,3},{2,0},{3,1},{4,6},{5,7},{6,4},{7,5},{8,10},{9,11},{10,... | collective-permute-start | bytes 196616 | tf_op jit(solution)/shard_map/ppermute | solution.py:23
  46.2 0.3 collective-permute-start.12
  46.5 4.2 %all-to-all-done = bf16[32,16,128]{2,1,0:T(8,128)(2,1)S(1)} async-done(((bf16[32,16,128]{2,1,0:T(8,128)(2,1)}), bf16[32,16,128]{2,1,0:T(8,128)(2,1)S(1)}, u32[]{:S(2)}, u32[]{:S(2)}) %all-to-all-start) | async-done | bytes 131104 | tf_op jit(solution)/shard_map/all_to_all | solution.py:264
  50.7 0.8 %shard_map.84 = f32[32,8,8]{2,1,0:T(8,128)} custom-call(bf16[8,4,16,128]{3,2,1,0:T(8,128)(2,1)S(1)} %bitcast.3), custom_call_target="tpu_custom_call" | custom-call | tf_op jit(solution)/shard_map/pallas_call | solution.py:31
  51.5 2.6 %all-to-all-start.1 = ((f32[32,8,8]{2,1,0:T(8,128)}), f32[32,8,8]{2,1,0:T(8,128)S(1)}, u32[]{:S(2)}, u32[]{:S(2)}) async-start(f32[32,8,8]{2,1,0:T(8,128)} %shard_map.84), calls=%async_computation.1 | async-start | bytes 262144 | tf_op jit(solution)/shard_map/all_to_all | solution.py:275
  54.0 0.0 collective-permute-done.10.refs_1_
  54.1 0.0 collective-permute-done.11.refs_2_
  54.1 0.0 collective-permute-done.12.refs_3_
  54.1 0.7 %shard_map.83 = bf16[64,2048]{1,0:T(8,128)(2,1)} custom-call(bf16[64,512]{1,0:T(8,128)(2,1)S(1)} %get-tuple-element.15.refs_0_, bf16[64,512]{1,0:T(8,128)(2,1)S(1)} %collective-permute-done.10.refs_1_, bf16[64,512]{1,0:T(8,128)(2,1)S(1)} %collective-permute-done.11.refs_2_, bf16[64,512]{1,0:T(8,128)(2,1)S(1)} %collective-permute-done.12.refs_3_), custom_call_target="tpu_custom_call" | custom-call | tf_op jit(solution)/shard_map/pallas_call | solution.py:31
  54.8 7.0 %all-to-all-done.1.tables_ref = f32[32,8,8]{2,1,0:T(8,128)S(1)} async-done(((f32[32,8,8]{2,1,0:T(8,128)}), f32[32,8,8]{2,1,0:T(8,128)S(1)}, u32[]{:S(2)}, u32[]{:S(2)}) %all-to-all-start.1) | async-done | bytes 8224 | tf_op jit(solution)/shard_map/all_to_all | solution.py:275
  61.8 0.7 %shard_map.85 = f32[8,8]{1,0:T(8,128)} custom-call(f32[32,8,8]{2,1,0:T(8,128)S(1)} %all-to-all-done.1.tables_ref), custom_call_target="tpu_custom_call" | custom-call | tf_op jit(solution)/shard_map/pallas_call | solution.py:31
  (3 shorter events, 0.1 us)
Async XLA Ops:
  2.0 13.2 %collective-permute-start = (bf16[384,512]{1,0:T(8,128)(2,1)S(1)}, bf16[384,512]{1,0:T(8,128)(2,1)S(1)}, u32[]{:S(2)}, u32[]{:S(2)}) collective-permute-start(bf16[384,512]{1,0:T(8,128)(2,1)S(1)} %get-tuple-element.11), channel_id=1, source_target_pairs={{0,1},{1,0},{2,3},{3,2},{4,5},{5,4},{6,7},{7,6},{8,9},{9,8},{10,11... | collective-permute-start | bytes 1179656 | tf_op jit(solution)/shard_map/ppermute | solution.py:23
  5.0 4.4 %collective-permute-start.3 = (bf16[32,1024]{1,0:T(8,128)(2,1)S(1)}, bf16[32,1024]{1,0:T(8,128)(2,1)S(1)}, u32[]{:S(2)}, u32[]{:S(2)}) collective-permute-start(bf16[32,1024]{1,0:T(8,128)(2,1)S(1)} %get-tuple-element.12.refs_0_), channel_id=1, source_target_pairs={{0,2},{1,3},{2,0},{3,1},{4,6},{5,7},{6,4},{7,5},{8,10},{9,11},{10,... | collective-permute-start | bytes 196616 | tf_op jit(solution)/shard_map/ppermute | solution.py:23
  6.5 7.0 %collective-permute-start.2 = (bf16[32,1024]{1,0:T(8,128)(2,1)S(1)}, bf16[32,1024]{1,0:T(8,128)(2,1)S(1)}, u32[]{:S(2)}, u32[]{:S(2)}) collective-permute-start(bf16[32,1024]{1,0:T(8,128)(2,1)S(1)} %get-tuple-element.12.refs_0_), channel_id=1, source_target_pairs={{0,4},{1,5},{2,6},{3,7},{4,0},{5,1},{6,2},{7,3},{8,12},{9,13},{10,... | collective-permute-start | bytes 196616 | tf_op jit(solution)/shard_map/ppermute | solution.py:23
  9.1 6.1 %collective-permute-start.1 = (bf16[32,1024]{1,0:T(8,128)(2,1)S(1)}, bf16[32,1024]{1,0:T(8,128)(2,1)S(1)}, u32[]{:S(2)}, u32[]{:S(2)}) collective-permute-start(bf16[32,1024]{1,0:T(8,128)(2,1)S(1)} %get-tuple-element.12.refs_0_), channel_id=1, source_target_pairs={{0,6},{1,7},{2,4},{3,5},{4,2},{5,3},{6,0},{7,1},{8,14},{9,15},{10,... | collective-permute-start | bytes 196616 | tf_op jit(solution)/shard_map/ppermute | solution.py:23
  15.2 11.4 %copy-start.1 = (bf16[192,2048]{1,0:T(8,128)(2,1)S(1)}, bf16[192,2048]{1,0:T(8,128)(2,1)}, u32[]{:S(2)}) copy-start(bf16[192,2048]{1,0:T(8,128)(2,1)} %up_ref.1) | copy-start | bytes 2359300
  15.3 11.3 %copy-start = (bf16[192,2048]{1,0:T(8,128)(2,1)S(1)}, bf16[192,2048]{1,0:T(8,128)(2,1)}, u32[]{:S(2)}) copy-start(bf16[192,2048]{1,0:T(8,128)(2,1)} %gate_ref.1) | copy-start | bytes 2359300
  15.3 11.3 %copy-start.2 = (f32[1,64]{1,0:T(1,128)S(1)}, f32[1,64]{1,0:T(1,128)}, u32[]{:S(2)}) copy-start(f32[1,64]{1,0:T(1,128)} %route_ref.1) | copy-start | bytes 772
  15.3 9.2 %collective-permute-start.4 = (bf16[384,512]{1,0:T(8,128)(2,1)S(1)}, bf16[384,512]{1,0:T(8,128)(2,1)S(1)}, u32[]{:S(2)}, u32[]{:S(2)}) collective-permute-start(bf16[384,512]{1,0:T(8,128)(2,1)S(1)} %shard_map.79), channel_id=1, source_target_pairs={{0,2},{1,3},{2,0},{3,1},{4,6},{5,7},{6,4},{7,5},{8,10},{9,11},{10,... | collective-permute-start | bytes 1179656 | tf_op jit(solution)/shard_map/ppermute | solution.py:23
  16.1 6.9 %collective-permute-start.5 = (bf16[128,1024]{1,0:T(8,128)(2,1)S(1)}, bf16[128,1024]{1,0:T(8,128)(2,1)S(1)}, u32[]{:S(2)}, u32[]{:S(2)}) collective-permute-start(bf16[128,1024]{1,0:T(8,128)(2,1)S(1)} %shard_map.78.after_ref.refs_1_), channel_id=1, source_target_pairs={{0,1},{1,0},{2,3},{3,2},{4,5},{5,4},{6,7},{7,6},{8,9},{9,8},{10,11... | collective-permute-start | bytes 786440 | tf_op jit(solution)/shard_map/ppermute | solution.py:23
  24.6 2.0 %collective-permute-start.6 = (bf16[256,1024]{1,0:T(8,128)(2,1)S(1)}, bf16[256,1024]{1,0:T(8,128)(2,1)S(1)}, u32[]{:S(2)}, u32[]{:S(2)}) collective-permute-start(bf16[256,1024]{1,0:T(8,128)(2,1)S(1)} %shard_map.80.mine_ref), channel_id=1, source_target_pairs={{0,8},{8,0},{16,24},{24,16},{1,9},{9,1},{17,25},{25,17},{2,10},{10... | collective-permute-start | bytes 1572872 | tf_op jit(solution)/shard_map/ppermute | solution.py:23
  27.5 6.8 %collective-permute-start.9 = (bf16[208,256]{1,0:T(8,128)(2,1)S(1)}, bf16[208,256]{1,0:T(8,128)(2,1)S(1)}, u32[]{:S(2)}, u32[]{:S(2)}) collective-permute-start(bf16[208,256]{1,0:T(8,128)(2,1)S(1)} %shard_map.81.refs_0_), channel_id=1, source_target_pairs={{0,3},{1,2},{2,1},{3,0},{4,7},{5,6},{6,5},{7,4},{8,11},{9,10},{10,... | collective-permute-start | bytes 319496 | tf_op jit(solution)/shard_map/ppermute | solution.py:23
  30.0 5.7 %collective-permute-start.8 = (bf16[208,256]{1,0:T(8,128)(2,1)S(1)}, bf16[208,256]{1,0:T(8,128)(2,1)S(1)}, u32[]{:S(2)}, u32[]{:S(2)}) collective-permute-start(bf16[208,256]{1,0:T(8,128)(2,1)S(1)} %shard_map.81.refs_0_), channel_id=1, source_target_pairs={{0,2},{1,3},{2,0},{3,1},{4,6},{5,7},{6,4},{7,5},{8,10},{9,11},{10,... | collective-permute-start | bytes 319496 | tf_op jit(solution)/shard_map/ppermute | solution.py:23
  30.4 5.3 %collective-permute-start.7 = (bf16[208,256]{1,0:T(8,128)(2,1)S(1)}, bf16[208,256]{1,0:T(8,128)(2,1)S(1)}, u32[]{:S(2)}, u32[]{:S(2)}) collective-permute-start(bf16[208,256]{1,0:T(8,128)(2,1)S(1)} %shard_map.81.refs_0_), channel_id=1, source_target_pairs={{0,1},{1,0},{2,3},{3,2},{4,5},{5,4},{6,7},{7,6},{8,9},{9,8},{10,11... | collective-permute-start | bytes 319496 | tf_op jit(solution)/shard_map/ppermute | solution.py:23
  37.2 13.5 %all-to-all-start = ((bf16[32,16,128]{2,1,0:T(8,128)(2,1)}), bf16[32,16,128]{2,1,0:T(8,128)(2,1)S(1)}, u32[]{:S(2)}, u32[]{:S(2)}) async-start(bf16[32,16,128]{2,1,0:T(8,128)(2,1)} %bitcast.1), calls=%async_computation | async-start | bytes 262144 | tf_op jit(solution)/shard_map/all_to_all | solution.py:264
  42.9 11.1 %collective-permute-start.10 = (bf16[64,512]{1,0:T(8,128)(2,1)S(1)}, bf16[64,512]{1,0:T(8,128)(2,1)S(1)}, u32[]{:S(2)}, u32[]{:S(2)}) collective-permute-start(bf16[64,512]{1,0:T(8,128)(2,1)S(1)} %get-tuple-element.16), channel_id=1, source_target_pairs={{0,1},{1,0},{2,3},{3,2},{4,5},{5,4},{6,7},{7,6},{8,9},{9,8},{10,11... | collective-permute-start | bytes 196616 | tf_op jit(solution)/shard_map/ppermute | solution.py:23
  44.8 9.3 %collective-permute-start.11 = (bf16[64,512]{1,0:T(8,128)(2,1)S(1)}, bf16[64,512]{1,0:T(8,128)(2,1)S(1)}, u32[]{:S(2)}, u32[]{:S(2)}) collective-permute-start(bf16[64,512]{1,0:T(8,128)(2,1)S(1)} %get-tuple-element.17), channel_id=1, source_target_pairs={{0,2},{1,3},{2,0},{3,1},{4,6},{5,7},{6,4},{7,5},{8,10},{9,11},{10,... | collective-permute-start | bytes 196616 | tf_op jit(solution)/shard_map/ppermute | solution.py:23
  46.2 7.8 %collective-permute-start.12 = (bf16[64,512]{1,0:T(8,128)(2,1)S(1)}, bf16[64,512]{1,0:T(8,128)(2,1)S(1)}, u32[]{:S(2)}, u32[]{:S(2)}) collective-permute-start(bf16[64,512]{1,0:T(8,128)(2,1)S(1)} %get-tuple-element.18), channel_id=1, source_target_pairs={{0,3},{1,2},{2,1},{3,0},{4,7},{5,6},{6,5},{7,4},{8,11},{9,10},{10,... | collective-permute-start | bytes 196616 | tf_op jit(solution)/shard_map/ppermute | solution.py:23
  51.5 10.3 %all-to-all-start.1 = ((f32[32,8,8]{2,1,0:T(8,128)}), f32[32,8,8]{2,1,0:T(8,128)S(1)}, u32[]{:S(2)}, u32[]{:S(2)}) async-start(f32[32,8,8]{2,1,0:T(8,128)} %shard_map.84), calls=%async_computation.1 | async-start | bytes 262144 | tf_op jit(solution)/shard_map/all_to_all | solution.py:275

commit v7 on v6

--- a/solution.py
+++ b/solution.py
@@ -1,5 +1,3 @@
-import functools
-
 import jax
 import jax.numpy as jnp
 from jax import lax
@@ -76,42 +74,26 @@
     out_ref[depth:] = got_ref[depth:]
 
 
-def stack_kernel(order, *refs):
-    pieces, out_ref = refs[1:-1], refs[-1]
-    rows = out_ref.shape[0] // lax.axis_size("tok")
-    count = 0
-    for piece in pieces:
-        for at in range(piece.shape[0] // rows):
-            place = lax.axis_index("tok") ^ order[count]
-            out_ref[pl.ds(pl.multiple_of(place * rows, rows), rows)] = piece[
-                at * rows : (at + 1) * rows
-            ]
-            count += 1
-
-
-def pair_up_kernel(after_ref, *refs):
+def stack_kernel(after_ref, *refs):
     rows = refs[0].shape[0]
-    for at, ref in enumerate(refs[:-1]):
-        refs[-1][at * rows : (at + 1) * rows] = ref[...]
-
-
-def together(pieces, after):
-    rows, width = pieces[0].shape
-    out = jax.ShapeDtypeStruct((rows * len(pieces), width), bf16)
-    return call(pair_up_kernel, out, [ANY] + [VMEM] * len(pieces), (after, *pieces))
-
-
-def hidden_kernel(mine_ref, other_ref, gate_ref, up_ref, route_ref, out_ref):
-    tokens, width = mine_ref.shape
-    gate, upward = [
-        sum(
-            dot_f32(ref[:, pl.ds(pl.multiple_of(half * width, width), width)], block[...], TRANSPOSED)
-            for half, block in ((core(), mine_ref), (1 - core(), other_ref))
-        )
-        for ref in (gate_ref, up_ref)
-    ]
-    depth = gate.shape[0]
-    out_ref[:depth] = (gate / (1.0 + jnp.exp(-gate)) * upward).astype(bf16)
+    z = lax.axis_index("tok") >> 1
+    for m, piece in enumerate(refs[:-1]):
+        refs[-1][pl.ds(pl.multiple_of((z ^ m) * rows, rows), rows)] = piece[...]
+
+
+def hidden_kernel(after_ref, near_ref, far_ref, near2_ref, far2_ref, gate_ref, up_ref, route_ref, out_ref):
+    count, width = near_ref.shape
+    depth = gate_ref.shape[0]
+    x = lax.axis_index("tok") & 1
+    own = pl.ds(pl.multiple_of(core() * width, width), width)
+    rest = pl.ds(pl.multiple_of((1 - core()) * width, width), width)
+    for at, block, block2 in ((x, near_ref[...], near2_ref[...]), (1 - x, far_ref[...], far2_ref[...])):
+        gate, upward = [
+            dot_f32(ref[:, own], block, TRANSPOSED) + dot_f32(ref[:, rest], block2, TRANSPOSED)
+            for ref in (gate_ref, up_ref)
+        ]
+        place = pl.ds(pl.multiple_of(at * count, count), count)
+        out_ref[:depth, place] = (gate / (1.0 + jnp.exp(-gate)) * upward).astype(bf16)
     route = route_ref[...]
     high = route.astype(bf16).astype(f32)
     middle = (route - high).astype(bf16).astype(f32)
@@ -119,7 +101,7 @@
     part = route.shape[1]
     row = lax.broadcasted_iota(jnp.int32, (TILE, part), 0)
     terms = jnp.where(row == 0, high, jnp.where(row == 1, middle, jnp.where(row == 2, low, 0.0)))
-    terms = jnp.concatenate([terms, jnp.zeros((TILE, tokens - part), f32)], 1)
+    terms = jnp.concatenate([terms, jnp.zeros((TILE, 2 * count - part), f32)], 1)
     out_ref[depth:] = terms.astype(bf16)
 
 
@@ -128,8 +110,14 @@
     block_refs, centered_ref = refs[HOLDERS + 3 : 2 * HOLDERS + 3], refs[2 * HOLDERS + 3]
     route_ref, features_ref = refs[2 * HOLDERS + 4 :]
     depth, tokens = own_ref.shape[0], hidden_refs[0].shape[1]
+    part, members = tokens // HOLDERS, lax.axis_size("tok")
+    rows = tokens // members
     downs = (own_ref[...], x_ref[:depth], z_ref[:depth], z_ref[depth:])
-    part = tokens // HOLDERS
+
+    def place(m, piece):
+        z = (holder() ^ m) * (members // HOLDERS // 2) + piece // 2
+        return pl.ds(pl.multiple_of(piece % 2 * (tokens // 2) + z * rows, rows), rows)
+
     eye = lax.broadcasted_iota(jnp.int32, (part, part), 0) == lax.broadcasted_iota(
         jnp.int32, (part, part), 1
     )
@@ -140,8 +128,9 @@
         terms = hidden_ref[depth:, :part].astype(f32)
         route = jnp.sum(terms[:HOLDERS], axis=0, keepdims=True)
         column = jnp.sum(jnp.where(eye, route, 0.0), axis=1, keepdims=True)
-        place = pl.multiple_of((holder() ^ m) * part, part)
-        route_ref[pl.ds(place, part)] = jnp.broadcast_to(column, (part, LANES))
+        column = jnp.broadcast_to(column, (part, LANES))
+        for piece in range(part // rows):
+            route_ref[place(m, piece)] = column[piece * rows : (piece + 1) * rows]
     features = (output * route_ref[:, :1]).astype(bf16)
     features_ref[...] = features
     wide = features.astype(f32)
@@ -158,7 +147,8 @@
             ]
             at += 1
     for m, block_ref in enumerate(block_refs):
-        block_ref[...] = features_ref[pl.ds(pl.multiple_of((holder() ^ m) * part, part), part)]
+        for piece in range(part // rows):
+            block_ref[piece * rows : (piece + 1) * rows] = features_ref[place(m, piece)]
 
 
 def place_kernel(*refs):
@@ -226,30 +216,35 @@
         ],
     )
     down_x = swapped(down_x, "tok", 1)
-    order = (0, *range(members - 2, 0, -2))
-    along = [swapped(own, "tok", m) if m else own for m in order]
-    along = together(along, down_x)
+    pieces = [swapped(own, "tok", 2 * m) if m else own for m in range(members // 2)]
+    near = call(
+        stack_kernel,
+        jax.ShapeDtypeStruct((tokens // 2, model // 2), bf16),
+        [ANY] + [VMEM] * len(pieces),
+        (down_x, *pieces),
+    )
     down_z = call(
         onward_kernel,
         jax.ShapeDtypeStruct(down_x.shape, bf16),
         [ANY, VMEM, VMEM],
-        (along, down_z, down_x),
-    )
+        (near, down_z, down_x),
+    )
+    far = swapped(near, "tok", 1)
     down_z = swapped(down_z, "tok", 2)
-    across = swapped(along, "tok", 1)
-    mine = call(
-        functools.partial(stack_kernel, (*order, *(m + 1 for m in order))),
-        jax.ShapeDtypeStruct((tokens, model // 2), bf16),
-        [ANY, VMEM, VMEM],
-        (down_z, along, across),
-    )
-    other = swapped(mine, "grp", 1)
-
     hidden = call(
         hidden_kernel,
         jax.ShapeDtypeStruct((depth + TILE, tokens), bf16),
-        [VMEM] * 5,
-        (mine, other, gate_weight, up_weight, route_weight),
+        [ANY] + [VMEM] * 7,
+        (
+            down_z,
+            near,
+            far,
+            swapped(near, "grp", 1),
+            swapped(far, "grp", 1),
+            gate_weight,
+            up_weight,
+            route_weight,
+        ),
     )
     hiddens = [swapped(hidden, "tok", m) if m else hidden for m in range(HOLDERS)]
     entries = tokens * tokens // LANES

time: 62.8 us -> 59.8 us (0.952)
  starting transfers between devices: 25.2 us -> 23.4 us
  waiting for transfers between devices: 30.6 us -> 29.4 us
    all_to_all x1, starting transfers between devices: 5.78 us -> 3.97 us  [shards(): lax.all_to_all(centered, ('grp', 'tok'), split_axis=0, concat_axis=0, til...]
    ppermute x13 -> x14, waiting for transfers between devices: 19.4 us -> 18.2 us  [swapped(): lax.ppermute(array, axis, [(i, i ^ mask) for i in range(lax.axis_size(axi...]
    pallas_call x9 -> x8, Pallas kernels: 5.98 us -> 6.09 us  [call(): pl.pallas_call(body, out_shape=outs, in_specs=in_specs, out_specs=jax.tre...]
    ppermute x13 -> x14, starting transfers between devices: 16.8 us -> 16.8 us  [swapped(): lax.ppermute(array, axis, [(i, i ^ mask) for i in range(lax.axis_size(axi...]
  transfers between devices with their start and end apart: 15 -> 16, of which waited for: 9 -> 9; matrix products, arithmetic and copies ran while one was open for 0% -> 0% of each run, Pallas kernels for 2% -> 3%
where the time goes in v7:
time: 59.8 us; the launch traced here: 59.6 us
  waiting for transfers between devices  29.4 us (49%)
  starting transfers between devices  23.4 us (39%)
  Pallas kernels  6.09 us (10%)
  between operations  0.73 us (1%)
    ppermute x14, waiting for transfers between devices, swapped(): lax.ppermute(array, axis, [(i, i ^ mask) for i in range(lax.axis_size(axi...  18.2 us
    ppermute x14, starting transfers between devices, swapped(): lax.ppermute(array, axis, [(i, i ^ mask) for i in range(lax.axis_size(axi...  16.8 us
    all_to_all x1, waiting for transfers between devices, shards(): lax.all_to_all(tables, ('grp', 'tok'), split_axis=0, concat_axis=0, tiled...  6.96 us
    pallas_call x8, Pallas kernels, call(): pl.pallas_call(body, out_shape=outs, in_specs=in_specs, out_specs=jax.tre...  6.09 us
    all_to_all x1, waiting for transfers between devices, shards(): lax.all_to_all(centered, ('grp', 'tok'), split_axis=0, concat_axis=0, til...  4.19 us
    all_to_all x1, starting transfers between devices, shards(): lax.all_to_all(centered, ('grp', 'tok'), split_axis=0, concat_axis=0, til...  3.97 us
    all_to_all x1, starting transfers between devices, shards(): lax.all_to_all(tables, ('grp', 'tok'), split_axis=0, concat_axis=0, tiled...  2.56 us
  transfers between devices with their start and end apart: 16, of which 9 were waited for; matrix products, arithmetic and copies ran while one was open for 0% of the time, Pallas kernels for 3%

profile of v7, /device:TPU:0, one launch (start us, length us, event | category | flops | bytes accessed | tf_op | source)
XLA Modules:
  0.0 59.6 jit_solution(13817694946847668546)
XLA Ops:
  0.6 1.3 %shard_map.77 = (bf16[32,1024]{1,0:T(8,128)(2,1)S(1)}, bf16[192,512]{1,0:T(8,128)(2,1)S(1)}, bf16[192,512]{1,0:T(8,128)(2,1)S(1)}, bf16[384,512]{1,0:T(8,128)(2,1)S(1)}) custom-call(bf16[32,2048]{1,0:T(8,128)(2,1)} %states_hbm.1, f32[1,2048]{1,0:T(1,128)} %bitcast.4, bf16[192,2048]{1,0:T(8,128)(2,1)} %down_hbm.1), custom_call_target="tpu_custom_call" | custom-call | tf_op jit(solution)/shard_map/pallas_call | solution.py:29
  2.0 3.0 %collective-permute-start = (bf16[384,512]{1,0:T(8,128)(2,1)S(1)}, bf16[384,512]{1,0:T(8,128)(2,1)S(1)}, u32[]{:S(2)}, u32[]{:S(2)}) collective-permute-start(bf16[384,512]{1,0:T(8,128)(2,1)S(1)} %get-tuple-element.11), channel_id=1, source_target_pairs={{0,1},{1,0},{2,3},{3,2},{4,5},{5,4},{6,7},{7,6},{8,9},{9,8},{10,11... | collective-permute-start | bytes 1179656 | tf_op jit(solution)/shard_map/ppermute | solution.py:21
  5.0 1.6 %collective-permute-start.1 = (bf16[32,1024]{1,0:T(8,128)(2,1)S(1)}, bf16[32,1024]{1,0:T(8,128)(2,1)S(1)}, u32[]{:S(2)}, u32[]{:S(2)}) collective-permute-start(bf16[32,1024]{1,0:T(8,128)(2,1)S(1)} %get-tuple-element.12.refs_0_), channel_id=1, source_target_pairs={{0,2},{1,3},{2,0},{3,1},{4,6},{5,7},{6,4},{7,5},{8,10},{9,11},{10,... | collective-permute-start | bytes 196616 | tf_op jit(solution)/shard_map/ppermute | solution.py:21
  6.5 2.6 %collective-permute-start.2 = (bf16[32,1024]{1,0:T(8,128)(2,1)S(1)}, bf16[32,1024]{1,0:T(8,128)(2,1)S(1)}, u32[]{:S(2)}, u32[]{:S(2)}) collective-permute-start(bf16[32,1024]{1,0:T(8,128)(2,1)S(1)} %get-tuple-element.12.refs_0_), channel_id=1, source_target_pairs={{0,4},{1,5},{2,6},{3,7},{4,0},{5,1},{6,2},{7,3},{8,12},{9,13},{10,... | collective-permute-start | bytes 196616 | tf_op jit(solution)/shard_map/ppermute | solution.py:21
  9.1 0.2 collective-permute-start.3
  9.4 0.0 collective-permute-done.1.refs_1_
  9.4 4.2 %collective-permute-done.2.refs_2_ = bf16[32,1024]{1,0:T(8,128)(2,1)S(1)} collective-permute-done((bf16[32,1024]{1,0:T(8,128)(2,1)S(1)}, bf16[32,1024]{1,0:T(8,128)(2,1)S(1)}, u32[]{:S(2)}, u32[]{:S(2)}) %collective-permute-start.2) | collective-permute-done | bytes 65568 | tf_op jit(solution)/shard_map/ppermute | solution.py:21
  13.5 1.7 %collective-permute-done.3.refs_3_ = bf16[32,1024]{1,0:T(8,128)(2,1)S(1)} collective-permute-done((bf16[32,1024]{1,0:T(8,128)(2,1)S(1)}, bf16[32,1024]{1,0:T(8,128)(2,1)S(1)}, u32[]{:S(2)}, u32[]{:S(2)}) %collective-permute-start.3) | collective-permute-done | bytes 65568 | tf_op jit(solution)/shard_map/ppermute | solution.py:21
  15.2 0.0 collective-permute-done.after_ref.got_ref.refs_5_
  15.2 0.0 copy-start.1
  15.2 0.0 copy-start
  15.2 0.7 %collective-permute-start.5 = (bf16[128,1024]{1,0:T(8,128)(2,1)S(1)}, bf16[128,1024]{1,0:T(8,128)(2,1)S(1)}, u32[]{:S(2)}, u32[]{:S(2)}) collective-permute-start(bf16[128,1024]{1,0:T(8,128)(2,1)S(1)} %shard_map.78.after_ref.near_ref), channel_id=1, source_target_pairs={{0,1},{1,0},{2,3},{3,2},{4,5},{5,4},{6,7},{7,6},{8,9},{9,8},{10,11... | collective-permute-start | bytes 786440 | tf_op jit(solution)/shard_map/ppermute | solution.py:21
  15.9 0.0 copy-start.2
  16.0 1.6 %collective-permute-start.4 = (bf16[384,512]{1,0:T(8,128)(2,1)S(1)}, bf16[384,512]{1,0:T(8,128)(2,1)S(1)}, u32[]{:S(2)}, u32[]{:S(2)}) collective-permute-start(bf16[384,512]{1,0:T(8,128)(2,1)S(1)} %shard_map.79), channel_id=1, source_target_pairs={{0,2},{1,3},{2,0},{3,1},{4,6},{5,7},{6,4},{7,5},{8,10},{9,11},{10,... | collective-permute-start | bytes 1179656 | tf_op jit(solution)/shard_map/ppermute | solution.py:21
  17.6 0.0 collective-permute-start.6
  17.6 4.1 %collective-permute-done.5.far_ref = bf16[128,1024]{1,0:T(8,128)(2,1)S(1)} collective-permute-done((bf16[128,1024]{1,0:T(8,128)(2,1)S(1)}, bf16[128,1024]{1,0:T(8,128)(2,1)S(1)}, u32[]{:S(2)}, u32[]{:S(2)}) %collective-permute-start.5) | collective-permute-done | bytes 262176 | tf_op jit(solution)/shard_map/ppermute | solution.py:21
  21.7 0.0 collective-permute-start.7
  21.7 0.0 collective-permute-done.6.near2_ref
  21.7 4.0 %collective-permute-done.4.after_ref.refs_6_ = bf16[384,512]{1,0:T(8,128)(2,1)S(1)} collective-permute-done((bf16[384,512]{1,0:T(8,128)(2,1)S(1)}, bf16[384,512]{1,0:T(8,128)(2,1)S(1)}, u32[]{:S(2)}, u32[]{:S(2)}) %collective-permute-start.4) | collective-permute-done | bytes 393248 | tf_op jit(solution)/shard_map/ppermute | solution.py:21
  25.7 0.0 collective-permute-done.7.far2_ref
  25.7 0.0 copy-done.1
  25.7 0.0 copy-done
  25.7 0.0 copy-done.2
  25.7 1.0 %shard_map.80.refs_0_ = bf16[208,256]{1,0:T(8,128)(2,1)S(1)} custom-call(bf16[384,512]{1,0:T(8,128)(2,1)S(1)} %collective-permute-done.4.after_ref.refs_6_, bf16[128,1024]{1,0:T(8,128)(2,1)S(1)} %shard_map.78.after_ref.near_ref, bf16[128,1024]{1,0:T(8,128)(2,1)S(1)} %collective-permute-done.5.far_ref, ...), custom_call_target="tpu_custom_call" | custom-call | tf_op jit(solution)/shard_map/pallas_call | solution.py:29
  26.8 1.6 %collective-permute-start.10 = (bf16[208,256]{1,0:T(8,128)(2,1)S(1)}, bf16[208,256]{1,0:T(8,128)(2,1)S(1)}, u32[]{:S(2)}, u32[]{:S(2)}) collective-permute-start(bf16[208,256]{1,0:T(8,128)(2,1)S(1)} %shard_map.80.refs_0_), channel_id=1, source_target_pairs={{0,3},{1,2},{2,1},{3,0},{4,7},{5,6},{6,5},{7,4},{8,11},{9,10},{10,... | collective-permute-start | bytes 319496 | tf_op jit(solution)/shard_map/ppermute | solution.py:21
  28.4 1.5 %collective-permute-start.8 = (bf16[208,256]{1,0:T(8,128)(2,1)S(1)}, bf16[208,256]{1,0:T(8,128)(2,1)S(1)}, u32[]{:S(2)}, u32[]{:S(2)}) collective-permute-start(bf16[208,256]{1,0:T(8,128)(2,1)S(1)} %shard_map.80.refs_0_), channel_id=1, source_target_pairs={{0,1},{1,0},{2,3},{3,2},{4,5},{5,4},{6,7},{7,6},{8,9},{9,8},{10,11... | collective-permute-start | bytes 319496 | tf_op jit(solution)/shard_map/ppermute | solution.py:21
  29.9 0.4 collective-permute-start.9
  30.3 2.4 %collective-permute-done.10.refs_3_ = bf16[208,256]{1,0:T(8,128)(2,1)S(1)} collective-permute-done((bf16[208,256]{1,0:T(8,128)(2,1)S(1)}, bf16[208,256]{1,0:T(8,128)(2,1)S(1)}, u32[]{:S(2)}, u32[]{:S(2)}) %collective-permute-start.10) | collective-permute-done | bytes 106528 | tf_op jit(solution)/shard_map/ppermute | solution.py:21
  32.7 1.1 %collective-permute-done.8.refs_1_ = bf16[208,256]{1,0:T(8,128)(2,1)S(1)} collective-permute-done((bf16[208,256]{1,0:T(8,128)(2,1)S(1)}, bf16[208,256]{1,0:T(8,128)(2,1)S(1)}, u32[]{:S(2)}, u32[]{:S(2)}) %collective-permute-start.8) | collective-permute-done | bytes 106528 | tf_op jit(solution)/shard_map/ppermute | solution.py:21
  33.8 0.8 %collective-permute-done.9.refs_2_ = bf16[208,256]{1,0:T(8,128)(2,1)S(1)} collective-permute-done((bf16[208,256]{1,0:T(8,128)(2,1)S(1)}, bf16[208,256]{1,0:T(8,128)(2,1)S(1)}, u32[]{:S(2)}, u32[]{:S(2)}) %collective-permute-start.9) | collective-permute-done | bytes 106528 | tf_op jit(solution)/shard_map/ppermute | solution.py:21
  34.6 1.4 %shard_map.81 = (bf16[64,512]{1,0:T(8,128)(2,1)S(1)}, bf16[64,512]{1,0:T(8,128)(2,1)S(1)}, bf16[64,512]{1,0:T(8,128)(2,1)S(1)}, bf16[64,512]{1,0:T(8,128)(2,1)S(1)}, bf16[512,128]{1,0:T(8,128)(2,1)}) custom-call(bf16[208,256]{1,0:T(8,128)(2,1)S(1)} %shard_map.80.refs_0_, bf16[208,256]{1,0:T(8,128)(2,1)S(1)} %collective-permute-done.8.refs_1_, ...), custom_call_target="tpu_custom_call" | custom-call | tf_op jit(solution)/shard_map/pallas_call | solution.py:29
  36.0 4.0 %all-to-all-start = ((bf16[32,16,128]{2,1,0:T(8,128)(2,1)}), bf16[32,16,128]{2,1,0:T(8,128)(2,1)S(1)}, u32[]{:S(2)}, u32[]{:S(2)}) async-start(bf16[32,16,128]{2,1,0:T(8,128)(2,1)} %bitcast.1), calls=%async_computation | async-start | bytes 262144 | tf_op jit(solution)/shard_map/all_to_all | solution.py:259
  40.0 1.8 %collective-permute-start.11 = (bf16[64,512]{1,0:T(8,128)(2,1)S(1)}, bf16[64,512]{1,0:T(8,128)(2,1)S(1)}, u32[]{:S(2)}, u32[]{:S(2)}) collective-permute-start(bf16[64,512]{1,0:T(8,128)(2,1)S(1)} %get-tuple-element.16), channel_id=1, source_target_pairs={{0,1},{1,0},{2,3},{3,2},{4,5},{5,4},{6,7},{7,6},{8,9},{9,8},{10,11... | collective-permute-start | bytes 196616 | tf_op jit(solution)/shard_map/ppermute | solution.py:21
  41.8 1.5 %collective-permute-start.12 = (bf16[64,512]{1,0:T(8,128)(2,1)S(1)}, bf16[64,512]{1,0:T(8,128)(2,1)S(1)}, u32[]{:S(2)}, u32[]{:S(2)}) collective-permute-start(bf16[64,512]{1,0:T(8,128)(2,1)S(1)} %get-tuple-element.17), channel_id=1, source_target_pairs={{0,2},{1,3},{2,0},{3,1},{4,6},{5,7},{6,4},{7,5},{8,10},{9,11},{10,... | collective-permute-start | bytes 196616 | tf_op jit(solution)/shard_map/ppermute | solution.py:21
  43.3 0.3 collective-permute-start.13
  43.5 4.2 %all-to-all-done = bf16[32,16,128]{2,1,0:T(8,128)(2,1)S(1)} async-done(((bf16[32,16,128]{2,1,0:T(8,128)(2,1)}), bf16[32,16,128]{2,1,0:T(8,128)(2,1)S(1)}, u32[]{:S(2)}, u32[]{:S(2)}) %all-to-all-start) | async-done | bytes 131104 | tf_op jit(solution)/shard_map/all_to_all | solution.py:259
  47.7 0.8 %shard_map.83 = f32[32,8,8]{2,1,0:T(8,128)} custom-call(bf16[8,4,16,128]{3,2,1,0:T(8,128)(2,1)S(1)} %bitcast.3), custom_call_target="tpu_custom_call" | custom-call | tf_op jit(solution)/shard_map/pallas_call | solution.py:29
  48.5 2.6 %all-to-all-start.1 = ((f32[32,8,8]{2,1,0:T(8,128)}), f32[32,8,8]{2,1,0:T(8,128)S(1)}, u32[]{:S(2)}, u32[]{:S(2)}) async-start(f32[32,8,8]{2,1,0:T(8,128)} %shard_map.83), calls=%async_computation.1 | async-start | bytes 262144 | tf_op jit(solution)/shard_map/all_to_all | solution.py:270
  51.1 0.0 collective-permute-done.11.refs_1_
  51.1 0.0 collective-permute-done.12.refs_2_
  51.1 0.0 collective-permute-done.13.refs_3_
  51.1 0.7 %shard_map.82 = bf16[64,2048]{1,0:T(8,128)(2,1)} custom-call(bf16[64,512]{1,0:T(8,128)(2,1)S(1)} %get-tuple-element.15.refs_0_, bf16[64,512]{1,0:T(8,128)(2,1)S(1)} %collective-permute-done.11.refs_1_, bf16[64,512]{1,0:T(8,128)(2,1)S(1)} %collective-permute-done.12.refs_2_, bf16[64,512]{1,0:T(8,128)(2,1)S(1)} %collective-permute-done.13.refs_3_), custom_call_target="tpu_custom_call" | custom-call | tf_op jit(solution)/shard_map/pallas_call | solution.py:29
  51.9 7.0 %all-to-all-done.1.tables_ref = f32[32,8,8]{2,1,0:T(8,128)S(1)} async-done(((f32[32,8,8]{2,1,0:T(8,128)}), f32[32,8,8]{2,1,0:T(8,128)S(1)}, u32[]{:S(2)}, u32[]{:S(2)}) %all-to-all-start.1) | async-done | bytes 8224 | tf_op jit(solution)/shard_map/all_to_all | solution.py:270
  58.9 0.7 %shard_map.84 = f32[8,8]{1,0:T(8,128)} custom-call(f32[32,8,8]{2,1,0:T(8,128)S(1)} %all-to-all-done.1.tables_ref), custom_call_target="tpu_custom_call" | custom-call | tf_op jit(solution)/shard_map/pallas_call | solution.py:29
  (2 shorter events, 0.1 us)
Async XLA Ops:
  2.0 13.2 %collective-permute-start = (bf16[384,512]{1,0:T(8,128)(2,1)S(1)}, bf16[384,512]{1,0:T(8,128)(2,1)S(1)}, u32[]{:S(2)}, u32[]{:S(2)}) collective-permute-start(bf16[384,512]{1,0:T(8,128)(2,1)S(1)} %get-tuple-element.11), channel_id=1, source_target_pairs={{0,1},{1,0},{2,3},{3,2},{4,5},{5,4},{6,7},{7,6},{8,9},{9,8},{10,11... | collective-permute-start | bytes 1179656 | tf_op jit(solution)/shard_map/ppermute | solution.py:21
  5.0 4.4 %collective-permute-start.1 = (bf16[32,1024]{1,0:T(8,128)(2,1)S(1)}, bf16[32,1024]{1,0:T(8,128)(2,1)S(1)}, u32[]{:S(2)}, u32[]{:S(2)}) collective-permute-start(bf16[32,1024]{1,0:T(8,128)(2,1)S(1)} %get-tuple-element.12.refs_0_), channel_id=1, source_target_pairs={{0,2},{1,3},{2,0},{3,1},{4,6},{5,7},{6,4},{7,5},{8,10},{9,11},{10,... | collective-permute-start | bytes 196616 | tf_op jit(solution)/shard_map/ppermute | solution.py:21
  6.5 7.0 %collective-permute-start.2 = (bf16[32,1024]{1,0:T(8,128)(2,1)S(1)}, bf16[32,1024]{1,0:T(8,128)(2,1)S(1)}, u32[]{:S(2)}, u32[]{:S(2)}) collective-permute-start(bf16[32,1024]{1,0:T(8,128)(2,1)S(1)} %get-tuple-element.12.refs_0_), channel_id=1, source_target_pairs={{0,4},{1,5},{2,6},{3,7},{4,0},{5,1},{6,2},{7,3},{8,12},{9,13},{10,... | collective-permute-start | bytes 196616 | tf_op jit(solution)/shard_map/ppermute | solution.py:21
  9.1 6.1 %collective-permute-start.3 = (bf16[32,1024]{1,0:T(8,128)(2,1)S(1)}, bf16[32,1024]{1,0:T(8,128)(2,1)S(1)}, u32[]{:S(2)}, u32[]{:S(2)}) collective-permute-start(bf16[32,1024]{1,0:T(8,128)(2,1)S(1)} %get-tuple-element.12.refs_0_), channel_id=1, source_target_pairs={{0,6},{1,7},{2,4},{3,5},{4,2},{5,3},{6,0},{7,1},{8,14},{9,15},{10,... | collective-permute-start | bytes 196616 | tf_op jit(solution)/shard_map/ppermute | solution.py:21
  15.2 10.5 %copy-start.1 = (bf16[192,2048]{1,0:T(8,128)(2,1)S(1)}, bf16[192,2048]{1,0:T(8,128)(2,1)}, u32[]{:S(2)}) copy-start(bf16[192,2048]{1,0:T(8,128)(2,1)} %up_ref.1) | copy-start | bytes 2359300
  15.2 10.5 %copy-start = (bf16[192,2048]{1,0:T(8,128)(2,1)S(1)}, bf16[192,2048]{1,0:T(8,128)(2,1)}, u32[]{:S(2)}) copy-start(bf16[192,2048]{1,0:T(8,128)(2,1)} %gate_ref.1) | copy-start | bytes 2359300
  15.2 6.4 %collective-permute-start.5 = (bf16[128,1024]{1,0:T(8,128)(2,1)S(1)}, bf16[128,1024]{1,0:T(8,128)(2,1)S(1)}, u32[]{:S(2)}, u32[]{:S(2)}) collective-permute-start(bf16[128,1024]{1,0:T(8,128)(2,1)S(1)} %shard_map.78.after_ref.near_ref), channel_id=1, source_target_pairs={{0,1},{1,0},{2,3},{3,2},{4,5},{5,4},{6,7},{7,6},{8,9},{9,8},{10,11... | collective-permute-start | bytes 786440 | tf_op jit(solution)/shard_map/ppermute | solution.py:21
  15.9 9.8 %copy-start.2 = (f32[1,64]{1,0:T(1,128)S(1)}, f32[1,64]{1,0:T(1,128)}, u32[]{:S(2)}) copy-start(f32[1,64]{1,0:T(1,128)} %route_ref.1) | copy-start | bytes 772
  16.0 9.8 %collective-permute-start.4 = (bf16[384,512]{1,0:T(8,128)(2,1)S(1)}, bf16[384,512]{1,0:T(8,128)(2,1)S(1)}, u32[]{:S(2)}, u32[]{:S(2)}) collective-permute-start(bf16[384,512]{1,0:T(8,128)(2,1)S(1)} %shard_map.79), channel_id=1, source_target_pairs={{0,2},{1,3},{2,0},{3,1},{4,6},{5,7},{6,4},{7,5},{8,10},{9,11},{10,... | collective-permute-start | bytes 1179656 | tf_op jit(solution)/shard_map/ppermute | solution.py:21
  17.6 4.1 %collective-permute-start.6 = (bf16[128,1024]{1,0:T(8,128)(2,1)S(1)}, bf16[128,1024]{1,0:T(8,128)(2,1)S(1)}, u32[]{:S(2)}, u32[]{:S(2)}) collective-permute-start(bf16[128,1024]{1,0:T(8,128)(2,1)S(1)} %shard_map.78.after_ref.near_ref), channel_id=1, source_target_pairs={{0,8},{8,0},{16,24},{24,16},{1,9},{9,1},{17,25},{25,17},{2,10},{10... | collective-permute-start | bytes 786440 | tf_op jit(solution)/shard_map/ppermute | solution.py:21
  21.7 4.1 %collective-permute-start.7 = (bf16[128,1024]{1,0:T(8,128)(2,1)S(1)}, bf16[128,1024]{1,0:T(8,128)(2,1)S(1)}, u32[]{:S(2)}, u32[]{:S(2)}) collective-permute-start(bf16[128,1024]{1,0:T(8,128)(2,1)S(1)} %collective-permute-done.5.far_ref), channel_id=1, source_target_pairs={{0,8},{8,0},{16,24},{24,16},{1,9},{9,1},{17,25},{25,17},{2,10},{10... | collective-permute-start | bytes 786440 | tf_op jit(solution)/shard_map/ppermute | solution.py:21
  26.8 6.0 %collective-permute-start.10 = (bf16[208,256]{1,0:T(8,128)(2,1)S(1)}, bf16[208,256]{1,0:T(8,128)(2,1)S(1)}, u32[]{:S(2)}, u32[]{:S(2)}) collective-permute-start(bf16[208,256]{1,0:T(8,128)(2,1)S(1)} %shard_map.80.refs_0_), channel_id=1, source_target_pairs={{0,3},{1,2},{2,1},{3,0},{4,7},{5,6},{6,5},{7,4},{8,11},{9,10},{10,... | collective-permute-start | bytes 319496 | tf_op jit(solution)/shard_map/ppermute | solution.py:21
  28.4 5.4 %collective-permute-start.8 = (bf16[208,256]{1,0:T(8,128)(2,1)S(1)}, bf16[208,256]{1,0:T(8,128)(2,1)S(1)}, u32[]{:S(2)}, u32[]{:S(2)}) collective-permute-start(bf16[208,256]{1,0:T(8,128)(2,1)S(1)} %shard_map.80.refs_0_), channel_id=1, source_target_pairs={{0,1},{1,0},{2,3},{3,2},{4,5},{5,4},{6,7},{7,6},{8,9},{9,8},{10,11... | collective-permute-start | bytes 319496 | tf_op jit(solution)/shard_map/ppermute | solution.py:21
  29.9 4.7 %collective-permute-start.9 = (bf16[208,256]{1,0:T(8,128)(2,1)S(1)}, bf16[208,256]{1,0:T(8,128)(2,1)S(1)}, u32[]{:S(2)}, u32[]{:S(2)}) collective-permute-start(bf16[208,256]{1,0:T(8,128)(2,1)S(1)} %shard_map.80.refs_0_), channel_id=1, source_target_pairs={{0,2},{1,3},{2,0},{3,1},{4,6},{5,7},{6,4},{7,5},{8,10},{9,11},{10,... | collective-permute-start | bytes 319496 | tf_op jit(solution)/shard_map/ppermute | solution.py:21
  36.0 11.7 %all-to-all-start = ((bf16[32,16,128]{2,1,0:T(8,128)(2,1)}), bf16[32,16,128]{2,1,0:T(8,128)(2,1)S(1)}, u32[]{:S(2)}, u32[]{:S(2)}) async-start(bf16[32,16,128]{2,1,0:T(8,128)(2,1)} %bitcast.1), calls=%async_computation | async-start | bytes 262144 | tf_op jit(solution)/shard_map/all_to_all | solution.py:259
  40.0 11.1 %collective-permute-start.11 = (bf16[64,512]{1,0:T(8,128)(2,1)S(1)}, bf16[64,512]{1,0:T(8,128)(2,1)S(1)}, u32[]{:S(2)}, u32[]{:S(2)}) collective-permute-start(bf16[64,512]{1,0:T(8,128)(2,1)S(1)} %get-tuple-element.16), channel_id=1, source_target_pairs={{0,1},{1,0},{2,3},{3,2},{4,5},{5,4},{6,7},{7,6},{8,9},{9,8},{10,11... | collective-permute-start | bytes 196616 | tf_op jit(solution)/shard_map/ppermute | solution.py:21
  41.8 9.3 %collective-permute-start.12 = (bf16[64,512]{1,0:T(8,128)(2,1)S(1)}, bf16[64,512]{1,0:T(8,128)(2,1)S(1)}, u32[]{:S(2)}, u32[]{:S(2)}) collective-permute-start(bf16[64,512]{1,0:T(8,128)(2,1)S(1)} %get-tuple-element.17), channel_id=1, source_target_pairs={{0,2},{1,3},{2,0},{3,1},{4,6},{5,7},{6,4},{7,5},{8,10},{9,11},{10,... | collective-permute-start | bytes 196616 | tf_op jit(solution)/shard_map/ppermute | solution.py:21
  43.3 7.8 %collective-permute-start.13 = (bf16[64,512]{1,0:T(8,128)(2,1)S(1)}, bf16[64,512]{1,0:T(8,128)(2,1)S(1)}, u32[]{:S(2)}, u32[]{:S(2)}) collective-permute-start(bf16[64,512]{1,0:T(8,128)(2,1)S(1)} %get-tuple-element.18), channel_id=1, source_target_pairs={{0,3},{1,2},{2,1},{3,0},{4,7},{5,6},{6,5},{7,4},{8,11},{9,10},{10,... | collective-permute-start | bytes 196616 | tf_op jit(solution)/shard_map/ppermute | solution.py:21
  48.5 10.3 %all-to-all-start.1 = ((f32[32,8,8]{2,1,0:T(8,128)}), f32[32,8,8]{2,1,0:T(8,128)S(1)}, u32[]{:S(2)}, u32[]{:S(2)}) async-start(f32[32,8,8]{2,1,0:T(8,128)} %shard_map.83), calls=%async_computation.1 | async-start | bytes 262144 | tf_op jit(solution)/shard_map/all_to_all | solution.py:270

commit v8 on v7

--- a/solution.py
+++ b/solution.py
@@ -105,10 +105,10 @@
     out_ref[depth:] = terms.astype(bf16)
 
 
-def features_kernel(*refs):
+def features_kernel(gathered, *refs):
     hidden_refs, (own_ref, x_ref, z_ref) = refs[:HOLDERS], refs[HOLDERS : HOLDERS + 3]
-    block_refs, centered_ref = refs[HOLDERS + 3 : 2 * HOLDERS + 3], refs[2 * HOLDERS + 3]
-    route_ref, features_ref = refs[2 * HOLDERS + 4 :]
+    block_refs, centered_refs = refs[HOLDERS + 3 : 2 * HOLDERS + 3], refs[2 * HOLDERS + 3 : -3]
+    route_ref, features_ref, whole_ref = refs[-3:]
     depth, tokens = own_ref.shape[0], hidden_refs[0].shape[1]
     part, members = tokens // HOLDERS, lax.axis_size("tok")
     rows = tokens // members
@@ -138,14 +138,26 @@
     column = jnp.sum(wide * mean, axis=1, keepdims=True)
     row = jnp.transpose(jnp.broadcast_to(column, (tokens, LANES)))[:1]
     gram = dot_f32(features, features, TRANSPOSED)
-    centered = (gram - column - row + jnp.sum(mean * mean)).astype(bf16)
-    at = 0
-    for i in range(tokens // TILE):
-        for j in range(tokens // LANES):
-            centered_ref[at * TILE : (at + 1) * TILE] = centered[
-                i * TILE : (i + 1) * TILE, j * LANES : (j + 1) * LANES
-            ]
-            at += 1
+    centered = gram - column - row + jnp.sum(mean * mean)
+    if gathered:
+        whole_ref[...] = centered.astype(bf16)
+        half = tokens // 2
+        count = half // HOLDERS
+        for m, centered_ref in enumerate(centered_refs):
+            first = (holder() ^ m) * count
+            for at, (row, left) in enumerate(((0, 0), (0, half), (half, half))):
+                rows_there = pl.ds(pl.multiple_of(first + row, count), count)
+                centered_ref[at * count : (at + 1) * count] = whole_ref[rows_there, left : left + half]
+    else:
+        (centered_ref,) = centered_refs
+        centered = centered.astype(bf16)
+        at = 0
+        for i in range(tokens // TILE):
+            for j in range(tokens // LANES):
+                centered_ref[at * TILE : (at + 1) * TILE] = centered[
+                    i * TILE : (i + 1) * TILE, j * LANES : (j + 1) * LANES
+                ]
+                at += 1
     for m, block_ref in enumerate(block_refs):
         for piece in range(part // rows):
             block_ref[piece * rows : (piece + 1) * rows] = features_ref[place(m, piece)]
@@ -163,32 +175,77 @@
         copy.wait()
 
 
-def pair_kernel(parts_ref, out_ref, flat_ref):
-    copies, experts, _ = out_ref.shape
+def sum_kernel(*refs):
+    total = refs[0][...].astype(f32)
+    for ref in refs[1:-1]:
+        total = total + ref[...].astype(f32)
+    refs[-1][...] = total.astype(bf16)
+
+
+def join_kernel(*refs):
+    low_ref, high_ref, out_ref = refs[-3:]
+    rows = low_ref.shape[0]
+    out_ref[:rows] = low_ref[...]
+    out_ref[rows:] = high_ref[...]
+
+
+def table_of(flat_ref, experts, weighted):
+    lane = lax.broadcasted_iota(jnp.int32, (experts, experts), 1)
+
+    def one(expert, table):
+        products = jnp.sum(weighted * flat_ref[pl.ds(expert, 1)], axis=1)
+        return jnp.where(lane == expert, jnp.sum(products, axis=1, keepdims=True), table)
+
+    return lax.fori_loop(0, experts, one, jnp.zeros((experts, experts), f32), unroll=experts <= 8)
+
+
+def pair_kernel(distances, low_ref, high_ref, out_ref, flat_ref):
+    experts, rows, _ = flat_ref.shape
+    here = lax.axis_index("grp") * (lax.axis_size("tok") // HOLDERS) + lax.axis_index("tok") // HOLDERS
+    for m in range(experts):
+        ref, at = (low_ref, m) if m < experts // 2 else (high_ref, m - experts // 2)
+        block = ref[at * rows : (at + 1) * rows].astype(f32)
+        flat_ref[pl.ds(here ^ distances[m], 1)] = block[None]
+    row = lax.broadcasted_iota(jnp.int32, flat_ref.shape, 1) // (rows // 3)
+    flat = flat_ref[...]
+    out_ref[...] = table_of(flat_ref, experts, jnp.where(row == 1, 2.0 * flat, flat))
+
+
+def parts_kernel(parts_ref, out_ref, flat_ref):
     parts = parts_ref[...].astype(f32)
     total = parts[:, 0]
-    for holder in range(1, parts.shape[1]):
-        total = total + parts[:, holder]
+    for m in range(1, parts.shape[1]):
+        total = total + parts[:, m]
     flat_ref[...] = total.astype(bf16).astype(f32)
-    lane = lax.broadcasted_iota(jnp.int32, (experts, experts), 1)
-
-    def one(expert, table):
-        products = jnp.sum(flat_ref[...] * flat_ref[pl.ds(expert, 1)], axis=1)
-        return jnp.where(lane == expert, jnp.sum(products, axis=1, keepdims=True), table)
-
-    table = lax.fori_loop(0, experts, one, jnp.zeros((experts, experts), f32), unroll=experts <= 8)
-    for copy in range(copies):
-        out_ref[copy] = table
-
-
-def cka_kernel(tables_ref, out_ref):
-    totals = jnp.sum(tables_ref[...], axis=0)
+    out_ref[...] = table_of(flat_ref, out_ref.shape[0], flat_ref[...])
+
+
+def cka_kernel(*refs):
+    tables, out_ref, kept_ref = refs[:-2], refs[-2], refs[-1]
+    for m, table in enumerate(tables):
+        kept_ref[pl.ds(holder() ^ m if m or len(tables) > 1 else 0, 1)] = table[...][None]
+    totals = jnp.sum(kept_ref[...], axis=0)
     shape = totals.shape
     eye = lax.broadcasted_iota(jnp.int32, shape, 0) == lax.broadcasted_iota(jnp.int32, shape, 1)
-    kept = jnp.where(eye, totals, 0.0)
-    down = jnp.sum(kept, axis=1, keepdims=True)
-    across = jnp.sum(kept, axis=0, keepdims=True)
+    diagonal = jnp.where(eye, totals, 0.0)
+    down = jnp.sum(diagonal, axis=1, keepdims=True)
+    across = jnp.sum(diagonal, axis=0, keepdims=True)
     out_ref[...] = totals / jnp.sqrt(down * across)
+
+
+def hold_kernel(*refs):
+    pass
+
+
+def held(arrays, after):
+    return call(
+        hold_kernel,
+        [jax.ShapeDtypeStruct(a.shape, a.dtype) for a in arrays],
+        [ANY] * (len(arrays) + 1),
+        (*arrays, after),
+        out_specs=[ANY] * len(arrays),
+        aliases={i: i for i in range(len(arrays))},
+    )
 
 
 def shards(probe_states, norm_gain, gate_weight, up_weight, down_weight, route_weight):
@@ -247,32 +304,74 @@
         ),
     )
     hiddens = [swapped(hidden, "tok", m) if m else hidden for m in range(HOLDERS)]
+    half = tokens // 2
+    part_shape = (3 * half // HOLDERS, half)
+    gathered = experts * part_shape[0] * part_shape[1] <= 1 << 20
     entries = tokens * tokens // LANES
-    *blocks, centered = call(
-        features_kernel,
+    outs = [part_shape] * HOLDERS if gathered else [(entries, LANES)]
+    outcome = call(
+        lambda *refs: features_kernel(gathered, *refs),
         [jax.ShapeDtypeStruct((token_part, part), bf16)] * HOLDERS
-        + [jax.ShapeDtypeStruct((entries, LANES), bf16)],
+        + [jax.ShapeDtypeStruct(shape, bf16) for shape in outs],
         [VMEM] * (HOLDERS + 3),
         (*hiddens, down_own, down_x, down_z),
-        scratch=[pltpu.VMEM((tokens, LANES), f32), pltpu.VMEM((tokens, part), bf16)],
-    )
-    arrived = lax.all_to_all(centered, ("grp", "tok"), split_axis=0, concat_axis=0, tiled=True)
-    arrived = arrived.reshape(experts, HOLDERS, entries // devices, LANES)
-    direct = devices * experts * experts <= 1 << 16
-    tables = call(
-        pair_kernel,
-        jax.ShapeDtypeStruct((devices if direct else 1, experts, experts), f32),
-        [VMEM],
-        (arrived,),
-        scratch=[pltpu.VMEM((experts, entries // devices, LANES), f32)],
-    )
-    if direct:
-        tables = lax.all_to_all(tables, ("grp", "tok"), split_axis=0, concat_axis=0, tiled=True)
+        scratch=[
+            pltpu.VMEM((tokens, LANES), f32),
+            pltpu.VMEM((tokens, part), bf16),
+            pltpu.VMEM((tokens, tokens), bf16),
+        ],
+    )
+    blocks, centered = outcome[:HOLDERS], outcome[HOLDERS:]
+    table_shape = jax.ShapeDtypeStruct((experts, experts), f32)
+    if gathered:
+        centered = [swapped(c, "tok", m) if m else c for m, c in enumerate(centered)]
+        low = call(
+            sum_kernel, jax.ShapeDtypeStruct(part_shape, bf16), [VMEM] * HOLDERS, centered
+        )
+        blocks = held(blocks, low)
+        blocks = [swapped(b, "tok", m) if m else b for m, b in enumerate(blocks)]
+        steps = [("tok", 1 << b) for b in range(2, members.bit_length() - 1)]
+        steps += [("grp", 1 << b) for b in range(groups.bit_length() - 2, -1, -1)]
+        distances = [0]
+        for at, (axis, mask) in enumerate(steps):
+            away = mask // HOLDERS if axis == "tok" else mask * (members // HOLDERS)
+            distances += [d ^ away for d in distances]
+            high = swapped(low, axis, mask)
+            if at < len(steps) - 1:
+                joined = jax.ShapeDtypeStruct((2 * low.shape[0], half), bf16)
+                after = blocks if at == len(steps) - 2 else []
+                low = call(
+                    join_kernel, joined, [ANY] * len(after) + [VMEM] * 2, (*after, low, high)
+                )
+        table = call(
+            lambda *refs: pair_kernel(distances, *refs),
+            table_shape,
+            [VMEM] * 2,
+            (low, high),
+            scratch=[pltpu.VMEM((experts, *part_shape), f32)],
+        )
+        tables = [swapped(table, "tok", m) if m else table for m in range(HOLDERS)]
     else:
-        tables = lax.psum(tables, ("grp", "tok"))
-    cka = call(cka_kernel, jax.ShapeDtypeStruct((experts, experts), f32), [VMEM], (tables,))
-
-    blocks = [swapped(b, "tok", m) if m else b for m, b in enumerate(blocks)]
+        blocks = [swapped(b, "tok", m) if m else b for m, b in enumerate(blocks)]
+        arrived = lax.all_to_all(
+            centered[0], ("grp", "tok"), split_axis=0, concat_axis=0, tiled=True
+        )
+        table = call(
+            parts_kernel,
+            table_shape,
+            [VMEM],
+            (arrived.reshape(experts, HOLDERS, entries // devices, LANES),),
+            scratch=[pltpu.VMEM((experts, entries // devices, LANES), f32)],
+        )
+        tables = [lax.psum(table, ("grp", "tok"))]
+    cka = call(
+        cka_kernel,
+        table_shape,
+        [VMEM] * len(tables),
+        tables,
+        scratch=[pltpu.VMEM((len(tables), experts, experts), f32)],
+    )
+
     features = call(
         place_kernel,
         jax.ShapeDtypeStruct((token_part, model), bf16),

time: 59.8 us -> 62 us (1.037)
  starting transfers between devices: 23.4 us -> 28.3 us
  waiting for transfers between devices: 29.4 us -> 27.7 us
  Pallas kernels: 6.09 us -> 5.12 us
    ppermute x14 -> x23, starting transfers between devices: 16.8 us -> 28.3 us  [swapped(): lax.ppermute(array, axis, [(i, i ^ mask) for i in range(lax.axis_size(axi...]
    all_to_all x2 -> x0, waiting for transfers between devices: 11.1 us -> none  [the longest x1 6.96 us: shards(): lax.all_to_all(tables, ('grp', 'tok'), split_axis=0, concat_axis=0, tiled...]
    ppermute x14 -> x23, waiting for transfers between devices: 18.2 us -> 27.7 us  [swapped(): lax.ppermute(array, axis, [(i, i ^ mask) for i in range(lax.axis_size(axi...]
    all_to_all x2 -> x0, starting transfers between devices: 6.54 us -> none  [the longest x1 3.97 us: shards(): lax.all_to_all(centered, ('grp', 'tok'), split_axis=0, concat_axis=0, til...]
    pallas_call x8 -> x12, Pallas kernels: 6.09 us -> 5.12 us  [call(): pl.pallas_call(body, out_shape=outs, in_specs=in_specs, out_specs=jax.tre...]
  transfers between devices with their start and end apart: 16 -> 23, of which waited for: 9 -> 14; matrix products, arithmetic and copies ran while one was open for 0% -> 0% of each run, Pallas kernels for 3% -> 1%
where the time goes in v8:
time: 62 us; the launch traced here: 61.9 us
  starting transfers between devices  28.3 us (46%)
  waiting for transfers between devices  27.7 us (45%)
  Pallas kernels  5.12 us (8%)
  between operations  0.73 us (1%)
    ppermute x23, starting transfers between devices, swapped(): lax.ppermute(array, axis, [(i, i ^ mask) for i in range(lax.axis_size(axi...  28.3 us
    ppermute x23, waiting for transfers between devices, swapped(): lax.ppermute(array, axis, [(i, i ^ mask) for i in range(lax.axis_size(axi...  27.7 us
    pallas_call x12, Pallas kernels, call(): pl.pallas_call(body, out_shape=outs, in_specs=in_specs, out_specs=jax.tre...  5.12 us
  transfers between devices with their start and end apart: 23, of which 14 were waited for; matrix products, arithmetic and copies ran while one was open for 0% of the time, Pallas kernels for 1%

profile of v8, /device:TPU:0, one launch (start us, length us, event | category | flops | bytes accessed | tf_op | source)
XLA Modules:
  0.0 61.9 jit_solution(4729798058460962591)
XLA Ops:
  0.6 1.3 %shard_map.77 = (bf16[32,1024]{1,0:T(8,128)(2,1)S(1)}, bf16[192,512]{1,0:T(8,128)(2,1)S(1)}, bf16[192,512]{1,0:T(8,128)(2,1)S(1)}, bf16[384,512]{1,0:T(8,128)(2,1)S(1)}) custom-call(bf16[32,2048]{1,0:T(8,128)(2,1)} %states_hbm.1, f32[1,2048]{1,0:T(1,128)} %bitcast.1, bf16[192,2048]{1,0:T(8,128)(2,1)} %down_hbm.1), custom_call_target="tpu_custom_call" | custom-call | tf_op jit(solution)/shard_map/pallas_call | solution.py:29
  2.0 3.0 %collective-permute-start = (bf16[384,512]{1,0:T(8,128)(2,1)S(1)}, bf16[384,512]{1,0:T(8,128)(2,1)S(1)}, u32[]{:S(2)}, u32[]{:S(2)}) collective-permute-start(bf16[384,512]{1,0:T(8,128)(2,1)S(1)} %get-tuple-element.18), channel_id=1, source_target_pairs={{0,1},{1,0},{2,3},{3,2},{4,5},{5,4},{6,7},{7,6},{8,9},{9,8},{10,11... | collective-permute-start | bytes 1179656 | tf_op jit(solution)/shard_map/ppermute | solution.py:21
  5.0 1.6 %collective-permute-start.1 = (bf16[32,1024]{1,0:T(8,128)(2,1)S(1)}, bf16[32,1024]{1,0:T(8,128)(2,1)S(1)}, u32[]{:S(2)}, u32[]{:S(2)}) collective-permute-start(bf16[32,1024]{1,0:T(8,128)(2,1)S(1)} %get-tuple-element.19.refs_0_), channel_id=1, source_target_pairs={{0,2},{1,3},{2,0},{3,1},{4,6},{5,7},{6,4},{7,5},{8,10},{9,11},{10,... | collective-permute-start | bytes 196616 | tf_op jit(solution)/shard_map/ppermute | solution.py:21
  6.5 2.6 %collective-permute-start.2 = (bf16[32,1024]{1,0:T(8,128)(2,1)S(1)}, bf16[32,1024]{1,0:T(8,128)(2,1)S(1)}, u32[]{:S(2)}, u32[]{:S(2)}) collective-permute-start(bf16[32,1024]{1,0:T(8,128)(2,1)S(1)} %get-tuple-element.19.refs_0_), channel_id=1, source_target_pairs={{0,4},{1,5},{2,6},{3,7},{4,0},{5,1},{6,2},{7,3},{8,12},{9,13},{10,... | collective-permute-start | bytes 196616 | tf_op jit(solution)/shard_map/ppermute | solution.py:21
  9.1 0.2 collective-permute-start.3
  9.4 0.0 collective-permute-done.1.refs_1_
  9.4 4.2 %collective-permute-done.2.refs_2_ = bf16[32,1024]{1,0:T(8,128)(2,1)S(1)} collective-permute-done((bf16[32,1024]{1,0:T(8,128)(2,1)S(1)}, bf16[32,1024]{1,0:T(8,128)(2,1)S(1)}, u32[]{:S(2)}, u32[]{:S(2)}) %collective-permute-start.2) | collective-permute-done | bytes 65568 | tf_op jit(solution)/shard_map/ppermute | solution.py:21
  13.5 1.7 %collective-permute-done.3.refs_3_ = bf16[32,1024]{1,0:T(8,128)(2,1)S(1)} collective-permute-done((bf16[32,1024]{1,0:T(8,128)(2,1)S(1)}, bf16[32,1024]{1,0:T(8,128)(2,1)S(1)}, u32[]{:S(2)}, u32[]{:S(2)}) %collective-permute-start.3) | collective-permute-done | bytes 65568 | tf_op jit(solution)/shard_map/ppermute | solution.py:21
  15.2 0.0 collective-permute-done.after_ref.got_ref.refs_5_
  15.2 0.0 copy-start.1
  15.2 0.0 copy-start
  15.2 0.7 %collective-permute-start.5 = (bf16[128,1024]{1,0:T(8,128)(2,1)S(1)}, bf16[128,1024]{1,0:T(8,128)(2,1)S(1)}, u32[]{:S(2)}, u32[]{:S(2)}) collective-permute-start(bf16[128,1024]{1,0:T(8,128)(2,1)S(1)} %shard_map.78.after_ref.near_ref), channel_id=1, source_target_pairs={{0,1},{1,0},{2,3},{3,2},{4,5},{5,4},{6,7},{7,6},{8,9},{9,8},{10,11... | collective-permute-start | bytes 786440 | tf_op jit(solution)/shard_map/ppermute | solution.py:21
  15.9 0.0 copy-start.2
  16.0 1.6 %collective-permute-start.4 = (bf16[384,512]{1,0:T(8,128)(2,1)S(1)}, bf16[384,512]{1,0:T(8,128)(2,1)S(1)}, u32[]{:S(2)}, u32[]{:S(2)}) collective-permute-start(bf16[384,512]{1,0:T(8,128)(2,1)S(1)} %shard_map.79), channel_id=1, source_target_pairs={{0,2},{1,3},{2,0},{3,1},{4,6},{5,7},{6,4},{7,5},{8,10},{9,11},{10,... | collective-permute-start | bytes 1179656 | tf_op jit(solution)/shard_map/ppermute | solution.py:21
  17.6 0.0 collective-permute-start.6
  17.6 4.1 %collective-permute-done.5.far_ref = bf16[128,1024]{1,0:T(8,128)(2,1)S(1)} collective-permute-done((bf16[128,1024]{1,0:T(8,128)(2,1)S(1)}, bf16[128,1024]{1,0:T(8,128)(2,1)S(1)}, u32[]{:S(2)}, u32[]{:S(2)}) %collective-permute-start.5) | collective-permute-done | bytes 262176 | tf_op jit(solution)/shard_map/ppermute | solution.py:21
  21.7 0.0 collective-permute-start.7
  21.7 0.0 collective-permute-done.6.near2_ref
  21.7 4.0 %collective-permute-done.4.after_ref.refs_6_ = bf16[384,512]{1,0:T(8,128)(2,1)S(1)} collective-permute-done((bf16[384,512]{1,0:T(8,128)(2,1)S(1)}, bf16[384,512]{1,0:T(8,128)(2,1)S(1)}, u32[]{:S(2)}, u32[]{:S(2)}) %collective-permute-start.4) | collective-permute-done | bytes 393248 | tf_op jit(solution)/shard_map/ppermute | solution.py:21
  25.7 0.0 collective-permute-done.7.far2_ref
  25.7 0.0 copy-done.1
  25.7 0.0 copy-done
  25.7 0.0 copy-done.2
  25.7 1.0 %shard_map.80.refs_0_ = bf16[208,256]{1,0:T(8,128)(2,1)S(1)} custom-call(bf16[384,512]{1,0:T(8,128)(2,1)S(1)} %collective-permute-done.4.after_ref.refs_6_, bf16[128,1024]{1,0:T(8,128)(2,1)S(1)} %shard_map.78.after_ref.near_ref, bf16[128,1024]{1,0:T(8,128)(2,1)S(1)} %collective-permute-done.5.far_ref, ...), custom_call_target="tpu_custom_call" | custom-call | tf_op jit(solution)/shard_map/pallas_call | solution.py:29
  26.8 1.6 %collective-permute-start.10 = (bf16[208,256]{1,0:T(8,128)(2,1)S(1)}, bf16[208,256]{1,0:T(8,128)(2,1)S(1)}, u32[]{:S(2)}, u32[]{:S(2)}) collective-permute-start(bf16[208,256]{1,0:T(8,128)(2,1)S(1)} %shard_map.80.refs_0_), channel_id=1, source_target_pairs={{0,3},{1,2},{2,1},{3,0},{4,7},{5,6},{6,5},{7,4},{8,11},{9,10},{10,... | collective-permute-start | bytes 319496 | tf_op jit(solution)/shard_map/ppermute | solution.py:21
  28.4 1.5 %collective-permute-start.8 = (bf16[208,256]{1,0:T(8,128)(2,1)S(1)}, bf16[208,256]{1,0:T(8,128)(2,1)S(1)}, u32[]{:S(2)}, u32[]{:S(2)}) collective-permute-start(bf16[208,256]{1,0:T(8,128)(2,1)S(1)} %shard_map.80.refs_0_), channel_id=1, source_target_pairs={{0,1},{1,0},{2,3},{3,2},{4,5},{5,4},{6,7},{7,6},{8,9},{9,8},{10,11... | collective-permute-start | bytes 319496 | tf_op jit(solution)/shard_map/ppermute | solution.py:21
  29.9 0.4 collective-permute-start.9
  30.3 2.4 %collective-permute-done.10.refs_3_ = bf16[208,256]{1,0:T(8,128)(2,1)S(1)} collective-permute-done((bf16[208,256]{1,0:T(8,128)(2,1)S(1)}, bf16[208,256]{1,0:T(8,128)(2,1)S(1)}, u32[]{:S(2)}, u32[]{:S(2)}) %collective-permute-start.10) | collective-permute-done | bytes 106528 | tf_op jit(solution)/shard_map/ppermute | solution.py:21
  32.7 1.1 %collective-permute-done.8.refs_1_ = bf16[208,256]{1,0:T(8,128)(2,1)S(1)} collective-permute-done((bf16[208,256]{1,0:T(8,128)(2,1)S(1)}, bf16[208,256]{1,0:T(8,128)(2,1)S(1)}, u32[]{:S(2)}, u32[]{:S(2)}) %collective-permute-start.8) | collective-permute-done | bytes 106528 | tf_op jit(solution)/shard_map/ppermute | solution.py:21
  33.8 0.8 %collective-permute-done.9.refs_2_ = bf16[208,256]{1,0:T(8,128)(2,1)S(1)} collective-permute-done((bf16[208,256]{1,0:T(8,128)(2,1)S(1)}, bf16[208,256]{1,0:T(8,128)(2,1)S(1)}, u32[]{:S(2)}, u32[]{:S(2)}) %collective-permute-start.9) | collective-permute-done | bytes 106528 | tf_op jit(solution)/shard_map/ppermute | solution.py:21
  34.6 0.8 %shard_map.81 = (bf16[64,512]{1,0:T(8,128)(2,1)S(1)}, bf16[64,512]{1,0:T(8,128)(2,1)S(1)}, bf16[64,512]{1,0:T(8,128)(2,1)S(1)}, bf16[64,512]{1,0:T(8,128)(2,1)S(...) custom-call(bf16[208,256]{1,0:T(8,128)(2,1)S(1)} %shard_map.80.refs_, ...), custom_call_target="tpu_custom_call" | custom-call | tf_op jit(solution)/shard_map/pallas_call | solution.py:29
  35.4 0.6 collective-permute-start.11
  36.0 0.7 %collective-permute-start.12 = (bf16[96,128]{1,0:T(8,128)(2,1)S(1)}, bf16[96,128]{1,0:T(8,128)(2,1)S(1)}, u32[]{:S(2)}, u32[]{:S(2)}) collective-permute-start(bf16[96,128]{1,0:T(8,128)(2,1)S(1)} %get-tuple-element.28), channel_id=1, source_target_pairs={{0,2},{1,3},{2,0},{3,1},{4,6},{5,7},{6,4},{7,5},{8,10},{9,11},{10,... | collective-permute-start | bytes 73736 | tf_op jit(solution)/shard_map/ppermute | solution.py:21
  36.6 2.3 %collective-permute-start.13 = (bf16[96,128]{1,0:T(8,128)(2,1)S(1)}, bf16[96,128]{1,0:T(8,128)(2,1)S(1)}, u32[]{:S(2)}, u32[]{:S(2)}) collective-permute-start(bf16[96,128]{1,0:T(8,128)(2,1)S(1)} %get-tuple-element.29), channel_id=1, source_target_pairs={{0,3},{1,2},{2,1},{3,0},{4,7},{5,6},{6,5},{7,4},{8,11},{9,10},{10,... | collective-permute-start | bytes 73736 | tf_op jit(solution)/shard_map/ppermute | solution.py:21
  38.9 0.3 collective-permute-done.11.refs_1_
  39.3 0.5 collective-permute-done.12.refs_2_
  39.8 1.6 %collective-permute-done.13.refs_3_ = bf16[96,128]{1,0:T(8,128)(2,1)S(1)} collective-permute-done((bf16[96,128]{1,0:T(8,128)(2,1)S(1)}, bf16[96,128]{1,0:T(8,128)(2,1)S(1)}, u32[]{:S(2)}, u32[]{:S(2)}) %collective-permute-start.13) | collective-permute-done | bytes 24608 | tf_op jit(solution)/shard_map/ppermute | solution.py:21
  41.4 2.9 %collective-permute-start.17 = (bf16[96,128]{1,0:T(8,128)(2,1)S(1)}, bf16[96,128]{1,0:T(8,128)(2,1)S(1)}, u32[]{:S(2)}, u32[]{:S(2)}) collective-permute-start(bf16[96,128]{1,0:T(8,128)(2,1)S(1)} %shard_map.82.refs_4_.refs_0_), channel_id=1, source_target_pairs={{0,4},{1,5},{2,6},{3,7},{4,0},{5,1},{6,2},{7,3},{8,12},{9,13},{10,... | collective-permute-start | bytes 73736 | tf_op jit(solution)/shard_map/ppermute | solution.py:21
  44.3 1.1 %collective-permute-start.14 = (bf16[64,512]{1,0:T(8,128)(2,1)S(1)}, bf16[64,512]{1,0:T(8,128)(2,1)S(1)}, u32[]{:S(2)}, u32[]{:S(2)}) collective-permute-start(bf16[64,512]{1,0:T(8,128)(2,1)S(1)} %get-tuple-element.31), channel_id=1, source_target_pairs={{0,1},{1,0},{2,3},{3,2},{4,5},{5,4},{6,7},{7,6},{8,9},{9,8},{10,11... | collective-permute-start | bytes 196616 | tf_op jit(solution)/shard_map/ppermute | solution.py:21
  45.3 1.8 %collective-permute-start.15 = (bf16[64,512]{1,0:T(8,128)(2,1)S(1)}, bf16[64,512]{1,0:T(8,128)(2,1)S(1)}, u32[]{:S(2)}, u32[]{:S(2)}) collective-permute-start(bf16[64,512]{1,0:T(8,128)(2,1)S(1)} %get-tuple-element.32), channel_id=1, source_target_pairs={{0,2},{1,3},{2,0},{3,1},{4,6},{5,7},{6,4},{7,5},{8,10},{9,11},{10,... | collective-permute-start | bytes 196616 | tf_op jit(solution)/shard_map/ppermute | solution.py:21
  47.2 0.6 collective-permute-start.16
  47.7 0.0 collective-permute-done.17.refs_1_
  47.7 1.6 %collective-permute-start.18 = (bf16[192,128]{1,0:T(8,128)(2,1)S(1)}, bf16[192,128]{1,0:T(8,128)(2,1)S(1)}, u32[]{:S(2)}, u32[]{:S(2)}) collective-permute-start(bf16[192,128]{1,0:T(8,128)(2,1)S(1)} %shard_map.85.refs_4_), channel_id=1, source_target_pairs={{0,16},{8,24},{16,0},{24,8},{1,17},{9,25},{17,1},{25,9},{2,18},{10... | collective-permute-start | bytes 147464 | tf_op jit(solution)/shard_map/ppermute | solution.py:21
  49.3 0.0 collective-permute-done.14.refs_1_
  49.3 0.3 collective-permute-done.15.refs_2_
  49.6 2.7 %collective-permute-done.16.refs_3_ = bf16[64,512]{1,0:T(8,128)(2,1)S(1)} collective-permute-done((bf16[64,512]{1,0:T(8,128)(2,1)S(1)}, bf16[64,512]{1,0:T(8,128)(2,1)S(1)}, u32[]{:S(2)}, u32[]{:S(2)}) %collective-permute-start.16) | collective-permute-done | bytes 65568 | tf_op jit(solution)/shard_map/ppermute | solution.py:21
  52.3 0.0 collective-permute-done.18.refs_5_
  52.3 0.1 collective-permute-start.19
  52.4 1.3 %collective-permute-done.19.refs_1_ = bf16[384,128]{1,0:T(8,128)(2,1)S(1)} collective-permute-done((bf16[384,128]{1,0:T(8,128)(2,1)S(1)}, bf16[384,128]{1,0:T(8,128)(2,1)S(1)}, u32[]{:S(2)}, u32[]{:S(2)}) %collective-permute-start.19) | collective-permute-done | bytes 98336 | tf_op jit(solution)/shard_map/ppermute | solution.py:21
  53.7 0.5 shard_map.87.refs_0_
  54.2 0.7 %collective-permute-start.20 = (f32[8,8]{1,0:T(8,128)S(1)}, f32[8,8]{1,0:T(8,128)S(1)}, u32[]{:S(2)}, u32[]{:S(2)}) collective-permute-start(f32[8,8]{1,0:T(8,128)S(1)} %shard_map.87.refs_0_), channel_id=1, source_target_pairs={{0,1},{1,0},{2,3},{3,2},{4,5},{5,4},{6,7},{7,6},{8,9},{9,8},{10,11... | collective-permute-start | bytes 776 | tf_op jit(solution)/shard_map/ppermute | solution.py:21
  54.8 1.8 %collective-permute-start.21 = (f32[8,8]{1,0:T(8,128)S(1)}, f32[8,8]{1,0:T(8,128)S(1)}, u32[]{:S(2)}, u32[]{:S(2)}) collective-permute-start(f32[8,8]{1,0:T(8,128)S(1)} %shard_map.87.refs_0_), channel_id=1, source_target_pairs={{0,2},{1,3},{2,0},{3,1},{4,6},{5,7},{6,4},{7,5},{8,10},{9,11},{10,... | collective-permute-start | bytes 776 | tf_op jit(solution)/shard_map/ppermute | solution.py:21
  56.7 1.0 %collective-permute-start.22 = (f32[8,8]{1,0:T(8,128)S(1)}, f32[8,8]{1,0:T(8,128)S(1)}, u32[]{:S(2)}, u32[]{:S(2)}) collective-permute-start(f32[8,8]{1,0:T(8,128)S(1)} %shard_map.87.refs_0_), channel_id=1, source_target_pairs={{0,3},{1,2},{2,1},{3,0},{4,7},{5,6},{6,5},{7,4},{8,11},{9,10},{10,... | collective-permute-start | bytes 776 | tf_op jit(solution)/shard_map/ppermute | solution.py:21
  57.7 0.7 %shard_map.84 = bf16[64,2048]{1,0:T(8,128)(2,1)} custom-call(bf16[64,512]{1,0:T(8,128)(2,1)S(1)} %get-tuple-element.30.refs_0_, bf16[64,512]{1,0:T(8,128)(2,1)S(1)} %collective-permute-done.14.refs_1_, bf16[64,512]{1,0:T(8,128)(2,1)S(1)} %collective-permute-done.15.refs_2_, bf16[64,512]{1,0:T(8,128)(2,1)S(1)} %collective-permute-done.16.refs_3_), custom_call_target="tpu_custom_call" | custom-call | tf_op jit(solution)/shard_map/pallas_call | solution.py:29
  58.4 0.0 collective-permute-done.20.refs_1_
  58.4 0.0 collective-permute-done.21.refs_2_
  58.4 2.7 %collective-permute-done.22.refs_3_ = f32[8,8]{1,0:T(8,128)S(1)} collective-permute-done((f32[8,8]{1,0:T(8,128)S(1)}, f32[8,8]{1,0:T(8,128)S(1)}, u32[]{:S(2)}, u32[]{:S(2)}) %collective-permute-start.22) | collective-permute-done | bytes 288 | tf_op jit(solution)/shard_map/ppermute | solution.py:21
  61.2 0.7 %shard_map.88 = f32[8,8]{1,0:T(8,128)} custom-call(f32[8,8]{1,0:T(8,128)S(1)} %shard_map.87.refs_0_, f32[8,8]{1,0:T(8,128)S(1)} %collective-permute-done.20.refs_1_, f32[8,8]{1,0:T(8,128)S(1)} %collective-permute-done.21.refs_2_, f32[8,8]{1,0:T(8,128)S(1)} %collective-permute-done.22.refs_3_), custom_call_target="tpu_custom_call" | custom-call | tf_op jit(solution)/shard_map/pallas_call | solution.py:29
  (6 shorter events, 0.1 us)
Async XLA Ops:
  2.0 13.2 %collective-permute-start = (bf16[384,512]{1,0:T(8,128)(2,1)S(1)}, bf16[384,512]{1,0:T(8,128)(2,1)S(1)}, u32[]{:S(2)}, u32[]{:S(2)}) collective-permute-start(bf16[384,512]{1,0:T(8,128)(2,1)S(1)} %get-tuple-element.18), channel_id=1, source_target_pairs={{0,1},{1,0},{2,3},{3,2},{4,5},{5,4},{6,7},{7,6},{8,9},{9,8},{10,11... | collective-permute-start | bytes 1179656 | tf_op jit(solution)/shard_map/ppermute | solution.py:21
  5.0 4.4 %collective-permute-start.1 = (bf16[32,1024]{1,0:T(8,128)(2,1)S(1)}, bf16[32,1024]{1,0:T(8,128)(2,1)S(1)}, u32[]{:S(2)}, u32[]{:S(2)}) collective-permute-start(bf16[32,1024]{1,0:T(8,128)(2,1)S(1)} %get-tuple-element.19.refs_0_), channel_id=1, source_target_pairs={{0,2},{1,3},{2,0},{3,1},{4,6},{5,7},{6,4},{7,5},{8,10},{9,11},{10,... | collective-permute-start | bytes 196616 | tf_op jit(solution)/shard_map/ppermute | solution.py:21
  6.5 7.0 %collective-permute-start.2 = (bf16[32,1024]{1,0:T(8,128)(2,1)S(1)}, bf16[32,1024]{1,0:T(8,128)(2,1)S(1)}, u32[]{:S(2)}, u32[]{:S(2)}) collective-permute-start(bf16[32,1024]{1,0:T(8,128)(2,1)S(1)} %get-tuple-element.19.refs_0_), channel_id=1, source_target_pairs={{0,4},{1,5},{2,6},{3,7},{4,0},{5,1},{6,2},{7,3},{8,12},{9,13},{10,... | collective-permute-start | bytes 196616 | tf_op jit(solution)/shard_map/ppermute | solution.py:21
  9.1 6.1 %collective-permute-start.3 = (bf16[32,1024]{1,0:T(8,128)(2,1)S(1)}, bf16[32,1024]{1,0:T(8,128)(2,1)S(1)}, u32[]{:S(2)}, u32[]{:S(2)}) collective-permute-start(bf16[32,1024]{1,0:T(8,128)(2,1)S(1)} %get-tuple-element.19.refs_0_), channel_id=1, source_target_pairs={{0,6},{1,7},{2,4},{3,5},{4,2},{5,3},{6,0},{7,1},{8,14},{9,15},{10,... | collective-permute-start | bytes 196616 | tf_op jit(solution)/shard_map/ppermute | solution.py:21
  15.2 10.5 %copy-start.1 = (bf16[192,2048]{1,0:T(8,128)(2,1)S(1)}, bf16[192,2048]{1,0:T(8,128)(2,1)}, u32[]{:S(2)}) copy-start(bf16[192,2048]{1,0:T(8,128)(2,1)} %up_ref.1) | copy-start | bytes 2359300
  15.2 10.5 %copy-start = (bf16[192,2048]{1,0:T(8,128)(2,1)S(1)}, bf16[192,2048]{1,0:T(8,128)(2,1)}, u32[]{:S(2)}) copy-start(bf16[192,2048]{1,0:T(8,128)(2,1)} %gate_ref.1) | copy-start | bytes 2359300
  15.2 6.4 %collective-permute-start.5 = (bf16[128,1024]{1,0:T(8,128)(2,1)S(1)}, bf16[128,1024]{1,0:T(8,128)(2,1)S(1)}, u32[]{:S(2)}, u32[]{:S(2)}) collective-permute-start(bf16[128,1024]{1,0:T(8,128)(2,1)S(1)} %shard_map.78.after_ref.near_ref), channel_id=1, source_target_pairs={{0,1},{1,0},{2,3},{3,2},{4,5},{5,4},{6,7},{7,6},{8,9},{9,8},{10,11... | collective-permute-start | bytes 786440 | tf_op jit(solution)/shard_map/ppermute | solution.py:21
  15.9 9.8 %copy-start.2 = (f32[1,64]{1,0:T(1,128)S(1)}, f32[1,64]{1,0:T(1,128)}, u32[]{:S(2)}) copy-start(f32[1,64]{1,0:T(1,128)} %route_ref.1) | copy-start | bytes 772
  16.0 9.8 %collective-permute-start.4 = (bf16[384,512]{1,0:T(8,128)(2,1)S(1)}, bf16[384,512]{1,0:T(8,128)(2,1)S(1)}, u32[]{:S(2)}, u32[]{:S(2)}) collective-permute-start(bf16[384,512]{1,0:T(8,128)(2,1)S(1)} %shard_map.79), channel_id=1, source_target_pairs={{0,2},{1,3},{2,0},{3,1},{4,6},{5,7},{6,4},{7,5},{8,10},{9,11},{10,... | collective-permute-start | bytes 1179656 | tf_op jit(solution)/shard_map/ppermute | solution.py:21
  17.6 4.1 %collective-permute-start.6 = (bf16[128,1024]{1,0:T(8,128)(2,1)S(1)}, bf16[128,1024]{1,0:T(8,128)(2,1)S(1)}, u32[]{:S(2)}, u32[]{:S(2)}) collective-permute-start(bf16[128,1024]{1,0:T(8,128)(2,1)S(1)} %shard_map.78.after_ref.near_ref), channel_id=1, source_target_pairs={{0,8},{8,0},{16,24},{24,16},{1,9},{9,1},{17,25},{25,17},{2,10},{10... | collective-permute-start | bytes 786440 | tf_op jit(solution)/shard_map/ppermute | solution.py:21
  21.7 4.1 %collective-permute-start.7 = (bf16[128,1024]{1,0:T(8,128)(2,1)S(1)}, bf16[128,1024]{1,0:T(8,128)(2,1)S(1)}, u32[]{:S(2)}, u32[]{:S(2)}) collective-permute-start(bf16[128,1024]{1,0:T(8,128)(2,1)S(1)} %collective-permute-done.5.far_ref), channel_id=1, source_target_pairs={{0,8},{8,0},{16,24},{24,16},{1,9},{9,1},{17,25},{25,17},{2,10},{10... | collective-permute-start | bytes 786440 | tf_op jit(solution)/shard_map/ppermute | solution.py:21
  26.8 6.0 %collective-permute-start.10 = (bf16[208,256]{1,0:T(8,128)(2,1)S(1)}, bf16[208,256]{1,0:T(8,128)(2,1)S(1)}, u32[]{:S(2)}, u32[]{:S(2)}) collective-permute-start(bf16[208,256]{1,0:T(8,128)(2,1)S(1)} %shard_map.80.refs_0_), channel_id=1, source_target_pairs={{0,3},{1,2},{2,1},{3,0},{4,7},{5,6},{6,5},{7,4},{8,11},{9,10},{10,... | collective-permute-start | bytes 319496 | tf_op jit(solution)/shard_map/ppermute | solution.py:21
  28.4 5.4 %collective-permute-start.8 = (bf16[208,256]{1,0:T(8,128)(2,1)S(1)}, bf16[208,256]{1,0:T(8,128)(2,1)S(1)}, u32[]{:S(2)}, u32[]{:S(2)}) collective-permute-start(bf16[208,256]{1,0:T(8,128)(2,1)S(1)} %shard_map.80.refs_0_), channel_id=1, source_target_pairs={{0,1},{1,0},{2,3},{3,2},{4,5},{5,4},{6,7},{7,6},{8,9},{9,8},{10,11... | collective-permute-start | bytes 319496 | tf_op jit(solution)/shard_map/ppermute | solution.py:21
  29.9 4.7 %collective-permute-start.9 = (bf16[208,256]{1,0:T(8,128)(2,1)S(1)}, bf16[208,256]{1,0:T(8,128)(2,1)S(1)}, u32[]{:S(2)}, u32[]{:S(2)}) collective-permute-start(bf16[208,256]{1,0:T(8,128)(2,1)S(1)} %shard_map.80.refs_0_), channel_id=1, source_target_pairs={{0,2},{1,3},{2,0},{3,1},{4,6},{5,7},{6,4},{7,5},{8,10},{9,11},{10,... | collective-permute-start | bytes 319496 | tf_op jit(solution)/shard_map/ppermute | solution.py:21
  35.4 3.9 %collective-permute-start.11 = (bf16[96,128]{1,0:T(8,128)(2,1)S(1)}, bf16[96,128]{1,0:T(8,128)(2,1)S(1)}, u32[]{:S(2)}, u32[]{:S(2)}) collective-permute-start(bf16[96,128]{1,0:T(8,128)(2,1)S(1)} %get-tuple-element.27), channel_id=1, source_target_pairs={{0,1},{1,0},{2,3},{3,2},{4,5},{5,4},{6,7},{7,6},{8,9},{9,8},{10,11... | collective-permute-start | bytes 73736 | tf_op jit(solution)/shard_map/ppermute | solution.py:21
  36.0 3.8 %collective-permute-start.12 = (bf16[96,128]{1,0:T(8,128)(2,1)S(1)}, bf16[96,128]{1,0:T(8,128)(2,1)S(1)}, u32[]{:S(2)}, u32[]{:S(2)}) collective-permute-start(bf16[96,128]{1,0:T(8,128)(2,1)S(1)} %get-tuple-element.28), channel_id=1, source_target_pairs={{0,2},{1,3},{2,0},{3,1},{4,6},{5,7},{6,4},{7,5},{8,10},{9,11},{10,... | collective-permute-start | bytes 73736 | tf_op jit(solution)/shard_map/ppermute | solution.py:21
  36.6 4.7 %collective-permute-start.13 = (bf16[96,128]{1,0:T(8,128)(2,1)S(1)}, bf16[96,128]{1,0:T(8,128)(2,1)S(1)}, u32[]{:S(2)}, u32[]{:S(2)}) collective-permute-start(bf16[96,128]{1,0:T(8,128)(2,1)S(1)} %get-tuple-element.29), channel_id=1, source_target_pairs={{0,3},{1,2},{2,1},{3,0},{4,7},{5,6},{6,5},{7,4},{8,11},{9,10},{10,... | collective-permute-start | bytes 73736 | tf_op jit(solution)/shard_map/ppermute | solution.py:21
  41.4 6.4 %collective-permute-start.17 = (bf16[96,128]{1,0:T(8,128)(2,1)S(1)}, bf16[96,128]{1,0:T(8,128)(2,1)S(1)}, u32[]{:S(2)}, u32[]{:S(2)}) collective-permute-start(bf16[96,128]{1,0:T(8,128)(2,1)S(1)} %shard_map.82.refs_4_.refs_0_), channel_id=1, source_target_pairs={{0,4},{1,5},{2,6},{3,7},{4,0},{5,1},{6,2},{7,3},{8,12},{9,13},{10,... | collective-permute-start | bytes 73736 | tf_op jit(solution)/shard_map/ppermute | solution.py:21
  44.3 5.1 %collective-permute-start.14 = (bf16[64,512]{1,0:T(8,128)(2,1)S(1)}, bf16[64,512]{1,0:T(8,128)(2,1)S(1)}, u32[]{:S(2)}, u32[]{:S(2)}) collective-permute-start(bf16[64,512]{1,0:T(8,128)(2,1)S(1)} %get-tuple-element.31), channel_id=1, source_target_pairs={{0,1},{1,0},{2,3},{3,2},{4,5},{5,4},{6,7},{7,6},{8,9},{9,8},{10,11... | collective-permute-start | bytes 196616 | tf_op jit(solution)/shard_map/ppermute | solution.py:21
  45.3 4.3 %collective-permute-start.15 = (bf16[64,512]{1,0:T(8,128)(2,1)S(1)}, bf16[64,512]{1,0:T(8,128)(2,1)S(1)}, u32[]{:S(2)}, u32[]{:S(2)}) collective-permute-start(bf16[64,512]{1,0:T(8,128)(2,1)S(1)} %get-tuple-element.32), channel_id=1, source_target_pairs={{0,2},{1,3},{2,0},{3,1},{4,6},{5,7},{6,4},{7,5},{8,10},{9,11},{10,... | collective-permute-start | bytes 196616 | tf_op jit(solution)/shard_map/ppermute | solution.py:21
  47.2 5.2 %collective-permute-start.16 = (bf16[64,512]{1,0:T(8,128)(2,1)S(1)}, bf16[64,512]{1,0:T(8,128)(2,1)S(1)}, u32[]{:S(2)}, u32[]{:S(2)}) collective-permute-start(bf16[64,512]{1,0:T(8,128)(2,1)S(1)} %get-tuple-element.33), channel_id=1, source_target_pairs={{0,3},{1,2},{2,1},{3,0},{4,7},{5,6},{6,5},{7,4},{8,11},{9,10},{10,... | collective-permute-start | bytes 196616 | tf_op jit(solution)/shard_map/ppermute | solution.py:21
  47.7 4.6 %collective-permute-start.18 = (bf16[192,128]{1,0:T(8,128)(2,1)S(1)}, bf16[192,128]{1,0:T(8,128)(2,1)S(1)}, u32[]{:S(2)}, u32[]{:S(2)}) collective-permute-start(bf16[192,128]{1,0:T(8,128)(2,1)S(1)} %shard_map.85.refs_4_), channel_id=1, source_target_pairs={{0,16},{8,24},{16,0},{24,8},{1,17},{9,25},{17,1},{25,9},{2,18},{10... | collective-permute-start | bytes 147464 | tf_op jit(solution)/shard_map/ppermute | solution.py:21
  52.3 1.4 %collective-permute-start.19 = (bf16[384,128]{1,0:T(8,128)(2,1)S(1)}, bf16[384,128]{1,0:T(8,128)(2,1)S(1)}, u32[]{:S(2)}, u32[]{:S(2)}) collective-permute-start(bf16[384,128]{1,0:T(8,128)(2,1)S(1)} %shard_map.86.refs_0_), channel_id=1, source_target_pairs={{0,8},{8,0},{16,24},{24,16},{1,9},{9,1},{17,25},{25,17},{2,10},{10... | collective-permute-start | bytes 294920 | tf_op jit(solution)/shard_map/ppermute | solution.py:21
  54.2 4.2 %collective-permute-start.20 = (f32[8,8]{1,0:T(8,128)S(1)}, f32[8,8]{1,0:T(8,128)S(1)}, u32[]{:S(2)}, u32[]{:S(2)}) collective-permute-start(f32[8,8]{1,0:T(8,128)S(1)} %shard_map.87.refs_0_), channel_id=1, source_target_pairs={{0,1},{1,0},{2,3},{3,2},{4,5},{5,4},{6,7},{7,6},{8,9},{9,8},{10,11... | collective-permute-start | bytes 776 | tf_op jit(solution)/shard_map/ppermute | solution.py:21
  54.8 3.6 %collective-permute-start.21 = (f32[8,8]{1,0:T(8,128)S(1)}, f32[8,8]{1,0:T(8,128)S(1)}, u32[]{:S(2)}, u32[]{:S(2)}) collective-permute-start(f32[8,8]{1,0:T(8,128)S(1)} %shard_map.87.refs_0_), channel_id=1, source_target_pairs={{0,2},{1,3},{2,0},{3,1},{4,6},{5,7},{6,4},{7,5},{8,10},{9,11},{10,... | collective-permute-start | bytes 776 | tf_op jit(solution)/shard_map/ppermute | solution.py:21
  56.7 4.5 %collective-permute-start.22 = (f32[8,8]{1,0:T(8,128)S(1)}, f32[8,8]{1,0:T(8,128)S(1)}, u32[]{:S(2)}, u32[]{:S(2)}) collective-permute-start(f32[8,8]{1,0:T(8,128)S(1)} %shard_map.87.refs_0_), channel_id=1, source_target_pairs={{0,3},{1,2},{2,1},{3,0},{4,7},{5,6},{6,5},{7,4},{8,11},{9,10},{10,... | collective-permute-start | bytes 776 | tf_op jit(solution)/shard_map/ppermute | solution.py:21

commit v9 on v8

--- a/solution.py
+++ b/solution.py
@@ -107,8 +107,8 @@
 
 def features_kernel(gathered, *refs):
     hidden_refs, (own_ref, x_ref, z_ref) = refs[:HOLDERS], refs[HOLDERS : HOLDERS + 3]
-    block_refs, centered_refs = refs[HOLDERS + 3 : 2 * HOLDERS + 3], refs[2 * HOLDERS + 3 : -3]
-    route_ref, features_ref, whole_ref = refs[-3:]
+    kept_ref, z_ref2, x_ref2 = refs[HOLDERS + 3 : HOLDERS + 6]
+    centered_refs, (route_ref, features_ref, whole_ref) = refs[HOLDERS + 6 : -3], refs[-3:]
     depth, tokens = own_ref.shape[0], hidden_refs[0].shape[1]
     part, members = tokens // HOLDERS, lax.axis_size("tok")
     rows = tokens // members
@@ -143,11 +143,14 @@
         whole_ref[...] = centered.astype(bf16)
         half = tokens // 2
         count = half // HOLDERS
-        for m, centered_ref in enumerate(centered_refs):
+        for m in range(HOLDERS):
             first = (holder() ^ m) * count
             for at, (row, left) in enumerate(((0, 0), (0, half), (half, half))):
                 rows_there = pl.ds(pl.multiple_of(first + row, count), count)
-                centered_ref[at * count : (at + 1) * count] = whole_ref[rows_there, left : left + half]
+                at += 3 * (m // 2)
+                centered_refs[m % 2][at * count : (at + 1) * count] = whole_ref[
+                    rows_there, left : left + half
+                ]
     else:
         (centered_ref,) = centered_refs
         centered = centered.astype(bf16)
@@ -158,14 +161,17 @@
                     i * TILE : (i + 1) * TILE, j * LANES : (j + 1) * LANES
                 ]
                 at += 1
-    for m, block_ref in enumerate(block_refs):
-        for piece in range(part // rows):
-            block_ref[piece * rows : (piece + 1) * rows] = features_ref[place(m, piece)]
-
-
-def place_kernel(*refs):
-    blocks, out_ref, sems = refs[:HOLDERS], refs[HOLDERS], refs[HOLDERS + 1]
-    width = blocks[0].shape[1]
+    for block_ref, distances in ((kept_ref, (0,)), (z_ref2, (2,)), (x_ref2, (1, 3))):
+        for at, m in enumerate(distances):
+            for piece in range(part // rows):
+                top = at * part + piece * rows
+                block_ref[top : top + rows] = features_ref[place(m, piece)]
+
+
+def place_kernel(kept_ref, x_ref, z_ref, out_ref, sems):
+    rows, width = kept_ref.shape
+    top, bottom = pl.ds(0, rows), pl.ds(rows, rows)
+    blocks = (kept_ref, x_ref.at[top], z_ref.at[top], z_ref.at[bottom])
     copies = []
     for m, block in enumerate(blocks):
         columns = pl.ds(pl.multiple_of((holder() ^ m) * width, width), width)
@@ -175,15 +181,18 @@
         copy.wait()
 
 
-def sum_kernel(*refs):
-    total = refs[0][...].astype(f32)
-    for ref in refs[1:-1]:
-        total = total + ref[...].astype(f32)
-    refs[-1][...] = total.astype(bf16)
-
-
-def join_kernel(*refs):
-    low_ref, high_ref, out_ref = refs[-3:]
+def fold_kernel(own_ref, got_ref, kept_ref, sent_ref):
+    rows = kept_ref.shape[0]
+    total = own_ref[...].astype(f32) + got_ref[...].astype(f32)
+    kept_ref[...] = total[:rows]
+    sent_ref[...] = total[rows:]
+
+
+def sum_kernel(own_ref, got_ref, out_ref):
+    out_ref[...] = (own_ref[...] + got_ref[...]).astype(out_ref.dtype)
+
+
+def join_kernel(low_ref, high_ref, out_ref):
     rows = low_ref.shape[0]
     out_ref[:rows] = low_ref[...]
     out_ref[rows:] = high_ref[...]
@@ -199,7 +208,7 @@
     return lax.fori_loop(0, experts, one, jnp.zeros((experts, experts), f32), unroll=experts <= 8)
 
 
-def pair_kernel(distances, low_ref, high_ref, out_ref, flat_ref):
+def pair_kernel(distances, after_ref, low_ref, high_ref, out_ref, flat_ref):
     experts, rows, _ = flat_ref.shape
     here = lax.axis_index("grp") * (lax.axis_size("tok") // HOLDERS) + lax.axis_index("tok") // HOLDERS
     for m in range(experts):
@@ -221,16 +230,15 @@
 
 
 def cka_kernel(*refs):
-    tables, out_ref, kept_ref = refs[:-2], refs[-2], refs[-1]
-    for m, table in enumerate(tables):
-        kept_ref[pl.ds(holder() ^ m if m or len(tables) > 1 else 0, 1)] = table[...][None]
-    totals = jnp.sum(kept_ref[...], axis=0)
+    totals = refs[0][...]
+    for ref in refs[1:-1]:
+        totals = totals + ref[...]
     shape = totals.shape
     eye = lax.broadcasted_iota(jnp.int32, shape, 0) == lax.broadcasted_iota(jnp.int32, shape, 1)
     diagonal = jnp.where(eye, totals, 0.0)
     down = jnp.sum(diagonal, axis=1, keepdims=True)
     across = jnp.sum(diagonal, axis=0, keepdims=True)
-    out_ref[...] = totals / jnp.sqrt(down * across)
+    refs[-1][...] = totals / jnp.sqrt(down * across)
 
 
 def hold_kernel(*refs):
@@ -308,10 +316,11 @@
     part_shape = (3 * half // HOLDERS, half)
     gathered = experts * part_shape[0] * part_shape[1] <= 1 << 20
     entries = tokens * tokens // LANES
-    outs = [part_shape] * HOLDERS if gathered else [(entries, LANES)]
-    outcome = call(
+    both = (2 * part_shape[0], half)
+    outs = [both] * 2 if gathered else [(entries, LANES)]
+    kept, for_z, for_x, *centered = call(
         lambda *refs: features_kernel(gathered, *refs),
-        [jax.ShapeDtypeStruct((token_part, part), bf16)] * HOLDERS
+        [jax.ShapeDtypeStruct((token_part * n, part), bf16) for n in (1, 1, 2)]
         + [jax.ShapeDtypeStruct(shape, bf16) for shape in outs],
         [VMEM] * (HOLDERS + 3),
         (*hiddens, down_own, down_x, down_z),
@@ -321,15 +330,25 @@
             pltpu.VMEM((tokens, tokens), bf16),
         ],
     )
-    blocks, centered = outcome[:HOLDERS], outcome[HOLDERS:]
+
+    def features_onward(got_x, after):
+        out = jax.ShapeDtypeStruct(got_x.shape, bf16)
+        return swapped(call(onward_kernel, out, [ANY, VMEM, VMEM], (after, for_z, got_x)), "tok", 2)
+
     table_shape = jax.ShapeDtypeStruct((experts, experts), f32)
     if gathered:
-        centered = [swapped(c, "tok", m) if m else c for m, c in enumerate(centered)]
+        ours, theirs = centered
+        wide = jax.ShapeDtypeStruct(part_shape, f32)
+        kept_part, sent_part = call(
+            fold_kernel, [wide] * 2, [VMEM] * 2, (ours, swapped(theirs, "tok", 1))
+        )
         low = call(
-            sum_kernel, jax.ShapeDtypeStruct(part_shape, bf16), [VMEM] * HOLDERS, centered
+            sum_kernel,
+            jax.ShapeDtypeStruct(part_shape, bf16),
+            [VMEM] * 2,
+            (kept_part, swapped(sent_part, "tok", 2)),
         )
-        blocks = held(blocks, low)
-        blocks = [swapped(b, "tok", m) if m else b for m, b in enumerate(blocks)]
+        got_x = swapped(held([for_x], low)[0], "tok", 1)
         steps = [("tok", 1 << b) for b in range(2, members.bit_length() - 1)]
         steps += [("grp", 1 << b) for b in range(groups.bit_length() - 2, -1, -1)]
         distances = [0]
@@ -339,20 +358,21 @@
             high = swapped(low, axis, mask)
             if at < len(steps) - 1:
                 joined = jax.ShapeDtypeStruct((2 * low.shape[0], half), bf16)
-                after = blocks if at == len(steps) - 2 else []
-                low = call(
-                    join_kernel, joined, [ANY] * len(after) + [VMEM] * 2, (*after, low, high)
-                )
+                low = call(join_kernel, joined, [VMEM] * 2, (low, high))
+                if at == 0:
+                    got_z = features_onward(got_x, low)
         table = call(
             lambda *refs: pair_kernel(distances, *refs),
             table_shape,
-            [VMEM] * 2,
-            (low, high),
+            [ANY] + [VMEM] * 2,
+            (got_z, low, high),
             scratch=[pltpu.VMEM((experts, *part_shape), f32)],
         )
-        tables = [swapped(table, "tok", m) if m else table for m in range(HOLDERS)]
+        table = call(sum_kernel, table_shape, [VMEM] * 2, (table, swapped(table, "tok", 1)))
+        tables = [table, swapped(table, "tok", 2)]
     else:
-        blocks = [swapped(b, "tok", m) if m else b for m, b in enumerate(blocks)]
+        got_x = swapped(for_x, "tok", 1)
+        got_z = features_onward(got_x, kept)
         arrived = lax.all_to_all(
             centered[0], ("grp", "tok"), split_axis=0, concat_axis=0, tiled=True
         )
@@ -364,19 +384,13 @@
             scratch=[pltpu.VMEM((experts, entries // devices, LANES), f32)],
         )
         tables = [lax.psum(table, ("grp", "tok"))]
-    cka = call(
-        cka_kernel,
-        table_shape,
-        [VMEM] * len(tables),
-        tables,
-        scratch=[pltpu.VMEM((len(tables), experts, experts), f32)],
-    )
+    cka = call(cka_kernel, table_shape, [VMEM] * len(tables), tables)
 
     features = call(
         place_kernel,
         jax.ShapeDtypeStruct((token_part, model), bf16),
-        [VMEM] * HOLDERS,
-        blocks,
+        [VMEM] * 3,
+        (kept, got_x, got_z),
         out_specs=ANY,
         scratch=[pltpu.SemaphoreType.DMA((HOLDERS,))],
     )

time: 62 us -> 64.5 us (1.040)
  waiting for transfers between devices: 27.7 us -> 36.9 us
  starting transfers between devices: 28.3 us -> 21.6 us
    ppermute x23 -> x20, waiting for transfers between devices: 27.7 us -> 36.9 us  [swapped(): lax.ppermute(array, axis, [(i, i ^ mask) for i in range(lax.axis_size(axi...]
    ppermute x23 -> x20, starting transfers between devices: 28.3 us -> 21.6 us  [swapped(): lax.ppermute(array, axis, [(i, i ^ mask) for i in range(lax.axis_size(axi...]
    pallas_call x12 -> x15, Pallas kernels: 5.12 us -> 5.13 us  [call(): pl.pallas_call(body, out_shape=outs, in_specs=in_specs, out_specs=jax.tre...]
  transfers between devices with their start and end apart: 23 -> 20, of which waited for: 14 -> 15; matrix products, arithmetic and copies ran while one was open for 0% -> 0% of each run, Pallas kernels for 1% -> 1%
where the time goes in v9:
time: 64.5 us; the launch traced here: 64.4 us
  waiting for transfers between devices  36.9 us (57%)
  starting transfers between devices  21.6 us (33%)
  Pallas kernels  5.13 us (8%)
  between operations  0.74 us (1%)
    ppermute x20, waiting for transfers between devices, swapped(): lax.ppermute(array, axis, [(i, i ^ mask) for i in range(lax.axis_size(axi...  36.9 us
    ppermute x20, starting transfers between devices, swapped(): lax.ppermute(array, axis, [(i, i ^ mask) for i in range(lax.axis_size(axi...  21.6 us
    pallas_call x15, Pallas kernels, call(): pl.pallas_call(body, out_shape=outs, in_specs=in_specs, out_specs=jax.tre...  5.13 us
  transfers between devices with their start and end apart: 20, of which 15 were waited for; matrix products, arithmetic and copies ran while one was open for 0% of the time, Pallas kernels for 1%

profile of v9, /device:TPU:0, one launch (start us, length us, event | category | flops | bytes accessed | tf_op | source)
XLA Modules:
  0.0 64.4 jit_solution(11734268805202138141)
XLA Ops:
  0.6 1.3 %shard_map.77 = (bf16[32,1024]{1,0:T(8,128)(2,1)S(1)}, bf16[192,512]{1,0:T(8,128)(2,1)S(1)}, bf16[192,512]{1,0:T(8,128)(2,1)S(1)}, bf16[384,512]{1,0:T(8,128)(2,1)S(1)}) custom-call(bf16[32,2048]{1,0:T(8,128)(2,1)} %states_hbm.1, f32[1,2048]{1,0:T(1,128)} %bitcast.1, bf16[192,2048]{1,0:T(8,128)(2,1)} %down_hbm.1), custom_call_target="tpu_custom_call" | custom-call | tf_op jit(solution)/shard_map/pallas_call | solution.py:29
  2.0 3.0 %collective-permute-start = (bf16[384,512]{1,0:T(8,128)(2,1)S(1)}, bf16[384,512]{1,0:T(8,128)(2,1)S(1)}, u32[]{:S(2)}, u32[]{:S(2)}) collective-permute-start(bf16[384,512]{1,0:T(8,128)(2,1)S(1)} %get-tuple-element.13), channel_id=1, source_target_pairs={{0,1},{1,0},{2,3},{3,2},{4,5},{5,4},{6,7},{7,6},{8,9},{9,8},{10,11... | collective-permute-start | bytes 1179656 | tf_op jit(solution)/shard_map/ppermute | solution.py:21
  5.0 1.6 %collective-permute-start.1 = (bf16[32,1024]{1,0:T(8,128)(2,1)S(1)}, bf16[32,1024]{1,0:T(8,128)(2,1)S(1)}, u32[]{:S(2)}, u32[]{:S(2)}) collective-permute-start(bf16[32,1024]{1,0:T(8,128)(2,1)S(1)} %get-tuple-element.14.refs_0_), channel_id=1, source_target_pairs={{0,2},{1,3},{2,0},{3,1},{4,6},{5,7},{6,4},{7,5},{8,10},{9,11},{10,... | collective-permute-start | bytes 196616 | tf_op jit(solution)/shard_map/ppermute | solution.py:21
  6.5 2.6 %collective-permute-start.2 = (bf16[32,1024]{1,0:T(8,128)(2,1)S(1)}, bf16[32,1024]{1,0:T(8,128)(2,1)S(1)}, u32[]{:S(2)}, u32[]{:S(2)}) collective-permute-start(bf16[32,1024]{1,0:T(8,128)(2,1)S(1)} %get-tuple-element.14.refs_0_), channel_id=1, source_target_pairs={{0,4},{1,5},{2,6},{3,7},{4,0},{5,1},{6,2},{7,3},{8,12},{9,13},{10,... | collective-permute-start | bytes 196616 | tf_op jit(solution)/shard_map/ppermute | solution.py:21
  9.1 0.2 collective-permute-start.3
  9.4 0.0 collective-permute-done.1.refs_1_
  9.4 4.2 %collective-permute-done.2.refs_2_ = bf16[32,1024]{1,0:T(8,128)(2,1)S(1)} collective-permute-done((bf16[32,1024]{1,0:T(8,128)(2,1)S(1)}, bf16[32,1024]{1,0:T(8,128)(2,1)S(1)}, u32[]{:S(2)}, u32[]{:S(2)}) %collective-permute-start.2) | collective-permute-done | bytes 65568 | tf_op jit(solution)/shard_map/ppermute | solution.py:21
  13.5 1.7 %collective-permute-done.3.refs_3_ = bf16[32,1024]{1,0:T(8,128)(2,1)S(1)} collective-permute-done((bf16[32,1024]{1,0:T(8,128)(2,1)S(1)}, bf16[32,1024]{1,0:T(8,128)(2,1)S(1)}, u32[]{:S(2)}, u32[]{:S(2)}) %collective-permute-start.3) | collective-permute-done | bytes 65568 | tf_op jit(solution)/shard_map/ppermute | solution.py:21
  15.2 0.0 collective-permute-done.after_ref.got_ref.refs_5_
  15.2 0.0 copy-start.1
  15.2 0.0 copy-start
  15.2 0.7 %collective-permute-start.5 = (bf16[128,1024]{1,0:T(8,128)(2,1)S(1)}, bf16[128,1024]{1,0:T(8,128)(2,1)S(1)}, u32[]{:S(2)}, u32[]{:S(2)}) collective-permute-start(bf16[128,1024]{1,0:T(8,128)(2,1)S(1)} %shard_map.78.after_ref.near_ref), channel_id=1, source_target_pairs={{0,1},{1,0},{2,3},{3,2},{4,5},{5,4},{6,7},{7,6},{8,9},{9,8},{10,11... | collective-permute-start | bytes 786440 | tf_op jit(solution)/shard_map/ppermute | solution.py:21
  15.9 0.0 copy-start.2
  16.0 1.6 %collective-permute-start.4 = (bf16[384,512]{1,0:T(8,128)(2,1)S(1)}, bf16[384,512]{1,0:T(8,128)(2,1)S(1)}, u32[]{:S(2)}, u32[]{:S(2)}) collective-permute-start(bf16[384,512]{1,0:T(8,128)(2,1)S(1)} %shard_map.79), channel_id=1, source_target_pairs={{0,2},{1,3},{2,0},{3,1},{4,6},{5,7},{6,4},{7,5},{8,10},{9,11},{10,... | collective-permute-start | bytes 1179656 | tf_op jit(solution)/shard_map/ppermute | solution.py:21
  17.6 0.0 collective-permute-start.6
  17.6 4.1 %collective-permute-done.5.far_ref = bf16[128,1024]{1,0:T(8,128)(2,1)S(1)} collective-permute-done((bf16[128,1024]{1,0:T(8,128)(2,1)S(1)}, bf16[128,1024]{1,0:T(8,128)(2,1)S(1)}, u32[]{:S(2)}, u32[]{:S(2)}) %collective-permute-start.5) | collective-permute-done | bytes 262176 | tf_op jit(solution)/shard_map/ppermute | solution.py:21
  21.7 0.0 collective-permute-start.7
  21.7 0.0 collective-permute-done.6.near2_ref
  21.7 4.0 %collective-permute-done.4.after_ref.refs_6_ = bf16[384,512]{1,0:T(8,128)(2,1)S(1)} collective-permute-done((bf16[384,512]{1,0:T(8,128)(2,1)S(1)}, bf16[384,512]{1,0:T(8,128)(2,1)S(1)}, u32[]{:S(2)}, u32[]{:S(2)}) %collective-permute-start.4) | collective-permute-done | bytes 393248 | tf_op jit(solution)/shard_map/ppermute | solution.py:21
  25.7 0.0 collective-permute-done.7.far2_ref
  25.7 0.0 copy-done.1
  25.7 0.0 copy-done
  25.7 0.0 copy-done.2
  25.7 1.0 %shard_map.80.refs_0_ = bf16[208,256]{1,0:T(8,128)(2,1)S(1)} custom-call(bf16[384,512]{1,0:T(8,128)(2,1)S(1)} %collective-permute-done.4.after_ref.refs_6_, bf16[128,1024]{1,0:T(8,128)(2,1)S(1)} %shard_map.78.after_ref.near_ref, bf16[128,1024]{1,0:T(8,128)(2,1)S(1)} %collective-permute-done.5.far_ref, ...), custom_call_target="tpu_custom_call" | custom-call | tf_op jit(solution)/shard_map/pallas_call | solution.py:29
  26.8 1.6 %collective-permute-start.10 = (bf16[208,256]{1,0:T(8,128)(2,1)S(1)}, bf16[208,256]{1,0:T(8,128)(2,1)S(1)}, u32[]{:S(2)}, u32[]{:S(2)}) collective-permute-start(bf16[208,256]{1,0:T(8,128)(2,1)S(1)} %shard_map.80.refs_0_), channel_id=1, source_target_pairs={{0,3},{1,2},{2,1},{3,0},{4,7},{5,6},{6,5},{7,4},{8,11},{9,10},{10,... | collective-permute-start | bytes 319496 | tf_op jit(solution)/shard_map/ppermute | solution.py:21
  28.4 1.5 %collective-permute-start.8 = (bf16[208,256]{1,0:T(8,128)(2,1)S(1)}, bf16[208,256]{1,0:T(8,128)(2,1)S(1)}, u32[]{:S(2)}, u32[]{:S(2)}) collective-permute-start(bf16[208,256]{1,0:T(8,128)(2,1)S(1)} %shard_map.80.refs_0_), channel_id=1, source_target_pairs={{0,1},{1,0},{2,3},{3,2},{4,5},{5,4},{6,7},{7,6},{8,9},{9,8},{10,11... | collective-permute-start | bytes 319496 | tf_op jit(solution)/shard_map/ppermute | solution.py:21
  29.9 0.4 collective-permute-start.9
  30.3 2.4 %collective-permute-done.10.refs_3_ = bf16[208,256]{1,0:T(8,128)(2,1)S(1)} collective-permute-done((bf16[208,256]{1,0:T(8,128)(2,1)S(1)}, bf16[208,256]{1,0:T(8,128)(2,1)S(1)}, u32[]{:S(2)}, u32[]{:S(2)}) %collective-permute-start.10) | collective-permute-done | bytes 106528 | tf_op jit(solution)/shard_map/ppermute | solution.py:21
  32.7 1.1 %collective-permute-done.8.refs_1_ = bf16[208,256]{1,0:T(8,128)(2,1)S(1)} collective-permute-done((bf16[208,256]{1,0:T(8,128)(2,1)S(1)}, bf16[208,256]{1,0:T(8,128)(2,1)S(1)}, u32[]{:S(2)}, u32[]{:S(2)}) %collective-permute-start.8) | collective-permute-done | bytes 106528 | tf_op jit(solution)/shard_map/ppermute | solution.py:21
  33.8 0.8 %collective-permute-done.9.refs_2_ = bf16[208,256]{1,0:T(8,128)(2,1)S(1)} collective-permute-done((bf16[208,256]{1,0:T(8,128)(2,1)S(1)}, bf16[208,256]{1,0:T(8,128)(2,1)S(1)}, u32[]{:S(2)}, u32[]{:S(2)}) %collective-permute-start.9) | collective-permute-done | bytes 106528 | tf_op jit(solution)/shard_map/ppermute | solution.py:21
  34.6 0.8 %shard_map.81 = (bf16[64,512]{1,0:T(8,128)(2,1)S(1)}, bf16[64,512]{1,0:T(8,128)(2,1)S(1)}, bf16[128,512]{1,0:T(8,128)(2,1)S(1)}, bf16[192,128]{1,0:T(8,128)(2,1)S(1)}, bf16[192,128]{1,0:T(8,128)(2,1)S(1)}) custom-call(bf16[208,256]{1,0:T(8,128)(2,1)S(1)} %shard_map.80.refs_0_, bf16[208,256]{1,0:T(8,128)(2,1)S(1)} %collective-permute-done.8.refs_1_, ...), custom_call_target="tpu_custom_call" | custom-call | tf_op jit(solution)/shard_map/pallas_call | solution.py:29
  35.4 0.6 collective-permute-start.11
  36.0 3.6 %collective-permute-done.11.got_ref = bf16[192,128]{1,0:T(8,128)(2,1)S(1)} collective-permute-done((bf16[192,128]{1,0:T(8,128)(2,1)S(1)}, bf16[192,128]{1,0:T(8,128)(2,1)S(1)}, u32[]{:S(2)}, u32[]{:S(2)}) %collective-permute-start.11) | collective-permute-done | bytes 49184 | tf_op jit(solution)/shard_map/ppermute | solution.py:21
  39.6 0.5 collective-permute-start.12
  40.1 3.6 %collective-permute-done.12.got_ref = f32[96,128]{1,0:T(8,128)S(1)} collective-permute-done((f32[96,128]{1,0:T(8,128)S(1)}, f32[96,128]{1,0:T(8,128)S(1)}, u32[]{:S(2)}, u32[]{:S(2)}) %collective-permute-start.12) | collective-permute-done | bytes 49184 | tf_op jit(solution)/shard_map/ppermute | solution.py:21
  43.7 0.6 collective-permute-start.13
  44.4 2.6 %collective-permute-start.14 = (bf16[96,128]{1,0:T(8,128)(2,1)S(1)}, bf16[96,128]{1,0:T(8,128)(2,1)S(1)}, u32[]{:S(2)}, u32[]{:S(2)}) collective-permute-start(bf16[96,128]{1,0:T(8,128)(2,1)S(1)} %shard_map.83.refs_1_.low_ref), channel_id=1, source_target_pairs={{0,4},{1,5},{2,6},{3,7},{4,0},{5,1},{6,2},{7,3},{8,12},{9,13},{10,... | collective-permute-start | bytes 73736 | tf_op jit(solution)/shard_map/ppermute | solution.py:21
  46.9 2.3 %collective-permute-done.14.high_ref = bf16[96,128]{1,0:T(8,128)(2,1)S(1)} collective-permute-done((bf16[96,128]{1,0:T(8,128)(2,1)S(1)}, bf16[96,128]{1,0:T(8,128)(2,1)S(1)}, u32[]{:S(2)}, u32[]{:S(2)}) %collective-permute-start.14) | collective-permute-done | bytes 24608 | tf_op jit(solution)/shard_map/ppermute | solution.py:21
  49.3 1.7 %collective-permute-start.16 = (bf16[192,128]{1,0:T(8,128)(2,1)S(1)}, bf16[192,128]{1,0:T(8,128)(2,1)S(1)}, u32[]{:S(2)}, u32[]{:S(2)}) collective-permute-start(bf16[192,128]{1,0:T(8,128)(2,1)S(1)} %shard_map.85.after_ref.low_ref), channel_id=1, source_target_pairs={{0,16},{8,24},{16,0},{24,8},{1,17},{9,25},{17,1},{25,9},{2,18},{10... | collective-permute-start | bytes 147464 | tf_op jit(solution)/shard_map/ppermute | solution.py:21
  50.9 0.0 collective-permute-done.13.got_ref.x_ref
  50.9 0.6 collective-permute-start.15
  51.5 1.9 %collective-permute-done.16.high_ref = bf16[192,128]{1,0:T(8,128)(2,1)S(1)} collective-permute-done((bf16[192,128]{1,0:T(8,128)(2,1)S(1)}, bf16[192,128]{1,0:T(8,128)(2,1)S(1)}, u32[]{:S(2)}, u32[]{:S(2)}) %collective-permute-start.16) | collective-permute-done | bytes 49184 | tf_op jit(solution)/shard_map/ppermute | solution.py:21
  53.4 0.1 collective-permute-start.17
  53.4 1.3 %collective-permute-done.17.refs_2_ = bf16[384,128]{1,0:T(8,128)(2,1)S(1)} collective-permute-done((bf16[384,128]{1,0:T(8,128)(2,1)S(1)}, bf16[384,128]{1,0:T(8,128)(2,1)S(1)}, u32[]{:S(2)}, u32[]{:S(2)}) %collective-permute-start.17) | collective-permute-done | bytes 98336 | tf_op jit(solution)/shard_map/ppermute | solution.py:21
  54.7 1.2 %collective-permute-done.15.z_ref.refs_0_ = bf16[128,512]{1,0:T(8,128)(2,1)S(1)} collective-permute-done((bf16[128,512]{1,0:T(8,128)(2,1)S(1)}, bf16[128,512]{1,0:T(8,128)(2,1)S(1)}, u32[]{:S(2)}, u32[]{:S(2)}) %collective-permute-start.15) | collective-permute-done | bytes 131104 | tf_op jit(solution)/shard_map/ppermute | solution.py:21
  56.0 0.5 shard_map.89.own_ref
  56.5 1.3 %collective-permute-start.18 = (f32[8,8]{1,0:T(8,128)S(1)}, f32[8,8]{1,0:T(8,128)S(1)}, u32[]{:S(2)}, u32[]{:S(2)}) collective-permute-start(f32[8,8]{1,0:T(8,128)S(1)} %shard_map.89.own_ref), channel_id=1, source_target_pairs={{0,1},{1,0},{2,3},{3,2},{4,5},{5,4},{6,7},{7,6},{8,9},{9,8},{10,11... | collective-permute-start | bytes 776 | tf_op jit(solution)/shard_map/ppermute | solution.py:21
  57.8 2.3 %collective-permute-done.18.got_ref = f32[8,8]{1,0:T(8,128)S(1)} collective-permute-done((f32[8,8]{1,0:T(8,128)S(1)}, f32[8,8]{1,0:T(8,128)S(1)}, u32[]{:S(2)}, u32[]{:S(2)}) %collective-permute-start.18) | collective-permute-done | bytes 288 | tf_op jit(solution)/shard_map/ppermute | solution.py:21
  60.1 0.5 collective-permute-start.19
  60.6 0.7 %shard_map.87 = bf16[64,2048]{1,0:T(8,128)(2,1)} custom-call(bf16[64,512]{1,0:T(8,128)(2,1)S(1)} %get-tuple-element.17.kept_ref, bf16[128,512]{1,0:T(8,128)(2,1)S(1)} %collective-permute-done.13.got_ref.x_ref, bf16[128,512]{1,0:T(8,128)(2,1)S(1)} %collective-permute-done.15.z_ref.refs_0_), custom_call_target="tpu_custom_call" | custom-call | tf_op jit(solution)/shard_map/pallas_call | solution.py:29
  61.3 2.4 %collective-permute-done.19.refs_1_ = f32[8,8]{1,0:T(8,128)S(1)} collective-permute-done((f32[8,8]{1,0:T(8,128)S(1)}, f32[8,8]{1,0:T(8,128)S(1)}, u32[]{:S(2)}, u32[]{:S(2)}) %collective-permute-start.19) | collective-permute-done | bytes 288 | tf_op jit(solution)/shard_map/ppermute | solution.py:21
  63.7 0.7 %shard_map.91 = f32[8,8]{1,0:T(8,128)} custom-call(f32[8,8]{1,0:T(8,128)S(1)} %shard_map.90.refs_0_, f32[8,8]{1,0:T(8,128)S(1)} %collective-permute-done.19.refs_1_), custom_call_target="tpu_custom_call" | custom-call | tf_op jit(solution)/shard_map/pallas_call | solution.py:29
  (9 shorter events, 0.1 us)
Async XLA Ops:
  2.0 13.2 %collective-permute-start = (bf16[384,512]{1,0:T(8,128)(2,1)S(1)}, bf16[384,512]{1,0:T(8,128)(2,1)S(1)}, u32[]{:S(2)}, u32[]{:S(2)}) collective-permute-start(bf16[384,512]{1,0:T(8,128)(2,1)S(1)} %get-tuple-element.13), channel_id=1, source_target_pairs={{0,1},{1,0},{2,3},{3,2},{4,5},{5,4},{6,7},{7,6},{8,9},{9,8},{10,11... | collective-permute-start | bytes 1179656 | tf_op jit(solution)/shard_map/ppermute | solution.py:21
  5.0 4.4 %collective-permute-start.1 = (bf16[32,1024]{1,0:T(8,128)(2,1)S(1)}, bf16[32,1024]{1,0:T(8,128)(2,1)S(1)}, u32[]{:S(2)}, u32[]{:S(2)}) collective-permute-start(bf16[32,1024]{1,0:T(8,128)(2,1)S(1)} %get-tuple-element.14.refs_0_), channel_id=1, source_target_pairs={{0,2},{1,3},{2,0},{3,1},{4,6},{5,7},{6,4},{7,5},{8,10},{9,11},{10,... | collective-permute-start | bytes 196616 | tf_op jit(solution)/shard_map/ppermute | solution.py:21
  6.5 7.0 %collective-permute-start.2 = (bf16[32,1024]{1,0:T(8,128)(2,1)S(1)}, bf16[32,1024]{1,0:T(8,128)(2,1)S(1)}, u32[]{:S(2)}, u32[]{:S(2)}) collective-permute-start(bf16[32,1024]{1,0:T(8,128)(2,1)S(1)} %get-tuple-element.14.refs_0_), channel_id=1, source_target_pairs={{0,4},{1,5},{2,6},{3,7},{4,0},{5,1},{6,2},{7,3},{8,12},{9,13},{10,... | collective-permute-start | bytes 196616 | tf_op jit(solution)/shard_map/ppermute | solution.py:21
  9.1 6.1 %collective-permute-start.3 = (bf16[32,1024]{1,0:T(8,128)(2,1)S(1)}, bf16[32,1024]{1,0:T(8,128)(2,1)S(1)}, u32[]{:S(2)}, u32[]{:S(2)}) collective-permute-start(bf16[32,1024]{1,0:T(8,128)(2,1)S(1)} %get-tuple-element.14.refs_0_), channel_id=1, source_target_pairs={{0,6},{1,7},{2,4},{3,5},{4,2},{5,3},{6,0},{7,1},{8,14},{9,15},{10,... | collective-permute-start | bytes 196616 | tf_op jit(solution)/shard_map/ppermute | solution.py:21
  15.2 10.5 %copy-start.1 = (bf16[192,2048]{1,0:T(8,128)(2,1)S(1)}, bf16[192,2048]{1,0:T(8,128)(2,1)}, u32[]{:S(2)}) copy-start(bf16[192,2048]{1,0:T(8,128)(2,1)} %up_ref.1) | copy-start | bytes 2359300
  15.2 10.5 %copy-start = (bf16[192,2048]{1,0:T(8,128)(2,1)S(1)}, bf16[192,2048]{1,0:T(8,128)(2,1)}, u32[]{:S(2)}) copy-start(bf16[192,2048]{1,0:T(8,128)(2,1)} %gate_ref.1) | copy-start | bytes 2359300
  15.2 6.4 %collective-permute-start.5 = (bf16[128,1024]{1,0:T(8,128)(2,1)S(1)}, bf16[128,1024]{1,0:T(8,128)(2,1)S(1)}, u32[]{:S(2)}, u32[]{:S(2)}) collective-permute-start(bf16[128,1024]{1,0:T(8,128)(2,1)S(1)} %shard_map.78.after_ref.near_ref), channel_id=1, source_target_pairs={{0,1},{1,0},{2,3},{3,2},{4,5},{5,4},{6,7},{7,6},{8,9},{9,8},{10,11... | collective-permute-start | bytes 786440 | tf_op jit(solution)/shard_map/ppermute | solution.py:21
  15.9 9.8 %copy-start.2 = (f32[1,64]{1,0:T(1,128)S(1)}, f32[1,64]{1,0:T(1,128)}, u32[]{:S(2)}) copy-start(f32[1,64]{1,0:T(1,128)} %route_ref.1) | copy-start | bytes 772
  16.0 9.8 %collective-permute-start.4 = (bf16[384,512]{1,0:T(8,128)(2,1)S(1)}, bf16[384,512]{1,0:T(8,128)(2,1)S(1)}, u32[]{:S(2)}, u32[]{:S(2)}) collective-permute-start(bf16[384,512]{1,0:T(8,128)(2,1)S(1)} %shard_map.79), channel_id=1, source_target_pairs={{0,2},{1,3},{2,0},{3,1},{4,6},{5,7},{6,4},{7,5},{8,10},{9,11},{10,... | collective-permute-start | bytes 1179656 | tf_op jit(solution)/shard_map/ppermute | solution.py:21
  17.6 4.1 %collective-permute-start.6 = (bf16[128,1024]{1,0:T(8,128)(2,1)S(1)}, bf16[128,1024]{1,0:T(8,128)(2,1)S(1)}, u32[]{:S(2)}, u32[]{:S(2)}) collective-permute-start(bf16[128,1024]{1,0:T(8,128)(2,1)S(1)} %shard_map.78.after_ref.near_ref), channel_id=1, source_target_pairs={{0,8},{8,0},{16,24},{24,16},{1,9},{9,1},{17,25},{25,17},{2,10},{10... | collective-permute-start | bytes 786440 | tf_op jit(solution)/shard_map/ppermute | solution.py:21
  21.7 4.1 %collective-permute-start.7 = (bf16[128,1024]{1,0:T(8,128)(2,1)S(1)}, bf16[128,1024]{1,0:T(8,128)(2,1)S(1)}, u32[]{:S(2)}, u32[]{:S(2)}) collective-permute-start(bf16[128,1024]{1,0:T(8,128)(2,1)S(1)} %collective-permute-done.5.far_ref), channel_id=1, source_target_pairs={{0,8},{8,0},{16,24},{24,16},{1,9},{9,1},{17,25},{25,17},{2,10},{10... | collective-permute-start | bytes 786440 | tf_op jit(solution)/shard_map/ppermute | solution.py:21
  26.8 6.0 %collective-permute-start.10 = (bf16[208,256]{1,0:T(8,128)(2,1)S(1)}, bf16[208,256]{1,0:T(8,128)(2,1)S(1)}, u32[]{:S(2)}, u32[]{:S(2)}) collective-permute-start(bf16[208,256]{1,0:T(8,128)(2,1)S(1)} %shard_map.80.refs_0_), channel_id=1, source_target_pairs={{0,3},{1,2},{2,1},{3,0},{4,7},{5,6},{6,5},{7,4},{8,11},{9,10},{10,... | collective-permute-start | bytes 319496 | tf_op jit(solution)/shard_map/ppermute | solution.py:21
  28.4 5.4 %collective-permute-start.8 = (bf16[208,256]{1,0:T(8,128)(2,1)S(1)}, bf16[208,256]{1,0:T(8,128)(2,1)S(1)}, u32[]{:S(2)}, u32[]{:S(2)}) collective-permute-start(bf16[208,256]{1,0:T(8,128)(2,1)S(1)} %shard_map.80.refs_0_), channel_id=1, source_target_pairs={{0,1},{1,0},{2,3},{3,2},{4,5},{5,4},{6,7},{7,6},{8,9},{9,8},{10,11... | collective-permute-start | bytes 319496 | tf_op jit(solution)/shard_map/ppermute | solution.py:21
  29.9 4.7 %collective-permute-start.9 = (bf16[208,256]{1,0:T(8,128)(2,1)S(1)}, bf16[208,256]{1,0:T(8,128)(2,1)S(1)}, u32[]{:S(2)}, u32[]{:S(2)}) collective-permute-start(bf16[208,256]{1,0:T(8,128)(2,1)S(1)} %shard_map.80.refs_0_), channel_id=1, source_target_pairs={{0,2},{1,3},{2,0},{3,1},{4,6},{5,7},{6,4},{7,5},{8,10},{9,11},{10,... | collective-permute-start | bytes 319496 | tf_op jit(solution)/shard_map/ppermute | solution.py:21
  35.4 4.2 %collective-permute-start.11 = (bf16[192,128]{1,0:T(8,128)(2,1)S(1)}, bf16[192,128]{1,0:T(8,128)(2,1)S(1)}, u32[]{:S(2)}, u32[]{:S(2)}) collective-permute-start(bf16[192,128]{1,0:T(8,128)(2,1)S(1)} %get-tuple-element.20), channel_id=1, source_target_pairs={{0,1},{1,0},{2,3},{3,2},{4,5},{5,4},{6,7},{7,6},{8,9},{9,8},{10,11... | collective-permute-start | bytes 147464 | tf_op jit(solution)/shard_map/ppermute | solution.py:21
  39.6 4.2 %collective-permute-start.12 = (f32[96,128]{1,0:T(8,128)S(1)}, f32[96,128]{1,0:T(8,128)S(1)}, u32[]{:S(2)}, u32[]{:S(2)}) collective-permute-start(f32[96,128]{1,0:T(8,128)S(1)} %get-tuple-element.22), channel_id=1, source_target_pairs={{0,2},{1,3},{2,0},{3,1},{4,6},{5,7},{6,4},{7,5},{8,10},{9,11},{10,... | collective-permute-start | bytes 147464 | tf_op jit(solution)/shard_map/ppermute | solution.py:21
  43.7 7.2 %collective-permute-start.13 = (bf16[128,512]{1,0:T(8,128)(2,1)S(1)}, bf16[128,512]{1,0:T(8,128)(2,1)S(1)}, u32[]{:S(2)}, u32[]{:S(2)}) collective-permute-start(bf16[128,512]{1,0:T(8,128)(2,1)S(1)} %shard_map.84), channel_id=1, source_target_pairs={{0,1},{1,0},{2,3},{3,2},{4,5},{5,4},{6,7},{7,6},{8,9},{9,8},{10,11... | collective-permute-start | bytes 393224 | tf_op jit(solution)/shard_map/ppermute | solution.py:21
  44.4 4.9 %collective-permute-start.14 = (bf16[96,128]{1,0:T(8,128)(2,1)S(1)}, bf16[96,128]{1,0:T(8,128)(2,1)S(1)}, u32[]{:S(2)}, u32[]{:S(2)}) collective-permute-start(bf16[96,128]{1,0:T(8,128)(2,1)S(1)} %shard_map.83.refs_1_.low_ref), channel_id=1, source_target_pairs={{0,4},{1,5},{2,6},{3,7},{4,0},{5,1},{6,2},{7,3},{8,12},{9,13},{10,... | collective-permute-start | bytes 73736 | tf_op jit(solution)/shard_map/ppermute | solution.py:21
  49.3 4.1 %collective-permute-start.16 = (bf16[192,128]{1,0:T(8,128)(2,1)S(1)}, bf16[192,128]{1,0:T(8,128)(2,1)S(1)}, u32[]{:S(2)}, u32[]{:S(2)}) collective-permute-start(bf16[192,128]{1,0:T(8,128)(2,1)S(1)} %shard_map.85.after_ref.low_ref), channel_id=1, source_target_pairs={{0,16},{8,24},{16,0},{24,8},{1,17},{9,25},{17,1},{25,9},{2,18},{10... | collective-permute-start | bytes 147464 | tf_op jit(solution)/shard_map/ppermute | solution.py:21
  50.9 5.0 %collective-permute-start.15 = (bf16[128,512]{1,0:T(8,128)(2,1)S(1)}, bf16[128,512]{1,0:T(8,128)(2,1)S(1)}, u32[]{:S(2)}, u32[]{:S(2)}) collective-permute-start(bf16[128,512]{1,0:T(8,128)(2,1)S(1)} %shard_map.86), channel_id=1, source_target_pairs={{0,2},{1,3},{2,0},{3,1},{4,6},{5,7},{6,4},{7,5},{8,10},{9,11},{10,... | collective-permute-start | bytes 393224 | tf_op jit(solution)/shard_map/ppermute | solution.py:21
  53.4 1.4 %collective-permute-start.17 = (bf16[384,128]{1,0:T(8,128)(2,1)S(1)}, bf16[384,128]{1,0:T(8,128)(2,1)S(1)}, u32[]{:S(2)}, u32[]{:S(2)}) collective-permute-start(bf16[384,128]{1,0:T(8,128)(2,1)S(1)} %shard_map.88.refs_1_), channel_id=1, source_target_pairs={{0,8},{8,0},{16,24},{24,16},{1,9},{9,1},{17,25},{25,17},{2,10},{10... | collective-permute-start | bytes 294920 | tf_op jit(solution)/shard_map/ppermute | solution.py:21
  56.5 3.6 %collective-permute-start.18 = (f32[8,8]{1,0:T(8,128)S(1)}, f32[8,8]{1,0:T(8,128)S(1)}, u32[]{:S(2)}, u32[]{:S(2)}) collective-permute-start(f32[8,8]{1,0:T(8,128)S(1)} %shard_map.89.own_ref), channel_id=1, source_target_pairs={{0,1},{1,0},{2,3},{3,2},{4,5},{5,4},{6,7},{7,6},{8,9},{9,8},{10,11... | collective-permute-start | bytes 776 | tf_op jit(solution)/shard_map/ppermute | solution.py:21
  60.1 3.6 %collective-permute-start.19 = (f32[8,8]{1,0:T(8,128)S(1)}, f32[8,8]{1,0:T(8,128)S(1)}, u32[]{:S(2)}, u32[]{:S(2)}) collective-permute-start(f32[8,8]{1,0:T(8,128)S(1)} %shard_map.90.refs_0_), channel_id=1, source_target_pairs={{0,2},{1,3},{2,0},{3,1},{4,6},{5,7},{6,4},{7,5},{8,10},{9,11},{10,... | collective-permute-start | bytes 776 | tf_op jit(solution)/shard_map/ppermute | solution.py:21

commit v10 on v7

--- a/solution.py
+++ b/solution.py
@@ -105,7 +105,7 @@
     out_ref[depth:] = terms.astype(bf16)
 
 
-def features_kernel(*refs):
+def features_kernel(shares, copies, *refs):
     hidden_refs, (own_ref, x_ref, z_ref) = refs[:HOLDERS], refs[HOLDERS : HOLDERS + 3]
     block_refs, centered_ref = refs[HOLDERS + 3 : 2 * HOLDERS + 3], refs[2 * HOLDERS + 3]
     route_ref, features_ref = refs[2 * HOLDERS + 4 :]
@@ -139,13 +139,19 @@
     row = jnp.transpose(jnp.broadcast_to(column, (tokens, LANES)))[:1]
     gram = dot_f32(features, features, TRANSPOSED)
     centered = (gram - column - row + jnp.sum(mean * mean)).astype(bf16)
-    at = 0
-    for i in range(tokens // TILE):
-        for j in range(tokens // LANES):
-            centered_ref[at * TILE : (at + 1) * TILE] = centered[
-                i * TILE : (i + 1) * TILE, j * LANES : (j + 1) * LANES
-            ]
-            at += 1
+    if copies > 1:
+        count = tokens // (shares // members)
+        for at in range(shares // members * copies):
+            first = at // copies * count
+            centered_ref[at * count : (at + 1) * count] = centered[first : first + count]
+    else:
+        at = 0
+        for i in range(tokens // TILE):
+            for j in range(tokens // LANES):
+                centered_ref[at * TILE : (at + 1) * TILE] = centered[
+                    i * TILE : (i + 1) * TILE, j * LANES : (j + 1) * LANES
+                ]
+                at += 1
     for m, block_ref in enumerate(block_refs):
         for piece in range(part // rows):
             block_ref[piece * rows : (piece + 1) * rows] = features_ref[place(m, piece)]
@@ -247,27 +253,40 @@
         ),
     )
     hiddens = [swapped(hidden, "tok", m) if m else hidden for m in range(HOLDERS)]
-    entries = tokens * tokens // LANES
+    shared = devices * experts * experts <= 1 << 16 and tokens % (devices // 2 * TILE) == 0
+    copies = 2 if shared else 1
+    shares = devices // copies
+    width = tokens if shared else LANES
+    share_rows = tokens * tokens // shares // width
     *blocks, centered = call(
-        features_kernel,
+        lambda *refs: features_kernel(shares, copies, *refs),
         [jax.ShapeDtypeStruct((token_part, part), bf16)] * HOLDERS
-        + [jax.ShapeDtypeStruct((entries, LANES), bf16)],
+        + [jax.ShapeDtypeStruct((devices * share_rows, width), bf16)],
         [VMEM] * (HOLDERS + 3),
         (*hiddens, down_own, down_x, down_z),
         scratch=[pltpu.VMEM((tokens, LANES), f32), pltpu.VMEM((tokens, part), bf16)],
     )
     arrived = lax.all_to_all(centered, ("grp", "tok"), split_axis=0, concat_axis=0, tiled=True)
-    arrived = arrived.reshape(experts, HOLDERS, entries // devices, LANES)
-    direct = devices * experts * experts <= 1 << 16
     tables = call(
         pair_kernel,
-        jax.ShapeDtypeStruct((devices if direct else 1, experts, experts), f32),
+        jax.ShapeDtypeStruct((shares if shared else 1, experts, experts), f32),
         [VMEM],
-        (arrived,),
-        scratch=[pltpu.VMEM((experts, entries // devices, LANES), f32)],
-    )
-    if direct:
-        tables = lax.all_to_all(tables, ("grp", "tok"), split_axis=0, concat_axis=0, tiled=True)
+        (arrived.reshape(experts, HOLDERS, share_rows, width),),
+        scratch=[pltpu.VMEM((experts, share_rows, width), f32)],
+    )
+    if shared:
+        same = [
+            [g * members + t for g in range(c, groups, copies) for t in range(members)]
+            for c in range(copies)
+        ]
+        tables = lax.all_to_all(
+            tables,
+            ("grp", "tok"),
+            split_axis=0,
+            concat_axis=0,
+            tiled=True,
+            axis_index_groups=same,
+        )
     else:
         tables = lax.psum(tables, ("grp", "tok"))
     cka = call(cka_kernel, jax.ShapeDtypeStruct((experts, experts), f32), [VMEM], (tables,))

time: 59.8 us -> 63.4 us (1.060)
  waiting for transfers between devices: 29.4 us -> 32 us
  starting transfers between devices: 23.4 us -> 24.3 us
    all_to_all x1, waiting for transfers between devices: 4.19 us -> 7.01 us  [shards(): lax.all_to_all(centered, ('grp', 'tok'), split_axis=0, concat_axis=0, til...]
    all_to_all x1, starting transfers between devices: 2.56 us -> 3.49 us  [shards(): lax.all_to_all(tables, ('grp', 'tok'), split_axis=0, concat_axis=0, tiled...]
where the time goes in v10:
time: 63.4 us; the launch traced here: 63.2 us
  waiting for transfers between devices  32 us (50%)
  starting transfers between devices  24.3 us (38%)
  Pallas kernels  6.17 us (10%)
  between operations  0.73 us (1%)
    ppermute x14, waiting for transfers between devices, swapped(): lax.ppermute(array, axis, [(i, i ^ mask) for i in range(lax.axis_size(axi...  18.2 us
    ppermute x14, starting transfers between devices, swapped(): lax.ppermute(array, axis, [(i, i ^ mask) for i in range(lax.axis_size(axi...  16.8 us
    all_to_all x1, waiting for transfers between devices, shards(): lax.all_to_all(centered, ('grp', 'tok'), split_axis=0, concat_axis=0, til...  7.01 us
    all_to_all x1, waiting for transfers between devices, shards(): lax.all_to_all(tables, ('grp', 'tok'), split_axis=0, concat_axis=0, tiled...  6.72 us
    pallas_call x8, Pallas kernels, call(): pl.pallas_call(body, out_shape=outs, in_specs=in_specs, out_specs=jax.tre...  6.17 us
    all_to_all x1, starting transfers between devices, shards(): lax.all_to_all(centered, ('grp', 'tok'), split_axis=0, concat_axis=0, til...  3.97 us
    all_to_all x1, starting transfers between devices, shards(): lax.all_to_all(tables, ('grp', 'tok'), split_axis=0, concat_axis=0, tiled...  3.49 us
  transfers between devices with their start and end apart: 16, of which 9 were waited for; matrix products, arithmetic and copies ran while one was open for 0% of the time, Pallas kernels for 3%

profile of v10, /device:TPU:0, one launch (start us, length us, event | category | flops | bytes accessed | tf_op | source)
XLA Modules:
  0.0 63.2 jit_solution(14898047652669714461)
XLA Ops:
  0.6 1.3 %shard_map.77 = (bf16[32,1024]{1,0:T(8,128)(2,1)S(1)}, bf16[192,512]{1,0:T(8,128)(2,1)S(1)}, bf16[192,512]{1,0:T(8,128)(2,1)S(1)}, bf16[384,512]{1,0:T(8,128)(2,1)S(1)}) custom-call(bf16[32,2048]{1,0:T(8,128)(2,1)} %states_hbm.1, f32[1,2048]{1,0:T(1,128)} %bitcast.4, bf16[192,2048]{1,0:T(8,128)(2,1)} %down_hbm.1), custom_call_target="tpu_custom_call" | custom-call | tf_op jit(solution)/shard_map/pallas_call | solution.py:29
  2.0 3.0 %collective-permute-start = (bf16[384,512]{1,0:T(8,128)(2,1)S(1)}, bf16[384,512]{1,0:T(8,128)(2,1)S(1)}, u32[]{:S(2)}, u32[]{:S(2)}) collective-permute-start(bf16[384,512]{1,0:T(8,128)(2,1)S(1)} %get-tuple-element.11), channel_id=1, source_target_pairs={{0,1},{1,0},{2,3},{3,2},{4,5},{5,4},{6,7},{7,6},{8,9},{9,8},{10,11... | collective-permute-start | bytes 1179656 | tf_op jit(solution)/shard_map/ppermute | solution.py:21
  5.0 1.6 %collective-permute-start.1 = (bf16[32,1024]{1,0:T(8,128)(2,1)S(1)}, bf16[32,1024]{1,0:T(8,128)(2,1)S(1)}, u32[]{:S(2)}, u32[]{:S(2)}) collective-permute-start(bf16[32,1024]{1,0:T(8,128)(2,1)S(1)} %get-tuple-element.12.refs_0_), channel_id=1, source_target_pairs={{0,2},{1,3},{2,0},{3,1},{4,6},{5,7},{6,4},{7,5},{8,10},{9,11},{10,... | collective-permute-start | bytes 196616 | tf_op jit(solution)/shard_map/ppermute | solution.py:21
  6.5 2.6 %collective-permute-start.2 = (bf16[32,1024]{1,0:T(8,128)(2,1)S(1)}, bf16[32,1024]{1,0:T(8,128)(2,1)S(1)}, u32[]{:S(2)}, u32[]{:S(2)}) collective-permute-start(bf16[32,1024]{1,0:T(8,128)(2,1)S(1)} %get-tuple-element.12.refs_0_), channel_id=1, source_target_pairs={{0,4},{1,5},{2,6},{3,7},{4,0},{5,1},{6,2},{7,3},{8,12},{9,13},{10,... | collective-permute-start | bytes 196616 | tf_op jit(solution)/shard_map/ppermute | solution.py:21
  9.1 0.2 collective-permute-start.3
  9.4 0.0 collective-permute-done.1.refs_1_
  9.4 4.2 %collective-permute-done.2.refs_2_ = bf16[32,1024]{1,0:T(8,128)(2,1)S(1)} collective-permute-done((bf16[32,1024]{1,0:T(8,128)(2,1)S(1)}, bf16[32,1024]{1,0:T(8,128)(2,1)S(1)}, u32[]{:S(2)}, u32[]{:S(2)}) %collective-permute-start.2) | collective-permute-done | bytes 65568 | tf_op jit(solution)/shard_map/ppermute | solution.py:21
  13.5 1.7 %collective-permute-done.3.refs_3_ = bf16[32,1024]{1,0:T(8,128)(2,1)S(1)} collective-permute-done((bf16[32,1024]{1,0:T(8,128)(2,1)S(1)}, bf16[32,1024]{1,0:T(8,128)(2,1)S(1)}, u32[]{:S(2)}, u32[]{:S(2)}) %collective-permute-start.3) | collective-permute-done | bytes 65568 | tf_op jit(solution)/shard_map/ppermute | solution.py:21
  15.2 0.0 collective-permute-done.after_ref.got_ref.refs_5_
  15.2 0.0 copy-start.1
  15.2 0.0 copy-start
  15.2 0.7 %collective-permute-start.5 = (bf16[128,1024]{1,0:T(8,128)(2,1)S(1)}, bf16[128,1024]{1,0:T(8,128)(2,1)S(1)}, u32[]{:S(2)}, u32[]{:S(2)}) collective-permute-start(bf16[128,1024]{1,0:T(8,128)(2,1)S(1)} %shard_map.78.after_ref.near_ref), channel_id=1, source_target_pairs={{0,1},{1,0},{2,3},{3,2},{4,5},{5,4},{6,7},{7,6},{8,9},{9,8},{10,11... | collective-permute-start | bytes 786440 | tf_op jit(solution)/shard_map/ppermute | solution.py:21
  15.9 0.0 copy-start.2
  16.0 1.6 %collective-permute-start.4 = (bf16[384,512]{1,0:T(8,128)(2,1)S(1)}, bf16[384,512]{1,0:T(8,128)(2,1)S(1)}, u32[]{:S(2)}, u32[]{:S(2)}) collective-permute-start(bf16[384,512]{1,0:T(8,128)(2,1)S(1)} %shard_map.79), channel_id=1, source_target_pairs={{0,2},{1,3},{2,0},{3,1},{4,6},{5,7},{6,4},{7,5},{8,10},{9,11},{10,... | collective-permute-start | bytes 1179656 | tf_op jit(solution)/shard_map/ppermute | solution.py:21
  17.6 0.0 collective-permute-start.6
  17.6 4.1 %collective-permute-done.5.far_ref = bf16[128,1024]{1,0:T(8,128)(2,1)S(1)} collective-permute-done((bf16[128,1024]{1,0:T(8,128)(2,1)S(1)}, bf16[128,1024]{1,0:T(8,128)(2,1)S(1)}, u32[]{:S(2)}, u32[]{:S(2)}) %collective-permute-start.5) | collective-permute-done | bytes 262176 | tf_op jit(solution)/shard_map/ppermute | solution.py:21
  21.7 0.0 collective-permute-start.7
  21.7 0.0 collective-permute-done.6.near2_ref
  21.7 4.0 %collective-permute-done.4.after_ref.refs_6_ = bf16[384,512]{1,0:T(8,128)(2,1)S(1)} collective-permute-done((bf16[384,512]{1,0:T(8,128)(2,1)S(1)}, bf16[384,512]{1,0:T(8,128)(2,1)S(1)}, u32[]{:S(2)}, u32[]{:S(2)}) %collective-permute-start.4) | collective-permute-done | bytes 393248 | tf_op jit(solution)/shard_map/ppermute | solution.py:21
  25.7 0.0 collective-permute-done.7.far2_ref
  25.7 0.0 copy-done.1
  25.7 0.0 copy-done
  25.7 0.0 copy-done.2
  25.7 1.0 %shard_map.80.refs_0_ = bf16[208,256]{1,0:T(8,128)(2,1)S(1)} custom-call(bf16[384,512]{1,0:T(8,128)(2,1)S(1)} %collective-permute-done.4.after_ref.refs_6_, bf16[128,1024]{1,0:T(8,128)(2,1)S(1)} %shard_map.78.after_ref.near_ref, bf16[128,1024]{1,0:T(8,128)(2,1)S(1)} %collective-permute-done.5.far_ref, ...), custom_call_target="tpu_custom_call" | custom-call | tf_op jit(solution)/shard_map/pallas_call | solution.py:29
  26.8 1.6 %collective-permute-start.10 = (bf16[208,256]{1,0:T(8,128)(2,1)S(1)}, bf16[208,256]{1,0:T(8,128)(2,1)S(1)}, u32[]{:S(2)}, u32[]{:S(2)}) collective-permute-start(bf16[208,256]{1,0:T(8,128)(2,1)S(1)} %shard_map.80.refs_0_), channel_id=1, source_target_pairs={{0,3},{1,2},{2,1},{3,0},{4,7},{5,6},{6,5},{7,4},{8,11},{9,10},{10,... | collective-permute-start | bytes 319496 | tf_op jit(solution)/shard_map/ppermute | solution.py:21
  28.4 1.5 %collective-permute-start.8 = (bf16[208,256]{1,0:T(8,128)(2,1)S(1)}, bf16[208,256]{1,0:T(8,128)(2,1)S(1)}, u32[]{:S(2)}, u32[]{:S(2)}) collective-permute-start(bf16[208,256]{1,0:T(8,128)(2,1)S(1)} %shard_map.80.refs_0_), channel_id=1, source_target_pairs={{0,1},{1,0},{2,3},{3,2},{4,5},{5,4},{6,7},{7,6},{8,9},{9,8},{10,11... | collective-permute-start | bytes 319496 | tf_op jit(solution)/shard_map/ppermute | solution.py:21
  29.9 0.4 collective-permute-start.9
  30.3 2.4 %collective-permute-done.10.refs_3_ = bf16[208,256]{1,0:T(8,128)(2,1)S(1)} collective-permute-done((bf16[208,256]{1,0:T(8,128)(2,1)S(1)}, bf16[208,256]{1,0:T(8,128)(2,1)S(1)}, u32[]{:S(2)}, u32[]{:S(2)}) %collective-permute-start.10) | collective-permute-done | bytes 106528 | tf_op jit(solution)/shard_map/ppermute | solution.py:21
  32.7 1.1 %collective-permute-done.8.refs_1_ = bf16[208,256]{1,0:T(8,128)(2,1)S(1)} collective-permute-done((bf16[208,256]{1,0:T(8,128)(2,1)S(1)}, bf16[208,256]{1,0:T(8,128)(2,1)S(1)}, u32[]{:S(2)}, u32[]{:S(2)}) %collective-permute-start.8) | collective-permute-done | bytes 106528 | tf_op jit(solution)/shard_map/ppermute | solution.py:21
  33.8 0.8 %collective-permute-done.9.refs_2_ = bf16[208,256]{1,0:T(8,128)(2,1)S(1)} collective-permute-done((bf16[208,256]{1,0:T(8,128)(2,1)S(1)}, bf16[208,256]{1,0:T(8,128)(2,1)S(1)}, u32[]{:S(2)}, u32[]{:S(2)}) %collective-permute-start.9) | collective-permute-done | bytes 106528 | tf_op jit(solution)/shard_map/ppermute | solution.py:21
  34.6 1.5 %shard_map.81 = (bf16[64,512]{1,0:T(8,128)(2,1)S(1)}, bf16[64,512]{1,0:T(8,128)(2,1)S(1)}, bf16[64,512]{1,0:T(8,128)(2,1)S(1)}, bf16[64,512]{1,0:T(8,128)(2,1)S(1)}, bf16[512,256]{1,0:T(8,128)(2,1)}) custom-call(bf16[208,256]{1,0:T(8,128)(2,1)S(1)} %shard_map.80.refs_0_, bf16[208,256]{1,0:T(8,128)(2,1)S(1)} %collective-permute-done.8.refs_1_, ...), custom_call_target="tpu_custom_call" | custom-call | tf_op jit(solution)/shard_map/pallas_call | solution.py:29
  36.1 4.0 %all-to-all-start = ((bf16[32,16,256]{2,1,0:T(8,128)(2,1)}), bf16[32,16,256]{2,1,0:T(8,128)(2,1)S(1)}, u32[]{:S(2)}, u32[]{:S(2)}) async-start(bf16[32,16,256]{2,1,0:T(8,128)(2,1)} %bitcast.1), calls=%async_computation | async-start | bytes 524288 | tf_op jit(solution)/shard_map/all_to_all | solution.py:269
  40.0 1.8 %collective-permute-start.11 = (bf16[64,512]{1,0:T(8,128)(2,1)S(1)}, bf16[64,512]{1,0:T(8,128)(2,1)S(1)}, u32[]{:S(2)}, u32[]{:S(2)}) collective-permute-start(bf16[64,512]{1,0:T(8,128)(2,1)S(1)} %get-tuple-element.16), channel_id=1, source_target_pairs={{0,1},{1,0},{2,3},{3,2},{4,5},{5,4},{6,7},{7,6},{8,9},{9,8},{10,11... | collective-permute-start | bytes 196616 | tf_op jit(solution)/shard_map/ppermute | solution.py:21
  41.9 1.5 %collective-permute-start.12 = (bf16[64,512]{1,0:T(8,128)(2,1)S(1)}, bf16[64,512]{1,0:T(8,128)(2,1)S(1)}, u32[]{:S(2)}, u32[]{:S(2)}) collective-permute-start(bf16[64,512]{1,0:T(8,128)(2,1)S(1)} %get-tuple-element.17), channel_id=1, source_target_pairs={{0,2},{1,3},{2,0},{3,1},{4,6},{5,7},{6,4},{7,5},{8,10},{9,11},{10,... | collective-permute-start | bytes 196616 | tf_op jit(solution)/shard_map/ppermute | solution.py:21
  43.3 0.3 collective-permute-start.13
  43.6 7.0 %all-to-all-done = bf16[32,16,256]{2,1,0:T(8,128)(2,1)S(1)} async-done(((bf16[32,16,256]{2,1,0:T(8,128)(2,1)}), bf16[32,16,256]{2,1,0:T(8,128)(2,1)S(1)}, u32[]{:S(2)}, u32[]{:S(2)}) %all-to-all-start) | async-done | bytes 262176 | tf_op jit(solution)/shard_map/all_to_all | solution.py:269
  50.6 0.9 %shard_map.83 = f32[16,8,8]{2,1,0:T(8,128)} custom-call(bf16[8,4,16,256]{3,2,1,0:T(8,128)(2,1)S(1)} %bitcast.3), custom_call_target="tpu_custom_call" | custom-call | tf_op jit(solution)/shard_map/pallas_call | solution.py:29
  51.5 3.5 %all-to-all-start.1 = ((f32[16,8,8]{2,1,0:T(8,128)}), f32[16,8,8]{2,1,0:T(8,128)S(1)}, u32[]{:S(2)}, u32[]{:S(2)}) async-start(f32[16,8,8]{2,1,0:T(8,128)} %shard_map.83), calls=%async_computation.1 | async-start | bytes 131072 | tf_op jit(solution)/shard_map/all_to_all | solution.py:282
  55.0 0.0 collective-permute-done.11.refs_1_
  55.0 0.0 collective-permute-done.12.refs_2_
  55.0 0.0 collective-permute-done.13.refs_3_
  55.0 0.7 %shard_map.82 = bf16[64,2048]{1,0:T(8,128)(2,1)} custom-call(bf16[64,512]{1,0:T(8,128)(2,1)S(1)} %get-tuple-element.15.refs_0_, bf16[64,512]{1,0:T(8,128)(2,1)S(1)} %collective-permute-done.11.refs_1_, bf16[64,512]{1,0:T(8,128)(2,1)S(1)} %collective-permute-done.12.refs_2_, bf16[64,512]{1,0:T(8,128)(2,1)S(1)} %collective-permute-done.13.refs_3_), custom_call_target="tpu_custom_call" | custom-call | tf_op jit(solution)/shard_map/pallas_call | solution.py:29
  55.7 6.7 %all-to-all-done.1.tables_ref = f32[16,8,8]{2,1,0:T(8,128)S(1)} async-done(((f32[16,8,8]{2,1,0:T(8,128)}), f32[16,8,8]{2,1,0:T(8,128)S(1)}, u32[]{:S(2)}, u32[]{:S(2)}) %all-to-all-start.1) | async-done | bytes 4128 | tf_op jit(solution)/shard_map/all_to_all | solution.py:282
  62.5 0.7 %shard_map.84 = f32[8,8]{1,0:T(8,128)} custom-call(f32[16,8,8]{2,1,0:T(8,128)S(1)} %all-to-all-done.1.tables_ref), custom_call_target="tpu_custom_call" | custom-call | tf_op jit(solution)/shard_map/pallas_call | solution.py:29
  (2 shorter events, 0.1 us)
Async XLA Ops:
  2.0 13.2 %collective-permute-start = (bf16[384,512]{1,0:T(8,128)(2,1)S(1)}, bf16[384,512]{1,0:T(8,128)(2,1)S(1)}, u32[]{:S(2)}, u32[]{:S(2)}) collective-permute-start(bf16[384,512]{1,0:T(8,128)(2,1)S(1)} %get-tuple-element.11), channel_id=1, source_target_pairs={{0,1},{1,0},{2,3},{3,2},{4,5},{5,4},{6,7},{7,6},{8,9},{9,8},{10,11... | collective-permute-start | bytes 1179656 | tf_op jit(solution)/shard_map/ppermute | solution.py:21
  5.0 4.4 %collective-permute-start.1 = (bf16[32,1024]{1,0:T(8,128)(2,1)S(1)}, bf16[32,1024]{1,0:T(8,128)(2,1)S(1)}, u32[]{:S(2)}, u32[]{:S(2)}) collective-permute-start(bf16[32,1024]{1,0:T(8,128)(2,1)S(1)} %get-tuple-element.12.refs_0_), channel_id=1, source_target_pairs={{0,2},{1,3},{2,0},{3,1},{4,6},{5,7},{6,4},{7,5},{8,10},{9,11},{10,... | collective-permute-start | bytes 196616 | tf_op jit(solution)/shard_map/ppermute | solution.py:21
  6.5 7.0 %collective-permute-start.2 = (bf16[32,1024]{1,0:T(8,128)(2,1)S(1)}, bf16[32,1024]{1,0:T(8,128)(2,1)S(1)}, u32[]{:S(2)}, u32[]{:S(2)}) collective-permute-start(bf16[32,1024]{1,0:T(8,128)(2,1)S(1)} %get-tuple-element.12.refs_0_), channel_id=1, source_target_pairs={{0,4},{1,5},{2,6},{3,7},{4,0},{5,1},{6,2},{7,3},{8,12},{9,13},{10,... | collective-permute-start | bytes 196616 | tf_op jit(solution)/shard_map/ppermute | solution.py:21
  9.1 6.1 %collective-permute-start.3 = (bf16[32,1024]{1,0:T(8,128)(2,1)S(1)}, bf16[32,1024]{1,0:T(8,128)(2,1)S(1)}, u32[]{:S(2)}, u32[]{:S(2)}) collective-permute-start(bf16[32,1024]{1,0:T(8,128)(2,1)S(1)} %get-tuple-element.12.refs_0_), channel_id=1, source_target_pairs={{0,6},{1,7},{2,4},{3,5},{4,2},{5,3},{6,0},{7,1},{8,14},{9,15},{10,... | collective-permute-start | bytes 196616 | tf_op jit(solution)/shard_map/ppermute | solution.py:21
  15.2 10.5 %copy-start.1 = (bf16[192,2048]{1,0:T(8,128)(2,1)S(1)}, bf16[192,2048]{1,0:T(8,128)(2,1)}, u32[]{:S(2)}) copy-start(bf16[192,2048]{1,0:T(8,128)(2,1)} %up_ref.1) | copy-start | bytes 2359300
  15.2 10.5 %copy-start = (bf16[192,2048]{1,0:T(8,128)(2,1)S(1)}, bf16[192,2048]{1,0:T(8,128)(2,1)}, u32[]{:S(2)}) copy-start(bf16[192,2048]{1,0:T(8,128)(2,1)} %gate_ref.1) | copy-start | bytes 2359300
  15.2 6.4 %collective-permute-start.5 = (bf16[128,1024]{1,0:T(8,128)(2,1)S(1)}, bf16[128,1024]{1,0:T(8,128)(2,1)S(1)}, u32[]{:S(2)}, u32[]{:S(2)}) collective-permute-start(bf16[128,1024]{1,0:T(8,128)(2,1)S(1)} %shard_map.78.after_ref.near_ref), channel_id=1, source_target_pairs={{0,1},{1,0},{2,3},{3,2},{4,5},{5,4},{6,7},{7,6},{8,9},{9,8},{10,11... | collective-permute-start | bytes 786440 | tf_op jit(solution)/shard_map/ppermute | solution.py:21
  15.9 9.8 %copy-start.2 = (f32[1,64]{1,0:T(1,128)S(1)}, f32[1,64]{1,0:T(1,128)}, u32[]{:S(2)}) copy-start(f32[1,64]{1,0:T(1,128)} %route_ref.1) | copy-start | bytes 772
  16.0 9.8 %collective-permute-start.4 = (bf16[384,512]{1,0:T(8,128)(2,1)S(1)}, bf16[384,512]{1,0:T(8,128)(2,1)S(1)}, u32[]{:S(2)}, u32[]{:S(2)}) collective-permute-start(bf16[384,512]{1,0:T(8,128)(2,1)S(1)} %shard_map.79), channel_id=1, source_target_pairs={{0,2},{1,3},{2,0},{3,1},{4,6},{5,7},{6,4},{7,5},{8,10},{9,11},{10,... | collective-permute-start | bytes 1179656 | tf_op jit(solution)/shard_map/ppermute | solution.py:21
  17.6 4.1 %collective-permute-start.6 = (bf16[128,1024]{1,0:T(8,128)(2,1)S(1)}, bf16[128,1024]{1,0:T(8,128)(2,1)S(1)}, u32[]{:S(2)}, u32[]{:S(2)}) collective-permute-start(bf16[128,1024]{1,0:T(8,128)(2,1)S(1)} %shard_map.78.after_ref.near_ref), channel_id=1, source_target_pairs={{0,8},{8,0},{16,24},{24,16},{1,9},{9,1},{17,25},{25,17},{2,10},{10... | collective-permute-start | bytes 786440 | tf_op jit(solution)/shard_map/ppermute | solution.py:21
  21.7 4.1 %collective-permute-start.7 = (bf16[128,1024]{1,0:T(8,128)(2,1)S(1)}, bf16[128,1024]{1,0:T(8,128)(2,1)S(1)}, u32[]{:S(2)}, u32[]{:S(2)}) collective-permute-start(bf16[128,1024]{1,0:T(8,128)(2,1)S(1)} %collective-permute-done.5.far_ref), channel_id=1, source_target_pairs={{0,8},{8,0},{16,24},{24,16},{1,9},{9,1},{17,25},{25,17},{2,10},{10... | collective-permute-start | bytes 786440 | tf_op jit(solution)/shard_map/ppermute | solution.py:21
  26.8 6.0 %collective-permute-start.10 = (bf16[208,256]{1,0:T(8,128)(2,1)S(1)}, bf16[208,256]{1,0:T(8,128)(2,1)S(1)}, u32[]{:S(2)}, u32[]{:S(2)}) collective-permute-start(bf16[208,256]{1,0:T(8,128)(2,1)S(1)} %shard_map.80.refs_0_), channel_id=1, source_target_pairs={{0,3},{1,2},{2,1},{3,0},{4,7},{5,6},{6,5},{7,4},{8,11},{9,10},{10,... | collective-permute-start | bytes 319496 | tf_op jit(solution)/shard_map/ppermute | solution.py:21
  28.4 5.4 %collective-permute-start.8 = (bf16[208,256]{1,0:T(8,128)(2,1)S(1)}, bf16[208,256]{1,0:T(8,128)(2,1)S(1)}, u32[]{:S(2)}, u32[]{:S(2)}) collective-permute-start(bf16[208,256]{1,0:T(8,128)(2,1)S(1)} %shard_map.80.refs_0_), channel_id=1, source_target_pairs={{0,1},{1,0},{2,3},{3,2},{4,5},{5,4},{6,7},{7,6},{8,9},{9,8},{10,11... | collective-permute-start | bytes 319496 | tf_op jit(solution)/shard_map/ppermute | solution.py:21
  29.9 4.7 %collective-permute-start.9 = (bf16[208,256]{1,0:T(8,128)(2,1)S(1)}, bf16[208,256]{1,0:T(8,128)(2,1)S(1)}, u32[]{:S(2)}, u32[]{:S(2)}) collective-permute-start(bf16[208,256]{1,0:T(8,128)(2,1)S(1)} %shard_map.80.refs_0_), channel_id=1, source_target_pairs={{0,2},{1,3},{2,0},{3,1},{4,6},{5,7},{6,4},{7,5},{8,10},{9,11},{10,... | collective-permute-start | bytes 319496 | tf_op jit(solution)/shard_map/ppermute | solution.py:21
  36.1 14.5 %all-to-all-start = ((bf16[32,16,256]{2,1,0:T(8,128)(2,1)}), bf16[32,16,256]{2,1,0:T(8,128)(2,1)S(1)}, u32[]{:S(2)}, u32[]{:S(2)}) async-start(bf16[32,16,256]{2,1,0:T(8,128)(2,1)} %bitcast.1), calls=%async_computation | async-start | bytes 524288 | tf_op jit(solution)/shard_map/all_to_all | solution.py:269
  40.0 14.9 %collective-permute-start.11 = (bf16[64,512]{1,0:T(8,128)(2,1)S(1)}, bf16[64,512]{1,0:T(8,128)(2,1)S(1)}, u32[]{:S(2)}, u32[]{:S(2)}) collective-permute-start(bf16[64,512]{1,0:T(8,128)(2,1)S(1)} %get-tuple-element.16), channel_id=1, source_target_pairs={{0,1},{1,0},{2,3},{3,2},{4,5},{5,4},{6,7},{7,6},{8,9},{9,8},{10,11... | collective-permute-start | bytes 196616 | tf_op jit(solution)/shard_map/ppermute | solution.py:21
  41.9 13.1 %collective-permute-start.12 = (bf16[64,512]{1,0:T(8,128)(2,1)S(1)}, bf16[64,512]{1,0:T(8,128)(2,1)S(1)}, u32[]{:S(2)}, u32[]{:S(2)}) collective-permute-start(bf16[64,512]{1,0:T(8,128)(2,1)S(1)} %get-tuple-element.17), channel_id=1, source_target_pairs={{0,2},{1,3},{2,0},{3,1},{4,6},{5,7},{6,4},{7,5},{8,10},{9,11},{10,... | collective-permute-start | bytes 196616 | tf_op jit(solution)/shard_map/ppermute | solution.py:21
  43.3 11.6 %collective-permute-start.13 = (bf16[64,512]{1,0:T(8,128)(2,1)S(1)}, bf16[64,512]{1,0:T(8,128)(2,1)S(1)}, u32[]{:S(2)}, u32[]{:S(2)}) collective-permute-start(bf16[64,512]{1,0:T(8,128)(2,1)S(1)} %get-tuple-element.18), channel_id=1, source_target_pairs={{0,3},{1,2},{2,1},{3,0},{4,7},{5,6},{6,5},{7,4},{8,11},{9,10},{10,... | collective-permute-start | bytes 196616 | tf_op jit(solution)/shard_map/ppermute | solution.py:21
  51.5 11.0 %all-to-all-start.1 = ((f32[16,8,8]{2,1,0:T(8,128)}), f32[16,8,8]{2,1,0:T(8,128)S(1)}, u32[]{:S(2)}, u32[]{:S(2)}) async-start(f32[16,8,8]{2,1,0:T(8,128)} %shard_map.83), calls=%async_computation.1 | async-start | bytes 131072 | tf_op jit(solution)/shard_map/all_to_all | solution.py:282

commit v11 on v4

--- a/solution.py
+++ b/solution.py
@@ -45,9 +45,8 @@
     return lax.axis_index("tok") & (HOLDERS - 1)
 
 
-def first_kernel(states_hbm, gain_hbm, down_hbm, *refs):
-    out_ref, downs = refs[0], refs[1 : 1 + HOLDERS]
-    states_ref, gain_ref, sems = refs[1 + HOLDERS :]
+def first_kernel(states_hbm, gain_hbm, down_hbm, out_ref, *refs):
+    downs, (states_ref, gain_ref, sems) = refs[:HOLDERS], refs[HOLDERS:]
     copies = [
         pltpu.make_async_copy(states_hbm, states_ref, sems.at[0]),
         pltpu.make_async_copy(gain_hbm, gain_ref, sems.at[1]),
@@ -84,25 +83,31 @@
     )
 
 
-def stack_kernel(*refs):
-    pieces, out_ref = refs[2:-1], refs[-1]
-    rows = pieces[0].shape[0]
-    for m, piece in enumerate(pieces):
-        place = lax.axis_index("tok") ^ m
-        out_ref[pl.ds(pl.multiple_of(place * rows, rows), rows)] = piece[...]
-
-
-def hidden_kernel(mine_ref, other_ref, gate_ref, up_ref, route_ref, out_ref):
-    tokens, width = mine_ref.shape
+def stack_kernel(after_ref, after2_ref, *refs):
+    rows = refs[0].shape[0]
+    z = lax.axis_index("tok") >> 1
+    for m, piece in enumerate(refs[:-1]):
+        refs[-1][pl.ds(pl.multiple_of((z ^ m) * rows, rows), rows)] = piece[...]
+
+
+def columns_of(half, width):
+    return pl.ds(pl.multiple_of(half * width, width), width)
+
+
+def gated(gate, upward):
+    return (gate / (1.0 + jnp.exp(-gate)) * upward).astype(bf16)
+
+
+def near_kernel(near_ref, near2_ref, far_ref, gate_ref, up_ref, route_ref, out_ref, gate_part_ref, up_part_ref):
+    count, width = near_ref.shape
+    depth = gate_ref.shape[0]
+    own, rest = columns_of(core(), width), columns_of(1 - core(), width)
+    near, near2, far = near_ref[...], near2_ref[...], far_ref[...]
     gate, upward = [
-        sum(
-            dot_f32(ref[:, pl.ds(pl.multiple_of(half * width, width), width)], block[...], TRANSPOSED)
-            for half, block in ((core(), mine_ref), (1 - core(), other_ref))
-        )
+        dot_f32(ref[:, own], near, TRANSPOSED) + dot_f32(ref[:, rest], near2, TRANSPOSED)
         for ref in (gate_ref, up_ref)
     ]
-    depth = gate.shape[0]
-    out_ref[:depth] = (gate / (1.0 + jnp.exp(-gate)) * upward).astype(bf16)
+    out_ref[:depth] = gated(gate, upward)
     route = route_ref[...]
     high = route.astype(bf16).astype(f32)
     middle = (route - high).astype(bf16).astype(f32)
@@ -110,45 +115,73 @@
     part = route.shape[1]
     row = lax.broadcasted_iota(jnp.int32, (TILE, part), 0)
     terms = jnp.where(row == 0, high, jnp.where(row == 1, middle, jnp.where(row == 2, low, 0.0)))
-    terms = jnp.concatenate([terms, jnp.zeros((TILE, tokens - part), f32)], 1)
+    terms = jnp.concatenate([terms, jnp.zeros((TILE, count - part), f32)], 1)
     out_ref[depth:] = terms.astype(bf16)
+    gate_part_ref[...] = dot_f32(gate_ref[:, own], far, TRANSPOSED)
+    up_part_ref[...] = dot_f32(up_ref[:, own], far, TRANSPOSED)
+
+
+def far_kernel(far2_ref, gate_ref, up_ref, gate_part_ref, up_part_ref, out_ref):
+    rest = columns_of(1 - core(), far2_ref.shape[1])
+    far2 = far2_ref[...]
+    gate, upward = [
+        part_ref[...] + dot_f32(ref[:, rest], far2, TRANSPOSED)
+        for ref, part_ref in ((gate_ref, gate_part_ref), (up_ref, up_part_ref))
+    ]
+    out_ref[...] = gated(gate, upward)
 
 
 def features_kernel(*refs):
-    hidden_refs, down_refs = refs[:HOLDERS], refs[HOLDERS : 2 * HOLDERS]
-    block_refs, centered_ref = refs[2 * HOLDERS : 3 * HOLDERS], refs[3 * HOLDERS]
-    route_ref, features_ref = refs[3 * HOLDERS + 1 :]
-    depth, tokens = down_refs[0].shape[0], hidden_refs[0].shape[1]
-    part = tokens // HOLDERS
+    near_refs, far_refs, down_refs = [refs[n * HOLDERS : (n + 1) * HOLDERS] for n in range(3)]
+    block_refs, centered_ref = refs[3 * HOLDERS : 4 * HOLDERS], refs[4 * HOLDERS]
+    route_ref, features_ref, whole_ref = refs[4 * HOLDERS + 1 :]
+    depth, half = far_refs[0].shape
+    tokens = 2 * half
+    part, members = tokens // HOLDERS, lax.axis_size("tok")
+    rows = tokens // members
+    x = lax.axis_index("tok") & 1
+
+    def place(m, piece):
+        z = (holder() ^ m) * (members // HOLDERS // 2) + piece // 2
+        return pl.ds(pl.multiple_of(piece % 2 * (tokens // 2) + z * rows, rows), rows)
+
     eye = lax.broadcasted_iota(jnp.int32, (part, part), 0) == lax.broadcasted_iota(
         jnp.int32, (part, part), 1
     )
-    output = None
-    for m, (hidden_ref, down_ref) in enumerate(zip(hidden_refs, down_refs)):
-        product = dot_f32(hidden_ref[:depth], down_ref[...], (((0,), (0,)), ((), ())))
-        output = product if output is None else output + product
-        terms = hidden_ref[depth:, :part].astype(f32)
+    here = there = None
+    for m in range(HOLDERS):
+        near, far, down = near_refs[m][:depth], far_refs[m][...], down_refs[m][...]
+        for_here, for_there = (far, near) if m & 1 else (near, far)
+        for_here = dot_f32(for_here, down, (((0,), (0,)), ((), ())))
+        for_there = dot_f32(for_there, down, (((0,), (0,)), ((), ())))
+        here = for_here if m == 0 else here + for_here
+        there = for_there if m == 0 else there + for_there
+        terms = near_refs[m][depth:, :part].astype(f32)
         route = jnp.sum(terms[:HOLDERS], axis=0, keepdims=True)
         column = jnp.sum(jnp.where(eye, route, 0.0), axis=1, keepdims=True)
-        place = pl.multiple_of((holder() ^ m) * part, part)
-        route_ref[pl.ds(place, part)] = jnp.broadcast_to(column, (part, LANES))
-    features = (output * route_ref[:, :1]).astype(bf16)
-    features_ref[...] = features
+        column = jnp.broadcast_to(column, (part, LANES))
+        for piece in range(part // rows):
+            route_ref[place(m, piece)] = column[piece * rows : (piece + 1) * rows]
+    for at, output in ((x, here), (1 - x, there)):
+        at = pl.ds(pl.multiple_of(at * half, half), half)
+        features_ref[at] = (output * route_ref[at][:, :1]).astype(bf16)
+    features = features_ref[...]
     wide = features.astype(f32)
     mean = jnp.sum(wide, axis=0, keepdims=True) / tokens
     column = jnp.sum(wide * mean, axis=1, keepdims=True)
     row = jnp.transpose(jnp.broadcast_to(column, (tokens, LANES)))[:1]
     gram = dot_f32(features, features, TRANSPOSED)
-    centered = (gram - column - row + jnp.sum(mean * mean)).astype(bf16)
+    whole_ref[...] = (gram - column - row + jnp.sum(mean * mean)).astype(bf16)
     at = 0
     for i in range(tokens // TILE):
         for j in range(tokens // LANES):
-            centered_ref[at * TILE : (at + 1) * TILE] = centered[
+            centered_ref[at * TILE : (at + 1) * TILE] = whole_ref[
                 i * TILE : (i + 1) * TILE, j * LANES : (j + 1) * LANES
             ]
             at += 1
     for m, block_ref in enumerate(block_refs):
-        block_ref[...] = features_ref[pl.ds(pl.multiple_of((holder() ^ m) * part, part), part)]
+        for piece in range(part // rows):
+            block_ref[piece * rows : (piece + 1) * rows] = features_ref[place(m, piece)]
 
 
 def place_kernel(*refs):
@@ -215,36 +248,46 @@
             pltpu.SemaphoreType.DMA((2 + HOLDERS,)),
         ],
     )
-    pieces = {0: own}
-    for m in range(members - 2, 0, -2):
-        pieces[m] = swapped(own, "tok", m)
-    for m in range(0, members, 2):
-        pieces[m + 1] = swapped(pieces[m], "tok", 1)
-    down_x, down_z = swapped(downs[1], "tok", 1), swapped(downs[2], "tok", 2)
-    mine = call(
+    down_x = swapped(downs[1], "tok", 1)
+    pieces = [swapped(own, "tok", 2 * m) if m else own for m in range(members // 2)]
+    down_z = swapped(downs[2], "tok", 2)
+    near = call(
         stack_kernel,
-        jax.ShapeDtypeStruct((tokens, model // 2), bf16),
-        [ANY] * 2 + [VMEM] * members,
-        (down_x, down_z, *[pieces[m] for m in range(members)]),
-    )
-    other = swapped(mine, "grp", 1)
-
-    downs = [downs[0], down_x, down_z, swapped(held(downs[3], mine), "tok", 3)]
-    hidden = call(
-        hidden_kernel,
-        jax.ShapeDtypeStruct((depth + TILE, tokens), bf16),
+        jax.ShapeDtypeStruct((tokens // 2, model // 2), bf16),
+        [ANY] * 2 + [VMEM] * len(pieces),
+        (down_x, down_z, *pieces),
+    )
+    far = swapped(near, "tok", 1)
+    near2 = swapped(near, "grp", 1)
+    down_xz = swapped(held(downs[3], near), "tok", 2)
+    half_shape = jax.ShapeDtypeStruct((depth, tokens // 2), f32)
+    near_hidden, gate_part, up_part = call(
+        near_kernel,
+        [jax.ShapeDtypeStruct((depth + TILE, tokens // 2), bf16), half_shape, half_shape],
+        [VMEM] * 6,
+        (near, near2, far, gate_weight, up_weight, route_weight),
+    )
+    near_hiddens = [swapped(near_hidden, "tok", m) if m else near_hidden for m in range(HOLDERS)]
+    down_xz = swapped(held(down_xz, far), "tok", 1)
+    far_hidden = call(
+        far_kernel,
+        jax.ShapeDtypeStruct((depth, tokens // 2), bf16),
         [VMEM] * 5,
-        (mine, other, gate_weight, up_weight, route_weight),
-    )
-    hiddens = [swapped(hidden, "tok", m) if m else hidden for m in range(HOLDERS)]
+        (swapped(far, "grp", 1), gate_weight, up_weight, gate_part, up_part),
+    )
+    far_hiddens = [swapped(far_hidden, "tok", m) if m else far_hidden for m in range(HOLDERS)]
     entries = tokens * tokens // LANES
     *blocks, centered = call(
         features_kernel,
         [jax.ShapeDtypeStruct((token_part, part), bf16)] * HOLDERS
         + [jax.ShapeDtypeStruct((entries, LANES), bf16)],
-        [VMEM] * (2 * HOLDERS),
-        (*hiddens, *downs),
-        scratch=[pltpu.VMEM((tokens, LANES), f32), pltpu.VMEM((tokens, part), bf16)],
+        [VMEM] * (3 * HOLDERS),
+        (*near_hiddens, *far_hiddens, downs[0], down_x, down_z, down_xz),
+        scratch=[
+            pltpu.VMEM((tokens, LANES), f32),
+            pltpu.VMEM((tokens, part), bf16),
+            pltpu.VMEM((tokens, tokens), bf16),
+        ],
     )
     arrived = lax.all_to_all(centered, ("grp", "tok"), split_axis=0, concat_axis=0, tiled=True)
     arrived = arrived.reshape(experts, HOLDERS, entries // devices, LANES)

time: 60.9 us -> 64 us (1.051)
  waiting for transfers between devices: 25.8 us -> 29.9 us
  starting transfers between devices: 28.1 us -> 26.9 us
    ppermute x17 -> x19, waiting for transfers between devices: 14.6 us -> 18.7 us  [swapped(): lax.ppermute(array, axis, [(i, i ^ mask) for i in range(lax.axis_size(axi...]
    ppermute x17 -> x19, starting transfers between devices: 21.5 us -> 20.9 us  [swapped(): lax.ppermute(array, axis, [(i, i ^ mask) for i in range(lax.axis_size(axi...]
    pallas_call x8 -> x10, Pallas kernels: 5.94 us -> 6.25 us  [call(): pl.pallas_call(body, out_shape=outs, in_specs=in_specs, out_specs=jax.tre...]
  transfers between devices with their start and end apart: 19 -> 21, of which waited for: 12 -> 8; matrix products, arithmetic and copies ran while one was open for 0% -> 0% of each run, Pallas kernels for 4% -> 4%
where the time goes in v11:
time: 64 us; the launch traced here: 63.8 us
  waiting for transfers between devices  29.9 us (47%)
  starting transfers between devices  26.9 us (42%)
  Pallas kernels  6.25 us (10%)
  between operations  0.76 us (1%)
    ppermute x19, starting transfers between devices, swapped(): lax.ppermute(array, axis, [(i, i ^ mask) for i in range(lax.axis_size(axi...  20.9 us
    ppermute x19, waiting for transfers between devices, swapped(): lax.ppermute(array, axis, [(i, i ^ mask) for i in range(lax.axis_size(axi...  18.7 us
    all_to_all x1, waiting for transfers between devices, shards(): lax.all_to_all(tables, ('grp', 'tok'), split_axis=0, concat_axis=0, tiled...  6.96 us
    pallas_call x10, Pallas kernels, call(): pl.pallas_call(body, out_shape=outs, in_specs=in_specs, out_specs=jax.tre...  6.25 us
    all_to_all x1, waiting for transfers between devices, shards(): lax.all_to_all(centered, ('grp', 'tok'), split_axis=0, concat_axis=0, til...  4.19 us
    all_to_all x1, starting transfers between devices, shards(): lax.all_to_all(centered, ('grp', 'tok'), split_axis=0, concat_axis=0, til...  3.4 us
    all_to_all x1, starting transfers between devices, shards(): lax.all_to_all(tables, ('grp', 'tok'), split_axis=0, concat_axis=0, tiled...  2.57 us
  transfers between devices with their start and end apart: 21, of which 8 were waited for; matrix products, arithmetic and copies ran while one was open for 0% of the time, Pallas kernels for 4%

profile of v11, /device:TPU:0, one launch (start us, length us, event | category | flops | bytes accessed | tf_op | source)
XLA Modules:
  0.0 63.8 jit_solution(18288354442330680748)
XLA Ops:
  0.6 1.3 %shard_map.77 = (bf16[32,1024]{1,0:T(8,128)(2,1)S(1)}, bf16[192,512]{1,0:T(8,128)(2,1)S(1)}, bf16[192,512]{1,0:T(8,128)(2,1)S(1)}, bf16[192,512]{1,0:T(8,128)(2,1)S(1)}, bf16[192,512]{1,0:T(8,128)(2,1)S(1)}) custom-call(bf16[32,2048]{1,0:T(8,128)(2,1)} %states_hbm.1, f32[1,2048]{1,0:T(1,128)} %bitcast.4, bf16[192,2048]{1,0:T(8,128)(2,1)} %down_hbm.1), custom_call_target="tpu_custom_call" | custom-call | tf_op jit(solution)/shard_map/pallas_call | solution.py:29
  2.0 3.0 %collective-permute-start = (bf16[192,512]{1,0:T(8,128)(2,1)S(1)}, bf16[192,512]{1,0:T(8,128)(2,1)S(1)}, u32[]{:S(2)}, u32[]{:S(2)}) collective-permute-start(bf16[192,512]{1,0:T(8,128)(2,1)S(1)} %get-tuple-element.15), channel_id=1, source_target_pairs={{0,1},{1,0},{2,3},{3,2},{4,5},{5,4},{6,7},{7,6},{8,9},{9,8},{10,11... | collective-permute-start | bytes 589832 | tf_op jit(solution)/shard_map/ppermute | solution.py:21
  5.0 1.6 %collective-permute-start.1 = (bf16[192,512]{1,0:T(8,128)(2,1)S(1)}, bf16[192,512]{1,0:T(8,128)(2,1)S(1)}, u32[]{:S(2)}, u32[]{:S(2)}) collective-permute-start(bf16[192,512]{1,0:T(8,128)(2,1)S(1)} %get-tuple-element.16), channel_id=1, source_target_pairs={{0,2},{1,3},{2,0},{3,1},{4,6},{5,7},{6,4},{7,5},{8,10},{9,11},{10,... | collective-permute-start | bytes 589832 | tf_op jit(solution)/shard_map/ppermute | solution.py:21
  6.5 0.4 collective-permute-start.2
  7.0 2.6 %collective-permute-start.3 = (bf16[32,1024]{1,0:T(8,128)(2,1)S(1)}, bf16[32,1024]{1,0:T(8,128)(2,1)S(1)}, u32[]{:S(2)}, u32[]{:S(2)}) collective-permute-start(bf16[32,1024]{1,0:T(8,128)(2,1)S(1)} %get-tuple-element.17.refs_0_), channel_id=1, source_target_pairs={{0,4},{1,5},{2,6},{3,7},{4,0},{5,1},{6,2},{7,3},{8,12},{9,13},{10,... | collective-permute-start | bytes 196616 | tf_op jit(solution)/shard_map/ppermute | solution.py:21
  9.6 1.3 %collective-permute-start.4 = (bf16[32,1024]{1,0:T(8,128)(2,1)S(1)}, bf16[32,1024]{1,0:T(8,128)(2,1)S(1)}, u32[]{:S(2)}, u32[]{:S(2)}) collective-permute-start(bf16[32,1024]{1,0:T(8,128)(2,1)S(1)} %get-tuple-element.17.refs_0_), channel_id=1, source_target_pairs={{0,6},{1,7},{2,4},{3,5},{4,2},{5,3},{6,0},{7,1},{8,14},{9,15},{10,... | collective-permute-start | bytes 196616 | tf_op jit(solution)/shard_map/ppermute | solution.py:21
  10.9 3.2 %collective-permute-done.2.refs_1_ = bf16[32,1024]{1,0:T(8,128)(2,1)S(1)} collective-permute-done((bf16[32,1024]{1,0:T(8,128)(2,1)S(1)}, bf16[32,1024]{1,0:T(8,128)(2,1)S(1)}, u32[]{:S(2)}, u32[]{:S(2)}) %collective-permute-start.2) | collective-permute-done | bytes 65568 | tf_op jit(solution)/shard_map/ppermute | solution.py:21
  14.1 0.0 collective-permute-done.3.refs_2_
  14.1 3.4 %collective-permute-done.4.refs_3_ = bf16[32,1024]{1,0:T(8,128)(2,1)S(1)} collective-permute-done((bf16[32,1024]{1,0:T(8,128)(2,1)S(1)}, bf16[32,1024]{1,0:T(8,128)(2,1)S(1)}, u32[]{:S(2)}, u32[]{:S(2)}) %collective-permute-start.4) | collective-permute-done | bytes 65568 | tf_op jit(solution)/shard_map/ppermute | solution.py:21
  17.6 0.0 collective-permute-done.after_ref.refs_9_
  17.6 0.0 collective-permute-done.1.after2_ref.refs_10_
  17.6 0.0 copy-start.1
  17.6 0.0 copy-start
  17.6 0.6 collective-permute-start.6
  18.2 0.0 copy-start.2
  18.2 0.0 collective-permute-start.14
  18.2 0.0 collective-permute-start.5
  18.2 6.0 %collective-permute-done.6.far_ref.refs_1_ = bf16[128,1024]{1,0:T(8,128)(2,1)S(1)} collective-permute-done((bf16[128,1024]{1,0:T(8,128)(2,1)S(1)}, bf16[128,1024]{1,0:T(8,128)(2,1)S(1)}, u32[]{:S(2)}, u32[]{:S(2)}) %collective-permute-start.6) | collective-permute-done | bytes 262176 | tf_op jit(solution)/shard_map/ppermute | solution.py:21
  24.3 0.0 collective-permute-start.10
  24.3 0.0 collective-permute-done.14.refs_0_
  24.3 1.1 %collective-permute-start.15 = (bf16[192,512]{1,0:T(8,128)(2,1)S(1)}, bf16[192,512]{1,0:T(8,128)(2,1)S(1)}, u32[]{:S(2)}, u32[]{:S(2)}) collective-permute-start(bf16[192,512]{1,0:T(8,128)(2,1)S(1)} %shard_map.82), channel_id=1, source_target_pairs={{0,1},{1,0},{2,3},{3,2},{4,5},{5,4},{6,7},{7,6},{8,9},{9,8},{10,11... | collective-permute-start | bytes 589832 | tf_op jit(solution)/shard_map/ppermute | solution.py:21
  25.4 0.0 collective-permute-done.5.near2_ref
  25.4 0.0 copy-done.1
  25.4 0.0 copy-done
  25.4 0.0 copy-done.2
  25.4 0.8 %shard_map.79 = (bf16[208,128]{1,0:T(8,128)(2,1)S(1)}, f32[192,128]{1,0:T(8,128)S(1)}, f32[192,128]{1,0:T(8,128)S(1)}) custom-call(bf16[128,1024]{1,0:T(8,128)(2,1)S(1)} %shard_map.78.near_ref.refs_1_, bf16[128,1024]{1,0:T(8,128)(2,1)S(1)} %collective-permute-done.5.near2_ref, bf16[128,1024]{1,0:T(8,128)(2,1)S(1)} %collective-permute-done.6.far_ref.refs_1_, ...), custom_call_target="tpu_custom_call" | custom-call | tf_op jit(solution)/shard_map/pallas_call | solution.py:29
  26.2 1.0 %collective-permute-start.7 = (bf16[208,128]{1,0:T(8,128)(2,1)S(1)}, bf16[208,128]{1,0:T(8,128)(2,1)S(1)}, u32[]{:S(2)}, u32[]{:S(2)}) collective-permute-start(bf16[208,128]{1,0:T(8,128)(2,1)S(1)} %get-tuple-element.18.refs_0_), channel_id=1, source_target_pairs={{0,1},{1,0},{2,3},{3,2},{4,5},{5,4},{6,7},{7,6},{8,9},{9,8},{10,11... | collective-permute-start | bytes 159752 | tf_op jit(solution)/shard_map/ppermute | solution.py:21
  27.2 0.0 collective-permute-start.8
  27.2 2.5 %collective-permute-start.9 = (bf16[208,128]{1,0:T(8,128)(2,1)S(1)}, bf16[208,128]{1,0:T(8,128)(2,1)S(1)}, u32[]{:S(2)}, u32[]{:S(2)}) collective-permute-start(bf16[208,128]{1,0:T(8,128)(2,1)S(1)} %get-tuple-element.18.refs_0_), channel_id=1, source_target_pairs={{0,3},{1,2},{2,1},{3,0},{4,7},{5,6},{6,5},{7,4},{8,11},{9,10},{10,... | collective-permute-start | bytes 159752 | tf_op jit(solution)/shard_map/ppermute | solution.py:21
  29.7 0.0 collective-permute-done.10.far2_ref
  29.8 0.4 shard_map.80.refs_4_
  30.1 1.0 %collective-permute-start.11 = (bf16[192,128]{1,0:T(8,128)(2,1)S(1)}, bf16[192,128]{1,0:T(8,128)(2,1)S(1)}, u32[]{:S(2)}, u32[]{:S(2)}) collective-permute-start(bf16[192,128]{1,0:T(8,128)(2,1)S(1)} %shard_map.80.refs_4_), channel_id=1, source_target_pairs={{0,1},{1,0},{2,3},{3,2},{4,5},{5,4},{6,7},{7,6},{8,9},{9,8},{10,11... | collective-permute-start | bytes 147464 | tf_op jit(solution)/shard_map/ppermute | solution.py:21
  31.1 3.2 %collective-permute-done.7.refs_1_ = bf16[208,128]{1,0:T(8,128)(2,1)S(1)} collective-permute-done((bf16[208,128]{1,0:T(8,128)(2,1)S(1)}, bf16[208,128]{1,0:T(8,128)(2,1)S(1)}, u32[]{:S(2)}, u32[]{:S(2)}) %collective-permute-start.7) | collective-permute-done | bytes 53280 | tf_op jit(solution)/shard_map/ppermute | solution.py:21
  34.3 0.0 collective-permute-start.12
  34.3 0.0 collective-permute-done.8.refs_2_
  34.3 2.1 %collective-permute-start.13 = (bf16[192,128]{1,0:T(8,128)(2,1)S(1)}, bf16[192,128]{1,0:T(8,128)(2,1)S(1)}, u32[]{:S(2)}, u32[]{:S(2)}) collective-permute-start(bf16[192,128]{1,0:T(8,128)(2,1)S(1)} %shard_map.80.refs_4_), channel_id=1, source_target_pairs={{0,3},{1,2},{2,1},{3,0},{4,7},{5,6},{6,5},{7,4},{8,11},{9,10},{10,... | collective-permute-start | bytes 147464 | tf_op jit(solution)/shard_map/ppermute | solution.py:21
  36.4 0.0 collective-permute-done.9.refs_3_
  36.4 0.0 collective-permute-done.15.refs_11_
  36.4 0.0 collective-permute-done.11.refs_5_
  36.4 2.0 %collective-permute-done.12.refs_6_ = bf16[192,128]{1,0:T(8,128)(2,1)S(1)} collective-permute-done((bf16[192,128]{1,0:T(8,128)(2,1)S(1)}, bf16[192,128]{1,0:T(8,128)(2,1)S(1)}, u32[]{:S(2)}, u32[]{:S(2)}) %collective-permute-start.12) | collective-permute-done | bytes 49184 | tf_op jit(solution)/shard_map/ppermute | solution.py:21
  38.4 0.9 %collective-permute-done.13.refs_7_ = bf16[192,128]{1,0:T(8,128)(2,1)S(1)} collective-permute-done((bf16[192,128]{1,0:T(8,128)(2,1)S(1)}, bf16[192,128]{1,0:T(8,128)(2,1)S(1)}, u32[]{:S(2)}, u32[]{:S(2)}) %collective-permute-start.13) | collective-permute-done | bytes 49184 | tf_op jit(solution)/shard_map/ppermute | solution.py:21
  39.3 1.5 %shard_map.83 = (bf16[64,512]{1,0:T(8,128)(2,1)S(1)}, bf16[64,512]{1,0:T(8,128)(2,1)S(1)}, bf16[64,512]{1,0:T(8,128)(2,1)S(1)}, bf16[64,512]{1,0:T(8,128)(2,1)S(1)}, bf16[512,128]{1,0:T(8,128)(2,1)}) custom-call(bf16[208,128]{1,0:T(8,128)(2,1)S(1)} %get-tuple-element.18.refs_0_, bf16[208,128]{1,0:T(8,128)(2,1)S(1)} %collective-permute-done.7.refs_1_, ...), custom_call_target="tpu_custom_call" | custom-call | tf_op jit(solution)/shard_map/pallas_call | solution.py:29
  40.8 3.4 %all-to-all-start = ((bf16[32,16,128]{2,1,0:T(8,128)(2,1)}), bf16[32,16,128]{2,1,0:T(8,128)(2,1)S(1)}, u32[]{:S(2)}, u32[]{:S(2)}) async-start(bf16[32,16,128]{2,1,0:T(8,128)(2,1)} %bitcast.1), calls=%async_computation | async-start | bytes 262144 | tf_op jit(solution)/shard_map/all_to_all | solution.py:292
  44.2 1.8 %collective-permute-start.16 = (bf16[64,512]{1,0:T(8,128)(2,1)S(1)}, bf16[64,512]{1,0:T(8,128)(2,1)S(1)}, u32[]{:S(2)}, u32[]{:S(2)}) collective-permute-start(bf16[64,512]{1,0:T(8,128)(2,1)S(1)} %get-tuple-element.24), channel_id=1, source_target_pairs={{0,1},{1,0},{2,3},{3,2},{4,5},{5,4},{6,7},{7,6},{8,9},{9,8},{10,11... | collective-permute-start | bytes 196616 | tf_op jit(solution)/shard_map/ppermute | solution.py:21
  46.0 1.5 %collective-permute-start.17 = (bf16[64,512]{1,0:T(8,128)(2,1)S(1)}, bf16[64,512]{1,0:T(8,128)(2,1)S(1)}, u32[]{:S(2)}, u32[]{:S(2)}) collective-permute-start(bf16[64,512]{1,0:T(8,128)(2,1)S(1)} %get-tuple-element.25), channel_id=1, source_target_pairs={{0,2},{1,3},{2,0},{3,1},{4,6},{5,7},{6,4},{7,5},{8,10},{9,11},{10,... | collective-permute-start | bytes 196616 | tf_op jit(solution)/shard_map/ppermute | solution.py:21
  47.5 0.3 collective-permute-start.18
  47.7 4.2 %all-to-all-done = bf16[32,16,128]{2,1,0:T(8,128)(2,1)S(1)} async-done(((bf16[32,16,128]{2,1,0:T(8,128)(2,1)}), bf16[32,16,128]{2,1,0:T(8,128)(2,1)S(1)}, u32[]{:S(2)}, u32[]{:S(2)}) %all-to-all-start) | async-done | bytes 131104 | tf_op jit(solution)/shard_map/all_to_all | solution.py:292
  51.9 0.8 %shard_map.85 = f32[32,8,8]{2,1,0:T(8,128)} custom-call(bf16[8,4,16,128]{3,2,1,0:T(8,128)(2,1)S(1)} %bitcast.3), custom_call_target="tpu_custom_call" | custom-call | tf_op jit(solution)/shard_map/pallas_call | solution.py:29
  52.8 2.6 %all-to-all-start.1 = ((f32[32,8,8]{2,1,0:T(8,128)}), f32[32,8,8]{2,1,0:T(8,128)S(1)}, u32[]{:S(2)}, u32[]{:S(2)}) async-start(f32[32,8,8]{2,1,0:T(8,128)} %shard_map.85), calls=%async_computation.1 | async-start | bytes 262144 | tf_op jit(solution)/shard_map/all_to_all | solution.py:303
  55.3 0.0 collective-permute-done.16.refs_1_
  55.3 0.0 collective-permute-done.17.refs_2_
  55.4 0.0 collective-permute-done.18.refs_3_
  55.4 0.7 %shard_map.84 = bf16[64,2048]{1,0:T(8,128)(2,1)} custom-call(bf16[64,512]{1,0:T(8,128)(2,1)S(1)} %get-tuple-element.23.refs_0_, bf16[64,512]{1,0:T(8,128)(2,1)S(1)} %collective-permute-done.16.refs_1_, bf16[64,512]{1,0:T(8,128)(2,1)S(1)} %collective-permute-done.17.refs_2_, bf16[64,512]{1,0:T(8,128)(2,1)S(1)} %collective-permute-done.18.refs_3_), custom_call_target="tpu_custom_call" | custom-call | tf_op jit(solution)/shard_map/pallas_call | solution.py:29
  56.1 7.0 %all-to-all-done.1.tables_ref = f32[32,8,8]{2,1,0:T(8,128)S(1)} async-done(((f32[32,8,8]{2,1,0:T(8,128)}), f32[32,8,8]{2,1,0:T(8,128)S(1)}, u32[]{:S(2)}, u32[]{:S(2)}) %all-to-all-start.1) | async-done | bytes 8224 | tf_op jit(solution)/shard_map/all_to_all | solution.py:303
  63.1 0.7 %shard_map.86 = f32[8,8]{1,0:T(8,128)} custom-call(f32[32,8,8]{2,1,0:T(8,128)S(1)} %all-to-all-done.1.tables_ref), custom_call_target="tpu_custom_call" | custom-call | tf_op jit(solution)/shard_map/pallas_call | solution.py:29
  (3 shorter events, 0.0 us)
Async XLA Ops:
  2.0 15.6 %collective-permute-start = (bf16[192,512]{1,0:T(8,128)(2,1)S(1)}, bf16[192,512]{1,0:T(8,128)(2,1)S(1)}, u32[]{:S(2)}, u32[]{:S(2)}) collective-permute-start(bf16[192,512]{1,0:T(8,128)(2,1)S(1)} %get-tuple-element.15), channel_id=1, source_target_pairs={{0,1},{1,0},{2,3},{3,2},{4,5},{5,4},{6,7},{7,6},{8,9},{9,8},{10,11... | collective-permute-start | bytes 589832 | tf_op jit(solution)/shard_map/ppermute | solution.py:21
  5.0 12.6 %collective-permute-start.1 = (bf16[192,512]{1,0:T(8,128)(2,1)S(1)}, bf16[192,512]{1,0:T(8,128)(2,1)S(1)}, u32[]{:S(2)}, u32[]{:S(2)}) collective-permute-start(bf16[192,512]{1,0:T(8,128)(2,1)S(1)} %get-tuple-element.16), channel_id=1, source_target_pairs={{0,2},{1,3},{2,0},{3,1},{4,6},{5,7},{6,4},{7,5},{8,10},{9,11},{10,... | collective-permute-start | bytes 589832 | tf_op jit(solution)/shard_map/ppermute | solution.py:21
  6.5 7.6 %collective-permute-start.2 = (bf16[32,1024]{1,0:T(8,128)(2,1)S(1)}, bf16[32,1024]{1,0:T(8,128)(2,1)S(1)}, u32[]{:S(2)}, u32[]{:S(2)}) collective-permute-start(bf16[32,1024]{1,0:T(8,128)(2,1)S(1)} %get-tuple-element.17.refs_0_), channel_id=1, source_target_pairs={{0,2},{1,3},{2,0},{3,1},{4,6},{5,7},{6,4},{7,5},{8,10},{9,11},{10,... | collective-permute-start | bytes 196616 | tf_op jit(solution)/shard_map/ppermute | solution.py:21
  7.0 7.1 %collective-permute-start.3 = (bf16[32,1024]{1,0:T(8,128)(2,1)S(1)}, bf16[32,1024]{1,0:T(8,128)(2,1)S(1)}, u32[]{:S(2)}, u32[]{:S(2)}) collective-permute-start(bf16[32,1024]{1,0:T(8,128)(2,1)S(1)} %get-tuple-element.17.refs_0_), channel_id=1, source_target_pairs={{0,4},{1,5},{2,6},{3,7},{4,0},{5,1},{6,2},{7,3},{8,12},{9,13},{10,... | collective-permute-start | bytes 196616 | tf_op jit(solution)/shard_map/ppermute | solution.py:21
  9.6 8.0 %collective-permute-start.4 = (bf16[32,1024]{1,0:T(8,128)(2,1)S(1)}, bf16[32,1024]{1,0:T(8,128)(2,1)S(1)}, u32[]{:S(2)}, u32[]{:S(2)}) collective-permute-start(bf16[32,1024]{1,0:T(8,128)(2,1)S(1)} %get-tuple-element.17.refs_0_), channel_id=1, source_target_pairs={{0,6},{1,7},{2,4},{3,5},{4,2},{5,3},{6,0},{7,1},{8,14},{9,15},{10,... | collective-permute-start | bytes 196616 | tf_op jit(solution)/shard_map/ppermute | solution.py:21
  17.6 7.8 %copy-start.1 = (bf16[192,2048]{1,0:T(8,128)(2,1)S(1)}, bf16[192,2048]{1,0:T(8,128)(2,1)}, u32[]{:S(2)}) copy-start(bf16[192,2048]{1,0:T(8,128)(2,1)} %up_ref.3) | copy-start | bytes 2359300
  17.6 7.8 %copy-start = (bf16[192,2048]{1,0:T(8,128)(2,1)S(1)}, bf16[192,2048]{1,0:T(8,128)(2,1)}, u32[]{:S(2)}) copy-start(bf16[192,2048]{1,0:T(8,128)(2,1)} %gate_ref.3) | copy-start | bytes 2359300
  17.6 6.6 %collective-permute-start.6 = (bf16[128,1024]{1,0:T(8,128)(2,1)S(1)}, bf16[128,1024]{1,0:T(8,128)(2,1)S(1)}, u32[]{:S(2)}, u32[]{:S(2)}) collective-permute-start(bf16[128,1024]{1,0:T(8,128)(2,1)S(1)} %shard_map.78.near_ref.refs_1_), channel_id=1, source_target_pairs={{0,1},{1,0},{2,3},{3,2},{4,5},{5,4},{6,7},{7,6},{8,9},{9,8},{10,11... | collective-permute-start | bytes 786440 | tf_op jit(solution)/shard_map/ppermute | solution.py:21
  18.2 7.2 %copy-start.2 = (f32[1,64]{1,0:T(1,128)S(1)}, f32[1,64]{1,0:T(1,128)}, u32[]{:S(2)}) copy-start(f32[1,64]{1,0:T(1,128)} %route_ref.1) | copy-start | bytes 772
  18.2 6.0 %collective-permute-start.14 = (bf16[192,512]{1,0:T(8,128)(2,1)S(1)}, bf16[192,512]{1,0:T(8,128)(2,1)S(1)}, u32[]{:S(2)}, u32[]{:S(2)}) collective-permute-start(bf16[192,512]{1,0:T(8,128)(2,1)S(1)} %shard_map.81), channel_id=1, source_target_pairs={{0,2},{1,3},{2,0},{3,1},{4,6},{5,7},{6,4},{7,5},{8,10},{9,11},{10,... | collective-permute-start | bytes 589832 | tf_op jit(solution)/shard_map/ppermute | solution.py:21
  18.2 7.2 %collective-permute-start.5 = (bf16[128,1024]{1,0:T(8,128)(2,1)S(1)}, bf16[128,1024]{1,0:T(8,128)(2,1)S(1)}, u32[]{:S(2)}, u32[]{:S(2)}) collective-permute-start(bf16[128,1024]{1,0:T(8,128)(2,1)S(1)} %shard_map.78.near_ref.refs_1_), channel_id=1, source_target_pairs={{0,8},{8,0},{16,24},{24,16},{1,9},{9,1},{17,25},{25,17},{2,10},{10... | collective-permute-start | bytes 786440 | tf_op jit(solution)/shard_map/ppermute | solution.py:21
  24.3 5.5 %collective-permute-start.10 = (bf16[128,1024]{1,0:T(8,128)(2,1)S(1)}, bf16[128,1024]{1,0:T(8,128)(2,1)S(1)}, u32[]{:S(2)}, u32[]{:S(2)}) collective-permute-start(bf16[128,1024]{1,0:T(8,128)(2,1)S(1)} %collective-permute-done.6.far_ref.refs_1_), channel_id=1, source_target_pairs={{0,8},{8,0},{16,24},{24,16},{1,9},{9,1},{17,25},{25,17},{2,10},{10... | collective-permute-start | bytes 786440 | tf_op jit(solution)/shard_map/ppermute | solution.py:21
  24.3 12.1 %collective-permute-start.15 = (bf16[192,512]{1,0:T(8,128)(2,1)S(1)}, bf16[192,512]{1,0:T(8,128)(2,1)S(1)}, u32[]{:S(2)}, u32[]{:S(2)}) collective-permute-start(bf16[192,512]{1,0:T(8,128)(2,1)S(1)} %shard_map.82), channel_id=1, source_target_pairs={{0,1},{1,0},{2,3},{3,2},{4,5},{5,4},{6,7},{7,6},{8,9},{9,8},{10,11... | collective-permute-start | bytes 589832 | tf_op jit(solution)/shard_map/ppermute | solution.py:21
  26.2 8.1 %collective-permute-start.7 = (bf16[208,128]{1,0:T(8,128)(2,1)S(1)}, bf16[208,128]{1,0:T(8,128)(2,1)S(1)}, u32[]{:S(2)}, u32[]{:S(2)}) collective-permute-start(bf16[208,128]{1,0:T(8,128)(2,1)S(1)} %get-tuple-element.18.refs_0_), channel_id=1, source_target_pairs={{0,1},{1,0},{2,3},{3,2},{4,5},{5,4},{6,7},{7,6},{8,9},{9,8},{10,11... | collective-permute-start | bytes 159752 | tf_op jit(solution)/shard_map/ppermute | solution.py:21
  27.2 7.1 %collective-permute-start.8 = (bf16[208,128]{1,0:T(8,128)(2,1)S(1)}, bf16[208,128]{1,0:T(8,128)(2,1)S(1)}, u32[]{:S(2)}, u32[]{:S(2)}) collective-permute-start(bf16[208,128]{1,0:T(8,128)(2,1)S(1)} %get-tuple-element.18.refs_0_), channel_id=1, source_target_pairs={{0,2},{1,3},{2,0},{3,1},{4,6},{5,7},{6,4},{7,5},{8,10},{9,11},{10,... | collective-permute-start | bytes 159752 | tf_op jit(solution)/shard_map/ppermute | solution.py:21
  27.2 9.2 %collective-permute-start.9 = (bf16[208,128]{1,0:T(8,128)(2,1)S(1)}, bf16[208,128]{1,0:T(8,128)(2,1)S(1)}, u32[]{:S(2)}, u32[]{:S(2)}) collective-permute-start(bf16[208,128]{1,0:T(8,128)(2,1)S(1)} %get-tuple-element.18.refs_0_), channel_id=1, source_target_pairs={{0,3},{1,2},{2,1},{3,0},{4,7},{5,6},{6,5},{7,4},{8,11},{9,10},{10,... | collective-permute-start | bytes 159752 | tf_op jit(solution)/shard_map/ppermute | solution.py:21
  30.1 6.3 %collective-permute-start.11 = (bf16[192,128]{1,0:T(8,128)(2,1)S(1)}, bf16[192,128]{1,0:T(8,128)(2,1)S(1)}, u32[]{:S(2)}, u32[]{:S(2)}) collective-permute-start(bf16[192,128]{1,0:T(8,128)(2,1)S(1)} %shard_map.80.refs_4_), channel_id=1, source_target_pairs={{0,1},{1,0},{2,3},{3,2},{4,5},{5,4},{6,7},{7,6},{8,9},{9,8},{10,11... | collective-permute-start | bytes 147464 | tf_op jit(solution)/shard_map/ppermute | solution.py:21
  34.3 4.1 %collective-permute-start.12 = (bf16[192,128]{1,0:T(8,128)(2,1)S(1)}, bf16[192,128]{1,0:T(8,128)(2,1)S(1)}, u32[]{:S(2)}, u32[]{:S(2)}) collective-permute-start(bf16[192,128]{1,0:T(8,128)(2,1)S(1)} %shard_map.80.refs_4_), channel_id=1, source_target_pairs={{0,2},{1,3},{2,0},{3,1},{4,6},{5,7},{6,4},{7,5},{8,10},{9,11},{10,... | collective-permute-start | bytes 147464 | tf_op jit(solution)/shard_map/ppermute | solution.py:21
  34.3 5.0 %collective-permute-start.13 = (bf16[192,128]{1,0:T(8,128)(2,1)S(1)}, bf16[192,128]{1,0:T(8,128)(2,1)S(1)}, u32[]{:S(2)}, u32[]{:S(2)}) collective-permute-start(bf16[192,128]{1,0:T(8,128)(2,1)S(1)} %shard_map.80.refs_4_), channel_id=1, source_target_pairs={{0,3},{1,2},{2,1},{3,0},{4,7},{5,6},{6,5},{7,4},{8,11},{9,10},{10,... | collective-permute-start | bytes 147464 | tf_op jit(solution)/shard_map/ppermute | solution.py:21
  40.8 11.2 %all-to-all-start = ((bf16[32,16,128]{2,1,0:T(8,128)(2,1)}), bf16[32,16,128]{2,1,0:T(8,128)(2,1)S(1)}, u32[]{:S(2)}, u32[]{:S(2)}) async-start(bf16[32,16,128]{2,1,0:T(8,128)(2,1)} %bitcast.1), calls=%async_computation | async-start | bytes 262144 | tf_op jit(solution)/shard_map/all_to_all | solution.py:292
  44.2 11.1 %collective-permute-start.16 = (bf16[64,512]{1,0:T(8,128)(2,1)S(1)}, bf16[64,512]{1,0:T(8,128)(2,1)S(1)}, u32[]{:S(2)}, u32[]{:S(2)}) collective-permute-start(bf16[64,512]{1,0:T(8,128)(2,1)S(1)} %get-tuple-element.24), channel_id=1, source_target_pairs={{0,1},{1,0},{2,3},{3,2},{4,5},{5,4},{6,7},{7,6},{8,9},{9,8},{10,11... | collective-permute-start | bytes 196616 | tf_op jit(solution)/shard_map/ppermute | solution.py:21
  46.0 9.3 %collective-permute-start.17 = (bf16[64,512]{1,0:T(8,128)(2,1)S(1)}, bf16[64,512]{1,0:T(8,128)(2,1)S(1)}, u32[]{:S(2)}, u32[]{:S(2)}) collective-permute-start(bf16[64,512]{1,0:T(8,128)(2,1)S(1)} %get-tuple-element.25), channel_id=1, source_target_pairs={{0,2},{1,3},{2,0},{3,1},{4,6},{5,7},{6,4},{7,5},{8,10},{9,11},{10,... | collective-permute-start | bytes 196616 | tf_op jit(solution)/shard_map/ppermute | solution.py:21
  47.5 7.9 %collective-permute-start.18 = (bf16[64,512]{1,0:T(8,128)(2,1)S(1)}, bf16[64,512]{1,0:T(8,128)(2,1)S(1)}, u32[]{:S(2)}, u32[]{:S(2)}) collective-permute-start(bf16[64,512]{1,0:T(8,128)(2,1)S(1)} %get-tuple-element.26), channel_id=1, source_target_pairs={{0,3},{1,2},{2,1},{3,0},{4,7},{5,6},{6,5},{7,4},{8,11},{9,10},{10,... | collective-permute-start | bytes 196616 | tf_op jit(solution)/shard_map/ppermute | solution.py:21
  52.8 10.3 %all-to-all-start.1 = ((f32[32,8,8]{2,1,0:T(8,128)}), f32[32,8,8]{2,1,0:T(8,128)S(1)}, u32[]{:S(2)}, u32[]{:S(2)}) async-start(f32[32,8,8]{2,1,0:T(8,128)} %shard_map.85), calls=%async_computation.1 | async-start | bytes 262144 | tf_op jit(solution)/shard_map/all_to_all | solution.py:303

commit v12 on v11

--- a/solution.py
+++ b/solution.py
@@ -45,26 +45,41 @@
     return lax.axis_index("tok") & (HOLDERS - 1)
 
 
-def first_kernel(states_hbm, gain_hbm, down_hbm, out_ref, *refs):
-    downs, (states_ref, gain_ref, sems) = refs[:HOLDERS], refs[HOLDERS:]
+def first_kernel(states_hbm, gain_hbm, down_hbm, route_hbm, out_ref, *refs):
+    downs, (states_ref, gain_ref, route_ref, sems) = refs[:HOLDERS], refs[HOLDERS:]
     copies = [
         pltpu.make_async_copy(states_hbm, states_ref, sems.at[0]),
         pltpu.make_async_copy(gain_hbm, gain_ref, sems.at[1]),
+        pltpu.make_async_copy(route_hbm, route_ref, sems.at[2]),
     ]
-    width = downs[0].shape[1]
+    depth, width = down_hbm.shape[0], downs[0].shape[1]
     for m, down_ref in enumerate(downs):
         columns = pl.ds(pl.multiple_of((holder() ^ m) * width, width), width)
-        copies.append(pltpu.make_async_copy(down_hbm.at[:, columns], down_ref, sems.at[2 + m]))
+        copies.append(
+            pltpu.make_async_copy(
+                down_hbm.at[:, columns], down_ref.at[pl.ds(0, depth)], sems.at[3 + m]
+            )
+        )
     for copy in copies:
         copy.start()
-    for copy in copies[:2]:
+    for copy in copies[:3]:
         copy.wait()
     states = states_ref[...].astype(f32)
     scale = lax.rsqrt(jnp.mean(states * states, axis=1, keepdims=True) + 1e-06)
     width = out_ref.shape[1]
     own = pl.ds(pl.multiple_of(core() * width, width), width)
     out_ref[...] = (states_ref[:, own].astype(f32) * scale * gain_ref[:, own]).astype(bf16)
-    for copy in copies[2:]:
+    route = route_ref[...]
+    high = route.astype(bf16).astype(f32)
+    middle = (route - high).astype(bf16).astype(f32)
+    low = route - high - middle
+    part = route.shape[1]
+    row = lax.broadcasted_iota(jnp.int32, (TILE, part), 0)
+    terms = jnp.where(row == 0, high, jnp.where(row == 1, middle, jnp.where(row == 2, low, 0.0)))
+    terms = jnp.concatenate([terms, jnp.zeros((TILE, downs[0].shape[1] - part), f32)], 1)
+    for down_ref in downs:
+        down_ref[depth:] = terms.astype(bf16)
+    for copy in copies[3:]:
         copy.wait()
 
 
@@ -83,7 +98,7 @@
     )
 
 
-def stack_kernel(after_ref, after2_ref, *refs):
+def stack_kernel(after_ref, *refs):
     rows = refs[0].shape[0]
     z = lax.axis_index("tok") >> 1
     for m, piece in enumerate(refs[:-1]):
@@ -98,48 +113,39 @@
     return (gate / (1.0 + jnp.exp(-gate)) * upward).astype(bf16)
 
 
-def near_kernel(near_ref, near2_ref, far_ref, gate_ref, up_ref, route_ref, out_ref, gate_part_ref, up_part_ref):
-    count, width = near_ref.shape
-    depth = gate_ref.shape[0]
+def near_kernel(near_ref, near2_ref, far_ref, gate_ref, up_ref, out_ref, gate_part_ref, up_part_ref):
+    width = near_ref.shape[1]
     own, rest = columns_of(core(), width), columns_of(1 - core(), width)
     near, near2, far = near_ref[...], near2_ref[...], far_ref[...]
     gate, upward = [
         dot_f32(ref[:, own], near, TRANSPOSED) + dot_f32(ref[:, rest], near2, TRANSPOSED)
         for ref in (gate_ref, up_ref)
     ]
-    out_ref[:depth] = gated(gate, upward)
-    route = route_ref[...]
-    high = route.astype(bf16).astype(f32)
-    middle = (route - high).astype(bf16).astype(f32)
-    low = route - high - middle
-    part = route.shape[1]
-    row = lax.broadcasted_iota(jnp.int32, (TILE, part), 0)
-    terms = jnp.where(row == 0, high, jnp.where(row == 1, middle, jnp.where(row == 2, low, 0.0)))
-    terms = jnp.concatenate([terms, jnp.zeros((TILE, count - part), f32)], 1)
-    out_ref[depth:] = terms.astype(bf16)
+    out_ref[...] = gated(gate, upward)
     gate_part_ref[...] = dot_f32(gate_ref[:, own], far, TRANSPOSED)
     up_part_ref[...] = dot_f32(up_ref[:, own], far, TRANSPOSED)
 
 
-def far_kernel(far2_ref, gate_ref, up_ref, gate_part_ref, up_part_ref, out_ref):
-    rest = columns_of(1 - core(), far2_ref.shape[1])
+def far_kernel(far2_ref, gate_ref, up_ref, near_hidden_ref, gate_part_ref, up_part_ref, out_ref):
+    count, width = far2_ref.shape
+    rest = columns_of(1 - core(), width)
     far2 = far2_ref[...]
     gate, upward = [
         part_ref[...] + dot_f32(ref[:, rest], far2, TRANSPOSED)
         for ref, part_ref in ((gate_ref, gate_part_ref), (up_ref, up_part_ref))
     ]
-    out_ref[...] = gated(gate, upward)
+    x = lax.axis_index("tok") & 1
+    out_ref[:, columns_of(x, count)] = near_hidden_ref[...]
+    out_ref[:, columns_of(1 - x, count)] = gated(gate, upward)
 
 
 def features_kernel(*refs):
-    near_refs, far_refs, down_refs = [refs[n * HOLDERS : (n + 1) * HOLDERS] for n in range(3)]
-    block_refs, centered_ref = refs[3 * HOLDERS : 4 * HOLDERS], refs[4 * HOLDERS]
-    route_ref, features_ref, whole_ref = refs[4 * HOLDERS + 1 :]
-    depth, half = far_refs[0].shape
-    tokens = 2 * half
+    hidden_refs, down_refs = refs[:HOLDERS], refs[HOLDERS : 2 * HOLDERS]
+    block_refs, shares_hbm = refs[2 * HOLDERS : 3 * HOLDERS], refs[3 * HOLDERS]
+    route_ref, features_ref, whole_ref, shares_ref, sem = refs[3 * HOLDERS + 1 :]
+    depth, tokens = hidden_refs[0].shape
     part, members = tokens // HOLDERS, lax.axis_size("tok")
     rows = tokens // members
-    x = lax.axis_index("tok") & 1
 
     def place(m, piece):
         z = (holder() ^ m) * (members // HOLDERS // 2) + piece // 2
@@ -148,24 +154,18 @@
     eye = lax.broadcasted_iota(jnp.int32, (part, part), 0) == lax.broadcasted_iota(
         jnp.int32, (part, part), 1
     )
-    here = there = None
-    for m in range(HOLDERS):
-        near, far, down = near_refs[m][:depth], far_refs[m][...], down_refs[m][...]
-        for_here, for_there = (far, near) if m & 1 else (near, far)
-        for_here = dot_f32(for_here, down, (((0,), (0,)), ((), ())))
-        for_there = dot_f32(for_there, down, (((0,), (0,)), ((), ())))
-        here = for_here if m == 0 else here + for_here
-        there = for_there if m == 0 else there + for_there
-        terms = near_refs[m][depth:, :part].astype(f32)
+    output = None
+    for m, (hidden_ref, down_ref) in enumerate(zip(hidden_refs, down_refs)):
+        product = dot_f32(hidden_ref[...], down_ref[:depth], (((0,), (0,)), ((), ())))
+        output = product if output is None else output + product
+        terms = down_ref[depth:, :part].astype(f32)
         route = jnp.sum(terms[:HOLDERS], axis=0, keepdims=True)
         column = jnp.sum(jnp.where(eye, route, 0.0), axis=1, keepdims=True)
         column = jnp.broadcast_to(column, (part, LANES))
         for piece in range(part // rows):
             route_ref[place(m, piece)] = column[piece * rows : (piece + 1) * rows]
-    for at, output in ((x, here), (1 - x, there)):
-        at = pl.ds(pl.multiple_of(at * half, half), half)
-        features_ref[at] = (output * route_ref[at][:, :1]).astype(bf16)
-    features = features_ref[...]
+    features = (output * route_ref[:, :1]).astype(bf16)
+    features_ref[...] = features
     wide = features.astype(f32)
     mean = jnp.sum(wide, axis=0, keepdims=True) / tokens
     column = jnp.sum(wide * mean, axis=1, keepdims=True)
@@ -175,13 +175,16 @@
     at = 0
     for i in range(tokens // TILE):
         for j in range(tokens // LANES):
-            centered_ref[at * TILE : (at + 1) * TILE] = whole_ref[
+            shares_ref[at * TILE : (at + 1) * TILE] = whole_ref[
                 i * TILE : (i + 1) * TILE, j * LANES : (j + 1) * LANES
             ]
             at += 1
+    copy = pltpu.make_async_copy(shares_ref, shares_hbm, sem)
+    copy.start()
     for m, block_ref in enumerate(block_refs):
         for piece in range(part // rows):
             block_ref[piece * rows : (piece + 1) * rows] = features_ref[place(m, piece)]
+    copy.wait()
 
 
 def place_kernel(*refs):
@@ -236,57 +239,60 @@
     own, *downs = call(
         first_kernel,
         [jax.ShapeDtypeStruct((rows, model // 2), bf16)]
-        + [jax.ShapeDtypeStruct((depth, part), bf16)] * HOLDERS,
-        [HBM] * 3,
+        + [jax.ShapeDtypeStruct((depth + TILE, part), bf16)] * HOLDERS,
+        [HBM] * 4,
         [
             pltpu.with_memory_space_constraint(a, pltpu.HBM)
-            for a in (probe_states, norm_gain[None, :], down_weight)
+            for a in (probe_states, norm_gain[None, :], down_weight, route_weight)
         ],
         scratch=[
             pltpu.VMEM((rows, model), bf16),
             pltpu.VMEM((1, model), f32),
-            pltpu.SemaphoreType.DMA((2 + HOLDERS,)),
+            pltpu.VMEM(route_weight.shape, f32),
+            pltpu.SemaphoreType.DMA((3 + HOLDERS,)),
         ],
     )
     down_x = swapped(downs[1], "tok", 1)
     pieces = [swapped(own, "tok", 2 * m) if m else own for m in range(members // 2)]
-    down_z = swapped(downs[2], "tok", 2)
     near = call(
         stack_kernel,
         jax.ShapeDtypeStruct((tokens // 2, model // 2), bf16),
-        [ANY] * 2 + [VMEM] * len(pieces),
-        (down_x, down_z, *pieces),
+        [ANY] + [VMEM] * len(pieces),
+        (down_x, *pieces),
     )
     far = swapped(near, "tok", 1)
     near2 = swapped(near, "grp", 1)
     down_xz = swapped(held(downs[3], near), "tok", 2)
-    half_shape = jax.ShapeDtypeStruct((depth, tokens // 2), f32)
+    down_z = swapped(held(downs[2], near), "tok", 2)
+    half_shape = (depth, tokens // 2)
     near_hidden, gate_part, up_part = call(
         near_kernel,
-        [jax.ShapeDtypeStruct((depth + TILE, tokens // 2), bf16), half_shape, half_shape],
+        [jax.ShapeDtypeStruct(half_shape, dtype) for dtype in (bf16, f32, f32)],
+        [VMEM] * 5,
+        (near, near2, far, gate_weight, up_weight),
+    )
+    down_xz = swapped(held(down_xz, far), "tok", 1)
+    hidden = call(
+        far_kernel,
+        jax.ShapeDtypeStruct((depth, tokens), bf16),
         [VMEM] * 6,
-        (near, near2, far, gate_weight, up_weight, route_weight),
-    )
-    near_hiddens = [swapped(near_hidden, "tok", m) if m else near_hidden for m in range(HOLDERS)]
-    down_xz = swapped(held(down_xz, far), "tok", 1)
-    far_hidden = call(
-        far_kernel,
-        jax.ShapeDtypeStruct((depth, tokens // 2), bf16),
-        [VMEM] * 5,
-        (swapped(far, "grp", 1), gate_weight, up_weight, gate_part, up_part),
-    )
-    far_hiddens = [swapped(far_hidden, "tok", m) if m else far_hidden for m in range(HOLDERS)]
+        (swapped(far, "grp", 1), gate_weight, up_weight, near_hidden, gate_part, up_part),
+    )
+    hiddens = [swapped(hidden, "tok", m) if m else hidden for m in range(HOLDERS)]
     entries = tokens * tokens // LANES
     *blocks, centered = call(
         features_kernel,
         [jax.ShapeDtypeStruct((token_part, part), bf16)] * HOLDERS
         + [jax.ShapeDtypeStruct((entries, LANES), bf16)],
-        [VMEM] * (3 * HOLDERS),
-        (*near_hiddens, *far_hiddens, downs[0], down_x, down_z, down_xz),
+        [VMEM] * (2 * HOLDERS),
+        (*hiddens, downs[0], down_x, down_z, down_xz),
+        out_specs=[VMEM] * HOLDERS + [HBM],
         scratch=[
             pltpu.VMEM((tokens, LANES), f32),
             pltpu.VMEM((tokens, part), bf16),
             pltpu.VMEM((tokens, tokens), bf16),
+            pltpu.VMEM((entries, LANES), bf16),
+            pltpu.SemaphoreType.DMA,
         ],
     )
     arrived = lax.all_to_all(centered, ("grp", "tok"), split_axis=0, concat_axis=0, tiled=True)

time: 64 us -> 58.1 us (0.908)
  starting transfers between devices: 26.9 us -> 22.6 us
  waiting for transfers between devices: 29.9 us -> 28.3 us
    ppermute x19 -> x16, starting transfers between devices: 20.9 us -> 16.9 us  [swapped(): lax.ppermute(array, axis, [(i, i ^ mask) for i in range(lax.axis_size(axi...]
    ppermute x19 -> x16, waiting for transfers between devices: 18.7 us -> 17.2 us  [swapped(): lax.ppermute(array, axis, [(i, i ^ mask) for i in range(lax.axis_size(axi...]
    pallas_call x10 -> x11, Pallas kernels: 6.25 us -> 6.23 us  [call(): pl.pallas_call(body, out_shape=outs, in_specs=in_specs, out_specs=jax.tre...]
  transfers between devices with their start and end apart: 21 -> 18, of which waited for: 8 -> 9; matrix products, arithmetic and copies ran while one was open for 0% -> 0% of each run, Pallas kernels for 4% -> 5%
where the time goes in v12:
time: 58.1 us; the launch traced here: 57.9 us
  waiting for transfers between devices  28.3 us (49%)
  starting transfers between devices  22.6 us (39%)
  Pallas kernels  6.23 us (11%)
  between operations  0.74 us (1%)
    ppermute x16, waiting for transfers between devices, swapped(): lax.ppermute(array, axis, [(i, i ^ mask) for i in range(lax.axis_size(axi...  17.2 us
    ppermute x16, starting transfers between devices, swapped(): lax.ppermute(array, axis, [(i, i ^ mask) for i in range(lax.axis_size(axi...  16.9 us
    all_to_all x1, waiting for transfers between devices, shards(): lax.all_to_all(tables, ('grp', 'tok'), split_axis=0, concat_axis=0, tiled...  6.96 us
    pallas_call x11, Pallas kernels, call(): pl.pallas_call(body, out_shape=outs, in_specs=in_specs, out_specs=jax.tre...  6.23 us
    all_to_all x1, waiting for transfers between devices, shards(): lax.all_to_all(centered, ('grp', 'tok'), split_axis=0, concat_axis=0, til...  4.19 us
    all_to_all x1, starting transfers between devices, shards(): lax.all_to_all(centered, ('grp', 'tok'), split_axis=0, concat_axis=0, til...  3.13 us
    all_to_all x1, starting transfers between devices, shards(): lax.all_to_all(tables, ('grp', 'tok'), split_axis=0, concat_axis=0, tiled...  2.56 us
  transfers between devices with their start and end apart: 18, of which 9 were waited for; matrix products, arithmetic and copies ran while one was open for 0% of the time, Pallas kernels for 5%

profile of v12, /device:TPU:0, one launch (start us, length us, event | category | flops | bytes accessed | tf_op | source)
XLA Modules:
  0.0 57.9 jit_solution(5065261622971240547)
XLA Ops:
  0.6 1.3 %shard_map.77 = (bf16[32,1024]{1,0:T(8,128)(2,1)S(1)}, bf16[208,512]{1,0:T(8,128)(2,1)S(1)}, bf16[208,512]{1,0:T(8,128)(2,1)S(1)}, bf16[208,512]{1,0:T(8,128)(2,1)S(1)}, bf16[208,512]{1,0:T(8,128)(2,1)S(1)}) custom-call(bf16[32,2048]{1,0:T(8,128)(2,1)} %states_hbm.1, f32[1,2048]{1,0:T(1,128)} %bitcast.4, bf16[192,2048]{1,0:T(8,128)(2,1)} %down_hbm.1, ...), custom_call_target="tpu_custom_call" | custom-call | tf_op jit(solution)/shard_map/pallas_call | solution.py:29
  2.0 3.0 %collective-permute-start = (bf16[208,512]{1,0:T(8,128)(2,1)S(1)}, bf16[208,512]{1,0:T(8,128)(2,1)S(1)}, u32[]{:S(2)}, u32[]{:S(2)}) collective-permute-start(bf16[208,512]{1,0:T(8,128)(2,1)S(1)} %get-tuple-element.15), channel_id=1, source_target_pairs={{0,1},{1,0},{2,3},{3,2},{4,5},{5,4},{6,7},{7,6},{8,9},{9,8},{10,11... | collective-permute-start | bytes 638984 | tf_op jit(solution)/shard_map/ppermute | solution.py:21
  5.0 3.6 %collective-permute-start.3 = (bf16[32,1024]{1,0:T(8,128)(2,1)S(1)}, bf16[32,1024]{1,0:T(8,128)(2,1)S(1)}, u32[]{:S(2)}, u32[]{:S(2)}) collective-permute-start(bf16[32,1024]{1,0:T(8,128)(2,1)S(1)} %get-tuple-element.16.refs_0_), channel_id=1, source_target_pairs={{0,6},{1,7},{2,4},{3,5},{4,2},{5,3},{6,0},{7,1},{8,14},{9,15},{10,... | collective-permute-start | bytes 196616 | tf_op jit(solution)/shard_map/ppermute | solution.py:21
  8.6 0.0 collective-permute-start.2
  8.6 0.8 %collective-permute-start.1 = (bf16[32,1024]{1,0:T(8,128)(2,1)S(1)}, bf16[32,1024]{1,0:T(8,128)(2,1)S(1)}, u32[]{:S(2)}, u32[]{:S(2)}) collective-permute-start(bf16[32,1024]{1,0:T(8,128)(2,1)S(1)} %get-tuple-element.16.refs_0_), channel_id=1, source_target_pairs={{0,2},{1,3},{2,0},{3,1},{4,6},{5,7},{6,4},{7,5},{8,10},{9,11},{10,... | collective-permute-start | bytes 196616 | tf_op jit(solution)/shard_map/ppermute | solution.py:21
  9.4 2.5 %collective-permute-done.3.refs_3_ = bf16[32,1024]{1,0:T(8,128)(2,1)S(1)} collective-permute-done((bf16[32,1024]{1,0:T(8,128)(2,1)S(1)}, bf16[32,1024]{1,0:T(8,128)(2,1)S(1)}, u32[]{:S(2)}, u32[]{:S(2)}) %collective-permute-start.3) | collective-permute-done | bytes 65568 | tf_op jit(solution)/shard_map/ppermute | solution.py:21
  11.9 2.1 %collective-permute-done.2.refs_2_ = bf16[32,1024]{1,0:T(8,128)(2,1)S(1)} collective-permute-done((bf16[32,1024]{1,0:T(8,128)(2,1)S(1)}, bf16[32,1024]{1,0:T(8,128)(2,1)S(1)}, u32[]{:S(2)}, u32[]{:S(2)}) %collective-permute-start.2) | collective-permute-done | bytes 65568 | tf_op jit(solution)/shard_map/ppermute | solution.py:21
  14.0 0.1 collective-permute-done.1.refs_1_
  14.0 0.0 collective-permute-done.after_ref.refs_5_
  14.1 0.5 collective-permute-start.4
  14.6 0.0 copy-start.1
  14.6 0.0 copy-start
  14.6 1.1 %collective-permute-start.11 = (bf16[208,512]{1,0:T(8,128)(2,1)S(1)}, bf16[208,512]{1,0:T(8,128)(2,1)S(1)}, u32[]{:S(2)}, u32[]{:S(2)}) collective-permute-start(bf16[208,512]{1,0:T(8,128)(2,1)S(1)} %shard_map.82), channel_id=1, source_target_pairs={{0,2},{1,3},{2,0},{3,1},{4,6},{5,7},{6,4},{7,5},{8,10},{9,11},{10,... | collective-permute-start | bytes 638984 | tf_op jit(solution)/shard_map/ppermute | solution.py:21
  15.6 0.0 collective-permute-start.6
  15.6 6.1 %collective-permute-done.4.far_ref.refs_1_ = bf16[128,1024]{1,0:T(8,128)(2,1)S(1)} collective-permute-done((bf16[128,1024]{1,0:T(8,128)(2,1)S(1)}, bf16[128,1024]{1,0:T(8,128)(2,1)S(1)}, u32[]{:S(2)}, u32[]{:S(2)}) %collective-permute-start.4) | collective-permute-done | bytes 262176 | tf_op jit(solution)/shard_map/ppermute | solution.py:21
  21.7 0.0 collective-permute-start.5
  21.7 0.3 collective-permute-start.10
  22.0 0.0 collective-permute-done.11.refs_0_
  22.0 0.5 collective-permute-start.12
  22.5 0.0 collective-permute-done.6.near2_ref
  22.5 0.0 copy-done.1
  22.6 0.0 copy-done
  22.6 0.8 %shard_map.79 = (bf16[192,128]{1,0:T(8,128)(2,1)S(1)}, f32[192,128]{1,0:T(8,128)S(1)}, f32[192,128]{1,0:T(8,128)S(1)}) custom-call(bf16[128,1024]{1,0:T(8,128)(2,1)S(1)} %shard_map.78.near_ref.refs_1_, bf16[128,1024]{1,0:T(8,128)(2,1)S(1)} %collective-permute-done.6.near2_ref, bf16[128,1024]{1,0:T(8,128)(2,1)S(1)} %collective-permute-done.4.far_ref.refs_1_, ...), custom_call_target="tpu_custom_call" | custom-call | tf_op jit(solution)/shard_map/pallas_call | solution.py:29
  23.3 0.0 collective-permute-done.5.far2_ref
  23.3 0.4 shard_map.80.refs_0_
  23.7 2.8 %collective-permute-start.9 = (bf16[192,256]{1,0:T(8,128)(2,1)S(1)}, bf16[192,256]{1,0:T(8,128)(2,1)S(1)}, u32[]{:S(2)}, u32[]{:S(2)}) collective-permute-start(bf16[192,256]{1,0:T(8,128)(2,1)S(1)} %shard_map.80.refs_0_), channel_id=1, source_target_pairs={{0,3},{1,2},{2,1},{3,0},{4,7},{5,6},{6,5},{7,4},{8,11},{9,10},{10,... | collective-permute-start | bytes 294920 | tf_op jit(solution)/shard_map/ppermute | solution.py:21
  26.5 0.3 collective-permute-start.8
  26.7 0.5 collective-permute-start.7
  27.3 2.5 %collective-permute-done.10.refs_6_ = bf16[208,512]{1,0:T(8,128)(2,1)S(1)} collective-permute-done((bf16[208,512]{1,0:T(8,128)(2,1)S(1)}, bf16[208,512]{1,0:T(8,128)(2,1)S(1)}, u32[]{:S(2)}, u32[]{:S(2)}) %collective-permute-start.10) | collective-permute-done | bytes 213024 | tf_op jit(solution)/shard_map/ppermute | solution.py:21
  29.8 2.4 %collective-permute-done.12.refs_7_ = bf16[208,512]{1,0:T(8,128)(2,1)S(1)} collective-permute-done((bf16[208,512]{1,0:T(8,128)(2,1)S(1)}, bf16[208,512]{1,0:T(8,128)(2,1)S(1)}, u32[]{:S(2)}, u32[]{:S(2)}) %collective-permute-start.12) | collective-permute-done | bytes 213024 | tf_op jit(solution)/shard_map/ppermute | solution.py:21
  32.2 0.0 collective-permute-done.9.refs_3_
  32.2 1.5 %collective-permute-done.8.refs_2_ = bf16[192,256]{1,0:T(8,128)(2,1)S(1)} collective-permute-done((bf16[192,256]{1,0:T(8,128)(2,1)S(1)}, bf16[192,256]{1,0:T(8,128)(2,1)S(1)}, u32[]{:S(2)}, u32[]{:S(2)}) %collective-permute-start.8) | collective-permute-done | bytes 98336 | tf_op jit(solution)/shard_map/ppermute | solution.py:21
  33.7 0.0 collective-permute-done.7.refs_1_
  33.7 1.5 %shard_map.84 = (bf16[64,512]{1,0:T(8,128)(2,1)S(1)}, bf16[64,512]{1,0:T(8,128)(2,1)S(1)}, bf16[64,512]{1,0:T(8,128)(2,1)S(1)}, bf16[64,512]{1,0:T(8,128)(2,1)S(1)}, bf16[512,128]{1,0:T(8,128)(2,1)}) custom-call(bf16[192,256]{1,0:T(8,128)(2,1)S(1)} %shard_map.80.refs_0_, bf16[192,256]{1,0:T(8,128)(2,1)S(1)} %collective-permute-done.7.refs_1_, ...), custom_call_target="tpu_custom_call" | custom-call | tf_op jit(solution)/shard_map/pallas_call | solution.py:29
  35.2 3.1 %all-to-all-start = ((bf16[32,16,128]{2,1,0:T(8,128)(2,1)}), bf16[32,16,128]{2,1,0:T(8,128)(2,1)S(1)}, u32[]{:S(2)}, u32[]{:S(2)}) async-start(bf16[32,16,128]{2,1,0:T(8,128)(2,1)} %bitcast.1), calls=%async_computation | async-start | bytes 262144 | tf_op jit(solution)/shard_map/all_to_all | solution.py:298
  38.3 1.8 %collective-permute-start.13 = (bf16[64,512]{1,0:T(8,128)(2,1)S(1)}, bf16[64,512]{1,0:T(8,128)(2,1)S(1)}, u32[]{:S(2)}, u32[]{:S(2)}) collective-permute-start(bf16[64,512]{1,0:T(8,128)(2,1)S(1)} %get-tuple-element.24), channel_id=1, source_target_pairs={{0,1},{1,0},{2,3},{3,2},{4,5},{5,4},{6,7},{7,6},{8,9},{9,8},{10,11... | collective-permute-start | bytes 196616 | tf_op jit(solution)/shard_map/ppermute | solution.py:21
  40.1 1.5 %collective-permute-start.14 = (bf16[64,512]{1,0:T(8,128)(2,1)S(1)}, bf16[64,512]{1,0:T(8,128)(2,1)S(1)}, u32[]{:S(2)}, u32[]{:S(2)}) collective-permute-start(bf16[64,512]{1,0:T(8,128)(2,1)S(1)} %get-tuple-element.25), channel_id=1, source_target_pairs={{0,2},{1,3},{2,0},{3,1},{4,6},{5,7},{6,4},{7,5},{8,10},{9,11},{10,... | collective-permute-start | bytes 196616 | tf_op jit(solution)/shard_map/ppermute | solution.py:21
  41.6 0.3 collective-permute-start.15
  41.8 4.2 %all-to-all-done = bf16[32,16,128]{2,1,0:T(8,128)(2,1)S(1)} async-done(((bf16[32,16,128]{2,1,0:T(8,128)(2,1)}), bf16[32,16,128]{2,1,0:T(8,128)(2,1)S(1)}, u32[]{:S(2)}, u32[]{:S(2)}) %all-to-all-start) | async-done | bytes 131104 | tf_op jit(solution)/shard_map/all_to_all | solution.py:298
  46.0 0.8 %shard_map.86 = f32[32,8,8]{2,1,0:T(8,128)} custom-call(bf16[8,4,16,128]{3,2,1,0:T(8,128)(2,1)S(1)} %bitcast.3), custom_call_target="tpu_custom_call" | custom-call | tf_op jit(solution)/shard_map/pallas_call | solution.py:29
  46.8 2.6 %all-to-all-start.1 = ((f32[32,8,8]{2,1,0:T(8,128)}), f32[32,8,8]{2,1,0:T(8,128)S(1)}, u32[]{:S(2)}, u32[]{:S(2)}) async-start(f32[32,8,8]{2,1,0:T(8,128)} %shard_map.86), calls=%async_computation.1 | async-start | bytes 262144 | tf_op jit(solution)/shard_map/all_to_all | solution.py:309
  49.4 0.0 collective-permute-done.13.refs_1_
  49.4 0.0 collective-permute-done.14.refs_2_
  49.4 0.0 collective-permute-done.15.refs_3_
  49.4 0.7 %shard_map.85 = bf16[64,2048]{1,0:T(8,128)(2,1)} custom-call(bf16[64,512]{1,0:T(8,128)(2,1)S(1)} %get-tuple-element.23.refs_0_, bf16[64,512]{1,0:T(8,128)(2,1)S(1)} %collective-permute-done.13.refs_1_, bf16[64,512]{1,0:T(8,128)(2,1)S(1)} %collective-permute-done.14.refs_2_, bf16[64,512]{1,0:T(8,128)(2,1)S(1)} %collective-permute-done.15.refs_3_), custom_call_target="tpu_custom_call" | custom-call | tf_op jit(solution)/shard_map/pallas_call | solution.py:29
  50.2 7.0 %all-to-all-done.1.tables_ref = f32[32,8,8]{2,1,0:T(8,128)S(1)} async-done(((f32[32,8,8]{2,1,0:T(8,128)}), f32[32,8,8]{2,1,0:T(8,128)S(1)}, u32[]{:S(2)}, u32[]{:S(2)}) %all-to-all-start.1) | async-done | bytes 8224 | tf_op jit(solution)/shard_map/all_to_all | solution.py:309
  57.1 0.7 %shard_map.87 = f32[8,8]{1,0:T(8,128)} custom-call(f32[32,8,8]{2,1,0:T(8,128)S(1)} %all-to-all-done.1.tables_ref), custom_call_target="tpu_custom_call" | custom-call | tf_op jit(solution)/shard_map/pallas_call | solution.py:29
  (4 shorter events, 0.0 us)
Async XLA Ops:
  2.0 12.0 %collective-permute-start = (bf16[208,512]{1,0:T(8,128)(2,1)S(1)}, bf16[208,512]{1,0:T(8,128)(2,1)S(1)}, u32[]{:S(2)}, u32[]{:S(2)}) collective-permute-start(bf16[208,512]{1,0:T(8,128)(2,1)S(1)} %get-tuple-element.15), channel_id=1, source_target_pairs={{0,1},{1,0},{2,3},{3,2},{4,5},{5,4},{6,7},{7,6},{8,9},{9,8},{10,11... | collective-permute-start | bytes 638984 | tf_op jit(solution)/shard_map/ppermute | solution.py:21
  5.0 6.9 %collective-permute-start.3 = (bf16[32,1024]{1,0:T(8,128)(2,1)S(1)}, bf16[32,1024]{1,0:T(8,128)(2,1)S(1)}, u32[]{:S(2)}, u32[]{:S(2)}) collective-permute-start(bf16[32,1024]{1,0:T(8,128)(2,1)S(1)} %get-tuple-element.16.refs_0_), channel_id=1, source_target_pairs={{0,6},{1,7},{2,4},{3,5},{4,2},{5,3},{6,0},{7,1},{8,14},{9,15},{10,... | collective-permute-start | bytes 196616 | tf_op jit(solution)/shard_map/ppermute | solution.py:21
  8.6 5.4 %collective-permute-start.2 = (bf16[32,1024]{1,0:T(8,128)(2,1)S(1)}, bf16[32,1024]{1,0:T(8,128)(2,1)S(1)}, u32[]{:S(2)}, u32[]{:S(2)}) collective-permute-start(bf16[32,1024]{1,0:T(8,128)(2,1)S(1)} %get-tuple-element.16.refs_0_), channel_id=1, source_target_pairs={{0,4},{1,5},{2,6},{3,7},{4,0},{5,1},{6,2},{7,3},{8,12},{9,13},{10,... | collective-permute-start | bytes 196616 | tf_op jit(solution)/shard_map/ppermute | solution.py:21
  8.6 5.4 %collective-permute-start.1 = (bf16[32,1024]{1,0:T(8,128)(2,1)S(1)}, bf16[32,1024]{1,0:T(8,128)(2,1)S(1)}, u32[]{:S(2)}, u32[]{:S(2)}) collective-permute-start(bf16[32,1024]{1,0:T(8,128)(2,1)S(1)} %get-tuple-element.16.refs_0_), channel_id=1, source_target_pairs={{0,2},{1,3},{2,0},{3,1},{4,6},{5,7},{6,4},{7,5},{8,10},{9,11},{10,... | collective-permute-start | bytes 196616 | tf_op jit(solution)/shard_map/ppermute | solution.py:21
  14.1 7.7 %collective-permute-start.4 = (bf16[128,1024]{1,0:T(8,128)(2,1)S(1)}, bf16[128,1024]{1,0:T(8,128)(2,1)S(1)}, u32[]{:S(2)}, u32[]{:S(2)}) collective-permute-start(bf16[128,1024]{1,0:T(8,128)(2,1)S(1)} %shard_map.78.near_ref.refs_1_), channel_id=1, source_target_pairs={{0,1},{1,0},{2,3},{3,2},{4,5},{5,4},{6,7},{7,6},{8,9},{9,8},{10,11... | collective-permute-start | bytes 786440 | tf_op jit(solution)/shard_map/ppermute | solution.py:21
  14.6 8.0 %copy-start.1 = (bf16[192,2048]{1,0:T(8,128)(2,1)S(1)}, bf16[192,2048]{1,0:T(8,128)(2,1)}, u32[]{:S(2)}) copy-start(bf16[192,2048]{1,0:T(8,128)(2,1)} %up_ref.3) | copy-start | bytes 2359300
  14.6 8.0 %copy-start = (bf16[192,2048]{1,0:T(8,128)(2,1)S(1)}, bf16[192,2048]{1,0:T(8,128)(2,1)}, u32[]{:S(2)}) copy-start(bf16[192,2048]{1,0:T(8,128)(2,1)} %gate_ref.3) | copy-start | bytes 2359300
  14.6 7.4 %collective-permute-start.11 = (bf16[208,512]{1,0:T(8,128)(2,1)S(1)}, bf16[208,512]{1,0:T(8,128)(2,1)S(1)}, u32[]{:S(2)}, u32[]{:S(2)}) collective-permute-start(bf16[208,512]{1,0:T(8,128)(2,1)S(1)} %shard_map.82), channel_id=1, source_target_pairs={{0,2},{1,3},{2,0},{3,1},{4,6},{5,7},{6,4},{7,5},{8,10},{9,11},{10,... | collective-permute-start | bytes 638984 | tf_op jit(solution)/shard_map/ppermute | solution.py:21
  15.6 6.9 %collective-permute-start.6 = (bf16[128,1024]{1,0:T(8,128)(2,1)S(1)}, bf16[128,1024]{1,0:T(8,128)(2,1)S(1)}, u32[]{:S(2)}, u32[]{:S(2)}) collective-permute-start(bf16[128,1024]{1,0:T(8,128)(2,1)S(1)} %shard_map.78.near_ref.refs_1_), channel_id=1, source_target_pairs={{0,8},{8,0},{16,24},{24,16},{1,9},{9,1},{17,25},{25,17},{2,10},{10... | collective-permute-start | bytes 786440 | tf_op jit(solution)/shard_map/ppermute | solution.py:21
  21.7 1.6 %collective-permute-start.5 = (bf16[128,1024]{1,0:T(8,128)(2,1)S(1)}, bf16[128,1024]{1,0:T(8,128)(2,1)S(1)}, u32[]{:S(2)}, u32[]{:S(2)}) collective-permute-start(bf16[128,1024]{1,0:T(8,128)(2,1)S(1)} %collective-permute-done.4.far_ref.refs_1_), channel_id=1, source_target_pairs={{0,8},{8,0},{16,24},{24,16},{1,9},{9,1},{17,25},{25,17},{2,10},{10... | collective-permute-start | bytes 786440 | tf_op jit(solution)/shard_map/ppermute | solution.py:21
  21.7 8.0 %collective-permute-start.10 = (bf16[208,512]{1,0:T(8,128)(2,1)S(1)}, bf16[208,512]{1,0:T(8,128)(2,1)S(1)}, u32[]{:S(2)}, u32[]{:S(2)}) collective-permute-start(bf16[208,512]{1,0:T(8,128)(2,1)S(1)} %shard_map.81), channel_id=1, source_target_pairs={{0,2},{1,3},{2,0},{3,1},{4,6},{5,7},{6,4},{7,5},{8,10},{9,11},{10,... | collective-permute-start | bytes 638984 | tf_op jit(solution)/shard_map/ppermute | solution.py:21
  22.0 10.2 %collective-permute-start.12 = (bf16[208,512]{1,0:T(8,128)(2,1)S(1)}, bf16[208,512]{1,0:T(8,128)(2,1)S(1)}, u32[]{:S(2)}, u32[]{:S(2)}) collective-permute-start(bf16[208,512]{1,0:T(8,128)(2,1)S(1)} %shard_map.83), channel_id=1, source_target_pairs={{0,1},{1,0},{2,3},{3,2},{4,5},{5,4},{6,7},{7,6},{8,9},{9,8},{10,11... | collective-permute-start | bytes 638984 | tf_op jit(solution)/shard_map/ppermute | solution.py:21
  23.7 8.5 %collective-permute-start.9 = (bf16[192,256]{1,0:T(8,128)(2,1)S(1)}, bf16[192,256]{1,0:T(8,128)(2,1)S(1)}, u32[]{:S(2)}, u32[]{:S(2)}) collective-permute-start(bf16[192,256]{1,0:T(8,128)(2,1)S(1)} %shard_map.80.refs_0_), channel_id=1, source_target_pairs={{0,3},{1,2},{2,1},{3,0},{4,7},{5,6},{6,5},{7,4},{8,11},{9,10},{10,... | collective-permute-start | bytes 294920 | tf_op jit(solution)/shard_map/ppermute | solution.py:21
  26.5 7.2 %collective-permute-start.8 = (bf16[192,256]{1,0:T(8,128)(2,1)S(1)}, bf16[192,256]{1,0:T(8,128)(2,1)S(1)}, u32[]{:S(2)}, u32[]{:S(2)}) collective-permute-start(bf16[192,256]{1,0:T(8,128)(2,1)S(1)} %shard_map.80.refs_0_), channel_id=1, source_target_pairs={{0,2},{1,3},{2,0},{3,1},{4,6},{5,7},{6,4},{7,5},{8,10},{9,11},{10,... | collective-permute-start | bytes 294920 | tf_op jit(solution)/shard_map/ppermute | solution.py:21
  26.7 6.9 %collective-permute-start.7 = (bf16[192,256]{1,0:T(8,128)(2,1)S(1)}, bf16[192,256]{1,0:T(8,128)(2,1)S(1)}, u32[]{:S(2)}, u32[]{:S(2)}) collective-permute-start(bf16[192,256]{1,0:T(8,128)(2,1)S(1)} %shard_map.80.refs_0_), channel_id=1, source_target_pairs={{0,1},{1,0},{2,3},{3,2},{4,5},{5,4},{6,7},{7,6},{8,9},{9,8},{10,11... | collective-permute-start | bytes 294920 | tf_op jit(solution)/shard_map/ppermute | solution.py:21
  35.2 10.9 %all-to-all-start = ((bf16[32,16,128]{2,1,0:T(8,128)(2,1)}), bf16[32,16,128]{2,1,0:T(8,128)(2,1)S(1)}, u32[]{:S(2)}, u32[]{:S(2)}) async-start(bf16[32,16,128]{2,1,0:T(8,128)(2,1)} %bitcast.1), calls=%async_computation | async-start | bytes 262144 | tf_op jit(solution)/shard_map/all_to_all | solution.py:298
  38.3 11.1 %collective-permute-start.13 = (bf16[64,512]{1,0:T(8,128)(2,1)S(1)}, bf16[64,512]{1,0:T(8,128)(2,1)S(1)}, u32[]{:S(2)}, u32[]{:S(2)}) collective-permute-start(bf16[64,512]{1,0:T(8,128)(2,1)S(1)} %get-tuple-element.24), channel_id=1, source_target_pairs={{0,1},{1,0},{2,3},{3,2},{4,5},{5,4},{6,7},{7,6},{8,9},{9,8},{10,11... | collective-permute-start | bytes 196616 | tf_op jit(solution)/shard_map/ppermute | solution.py:21
  40.1 9.3 %collective-permute-start.14 = (bf16[64,512]{1,0:T(8,128)(2,1)S(1)}, bf16[64,512]{1,0:T(8,128)(2,1)S(1)}, u32[]{:S(2)}, u32[]{:S(2)}) collective-permute-start(bf16[64,512]{1,0:T(8,128)(2,1)S(1)} %get-tuple-element.25), channel_id=1, source_target_pairs={{0,2},{1,3},{2,0},{3,1},{4,6},{5,7},{6,4},{7,5},{8,10},{9,11},{10,... | collective-permute-start | bytes 196616 | tf_op jit(solution)/shard_map/ppermute | solution.py:21
  41.6 7.8 %collective-permute-start.15 = (bf16[64,512]{1,0:T(8,128)(2,1)S(1)}, bf16[64,512]{1,0:T(8,128)(2,1)S(1)}, u32[]{:S(2)}, u32[]{:S(2)}) collective-permute-start(bf16[64,512]{1,0:T(8,128)(2,1)S(1)} %get-tuple-element.26), channel_id=1, source_target_pairs={{0,3},{1,2},{2,1},{3,0},{4,7},{5,6},{6,5},{7,4},{8,11},{9,10},{10,... | collective-permute-start | bytes 196616 | tf_op jit(solution)/shard_map/ppermute | solution.py:21
  46.8 10.3 %all-to-all-start.1 = ((f32[32,8,8]{2,1,0:T(8,128)}), f32[32,8,8]{2,1,0:T(8,128)S(1)}, u32[]{:S(2)}, u32[]{:S(2)}) async-start(f32[32,8,8]{2,1,0:T(8,128)} %shard_map.86), calls=%async_computation.1 | async-start | bytes 262144 | tf_op jit(solution)/shard_map/all_to_all | solution.py:309

commit v13 on v12

--- a/solution.py
+++ b/solution.py
@@ -46,13 +46,14 @@
 
 
 def first_kernel(states_hbm, gain_hbm, down_hbm, route_hbm, out_ref, *refs):
-    downs, (states_ref, gain_ref, route_ref, sems) = refs[:HOLDERS], refs[HOLDERS:]
+    kept_ref, z_ref, x_ref, states_ref, gain_ref, route_ref, sems = refs
+    depth, width = down_hbm.shape[0], kept_ref.shape[1]
+    downs = (kept_ref, x_ref.at[pl.ds(0, depth + TILE)], z_ref, x_ref.at[pl.ds(depth + TILE, depth + TILE)])
     copies = [
         pltpu.make_async_copy(states_hbm, states_ref, sems.at[0]),
         pltpu.make_async_copy(gain_hbm, gain_ref, sems.at[1]),
         pltpu.make_async_copy(route_hbm, route_ref, sems.at[2]),
     ]
-    depth, width = down_hbm.shape[0], downs[0].shape[1]
     for m, down_ref in enumerate(downs):
         columns = pl.ds(pl.multiple_of((holder() ^ m) * width, width), width)
         copies.append(
@@ -76,26 +77,17 @@
     part = route.shape[1]
     row = lax.broadcasted_iota(jnp.int32, (TILE, part), 0)
     terms = jnp.where(row == 0, high, jnp.where(row == 1, middle, jnp.where(row == 2, low, 0.0)))
-    terms = jnp.concatenate([terms, jnp.zeros((TILE, downs[0].shape[1] - part), f32)], 1)
+    terms = jnp.concatenate([terms, jnp.zeros((TILE, kept_ref.shape[1] - part), f32)], 1)
     for down_ref in downs:
-        down_ref[depth:] = terms.astype(bf16)
+        down_ref[pl.ds(depth, TILE)] = terms.astype(bf16)
     for copy in copies[3:]:
         copy.wait()
 
 
-def hold_kernel(*refs):
-    pass
-
-
-def held(array, after):
-    return call(
-        hold_kernel,
-        jax.ShapeDtypeStruct(array.shape, array.dtype),
-        [ANY] * 2,
-        (array, after),
-        out_specs=ANY,
-        aliases={0: 0},
-    )
+def onward_kernel(after_ref, own_ref, got_ref, out_ref):
+    count = own_ref.shape[0]
+    out_ref[:count] = own_ref[...]
+    out_ref[count:] = got_ref[count:]
 
 
 def stack_kernel(after_ref, *refs):
@@ -126,7 +118,7 @@
     up_part_ref[...] = dot_f32(up_ref[:, own], far, TRANSPOSED)
 
 
-def far_kernel(far2_ref, gate_ref, up_ref, near_hidden_ref, gate_part_ref, up_part_ref, out_ref):
+def far_kernel(after_ref, far2_ref, gate_ref, up_ref, near_hidden_ref, gate_part_ref, up_part_ref, out_ref):
     count, width = far2_ref.shape
     rest = columns_of(1 - core(), width)
     far2 = far2_ref[...]
@@ -140,10 +132,12 @@
 
 
 def features_kernel(*refs):
-    hidden_refs, down_refs = refs[:HOLDERS], refs[HOLDERS : 2 * HOLDERS]
-    block_refs, shares_hbm = refs[2 * HOLDERS : 3 * HOLDERS], refs[3 * HOLDERS]
-    route_ref, features_ref, whole_ref, shares_ref, sem = refs[3 * HOLDERS + 1 :]
+    hidden_refs, (kept_ref, x_ref, z_ref) = refs[:HOLDERS], refs[HOLDERS : HOLDERS + 3]
+    block_refs, shares_hbm = refs[HOLDERS + 3 : 2 * HOLDERS + 3], refs[2 * HOLDERS + 3]
+    route_ref, features_ref, whole_ref, shares_ref, sem = refs[2 * HOLDERS + 4 :]
     depth, tokens = hidden_refs[0].shape
+    count = kept_ref.shape[0]
+    downs = (kept_ref[...], x_ref[:count], z_ref[:count], z_ref[count:])
     part, members = tokens // HOLDERS, lax.axis_size("tok")
     rows = tokens // members
 
@@ -155,10 +149,10 @@
         jnp.int32, (part, part), 1
     )
     output = None
-    for m, (hidden_ref, down_ref) in enumerate(zip(hidden_refs, down_refs)):
-        product = dot_f32(hidden_ref[...], down_ref[:depth], (((0,), (0,)), ((), ())))
+    for m, (hidden_ref, down) in enumerate(zip(hidden_refs, downs)):
+        product = dot_f32(hidden_ref[...], down[:depth], (((0,), (0,)), ((), ())))
         output = product if output is None else output + product
-        terms = down_ref[depth:, :part].astype(f32)
+        terms = down[depth:, :part].astype(f32)
         route = jnp.sum(terms[:HOLDERS], axis=0, keepdims=True)
         column = jnp.sum(jnp.where(eye, route, 0.0), axis=1, keepdims=True)
         column = jnp.broadcast_to(column, (part, LANES))
@@ -236,10 +230,10 @@
     depth = gate_weight.shape[0]
     part, token_part = model // HOLDERS, tokens // HOLDERS
 
-    own, *downs = call(
+    own, down_own, down_z, down_x = call(
         first_kernel,
         [jax.ShapeDtypeStruct((rows, model // 2), bf16)]
-        + [jax.ShapeDtypeStruct((depth + TILE, part), bf16)] * HOLDERS,
+        + [jax.ShapeDtypeStruct(((depth + TILE) * n, part), bf16) for n in (1, 1, 2)],
         [HBM] * 4,
         [
             pltpu.with_memory_space_constraint(a, pltpu.HBM)
@@ -252,7 +246,7 @@
             pltpu.SemaphoreType.DMA((3 + HOLDERS,)),
         ],
     )
-    down_x = swapped(downs[1], "tok", 1)
+    down_x = swapped(down_x, "tok", 1)
     pieces = [swapped(own, "tok", 2 * m) if m else own for m in range(members // 2)]
     near = call(
         stack_kernel,
@@ -262,8 +256,13 @@
     )
     far = swapped(near, "tok", 1)
     near2 = swapped(near, "grp", 1)
-    down_xz = swapped(held(downs[3], near), "tok", 2)
-    down_z = swapped(held(downs[2], near), "tok", 2)
+    down_z = call(
+        onward_kernel,
+        jax.ShapeDtypeStruct(down_x.shape, bf16),
+        [ANY, VMEM, VMEM],
+        (near, down_z, down_x),
+    )
+    down_z = swapped(down_z, "tok", 2)
     half_shape = (depth, tokens // 2)
     near_hidden, gate_part, up_part = call(
         near_kernel,
@@ -271,12 +270,11 @@
         [VMEM] * 5,
         (near, near2, far, gate_weight, up_weight),
     )
-    down_xz = swapped(held(down_xz, far), "tok", 1)
     hidden = call(
         far_kernel,
         jax.ShapeDtypeStruct((depth, tokens), bf16),
-        [VMEM] * 6,
-        (swapped(far, "grp", 1), gate_weight, up_weight, near_hidden, gate_part, up_part),
+        [ANY] + [VMEM] * 6,
+        (down_z, swapped(far, "grp", 1), gate_weight, up_weight, near_hidden, gate_part, up_part),
     )
     hiddens = [swapped(hidden, "tok", m) if m else hidden for m in range(HOLDERS)]
     entries = tokens * tokens // LANES
@@ -284,8 +282,8 @@
         features_kernel,
         [jax.ShapeDtypeStruct((token_part, part), bf16)] * HOLDERS
         + [jax.ShapeDtypeStruct((entries, LANES), bf16)],
-        [VMEM] * (2 * HOLDERS),
-        (*hiddens, downs[0], down_x, down_z, down_xz),
+        [VMEM] * (HOLDERS + 3),
+        (*hiddens, down_own, down_x, down_z),
         out_specs=[VMEM] * HOLDERS + [HBM],
         scratch=[
             pltpu.VMEM((tokens, LANES), f32),

time: 58.1 us -> 60.5 us (1.041)
  starting transfers between devices: 22.6 us -> 24 us
  waiting for transfers between devices: 28.3 us -> 29.2 us
    ppermute x16 -> x14, waiting for transfers between devices: 17.2 us -> 18.1 us  [swapped(): lax.ppermute(array, axis, [(i, i ^ mask) for i in range(lax.axis_size(axi...]
    all_to_all x1, starting transfers between devices: 3.13 us -> 3.93 us  [shards(): lax.all_to_all(centered, ('grp', 'tok'), split_axis=0, concat_axis=0, til...]
    ppermute x16 -> x14, starting transfers between devices: 16.9 us -> 17.5 us  [swapped(): lax.ppermute(array, axis, [(i, i ^ mask) for i in range(lax.axis_size(axi...]
    pallas_call x11 -> x9, Pallas kernels: 6.23 us -> 6.25 us  [call(): pl.pallas_call(body, out_shape=outs, in_specs=in_specs, out_specs=jax.tre...]
  transfers between devices with their start and end apart: 18 -> 16, of which waited for: 9 -> 9; matrix products, arithmetic and copies ran while one was open for 0% -> 0% of each run, Pallas kernels for 5% -> 4%
where the time goes in v13:
time: 60.5 us; the launch traced here: 60.2 us
  waiting for transfers between devices  29.2 us (48%)
  starting transfers between devices  24 us (40%)
  Pallas kernels  6.25 us (10%)
  between operations  0.75 us (1%)
    ppermute x14, waiting for transfers between devices, swapped(): lax.ppermute(array, axis, [(i, i ^ mask) for i in range(lax.axis_size(axi...  18.1 us
    ppermute x14, starting transfers between devices, swapped(): lax.ppermute(array, axis, [(i, i ^ mask) for i in range(lax.axis_size(axi...  17.5 us
    all_to_all x1, waiting for transfers between devices, shards(): lax.all_to_all(tables, ('grp', 'tok'), split_axis=0, concat_axis=0, tiled...  6.96 us
    pallas_call x9, Pallas kernels, call(): pl.pallas_call(body, out_shape=outs, in_specs=in_specs, out_specs=jax.tre...  6.25 us
    all_to_all x1, waiting for transfers between devices, shards(): lax.all_to_all(centered, ('grp', 'tok'), split_axis=0, concat_axis=0, til...  4.19 us
    all_to_all x1, starting transfers between devices, shards(): lax.all_to_all(centered, ('grp', 'tok'), split_axis=0, concat_axis=0, til...  3.93 us
    all_to_all x1, starting transfers between devices, shards(): lax.all_to_all(tables, ('grp', 'tok'), split_axis=0, concat_axis=0, tiled...  2.56 us
  transfers between devices with their start and end apart: 16, of which 9 were waited for; matrix products, arithmetic and copies ran while one was open for 0% of the time, Pallas kernels for 4%

profile of v13, /device:TPU:0, one launch (start us, length us, event | category | flops | bytes accessed | tf_op | source)
XLA Modules:
  0.0 60.2 jit_solution(15611623339891002588)
XLA Ops:
  0.6 1.3 %shard_map.77 = (bf16[32,1024]{1,0:T(8,128)(2,1)S(1)}, bf16[208,512]{1,0:T(8,128)(2,1)S(1)}, bf16[208,512]{1,0:T(8,128)(2,1)S(1)}, bf16[416,512]{1,0:T(8,128)(2,1)S(1)}) custom-call(bf16[32,2048]{1,0:T(8,128)(2,1)} %states_hbm.1, f32[1,2048]{1,0:T(1,128)} %bitcast.4, bf16[192,2048]{1,0:T(8,128)(2,1)} %down_hbm.1, f32[1,64]{1,0:T(1,128)} %route_hbm.1), custom_call_target="tpu_custom_call" | custom-call | tf_op jit(solution)/shard_map/pallas_call | solution.py:29
  2.0 3.0 %collective-permute-start = (bf16[416,512]{1,0:T(8,128)(2,1)S(1)}, bf16[416,512]{1,0:T(8,128)(2,1)S(1)}, u32[]{:S(2)}, u32[]{:S(2)}) collective-permute-start(bf16[416,512]{1,0:T(8,128)(2,1)S(1)} %get-tuple-element.14), channel_id=1, source_target_pairs={{0,1},{1,0},{2,3},{3,2},{4,5},{5,4},{6,7},{7,6},{8,9},{9,8},{10,11... | collective-permute-start | bytes 1277960 | tf_op jit(solution)/shard_map/ppermute | solution.py:21
  5.0 1.6 %collective-permute-start.1 = (bf16[32,1024]{1,0:T(8,128)(2,1)S(1)}, bf16[32,1024]{1,0:T(8,128)(2,1)S(1)}, u32[]{:S(2)}, u32[]{:S(2)}) collective-permute-start(bf16[32,1024]{1,0:T(8,128)(2,1)S(1)} %get-tuple-element.15.refs_0_), channel_id=1, source_target_pairs={{0,2},{1,3},{2,0},{3,1},{4,6},{5,7},{6,4},{7,5},{8,10},{9,11},{10,... | collective-permute-start | bytes 196616 | tf_op jit(solution)/shard_map/ppermute | solution.py:21
  6.6 2.6 %collective-permute-start.2 = (bf16[32,1024]{1,0:T(8,128)(2,1)S(1)}, bf16[32,1024]{1,0:T(8,128)(2,1)S(1)}, u32[]{:S(2)}, u32[]{:S(2)}) collective-permute-start(bf16[32,1024]{1,0:T(8,128)(2,1)S(1)} %get-tuple-element.15.refs_0_), channel_id=1, source_target_pairs={{0,4},{1,5},{2,6},{3,7},{4,0},{5,1},{6,2},{7,3},{8,12},{9,13},{10,... | collective-permute-start | bytes 196616 | tf_op jit(solution)/shard_map/ppermute | solution.py:21
  9.2 0.2 collective-permute-start.3
  9.4 0.0 collective-permute-done.1.refs_1_
  9.4 4.2 %collective-permute-done.2.refs_2_ = bf16[32,1024]{1,0:T(8,128)(2,1)S(1)} collective-permute-done((bf16[32,1024]{1,0:T(8,128)(2,1)S(1)}, bf16[32,1024]{1,0:T(8,128)(2,1)S(1)}, u32[]{:S(2)}, u32[]{:S(2)}) %collective-permute-start.2) | collective-permute-done | bytes 65568 | tf_op jit(solution)/shard_map/ppermute | solution.py:21
  13.5 1.7 %collective-permute-done.3.refs_3_ = bf16[32,1024]{1,0:T(8,128)(2,1)S(1)} collective-permute-done((bf16[32,1024]{1,0:T(8,128)(2,1)S(1)}, bf16[32,1024]{1,0:T(8,128)(2,1)S(1)}, u32[]{:S(2)}, u32[]{:S(2)}) %collective-permute-start.3) | collective-permute-done | bytes 65568 | tf_op jit(solution)/shard_map/ppermute | solution.py:21
  15.2 0.0 collective-permute-done.after_ref.got_ref.refs_5_
  15.2 0.0 copy-start.1
  15.3 0.0 copy-start
  15.3 1.4 %collective-permute-start.5 = (bf16[128,1024]{1,0:T(8,128)(2,1)S(1)}, bf16[128,1024]{1,0:T(8,128)(2,1)S(1)}, u32[]{:S(2)}, u32[]{:S(2)}) collective-permute-start(bf16[128,1024]{1,0:T(8,128)(2,1)S(1)} %shard_map.78.after_ref.near_ref), channel_id=1, source_target_pairs={{0,1},{1,0},{2,3},{3,2},{4,5},{5,4},{6,7},{7,6},{8,9},{9,8},{10,11... | collective-permute-start | bytes 786440 | tf_op jit(solution)/shard_map/ppermute | solution.py:21
  16.7 1.6 %collective-permute-start.4 = (bf16[416,512]{1,0:T(8,128)(2,1)S(1)}, bf16[416,512]{1,0:T(8,128)(2,1)S(1)}, u32[]{:S(2)}, u32[]{:S(2)}) collective-permute-start(bf16[416,512]{1,0:T(8,128)(2,1)S(1)} %shard_map.79), channel_id=1, source_target_pairs={{0,2},{1,3},{2,0},{3,1},{4,6},{5,7},{6,4},{7,5},{8,10},{9,11},{10,... | collective-permute-start | bytes 1277960 | tf_op jit(solution)/shard_map/ppermute | solution.py:21
  18.3 0.0 collective-permute-start.7
  18.3 4.1 %collective-permute-done.5.far_ref = bf16[128,1024]{1,0:T(8,128)(2,1)S(1)} collective-permute-done((bf16[128,1024]{1,0:T(8,128)(2,1)S(1)}, bf16[128,1024]{1,0:T(8,128)(2,1)S(1)}, u32[]{:S(2)}, u32[]{:S(2)}) %collective-permute-start.5) | collective-permute-done | bytes 262176 | tf_op jit(solution)/shard_map/ppermute | solution.py:21
  22.4 0.0 collective-permute-start.6
  22.4 0.0 collective-permute-done.7.near2_ref
  22.4 0.0 copy-done.1
  22.4 0.0 copy-done
  22.4 0.8 %shard_map.80 = (bf16[192,128]{1,0:T(8,128)(2,1)S(1)}, f32[192,128]{1,0:T(8,128)S(1)}, f32[192,128]{1,0:T(8,128)S(1)}) custom-call(bf16[128,1024]{1,0:T(8,128)(2,1)S(1)} %shard_map.78.after_ref.near_ref, bf16[128,1024]{1,0:T(8,128)(2,1)S(1)} %collective-permute-done.7.near2_ref, bf16[128,1024]{1,0:T(8,128)(2,1)S(1)} %collective-permute-done.5.far_ref, ...), custom_call_target="tpu_custom_call" | custom-call | tf_op jit(solution)/shard_map/pallas_call | solution.py:29
  23.2 4.0 %collective-permute-done.4.after_ref.refs_6_ = bf16[416,512]{1,0:T(8,128)(2,1)S(1)} collective-permute-done((bf16[416,512]{1,0:T(8,128)(2,1)S(1)}, bf16[416,512]{1,0:T(8,128)(2,1)S(1)}, u32[]{:S(2)}, u32[]{:S(2)}) %collective-permute-start.4) | collective-permute-done | bytes 426016 | tf_op jit(solution)/shard_map/ppermute | solution.py:21
  27.2 0.0 collective-permute-done.6.far2_ref
  27.2 0.4 shard_map.81.refs_0_
  27.5 1.6 %collective-permute-start.10 = (bf16[192,256]{1,0:T(8,128)(2,1)S(1)}, bf16[192,256]{1,0:T(8,128)(2,1)S(1)}, u32[]{:S(2)}, u32[]{:S(2)}) collective-permute-start(bf16[192,256]{1,0:T(8,128)(2,1)S(1)} %shard_map.81.refs_0_), channel_id=1, source_target_pairs={{0,3},{1,2},{2,1},{3,0},{4,7},{5,6},{6,5},{7,4},{8,11},{9,10},{10,... | collective-permute-start | bytes 294920 | tf_op jit(solution)/shard_map/ppermute | solution.py:21
  29.1 1.5 %collective-permute-start.8 = (bf16[192,256]{1,0:T(8,128)(2,1)S(1)}, bf16[192,256]{1,0:T(8,128)(2,1)S(1)}, u32[]{:S(2)}, u32[]{:S(2)}) collective-permute-start(bf16[192,256]{1,0:T(8,128)(2,1)S(1)} %shard_map.81.refs_0_), channel_id=1, source_target_pairs={{0,1},{1,0},{2,3},{3,2},{4,5},{5,4},{6,7},{7,6},{8,9},{9,8},{10,11... | collective-permute-start | bytes 294920 | tf_op jit(solution)/shard_map/ppermute | solution.py:21
  30.6 0.4 collective-permute-start.9
  31.1 2.1 %collective-permute-done.10.refs_3_ = bf16[192,256]{1,0:T(8,128)(2,1)S(1)} collective-permute-done((bf16[192,256]{1,0:T(8,128)(2,1)S(1)}, bf16[192,256]{1,0:T(8,128)(2,1)S(1)}, u32[]{:S(2)}, u32[]{:S(2)}) %collective-permute-start.10) | collective-permute-done | bytes 98336 | tf_op jit(solution)/shard_map/ppermute | solution.py:21
  33.2 1.0 %collective-permute-done.8.refs_1_ = bf16[192,256]{1,0:T(8,128)(2,1)S(1)} collective-permute-done((bf16[192,256]{1,0:T(8,128)(2,1)S(1)}, bf16[192,256]{1,0:T(8,128)(2,1)S(1)}, u32[]{:S(2)}, u32[]{:S(2)}) %collective-permute-start.8) | collective-permute-done | bytes 98336 | tf_op jit(solution)/shard_map/ppermute | solution.py:21
  34.2 1.1 %collective-permute-done.9.refs_2_ = bf16[192,256]{1,0:T(8,128)(2,1)S(1)} collective-permute-done((bf16[192,256]{1,0:T(8,128)(2,1)S(1)}, bf16[192,256]{1,0:T(8,128)(2,1)S(1)}, u32[]{:S(2)}, u32[]{:S(2)}) %collective-permute-start.9) | collective-permute-done | bytes 98336 | tf_op jit(solution)/shard_map/ppermute | solution.py:21
  35.3 1.5 %shard_map.82 = (bf16[64,512]{1,0:T(8,128)(2,1)S(1)}, bf16[64,512]{1,0:T(8,128)(2,1)S(1)}, bf16[64,512]{1,0:T(8,128)(2,1)S(1)}, bf16[64,512]{1,0:T(8,128)(2,1)S(1)}, bf16[512,128]{1,0:T(8,128)(2,1)}) custom-call(bf16[192,256]{1,0:T(8,128)(2,1)S(1)} %shard_map.81.refs_0_, bf16[192,256]{1,0:T(8,128)(2,1)S(1)} %collective-permute-done.8.refs_1_, ...), custom_call_target="tpu_custom_call" | custom-call | tf_op jit(solution)/shard_map/pallas_call | solution.py:29
  36.7 3.9 %all-to-all-start = ((bf16[32,16,128]{2,1,0:T(8,128)(2,1)}), bf16[32,16,128]{2,1,0:T(8,128)(2,1)S(1)}, u32[]{:S(2)}, u32[]{:S(2)}) async-start(bf16[32,16,128]{2,1,0:T(8,128)(2,1)} %bitcast.1), calls=%async_computation | async-start | bytes 262144 | tf_op jit(solution)/shard_map/all_to_all | solution.py:296
  40.7 1.8 %collective-permute-start.11 = (bf16[64,512]{1,0:T(8,128)(2,1)S(1)}, bf16[64,512]{1,0:T(8,128)(2,1)S(1)}, u32[]{:S(2)}, u32[]{:S(2)}) collective-permute-start(bf16[64,512]{1,0:T(8,128)(2,1)S(1)} %get-tuple-element.22), channel_id=1, source_target_pairs={{0,1},{1,0},{2,3},{3,2},{4,5},{5,4},{6,7},{7,6},{8,9},{9,8},{10,11... | collective-permute-start | bytes 196616 | tf_op jit(solution)/shard_map/ppermute | solution.py:21
  42.5 1.5 %collective-permute-start.12 = (bf16[64,512]{1,0:T(8,128)(2,1)S(1)}, bf16[64,512]{1,0:T(8,128)(2,1)S(1)}, u32[]{:S(2)}, u32[]{:S(2)}) collective-permute-start(bf16[64,512]{1,0:T(8,128)(2,1)S(1)} %get-tuple-element.23), channel_id=1, source_target_pairs={{0,2},{1,3},{2,0},{3,1},{4,6},{5,7},{6,4},{7,5},{8,10},{9,11},{10,... | collective-permute-start | bytes 196616 | tf_op jit(solution)/shard_map/ppermute | solution.py:21
  44.0 0.3 collective-permute-start.13
  44.2 4.2 %all-to-all-done = bf16[32,16,128]{2,1,0:T(8,128)(2,1)S(1)} async-done(((bf16[32,16,128]{2,1,0:T(8,128)(2,1)}), bf16[32,16,128]{2,1,0:T(8,128)(2,1)S(1)}, u32[]{:S(2)}, u32[]{:S(2)}) %all-to-all-start) | async-done | bytes 131104 | tf_op jit(solution)/shard_map/all_to_all | solution.py:296
  48.4 0.8 %shard_map.84 = f32[32,8,8]{2,1,0:T(8,128)} custom-call(bf16[8,4,16,128]{3,2,1,0:T(8,128)(2,1)S(1)} %bitcast.3), custom_call_target="tpu_custom_call" | custom-call | tf_op jit(solution)/shard_map/pallas_call | solution.py:29
  49.2 2.6 %all-to-all-start.1 = ((f32[32,8,8]{2,1,0:T(8,128)}), f32[32,8,8]{2,1,0:T(8,128)S(1)}, u32[]{:S(2)}, u32[]{:S(2)}) async-start(f32[32,8,8]{2,1,0:T(8,128)} %shard_map.84), calls=%async_computation.1 | async-start | bytes 262144 | tf_op jit(solution)/shard_map/all_to_all | solution.py:307
  51.8 0.0 collective-permute-done.11.refs_1_
  51.8 0.0 collective-permute-done.12.refs_2_
  51.8 0.0 collective-permute-done.13.refs_3_
  51.8 0.7 %shard_map.83 = bf16[64,2048]{1,0:T(8,128)(2,1)} custom-call(bf16[64,512]{1,0:T(8,128)(2,1)S(1)} %get-tuple-element.21.refs_0_, bf16[64,512]{1,0:T(8,128)(2,1)S(1)} %collective-permute-done.11.refs_1_, bf16[64,512]{1,0:T(8,128)(2,1)S(1)} %collective-permute-done.12.refs_2_, bf16[64,512]{1,0:T(8,128)(2,1)S(1)} %collective-permute-done.13.refs_3_), custom_call_target="tpu_custom_call" | custom-call | tf_op jit(solution)/shard_map/pallas_call | solution.py:29
  52.6 7.0 %all-to-all-done.1.tables_ref = f32[32,8,8]{2,1,0:T(8,128)S(1)} async-done(((f32[32,8,8]{2,1,0:T(8,128)}), f32[32,8,8]{2,1,0:T(8,128)S(1)}, u32[]{:S(2)}, u32[]{:S(2)}) %all-to-all-start.1) | async-done | bytes 8224 | tf_op jit(solution)/shard_map/all_to_all | solution.py:307
  59.5 0.7 %shard_map.85 = f32[8,8]{1,0:T(8,128)} custom-call(f32[32,8,8]{2,1,0:T(8,128)S(1)} %all-to-all-done.1.tables_ref), custom_call_target="tpu_custom_call" | custom-call | tf_op jit(solution)/shard_map/pallas_call | solution.py:29
  (2 shorter events, 0.1 us)
Async XLA Ops:
  2.0 13.2 %collective-permute-start = (bf16[416,512]{1,0:T(8,128)(2,1)S(1)}, bf16[416,512]{1,0:T(8,128)(2,1)S(1)}, u32[]{:S(2)}, u32[]{:S(2)}) collective-permute-start(bf16[416,512]{1,0:T(8,128)(2,1)S(1)} %get-tuple-element.14), channel_id=1, source_target_pairs={{0,1},{1,0},{2,3},{3,2},{4,5},{5,4},{6,7},{7,6},{8,9},{9,8},{10,11... | collective-permute-start | bytes 1277960 | tf_op jit(solution)/shard_map/ppermute | solution.py:21
  5.0 4.4 %collective-permute-start.1 = (bf16[32,1024]{1,0:T(8,128)(2,1)S(1)}, bf16[32,1024]{1,0:T(8,128)(2,1)S(1)}, u32[]{:S(2)}, u32[]{:S(2)}) collective-permute-start(bf16[32,1024]{1,0:T(8,128)(2,1)S(1)} %get-tuple-element.15.refs_0_), channel_id=1, source_target_pairs={{0,2},{1,3},{2,0},{3,1},{4,6},{5,7},{6,4},{7,5},{8,10},{9,11},{10,... | collective-permute-start | bytes 196616 | tf_op jit(solution)/shard_map/ppermute | solution.py:21
  6.6 7.0 %collective-permute-start.2 = (bf16[32,1024]{1,0:T(8,128)(2,1)S(1)}, bf16[32,1024]{1,0:T(8,128)(2,1)S(1)}, u32[]{:S(2)}, u32[]{:S(2)}) collective-permute-start(bf16[32,1024]{1,0:T(8,128)(2,1)S(1)} %get-tuple-element.15.refs_0_), channel_id=1, source_target_pairs={{0,4},{1,5},{2,6},{3,7},{4,0},{5,1},{6,2},{7,3},{8,12},{9,13},{10,... | collective-permute-start | bytes 196616 | tf_op jit(solution)/shard_map/ppermute | solution.py:21
  9.2 6.1 %collective-permute-start.3 = (bf16[32,1024]{1,0:T(8,128)(2,1)S(1)}, bf16[32,1024]{1,0:T(8,128)(2,1)S(1)}, u32[]{:S(2)}, u32[]{:S(2)}) collective-permute-start(bf16[32,1024]{1,0:T(8,128)(2,1)S(1)} %get-tuple-element.15.refs_0_), channel_id=1, source_target_pairs={{0,6},{1,7},{2,4},{3,5},{4,2},{5,3},{6,0},{7,1},{8,14},{9,15},{10,... | collective-permute-start | bytes 196616 | tf_op jit(solution)/shard_map/ppermute | solution.py:21
  15.2 7.2 %copy-start.1 = (bf16[192,2048]{1,0:T(8,128)(2,1)S(1)}, bf16[192,2048]{1,0:T(8,128)(2,1)}, u32[]{:S(2)}) copy-start(bf16[192,2048]{1,0:T(8,128)(2,1)} %up_ref.3) | copy-start | bytes 2359300
  15.3 7.2 %copy-start = (bf16[192,2048]{1,0:T(8,128)(2,1)S(1)}, bf16[192,2048]{1,0:T(8,128)(2,1)}, u32[]{:S(2)}) copy-start(bf16[192,2048]{1,0:T(8,128)(2,1)} %gate_ref.3) | copy-start | bytes 2359300
  15.3 7.1 %collective-permute-start.5 = (bf16[128,1024]{1,0:T(8,128)(2,1)S(1)}, bf16[128,1024]{1,0:T(8,128)(2,1)S(1)}, u32[]{:S(2)}, u32[]{:S(2)}) collective-permute-start(bf16[128,1024]{1,0:T(8,128)(2,1)S(1)} %shard_map.78.after_ref.near_ref), channel_id=1, source_target_pairs={{0,1},{1,0},{2,3},{3,2},{4,5},{5,4},{6,7},{7,6},{8,9},{9,8},{10,11... | collective-permute-start | bytes 786440 | tf_op jit(solution)/shard_map/ppermute | solution.py:21
  16.7 10.5 %collective-permute-start.4 = (bf16[416,512]{1,0:T(8,128)(2,1)S(1)}, bf16[416,512]{1,0:T(8,128)(2,1)S(1)}, u32[]{:S(2)}, u32[]{:S(2)}) collective-permute-start(bf16[416,512]{1,0:T(8,128)(2,1)S(1)} %shard_map.79), channel_id=1, source_target_pairs={{0,2},{1,3},{2,0},{3,1},{4,6},{5,7},{6,4},{7,5},{8,10},{9,11},{10,... | collective-permute-start | bytes 1277960 | tf_op jit(solution)/shard_map/ppermute | solution.py:21
  18.3 4.1 %collective-permute-start.7 = (bf16[128,1024]{1,0:T(8,128)(2,1)S(1)}, bf16[128,1024]{1,0:T(8,128)(2,1)S(1)}, u32[]{:S(2)}, u32[]{:S(2)}) collective-permute-start(bf16[128,1024]{1,0:T(8,128)(2,1)S(1)} %shard_map.78.after_ref.near_ref), channel_id=1, source_target_pairs={{0,8},{8,0},{16,24},{24,16},{1,9},{9,1},{17,25},{25,17},{2,10},{10... | collective-permute-start | bytes 786440 | tf_op jit(solution)/shard_map/ppermute | solution.py:21
  22.4 4.8 %collective-permute-start.6 = (bf16[128,1024]{1,0:T(8,128)(2,1)S(1)}, bf16[128,1024]{1,0:T(8,128)(2,1)S(1)}, u32[]{:S(2)}, u32[]{:S(2)}) collective-permute-start(bf16[128,1024]{1,0:T(8,128)(2,1)S(1)} %collective-permute-done.5.far_ref), channel_id=1, source_target_pairs={{0,8},{8,0},{16,24},{24,16},{1,9},{9,1},{17,25},{25,17},{2,10},{10... | collective-permute-start | bytes 786440 | tf_op jit(solution)/shard_map/ppermute | solution.py:21
  27.5 5.6 %collective-permute-start.10 = (bf16[192,256]{1,0:T(8,128)(2,1)S(1)}, bf16[192,256]{1,0:T(8,128)(2,1)S(1)}, u32[]{:S(2)}, u32[]{:S(2)}) collective-permute-start(bf16[192,256]{1,0:T(8,128)(2,1)S(1)} %shard_map.81.refs_0_), channel_id=1, source_target_pairs={{0,3},{1,2},{2,1},{3,0},{4,7},{5,6},{6,5},{7,4},{8,11},{9,10},{10,... | collective-permute-start | bytes 294920 | tf_op jit(solution)/shard_map/ppermute | solution.py:21
  29.1 5.0 %collective-permute-start.8 = (bf16[192,256]{1,0:T(8,128)(2,1)S(1)}, bf16[192,256]{1,0:T(8,128)(2,1)S(1)}, u32[]{:S(2)}, u32[]{:S(2)}) collective-permute-start(bf16[192,256]{1,0:T(8,128)(2,1)S(1)} %shard_map.81.refs_0_), channel_id=1, source_target_pairs={{0,1},{1,0},{2,3},{3,2},{4,5},{5,4},{6,7},{7,6},{8,9},{9,8},{10,11... | collective-permute-start | bytes 294920 | tf_op jit(solution)/shard_map/ppermute | solution.py:21
  30.6 4.6 %collective-permute-start.9 = (bf16[192,256]{1,0:T(8,128)(2,1)S(1)}, bf16[192,256]{1,0:T(8,128)(2,1)S(1)}, u32[]{:S(2)}, u32[]{:S(2)}) collective-permute-start(bf16[192,256]{1,0:T(8,128)(2,1)S(1)} %shard_map.81.refs_0_), channel_id=1, source_target_pairs={{0,2},{1,3},{2,0},{3,1},{4,6},{5,7},{6,4},{7,5},{8,10},{9,11},{10,... | collective-permute-start | bytes 294920 | tf_op jit(solution)/shard_map/ppermute | solution.py:21
  36.7 11.7 %all-to-all-start = ((bf16[32,16,128]{2,1,0:T(8,128)(2,1)}), bf16[32,16,128]{2,1,0:T(8,128)(2,1)S(1)}, u32[]{:S(2)}, u32[]{:S(2)}) async-start(bf16[32,16,128]{2,1,0:T(8,128)(2,1)} %bitcast.1), calls=%async_computation | async-start | bytes 262144 | tf_op jit(solution)/shard_map/all_to_all | solution.py:296
  40.7 11.1 %collective-permute-start.11 = (bf16[64,512]{1,0:T(8,128)(2,1)S(1)}, bf16[64,512]{1,0:T(8,128)(2,1)S(1)}, u32[]{:S(2)}, u32[]{:S(2)}) collective-permute-start(bf16[64,512]{1,0:T(8,128)(2,1)S(1)} %get-tuple-element.22), channel_id=1, source_target_pairs={{0,1},{1,0},{2,3},{3,2},{4,5},{5,4},{6,7},{7,6},{8,9},{9,8},{10,11... | collective-permute-start | bytes 196616 | tf_op jit(solution)/shard_map/ppermute | solution.py:21
  42.5 9.3 %collective-permute-start.12 = (bf16[64,512]{1,0:T(8,128)(2,1)S(1)}, bf16[64,512]{1,0:T(8,128)(2,1)S(1)}, u32[]{:S(2)}, u32[]{:S(2)}) collective-permute-start(bf16[64,512]{1,0:T(8,128)(2,1)S(1)} %get-tuple-element.23), channel_id=1, source_target_pairs={{0,2},{1,3},{2,0},{3,1},{4,6},{5,7},{6,4},{7,5},{8,10},{9,11},{10,... | collective-permute-start | bytes 196616 | tf_op jit(solution)/shard_map/ppermute | solution.py:21
  44.0 7.8 %collective-permute-start.13 = (bf16[64,512]{1,0:T(8,128)(2,1)S(1)}, bf16[64,512]{1,0:T(8,128)(2,1)S(1)}, u32[]{:S(2)}, u32[]{:S(2)}) collective-permute-start(bf16[64,512]{1,0:T(8,128)(2,1)S(1)} %get-tuple-element.24), channel_id=1, source_target_pairs={{0,3},{1,2},{2,1},{3,0},{4,7},{5,6},{6,5},{7,4},{8,11},{9,10},{10,... | collective-permute-start | bytes 196616 | tf_op jit(solution)/shard_map/ppermute | solution.py:21
  49.2 10.3 %all-to-all-start.1 = ((f32[32,8,8]{2,1,0:T(8,128)}), f32[32,8,8]{2,1,0:T(8,128)S(1)}, u32[]{:S(2)}, u32[]{:S(2)}) async-start(f32[32,8,8]{2,1,0:T(8,128)} %shard_map.84), calls=%async_computation.1 | async-start | bytes 262144 | tf_op jit(solution)/shard_map/all_to_all | solution.py:307

commit v14 on v13

--- a/solution.py
+++ b/solution.py
@@ -45,17 +45,20 @@
     return lax.axis_index("tok") & (HOLDERS - 1)
 
 
+def columns_of(half, width):
+    return pl.ds(pl.multiple_of(half * width, width), width)
+
+
 def first_kernel(states_hbm, gain_hbm, down_hbm, route_hbm, out_ref, *refs):
-    kept_ref, z_ref, x_ref, states_ref, gain_ref, route_ref, sems = refs
-    depth, width = down_hbm.shape[0], kept_ref.shape[1]
-    downs = (kept_ref, x_ref.at[pl.ds(0, depth + TILE)], z_ref, x_ref.at[pl.ds(depth + TILE, depth + TILE)])
+    downs, (states_ref, gain_ref, route_ref, sems) = refs[:HOLDERS], refs[HOLDERS:]
+    depth, width = down_hbm.shape[0], downs[0].shape[1]
     copies = [
         pltpu.make_async_copy(states_hbm, states_ref, sems.at[0]),
         pltpu.make_async_copy(gain_hbm, gain_ref, sems.at[1]),
         pltpu.make_async_copy(route_hbm, route_ref, sems.at[2]),
     ]
     for m, down_ref in enumerate(downs):
-        columns = pl.ds(pl.multiple_of((holder() ^ m) * width, width), width)
+        columns = columns_of(holder() ^ m, width)
         copies.append(
             pltpu.make_async_copy(
                 down_hbm.at[:, columns], down_ref.at[pl.ds(0, depth)], sems.at[3 + m]
@@ -67,8 +70,7 @@
         copy.wait()
     states = states_ref[...].astype(f32)
     scale = lax.rsqrt(jnp.mean(states * states, axis=1, keepdims=True) + 1e-06)
-    width = out_ref.shape[1]
-    own = pl.ds(pl.multiple_of(core() * width, width), width)
+    own = columns_of(core(), out_ref.shape[1])
     out_ref[...] = (states_ref[:, own].astype(f32) * scale * gain_ref[:, own]).astype(bf16)
     route = route_ref[...]
     high = route.astype(bf16).astype(f32)
@@ -77,17 +79,32 @@
     part = route.shape[1]
     row = lax.broadcasted_iota(jnp.int32, (TILE, part), 0)
     terms = jnp.where(row == 0, high, jnp.where(row == 1, middle, jnp.where(row == 2, low, 0.0)))
-    terms = jnp.concatenate([terms, jnp.zeros((TILE, kept_ref.shape[1] - part), f32)], 1)
+    terms = jnp.concatenate([terms, jnp.zeros((TILE, width - part), f32)], 1)
     for down_ref in downs:
         down_ref[pl.ds(depth, TILE)] = terms.astype(bf16)
     for copy in copies[3:]:
         copy.wait()
 
 
-def onward_kernel(after_ref, own_ref, got_ref, out_ref):
-    count = own_ref.shape[0]
-    out_ref[:count] = own_ref[...]
-    out_ref[count:] = got_ref[count:]
+def hold_kernel(*refs):
+    pass
+
+
+def held(array, after):
+    return call(
+        hold_kernel,
+        jax.ShapeDtypeStruct(array.shape, array.dtype),
+        [ANY] * 2,
+        (array, after),
+        out_specs=ANY,
+        aliases={0: 0},
+    )
+
+
+def join_kernel(after_ref, first_ref, second_ref, out_ref):
+    count = first_ref.shape[0]
+    out_ref[:count] = first_ref[...]
+    out_ref[count:] = second_ref[...]
 
 
 def stack_kernel(after_ref, *refs):
@@ -95,10 +112,6 @@
     z = lax.axis_index("tok") >> 1
     for m, piece in enumerate(refs[:-1]):
         refs[-1][pl.ds(pl.multiple_of((z ^ m) * rows, rows), rows)] = piece[...]
-
-
-def columns_of(half, width):
-    return pl.ds(pl.multiple_of(half * width, width), width)
 
 
 def gated(gate, upward):
@@ -137,7 +150,7 @@
     route_ref, features_ref, whole_ref, shares_ref, sem = refs[2 * HOLDERS + 4 :]
     depth, tokens = hidden_refs[0].shape
     count = kept_ref.shape[0]
-    downs = (kept_ref[...], x_ref[:count], z_ref[:count], z_ref[count:])
+    downs = (kept_ref[...], x_ref[...], z_ref[:count], z_ref[count:])
     part, members = tokens // HOLDERS, lax.axis_size("tok")
     rows = tokens // members
 
@@ -230,10 +243,10 @@
     depth = gate_weight.shape[0]
     part, token_part = model // HOLDERS, tokens // HOLDERS
 
-    own, down_own, down_z, down_x = call(
+    own, down_own, down_x, down_z, down_xz = call(
         first_kernel,
         [jax.ShapeDtypeStruct((rows, model // 2), bf16)]
-        + [jax.ShapeDtypeStruct(((depth + TILE) * n, part), bf16) for n in (1, 1, 2)],
+        + [jax.ShapeDtypeStruct((depth + TILE, part), bf16)] * HOLDERS,
         [HBM] * 4,
         [
             pltpu.with_memory_space_constraint(a, pltpu.HBM)
@@ -246,23 +259,24 @@
             pltpu.SemaphoreType.DMA((3 + HOLDERS,)),
         ],
     )
-    down_x = swapped(down_x, "tok", 1)
+    down_xz = swapped(down_xz, "tok", 1)
     pieces = [swapped(own, "tok", 2 * m) if m else own for m in range(members // 2)]
     near = call(
         stack_kernel,
         jax.ShapeDtypeStruct((tokens // 2, model // 2), bf16),
         [ANY] + [VMEM] * len(pieces),
-        (down_x, *pieces),
+        (down_xz, *pieces),
     )
     far = swapped(near, "tok", 1)
     near2 = swapped(near, "grp", 1)
     down_z = call(
-        onward_kernel,
-        jax.ShapeDtypeStruct(down_x.shape, bf16),
+        join_kernel,
+        jax.ShapeDtypeStruct((2 * (depth + TILE), part), bf16),
         [ANY, VMEM, VMEM],
-        (near, down_z, down_x),
+        (near, down_z, down_xz),
     )
     down_z = swapped(down_z, "tok", 2)
+    down_x = swapped(held(down_x, far), "tok", 1)
     half_shape = (depth, tokens // 2)
     near_hidden, gate_part, up_part = call(
         near_kernel,

time: 60.5 us -> 57.5 us (0.950)
  starting transfers between devices: 24 us -> 21.9 us
  waiting for transfers between devices: 29.2 us -> 28.4 us
    all_to_all x1, starting transfers between devices: 3.93 us -> 2.63 us  [shards(): lax.all_to_all(centered, ('grp', 'tok'), split_axis=0, concat_axis=0, til...]
    ppermute x14 -> x15, starting transfers between devices: 17.5 us -> 16.7 us  [swapped(): lax.ppermute(array, axis, [(i, i ^ mask) for i in range(lax.axis_size(axi...]
    ppermute x14 -> x15, waiting for transfers between devices: 18.1 us -> 17.3 us  [swapped(): lax.ppermute(array, axis, [(i, i ^ mask) for i in range(lax.axis_size(axi...]
    pallas_call x9 -> x10, Pallas kernels: 6.25 us -> 6.26 us  [call(): pl.pallas_call(body, out_shape=outs, in_specs=in_specs, out_specs=jax.tre...]
  transfers between devices with their start and end apart: 16 -> 17, of which waited for: 9 -> 10; matrix products, arithmetic and copies ran while one was open for 0% -> 0% of each run, Pallas kernels for 4% -> 5%
where the time goes in v14:
time: 57.5 us; the launch traced here: 57.3 us
  waiting for transfers between devices  28.4 us (49%)
  starting transfers between devices  21.9 us (38%)
  Pallas kernels  6.26 us (11%)
  between operations  0.74 us (1%)
    ppermute x15, waiting for transfers between devices, swapped(): lax.ppermute(array, axis, [(i, i ^ mask) for i in range(lax.axis_size(axi...  17.3 us
    ppermute x15, starting transfers between devices, swapped(): lax.ppermute(array, axis, [(i, i ^ mask) for i in range(lax.axis_size(axi...  16.7 us
    all_to_all x1, waiting for transfers between devices, shards(): lax.all_to_all(tables, ('grp', 'tok'), split_axis=0, concat_axis=0, tiled...  6.96 us
    pallas_call x10, Pallas kernels, call(): pl.pallas_call(body, out_shape=outs, in_specs=in_specs, out_specs=jax.tre...  6.26 us
    all_to_all x1, waiting for transfers between devices, shards(): lax.all_to_all(centered, ('grp', 'tok'), split_axis=0, concat_axis=0, til...  4.19 us
    all_to_all x1, starting transfers between devices, shards(): lax.all_to_all(centered, ('grp', 'tok'), split_axis=0, concat_axis=0, til...  2.63 us
    all_to_all x1, starting transfers between devices, shards(): lax.all_to_all(tables, ('grp', 'tok'), split_axis=0, concat_axis=0, tiled...  2.56 us
  transfers between devices with their start and end apart: 17, of which 10 were waited for; matrix products, arithmetic and copies ran while one was open for 0% of the time, Pallas kernels for 5%

profile of v14, /device:TPU:0, one launch (start us, length us, event | category | flops | bytes accessed | tf_op | source)
XLA Modules:
  0.0 57.3 jit_solution(16967073934339115047)
XLA Ops:
  0.6 1.3 %shard_map.77 = (bf16[32,1024]{1,0:T(8,128)(2,1)S(1)}, bf16[208,512]{1,0:T(8,128)(2,1)S(1)}, bf16[208,512]{1,0:T(8,128)(2,1)S(1)}, bf16[208,512]{1,0:T(8,128)(2,1)S(1)}, bf16[208,512]{1,0:T(8,128)(2,1)S(1)}) custom-call(bf16[32,2048]{1,0:T(8,128)(2,1)} %states_hbm.1, f32[1,2048]{1,0:T(1,128)} %bitcast.4, bf16[192,2048]{1,0:T(8,128)(2,1)} %down_hbm.1, ...), custom_call_target="tpu_custom_call" | custom-call | tf_op jit(solution)/shard_map/pallas_call | solution.py:29
  2.0 3.0 %collective-permute-start = (bf16[208,512]{1,0:T(8,128)(2,1)S(1)}, bf16[208,512]{1,0:T(8,128)(2,1)S(1)}, u32[]{:S(2)}, u32[]{:S(2)}) collective-permute-start(bf16[208,512]{1,0:T(8,128)(2,1)S(1)} %get-tuple-element.15), channel_id=1, source_target_pairs={{0,1},{1,0},{2,3},{3,2},{4,5},{5,4},{6,7},{7,6},{8,9},{9,8},{10,11... | collective-permute-start | bytes 638984 | tf_op jit(solution)/shard_map/ppermute | solution.py:21
  5.0 3.6 %collective-permute-start.3 = (bf16[32,1024]{1,0:T(8,128)(2,1)S(1)}, bf16[32,1024]{1,0:T(8,128)(2,1)S(1)}, u32[]{:S(2)}, u32[]{:S(2)}) collective-permute-start(bf16[32,1024]{1,0:T(8,128)(2,1)S(1)} %get-tuple-element.16.refs_0_), channel_id=1, source_target_pairs={{0,6},{1,7},{2,4},{3,5},{4,2},{5,3},{6,0},{7,1},{8,14},{9,15},{10,... | collective-permute-start | bytes 196616 | tf_op jit(solution)/shard_map/ppermute | solution.py:21
  8.6 0.0 collective-permute-start.2
  8.6 0.8 %collective-permute-start.1 = (bf16[32,1024]{1,0:T(8,128)(2,1)S(1)}, bf16[32,1024]{1,0:T(8,128)(2,1)S(1)}, u32[]{:S(2)}, u32[]{:S(2)}) collective-permute-start(bf16[32,1024]{1,0:T(8,128)(2,1)S(1)} %get-tuple-element.16.refs_0_), channel_id=1, source_target_pairs={{0,2},{1,3},{2,0},{3,1},{4,6},{5,7},{6,4},{7,5},{8,10},{9,11},{10,... | collective-permute-start | bytes 196616 | tf_op jit(solution)/shard_map/ppermute | solution.py:21
  9.4 2.5 %collective-permute-done.3.refs_3_ = bf16[32,1024]{1,0:T(8,128)(2,1)S(1)} collective-permute-done((bf16[32,1024]{1,0:T(8,128)(2,1)S(1)}, bf16[32,1024]{1,0:T(8,128)(2,1)S(1)}, u32[]{:S(2)}, u32[]{:S(2)}) %collective-permute-start.3) | collective-permute-done | bytes 65568 | tf_op jit(solution)/shard_map/ppermute | solution.py:21
  11.9 2.1 %collective-permute-done.2.refs_2_ = bf16[32,1024]{1,0:T(8,128)(2,1)S(1)} collective-permute-done((bf16[32,1024]{1,0:T(8,128)(2,1)S(1)}, bf16[32,1024]{1,0:T(8,128)(2,1)S(1)}, u32[]{:S(2)}, u32[]{:S(2)}) %collective-permute-start.2) | collective-permute-done | bytes 65568 | tf_op jit(solution)/shard_map/ppermute | solution.py:21
  14.0 0.1 collective-permute-done.1.refs_1_
  14.0 0.0 collective-permute-done.after_ref.second_ref
  14.1 0.5 collective-permute-start.5
  14.6 0.0 copy-start
  14.6 0.0 copy-start.1
  14.6 1.1 %collective-permute-start.4 = (bf16[416,512]{1,0:T(8,128)(2,1)S(1)}, bf16[416,512]{1,0:T(8,128)(2,1)S(1)}, u32[]{:S(2)}, u32[]{:S(2)}) collective-permute-start(bf16[416,512]{1,0:T(8,128)(2,1)S(1)} %shard_map.79), channel_id=1, source_target_pairs={{0,2},{1,3},{2,0},{3,1},{4,6},{5,7},{6,4},{7,5},{8,10},{9,11},{10,... | collective-permute-start | bytes 1277960 | tf_op jit(solution)/shard_map/ppermute | solution.py:21
  15.7 0.0 collective-permute-start.7
  15.7 6.0 %collective-permute-done.5.far_ref.refs_1_ = bf16[128,1024]{1,0:T(8,128)(2,1)S(1)} collective-permute-done((bf16[128,1024]{1,0:T(8,128)(2,1)S(1)}, bf16[128,1024]{1,0:T(8,128)(2,1)S(1)}, u32[]{:S(2)}, u32[]{:S(2)}) %collective-permute-start.5) | collective-permute-done | bytes 262176 | tf_op jit(solution)/shard_map/ppermute | solution.py:21
  21.7 0.0 collective-permute-start.6
  21.7 0.5 collective-permute-start.11
  22.3 0.0 collective-permute-done.7.near2_ref
  22.3 0.0 copy-done
  22.3 0.0 copy-done.1
  22.3 0.8 %shard_map.80 = (bf16[192,128]{1,0:T(8,128)(2,1)S(1)}, f32[192,128]{1,0:T(8,128)S(1)}, f32[192,128]{1,0:T(8,128)S(1)}) custom-call(bf16[128,1024]{1,0:T(8,128)(2,1)S(1)} %shard_map.78.after_ref.near_ref, bf16[128,1024]{1,0:T(8,128)(2,1)S(1)} %collective-permute-done.7.near2_ref, bf16[128,1024]{1,0:T(8,128)(2,1)S(1)} %collective-permute-done.5.far_ref.refs_1_, ...), custom_call_target="tpu_custom_call" | custom-call | tf_op jit(solution)/shard_map/pallas_call | solution.py:29
  23.1 2.5 %collective-permute-done.4.after_ref.refs_6_ = bf16[416,512]{1,0:T(8,128)(2,1)S(1)} collective-permute-done((bf16[416,512]{1,0:T(8,128)(2,1)S(1)}, bf16[416,512]{1,0:T(8,128)(2,1)S(1)}, u32[]{:S(2)}, u32[]{:S(2)}) %collective-permute-start.4) | collective-permute-done | bytes 426016 | tf_op jit(solution)/shard_map/ppermute | solution.py:21
  25.6 0.0 collective-permute-done.6.far2_ref
  25.6 0.4 shard_map.81.refs_0_
  26.0 1.3 %collective-permute-start.10 = (bf16[192,256]{1,0:T(8,128)(2,1)S(1)}, bf16[192,256]{1,0:T(8,128)(2,1)S(1)}, u32[]{:S(2)}, u32[]{:S(2)}) collective-permute-start(bf16[192,256]{1,0:T(8,128)(2,1)S(1)} %shard_map.81.refs_0_), channel_id=1, source_target_pairs={{0,3},{1,2},{2,1},{3,0},{4,7},{5,6},{6,5},{7,4},{8,11},{9,10},{10,... | collective-permute-start | bytes 294920 | tf_op jit(solution)/shard_map/ppermute | solution.py:21
  27.3 1.7 %collective-permute-start.9 = (bf16[192,256]{1,0:T(8,128)(2,1)S(1)}, bf16[192,256]{1,0:T(8,128)(2,1)S(1)}, u32[]{:S(2)}, u32[]{:S(2)}) collective-permute-start(bf16[192,256]{1,0:T(8,128)(2,1)S(1)} %shard_map.81.refs_0_), channel_id=1, source_target_pairs={{0,2},{1,3},{2,0},{3,1},{4,6},{5,7},{6,4},{7,5},{8,10},{9,11},{10,... | collective-permute-start | bytes 294920 | tf_op jit(solution)/shard_map/ppermute | solution.py:21
  29.0 0.5 collective-permute-start.8
  29.5 2.4 %collective-permute-done.11.refs_5_ = bf16[208,512]{1,0:T(8,128)(2,1)S(1)} collective-permute-done((bf16[208,512]{1,0:T(8,128)(2,1)S(1)}, bf16[208,512]{1,0:T(8,128)(2,1)S(1)}, u32[]{:S(2)}, u32[]{:S(2)}) %collective-permute-start.11) | collective-permute-done | bytes 213024 | tf_op jit(solution)/shard_map/ppermute | solution.py:21
  31.9 0.0 collective-permute-done.10.refs_3_
  31.9 0.7 %collective-permute-done.9.refs_2_ = bf16[192,256]{1,0:T(8,128)(2,1)S(1)} collective-permute-done((bf16[192,256]{1,0:T(8,128)(2,1)S(1)}, bf16[192,256]{1,0:T(8,128)(2,1)S(1)}, u32[]{:S(2)}, u32[]{:S(2)}) %collective-permute-start.9) | collective-permute-done | bytes 98336 | tf_op jit(solution)/shard_map/ppermute | solution.py:21
  32.6 1.0 %collective-permute-done.8.refs_1_ = bf16[192,256]{1,0:T(8,128)(2,1)S(1)} collective-permute-done((bf16[192,256]{1,0:T(8,128)(2,1)S(1)}, bf16[192,256]{1,0:T(8,128)(2,1)S(1)}, u32[]{:S(2)}, u32[]{:S(2)}) %collective-permute-start.8) | collective-permute-done | bytes 98336 | tf_op jit(solution)/shard_map/ppermute | solution.py:21
  33.6 1.5 %shard_map.83 = (bf16[64,512]{1,0:T(8,128)(2,1)S(1)}, bf16[64,512]{1,0:T(8,128)(2,1)S(1)}, bf16[64,512]{1,0:T(8,128)(2,1)S(1)}, bf16[64,512]{1,0:T(8,128)(2,1)S(1)}, bf16[512,128]{1,0:T(8,128)(2,1)}) custom-call(bf16[192,256]{1,0:T(8,128)(2,1)S(1)} %shard_map.81.refs_0_, bf16[192,256]{1,0:T(8,128)(2,1)S(1)} %collective-permute-done.8.refs_1_, ...), custom_call_target="tpu_custom_call" | custom-call | tf_op jit(solution)/shard_map/pallas_call | solution.py:29
  35.1 2.6 %all-to-all-start = ((bf16[32,16,128]{2,1,0:T(8,128)(2,1)}), bf16[32,16,128]{2,1,0:T(8,128)(2,1)S(1)}, u32[]{:S(2)}, u32[]{:S(2)}) async-start(bf16[32,16,128]{2,1,0:T(8,128)(2,1)} %bitcast.1), calls=%async_computation | async-start | bytes 262144 | tf_op jit(solution)/shard_map/all_to_all | solution.py:310
  37.7 1.8 %collective-permute-start.12 = (bf16[64,512]{1,0:T(8,128)(2,1)S(1)}, bf16[64,512]{1,0:T(8,128)(2,1)S(1)}, u32[]{:S(2)}, u32[]{:S(2)}) collective-permute-start(bf16[64,512]{1,0:T(8,128)(2,1)S(1)} %get-tuple-element.24), channel_id=1, source_target_pairs={{0,1},{1,0},{2,3},{3,2},{4,5},{5,4},{6,7},{7,6},{8,9},{9,8},{10,11... | collective-permute-start | bytes 196616 | tf_op jit(solution)/shard_map/ppermute | solution.py:21
  39.6 1.5 %collective-permute-start.13 = (bf16[64,512]{1,0:T(8,128)(2,1)S(1)}, bf16[64,512]{1,0:T(8,128)(2,1)S(1)}, u32[]{:S(2)}, u32[]{:S(2)}) collective-permute-start(bf16[64,512]{1,0:T(8,128)(2,1)S(1)} %get-tuple-element.25), channel_id=1, source_target_pairs={{0,2},{1,3},{2,0},{3,1},{4,6},{5,7},{6,4},{7,5},{8,10},{9,11},{10,... | collective-permute-start | bytes 196616 | tf_op jit(solution)/shard_map/ppermute | solution.py:21
  41.0 0.3 collective-permute-start.14
  41.3 4.2 %all-to-all-done = bf16[32,16,128]{2,1,0:T(8,128)(2,1)S(1)} async-done(((bf16[32,16,128]{2,1,0:T(8,128)(2,1)}), bf16[32,16,128]{2,1,0:T(8,128)(2,1)S(1)}, u32[]{:S(2)}, u32[]{:S(2)}) %all-to-all-start) | async-done | bytes 131104 | tf_op jit(solution)/shard_map/all_to_all | solution.py:310
  45.5 0.8 %shard_map.85 = f32[32,8,8]{2,1,0:T(8,128)} custom-call(bf16[8,4,16,128]{3,2,1,0:T(8,128)(2,1)S(1)} %bitcast.3), custom_call_target="tpu_custom_call" | custom-call | tf_op jit(solution)/shard_map/pallas_call | solution.py:29
  46.3 2.6 %all-to-all-start.1 = ((f32[32,8,8]{2,1,0:T(8,128)}), f32[32,8,8]{2,1,0:T(8,128)S(1)}, u32[]{:S(2)}, u32[]{:S(2)}) async-start(f32[32,8,8]{2,1,0:T(8,128)} %shard_map.85), calls=%async_computation.1 | async-start | bytes 262144 | tf_op jit(solution)/shard_map/all_to_all | solution.py:321
  48.8 0.0 collective-permute-done.12.refs_1_
  48.8 0.0 collective-permute-done.13.refs_2_
  48.9 0.0 collective-permute-done.14.refs_3_
  48.9 0.7 %shard_map.84 = bf16[64,2048]{1,0:T(8,128)(2,1)} custom-call(bf16[64,512]{1,0:T(8,128)(2,1)S(1)} %get-tuple-element.23.refs_0_, bf16[64,512]{1,0:T(8,128)(2,1)S(1)} %collective-permute-done.12.refs_1_, bf16[64,512]{1,0:T(8,128)(2,1)S(1)} %collective-permute-done.13.refs_2_, bf16[64,512]{1,0:T(8,128)(2,1)S(1)} %collective-permute-done.14.refs_3_), custom_call_target="tpu_custom_call" | custom-call | tf_op jit(solution)/shard_map/pallas_call | solution.py:29
  49.6 7.0 %all-to-all-done.1.tables_ref = f32[32,8,8]{2,1,0:T(8,128)S(1)} async-done(((f32[32,8,8]{2,1,0:T(8,128)}), f32[32,8,8]{2,1,0:T(8,128)S(1)}, u32[]{:S(2)}, u32[]{:S(2)}) %all-to-all-start.1) | async-done | bytes 8224 | tf_op jit(solution)/shard_map/all_to_all | solution.py:321
  56.6 0.7 %shard_map.86 = f32[8,8]{1,0:T(8,128)} custom-call(f32[32,8,8]{2,1,0:T(8,128)S(1)} %all-to-all-done.1.tables_ref), custom_call_target="tpu_custom_call" | custom-call | tf_op jit(solution)/shard_map/pallas_call | solution.py:29
  (3 shorter events, 0.1 us)
Async XLA Ops:
  2.0 12.0 %collective-permute-start = (bf16[208,512]{1,0:T(8,128)(2,1)S(1)}, bf16[208,512]{1,0:T(8,128)(2,1)S(1)}, u32[]{:S(2)}, u32[]{:S(2)}) collective-permute-start(bf16[208,512]{1,0:T(8,128)(2,1)S(1)} %get-tuple-element.15), channel_id=1, source_target_pairs={{0,1},{1,0},{2,3},{3,2},{4,5},{5,4},{6,7},{7,6},{8,9},{9,8},{10,11... | collective-permute-start | bytes 638984 | tf_op jit(solution)/shard_map/ppermute | solution.py:21
  5.0 6.9 %collective-permute-start.3 = (bf16[32,1024]{1,0:T(8,128)(2,1)S(1)}, bf16[32,1024]{1,0:T(8,128)(2,1)S(1)}, u32[]{:S(2)}, u32[]{:S(2)}) collective-permute-start(bf16[32,1024]{1,0:T(8,128)(2,1)S(1)} %get-tuple-element.16.refs_0_), channel_id=1, source_target_pairs={{0,6},{1,7},{2,4},{3,5},{4,2},{5,3},{6,0},{7,1},{8,14},{9,15},{10,... | collective-permute-start | bytes 196616 | tf_op jit(solution)/shard_map/ppermute | solution.py:21
  8.6 5.4 %collective-permute-start.2 = (bf16[32,1024]{1,0:T(8,128)(2,1)S(1)}, bf16[32,1024]{1,0:T(8,128)(2,1)S(1)}, u32[]{:S(2)}, u32[]{:S(2)}) collective-permute-start(bf16[32,1024]{1,0:T(8,128)(2,1)S(1)} %get-tuple-element.16.refs_0_), channel_id=1, source_target_pairs={{0,4},{1,5},{2,6},{3,7},{4,0},{5,1},{6,2},{7,3},{8,12},{9,13},{10,... | collective-permute-start | bytes 196616 | tf_op jit(solution)/shard_map/ppermute | solution.py:21
  8.6 5.4 %collective-permute-start.1 = (bf16[32,1024]{1,0:T(8,128)(2,1)S(1)}, bf16[32,1024]{1,0:T(8,128)(2,1)S(1)}, u32[]{:S(2)}, u32[]{:S(2)}) collective-permute-start(bf16[32,1024]{1,0:T(8,128)(2,1)S(1)} %get-tuple-element.16.refs_0_), channel_id=1, source_target_pairs={{0,2},{1,3},{2,0},{3,1},{4,6},{5,7},{6,4},{7,5},{8,10},{9,11},{10,... | collective-permute-start | bytes 196616 | tf_op jit(solution)/shard_map/ppermute | solution.py:21
  14.1 7.7 %collective-permute-start.5 = (bf16[128,1024]{1,0:T(8,128)(2,1)S(1)}, bf16[128,1024]{1,0:T(8,128)(2,1)S(1)}, u32[]{:S(2)}, u32[]{:S(2)}) collective-permute-start(bf16[128,1024]{1,0:T(8,128)(2,1)S(1)} %shard_map.78.after_ref.near_ref), channel_id=1, source_target_pairs={{0,1},{1,0},{2,3},{3,2},{4,5},{5,4},{6,7},{7,6},{8,9},{9,8},{10,11... | collective-permute-start | bytes 786440 | tf_op jit(solution)/shard_map/ppermute | solution.py:21
  14.6 7.7 %copy-start = (bf16[192,2048]{1,0:T(8,128)(2,1)S(1)}, bf16[192,2048]{1,0:T(8,128)(2,1)}, u32[]{:S(2)}) copy-start(bf16[192,2048]{1,0:T(8,128)(2,1)} %gate_ref.3) | copy-start | bytes 2359300
  14.6 7.7 %copy-start.1 = (bf16[192,2048]{1,0:T(8,128)(2,1)S(1)}, bf16[192,2048]{1,0:T(8,128)(2,1)}, u32[]{:S(2)}) copy-start(bf16[192,2048]{1,0:T(8,128)(2,1)} %up_ref.3) | copy-start | bytes 2359300
  14.6 11.0 %collective-permute-start.4 = (bf16[416,512]{1,0:T(8,128)(2,1)S(1)}, bf16[416,512]{1,0:T(8,128)(2,1)S(1)}, u32[]{:S(2)}, u32[]{:S(2)}) collective-permute-start(bf16[416,512]{1,0:T(8,128)(2,1)S(1)} %shard_map.79), channel_id=1, source_target_pairs={{0,2},{1,3},{2,0},{3,1},{4,6},{5,7},{6,4},{7,5},{8,10},{9,11},{10,... | collective-permute-start | bytes 1277960 | tf_op jit(solution)/shard_map/ppermute | solution.py:21
  15.7 6.5 %collective-permute-start.7 = (bf16[128,1024]{1,0:T(8,128)(2,1)S(1)}, bf16[128,1024]{1,0:T(8,128)(2,1)S(1)}, u32[]{:S(2)}, u32[]{:S(2)}) collective-permute-start(bf16[128,1024]{1,0:T(8,128)(2,1)S(1)} %shard_map.78.after_ref.near_ref), channel_id=1, source_target_pairs={{0,8},{8,0},{16,24},{24,16},{1,9},{9,1},{17,25},{25,17},{2,10},{10... | collective-permute-start | bytes 786440 | tf_op jit(solution)/shard_map/ppermute | solution.py:21
  21.7 3.9 %collective-permute-start.6 = (bf16[128,1024]{1,0:T(8,128)(2,1)S(1)}, bf16[128,1024]{1,0:T(8,128)(2,1)S(1)}, u32[]{:S(2)}, u32[]{:S(2)}) collective-permute-start(bf16[128,1024]{1,0:T(8,128)(2,1)S(1)} %collective-permute-done.5.far_ref.refs_1_), channel_id=1, source_target_pairs={{0,8},{8,0},{16,24},{24,16},{1,9},{9,1},{17,25},{25,17},{2,10},{10... | collective-permute-start | bytes 786440 | tf_op jit(solution)/shard_map/ppermute | solution.py:21
  21.7 10.2 %collective-permute-start.11 = (bf16[208,512]{1,0:T(8,128)(2,1)S(1)}, bf16[208,512]{1,0:T(8,128)(2,1)S(1)}, u32[]{:S(2)}, u32[]{:S(2)}) collective-permute-start(bf16[208,512]{1,0:T(8,128)(2,1)S(1)} %shard_map.82), channel_id=1, source_target_pairs={{0,1},{1,0},{2,3},{3,2},{4,5},{5,4},{6,7},{7,6},{8,9},{9,8},{10,11... | collective-permute-start | bytes 638984 | tf_op jit(solution)/shard_map/ppermute | solution.py:21
  26.0 5.9 %collective-permute-start.10 = (bf16[192,256]{1,0:T(8,128)(2,1)S(1)}, bf16[192,256]{1,0:T(8,128)(2,1)S(1)}, u32[]{:S(2)}, u32[]{:S(2)}) collective-permute-start(bf16[192,256]{1,0:T(8,128)(2,1)S(1)} %shard_map.81.refs_0_), channel_id=1, source_target_pairs={{0,3},{1,2},{2,1},{3,0},{4,7},{5,6},{6,5},{7,4},{8,11},{9,10},{10,... | collective-permute-start | bytes 294920 | tf_op jit(solution)/shard_map/ppermute | solution.py:21
  27.3 5.4 %collective-permute-start.9 = (bf16[192,256]{1,0:T(8,128)(2,1)S(1)}, bf16[192,256]{1,0:T(8,128)(2,1)S(1)}, u32[]{:S(2)}, u32[]{:S(2)}) collective-permute-start(bf16[192,256]{1,0:T(8,128)(2,1)S(1)} %shard_map.81.refs_0_), channel_id=1, source_target_pairs={{0,2},{1,3},{2,0},{3,1},{4,6},{5,7},{6,4},{7,5},{8,10},{9,11},{10,... | collective-permute-start | bytes 294920 | tf_op jit(solution)/shard_map/ppermute | solution.py:21
  29.0 4.6 %collective-permute-start.8 = (bf16[192,256]{1,0:T(8,128)(2,1)S(1)}, bf16[192,256]{1,0:T(8,128)(2,1)S(1)}, u32[]{:S(2)}, u32[]{:S(2)}) collective-permute-start(bf16[192,256]{1,0:T(8,128)(2,1)S(1)} %shard_map.81.refs_0_), channel_id=1, source_target_pairs={{0,1},{1,0},{2,3},{3,2},{4,5},{5,4},{6,7},{7,6},{8,9},{9,8},{10,11... | collective-permute-start | bytes 294920 | tf_op jit(solution)/shard_map/ppermute | solution.py:21
  35.1 10.4 %all-to-all-start = ((bf16[32,16,128]{2,1,0:T(8,128)(2,1)}), bf16[32,16,128]{2,1,0:T(8,128)(2,1)S(1)}, u32[]{:S(2)}, u32[]{:S(2)}) async-start(bf16[32,16,128]{2,1,0:T(8,128)(2,1)} %bitcast.1), calls=%async_computation | async-start | bytes 262144 | tf_op jit(solution)/shard_map/all_to_all | solution.py:310
  37.7 11.1 %collective-permute-start.12 = (bf16[64,512]{1,0:T(8,128)(2,1)S(1)}, bf16[64,512]{1,0:T(8,128)(2,1)S(1)}, u32[]{:S(2)}, u32[]{:S(2)}) collective-permute-start(bf16[64,512]{1,0:T(8,128)(2,1)S(1)} %get-tuple-element.24), channel_id=1, source_target_pairs={{0,1},{1,0},{2,3},{3,2},{4,5},{5,4},{6,7},{7,6},{8,9},{9,8},{10,11... | collective-permute-start | bytes 196616 | tf_op jit(solution)/shard_map/ppermute | solution.py:21
  39.6 9.3 %collective-permute-start.13 = (bf16[64,512]{1,0:T(8,128)(2,1)S(1)}, bf16[64,512]{1,0:T(8,128)(2,1)S(1)}, u32[]{:S(2)}, u32[]{:S(2)}) collective-permute-start(bf16[64,512]{1,0:T(8,128)(2,1)S(1)} %get-tuple-element.25), channel_id=1, source_target_pairs={{0,2},{1,3},{2,0},{3,1},{4,6},{5,7},{6,4},{7,5},{8,10},{9,11},{10,... | collective-permute-start | bytes 196616 | tf_op jit(solution)/shard_map/ppermute | solution.py:21
  41.0 7.8 %collective-permute-start.14 = (bf16[64,512]{1,0:T(8,128)(2,1)S(1)}, bf16[64,512]{1,0:T(8,128)(2,1)S(1)}, u32[]{:S(2)}, u32[]{:S(2)}) collective-permute-start(bf16[64,512]{1,0:T(8,128)(2,1)S(1)} %get-tuple-element.26), channel_id=1, source_target_pairs={{0,3},{1,2},{2,1},{3,0},{4,7},{5,6},{6,5},{7,4},{8,11},{9,10},{10,... | collective-permute-start | bytes 196616 | tf_op jit(solution)/shard_map/ppermute | solution.py:21
  46.3 10.3 %all-to-all-start.1 = ((f32[32,8,8]{2,1,0:T(8,128)}), f32[32,8,8]{2,1,0:T(8,128)S(1)}, u32[]{:S(2)}, u32[]{:S(2)}) async-start(f32[32,8,8]{2,1,0:T(8,128)} %shard_map.85), calls=%async_computation.1 | async-start | bytes 262144 | tf_op jit(solution)/shard_map/all_to_all | solution.py:321

commit v15 on v14

--- a/solution.py
+++ b/solution.py
@@ -50,20 +50,24 @@
 
 
 def first_kernel(states_hbm, gain_hbm, down_hbm, route_hbm, out_ref, *refs):
-    downs, (states_ref, gain_ref, route_ref, sems) = refs[:HOLDERS], refs[HOLDERS:]
-    depth, width = down_hbm.shape[0], downs[0].shape[1]
+    kept_ref, z_ref, early_ref, late_ref, states_ref, gain_ref, route_ref, sems = refs
+    depth, width = down_hbm.shape[0], kept_ref.shape[1]
+    count, late = depth + TILE, late_ref.shape[0] - TILE
+    blocks = (
+        (0, 0, depth, kept_ref.at[pl.ds(0, depth)]),
+        (2, 0, depth, z_ref.at[pl.ds(0, depth)]),
+        (3, 0, depth, early_ref.at[pl.ds(0, depth)]),
+        (1, 0, depth - late, early_ref.at[pl.ds(count, depth - late)]),
+        (1, depth - late, late, late_ref.at[pl.ds(0, late)]),
+    )
     copies = [
         pltpu.make_async_copy(states_hbm, states_ref, sems.at[0]),
         pltpu.make_async_copy(gain_hbm, gain_ref, sems.at[1]),
         pltpu.make_async_copy(route_hbm, route_ref, sems.at[2]),
     ]
-    for m, down_ref in enumerate(downs):
-        columns = columns_of(holder() ^ m, width)
-        copies.append(
-            pltpu.make_async_copy(
-                down_hbm.at[:, columns], down_ref.at[pl.ds(0, depth)], sems.at[3 + m]
-            )
-        )
+    for at, (m, top, size, block) in enumerate(blocks):
+        source = down_hbm.at[pl.ds(top, size), columns_of(holder() ^ m, width)]
+        copies.append(pltpu.make_async_copy(source, block, sems.at[3 + at]))
     for copy in copies:
         copy.start()
     for copy in copies[:3]:
@@ -80,8 +84,8 @@
     row = lax.broadcasted_iota(jnp.int32, (TILE, part), 0)
     terms = jnp.where(row == 0, high, jnp.where(row == 1, middle, jnp.where(row == 2, low, 0.0)))
     terms = jnp.concatenate([terms, jnp.zeros((TILE, width - part), f32)], 1)
-    for down_ref in downs:
-        down_ref[pl.ds(depth, TILE)] = terms.astype(bf16)
+    for ref, top in ((kept_ref, depth), (z_ref, depth), (early_ref, depth), (late_ref, late)):
+        ref[pl.ds(top, TILE)] = terms.astype(bf16)
     for copy in copies[3:]:
         copy.wait()
 
@@ -104,13 +108,13 @@
 def join_kernel(after_ref, first_ref, second_ref, out_ref):
     count = first_ref.shape[0]
     out_ref[:count] = first_ref[...]
-    out_ref[count:] = second_ref[...]
+    out_ref[count:] = second_ref[:count]
 
 
 def stack_kernel(after_ref, *refs):
     rows = refs[0].shape[0]
     z = lax.axis_index("tok") >> 1
-    for m, piece in enumerate(refs[:-1]):
+    for m, piece in enumerate(refs[-2::-1]):
         refs[-1][pl.ds(pl.multiple_of((z ^ m) * rows, rows), rows)] = piece[...]
 
 
@@ -145,12 +149,13 @@
 
 
 def features_kernel(*refs):
-    hidden_refs, (kept_ref, x_ref, z_ref) = refs[:HOLDERS], refs[HOLDERS : HOLDERS + 3]
-    block_refs, shares_hbm = refs[HOLDERS + 3 : 2 * HOLDERS + 3], refs[2 * HOLDERS + 3]
-    route_ref, features_ref, whole_ref, shares_ref, sem = refs[2 * HOLDERS + 4 :]
+    hidden_refs, (kept_ref, z_ref, early_ref, late_ref) = refs[:HOLDERS], refs[HOLDERS : 2 * HOLDERS]
+    block_refs, shares_hbm = refs[2 * HOLDERS : 3 * HOLDERS], refs[3 * HOLDERS]
+    route_ref, features_ref, whole_ref, shares_ref, sem = refs[3 * HOLDERS + 1 :]
     depth, tokens = hidden_refs[0].shape
     count = kept_ref.shape[0]
-    downs = (kept_ref[...], x_ref[...], z_ref[:count], z_ref[count:])
+    x_block = jnp.concatenate([early_ref[count:], late_ref[...]])
+    downs = (kept_ref[...], x_block, z_ref[:count], z_ref[count:])
     part, members = tokens // HOLDERS, lax.axis_size("tok")
     rows = tokens // members
 
@@ -243,10 +248,12 @@
     depth = gate_weight.shape[0]
     part, token_part = model // HOLDERS, tokens // HOLDERS
 
-    own, down_own, down_x, down_z, down_xz = call(
+    count = depth + TILE
+    late = depth // 2 // TILE * TILE + TILE
+    own, down_own, down_z, down_early, down_late = call(
         first_kernel,
         [jax.ShapeDtypeStruct((rows, model // 2), bf16)]
-        + [jax.ShapeDtypeStruct((depth + TILE, part), bf16)] * HOLDERS,
+        + [jax.ShapeDtypeStruct((n, part), bf16) for n in (count, count, 2 * count - late, late)],
         [HBM] * 4,
         [
             pltpu.with_memory_space_constraint(a, pltpu.HBM)
@@ -256,27 +263,27 @@
             pltpu.VMEM((rows, model), bf16),
             pltpu.VMEM((1, model), f32),
             pltpu.VMEM(route_weight.shape, f32),
-            pltpu.SemaphoreType.DMA((3 + HOLDERS,)),
+            pltpu.SemaphoreType.DMA((8,)),
         ],
     )
-    down_xz = swapped(down_xz, "tok", 1)
-    pieces = [swapped(own, "tok", 2 * m) if m else own for m in range(members // 2)]
+    down_early = swapped(down_early, "tok", 1)
+    pieces = [swapped(own, "tok", 2 * m) for m in range(members // 2 - 1, 0, -1)] + [own]
     near = call(
         stack_kernel,
         jax.ShapeDtypeStruct((tokens // 2, model // 2), bf16),
         [ANY] + [VMEM] * len(pieces),
-        (down_xz, *pieces),
+        (down_early, *pieces),
     )
     far = swapped(near, "tok", 1)
     near2 = swapped(near, "grp", 1)
     down_z = call(
         join_kernel,
-        jax.ShapeDtypeStruct((2 * (depth + TILE), part), bf16),
+        jax.ShapeDtypeStruct((2 * count, part), bf16),
         [ANY, VMEM, VMEM],
-        (near, down_z, down_xz),
+        (near, down_z, down_early),
     )
     down_z = swapped(down_z, "tok", 2)
-    down_x = swapped(held(down_x, far), "tok", 1)
+    down_late = swapped(held(down_late, far), "tok", 1)
     half_shape = (depth, tokens // 2)
     near_hidden, gate_part, up_part = call(
         near_kernel,
@@ -296,8 +303,8 @@
         features_kernel,
         [jax.ShapeDtypeStruct((token_part, part), bf16)] * HOLDERS
         + [jax.ShapeDtypeStruct((entries, LANES), bf16)],
-        [VMEM] * (HOLDERS + 3),
-        (*hiddens, down_own, down_x, down_z),
+        [VMEM] * (2 * HOLDERS),
+        (*hiddens, down_own, down_z, down_early, down_late),
         out_specs=[VMEM] * HOLDERS + [HBM],
         scratch=[
             pltpu.VMEM((tokens, LANES), f32),

time: 57.5 us -> 58 us (level)
  starting transfers between devices: 21.9 us -> 23.3 us
  waiting for transfers between devices: 28.4 us -> 27.5 us
    all_to_all x1, starting transfers between devices: 2.63 us -> 3.92 us  [shards(): lax.all_to_all(centered, ('grp', 'tok'), split_axis=0, concat_axis=0, til...]
    ppermute x15, waiting for transfers between devices: 17.3 us -> 16.3 us  [swapped(): lax.ppermute(array, axis, [(i, i ^ mask) for i in range(lax.axis_size(axi...]
where the time goes in v15:
time: 58 us; the launch traced here: 57.8 us
  waiting for transfers between devices  27.5 us (47%)
  starting transfers between devices  23.3 us (40%)
  Pallas kernels  6.25 us (11%)
  between operations  0.74 us (1%)
    ppermute x15, starting transfers between devices, swapped(): lax.ppermute(array, axis, [(i, i ^ mask) for i in range(lax.axis_size(axi...  16.8 us
    ppermute x15, waiting for transfers between devices, swapped(): lax.ppermute(array, axis, [(i, i ^ mask) for i in range(lax.axis_size(axi...  16.3 us
    all_to_all x1, waiting for transfers between devices, shards(): lax.all_to_all(tables, ('grp', 'tok'), split_axis=0, concat_axis=0, tiled...  6.96 us
    pallas_call x10, Pallas kernels, call(): pl.pallas_call(body, out_shape=outs, in_specs=in_specs, out_specs=jax.tre...  6.25 us
    all_to_all x1, waiting for transfers between devices, shards(): lax.all_to_all(centered, ('grp', 'tok'), split_axis=0, concat_axis=0, til...  4.19 us
    all_to_all x1, starting transfers between devices, shards(): lax.all_to_all(centered, ('grp', 'tok'), split_axis=0, concat_axis=0, til...  3.92 us
    all_to_all x1, starting transfers between devices, shards(): lax.all_to_all(tables, ('grp', 'tok'), split_axis=0, concat_axis=0, tiled...  2.56 us
  transfers between devices with their start and end apart: 17, of which 10 were waited for; matrix products, arithmetic and copies ran while one was open for 0% of the time, Pallas kernels for 5%

profile of v15, /device:TPU:0, one launch (start us, length us, event | category | flops | bytes accessed | tf_op | source)
XLA Modules:
  0.0 57.8 jit_solution(3994198811928839321)
XLA Ops:
  0.6 1.4 %shard_map.77 = (bf16[32,1024]{1,0:T(8,128)(2,1)S(1)}, bf16[208,512]{1,0:T(8,128)(2,1)S(1)}, bf16[208,512]{1,0:T(8,128)(2,1)S(1)}, bf16[304,512]{1,0:T(8,128)(2,1)S(1)}, bf16[112,512]{1,0:T(8,128)(2,1)S(1)}) custom-call(bf16[32,2048]{1,0:T(8,128)(2,1)} %states_hbm.1, f32[1,2048]{1,0:T(1,128)} %bitcast.4, bf16[192,2048]{1,0:T(8,128)(2,1)} %down_hbm.1, ...), custom_call_target="tpu_custom_call" | custom-call | tf_op jit(solution)/shard_map/pallas_call | solution.py:29
  2.0 3.0 %collective-permute-start = (bf16[304,512]{1,0:T(8,128)(2,1)S(1)}, bf16[304,512]{1,0:T(8,128)(2,1)S(1)}, u32[]{:S(2)}, u32[]{:S(2)}) collective-permute-start(bf16[304,512]{1,0:T(8,128)(2,1)S(1)} %get-tuple-element.15), channel_id=1, source_target_pairs={{0,1},{1,0},{2,3},{3,2},{4,5},{5,4},{6,7},{7,6},{8,9},{9,8},{10,11... | collective-permute-start | bytes 933896 | tf_op jit(solution)/shard_map/ppermute | solution.py:21
  5.0 3.6 %collective-permute-start.1 = (bf16[32,1024]{1,0:T(8,128)(2,1)S(1)}, bf16[32,1024]{1,0:T(8,128)(2,1)S(1)}, u32[]{:S(2)}, u32[]{:S(2)}) collective-permute-start(bf16[32,1024]{1,0:T(8,128)(2,1)S(1)} %get-tuple-element.16.refs_3_), channel_id=1, source_target_pairs={{0,6},{1,7},{2,4},{3,5},{4,2},{5,3},{6,0},{7,1},{8,14},{9,15},{10,... | collective-permute-start | bytes 196616 | tf_op jit(solution)/shard_map/ppermute | solution.py:21
  8.6 0.0 collective-permute-start.2
  8.6 0.8 %collective-permute-start.3 = (bf16[32,1024]{1,0:T(8,128)(2,1)S(1)}, bf16[32,1024]{1,0:T(8,128)(2,1)S(1)}, u32[]{:S(2)}, u32[]{:S(2)}) collective-permute-start(bf16[32,1024]{1,0:T(8,128)(2,1)S(1)} %get-tuple-element.16.refs_3_), channel_id=1, source_target_pairs={{0,2},{1,3},{2,0},{3,1},{4,6},{5,7},{6,4},{7,5},{8,10},{9,11},{10,... | collective-permute-start | bytes 196616 | tf_op jit(solution)/shard_map/ppermute | solution.py:21
  9.4 2.5 %collective-permute-done.1.refs_0_ = bf16[32,1024]{1,0:T(8,128)(2,1)S(1)} collective-permute-done((bf16[32,1024]{1,0:T(8,128)(2,1)S(1)}, bf16[32,1024]{1,0:T(8,128)(2,1)S(1)}, u32[]{:S(2)}, u32[]{:S(2)}) %collective-permute-start.1) | collective-permute-done | bytes 65568 | tf_op jit(solution)/shard_map/ppermute | solution.py:21
  11.9 2.1 %collective-permute-done.2.refs_1_ = bf16[32,1024]{1,0:T(8,128)(2,1)S(1)} collective-permute-done((bf16[32,1024]{1,0:T(8,128)(2,1)S(1)}, bf16[32,1024]{1,0:T(8,128)(2,1)S(1)}, u32[]{:S(2)}, u32[]{:S(2)}) %collective-permute-start.2) | collective-permute-done | bytes 65568 | tf_op jit(solution)/shard_map/ppermute | solution.py:21
  14.0 0.1 collective-permute-done.3.refs_2_
  14.0 0.0 collective-permute-done.after_ref.second_ref.refs_6_
  14.1 0.5 collective-permute-start.5
  14.6 0.0 copy-start
  14.6 0.0 copy-start.1
  14.6 1.3 %collective-permute-start.4 = (bf16[416,512]{1,0:T(8,128)(2,1)S(1)}, bf16[416,512]{1,0:T(8,128)(2,1)S(1)}, u32[]{:S(2)}, u32[]{:S(2)}) collective-permute-start(bf16[416,512]{1,0:T(8,128)(2,1)S(1)} %shard_map.79), channel_id=1, source_target_pairs={{0,2},{1,3},{2,0},{3,1},{4,6},{5,7},{6,4},{7,5},{8,10},{9,11},{10,... | collective-permute-start | bytes 1277960 | tf_op jit(solution)/shard_map/ppermute | solution.py:21
  15.9 0.0 collective-permute-start.7
  15.9 5.9 %collective-permute-done.5.far_ref.refs_1_ = bf16[128,1024]{1,0:T(8,128)(2,1)S(1)} collective-permute-done((bf16[128,1024]{1,0:T(8,128)(2,1)S(1)}, bf16[128,1024]{1,0:T(8,128)(2,1)S(1)}, u32[]{:S(2)}, u32[]{:S(2)}) %collective-permute-start.5) | collective-permute-done | bytes 262176 | tf_op jit(solution)/shard_map/ppermute | solution.py:21
  21.7 0.0 collective-permute-start.6
  21.7 0.5 collective-permute-start.11
  22.3 0.0 collective-permute-done.7.near2_ref
  22.3 0.0 copy-done
  22.3 0.0 copy-done.1
  22.3 0.8 %shard_map.80 = (bf16[192,128]{1,0:T(8,128)(2,1)S(1)}, f32[192,128]{1,0:T(8,128)S(1)}, f32[192,128]{1,0:T(8,128)S(1)}) custom-call(bf16[128,1024]{1,0:T(8,128)(2,1)S(1)} %shard_map.78.after_ref.near_ref, bf16[128,1024]{1,0:T(8,128)(2,1)S(1)} %collective-permute-done.7.near2_ref, bf16[128,1024]{1,0:T(8,128)(2,1)S(1)} %collective-permute-done.5.far_ref.refs_1_, ...), custom_call_target="tpu_custom_call" | custom-call | tf_op jit(solution)/shard_map/pallas_call | solution.py:29
  23.0 2.6 %collective-permute-done.4.after_ref.refs_5_ = bf16[416,512]{1,0:T(8,128)(2,1)S(1)} collective-permute-done((bf16[416,512]{1,0:T(8,128)(2,1)S(1)}, bf16[416,512]{1,0:T(8,128)(2,1)S(1)}, u32[]{:S(2)}, u32[]{:S(2)}) %collective-permute-start.4) | collective-permute-done | bytes 426016 | tf_op jit(solution)/shard_map/ppermute | solution.py:21
  25.6 0.0 collective-permute-done.6.far2_ref
  25.6 0.4 shard_map.81.refs_0_
  26.0 1.3 %collective-permute-start.10 = (bf16[192,256]{1,0:T(8,128)(2,1)S(1)}, bf16[192,256]{1,0:T(8,128)(2,1)S(1)}, u32[]{:S(2)}, u32[]{:S(2)}) collective-permute-start(bf16[192,256]{1,0:T(8,128)(2,1)S(1)} %shard_map.81.refs_0_), channel_id=1, source_target_pairs={{0,3},{1,2},{2,1},{3,0},{4,7},{5,6},{6,5},{7,4},{8,11},{9,10},{10,... | collective-permute-start | bytes 294920 | tf_op jit(solution)/shard_map/ppermute | solution.py:21
  27.3 0.9 %collective-permute-start.8 = (bf16[192,256]{1,0:T(8,128)(2,1)S(1)}, bf16[192,256]{1,0:T(8,128)(2,1)S(1)}, u32[]{:S(2)}, u32[]{:S(2)}) collective-permute-start(bf16[192,256]{1,0:T(8,128)(2,1)S(1)} %shard_map.81.refs_0_), channel_id=1, source_target_pairs={{0,1},{1,0},{2,3},{3,2},{4,5},{5,4},{6,7},{7,6},{8,9},{9,8},{10,11... | collective-permute-start | bytes 294920 | tf_op jit(solution)/shard_map/ppermute | solution.py:21
  28.2 1.3 %collective-permute-start.9 = (bf16[192,256]{1,0:T(8,128)(2,1)S(1)}, bf16[192,256]{1,0:T(8,128)(2,1)S(1)}, u32[]{:S(2)}, u32[]{:S(2)}) collective-permute-start(bf16[192,256]{1,0:T(8,128)(2,1)S(1)} %shard_map.81.refs_0_), channel_id=1, source_target_pairs={{0,2},{1,3},{2,0},{3,1},{4,6},{5,7},{6,4},{7,5},{8,10},{9,11},{10,... | collective-permute-start | bytes 294920 | tf_op jit(solution)/shard_map/ppermute | solution.py:21
  29.5 0.0 collective-permute-done.11.refs_7_
  29.5 2.1 %collective-permute-done.10.refs_3_ = bf16[192,256]{1,0:T(8,128)(2,1)S(1)} collective-permute-done((bf16[192,256]{1,0:T(8,128)(2,1)S(1)}, bf16[192,256]{1,0:T(8,128)(2,1)S(1)}, u32[]{:S(2)}, u32[]{:S(2)}) %collective-permute-start.10) | collective-permute-done | bytes 98336 | tf_op jit(solution)/shard_map/ppermute | solution.py:21
  31.6 1.0 %collective-permute-done.8.refs_1_ = bf16[192,256]{1,0:T(8,128)(2,1)S(1)} collective-permute-done((bf16[192,256]{1,0:T(8,128)(2,1)S(1)}, bf16[192,256]{1,0:T(8,128)(2,1)S(1)}, u32[]{:S(2)}, u32[]{:S(2)}) %collective-permute-start.8) | collective-permute-done | bytes 98336 | tf_op jit(solution)/shard_map/ppermute | solution.py:21
  32.6 0.2 collective-permute-done.9.refs_2_
  32.8 1.5 %shard_map.83 = (bf16[64,512]{1,0:T(8,128)(2,1)S(1)}, bf16[64,512]{1,0:T(8,128)(2,1)S(1)}, bf16[64,512]{1,0:T(8,128)(2,1)S(1)}, bf16[64,512]{1,0:T(8,128)(2,1)S(1)}, bf16[512,128]{1,0:T(8,128)(2,1)}) custom-call(bf16[192,256]{1,0:T(8,128)(2,1)S(1)} %shard_map.81.refs_0_, bf16[192,256]{1,0:T(8,128)(2,1)S(1)} %collective-permute-done.8.refs_1_, ...), custom_call_target="tpu_custom_call" | custom-call | tf_op jit(solution)/shard_map/pallas_call | solution.py:29
  34.3 3.9 %all-to-all-start = ((bf16[32,16,128]{2,1,0:T(8,128)(2,1)}), bf16[32,16,128]{2,1,0:T(8,128)(2,1)S(1)}, u32[]{:S(2)}, u32[]{:S(2)}) async-start(bf16[32,16,128]{2,1,0:T(8,128)(2,1)} %bitcast.1), calls=%async_computation | async-start | bytes 262144 | tf_op jit(solution)/shard_map/all_to_all | solution.py:317
  38.2 1.8 %collective-permute-start.12 = (bf16[64,512]{1,0:T(8,128)(2,1)S(1)}, bf16[64,512]{1,0:T(8,128)(2,1)S(1)}, u32[]{:S(2)}, u32[]{:S(2)}) collective-permute-start(bf16[64,512]{1,0:T(8,128)(2,1)S(1)} %get-tuple-element.24), channel_id=1, source_target_pairs={{0,1},{1,0},{2,3},{3,2},{4,5},{5,4},{6,7},{7,6},{8,9},{9,8},{10,11... | collective-permute-start | bytes 196616 | tf_op jit(solution)/shard_map/ppermute | solution.py:21
  40.0 1.5 %collective-permute-start.13 = (bf16[64,512]{1,0:T(8,128)(2,1)S(1)}, bf16[64,512]{1,0:T(8,128)(2,1)S(1)}, u32[]{:S(2)}, u32[]{:S(2)}) collective-permute-start(bf16[64,512]{1,0:T(8,128)(2,1)S(1)} %get-tuple-element.25), channel_id=1, source_target_pairs={{0,2},{1,3},{2,0},{3,1},{4,6},{5,7},{6,4},{7,5},{8,10},{9,11},{10,... | collective-permute-start | bytes 196616 | tf_op jit(solution)/shard_map/ppermute | solution.py:21
  41.5 0.3 collective-permute-start.14
  41.7 4.2 %all-to-all-done = bf16[32,16,128]{2,1,0:T(8,128)(2,1)S(1)} async-done(((bf16[32,16,128]{2,1,0:T(8,128)(2,1)}), bf16[32,16,128]{2,1,0:T(8,128)(2,1)S(1)}, u32[]{:S(2)}, u32[]{:S(2)}) %all-to-all-start) | async-done | bytes 131104 | tf_op jit(solution)/shard_map/all_to_all | solution.py:317
  45.9 0.8 %shard_map.85 = f32[32,8,8]{2,1,0:T(8,128)} custom-call(bf16[8,4,16,128]{3,2,1,0:T(8,128)(2,1)S(1)} %bitcast.3), custom_call_target="tpu_custom_call" | custom-call | tf_op jit(solution)/shard_map/pallas_call | solution.py:29
  46.7 2.6 %all-to-all-start.1 = ((f32[32,8,8]{2,1,0:T(8,128)}), f32[32,8,8]{2,1,0:T(8,128)S(1)}, u32[]{:S(2)}, u32[]{:S(2)}) async-start(f32[32,8,8]{2,1,0:T(8,128)} %shard_map.85), calls=%async_computation.1 | async-start | bytes 262144 | tf_op jit(solution)/shard_map/all_to_all | solution.py:328
  49.3 0.0 collective-permute-done.12.refs_1_
  49.3 0.0 collective-permute-done.13.refs_2_
  49.3 0.0 collective-permute-done.14.refs_3_
  49.3 0.7 %shard_map.84 = bf16[64,2048]{1,0:T(8,128)(2,1)} custom-call(bf16[64,512]{1,0:T(8,128)(2,1)S(1)} %get-tuple-element.23.refs_0_, bf16[64,512]{1,0:T(8,128)(2,1)S(1)} %collective-permute-done.12.refs_1_, bf16[64,512]{1,0:T(8,128)(2,1)S(1)} %collective-permute-done.13.refs_2_, bf16[64,512]{1,0:T(8,128)(2,1)S(1)} %collective-permute-done.14.refs_3_), custom_call_target="tpu_custom_call" | custom-call | tf_op jit(solution)/shard_map/pallas_call | solution.py:29
  50.1 7.0 %all-to-all-done.1.tables_ref = f32[32,8,8]{2,1,0:T(8,128)S(1)} async-done(((f32[32,8,8]{2,1,0:T(8,128)}), f32[32,8,8]{2,1,0:T(8,128)S(1)}, u32[]{:S(2)}, u32[]{:S(2)}) %all-to-all-start.1) | async-done | bytes 8224 | tf_op jit(solution)/shard_map/all_to_all | solution.py:328
  57.1 0.7 %shard_map.86 = f32[8,8]{1,0:T(8,128)} custom-call(f32[32,8,8]{2,1,0:T(8,128)S(1)} %all-to-all-done.1.tables_ref), custom_call_target="tpu_custom_call" | custom-call | tf_op jit(solution)/shard_map/pallas_call | solution.py:29
  (3 shorter events, 0.1 us)
Async XLA Ops:
  2.0 12.0 %collective-permute-start = (bf16[304,512]{1,0:T(8,128)(2,1)S(1)}, bf16[304,512]{1,0:T(8,128)(2,1)S(1)}, u32[]{:S(2)}, u32[]{:S(2)}) collective-permute-start(bf16[304,512]{1,0:T(8,128)(2,1)S(1)} %get-tuple-element.15), channel_id=1, source_target_pairs={{0,1},{1,0},{2,3},{3,2},{4,5},{5,4},{6,7},{7,6},{8,9},{9,8},{10,11... | collective-permute-start | bytes 933896 | tf_op jit(solution)/shard_map/ppermute | solution.py:21
  5.0 6.9 %collective-permute-start.1 = (bf16[32,1024]{1,0:T(8,128)(2,1)S(1)}, bf16[32,1024]{1,0:T(8,128)(2,1)S(1)}, u32[]{:S(2)}, u32[]{:S(2)}) collective-permute-start(bf16[32,1024]{1,0:T(8,128)(2,1)S(1)} %get-tuple-element.16.refs_3_), channel_id=1, source_target_pairs={{0,6},{1,7},{2,4},{3,5},{4,2},{5,3},{6,0},{7,1},{8,14},{9,15},{10,... | collective-permute-start | bytes 196616 | tf_op jit(solution)/shard_map/ppermute | solution.py:21
  8.6 5.4 %collective-permute-start.2 = (bf16[32,1024]{1,0:T(8,128)(2,1)S(1)}, bf16[32,1024]{1,0:T(8,128)(2,1)S(1)}, u32[]{:S(2)}, u32[]{:S(2)}) collective-permute-start(bf16[32,1024]{1,0:T(8,128)(2,1)S(1)} %get-tuple-element.16.refs_3_), channel_id=1, source_target_pairs={{0,4},{1,5},{2,6},{3,7},{4,0},{5,1},{6,2},{7,3},{8,12},{9,13},{10,... | collective-permute-start | bytes 196616 | tf_op jit(solution)/shard_map/ppermute | solution.py:21
  8.6 5.4 %collective-permute-start.3 = (bf16[32,1024]{1,0:T(8,128)(2,1)S(1)}, bf16[32,1024]{1,0:T(8,128)(2,1)S(1)}, u32[]{:S(2)}, u32[]{:S(2)}) collective-permute-start(bf16[32,1024]{1,0:T(8,128)(2,1)S(1)} %get-tuple-element.16.refs_3_), channel_id=1, source_target_pairs={{0,2},{1,3},{2,0},{3,1},{4,6},{5,7},{6,4},{7,5},{8,10},{9,11},{10,... | collective-permute-start | bytes 196616 | tf_op jit(solution)/shard_map/ppermute | solution.py:21
  14.1 7.7 %collective-permute-start.5 = (bf16[128,1024]{1,0:T(8,128)(2,1)S(1)}, bf16[128,1024]{1,0:T(8,128)(2,1)S(1)}, u32[]{:S(2)}, u32[]{:S(2)}) collective-permute-start(bf16[128,1024]{1,0:T(8,128)(2,1)S(1)} %shard_map.78.after_ref.near_ref), channel_id=1, source_target_pairs={{0,1},{1,0},{2,3},{3,2},{4,5},{5,4},{6,7},{7,6},{8,9},{9,8},{10,11... | collective-permute-start | bytes 786440 | tf_op jit(solution)/shard_map/ppermute | solution.py:21
  14.6 7.7 %copy-start = (bf16[192,2048]{1,0:T(8,128)(2,1)S(1)}, bf16[192,2048]{1,0:T(8,128)(2,1)}, u32[]{:S(2)}) copy-start(bf16[192,2048]{1,0:T(8,128)(2,1)} %gate_ref.3) | copy-start | bytes 2359300
  14.6 7.7 %copy-start.1 = (bf16[192,2048]{1,0:T(8,128)(2,1)S(1)}, bf16[192,2048]{1,0:T(8,128)(2,1)}, u32[]{:S(2)}) copy-start(bf16[192,2048]{1,0:T(8,128)(2,1)} %up_ref.3) | copy-start | bytes 2359300
  14.6 11.0 %collective-permute-start.4 = (bf16[416,512]{1,0:T(8,128)(2,1)S(1)}, bf16[416,512]{1,0:T(8,128)(2,1)S(1)}, u32[]{:S(2)}, u32[]{:S(2)}) collective-permute-start(bf16[416,512]{1,0:T(8,128)(2,1)S(1)} %shard_map.79), channel_id=1, source_target_pairs={{0,2},{1,3},{2,0},{3,1},{4,6},{5,7},{6,4},{7,5},{8,10},{9,11},{10,... | collective-permute-start | bytes 1277960 | tf_op jit(solution)/shard_map/ppermute | solution.py:21
  15.9 6.4 %collective-permute-start.7 = (bf16[128,1024]{1,0:T(8,128)(2,1)S(1)}, bf16[128,1024]{1,0:T(8,128)(2,1)S(1)}, u32[]{:S(2)}, u32[]{:S(2)}) collective-permute-start(bf16[128,1024]{1,0:T(8,128)(2,1)S(1)} %shard_map.78.after_ref.near_ref), channel_id=1, source_target_pairs={{0,8},{8,0},{16,24},{24,16},{1,9},{9,1},{17,25},{25,17},{2,10},{10... | collective-permute-start | bytes 786440 | tf_op jit(solution)/shard_map/ppermute | solution.py:21
  21.7 3.9 %collective-permute-start.6 = (bf16[128,1024]{1,0:T(8,128)(2,1)S(1)}, bf16[128,1024]{1,0:T(8,128)(2,1)S(1)}, u32[]{:S(2)}, u32[]{:S(2)}) collective-permute-start(bf16[128,1024]{1,0:T(8,128)(2,1)S(1)} %collective-permute-done.5.far_ref.refs_1_), channel_id=1, source_target_pairs={{0,8},{8,0},{16,24},{24,16},{1,9},{9,1},{17,25},{25,17},{2,10},{10... | collective-permute-start | bytes 786440 | tf_op jit(solution)/shard_map/ppermute | solution.py:21
  21.7 7.8 %collective-permute-start.11 = (bf16[112,512]{1,0:T(8,128)(2,1)S(1)}, bf16[112,512]{1,0:T(8,128)(2,1)S(1)}, u32[]{:S(2)}, u32[]{:S(2)}) collective-permute-start(bf16[112,512]{1,0:T(8,128)(2,1)S(1)} %shard_map.82), channel_id=1, source_target_pairs={{0,1},{1,0},{2,3},{3,2},{4,5},{5,4},{6,7},{7,6},{8,9},{9,8},{10,11... | collective-permute-start | bytes 344072 | tf_op jit(solution)/shard_map/ppermute | solution.py:21
  26.0 5.7 %collective-permute-start.10 = (bf16[192,256]{1,0:T(8,128)(2,1)S(1)}, bf16[192,256]{1,0:T(8,128)(2,1)S(1)}, u32[]{:S(2)}, u32[]{:S(2)}) collective-permute-start(bf16[192,256]{1,0:T(8,128)(2,1)S(1)} %shard_map.81.refs_0_), channel_id=1, source_target_pairs={{0,3},{1,2},{2,1},{3,0},{4,7},{5,6},{6,5},{7,4},{8,11},{9,10},{10,... | collective-permute-start | bytes 294920 | tf_op jit(solution)/shard_map/ppermute | solution.py:21
  27.3 5.3 %collective-permute-start.8 = (bf16[192,256]{1,0:T(8,128)(2,1)S(1)}, bf16[192,256]{1,0:T(8,128)(2,1)S(1)}, u32[]{:S(2)}, u32[]{:S(2)}) collective-permute-start(bf16[192,256]{1,0:T(8,128)(2,1)S(1)} %shard_map.81.refs_0_), channel_id=1, source_target_pairs={{0,1},{1,0},{2,3},{3,2},{4,5},{5,4},{6,7},{7,6},{8,9},{9,8},{10,11... | collective-permute-start | bytes 294920 | tf_op jit(solution)/shard_map/ppermute | solution.py:21
  28.2 4.6 %collective-permute-start.9 = (bf16[192,256]{1,0:T(8,128)(2,1)S(1)}, bf16[192,256]{1,0:T(8,128)(2,1)S(1)}, u32[]{:S(2)}, u32[]{:S(2)}) collective-permute-start(bf16[192,256]{1,0:T(8,128)(2,1)S(1)} %shard_map.81.refs_0_), channel_id=1, source_target_pairs={{0,2},{1,3},{2,0},{3,1},{4,6},{5,7},{6,4},{7,5},{8,10},{9,11},{10,... | collective-permute-start | bytes 294920 | tf_op jit(solution)/shard_map/ppermute | solution.py:21
  34.3 11.7 %all-to-all-start = ((bf16[32,16,128]{2,1,0:T(8,128)(2,1)}), bf16[32,16,128]{2,1,0:T(8,128)(2,1)S(1)}, u32[]{:S(2)}, u32[]{:S(2)}) async-start(bf16[32,16,128]{2,1,0:T(8,128)(2,1)} %bitcast.1), calls=%async_computation | async-start | bytes 262144 | tf_op jit(solution)/shard_map/all_to_all | solution.py:317
  38.2 11.1 %collective-permute-start.12 = (bf16[64,512]{1,0:T(8,128)(2,1)S(1)}, bf16[64,512]{1,0:T(8,128)(2,1)S(1)}, u32[]{:S(2)}, u32[]{:S(2)}) collective-permute-start(bf16[64,512]{1,0:T(8,128)(2,1)S(1)} %get-tuple-element.24), channel_id=1, source_target_pairs={{0,1},{1,0},{2,3},{3,2},{4,5},{5,4},{6,7},{7,6},{8,9},{9,8},{10,11... | collective-permute-start | bytes 196616 | tf_op jit(solution)/shard_map/ppermute | solution.py:21
  40.0 9.3 %collective-permute-start.13 = (bf16[64,512]{1,0:T(8,128)(2,1)S(1)}, bf16[64,512]{1,0:T(8,128)(2,1)S(1)}, u32[]{:S(2)}, u32[]{:S(2)}) collective-permute-start(bf16[64,512]{1,0:T(8,128)(2,1)S(1)} %get-tuple-element.25), channel_id=1, source_target_pairs={{0,2},{1,3},{2,0},{3,1},{4,6},{5,7},{6,4},{7,5},{8,10},{9,11},{10,... | collective-permute-start | bytes 196616 | tf_op jit(solution)/shard_map/ppermute | solution.py:21
  41.5 7.8 %collective-permute-start.14 = (bf16[64,512]{1,0:T(8,128)(2,1)S(1)}, bf16[64,512]{1,0:T(8,128)(2,1)S(1)}, u32[]{:S(2)}, u32[]{:S(2)}) collective-permute-start(bf16[64,512]{1,0:T(8,128)(2,1)S(1)} %get-tuple-element.26), channel_id=1, source_target_pairs={{0,3},{1,2},{2,1},{3,0},{4,7},{5,6},{6,5},{7,4},{8,11},{9,10},{10,... | collective-permute-start | bytes 196616 | tf_op jit(solution)/shard_map/ppermute | solution.py:21
  46.7 10.3 %all-to-all-start.1 = ((f32[32,8,8]{2,1,0:T(8,128)}), f32[32,8,8]{2,1,0:T(8,128)S(1)}, u32[]{:S(2)}, u32[]{:S(2)}) async-start(f32[32,8,8]{2,1,0:T(8,128)} %shard_map.85), calls=%async_computation.1 | async-start | bytes 262144 | tf_op jit(solution)/shard_map/all_to_all | solution.py:328

commit v16 on v14

--- a/solution.py
+++ b/solution.py
@@ -110,7 +110,7 @@
 def stack_kernel(after_ref, *refs):
     rows = refs[0].shape[0]
     z = lax.axis_index("tok") >> 1
-    for m, piece in enumerate(refs[:-1]):
+    for m, piece in enumerate(refs[-2::-1]):
         refs[-1][pl.ds(pl.multiple_of((z ^ m) * rows, rows), rows)] = piece[...]
 
 
@@ -194,19 +194,8 @@
     copy.wait()
 
 
-def place_kernel(*refs):
-    blocks, out_ref, sems = refs[:HOLDERS], refs[HOLDERS], refs[HOLDERS + 1]
-    width = blocks[0].shape[1]
-    copies = []
-    for m, block in enumerate(blocks):
-        columns = pl.ds(pl.multiple_of((holder() ^ m) * width, width), width)
-        copies.append(pltpu.make_async_copy(block, out_ref.at[:, columns], sems.at[m]))
-        copies[-1].start()
-    for copy in copies:
-        copy.wait()
-
-
-def pair_kernel(parts_ref, out_ref, flat_ref):
+def pair_kernel(*refs):
+    parts_ref, out_ref, flat_ref = refs[HOLDERS:]
     copies, experts, _ = out_ref.shape
     parts = parts_ref[...].astype(f32)
     total = parts[:, 0]
@@ -224,7 +213,14 @@
         out_ref[copy] = table
 
 
-def cka_kernel(tables_ref, out_ref):
+def last_kernel(tables_ref, *refs):
+    blocks, (features_ref, out_ref, sems) = refs[:HOLDERS], refs[HOLDERS:]
+    width = blocks[0].shape[1]
+    copies = []
+    for m, block in enumerate(blocks):
+        columns = columns_of(holder() ^ m, width)
+        copies.append(pltpu.make_async_copy(block, features_ref.at[:, columns], sems.at[m]))
+        copies[-1].start()
     totals = jnp.sum(tables_ref[...], axis=0)
     shape = totals.shape
     eye = lax.broadcasted_iota(jnp.int32, shape, 0) == lax.broadcasted_iota(jnp.int32, shape, 1)
@@ -232,6 +228,8 @@
     down = jnp.sum(kept, axis=1, keepdims=True)
     across = jnp.sum(kept, axis=0, keepdims=True)
     out_ref[...] = totals / jnp.sqrt(down * across)
+    for copy in copies:
+        copy.wait()
 
 
 def shards(probe_states, norm_gain, gate_weight, up_weight, down_weight, route_weight):
@@ -260,7 +258,7 @@
         ],
     )
     down_xz = swapped(down_xz, "tok", 1)
-    pieces = [swapped(own, "tok", 2 * m) if m else own for m in range(members // 2)]
+    pieces = [swapped(own, "tok", 2 * m) for m in range(members // 2 - 1, 0, -1)] + [own]
     near = call(
         stack_kernel,
         jax.ShapeDtypeStruct((tokens // 2, model // 2), bf16),
@@ -309,30 +307,30 @@
     )
     arrived = lax.all_to_all(centered, ("grp", "tok"), split_axis=0, concat_axis=0, tiled=True)
     arrived = arrived.reshape(experts, HOLDERS, entries // devices, LANES)
+    blocks = [swapped(b, "tok", m) if m else b for m, b in enumerate(blocks)]
     direct = devices * experts * experts <= 1 << 16
     tables = call(
         pair_kernel,
         jax.ShapeDtypeStruct((devices if direct else 1, experts, experts), f32),
-        [VMEM],
-        (arrived,),
+        [ANY] * HOLDERS + [VMEM],
+        (*blocks, arrived),
         scratch=[pltpu.VMEM((experts, entries // devices, LANES), f32)],
     )
     if direct:
         tables = lax.all_to_all(tables, ("grp", "tok"), split_axis=0, concat_axis=0, tiled=True)
     else:
         tables = lax.psum(tables, ("grp", "tok"))
-    cka = call(cka_kernel, jax.ShapeDtypeStruct((experts, experts), f32), [VMEM], (tables,))
-
-    blocks = [swapped(b, "tok", m) if m else b for m, b in enumerate(blocks)]
-    features = call(
-        place_kernel,
-        jax.ShapeDtypeStruct((token_part, model), bf16),
-        [VMEM] * HOLDERS,
-        blocks,
-        out_specs=ANY,
+    return call(
+        last_kernel,
+        (
+            jax.ShapeDtypeStruct((token_part, model), bf16),
+            jax.ShapeDtypeStruct((experts, experts), f32),
+        ),
+        [VMEM] * (HOLDERS + 1),
+        (tables, *blocks),
+        out_specs=(HBM, VMEM),
         scratch=[pltpu.SemaphoreType.DMA((HOLDERS,))],
     )
-    return (features, cka)
 
 
 def solution(mesh):

time: 57.5 us -> 60.2 us (1.047)
  blocking collectives: 0 us -> 11.7 us
  waiting for transfers between devices: 28.4 us -> 23.2 us
  starting transfers between devices: 21.9 us -> 18.9 us
  Pallas kernels: 6.26 us -> 5.49 us
    all_to_all x0 -> x1, blocking collectives: none -> 11.7 us  [shards(): lax.all_to_all(tables, ('grp', 'tok'), split_axis=0, concat_axis=0, tiled...]
    all_to_all x1 -> x0, waiting for transfers between devices: 6.96 us -> none  [shards(): lax.all_to_all(tables, ('grp', 'tok'), split_axis=0, concat_axis=0, tiled...]
    ppermute x15, waiting for transfers between devices: 17.3 us -> 23.2 us  [swapped(): lax.ppermute(array, axis, [(i, i ^ mask) for i in range(lax.axis_size(axi...]
    all_to_all x1, waiting for transfers between devices: 4.19 us -> 0.01 us  [shards(): lax.all_to_all(centered, ('grp', 'tok'), split_axis=0, concat_axis=0, til...]
    all_to_all x1 -> x0, starting transfers between devices: 2.56 us -> none  [shards(): lax.all_to_all(tables, ('grp', 'tok'), split_axis=0, concat_axis=0, tiled...]
    ppermute x15, starting transfers between devices: 16.7 us -> 15.8 us  [swapped(): lax.ppermute(array, axis, [(i, i ^ mask) for i in range(lax.axis_size(axi...]
    pallas_call x10 -> x9, Pallas kernels: 6.26 us -> 5.49 us  [call(): pl.pallas_call(body, out_shape=outs, in_specs=in_specs, out_specs=jax.tre...]
  transfers between devices with their start and end apart: 17 -> 16, of which waited for: 10 -> 10; matrix products, arithmetic and copies ran while one was open for 0% -> 0% of each run, Pallas kernels for 5% -> 2%
where the time goes in v16:
time: 60.2 us; the launch traced here: 60 us
  waiting for transfers between devices  23.2 us (39%)
  starting transfers between devices  18.9 us (31%)
  blocking collectives  11.7 us (19%)
  Pallas kernels  5.49 us (9%)
  between operations  0.72 us (1%)
    ppermute x15, waiting for transfers between devices, swapped(): lax.ppermute(array, axis, [(i, i ^ mask) for i in range(lax.axis_size(axi...  23.2 us
    ppermute x15, starting transfers between devices, swapped(): lax.ppermute(array, axis, [(i, i ^ mask) for i in range(lax.axis_size(axi...  15.8 us
    all_to_all x1, blocking collectives, shards(): lax.all_to_all(tables, ('grp', 'tok'), split_axis=0, concat_axis=0, tiled...  11.7 us
    pallas_call x9, Pallas kernels, call(): pl.pallas_call(body, out_shape=outs, in_specs=in_specs, out_specs=jax.tre...  5.49 us
    all_to_all x1, starting transfers between devices, shards(): lax.all_to_all(centered, ('grp', 'tok'), split_axis=0, concat_axis=0, til...  3.12 us
  transfers between devices with their start and end apart: 16, of which 10 were waited for; matrix products, arithmetic and copies ran while one was open for 0% of the time, Pallas kernels for 2%

profile of v16, /device:TPU:0, one launch (start us, length us, event | category | flops | bytes accessed | tf_op | source)
XLA Modules:
  0.0 60.0 jit_solution(16414777047519459413)
XLA Ops:
  0.6 1.3 %shard_map.77 = (bf16[32,1024]{1,0:T(8,128)(2,1)S(1)}, bf16[208,512]{1,0:T(8,128)(2,1)S(1)}, bf16[208,512]{1,0:T(8,128)(2,1)S(1)}, bf16[208,512]{1,0:T(8,128)(2,1)S(1)}, bf16[208,512]{1,0:T(8,128)(2,1)S(1)}) custom-call(bf16[32,2048]{1,0:T(8,128)(2,1)} %states_hbm.1, f32[1,2048]{1,0:T(1,128)} %bitcast.4, bf16[192,2048]{1,0:T(8,128)(2,1)} %down_hbm.1, ...), custom_call_target="tpu_custom_call" | custom-call | tf_op jit(solution)/shard_map/pallas_call | solution.py:29
  2.0 3.0 %collective-permute-start = (bf16[208,512]{1,0:T(8,128)(2,1)S(1)}, bf16[208,512]{1,0:T(8,128)(2,1)S(1)}, u32[]{:S(2)}, u32[]{:S(2)}) collective-permute-start(bf16[208,512]{1,0:T(8,128)(2,1)S(1)} %get-tuple-element.15), channel_id=1, source_target_pairs={{0,1},{1,0},{2,3},{3,2},{4,5},{5,4},{6,7},{7,6},{8,9},{9,8},{10,11... | collective-permute-start | bytes 638984 | tf_op jit(solution)/shard_map/ppermute | solution.py:21
  5.0 1.6 %collective-permute-start.3 = (bf16[32,1024]{1,0:T(8,128)(2,1)S(1)}, bf16[32,1024]{1,0:T(8,128)(2,1)S(1)}, u32[]{:S(2)}, u32[]{:S(2)}) collective-permute-start(bf16[32,1024]{1,0:T(8,128)(2,1)S(1)} %get-tuple-element.16.refs_3_), channel_id=1, source_target_pairs={{0,2},{1,3},{2,0},{3,1},{4,6},{5,7},{6,4},{7,5},{8,10},{9,11},{10,... | collective-permute-start | bytes 196616 | tf_op jit(solution)/shard_map/ppermute | solution.py:21
  6.6 2.6 %collective-permute-start.2 = (bf16[32,1024]{1,0:T(8,128)(2,1)S(1)}, bf16[32,1024]{1,0:T(8,128)(2,1)S(1)}, u32[]{:S(2)}, u32[]{:S(2)}) collective-permute-start(bf16[32,1024]{1,0:T(8,128)(2,1)S(1)} %get-tuple-element.16.refs_3_), channel_id=1, source_target_pairs={{0,4},{1,5},{2,6},{3,7},{4,0},{5,1},{6,2},{7,3},{8,12},{9,13},{10,... | collective-permute-start | bytes 196616 | tf_op jit(solution)/shard_map/ppermute | solution.py:21
  9.2 0.2 collective-permute-start.1
  9.4 0.0 collective-permute-done.3.refs_2_
  9.4 4.2 %collective-permute-done.2.refs_1_ = bf16[32,1024]{1,0:T(8,128)(2,1)S(1)} collective-permute-done((bf16[32,1024]{1,0:T(8,128)(2,1)S(1)}, bf16[32,1024]{1,0:T(8,128)(2,1)S(1)}, u32[]{:S(2)}, u32[]{:S(2)}) %collective-permute-start.2) | collective-permute-done | bytes 65568 | tf_op jit(solution)/shard_map/ppermute | solution.py:21
  13.5 1.7 %collective-permute-done.1.refs_0_ = bf16[32,1024]{1,0:T(8,128)(2,1)S(1)} collective-permute-done((bf16[32,1024]{1,0:T(8,128)(2,1)S(1)}, bf16[32,1024]{1,0:T(8,128)(2,1)S(1)}, u32[]{:S(2)}, u32[]{:S(2)}) %collective-permute-start.1) | collective-permute-done | bytes 65568 | tf_op jit(solution)/shard_map/ppermute | solution.py:21
  15.2 0.0 collective-permute-done.after_ref.second_ref
  15.3 0.6 collective-permute-start.5
  15.9 0.0 copy-start
  15.9 0.0 copy-start.1
  15.9 0.1 collective-permute-start.4
  16.0 0.1 collective-permute-start.7
  16.0 5.6 %collective-permute-done.5.far_ref.refs_1_ = bf16[128,1024]{1,0:T(8,128)(2,1)S(1)} collective-permute-done((bf16[128,1024]{1,0:T(8,128)(2,1)S(1)}, bf16[128,1024]{1,0:T(8,128)(2,1)S(1)}, u32[]{:S(2)}, u32[]{:S(2)}) %collective-permute-start.5) | collective-permute-done | bytes 262176 | tf_op jit(solution)/shard_map/ppermute | solution.py:21
  21.7 0.0 collective-permute-start.6
  21.7 0.5 collective-permute-start.11
  22.2 0.0 collective-permute-done.7.near2_ref
  22.2 0.0 copy-done
  22.2 0.0 copy-done.1
  22.2 0.8 %shard_map.80 = (bf16[192,128]{1,0:T(8,128)(2,1)S(1)}, f32[192,128]{1,0:T(8,128)S(1)}, f32[192,128]{1,0:T(8,128)S(1)}) custom-call(bf16[128,1024]{1,0:T(8,128)(2,1)S(1)} %shard_map.78.after_ref.near_ref, bf16[128,1024]{1,0:T(8,128)(2,1)S(1)} %collective-permute-done.7.near2_ref, bf16[128,1024]{1,0:T(8,128)(2,1)S(1)} %collective-permute-done.5.far_ref.refs_1_, ...), custom_call_target="tpu_custom_call" | custom-call | tf_op jit(solution)/shard_map/pallas_call | solution.py:29
  23.0 2.3 %collective-permute-done.4.after_ref.refs_6_ = bf16[416,512]{1,0:T(8,128)(2,1)S(1)} collective-permute-done((bf16[416,512]{1,0:T(8,128)(2,1)S(1)}, bf16[416,512]{1,0:T(8,128)(2,1)S(1)}, u32[]{:S(2)}, u32[]{:S(2)}) %collective-permute-start.4) | collective-permute-done | bytes 426016 | tf_op jit(solution)/shard_map/ppermute | solution.py:21
  25.3 0.0 collective-permute-done.6.far2_ref
  25.3 0.4 shard_map.81.refs_0_
  25.7 1.3 %collective-permute-start.10 = (bf16[192,256]{1,0:T(8,128)(2,1)S(1)}, bf16[192,256]{1,0:T(8,128)(2,1)S(1)}, u32[]{:S(2)}, u32[]{:S(2)}) collective-permute-start(bf16[192,256]{1,0:T(8,128)(2,1)S(1)} %shard_map.81.refs_0_), channel_id=1, source_target_pairs={{0,3},{1,2},{2,1},{3,0},{4,7},{5,6},{6,5},{7,4},{8,11},{9,10},{10,... | collective-permute-start | bytes 294920 | tf_op jit(solution)/shard_map/ppermute | solution.py:21
  27.0 1.7 %collective-permute-start.9 = (bf16[192,256]{1,0:T(8,128)(2,1)S(1)}, bf16[192,256]{1,0:T(8,128)(2,1)S(1)}, u32[]{:S(2)}, u32[]{:S(2)}) collective-permute-start(bf16[192,256]{1,0:T(8,128)(2,1)S(1)} %shard_map.81.refs_0_), channel_id=1, source_target_pairs={{0,2},{1,3},{2,0},{3,1},{4,6},{5,7},{6,4},{7,5},{8,10},{9,11},{10,... | collective-permute-start | bytes 294920 | tf_op jit(solution)/shard_map/ppermute | solution.py:21
  28.7 0.5 collective-permute-start.8
  29.3 2.6 %collective-permute-done.11.refs_5_ = bf16[208,512]{1,0:T(8,128)(2,1)S(1)} collective-permute-done((bf16[208,512]{1,0:T(8,128)(2,1)S(1)}, bf16[208,512]{1,0:T(8,128)(2,1)S(1)}, u32[]{:S(2)}, u32[]{:S(2)}) %collective-permute-start.11) | collective-permute-done | bytes 213024 | tf_op jit(solution)/shard_map/ppermute | solution.py:21
  31.9 0.0 collective-permute-done.10.refs_3_
  31.9 0.6 collective-permute-done.9.refs_2_
  32.4 1.1 %collective-permute-done.8.refs_1_ = bf16[192,256]{1,0:T(8,128)(2,1)S(1)} collective-permute-done((bf16[192,256]{1,0:T(8,128)(2,1)S(1)}, bf16[192,256]{1,0:T(8,128)(2,1)S(1)}, u32[]{:S(2)}, u32[]{:S(2)}) %collective-permute-start.8) | collective-permute-done | bytes 98336 | tf_op jit(solution)/shard_map/ppermute | solution.py:21
  33.6 1.5 %shard_map.83 = (bf16[64,512]{1,0:T(8,128)(2,1)S(1)}, bf16[64,512]{1,0:T(8,128)(2,1)S(1)}, bf16[64,512]{1,0:T(8,128)(2,1)S(1)}, bf16[64,512]{1,0:T(8,128)(2,1)S(1)}, bf16[512,128]{1,0:T(8,128)(2,1)}) custom-call(bf16[192,256]{1,0:T(8,128)(2,1)S(1)} %shard_map.81.refs_0_, bf16[192,256]{1,0:T(8,128)(2,1)S(1)} %collective-permute-done.8.refs_1_, ...), custom_call_target="tpu_custom_call" | custom-call | tf_op jit(solution)/shard_map/pallas_call | solution.py:29
  35.0 3.1 %all-to-all-start = ((bf16[32,16,128]{2,1,0:T(8,128)(2,1)}), bf16[32,16,128]{2,1,0:T(8,128)(2,1)S(1)}, u32[]{:S(2)}, u32[]{:S(2)}) async-start(bf16[32,16,128]{2,1,0:T(8,128)(2,1)} %bitcast.1), calls=%async_computation | async-start | bytes 262144 | tf_op jit(solution)/shard_map/all_to_all | solution.py:308
  38.2 1.8 %collective-permute-start.12 = (bf16[64,512]{1,0:T(8,128)(2,1)S(1)}, bf16[64,512]{1,0:T(8,128)(2,1)S(1)}, u32[]{:S(2)}, u32[]{:S(2)}) collective-permute-start(bf16[64,512]{1,0:T(8,128)(2,1)S(1)} %get-tuple-element.24), channel_id=1, source_target_pairs={{0,1},{1,0},{2,3},{3,2},{4,5},{5,4},{6,7},{7,6},{8,9},{9,8},{10,11... | collective-permute-start | bytes 196616 | tf_op jit(solution)/shard_map/ppermute | solution.py:21
  40.0 1.5 %collective-permute-start.13 = (bf16[64,512]{1,0:T(8,128)(2,1)S(1)}, bf16[64,512]{1,0:T(8,128)(2,1)S(1)}, u32[]{:S(2)}, u32[]{:S(2)}) collective-permute-start(bf16[64,512]{1,0:T(8,128)(2,1)S(1)} %get-tuple-element.25), channel_id=1, source_target_pairs={{0,2},{1,3},{2,0},{3,1},{4,6},{5,7},{6,4},{7,5},{8,10},{9,11},{10,... | collective-permute-start | bytes 196616 | tf_op jit(solution)/shard_map/ppermute | solution.py:21
  41.5 0.3 collective-permute-start.14
  41.7 1.5 %collective-permute-done.12.refs_1_ = bf16[64,512]{1,0:T(8,128)(2,1)S(1)} collective-permute-done((bf16[64,512]{1,0:T(8,128)(2,1)S(1)}, bf16[64,512]{1,0:T(8,128)(2,1)S(1)}, u32[]{:S(2)}, u32[]{:S(2)}) %collective-permute-start.12) | collective-permute-done | bytes 65568 | tf_op jit(solution)/shard_map/ppermute | solution.py:21
  43.2 2.3 %collective-permute-done.13.refs_2_ = bf16[64,512]{1,0:T(8,128)(2,1)S(1)} collective-permute-done((bf16[64,512]{1,0:T(8,128)(2,1)S(1)}, bf16[64,512]{1,0:T(8,128)(2,1)S(1)}, u32[]{:S(2)}, u32[]{:S(2)}) %collective-permute-start.13) | collective-permute-done | bytes 65568 | tf_op jit(solution)/shard_map/ppermute | solution.py:21
  45.6 1.3 %collective-permute-done.14.refs_3_ = bf16[64,512]{1,0:T(8,128)(2,1)S(1)} collective-permute-done((bf16[64,512]{1,0:T(8,128)(2,1)S(1)}, bf16[64,512]{1,0:T(8,128)(2,1)S(1)}, u32[]{:S(2)}, u32[]{:S(2)}) %collective-permute-start.14) | collective-permute-done | bytes 65568 | tf_op jit(solution)/shard_map/ppermute | solution.py:21
  46.8 0.0 all-to-all-done
  46.9 0.2 shard_map.84
  47.0 11.7 %all_to_all.14.tables_ref = f32[32,8,8]{2,1,0:T(8,128)S(1)} all-to-all(f32[32,8,8]{2,1,0:T(8,128)S(1)} %shard_map.84), channel_id=1, replica_groups=mesh['grp'=4,'tok'=8] {'grp','tok'}, dimensions={0} | all-to-all | bytes 16384 | tf_op jit(solution)/shard_map/all_to_all | solution.py:320
  58.7 1.3 %shard_map.85 = (bf16[64,2048]{1,0:T(8,128)(2,1)}, f32[8,8]{1,0:T(8,128)}) custom-call(f32[32,8,8]{2,1,0:T(8,128)S(1)} %all_to_all.14.tables_ref, bf16[64,512]{1,0:T(8,128)(2,1)S(1)} %get-tuple-element.23.refs_0_, bf16[64,512]{1,0:T(8,128)(2,1)S(1)} %collective-permute-done.12.refs_1_, bf16[64,512]{1,0:T(8,128)(2,1)S(1)} %collective-permute-done.13.refs_2_, ...), custom_call_target="tpu_custom_call" | custom-call | tf_op jit(solution)/shard_map/pallas_call | solution.py:29
  (3 shorter events, 0.1 us)
Async XLA Ops:
  2.0 13.2 %collective-permute-start = (bf16[208,512]{1,0:T(8,128)(2,1)S(1)}, bf16[208,512]{1,0:T(8,128)(2,1)S(1)}, u32[]{:S(2)}, u32[]{:S(2)}) collective-permute-start(bf16[208,512]{1,0:T(8,128)(2,1)S(1)} %get-tuple-element.15), channel_id=1, source_target_pairs={{0,1},{1,0},{2,3},{3,2},{4,5},{5,4},{6,7},{7,6},{8,9},{9,8},{10,11... | collective-permute-start | bytes 638984 | tf_op jit(solution)/shard_map/ppermute | solution.py:21
  5.0 4.4 %collective-permute-start.3 = (bf16[32,1024]{1,0:T(8,128)(2,1)S(1)}, bf16[32,1024]{1,0:T(8,128)(2,1)S(1)}, u32[]{:S(2)}, u32[]{:S(2)}) collective-permute-start(bf16[32,1024]{1,0:T(8,128)(2,1)S(1)} %get-tuple-element.16.refs_3_), channel_id=1, source_target_pairs={{0,2},{1,3},{2,0},{3,1},{4,6},{5,7},{6,4},{7,5},{8,10},{9,11},{10,... | collective-permute-start | bytes 196616 | tf_op jit(solution)/shard_map/ppermute | solution.py:21
  6.6 7.0 %collective-permute-start.2 = (bf16[32,1024]{1,0:T(8,128)(2,1)S(1)}, bf16[32,1024]{1,0:T(8,128)(2,1)S(1)}, u32[]{:S(2)}, u32[]{:S(2)}) collective-permute-start(bf16[32,1024]{1,0:T(8,128)(2,1)S(1)} %get-tuple-element.16.refs_3_), channel_id=1, source_target_pairs={{0,4},{1,5},{2,6},{3,7},{4,0},{5,1},{6,2},{7,3},{8,12},{9,13},{10,... | collective-permute-start | bytes 196616 | tf_op jit(solution)/shard_map/ppermute | solution.py:21
  9.2 6.1 %collective-permute-start.1 = (bf16[32,1024]{1,0:T(8,128)(2,1)S(1)}, bf16[32,1024]{1,0:T(8,128)(2,1)S(1)}, u32[]{:S(2)}, u32[]{:S(2)}) collective-permute-start(bf16[32,1024]{1,0:T(8,128)(2,1)S(1)} %get-tuple-element.16.refs_3_), channel_id=1, source_target_pairs={{0,6},{1,7},{2,4},{3,5},{4,2},{5,3},{6,0},{7,1},{8,14},{9,15},{10,... | collective-permute-start | bytes 196616 | tf_op jit(solution)/shard_map/ppermute | solution.py:21
  15.3 6.4 %collective-permute-start.5 = (bf16[128,1024]{1,0:T(8,128)(2,1)S(1)}, bf16[128,1024]{1,0:T(8,128)(2,1)S(1)}, u32[]{:S(2)}, u32[]{:S(2)}) collective-permute-start(bf16[128,1024]{1,0:T(8,128)(2,1)S(1)} %shard_map.78.after_ref.near_ref), channel_id=1, source_target_pairs={{0,1},{1,0},{2,3},{3,2},{4,5},{5,4},{6,7},{7,6},{8,9},{9,8},{10,11... | collective-permute-start | bytes 786440 | tf_op jit(solution)/shard_map/ppermute | solution.py:21
  15.9 6.4 %copy-start = (bf16[192,2048]{1,0:T(8,128)(2,1)S(1)}, bf16[192,2048]{1,0:T(8,128)(2,1)}, u32[]{:S(2)}) copy-start(bf16[192,2048]{1,0:T(8,128)(2,1)} %gate_ref.3) | copy-start | bytes 2359300
  15.9 6.4 %copy-start.1 = (bf16[192,2048]{1,0:T(8,128)(2,1)S(1)}, bf16[192,2048]{1,0:T(8,128)(2,1)}, u32[]{:S(2)}) copy-start(bf16[192,2048]{1,0:T(8,128)(2,1)} %up_ref.3) | copy-start | bytes 2359300
  15.9 9.5 %collective-permute-start.4 = (bf16[416,512]{1,0:T(8,128)(2,1)S(1)}, bf16[416,512]{1,0:T(8,128)(2,1)S(1)}, u32[]{:S(2)}, u32[]{:S(2)}) collective-permute-start(bf16[416,512]{1,0:T(8,128)(2,1)S(1)} %shard_map.79), channel_id=1, source_target_pairs={{0,2},{1,3},{2,0},{3,1},{4,6},{5,7},{6,4},{7,5},{8,10},{9,11},{10,... | collective-permute-start | bytes 1277960 | tf_op jit(solution)/shard_map/ppermute | solution.py:21
  16.0 6.3 %collective-permute-start.7 = (bf16[128,1024]{1,0:T(8,128)(2,1)S(1)}, bf16[128,1024]{1,0:T(8,128)(2,1)S(1)}, u32[]{:S(2)}, u32[]{:S(2)}) collective-permute-start(bf16[128,1024]{1,0:T(8,128)(2,1)S(1)} %shard_map.78.after_ref.near_ref), channel_id=1, source_target_pairs={{0,8},{8,0},{16,24},{24,16},{1,9},{9,1},{17,25},{25,17},{2,10},{10... | collective-permute-start | bytes 786440 | tf_op jit(solution)/shard_map/ppermute | solution.py:21
  21.7 3.7 %collective-permute-start.6 = (bf16[128,1024]{1,0:T(8,128)(2,1)S(1)}, bf16[128,1024]{1,0:T(8,128)(2,1)S(1)}, u32[]{:S(2)}, u32[]{:S(2)}) collective-permute-start(bf16[128,1024]{1,0:T(8,128)(2,1)S(1)} %collective-permute-done.5.far_ref.refs_1_), channel_id=1, source_target_pairs={{0,8},{8,0},{16,24},{24,16},{1,9},{9,1},{17,25},{25,17},{2,10},{10... | collective-permute-start | bytes 786440 | tf_op jit(solution)/shard_map/ppermute | solution.py:21
  21.7 10.2 %collective-permute-start.11 = (bf16[208,512]{1,0:T(8,128)(2,1)S(1)}, bf16[208,512]{1,0:T(8,128)(2,1)S(1)}, u32[]{:S(2)}, u32[]{:S(2)}) collective-permute-start(bf16[208,512]{1,0:T(8,128)(2,1)S(1)} %shard_map.82), channel_id=1, source_target_pairs={{0,1},{1,0},{2,3},{3,2},{4,5},{5,4},{6,7},{7,6},{8,9},{9,8},{10,11... | collective-permute-start | bytes 638984 | tf_op jit(solution)/shard_map/ppermute | solution.py:21
  25.7 6.1 %collective-permute-start.10 = (bf16[192,256]{1,0:T(8,128)(2,1)S(1)}, bf16[192,256]{1,0:T(8,128)(2,1)S(1)}, u32[]{:S(2)}, u32[]{:S(2)}) collective-permute-start(bf16[192,256]{1,0:T(8,128)(2,1)S(1)} %shard_map.81.refs_0_), channel_id=1, source_target_pairs={{0,3},{1,2},{2,1},{3,0},{4,7},{5,6},{6,5},{7,4},{8,11},{9,10},{10,... | collective-permute-start | bytes 294920 | tf_op jit(solution)/shard_map/ppermute | solution.py:21
  27.0 5.4 %collective-permute-start.9 = (bf16[192,256]{1,0:T(8,128)(2,1)S(1)}, bf16[192,256]{1,0:T(8,128)(2,1)S(1)}, u32[]{:S(2)}, u32[]{:S(2)}) collective-permute-start(bf16[192,256]{1,0:T(8,128)(2,1)S(1)} %shard_map.81.refs_0_), channel_id=1, source_target_pairs={{0,2},{1,3},{2,0},{3,1},{4,6},{5,7},{6,4},{7,5},{8,10},{9,11},{10,... | collective-permute-start | bytes 294920 | tf_op jit(solution)/shard_map/ppermute | solution.py:21
  28.7 4.8 %collective-permute-start.8 = (bf16[192,256]{1,0:T(8,128)(2,1)S(1)}, bf16[192,256]{1,0:T(8,128)(2,1)S(1)}, u32[]{:S(2)}, u32[]{:S(2)}) collective-permute-start(bf16[192,256]{1,0:T(8,128)(2,1)S(1)} %shard_map.81.refs_0_), channel_id=1, source_target_pairs={{0,1},{1,0},{2,3},{3,2},{4,5},{5,4},{6,7},{7,6},{8,9},{9,8},{10,11... | collective-permute-start | bytes 294920 | tf_op jit(solution)/shard_map/ppermute | solution.py:21
  35.0 11.8 %all-to-all-start = ((bf16[32,16,128]{2,1,0:T(8,128)(2,1)}), bf16[32,16,128]{2,1,0:T(8,128)(2,1)S(1)}, u32[]{:S(2)}, u32[]{:S(2)}) async-start(bf16[32,16,128]{2,1,0:T(8,128)(2,1)} %bitcast.1), calls=%async_computation | async-start | bytes 262144 | tf_op jit(solution)/shard_map/all_to_all | solution.py:308
  38.2 5.1 %collective-permute-start.12 = (bf16[64,512]{1,0:T(8,128)(2,1)S(1)}, bf16[64,512]{1,0:T(8,128)(2,1)S(1)}, u32[]{:S(2)}, u32[]{:S(2)}) collective-permute-start(bf16[64,512]{1,0:T(8,128)(2,1)S(1)} %get-tuple-element.24), channel_id=1, source_target_pairs={{0,1},{1,0},{2,3},{3,2},{4,5},{5,4},{6,7},{7,6},{8,9},{9,8},{10,11... | collective-permute-start | bytes 196616 | tf_op jit(solution)/shard_map/ppermute | solution.py:21
  40.0 5.6 %collective-permute-start.13 = (bf16[64,512]{1,0:T(8,128)(2,1)S(1)}, bf16[64,512]{1,0:T(8,128)(2,1)S(1)}, u32[]{:S(2)}, u32[]{:S(2)}) collective-permute-start(bf16[64,512]{1,0:T(8,128)(2,1)S(1)} %get-tuple-element.25), channel_id=1, source_target_pairs={{0,2},{1,3},{2,0},{3,1},{4,6},{5,7},{6,4},{7,5},{8,10},{9,11},{10,... | collective-permute-start | bytes 196616 | tf_op jit(solution)/shard_map/ppermute | solution.py:21
  41.5 5.4 %collective-permute-start.14 = (bf16[64,512]{1,0:T(8,128)(2,1)S(1)}, bf16[64,512]{1,0:T(8,128)(2,1)S(1)}, u32[]{:S(2)}, u32[]{:S(2)}) collective-permute-start(bf16[64,512]{1,0:T(8,128)(2,1)S(1)} %get-tuple-element.26), channel_id=1, source_target_pairs={{0,3},{1,2},{2,1},{3,0},{4,7},{5,6},{6,5},{7,4},{8,11},{9,10},{10,... | collective-permute-start | bytes 196616 | tf_op jit(solution)/shard_map/ppermute | solution.py:21

commit v17 on v15

--- a/solution.py
+++ b/solution.py
@@ -50,15 +50,22 @@
 
 
 def first_kernel(states_hbm, gain_hbm, down_hbm, route_hbm, out_ref, *refs):
-    kept_ref, z_ref, early_ref, late_ref, states_ref, gain_ref, route_ref, sems = refs
+    with_z_ref, kept_ref, z_ref, early_ref, late_ref = refs[:5]
+    states_ref, gain_ref, route_ref, sems = refs[5:]
     depth, width = down_hbm.shape[0], kept_ref.shape[1]
-    count, late = depth + TILE, late_ref.shape[0] - TILE
+    rows, count = states_ref.shape[0], depth + TILE
+    beside, first_x = with_z_ref.shape[0] - rows, early_ref.shape[0] - count
+    left, right = with_z_ref.at[pl.ds(rows, beside), pl.ds(0, width)], with_z_ref.at[
+        pl.ds(rows, beside), pl.ds(width, width)
+    ]
     blocks = (
         (0, 0, depth, kept_ref.at[pl.ds(0, depth)]),
-        (2, 0, depth, z_ref.at[pl.ds(0, depth)]),
+        (2, 0, beside, left),
+        (2, beside, beside, right),
+        (2, 2 * beside, depth - 2 * beside, z_ref.at[pl.ds(0, depth - 2 * beside)]),
         (3, 0, depth, early_ref.at[pl.ds(0, depth)]),
-        (1, 0, depth - late, early_ref.at[pl.ds(count, depth - late)]),
-        (1, depth - late, late, late_ref.at[pl.ds(0, late)]),
+        (1, 0, first_x, early_ref.at[pl.ds(count, first_x)]),
+        (1, first_x, depth - first_x, late_ref.at[pl.ds(0, depth - first_x)]),
     )
     copies = [
         pltpu.make_async_copy(states_hbm, states_ref, sems.at[0]),
@@ -75,7 +82,9 @@
     states = states_ref[...].astype(f32)
     scale = lax.rsqrt(jnp.mean(states * states, axis=1, keepdims=True) + 1e-06)
     own = columns_of(core(), out_ref.shape[1])
-    out_ref[...] = (states_ref[:, own].astype(f32) * scale * gain_ref[:, own]).astype(bf16)
+    normed = (states_ref[:, own].astype(f32) * scale * gain_ref[:, own]).astype(bf16)
+    out_ref[...] = normed
+    with_z_ref[:rows] = normed
     route = route_ref[...]
     high = route.astype(bf16).astype(f32)
     middle = (route - high).astype(bf16).astype(f32)
@@ -84,8 +93,13 @@
     row = lax.broadcasted_iota(jnp.int32, (TILE, part), 0)
     terms = jnp.where(row == 0, high, jnp.where(row == 1, middle, jnp.where(row == 2, low, 0.0)))
     terms = jnp.concatenate([terms, jnp.zeros((TILE, width - part), f32)], 1)
-    for ref, top in ((kept_ref, depth), (z_ref, depth), (early_ref, depth), (late_ref, late)):
-        ref[pl.ds(top, TILE)] = terms.astype(bf16)
+    for ref, top in (
+        (kept_ref, depth),
+        (z_ref, depth - 2 * beside),
+        (early_ref, depth),
+        (late_ref, depth - first_x),
+    ):
+        ref[top : top + TILE] = terms.astype(bf16)
     for copy in copies[3:]:
         copy.wait()
 
@@ -108,14 +122,14 @@
 def join_kernel(after_ref, first_ref, second_ref, out_ref):
     count = first_ref.shape[0]
     out_ref[:count] = first_ref[...]
-    out_ref[count:] = second_ref[:count]
+    out_ref[count:] = second_ref[: out_ref.shape[0] - count]
 
 
 def stack_kernel(after_ref, *refs):
-    rows = refs[0].shape[0]
+    rows = refs[-2].shape[0]
     z = lax.axis_index("tok") >> 1
     for m, piece in enumerate(refs[-2::-1]):
-        refs[-1][pl.ds(pl.multiple_of((z ^ m) * rows, rows), rows)] = piece[...]
+        refs[-1][pl.ds(pl.multiple_of((z ^ m) * rows, rows), rows)] = piece[:rows]
 
 
 def gated(gate, upward):
@@ -149,15 +163,19 @@
 
 
 def features_kernel(*refs):
-    hidden_refs, (kept_ref, z_ref, early_ref, late_ref) = refs[:HOLDERS], refs[HOLDERS : 2 * HOLDERS]
-    block_refs, shares_hbm = refs[2 * HOLDERS : 3 * HOLDERS], refs[3 * HOLDERS]
-    route_ref, features_ref, whole_ref, shares_ref, sem = refs[3 * HOLDERS + 1 :]
+    hidden_refs, (kept_ref, with_z_ref, z_ref, early_ref, late_ref) = refs[:HOLDERS], refs[HOLDERS:][:5]
+    block_refs, shares_hbm = refs[HOLDERS + 5 : 2 * HOLDERS + 5], refs[2 * HOLDERS + 5]
+    route_ref, features_ref, whole_ref, shares_ref, sem = refs[2 * HOLDERS + 6 :]
     depth, tokens = hidden_refs[0].shape
-    count = kept_ref.shape[0]
-    x_block = jnp.concatenate([early_ref[count:], late_ref[...]])
-    downs = (kept_ref[...], x_block, z_ref[:count], z_ref[count:])
     part, members = tokens // HOLDERS, lax.axis_size("tok")
     rows = tokens // members
+    count, width = kept_ref.shape
+    beside = (2 * count - z_ref.shape[0]) // 2
+    x_block = jnp.concatenate([early_ref[count:], late_ref[...]])
+    z_block = jnp.concatenate(
+        [with_z_ref[rows:, :width], with_z_ref[rows:, width:], z_ref[: count - 2 * beside]]
+    )
+    downs = (kept_ref[...], x_block, z_block, z_ref[count - 2 * beside :])
 
     def place(m, piece):
         z = (holder() ^ m) * (members // HOLDERS // 2) + piece // 2
@@ -249,11 +267,14 @@
     part, token_part = model // HOLDERS, tokens // HOLDERS
 
     count = depth + TILE
-    late = depth // 2 // TILE * TILE + TILE
-    own, down_own, down_z, down_early, down_late = call(
+    beside, first_x = depth // 4 // TILE * TILE, depth // 4 // TILE * TILE
+    own, with_z, down_own, down_z, down_early, down_late = call(
         first_kernel,
-        [jax.ShapeDtypeStruct((rows, model // 2), bf16)]
-        + [jax.ShapeDtypeStruct((n, part), bf16) for n in (count, count, 2 * count - late, late)],
+        [jax.ShapeDtypeStruct((n, model // 2), bf16) for n in (rows, rows + beside)]
+        + [
+            jax.ShapeDtypeStruct((n, part), bf16)
+            for n in (count, count - 2 * beside, count + first_x, count - first_x)
+        ],
         [HBM] * 4,
         [
             pltpu.with_memory_space_constraint(a, pltpu.HBM)
@@ -263,11 +284,12 @@
             pltpu.VMEM((rows, model), bf16),
             pltpu.VMEM((1, model), f32),
             pltpu.VMEM(route_weight.shape, f32),
-            pltpu.SemaphoreType.DMA((8,)),
+            pltpu.SemaphoreType.DMA((10,)),
         ],
     )
     down_early = swapped(down_early, "tok", 1)
-    pieces = [swapped(own, "tok", 2 * m) for m in range(members // 2 - 1, 0, -1)] + [own]
+    with_z = swapped(with_z, "tok", 2)
+    pieces = [swapped(own, "tok", 2 * m) for m in range(members // 2 - 1, 1, -1)] + [with_z, own]
     near = call(
         stack_kernel,
         jax.ShapeDtypeStruct((tokens // 2, model // 2), bf16),
@@ -278,7 +300,7 @@
     near2 = swapped(near, "grp", 1)
     down_z = call(
         join_kernel,
-        jax.ShapeDtypeStruct((2 * count, part), bf16),
+        jax.ShapeDtypeStruct((2 * (count - beside), part), bf16),
         [ANY, VMEM, VMEM],
         (near, down_z, down_early),
     )
@@ -303,8 +325,8 @@
         features_kernel,
         [jax.ShapeDtypeStruct((token_part, part), bf16)] * HOLDERS
         + [jax.ShapeDtypeStruct((entries, LANES), bf16)],
-        [VMEM] * (2 * HOLDERS),
-        (*hiddens, down_own, down_z, down_early, down_late),
+        [VMEM] * (HOLDERS + 5),
+        (*hiddens, down_own, with_z, down_z, down_early, down_late),
         out_specs=[VMEM] * HOLDERS + [HBM],
         scratch=[
             pltpu.VMEM((tokens, LANES), f32),

time: 58 us -> 57.7 us (level)
  starting transfers between devices: 23.3 us -> 21.5 us
  waiting for transfers between devices: 27.5 us -> 28.9 us
    ppermute x15, waiting for transfers between devices: 16.3 us -> 17.8 us  [swapped(): lax.ppermute(array, axis, [(i, i ^ mask) for i in range(lax.axis_size(axi...]
    ppermute x15, starting transfers between devices: 16.8 us -> 15.8 us  [swapped(): lax.ppermute(array, axis, [(i, i ^ mask) for i in range(lax.axis_size(axi...]
    all_to_all x1, starting transfers between devices: 3.92 us -> 3.15 us  [shards(): lax.all_to_all(centered, ('grp', 'tok'), split_axis=0, concat_axis=0, til...]
  transfers between devices with their start and end apart: 17 -> 17, of which waited for: 10 -> 8; matrix products, arithmetic and copies ran while one was open for 0% -> 0% of each run, Pallas kernels for 5% -> 5%
where the time goes in v17:
time: 57.7 us; the launch traced here: 57.4 us
  waiting for transfers between devices  28.9 us (50%)
  starting transfers between devices  21.5 us (37%)
  Pallas kernels  6.28 us (11%)
  between operations  0.75 us (1%)
    ppermute x15, waiting for transfers between devices, swapped(): lax.ppermute(array, axis, [(i, i ^ mask) for i in range(lax.axis_size(axi...  17.8 us
    ppermute x15, starting transfers between devices, swapped(): lax.ppermute(array, axis, [(i, i ^ mask) for i in range(lax.axis_size(axi...  15.8 us
    all_to_all x1, waiting for transfers between devices, shards(): lax.all_to_all(tables, ('grp', 'tok'), split_axis=0, concat_axis=0, tiled...  6.96 us
    pallas_call x10, Pallas kernels, call(): pl.pallas_call(body, out_shape=outs, in_specs=in_specs, out_specs=jax.tre...  6.28 us
    all_to_all x1, waiting for transfers between devices, shards(): lax.all_to_all(centered, ('grp', 'tok'), split_axis=0, concat_axis=0, til...  4.19 us
    all_to_all x1, starting transfers between devices, shards(): lax.all_to_all(centered, ('grp', 'tok'), split_axis=0, concat_axis=0, til...  3.15 us
    all_to_all x1, starting transfers between devices, shards(): lax.all_to_all(tables, ('grp', 'tok'), split_axis=0, concat_axis=0, tiled...  2.56 us
  transfers between devices with their start and end apart: 17, of which 8 were waited for; matrix products, arithmetic and copies ran while one was open for 0% of the time, Pallas kernels for 5%

profile of v17, /device:TPU:0, one launch (start us, length us, event | category | flops | bytes accessed | tf_op | source)
XLA Modules:
  0.0 57.4 jit_solution(4786859735918815546)
XLA Ops:
  0.6 1.4 %shard_map.77 = (bf16[32,1024]{1,0:T(8,128)(2,1)S(1)}, bf16[80,1024]{1,0:T(8,128)(2,1)S(1)}, bf16[208,512]{1,0:T(8,128)(2,1)S(1)}, bf16[112,512]{1,0:T(8,128)(2,...) custom-call(bf16[32,2048]{1,0:T(8,128)(2,1)} %states_hbm.1, f32[1,2048]{1,0:T(1,128)} %bitcast.4, ...), custom_call_target="tpu_custom_call" | custom-call | tf_op jit(solution)/shard_map/pallas_call | solution.py:29
  2.0 3.0 %collective-permute-start = (bf16[256,512]{1,0:T(8,128)(2,1)S(1)}, bf16[256,512]{1,0:T(8,128)(2,1)S(1)}, u32[]{:S(2)}, u32[]{:S(2)}) collective-permute-start(bf16[256,512]{1,0:T(8,128)(2,1)S(1)} %get-tuple-element.16), channel_id=1, source_target_pairs={{0,1},{1,0},{2,3},{3,2},{4,5},{5,4},{6,7},{7,6},{8,9},{9,8},{10,11... | collective-permute-start | bytes 786440 | tf_op jit(solution)/shard_map/ppermute | solution.py:21
  5.0 1.6 %collective-permute-start.3 = (bf16[80,1024]{1,0:T(8,128)(2,1)S(1)}, bf16[80,1024]{1,0:T(8,128)(2,1)S(1)}, u32[]{:S(2)}, u32[]{:S(2)}) collective-permute-start(bf16[80,1024]{1,0:T(8,128)(2,1)S(1)} %get-tuple-element.18), channel_id=1, source_target_pairs={{0,2},{1,3},{2,0},{3,1},{4,6},{5,7},{6,4},{7,5},{8,10},{9,11},{10,... | collective-permute-start | bytes 491528 | tf_op jit(solution)/shard_map/ppermute | solution.py:21
  6.6 2.5 %collective-permute-start.1 = (bf16[32,1024]{1,0:T(8,128)(2,1)S(1)}, bf16[32,1024]{1,0:T(8,128)(2,1)S(1)}, u32[]{:S(2)}, u32[]{:S(2)}) collective-permute-start(bf16[32,1024]{1,0:T(8,128)(2,1)S(1)} %get-tuple-element.17.refs_3_), channel_id=1, source_target_pairs={{0,6},{1,7},{2,4},{3,5},{4,2},{5,3},{6,0},{7,1},{8,14},{9,15},{10,... | collective-permute-start | bytes 196616 | tf_op jit(solution)/shard_map/ppermute | solution.py:21
  9.1 0.1 collective-permute-start.2
  9.2 5.7 %collective-permute-done.1.refs_0_ = bf16[32,1024]{1,0:T(8,128)(2,1)S(1)} collective-permute-done((bf16[32,1024]{1,0:T(8,128)(2,1)S(1)}, bf16[32,1024]{1,0:T(8,128)(2,1)S(1)}, u32[]{:S(2)}, u32[]{:S(2)}) %collective-permute-start.1) | collective-permute-done | bytes 65568 | tf_op jit(solution)/shard_map/ppermute | solution.py:21
  14.9 1.0 %collective-permute-done.2.refs_1_ = bf16[32,1024]{1,0:T(8,128)(2,1)S(1)} collective-permute-done((bf16[32,1024]{1,0:T(8,128)(2,1)S(1)}, bf16[32,1024]{1,0:T(8,128)(2,1)S(1)}, u32[]{:S(2)}, u32[]{:S(2)}) %collective-permute-start.2) | collective-permute-done | bytes 65568 | tf_op jit(solution)/shard_map/ppermute | solution.py:21
  15.9 0.0 collective-permute-done.3.refs_2_.refs_5_
  15.9 0.0 collective-permute-done.after_ref.second_ref.refs_7_
  15.9 0.0 copy-start.1
  15.9 0.0 copy-start
  16.0 0.6 %collective-permute-start.5 = (bf16[128,1024]{1,0:T(8,128)(2,1)S(1)}, bf16[128,1024]{1,0:T(8,128)(2,1)S(1)}, u32[]{:S(2)}, u32[]{:S(2)}) collective-permute-start(bf16[128,1024]{1,0:T(8,128)(2,1)S(1)} %shard_map.78.after_ref.near_ref), channel_id=1, source_target_pairs={{0,1},{1,0},{2,3},{3,2},{4,5},{5,4},{6,7},{7,6},{8,9},{9,8},{10,11... | collective-permute-start | bytes 786440 | tf_op jit(solution)/shard_map/ppermute | solution.py:21
  16.6 0.3 collective-permute-start.4
  16.9 0.0 collective-permute-start.7
  16.9 5.5 %collective-permute-done.5.far_ref.refs_1_ = bf16[128,1024]{1,0:T(8,128)(2,1)S(1)} collective-permute-done((bf16[128,1024]{1,0:T(8,128)(2,1)S(1)}, bf16[128,1024]{1,0:T(8,128)(2,1)S(1)}, u32[]{:S(2)}, u32[]{:S(2)}) %collective-permute-start.5) | collective-permute-done | bytes 262176 | tf_op jit(solution)/shard_map/ppermute | solution.py:21
  22.4 0.0 collective-permute-start.6
  22.4 0.5 collective-permute-start.11
  22.9 0.0 collective-permute-done.7.near2_ref
  22.9 0.0 copy-done.1
  22.9 0.0 copy-done
  22.9 0.8 %shard_map.80 = (bf16[192,128]{1,0:T(8,128)(2,1)S(1)}, f32[192,128]{1,0:T(8,128)S(1)}, f32[192,128]{1,0:T(8,128)S(1)}) custom-call(bf16[128,1024]{1,0:T(8,128)(2,1)S(1)} %shard_map.78.after_ref.near_ref, bf16[128,1024]{1,0:T(8,128)(2,1)S(1)} %collective-permute-done.7.near2_ref, bf16[128,1024]{1,0:T(8,128)(2,1)S(1)} %collective-permute-done.5.far_ref.refs_1_, ...), custom_call_target="tpu_custom_call" | custom-call | tf_op jit(solution)/shard_map/pallas_call | solution.py:29
  23.7 0.0 collective-permute-done.4.after_ref.refs_6_
  23.7 0.2 collective-permute-done.6.far2_ref
  23.9 0.4 shard_map.81.refs_0_
  24.3 1.6 %collective-permute-start.10 = (bf16[192,256]{1,0:T(8,128)(2,1)S(1)}, bf16[192,256]{1,0:T(8,128)(2,1)S(1)}, u32[]{:S(2)}, u32[]{:S(2)}) collective-permute-start(bf16[192,256]{1,0:T(8,128)(2,1)S(1)} %shard_map.81.refs_0_), channel_id=1, source_target_pairs={{0,3},{1,2},{2,1},{3,0},{4,7},{5,6},{6,5},{7,4},{8,11},{9,10},{10,... | collective-permute-start | bytes 294920 | tf_op jit(solution)/shard_map/ppermute | solution.py:21
  25.9 0.5 collective-permute-start.8
  26.4 1.4 %collective-permute-start.9 = (bf16[192,256]{1,0:T(8,128)(2,1)S(1)}, bf16[192,256]{1,0:T(8,128)(2,1)S(1)}, u32[]{:S(2)}, u32[]{:S(2)}) collective-permute-start(bf16[192,256]{1,0:T(8,128)(2,1)S(1)} %shard_map.81.refs_0_), channel_id=1, source_target_pairs={{0,2},{1,3},{2,0},{3,1},{4,6},{5,7},{6,4},{7,5},{8,10},{9,11},{10,... | collective-permute-start | bytes 294920 | tf_op jit(solution)/shard_map/ppermute | solution.py:21
  27.9 3.6 %collective-permute-done.11.refs_8_ = bf16[160,512]{1,0:T(8,128)(2,1)S(1)} collective-permute-done((bf16[160,512]{1,0:T(8,128)(2,1)S(1)}, bf16[160,512]{1,0:T(8,128)(2,1)S(1)}, u32[]{:S(2)}, u32[]{:S(2)}) %collective-permute-start.11) | collective-permute-done | bytes 163872 | tf_op jit(solution)/shard_map/ppermute | solution.py:21
  31.5 0.0 collective-permute-done.10.refs_3_
  31.5 1.7 %collective-permute-done.8.refs_1_ = bf16[192,256]{1,0:T(8,128)(2,1)S(1)} collective-permute-done((bf16[192,256]{1,0:T(8,128)(2,1)S(1)}, bf16[192,256]{1,0:T(8,128)(2,1)S(1)}, u32[]{:S(2)}, u32[]{:S(2)}) %collective-permute-start.8) | collective-permute-done | bytes 98336 | tf_op jit(solution)/shard_map/ppermute | solution.py:21
  33.2 0.0 collective-permute-done.9.refs_2_
  33.2 1.5 %shard_map.83 = (bf16[64,512]{1,0:T(8,128)(2,1)S(1)}, bf16[64,512]{1,0:T(8,128)(2,1)S(1)}, bf16[64,512]{1,0:T(8,128)(2,1)S(1)}, bf16[64,512]{1,0:T(8,128)(2,1)S(1)}, bf16[512,128]{1,0:T(8,128)(2,1)}) custom-call(bf16[192,256]{1,0:T(8,128)(2,1)S(1)} %shard_map.81.refs_0_, bf16[192,256]{1,0:T(8,128)(2,1)S(1)} %collective-permute-done.8.refs_1_, ...), custom_call_target="tpu_custom_call" | custom-call | tf_op jit(solution)/shard_map/pallas_call | solution.py:29
  34.7 3.2 %all-to-all-start = ((bf16[32,16,128]{2,1,0:T(8,128)(2,1)}), bf16[32,16,128]{2,1,0:T(8,128)(2,1)S(1)}, u32[]{:S(2)}, u32[]{:S(2)}) async-start(bf16[32,16,128]{2,1,0:T(8,128)(2,1)} %bitcast.1), calls=%async_computation | async-start | bytes 262144 | tf_op jit(solution)/shard_map/all_to_all | solution.py:339
  37.9 1.8 %collective-permute-start.12 = (bf16[64,512]{1,0:T(8,128)(2,1)S(1)}, bf16[64,512]{1,0:T(8,128)(2,1)S(1)}, u32[]{:S(2)}, u32[]{:S(2)}) collective-permute-start(bf16[64,512]{1,0:T(8,128)(2,1)S(1)} %get-tuple-element.26), channel_id=1, source_target_pairs={{0,1},{1,0},{2,3},{3,2},{4,5},{5,4},{6,7},{7,6},{8,9},{9,8},{10,11... | collective-permute-start | bytes 196616 | tf_op jit(solution)/shard_map/ppermute | solution.py:21
  39.7 1.5 %collective-permute-start.13 = (bf16[64,512]{1,0:T(8,128)(2,1)S(1)}, bf16[64,512]{1,0:T(8,128)(2,1)S(1)}, u32[]{:S(2)}, u32[]{:S(2)}) collective-permute-start(bf16[64,512]{1,0:T(8,128)(2,1)S(1)} %get-tuple-element.27), channel_id=1, source_target_pairs={{0,2},{1,3},{2,0},{3,1},{4,6},{5,7},{6,4},{7,5},{8,10},{9,11},{10,... | collective-permute-start | bytes 196616 | tf_op jit(solution)/shard_map/ppermute | solution.py:21
  41.2 0.3 collective-permute-start.14
  41.4 4.2 %all-to-all-done = bf16[32,16,128]{2,1,0:T(8,128)(2,1)S(1)} async-done(((bf16[32,16,128]{2,1,0:T(8,128)(2,1)}), bf16[32,16,128]{2,1,0:T(8,128)(2,1)S(1)}, u32[]{:S(2)}, u32[]{:S(2)}) %all-to-all-start) | async-done | bytes 131104 | tf_op jit(solution)/shard_map/all_to_all | solution.py:339
  45.6 0.8 %shard_map.85 = f32[32,8,8]{2,1,0:T(8,128)} custom-call(bf16[8,4,16,128]{3,2,1,0:T(8,128)(2,1)S(1)} %bitcast.3), custom_call_target="tpu_custom_call" | custom-call | tf_op jit(solution)/shard_map/pallas_call | solution.py:29
  46.4 2.6 %all-to-all-start.1 = ((f32[32,8,8]{2,1,0:T(8,128)}), f32[32,8,8]{2,1,0:T(8,128)S(1)}, u32[]{:S(2)}, u32[]{:S(2)}) async-start(f32[32,8,8]{2,1,0:T(8,128)} %shard_map.85), calls=%async_computation.1 | async-start | bytes 262144 | tf_op jit(solution)/shard_map/all_to_all | solution.py:350
  49.0 0.0 collective-permute-done.12.refs_1_
  49.0 0.0 collective-permute-done.13.refs_2_
  49.0 0.0 collective-permute-done.14.refs_3_
  49.0 0.7 %shard_map.84 = bf16[64,2048]{1,0:T(8,128)(2,1)} custom-call(bf16[64,512]{1,0:T(8,128)(2,1)S(1)} %get-tuple-element.25.refs_0_, bf16[64,512]{1,0:T(8,128)(2,1)S(1)} %collective-permute-done.12.refs_1_, bf16[64,512]{1,0:T(8,128)(2,1)S(1)} %collective-permute-done.13.refs_2_, bf16[64,512]{1,0:T(8,128)(2,1)S(1)} %collective-permute-done.14.refs_3_), custom_call_target="tpu_custom_call" | custom-call | tf_op jit(solution)/shard_map/pallas_call | solution.py:29
  49.8 7.0 %all-to-all-done.1.tables_ref = f32[32,8,8]{2,1,0:T(8,128)S(1)} async-done(((f32[32,8,8]{2,1,0:T(8,128)}), f32[32,8,8]{2,1,0:T(8,128)S(1)}, u32[]{:S(2)}, u32[]{:S(2)}) %all-to-all-start.1) | async-done | bytes 8224 | tf_op jit(solution)/shard_map/all_to_all | solution.py:350
  56.7 0.7 %shard_map.86 = f32[8,8]{1,0:T(8,128)} custom-call(f32[32,8,8]{2,1,0:T(8,128)S(1)} %all-to-all-done.1.tables_ref), custom_call_target="tpu_custom_call" | custom-call | tf_op jit(solution)/shard_map/pallas_call | solution.py:29
  (3 shorter events, 0.1 us)
Async XLA Ops:
  2.0 13.9 %collective-permute-start = (bf16[256,512]{1,0:T(8,128)(2,1)S(1)}, bf16[256,512]{1,0:T(8,128)(2,1)S(1)}, u32[]{:S(2)}, u32[]{:S(2)}) collective-permute-start(bf16[256,512]{1,0:T(8,128)(2,1)S(1)} %get-tuple-element.16), channel_id=1, source_target_pairs={{0,1},{1,0},{2,3},{3,2},{4,5},{5,4},{6,7},{7,6},{8,9},{9,8},{10,11... | collective-permute-start | bytes 786440 | tf_op jit(solution)/shard_map/ppermute | solution.py:21
  5.0 10.9 %collective-permute-start.3 = (bf16[80,1024]{1,0:T(8,128)(2,1)S(1)}, bf16[80,1024]{1,0:T(8,128)(2,1)S(1)}, u32[]{:S(2)}, u32[]{:S(2)}) collective-permute-start(bf16[80,1024]{1,0:T(8,128)(2,1)S(1)} %get-tuple-element.18), channel_id=1, source_target_pairs={{0,2},{1,3},{2,0},{3,1},{4,6},{5,7},{6,4},{7,5},{8,10},{9,11},{10,... | collective-permute-start | bytes 491528 | tf_op jit(solution)/shard_map/ppermute | solution.py:21
  6.6 8.3 %collective-permute-start.1 = (bf16[32,1024]{1,0:T(8,128)(2,1)S(1)}, bf16[32,1024]{1,0:T(8,128)(2,1)S(1)}, u32[]{:S(2)}, u32[]{:S(2)}) collective-permute-start(bf16[32,1024]{1,0:T(8,128)(2,1)S(1)} %get-tuple-element.17.refs_3_), channel_id=1, source_target_pairs={{0,6},{1,7},{2,4},{3,5},{4,2},{5,3},{6,0},{7,1},{8,14},{9,15},{10,... | collective-permute-start | bytes 196616 | tf_op jit(solution)/shard_map/ppermute | solution.py:21
  9.1 6.8 %collective-permute-start.2 = (bf16[32,1024]{1,0:T(8,128)(2,1)S(1)}, bf16[32,1024]{1,0:T(8,128)(2,1)S(1)}, u32[]{:S(2)}, u32[]{:S(2)}) collective-permute-start(bf16[32,1024]{1,0:T(8,128)(2,1)S(1)} %get-tuple-element.17.refs_3_), channel_id=1, source_target_pairs={{0,4},{1,5},{2,6},{3,7},{4,0},{5,1},{6,2},{7,3},{8,12},{9,13},{10,... | collective-permute-start | bytes 196616 | tf_op jit(solution)/shard_map/ppermute | solution.py:21
  15.9 7.0 %copy-start.1 = (bf16[192,2048]{1,0:T(8,128)(2,1)S(1)}, bf16[192,2048]{1,0:T(8,128)(2,1)}, u32[]{:S(2)}) copy-start(bf16[192,2048]{1,0:T(8,128)(2,1)} %up_ref.3) | copy-start | bytes 2359300
  15.9 7.0 %copy-start = (bf16[192,2048]{1,0:T(8,128)(2,1)S(1)}, bf16[192,2048]{1,0:T(8,128)(2,1)}, u32[]{:S(2)}) copy-start(bf16[192,2048]{1,0:T(8,128)(2,1)} %gate_ref.3) | copy-start | bytes 2359300
  16.0 6.4 %collective-permute-start.5 = (bf16[128,1024]{1,0:T(8,128)(2,1)S(1)}, bf16[128,1024]{1,0:T(8,128)(2,1)S(1)}, u32[]{:S(2)}, u32[]{:S(2)}) collective-permute-start(bf16[128,1024]{1,0:T(8,128)(2,1)S(1)} %shard_map.78.after_ref.near_ref), channel_id=1, source_target_pairs={{0,1},{1,0},{2,3},{3,2},{4,5},{5,4},{6,7},{7,6},{8,9},{9,8},{10,11... | collective-permute-start | bytes 786440 | tf_op jit(solution)/shard_map/ppermute | solution.py:21
  16.6 7.1 %collective-permute-start.4 = (bf16[320,512]{1,0:T(8,128)(2,1)S(1)}, bf16[320,512]{1,0:T(8,128)(2,1)S(1)}, u32[]{:S(2)}, u32[]{:S(2)}) collective-permute-start(bf16[320,512]{1,0:T(8,128)(2,1)S(1)} %shard_map.79), channel_id=1, source_target_pairs={{0,2},{1,3},{2,0},{3,1},{4,6},{5,7},{6,4},{7,5},{8,10},{9,11},{10,... | collective-permute-start | bytes 983048 | tf_op jit(solution)/shard_map/ppermute | solution.py:21
  16.9 6.0 %collective-permute-start.7 = (bf16[128,1024]{1,0:T(8,128)(2,1)S(1)}, bf16[128,1024]{1,0:T(8,128)(2,1)S(1)}, u32[]{:S(2)}, u32[]{:S(2)}) collective-permute-start(bf16[128,1024]{1,0:T(8,128)(2,1)S(1)} %shard_map.78.after_ref.near_ref), channel_id=1, source_target_pairs={{0,8},{8,0},{16,24},{24,16},{1,9},{9,1},{17,25},{25,17},{2,10},{10... | collective-permute-start | bytes 786440 | tf_op jit(solution)/shard_map/ppermute | solution.py:21
  22.4 1.5 %collective-permute-start.6 = (bf16[128,1024]{1,0:T(8,128)(2,1)S(1)}, bf16[128,1024]{1,0:T(8,128)(2,1)S(1)}, u32[]{:S(2)}, u32[]{:S(2)}) collective-permute-start(bf16[128,1024]{1,0:T(8,128)(2,1)S(1)} %collective-permute-done.5.far_ref.refs_1_), channel_id=1, source_target_pairs={{0,8},{8,0},{16,24},{24,16},{1,9},{9,1},{17,25},{25,17},{2,10},{10... | collective-permute-start | bytes 786440 | tf_op jit(solution)/shard_map/ppermute | solution.py:21
  22.4 9.1 %collective-permute-start.11 = (bf16[160,512]{1,0:T(8,128)(2,1)S(1)}, bf16[160,512]{1,0:T(8,128)(2,1)S(1)}, u32[]{:S(2)}, u32[]{:S(2)}) collective-permute-start(bf16[160,512]{1,0:T(8,128)(2,1)S(1)} %shard_map.82), channel_id=1, source_target_pairs={{0,1},{1,0},{2,3},{3,2},{4,5},{5,4},{6,7},{7,6},{8,9},{9,8},{10,11... | collective-permute-start | bytes 491528 | tf_op jit(solution)/shard_map/ppermute | solution.py:21
  24.3 7.2 %collective-permute-start.10 = (bf16[192,256]{1,0:T(8,128)(2,1)S(1)}, bf16[192,256]{1,0:T(8,128)(2,1)S(1)}, u32[]{:S(2)}, u32[]{:S(2)}) collective-permute-start(bf16[192,256]{1,0:T(8,128)(2,1)S(1)} %shard_map.81.refs_0_), channel_id=1, source_target_pairs={{0,3},{1,2},{2,1},{3,0},{4,7},{5,6},{6,5},{7,4},{8,11},{9,10},{10,... | collective-permute-start | bytes 294920 | tf_op jit(solution)/shard_map/ppermute | solution.py:21
  25.9 7.3 %collective-permute-start.8 = (bf16[192,256]{1,0:T(8,128)(2,1)S(1)}, bf16[192,256]{1,0:T(8,128)(2,1)S(1)}, u32[]{:S(2)}, u32[]{:S(2)}) collective-permute-start(bf16[192,256]{1,0:T(8,128)(2,1)S(1)} %shard_map.81.refs_0_), channel_id=1, source_target_pairs={{0,1},{1,0},{2,3},{3,2},{4,5},{5,4},{6,7},{7,6},{8,9},{9,8},{10,11... | collective-permute-start | bytes 294920 | tf_op jit(solution)/shard_map/ppermute | solution.py:21
  26.4 6.8 %collective-permute-start.9 = (bf16[192,256]{1,0:T(8,128)(2,1)S(1)}, bf16[192,256]{1,0:T(8,128)(2,1)S(1)}, u32[]{:S(2)}, u32[]{:S(2)}) collective-permute-start(bf16[192,256]{1,0:T(8,128)(2,1)S(1)} %shard_map.81.refs_0_), channel_id=1, source_target_pairs={{0,2},{1,3},{2,0},{3,1},{4,6},{5,7},{6,4},{7,5},{8,10},{9,11},{10,... | collective-permute-start | bytes 294920 | tf_op jit(solution)/shard_map/ppermute | solution.py:21
  34.7 10.9 %all-to-all-start = ((bf16[32,16,128]{2,1,0:T(8,128)(2,1)}), bf16[32,16,128]{2,1,0:T(8,128)(2,1)S(1)}, u32[]{:S(2)}, u32[]{:S(2)}) async-start(bf16[32,16,128]{2,1,0:T(8,128)(2,1)} %bitcast.1), calls=%async_computation | async-start | bytes 262144 | tf_op jit(solution)/shard_map/all_to_all | solution.py:339
  37.9 11.1 %collective-permute-start.12 = (bf16[64,512]{1,0:T(8,128)(2,1)S(1)}, bf16[64,512]{1,0:T(8,128)(2,1)S(1)}, u32[]{:S(2)}, u32[]{:S(2)}) collective-permute-start(bf16[64,512]{1,0:T(8,128)(2,1)S(1)} %get-tuple-element.26), channel_id=1, source_target_pairs={{0,1},{1,0},{2,3},{3,2},{4,5},{5,4},{6,7},{7,6},{8,9},{9,8},{10,11... | collective-permute-start | bytes 196616 | tf_op jit(solution)/shard_map/ppermute | solution.py:21
  39.7 9.3 %collective-permute-start.13 = (bf16[64,512]{1,0:T(8,128)(2,1)S(1)}, bf16[64,512]{1,0:T(8,128)(2,1)S(1)}, u32[]{:S(2)}, u32[]{:S(2)}) collective-permute-start(bf16[64,512]{1,0:T(8,128)(2,1)S(1)} %get-tuple-element.27), channel_id=1, source_target_pairs={{0,2},{1,3},{2,0},{3,1},{4,6},{5,7},{6,4},{7,5},{8,10},{9,11},{10,... | collective-permute-start | bytes 196616 | tf_op jit(solution)/shard_map/ppermute | solution.py:21
  41.2 7.8 %collective-permute-start.14 = (bf16[64,512]{1,0:T(8,128)(2,1)S(1)}, bf16[64,512]{1,0:T(8,128)(2,1)S(1)}, u32[]{:S(2)}, u32[]{:S(2)}) collective-permute-start(bf16[64,512]{1,0:T(8,128)(2,1)S(1)} %get-tuple-element.28), channel_id=1, source_target_pairs={{0,3},{1,2},{2,1},{3,0},{4,7},{5,6},{6,5},{7,4},{8,11},{9,10},{10,... | collective-permute-start | bytes 196616 | tf_op jit(solution)/shard_map/ppermute | solution.py:21
  46.4 10.3 %all-to-all-start.1 = ((f32[32,8,8]{2,1,0:T(8,128)}), f32[32,8,8]{2,1,0:T(8,128)S(1)}, u32[]{:S(2)}, u32[]{:S(2)}) async-start(f32[32,8,8]{2,1,0:T(8,128)} %shard_map.85), calls=%async_computation.1 | async-start | bytes 262144 | tf_op jit(solution)/shard_map/all_to_all | solution.py:350

commit v18 on v17

--- a/solution.py
+++ b/solution.py
@@ -267,7 +267,7 @@
     part, token_part = model // HOLDERS, tokens // HOLDERS
 
     count = depth + TILE
-    beside, first_x = depth // 4 // TILE * TILE, depth // 4 // TILE * TILE
+    beside, first_x = depth // 4 // TILE * TILE, depth // 2 // TILE * TILE
     own, with_z, down_own, down_z, down_early, down_late = call(
         first_kernel,
         [jax.ShapeDtypeStruct((n, model // 2), bf16) for n in (rows, rows + beside)]

time: 57.7 us -> 57 us (0.988)
  waiting for transfers between devices: 28.9 us -> 27.9 us
    ppermute x15, waiting for transfers between devices: 17.8 us -> 16.7 us  [swapped(): lax.ppermute(array, axis, [(i, i ^ mask) for i in range(lax.axis_size(axi...]
  transfers between devices with their start and end apart: 17 -> 17, of which waited for: 8 -> 9; matrix products, arithmetic and copies ran while one was open for 0% -> 0% of each run, Pallas kernels for 5% -> 5%
where the time goes in v18:
time: 57 us; the launch traced here: 56.7 us
  waiting for transfers between devices  27.9 us (49%)
  starting transfers between devices  21.8 us (38%)
  Pallas kernels  6.29 us (11%)
  between operations  0.76 us (1%)
    ppermute x15, waiting for transfers between devices, swapped(): lax.ppermute(array, axis, [(i, i ^ mask) for i in range(lax.axis_size(axi...  16.7 us
    ppermute x15, starting transfers between devices, swapped(): lax.ppermute(array, axis, [(i, i ^ mask) for i in range(lax.axis_size(axi...  15.8 us
    all_to_all x1, waiting for transfers between devices, shards(): lax.all_to_all(tables, ('grp', 'tok'), split_axis=0, concat_axis=0, tiled...  6.96 us
    pallas_call x10, Pallas kernels, call(): pl.pallas_call(body, out_shape=outs, in_specs=in_specs, out_specs=jax.tre...  6.29 us
    all_to_all x1, waiting for transfers between devices, shards(): lax.all_to_all(centered, ('grp', 'tok'), split_axis=0, concat_axis=0, til...  4.19 us
    all_to_all x1, starting transfers between devices, shards(): lax.all_to_all(centered, ('grp', 'tok'), split_axis=0, concat_axis=0, til...  3.48 us
    all_to_all x1, starting transfers between devices, shards(): lax.all_to_all(tables, ('grp', 'tok'), split_axis=0, concat_axis=0, tiled...  2.56 us
  transfers between devices with their start and end apart: 17, of which 9 were waited for; matrix products, arithmetic and copies ran while one was open for 0% of the time, Pallas kernels for 5%

profile of v18, /device:TPU:0, one launch (start us, length us, event | category | flops | bytes accessed | tf_op | source)
XLA Modules:
  0.0 56.7 jit_solution(10053136114172754105)
XLA Ops:
  0.6 1.4 %shard_map.77 = (bf16[32,1024]{1,0:T(8,128)(2,1)S(1)}, bf16[80,1024]{1,0:T(8,128)(2,1)S(1)}, bf16[208,512]{1,0:T(8,128)(2,1)S(1)}, bf16[112,512]{1,0:T(8,128)(2,...) custom-call(bf16[32,2048]{1,0:T(8,128)(2,1)} %states_hbm.1, f32[1,2048]{1,0:T(1,128)} %bitcast.4, ...), custom_call_target="tpu_custom_call" | custom-call | tf_op jit(solution)/shard_map/pallas_call | solution.py:29
  2.0 3.0 %collective-permute-start = (bf16[304,512]{1,0:T(8,128)(2,1)S(1)}, bf16[304,512]{1,0:T(8,128)(2,1)S(1)}, u32[]{:S(2)}, u32[]{:S(2)}) collective-permute-start(bf16[304,512]{1,0:T(8,128)(2,1)S(1)} %get-tuple-element.16), channel_id=1, source_target_pairs={{0,1},{1,0},{2,3},{3,2},{4,5},{5,4},{6,7},{7,6},{8,9},{9,8},{10,11... | collective-permute-start | bytes 933896 | tf_op jit(solution)/shard_map/ppermute | solution.py:21
  5.0 1.6 %collective-permute-start.3 = (bf16[80,1024]{1,0:T(8,128)(2,1)S(1)}, bf16[80,1024]{1,0:T(8,128)(2,1)S(1)}, u32[]{:S(2)}, u32[]{:S(2)}) collective-permute-start(bf16[80,1024]{1,0:T(8,128)(2,1)S(1)} %get-tuple-element.18), channel_id=1, source_target_pairs={{0,2},{1,3},{2,0},{3,1},{4,6},{5,7},{6,4},{7,5},{8,10},{9,11},{10,... | collective-permute-start | bytes 491528 | tf_op jit(solution)/shard_map/ppermute | solution.py:21
  6.6 2.5 %collective-permute-start.1 = (bf16[32,1024]{1,0:T(8,128)(2,1)S(1)}, bf16[32,1024]{1,0:T(8,128)(2,1)S(1)}, u32[]{:S(2)}, u32[]{:S(2)}) collective-permute-start(bf16[32,1024]{1,0:T(8,128)(2,1)S(1)} %get-tuple-element.17.refs_3_), channel_id=1, source_target_pairs={{0,6},{1,7},{2,4},{3,5},{4,2},{5,3},{6,0},{7,1},{8,14},{9,15},{10,... | collective-permute-start | bytes 196616 | tf_op jit(solution)/shard_map/ppermute | solution.py:21
  9.1 0.1 collective-permute-start.2
  9.2 5.7 %collective-permute-done.1.refs_0_ = bf16[32,1024]{1,0:T(8,128)(2,1)S(1)} collective-permute-done((bf16[32,1024]{1,0:T(8,128)(2,1)S(1)}, bf16[32,1024]{1,0:T(8,128)(2,1)S(1)}, u32[]{:S(2)}, u32[]{:S(2)}) %collective-permute-start.1) | collective-permute-done | bytes 65568 | tf_op jit(solution)/shard_map/ppermute | solution.py:21
  14.9 1.0 %collective-permute-done.2.refs_1_ = bf16[32,1024]{1,0:T(8,128)(2,1)S(1)} collective-permute-done((bf16[32,1024]{1,0:T(8,128)(2,1)S(1)}, bf16[32,1024]{1,0:T(8,128)(2,1)S(1)}, u32[]{:S(2)}, u32[]{:S(2)}) %collective-permute-start.2) | collective-permute-done | bytes 65568 | tf_op jit(solution)/shard_map/ppermute | solution.py:21
  15.9 0.0 collective-permute-done.3.refs_2_.refs_5_
  15.9 0.0 collective-permute-done.after_ref.second_ref.refs_7_
  15.9 0.0 copy-start.1
  15.9 0.0 copy-start
  15.9 0.6 %collective-permute-start.5 = (bf16[128,1024]{1,0:T(8,128)(2,1)S(1)}, bf16[128,1024]{1,0:T(8,128)(2,1)S(1)}, u32[]{:S(2)}, u32[]{:S(2)}) collective-permute-start(bf16[128,1024]{1,0:T(8,128)(2,1)S(1)} %shard_map.78.after_ref.near_ref), channel_id=1, source_target_pairs={{0,1},{1,0},{2,3},{3,2},{4,5},{5,4},{6,7},{7,6},{8,9},{9,8},{10,11... | collective-permute-start | bytes 786440 | tf_op jit(solution)/shard_map/ppermute | solution.py:21
  16.6 0.3 collective-permute-start.4
  16.9 0.0 collective-permute-start.7
  16.9 5.5 %collective-permute-done.5.far_ref.refs_1_ = bf16[128,1024]{1,0:T(8,128)(2,1)S(1)} collective-permute-done((bf16[128,1024]{1,0:T(8,128)(2,1)S(1)}, bf16[128,1024]{1,0:T(8,128)(2,1)S(1)}, u32[]{:S(2)}, u32[]{:S(2)}) %collective-permute-start.5) | collective-permute-done | bytes 262176 | tf_op jit(solution)/shard_map/ppermute | solution.py:21
  22.4 0.0 collective-permute-start.6
  22.4 0.5 collective-permute-start.11
  22.9 0.0 collective-permute-done.7.near2_ref
  22.9 0.0 copy-done.1
  22.9 0.0 copy-done
  22.9 0.8 %shard_map.80 = (bf16[192,128]{1,0:T(8,128)(2,1)S(1)}, f32[192,128]{1,0:T(8,128)S(1)}, f32[192,128]{1,0:T(8,128)S(1)}) custom-call(bf16[128,1024]{1,0:T(8,128)(2,1)S(1)} %shard_map.78.after_ref.near_ref, bf16[128,1024]{1,0:T(8,128)(2,1)S(1)} %collective-permute-done.7.near2_ref, bf16[128,1024]{1,0:T(8,128)(2,1)S(1)} %collective-permute-done.5.far_ref.refs_1_, ...), custom_call_target="tpu_custom_call" | custom-call | tf_op jit(solution)/shard_map/pallas_call | solution.py:29
  23.7 0.0 collective-permute-done.4.after_ref.refs_6_
  23.7 0.2 collective-permute-done.6.far2_ref
  23.9 0.4 shard_map.81.refs_0_
  24.3 1.6 %collective-permute-start.10 = (bf16[192,256]{1,0:T(8,128)(2,1)S(1)}, bf16[192,256]{1,0:T(8,128)(2,1)S(1)}, u32[]{:S(2)}, u32[]{:S(2)}) collective-permute-start(bf16[192,256]{1,0:T(8,128)(2,1)S(1)} %shard_map.81.refs_0_), channel_id=1, source_target_pairs={{0,3},{1,2},{2,1},{3,0},{4,7},{5,6},{6,5},{7,4},{8,11},{9,10},{10,... | collective-permute-start | bytes 294920 | tf_op jit(solution)/shard_map/ppermute | solution.py:21
  25.9 0.5 collective-permute-start.8
  26.4 1.4 %collective-permute-start.9 = (bf16[192,256]{1,0:T(8,128)(2,1)S(1)}, bf16[192,256]{1,0:T(8,128)(2,1)S(1)}, u32[]{:S(2)}, u32[]{:S(2)}) collective-permute-start(bf16[192,256]{1,0:T(8,128)(2,1)S(1)} %shard_map.81.refs_0_), channel_id=1, source_target_pairs={{0,2},{1,3},{2,0},{3,1},{4,6},{5,7},{6,4},{7,5},{8,10},{9,11},{10,... | collective-permute-start | bytes 294920 | tf_op jit(solution)/shard_map/ppermute | solution.py:21
  27.9 0.1 collective-permute-done.11.refs_8_
  28.0 3.0 %collective-permute-done.10.refs_3_ = bf16[192,256]{1,0:T(8,128)(2,1)S(1)} collective-permute-done((bf16[192,256]{1,0:T(8,128)(2,1)S(1)}, bf16[192,256]{1,0:T(8,128)(2,1)S(1)}, u32[]{:S(2)}, u32[]{:S(2)}) %collective-permute-start.10) | collective-permute-done | bytes 98336 | tf_op jit(solution)/shard_map/ppermute | solution.py:21
  30.9 1.3 %collective-permute-done.8.refs_1_ = bf16[192,256]{1,0:T(8,128)(2,1)S(1)} collective-permute-done((bf16[192,256]{1,0:T(8,128)(2,1)S(1)}, bf16[192,256]{1,0:T(8,128)(2,1)S(1)}, u32[]{:S(2)}, u32[]{:S(2)}) %collective-permute-start.8) | collective-permute-done | bytes 98336 | tf_op jit(solution)/shard_map/ppermute | solution.py:21
  32.2 0.0 collective-permute-done.9.refs_2_
  32.2 1.5 %shard_map.83 = (bf16[64,512]{1,0:T(8,128)(2,1)S(1)}, bf16[64,512]{1,0:T(8,128)(2,1)S(1)}, bf16[64,512]{1,0:T(8,128)(2,1)S(1)}, bf16[64,512]{1,0:T(8,128)(2,1)S(1)}, bf16[512,128]{1,0:T(8,128)(2,1)}) custom-call(bf16[192,256]{1,0:T(8,128)(2,1)S(1)} %shard_map.81.refs_0_, bf16[192,256]{1,0:T(8,128)(2,1)S(1)} %collective-permute-done.8.refs_1_, ...), custom_call_target="tpu_custom_call" | custom-call | tf_op jit(solution)/shard_map/pallas_call | solution.py:29
  33.7 3.5 %all-to-all-start = ((bf16[32,16,128]{2,1,0:T(8,128)(2,1)}), bf16[32,16,128]{2,1,0:T(8,128)(2,1)S(1)}, u32[]{:S(2)}, u32[]{:S(2)}) async-start(bf16[32,16,128]{2,1,0:T(8,128)(2,1)} %bitcast.1), calls=%async_computation | async-start | bytes 262144 | tf_op jit(solution)/shard_map/all_to_all | solution.py:339
  37.2 1.8 %collective-permute-start.12 = (bf16[64,512]{1,0:T(8,128)(2,1)S(1)}, bf16[64,512]{1,0:T(8,128)(2,1)S(1)}, u32[]{:S(2)}, u32[]{:S(2)}) collective-permute-start(bf16[64,512]{1,0:T(8,128)(2,1)S(1)} %get-tuple-element.26), channel_id=1, source_target_pairs={{0,1},{1,0},{2,3},{3,2},{4,5},{5,4},{6,7},{7,6},{8,9},{9,8},{10,11... | collective-permute-start | bytes 196616 | tf_op jit(solution)/shard_map/ppermute | solution.py:21
  39.0 1.5 %collective-permute-start.13 = (bf16[64,512]{1,0:T(8,128)(2,1)S(1)}, bf16[64,512]{1,0:T(8,128)(2,1)S(1)}, u32[]{:S(2)}, u32[]{:S(2)}) collective-permute-start(bf16[64,512]{1,0:T(8,128)(2,1)S(1)} %get-tuple-element.27), channel_id=1, source_target_pairs={{0,2},{1,3},{2,0},{3,1},{4,6},{5,7},{6,4},{7,5},{8,10},{9,11},{10,... | collective-permute-start | bytes 196616 | tf_op jit(solution)/shard_map/ppermute | solution.py:21
  40.5 0.3 collective-permute-start.14
  40.7 4.2 %all-to-all-done = bf16[32,16,128]{2,1,0:T(8,128)(2,1)S(1)} async-done(((bf16[32,16,128]{2,1,0:T(8,128)(2,1)}), bf16[32,16,128]{2,1,0:T(8,128)(2,1)S(1)}, u32[]{:S(2)}, u32[]{:S(2)}) %all-to-all-start) | async-done | bytes 131104 | tf_op jit(solution)/shard_map/all_to_all | solution.py:339
  44.9 0.8 %shard_map.85 = f32[32,8,8]{2,1,0:T(8,128)} custom-call(bf16[8,4,16,128]{3,2,1,0:T(8,128)(2,1)S(1)} %bitcast.3), custom_call_target="tpu_custom_call" | custom-call | tf_op jit(solution)/shard_map/pallas_call | solution.py:29
  45.7 2.6 %all-to-all-start.1 = ((f32[32,8,8]{2,1,0:T(8,128)}), f32[32,8,8]{2,1,0:T(8,128)S(1)}, u32[]{:S(2)}, u32[]{:S(2)}) async-start(f32[32,8,8]{2,1,0:T(8,128)} %shard_map.85), calls=%async_computation.1 | async-start | bytes 262144 | tf_op jit(solution)/shard_map/all_to_all | solution.py:350
  48.3 0.0 collective-permute-done.12.refs_1_
  48.3 0.0 collective-permute-done.13.refs_2_
  48.3 0.0 collective-permute-done.14.refs_3_
  48.3 0.7 %shard_map.84 = bf16[64,2048]{1,0:T(8,128)(2,1)} custom-call(bf16[64,512]{1,0:T(8,128)(2,1)S(1)} %get-tuple-element.25.refs_0_, bf16[64,512]{1,0:T(8,128)(2,1)S(1)} %collective-permute-done.12.refs_1_, bf16[64,512]{1,0:T(8,128)(2,1)S(1)} %collective-permute-done.13.refs_2_, bf16[64,512]{1,0:T(8,128)(2,1)S(1)} %collective-permute-done.14.refs_3_), custom_call_target="tpu_custom_call" | custom-call | tf_op jit(solution)/shard_map/pallas_call | solution.py:29
  49.1 7.0 %all-to-all-done.1.tables_ref = f32[32,8,8]{2,1,0:T(8,128)S(1)} async-done(((f32[32,8,8]{2,1,0:T(8,128)}), f32[32,8,8]{2,1,0:T(8,128)S(1)}, u32[]{:S(2)}, u32[]{:S(2)}) %all-to-all-start.1) | async-done | bytes 8224 | tf_op jit(solution)/shard_map/all_to_all | solution.py:350
  56.0 0.7 %shard_map.86 = f32[8,8]{1,0:T(8,128)} custom-call(f32[32,8,8]{2,1,0:T(8,128)S(1)} %all-to-all-done.1.tables_ref), custom_call_target="tpu_custom_call" | custom-call | tf_op jit(solution)/shard_map/pallas_call | solution.py:29
  (3 shorter events, 0.1 us)
Async XLA Ops:
  2.0 13.9 %collective-permute-start = (bf16[304,512]{1,0:T(8,128)(2,1)S(1)}, bf16[304,512]{1,0:T(8,128)(2,1)S(1)}, u32[]{:S(2)}, u32[]{:S(2)}) collective-permute-start(bf16[304,512]{1,0:T(8,128)(2,1)S(1)} %get-tuple-element.16), channel_id=1, source_target_pairs={{0,1},{1,0},{2,3},{3,2},{4,5},{5,4},{6,7},{7,6},{8,9},{9,8},{10,11... | collective-permute-start | bytes 933896 | tf_op jit(solution)/shard_map/ppermute | solution.py:21
  5.0 10.9 %collective-permute-start.3 = (bf16[80,1024]{1,0:T(8,128)(2,1)S(1)}, bf16[80,1024]{1,0:T(8,128)(2,1)S(1)}, u32[]{:S(2)}, u32[]{:S(2)}) collective-permute-start(bf16[80,1024]{1,0:T(8,128)(2,1)S(1)} %get-tuple-element.18), channel_id=1, source_target_pairs={{0,2},{1,3},{2,0},{3,1},{4,6},{5,7},{6,4},{7,5},{8,10},{9,11},{10,... | collective-permute-start | bytes 491528 | tf_op jit(solution)/shard_map/ppermute | solution.py:21
  6.6 8.3 %collective-permute-start.1 = (bf16[32,1024]{1,0:T(8,128)(2,1)S(1)}, bf16[32,1024]{1,0:T(8,128)(2,1)S(1)}, u32[]{:S(2)}, u32[]{:S(2)}) collective-permute-start(bf16[32,1024]{1,0:T(8,128)(2,1)S(1)} %get-tuple-element.17.refs_3_), channel_id=1, source_target_pairs={{0,6},{1,7},{2,4},{3,5},{4,2},{5,3},{6,0},{7,1},{8,14},{9,15},{10,... | collective-permute-start | bytes 196616 | tf_op jit(solution)/shard_map/ppermute | solution.py:21
  9.1 6.8 %collective-permute-start.2 = (bf16[32,1024]{1,0:T(8,128)(2,1)S(1)}, bf16[32,1024]{1,0:T(8,128)(2,1)S(1)}, u32[]{:S(2)}, u32[]{:S(2)}) collective-permute-start(bf16[32,1024]{1,0:T(8,128)(2,1)S(1)} %get-tuple-element.17.refs_3_), channel_id=1, source_target_pairs={{0,4},{1,5},{2,6},{3,7},{4,0},{5,1},{6,2},{7,3},{8,12},{9,13},{10,... | collective-permute-start | bytes 196616 | tf_op jit(solution)/shard_map/ppermute | solution.py:21
  15.9 7.0 %copy-start.1 = (bf16[192,2048]{1,0:T(8,128)(2,1)S(1)}, bf16[192,2048]{1,0:T(8,128)(2,1)}, u32[]{:S(2)}) copy-start(bf16[192,2048]{1,0:T(8,128)(2,1)} %up_ref.3) | copy-start | bytes 2359300
  15.9 7.0 %copy-start = (bf16[192,2048]{1,0:T(8,128)(2,1)S(1)}, bf16[192,2048]{1,0:T(8,128)(2,1)}, u32[]{:S(2)}) copy-start(bf16[192,2048]{1,0:T(8,128)(2,1)} %gate_ref.3) | copy-start | bytes 2359300
  15.9 6.4 %collective-permute-start.5 = (bf16[128,1024]{1,0:T(8,128)(2,1)S(1)}, bf16[128,1024]{1,0:T(8,128)(2,1)S(1)}, u32[]{:S(2)}, u32[]{:S(2)}) collective-permute-start(bf16[128,1024]{1,0:T(8,128)(2,1)S(1)} %shard_map.78.after_ref.near_ref), channel_id=1, source_target_pairs={{0,1},{1,0},{2,3},{3,2},{4,5},{5,4},{6,7},{7,6},{8,9},{9,8},{10,11... | collective-permute-start | bytes 786440 | tf_op jit(solution)/shard_map/ppermute | solution.py:21
  16.6 7.1 %collective-permute-start.4 = (bf16[320,512]{1,0:T(8,128)(2,1)S(1)}, bf16[320,512]{1,0:T(8,128)(2,1)S(1)}, u32[]{:S(2)}, u32[]{:S(2)}) collective-permute-start(bf16[320,512]{1,0:T(8,128)(2,1)S(1)} %shard_map.79), channel_id=1, source_target_pairs={{0,2},{1,3},{2,0},{3,1},{4,6},{5,7},{6,4},{7,5},{8,10},{9,11},{10,... | collective-permute-start | bytes 983048 | tf_op jit(solution)/shard_map/ppermute | solution.py:21
  16.9 6.0 %collective-permute-start.7 = (bf16[128,1024]{1,0:T(8,128)(2,1)S(1)}, bf16[128,1024]{1,0:T(8,128)(2,1)S(1)}, u32[]{:S(2)}, u32[]{:S(2)}) collective-permute-start(bf16[128,1024]{1,0:T(8,128)(2,1)S(1)} %shard_map.78.after_ref.near_ref), channel_id=1, source_target_pairs={{0,8},{8,0},{16,24},{24,16},{1,9},{9,1},{17,25},{25,17},{2,10},{10... | collective-permute-start | bytes 786440 | tf_op jit(solution)/shard_map/ppermute | solution.py:21
  22.4 1.5 %collective-permute-start.6 = (bf16[128,1024]{1,0:T(8,128)(2,1)S(1)}, bf16[128,1024]{1,0:T(8,128)(2,1)S(1)}, u32[]{:S(2)}, u32[]{:S(2)}) collective-permute-start(bf16[128,1024]{1,0:T(8,128)(2,1)S(1)} %collective-permute-done.5.far_ref.refs_1_), channel_id=1, source_target_pairs={{0,8},{8,0},{16,24},{24,16},{1,9},{9,1},{17,25},{25,17},{2,10},{10... | collective-permute-start | bytes 786440 | tf_op jit(solution)/shard_map/ppermute | solution.py:21
  22.4 5.6 %collective-permute-start.11 = (bf16[112,512]{1,0:T(8,128)(2,1)S(1)}, bf16[112,512]{1,0:T(8,128)(2,1)S(1)}, u32[]{:S(2)}, u32[]{:S(2)}) collective-permute-start(bf16[112,512]{1,0:T(8,128)(2,1)S(1)} %shard_map.82), channel_id=1, source_target_pairs={{0,1},{1,0},{2,3},{3,2},{4,5},{5,4},{6,7},{7,6},{8,9},{9,8},{10,11... | collective-permute-start | bytes 344072 | tf_op jit(solution)/shard_map/ppermute | solution.py:21
  24.3 6.6 %collective-permute-start.10 = (bf16[192,256]{1,0:T(8,128)(2,1)S(1)}, bf16[192,256]{1,0:T(8,128)(2,1)S(1)}, u32[]{:S(2)}, u32[]{:S(2)}) collective-permute-start(bf16[192,256]{1,0:T(8,128)(2,1)S(1)} %shard_map.81.refs_0_), channel_id=1, source_target_pairs={{0,3},{1,2},{2,1},{3,0},{4,7},{5,6},{6,5},{7,4},{8,11},{9,10},{10,... | collective-permute-start | bytes 294920 | tf_op jit(solution)/shard_map/ppermute | solution.py:21
  25.9 6.3 %collective-permute-start.8 = (bf16[192,256]{1,0:T(8,128)(2,1)S(1)}, bf16[192,256]{1,0:T(8,128)(2,1)S(1)}, u32[]{:S(2)}, u32[]{:S(2)}) collective-permute-start(bf16[192,256]{1,0:T(8,128)(2,1)S(1)} %shard_map.81.refs_0_), channel_id=1, source_target_pairs={{0,1},{1,0},{2,3},{3,2},{4,5},{5,4},{6,7},{7,6},{8,9},{9,8},{10,11... | collective-permute-start | bytes 294920 | tf_op jit(solution)/shard_map/ppermute | solution.py:21
  26.4 5.8 %collective-permute-start.9 = (bf16[192,256]{1,0:T(8,128)(2,1)S(1)}, bf16[192,256]{1,0:T(8,128)(2,1)S(1)}, u32[]{:S(2)}, u32[]{:S(2)}) collective-permute-start(bf16[192,256]{1,0:T(8,128)(2,1)S(1)} %shard_map.81.refs_0_), channel_id=1, source_target_pairs={{0,2},{1,3},{2,0},{3,1},{4,6},{5,7},{6,4},{7,5},{8,10},{9,11},{10,... | collective-permute-start | bytes 294920 | tf_op jit(solution)/shard_map/ppermute | solution.py:21
  33.7 11.2 %all-to-all-start = ((bf16[32,16,128]{2,1,0:T(8,128)(2,1)}), bf16[32,16,128]{2,1,0:T(8,128)(2,1)S(1)}, u32[]{:S(2)}, u32[]{:S(2)}) async-start(bf16[32,16,128]{2,1,0:T(8,128)(2,1)} %bitcast.1), calls=%async_computation | async-start | bytes 262144 | tf_op jit(solution)/shard_map/all_to_all | solution.py:339
  37.2 11.1 %collective-permute-start.12 = (bf16[64,512]{1,0:T(8,128)(2,1)S(1)}, bf16[64,512]{1,0:T(8,128)(2,1)S(1)}, u32[]{:S(2)}, u32[]{:S(2)}) collective-permute-start(bf16[64,512]{1,0:T(8,128)(2,1)S(1)} %get-tuple-element.26), channel_id=1, source_target_pairs={{0,1},{1,0},{2,3},{3,2},{4,5},{5,4},{6,7},{7,6},{8,9},{9,8},{10,11... | collective-permute-start | bytes 196616 | tf_op jit(solution)/shard_map/ppermute | solution.py:21
  39.0 9.3 %collective-permute-start.13 = (bf16[64,512]{1,0:T(8,128)(2,1)S(1)}, bf16[64,512]{1,0:T(8,128)(2,1)S(1)}, u32[]{:S(2)}, u32[]{:S(2)}) collective-permute-start(bf16[64,512]{1,0:T(8,128)(2,1)S(1)} %get-tuple-element.27), channel_id=1, source_target_pairs={{0,2},{1,3},{2,0},{3,1},{4,6},{5,7},{6,4},{7,5},{8,10},{9,11},{10,... | collective-permute-start | bytes 196616 | tf_op jit(solution)/shard_map/ppermute | solution.py:21
  40.5 7.8 %collective-permute-start.14 = (bf16[64,512]{1,0:T(8,128)(2,1)S(1)}, bf16[64,512]{1,0:T(8,128)(2,1)S(1)}, u32[]{:S(2)}, u32[]{:S(2)}) collective-permute-start(bf16[64,512]{1,0:T(8,128)(2,1)S(1)} %get-tuple-element.28), channel_id=1, source_target_pairs={{0,3},{1,2},{2,1},{3,0},{4,7},{5,6},{6,5},{7,4},{8,11},{9,10},{10,... | collective-permute-start | bytes 196616 | tf_op jit(solution)/shard_map/ppermute | solution.py:21
  45.7 10.3 %all-to-all-start.1 = ((f32[32,8,8]{2,1,0:T(8,128)}), f32[32,8,8]{2,1,0:T(8,128)S(1)}, u32[]{:S(2)}, u32[]{:S(2)}) async-start(f32[32,8,8]{2,1,0:T(8,128)} %shard_map.85), calls=%async_computation.1 | async-start | bytes 262144 | tf_op jit(solution)/shard_map/all_to_all | solution.py:350

commit v19 on v17

--- a/solution.py
+++ b/solution.py
@@ -125,11 +125,29 @@
     out_ref[count:] = second_ref[: out_ref.shape[0] - count]
 
 
-def stack_kernel(after_ref, *refs):
-    rows = refs[-2].shape[0]
-    z = lax.axis_index("tok") >> 1
-    for m, piece in enumerate(refs[-2::-1]):
-        refs[-1][pl.ds(pl.multiple_of((z ^ m) * rows, rows), rows)] = piece[:rows]
+def to_place(out_ref, m, piece):
+    rows = piece.shape[0]
+    place = (lax.axis_index("tok") >> 1) ^ m
+    out_ref[pl.ds(pl.multiple_of(place * rows, rows), rows)] = piece
+
+
+def near_stack_kernel(after_ref, *refs):
+    pieces, (near_ref, others_ref) = refs[:-3], refs[-2:]
+    count = len(pieces)
+    rows = near_ref.shape[0] // count
+    for at, ref in enumerate(pieces):
+        m = count - 1 - at
+        piece = ref[:rows]
+        to_place(near_ref, m, piece)
+        if m:
+            others_ref[(m - 1) * rows : m * rows] = piece
+
+
+def far_stack_kernel(own_ref, others_ref, out_ref):
+    rows = own_ref.shape[0]
+    to_place(out_ref, 0, own_ref[...])
+    for m in range(1, out_ref.shape[0] // rows):
+        to_place(out_ref, m, others_ref[(m - 1) * rows : m * rows])
 
 
 def gated(gate, upward):
@@ -290,13 +308,18 @@
     down_early = swapped(down_early, "tok", 1)
     with_z = swapped(with_z, "tok", 2)
     pieces = [swapped(own, "tok", 2 * m) for m in range(members // 2 - 1, 1, -1)] + [with_z, own]
-    near = call(
-        stack_kernel,
-        jax.ShapeDtypeStruct((tokens // 2, model // 2), bf16),
-        [ANY] + [VMEM] * len(pieces),
-        (down_early, *pieces),
-    )
-    far = swapped(near, "tok", 1)
+    half_width = model // 2
+    near_shape = jax.ShapeDtypeStruct((tokens // 2, half_width), bf16)
+    far_own = swapped(held(own, pieces[0]), "tok", 1)
+    near, others = call(
+        near_stack_kernel,
+        [near_shape, jax.ShapeDtypeStruct((tokens // 2 - rows, half_width), bf16)],
+        [ANY] + [VMEM] * len(pieces) + [ANY],
+        (down_early, *pieces, far_own),
+    )
+    far = call(
+        far_stack_kernel, near_shape, [VMEM] * 2, (far_own, swapped(others, "tok", 1))
+    )
     near2 = swapped(near, "grp", 1)
     down_z = call(
         join_kernel,

time: 57.7 us -> 60.9 us (1.055)
  waiting for transfers between devices: 28.9 us -> 31.7 us
    ppermute x15 -> x16, waiting for transfers between devices: 17.8 us -> 20.5 us  [swapped(): lax.ppermute(array, axis, [(i, i ^ mask) for i in range(lax.axis_size(axi...]
    ppermute x15 -> x16, starting transfers between devices: 15.8 us -> 16.2 us  [swapped(): lax.ppermute(array, axis, [(i, i ^ mask) for i in range(lax.axis_size(axi...]
    pallas_call x10 -> x12, Pallas kernels: 6.28 us -> 6.31 us  [call(): pl.pallas_call(body, out_shape=outs, in_specs=in_specs, out_specs=jax.tre...]
  transfers between devices with their start and end apart: 17 -> 18, of which waited for: 8 -> 11; matrix products, arithmetic and copies ran while one was open for 0% -> 0% of each run, Pallas kernels for 5% -> 4%
where the time goes in v19:
time: 60.9 us; the launch traced here: 60.7 us
  waiting for transfers between devices  31.7 us (52%)
  starting transfers between devices  21.9 us (36%)
  Pallas kernels  6.31 us (10%)
  between operations  0.79 us (1%)
    ppermute x16, waiting for transfers between devices, swapped(): lax.ppermute(array, axis, [(i, i ^ mask) for i in range(lax.axis_size(axi...  20.5 us
    ppermute x16, starting transfers between devices, swapped(): lax.ppermute(array, axis, [(i, i ^ mask) for i in range(lax.axis_size(axi...  16.2 us
    all_to_all x1, waiting for transfers between devices, shards(): lax.all_to_all(tables, ('grp', 'tok'), split_axis=0, concat_axis=0, tiled...  6.96 us
    pallas_call x12, Pallas kernels, call(): pl.pallas_call(body, out_shape=outs, in_specs=in_specs, out_specs=jax.tre...  6.31 us
    all_to_all x1, waiting for transfers between devices, shards(): lax.all_to_all(centered, ('grp', 'tok'), split_axis=0, concat_axis=0, til...  4.19 us
    all_to_all x1, starting transfers between devices, shards(): lax.all_to_all(centered, ('grp', 'tok'), split_axis=0, concat_axis=0, til...  3.09 us
    all_to_all x1, starting transfers between devices, shards(): lax.all_to_all(tables, ('grp', 'tok'), split_axis=0, concat_axis=0, tiled...  2.57 us
  transfers between devices with their start and end apart: 18, of which 11 were waited for; matrix products, arithmetic and copies ran while one was open for 0% of the time, Pallas kernels for 4%

profile of v19, /device:TPU:0, one launch (start us, length us, event | category | flops | bytes accessed | tf_op | source)
XLA Modules:
  0.0 60.7 jit_solution(17639545985492684795)
XLA Ops:
  0.6 1.4 %shard_map.77 = (bf16[32,1024]{1,0:T(8,128)(2,1)S(1)}, bf16[80,1024]{1,0:T(8,128)(2,1)S(1)}, bf16[208,512]{1,0:T(8,128)(2,1)S(1)}, bf16[112,512]{1,0:T(8,128)(2,...) custom-call(bf16[32,2048]{1,0:T(8,128)(2,1)} %states_hbm.1, f32[1,2048]{1,0:T(1,128)} %bitcast.4, ...), custom_call_target="tpu_custom_call" | custom-call | tf_op jit(solution)/shard_map/pallas_call | solution.py:29
  2.0 3.0 %collective-permute-start = (bf16[256,512]{1,0:T(8,128)(2,1)S(1)}, bf16[256,512]{1,0:T(8,128)(2,1)S(1)}, u32[]{:S(2)}, u32[]{:S(2)}) collective-permute-start(bf16[256,512]{1,0:T(8,128)(2,1)S(1)} %get-tuple-element.18), channel_id=1, source_target_pairs={{0,1},{1,0},{2,3},{3,2},{4,5},{5,4},{6,7},{7,6},{8,9},{9,8},{10,11... | collective-permute-start | bytes 786440 | tf_op jit(solution)/shard_map/ppermute | solution.py:21
  5.0 1.6 %collective-permute-start.3 = (bf16[80,1024]{1,0:T(8,128)(2,1)S(1)}, bf16[80,1024]{1,0:T(8,128)(2,1)S(1)}, u32[]{:S(2)}, u32[]{:S(2)}) collective-permute-start(bf16[80,1024]{1,0:T(8,128)(2,1)S(1)} %get-tuple-element.20), channel_id=1, source_target_pairs={{0,2},{1,3},{2,0},{3,1},{4,6},{5,7},{6,4},{7,5},{8,10},{9,11},{10,... | collective-permute-start | bytes 491528 | tf_op jit(solution)/shard_map/ppermute | solution.py:21
  6.6 2.5 %collective-permute-start.1 = (bf16[32,1024]{1,0:T(8,128)(2,1)S(1)}, bf16[32,1024]{1,0:T(8,128)(2,1)S(1)}, u32[]{:S(2)}, u32[]{:S(2)}) collective-permute-start(bf16[32,1024]{1,0:T(8,128)(2,1)S(1)} %get-tuple-element.19.refs_3_), channel_id=1, source_target_pairs={{0,6},{1,7},{2,4},{3,5},{4,2},{5,3},{6,0},{7,1},{8,14},{9,15},{10,... | collective-permute-start | bytes 196616 | tf_op jit(solution)/shard_map/ppermute | solution.py:21
  9.1 0.1 collective-permute-start.2
  9.2 5.7 %collective-permute-done.1.refs_1_.refs_0_ = bf16[32,1024]{1,0:T(8,128)(2,1)S(1)} collective-permute-done((bf16[32,1024]{1,0:T(8,128)(2,1)S(1)}, bf16[32,1024]{1,0:T(8,128)(2,1)S(1)}, u32[]{:S(2)}, u32[]{:S(2)}) %collective-permute-start.1) | collective-permute-done | bytes 65568 | tf_op jit(solution)/shard_map/ppermute | solution.py:21
  14.9 0.5 collective-permute-start.4
  15.4 0.5 collective-permute-done.2.refs_1_
  15.9 3.9 %collective-permute-done.4.refs_4_.own_ref = bf16[32,1024]{1,0:T(8,128)(2,1)S(1)} collective-permute-done((bf16[32,1024]{1,0:T(8,128)(2,1)S(1)}, bf16[32,1024]{1,0:T(8,128)(2,1)S(1)}, u32[]{:S(2)}, u32[]{:S(2)}) %collective-permute-start.4) | collective-permute-done | bytes 65568 | tf_op jit(solution)/shard_map/ppermute | solution.py:21
  19.8 0.0 collective-permute-done.3.refs_2_.refs_5_
  19.8 0.0 collective-permute-done.after_ref.second_ref.refs_7_
  19.8 0.6 collective-permute-start.6
  20.4 0.0 copy-start.1
  20.4 0.0 copy-start
  20.5 0.1 collective-permute-start.5
  20.5 0.1 collective-permute-start.8
  20.6 4.9 %collective-permute-done.6.others_ref = bf16[96,1024]{1,0:T(8,128)(2,1)S(1)} collective-permute-done((bf16[96,1024]{1,0:T(8,128)(2,1)S(1)}, bf16[96,1024]{1,0:T(8,128)(2,1)S(1)}, u32[]{:S(2)}, u32[]{:S(2)}) %collective-permute-start.6) | collective-permute-done | bytes 196640 | tf_op jit(solution)/shard_map/ppermute | solution.py:21
  25.6 0.1 collective-permute-start.7
  25.7 0.6 collective-permute-start.12
  26.3 0.0 collective-permute-done.8.near2_ref
  26.3 0.0 copy-done.1
  26.3 0.0 copy-done
  26.3 0.8 %shard_map.82 = (bf16[192,128]{1,0:T(8,128)(2,1)S(1)}, f32[192,128]{1,0:T(8,128)S(1)}, f32[192,128]{1,0:T(8,128)S(1)}) custom-call(bf16[128,1024]{1,0:T(8,128)(2,1)S(1)} %get-tuple-element.21.after_ref.near_ref, bf16[128,1024]{1,0:T(8,128)(2,1)S(1)} %collective-permute-done.8.near2_ref, bf16[128,1024]{1,0:T(8,128)(2,1)S(1)} %shard_map.81.far_ref.refs_1_, ...), custom_call_target="tpu_custom_call" | custom-call | tf_op jit(solution)/shard_map/pallas_call | solution.py:29
  27.1 0.5 collective-permute-done.5.after_ref.refs_6_
  27.6 0.0 collective-permute-done.7.far2_ref
  27.6 0.4 shard_map.83.refs_0_
  28.0 0.1 collective-permute-start.10
  28.1 2.9 %collective-permute-start.11 = (bf16[192,256]{1,0:T(8,128)(2,1)S(1)}, bf16[192,256]{1,0:T(8,128)(2,1)S(1)}, u32[]{:S(2)}, u32[]{:S(2)}) collective-permute-start(bf16[192,256]{1,0:T(8,128)(2,1)S(1)} %shard_map.83.refs_0_), channel_id=1, source_target_pairs={{0,3},{1,2},{2,1},{3,0},{4,7},{5,6},{6,5},{7,4},{8,11},{9,10},{10,... | collective-permute-start | bytes 294920 | tf_op jit(solution)/shard_map/ppermute | solution.py:21
  31.0 0.5 collective-permute-start.9
  31.5 0.8 %collective-permute-done.12.refs_8_ = bf16[160,512]{1,0:T(8,128)(2,1)S(1)} collective-permute-done((bf16[160,512]{1,0:T(8,128)(2,1)S(1)}, bf16[160,512]{1,0:T(8,128)(2,1)S(1)}, u32[]{:S(2)}, u32[]{:S(2)}) %collective-permute-start.12) | collective-permute-done | bytes 163872 | tf_op jit(solution)/shard_map/ppermute | solution.py:21
  32.3 1.2 %collective-permute-done.10.refs_2_ = bf16[192,256]{1,0:T(8,128)(2,1)S(1)} collective-permute-done((bf16[192,256]{1,0:T(8,128)(2,1)S(1)}, bf16[192,256]{1,0:T(8,128)(2,1)S(1)}, u32[]{:S(2)}, u32[]{:S(2)}) %collective-permute-start.10) | collective-permute-done | bytes 98336 | tf_op jit(solution)/shard_map/ppermute | solution.py:21
  33.5 2.0 %collective-permute-done.11.refs_3_ = bf16[192,256]{1,0:T(8,128)(2,1)S(1)} collective-permute-done((bf16[192,256]{1,0:T(8,128)(2,1)S(1)}, bf16[192,256]{1,0:T(8,128)(2,1)S(1)}, u32[]{:S(2)}, u32[]{:S(2)}) %collective-permute-start.11) | collective-permute-done | bytes 98336 | tf_op jit(solution)/shard_map/ppermute | solution.py:21
  35.5 1.0 %collective-permute-done.9.refs_1_ = bf16[192,256]{1,0:T(8,128)(2,1)S(1)} collective-permute-done((bf16[192,256]{1,0:T(8,128)(2,1)S(1)}, bf16[192,256]{1,0:T(8,128)(2,1)S(1)}, u32[]{:S(2)}, u32[]{:S(2)}) %collective-permute-start.9) | collective-permute-done | bytes 98336 | tf_op jit(solution)/shard_map/ppermute | solution.py:21
  36.5 1.5 %shard_map.85 = (bf16[64,512]{1,0:T(8,128)(2,1)S(1)}, bf16[64,512]{1,0:T(8,128)(2,1)S(1)}, bf16[64,512]{1,0:T(8,128)(2,1)S(1)}, bf16[64,512]{1,0:T(8,128)(2,1)S(1)}, bf16[512,128]{1,0:T(8,128)(2,1)}) custom-call(bf16[192,256]{1,0:T(8,128)(2,1)S(1)} %shard_map.83.refs_0_, bf16[192,256]{1,0:T(8,128)(2,1)S(1)} %collective-permute-done.9.refs_1_, ...), custom_call_target="tpu_custom_call" | custom-call | tf_op jit(solution)/shard_map/pallas_call | solution.py:29
  38.0 3.1 %all-to-all-start = ((bf16[32,16,128]{2,1,0:T(8,128)(2,1)}), bf16[32,16,128]{2,1,0:T(8,128)(2,1)S(1)}, u32[]{:S(2)}, u32[]{:S(2)}) async-start(bf16[32,16,128]{2,1,0:T(8,128)(2,1)} %bitcast.1), calls=%async_computation | async-start | bytes 262144 | tf_op jit(solution)/shard_map/all_to_all | solution.py:362
  41.1 1.8 %collective-permute-start.13 = (bf16[64,512]{1,0:T(8,128)(2,1)S(1)}, bf16[64,512]{1,0:T(8,128)(2,1)S(1)}, u32[]{:S(2)}, u32[]{:S(2)}) collective-permute-start(bf16[64,512]{1,0:T(8,128)(2,1)S(1)} %get-tuple-element.30), channel_id=1, source_target_pairs={{0,1},{1,0},{2,3},{3,2},{4,5},{5,4},{6,7},{7,6},{8,9},{9,8},{10,11... | collective-permute-start | bytes 196616 | tf_op jit(solution)/shard_map/ppermute | solution.py:21
  42.9 1.5 %collective-permute-start.14 = (bf16[64,512]{1,0:T(8,128)(2,1)S(1)}, bf16[64,512]{1,0:T(8,128)(2,1)S(1)}, u32[]{:S(2)}, u32[]{:S(2)}) collective-permute-start(bf16[64,512]{1,0:T(8,128)(2,1)S(1)} %get-tuple-element.31), channel_id=1, source_target_pairs={{0,2},{1,3},{2,0},{3,1},{4,6},{5,7},{6,4},{7,5},{8,10},{9,11},{10,... | collective-permute-start | bytes 196616 | tf_op jit(solution)/shard_map/ppermute | solution.py:21
  44.4 0.3 collective-permute-start.15
  44.6 4.2 %all-to-all-done = bf16[32,16,128]{2,1,0:T(8,128)(2,1)S(1)} async-done(((bf16[32,16,128]{2,1,0:T(8,128)(2,1)}), bf16[32,16,128]{2,1,0:T(8,128)(2,1)S(1)}, u32[]{:S(2)}, u32[]{:S(2)}) %all-to-all-start) | async-done | bytes 131104 | tf_op jit(solution)/shard_map/all_to_all | solution.py:362
  48.8 0.8 %shard_map.87 = f32[32,8,8]{2,1,0:T(8,128)} custom-call(bf16[8,4,16,128]{3,2,1,0:T(8,128)(2,1)S(1)} %bitcast.3), custom_call_target="tpu_custom_call" | custom-call | tf_op jit(solution)/shard_map/pallas_call | solution.py:29
  49.6 2.6 %all-to-all-start.1 = ((f32[32,8,8]{2,1,0:T(8,128)}), f32[32,8,8]{2,1,0:T(8,128)S(1)}, u32[]{:S(2)}, u32[]{:S(2)}) async-start(f32[32,8,8]{2,1,0:T(8,128)} %shard_map.87), calls=%async_computation.1 | async-start | bytes 262144 | tf_op jit(solution)/shard_map/all_to_all | solution.py:373
  52.2 0.0 collective-permute-done.13.refs_1_
  52.2 0.0 collective-permute-done.14.refs_2_
  52.2 0.0 collective-permute-done.15.refs_3_
  52.2 0.7 %shard_map.86 = bf16[64,2048]{1,0:T(8,128)(2,1)} custom-call(bf16[64,512]{1,0:T(8,128)(2,1)S(1)} %get-tuple-element.29.refs_0_, bf16[64,512]{1,0:T(8,128)(2,1)S(1)} %collective-permute-done.13.refs_1_, bf16[64,512]{1,0:T(8,128)(2,1)S(1)} %collective-permute-done.14.refs_2_, bf16[64,512]{1,0:T(8,128)(2,1)S(1)} %collective-permute-done.15.refs_3_), custom_call_target="tpu_custom_call" | custom-call | tf_op jit(solution)/shard_map/pallas_call | solution.py:29
  53.0 7.0 %all-to-all-done.1.tables_ref = f32[32,8,8]{2,1,0:T(8,128)S(1)} async-done(((f32[32,8,8]{2,1,0:T(8,128)}), f32[32,8,8]{2,1,0:T(8,128)S(1)}, u32[]{:S(2)}, u32[]{:S(2)}) %all-to-all-start.1) | async-done | bytes 8224 | tf_op jit(solution)/shard_map/all_to_all | solution.py:373
  59.9 0.7 %shard_map.88 = f32[8,8]{1,0:T(8,128)} custom-call(f32[32,8,8]{2,1,0:T(8,128)S(1)} %all-to-all-done.1.tables_ref), custom_call_target="tpu_custom_call" | custom-call | tf_op jit(solution)/shard_map/pallas_call | solution.py:29
  (6 shorter events, 0.1 us)
Async XLA Ops:
  2.0 17.8 %collective-permute-start = (bf16[256,512]{1,0:T(8,128)(2,1)S(1)}, bf16[256,512]{1,0:T(8,128)(2,1)S(1)}, u32[]{:S(2)}, u32[]{:S(2)}) collective-permute-start(bf16[256,512]{1,0:T(8,128)(2,1)S(1)} %get-tuple-element.18), channel_id=1, source_target_pairs={{0,1},{1,0},{2,3},{3,2},{4,5},{5,4},{6,7},{7,6},{8,9},{9,8},{10,11... | collective-permute-start | bytes 786440 | tf_op jit(solution)/shard_map/ppermute | solution.py:21
  5.0 14.8 %collective-permute-start.3 = (bf16[80,1024]{1,0:T(8,128)(2,1)S(1)}, bf16[80,1024]{1,0:T(8,128)(2,1)S(1)}, u32[]{:S(2)}, u32[]{:S(2)}) collective-permute-start(bf16[80,1024]{1,0:T(8,128)(2,1)S(1)} %get-tuple-element.20), channel_id=1, source_target_pairs={{0,2},{1,3},{2,0},{3,1},{4,6},{5,7},{6,4},{7,5},{8,10},{9,11},{10,... | collective-permute-start | bytes 491528 | tf_op jit(solution)/shard_map/ppermute | solution.py:21
  6.6 8.3 %collective-permute-start.1 = (bf16[32,1024]{1,0:T(8,128)(2,1)S(1)}, bf16[32,1024]{1,0:T(8,128)(2,1)S(1)}, u32[]{:S(2)}, u32[]{:S(2)}) collective-permute-start(bf16[32,1024]{1,0:T(8,128)(2,1)S(1)} %get-tuple-element.19.refs_3_), channel_id=1, source_target_pairs={{0,6},{1,7},{2,4},{3,5},{4,2},{5,3},{6,0},{7,1},{8,14},{9,15},{10,... | collective-permute-start | bytes 196616 | tf_op jit(solution)/shard_map/ppermute | solution.py:21
  9.1 6.8 %collective-permute-start.2 = (bf16[32,1024]{1,0:T(8,128)(2,1)S(1)}, bf16[32,1024]{1,0:T(8,128)(2,1)S(1)}, u32[]{:S(2)}, u32[]{:S(2)}) collective-permute-start(bf16[32,1024]{1,0:T(8,128)(2,1)S(1)} %get-tuple-element.19.refs_3_), channel_id=1, source_target_pairs={{0,4},{1,5},{2,6},{3,7},{4,0},{5,1},{6,2},{7,3},{8,12},{9,13},{10,... | collective-permute-start | bytes 196616 | tf_op jit(solution)/shard_map/ppermute | solution.py:21
  14.9 4.9 %collective-permute-start.4 = (bf16[32,1024]{1,0:T(8,128)(2,1)S(1)}, bf16[32,1024]{1,0:T(8,128)(2,1)S(1)}, u32[]{:S(2)}, u32[]{:S(2)}) collective-permute-start(bf16[32,1024]{1,0:T(8,128)(2,1)S(1)} %shard_map.78), channel_id=1, source_target_pairs={{0,1},{1,0},{2,3},{3,2},{4,5},{5,4},{6,7},{7,6},{8,9},{9,8},{10,11... | collective-permute-start | bytes 196616 | tf_op jit(solution)/shard_map/ppermute | solution.py:21
  19.8 5.7 %collective-permute-start.6 = (bf16[96,1024]{1,0:T(8,128)(2,1)S(1)}, bf16[96,1024]{1,0:T(8,128)(2,1)S(1)}, u32[]{:S(2)}, u32[]{:S(2)}) collective-permute-start(bf16[96,1024]{1,0:T(8,128)(2,1)S(1)} %get-tuple-element.23), channel_id=1, source_target_pairs={{0,1},{1,0},{2,3},{3,2},{4,5},{5,4},{6,7},{7,6},{8,9},{9,8},{10,11... | collective-permute-start | bytes 589832 | tf_op jit(solution)/shard_map/ppermute | solution.py:21
  20.4 5.9 %copy-start.1 = (bf16[192,2048]{1,0:T(8,128)(2,1)S(1)}, bf16[192,2048]{1,0:T(8,128)(2,1)}, u32[]{:S(2)}) copy-start(bf16[192,2048]{1,0:T(8,128)(2,1)} %up_ref.3) | copy-start | bytes 2359300
  20.4 5.8 %copy-start = (bf16[192,2048]{1,0:T(8,128)(2,1)S(1)}, bf16[192,2048]{1,0:T(8,128)(2,1)}, u32[]{:S(2)}) copy-start(bf16[192,2048]{1,0:T(8,128)(2,1)} %gate_ref.3) | copy-start | bytes 2359300
  20.5 7.1 %collective-permute-start.5 = (bf16[320,512]{1,0:T(8,128)(2,1)S(1)}, bf16[320,512]{1,0:T(8,128)(2,1)S(1)}, u32[]{:S(2)}, u32[]{:S(2)}) collective-permute-start(bf16[320,512]{1,0:T(8,128)(2,1)S(1)} %shard_map.80), channel_id=1, source_target_pairs={{0,2},{1,3},{2,0},{3,1},{4,6},{5,7},{6,4},{7,5},{8,10},{9,11},{10,... | collective-permute-start | bytes 983048 | tf_op jit(solution)/shard_map/ppermute | solution.py:21
  20.5 5.7 %collective-permute-start.8 = (bf16[128,1024]{1,0:T(8,128)(2,1)S(1)}, bf16[128,1024]{1,0:T(8,128)(2,1)S(1)}, u32[]{:S(2)}, u32[]{:S(2)}) collective-permute-start(bf16[128,1024]{1,0:T(8,128)(2,1)S(1)} %get-tuple-element.21.after_ref.near_ref), channel_id=1, source_target_pairs={{0,8},{8,0},{16,24},{24,16},{1,9},{9,1},{17,25},{25,17},{2,10},{10... | collective-permute-start | bytes 786440 | tf_op jit(solution)/shard_map/ppermute | solution.py:21
  25.6 2.0 %collective-permute-start.7 = (bf16[128,1024]{1,0:T(8,128)(2,1)S(1)}, bf16[128,1024]{1,0:T(8,128)(2,1)S(1)}, u32[]{:S(2)}, u32[]{:S(2)}) collective-permute-start(bf16[128,1024]{1,0:T(8,128)(2,1)S(1)} %shard_map.81.far_ref.refs_1_), channel_id=1, source_target_pairs={{0,8},{8,0},{16,24},{24,16},{1,9},{9,1},{17,25},{25,17},{2,10},{10... | collective-permute-start | bytes 786440 | tf_op jit(solution)/shard_map/ppermute | solution.py:21
  25.7 6.6 %collective-permute-start.12 = (bf16[160,512]{1,0:T(8,128)(2,1)S(1)}, bf16[160,512]{1,0:T(8,128)(2,1)S(1)}, u32[]{:S(2)}, u32[]{:S(2)}) collective-permute-start(bf16[160,512]{1,0:T(8,128)(2,1)S(1)} %shard_map.84), channel_id=1, source_target_pairs={{0,1},{1,0},{2,3},{3,2},{4,5},{5,4},{6,7},{7,6},{8,9},{9,8},{10,11... | collective-permute-start | bytes 491528 | tf_op jit(solution)/shard_map/ppermute | solution.py:21
  28.0 5.5 %collective-permute-start.10 = (bf16[192,256]{1,0:T(8,128)(2,1)S(1)}, bf16[192,256]{1,0:T(8,128)(2,1)S(1)}, u32[]{:S(2)}, u32[]{:S(2)}) collective-permute-start(bf16[192,256]{1,0:T(8,128)(2,1)S(1)} %shard_map.83.refs_0_), channel_id=1, source_target_pairs={{0,2},{1,3},{2,0},{3,1},{4,6},{5,7},{6,4},{7,5},{8,10},{9,11},{10,... | collective-permute-start | bytes 294920 | tf_op jit(solution)/shard_map/ppermute | solution.py:21
  28.1 7.4 %collective-permute-start.11 = (bf16[192,256]{1,0:T(8,128)(2,1)S(1)}, bf16[192,256]{1,0:T(8,128)(2,1)S(1)}, u32[]{:S(2)}, u32[]{:S(2)}) collective-permute-start(bf16[192,256]{1,0:T(8,128)(2,1)S(1)} %shard_map.83.refs_0_), channel_id=1, source_target_pairs={{0,3},{1,2},{2,1},{3,0},{4,7},{5,6},{6,5},{7,4},{8,11},{9,10},{10,... | collective-permute-start | bytes 294920 | tf_op jit(solution)/shard_map/ppermute | solution.py:21
  31.0 5.5 %collective-permute-start.9 = (bf16[192,256]{1,0:T(8,128)(2,1)S(1)}, bf16[192,256]{1,0:T(8,128)(2,1)S(1)}, u32[]{:S(2)}, u32[]{:S(2)}) collective-permute-start(bf16[192,256]{1,0:T(8,128)(2,1)S(1)} %shard_map.83.refs_0_), channel_id=1, source_target_pairs={{0,1},{1,0},{2,3},{3,2},{4,5},{5,4},{6,7},{7,6},{8,9},{9,8},{10,11... | collective-permute-start | bytes 294920 | tf_op jit(solution)/shard_map/ppermute | solution.py:21
  38.0 10.8 %all-to-all-start = ((bf16[32,16,128]{2,1,0:T(8,128)(2,1)}), bf16[32,16,128]{2,1,0:T(8,128)(2,1)S(1)}, u32[]{:S(2)}, u32[]{:S(2)}) async-start(bf16[32,16,128]{2,1,0:T(8,128)(2,1)} %bitcast.1), calls=%async_computation | async-start | bytes 262144 | tf_op jit(solution)/shard_map/all_to_all | solution.py:362
  41.1 11.1 %collective-permute-start.13 = (bf16[64,512]{1,0:T(8,128)(2,1)S(1)}, bf16[64,512]{1,0:T(8,128)(2,1)S(1)}, u32[]{:S(2)}, u32[]{:S(2)}) collective-permute-start(bf16[64,512]{1,0:T(8,128)(2,1)S(1)} %get-tuple-element.30), channel_id=1, source_target_pairs={{0,1},{1,0},{2,3},{3,2},{4,5},{5,4},{6,7},{7,6},{8,9},{9,8},{10,11... | collective-permute-start | bytes 196616 | tf_op jit(solution)/shard_map/ppermute | solution.py:21
  42.9 9.3 %collective-permute-start.14 = (bf16[64,512]{1,0:T(8,128)(2,1)S(1)}, bf16[64,512]{1,0:T(8,128)(2,1)S(1)}, u32[]{:S(2)}, u32[]{:S(2)}) collective-permute-start(bf16[64,512]{1,0:T(8,128)(2,1)S(1)} %get-tuple-element.31), channel_id=1, source_target_pairs={{0,2},{1,3},{2,0},{3,1},{4,6},{5,7},{6,4},{7,5},{8,10},{9,11},{10,... | collective-permute-start | bytes 196616 | tf_op jit(solution)/shard_map/ppermute | solution.py:21
  44.4 7.8 %collective-permute-start.15 = (bf16[64,512]{1,0:T(8,128)(2,1)S(1)}, bf16[64,512]{1,0:T(8,128)(2,1)S(1)}, u32[]{:S(2)}, u32[]{:S(2)}) collective-permute-start(bf16[64,512]{1,0:T(8,128)(2,1)S(1)} %get-tuple-element.32), channel_id=1, source_target_pairs={{0,3},{1,2},{2,1},{3,0},{4,7},{5,6},{6,5},{7,4},{8,11},{9,10},{10,... | collective-permute-start | bytes 196616 | tf_op jit(solution)/shard_map/ppermute | solution.py:21
  49.6 10.3 %all-to-all-start.1 = ((f32[32,8,8]{2,1,0:T(8,128)}), f32[32,8,8]{2,1,0:T(8,128)S(1)}, u32[]{:S(2)}, u32[]{:S(2)}) async-start(f32[32,8,8]{2,1,0:T(8,128)} %shard_map.87), calls=%async_computation.1 | async-start | bytes 262144 | tf_op jit(solution)/shard_map/all_to_all | solution.py:373

commit v20 on v18

--- a/solution.py
+++ b/solution.py
@@ -230,28 +230,45 @@
 
 
 def pair_kernel(parts_ref, out_ref, flat_ref):
-    copies, experts, _ = out_ref.shape
+    experts = flat_ref.shape[0]
     parts = parts_ref[...].astype(f32)
     total = parts[:, 0]
-    for holder in range(1, parts.shape[1]):
-        total = total + parts[:, holder]
+    for m in range(1, parts.shape[1]):
+        total = total + parts[:, m]
     flat_ref[...] = total.astype(bf16).astype(f32)
-    lane = lax.broadcasted_iota(jnp.int32, (experts, experts), 1)
+    in_row = out_ref.shape[1] == 1
+    shape = (experts, out_ref.shape[2])
+    row = lax.broadcasted_iota(jnp.int32, shape, 0)
+    lane = lax.broadcasted_iota(jnp.int32, shape, 1)
 
     def one(expert, table):
         products = jnp.sum(flat_ref[...] * flat_ref[pl.ds(expert, 1)], axis=1)
-        return jnp.where(lane == expert, jnp.sum(products, axis=1, keepdims=True), table)
-
-    table = lax.fori_loop(0, experts, one, jnp.zeros((experts, experts), f32), unroll=experts <= 8)
-    for copy in range(copies):
-        out_ref[copy] = table
+        here = lane == expert * experts + row if in_row else lane == expert
+        return jnp.where(here, jnp.sum(products, axis=1, keepdims=True), table)
+
+    table = lax.fori_loop(0, experts, one, jnp.zeros(shape, f32), unroll=experts <= 8)
+    if in_row:
+        table = jnp.sum(table, axis=0, keepdims=True)
+    out_ref[...] = jnp.broadcast_to(table[None], out_ref.shape)
 
 
 def cka_kernel(tables_ref, out_ref):
     totals = jnp.sum(tables_ref[...], axis=0)
-    shape = totals.shape
-    eye = lax.broadcasted_iota(jnp.int32, shape, 0) == lax.broadcasted_iota(jnp.int32, shape, 1)
-    kept = jnp.where(eye, totals, 0.0)
+    shape = out_ref.shape
+    row = lax.broadcasted_iota(jnp.int32, shape, 0)
+    lane = lax.broadcasted_iota(jnp.int32, shape, 1)
+    if totals.shape != shape:
+        experts = shape[0]
+        wide = (experts, totals.shape[1])
+        spread = jnp.broadcast_to(totals, wide)
+        at = lax.broadcasted_iota(jnp.int32, wide, 1) - experts * lax.broadcasted_iota(
+            jnp.int32, wide, 0
+        )
+        totals = jnp.zeros(shape, f32)
+        for column in range(experts):
+            values = jnp.sum(jnp.where(at == column, spread, 0.0), axis=1, keepdims=True)
+            totals = jnp.where(lane == column, values, totals)
+    kept = jnp.where(row == lane, totals, 0.0)
     down = jnp.sum(kept, axis=1, keepdims=True)
     across = jnp.sum(kept, axis=0, keepdims=True)
     out_ref[...] = totals / jnp.sqrt(down * across)
@@ -267,7 +284,7 @@
     part, token_part = model // HOLDERS, tokens // HOLDERS
 
     count = depth + TILE
-    beside, first_x = depth // 4 // TILE * TILE, depth // 2 // TILE * TILE
+    beside, first_x = depth // 6 // TILE * TILE, depth // 2 // TILE * TILE
     own, with_z, down_own, down_z, down_early, down_late = call(
         first_kernel,
         [jax.ShapeDtypeStruct((n, model // 2), bf16) for n in (rows, rows + beside)]
@@ -338,10 +355,10 @@
     )
     arrived = lax.all_to_all(centered, ("grp", "tok"), split_axis=0, concat_axis=0, tiled=True)
     arrived = arrived.reshape(experts, HOLDERS, entries // devices, LANES)
-    direct = devices * experts * experts <= 1 << 16
+    direct = experts * experts <= LANES
     tables = call(
         pair_kernel,
-        jax.ShapeDtypeStruct((devices if direct else 1, experts, experts), f32),
+        jax.ShapeDtypeStruct((devices, 1, LANES) if direct else (1, experts, experts), f32),
         [VMEM],
         (arrived,),
         scratch=[pltpu.VMEM((experts, entries // devices, LANES), f32)],

time: 57 us -> 57.3 us (level)
  starting transfers between devices: 21.8 us -> 22.9 us
  waiting for transfers between devices: 27.9 us -> 27.1 us
    all_to_all x1, starting transfers between devices: 3.48 us -> 4.8 us  [shards(): lax.all_to_all(centered, ('grp', 'tok'), split_axis=0, concat_axis=0, til...]
    all_to_all x1, waiting for transfers between devices: 6.96 us -> 6.33 us  [shards(): lax.all_to_all(tables, ('grp', 'tok'), split_axis=0, concat_axis=0, tiled...]
  transfers between devices with their start and end apart: 17 -> 17, of which waited for: 9 -> 8; matrix products, arithmetic and copies ran while one was open for 0% -> 0% of each run, Pallas kernels for 5% -> 5%
where the time goes in v20:
time: 57.3 us; the launch traced here: 57.1 us
  waiting for transfers between devices  27.1 us (47%)
  starting transfers between devices  22.9 us (40%)
  Pallas kernels  6.32 us (11%)
  between operations  0.75 us (1%)
    ppermute x15, waiting for transfers between devices, swapped(): lax.ppermute(array, axis, [(i, i ^ mask) for i in range(lax.axis_size(axi...  16.6 us
    ppermute x15, starting transfers between devices, swapped(): lax.ppermute(array, axis, [(i, i ^ mask) for i in range(lax.axis_size(axi...  15.6 us
    all_to_all x1, waiting for transfers between devices, shards(): lax.all_to_all(tables, ('grp', 'tok'), split_axis=0, concat_axis=0, tiled...  6.33 us
    pallas_call x10, Pallas kernels, call(): pl.pallas_call(body, out_shape=outs, in_specs=in_specs, out_specs=jax.tre...  6.32 us
    all_to_all x1, starting transfers between devices, shards(): lax.all_to_all(centered, ('grp', 'tok'), split_axis=0, concat_axis=0, til...  4.8 us
    all_to_all x1, waiting for transfers between devices, shards(): lax.all_to_all(centered, ('grp', 'tok'), split_axis=0, concat_axis=0, til...  4.19 us
    all_to_all x1, starting transfers between devices, shards(): lax.all_to_all(tables, ('grp', 'tok'), split_axis=0, concat_axis=0, tiled...  2.55 us
  transfers between devices with their start and end apart: 17, of which 8 were waited for; matrix products, arithmetic and copies ran while one was open for 0% of the time, Pallas kernels for 5%

profile of v20, /device:TPU:0, one launch (start us, length us, event | category | flops | bytes accessed | tf_op | source)
XLA Modules:
  0.0 57.1 jit_solution(16468371290910552669)
XLA Ops:
  0.6 1.4 %shard_map.77 = (bf16[32,1024]{1,0:T(8,128)(2,1)S(1)}, bf16[64,1024]{1,0:T(8,128)(2,1)S(1)}, bf16[208,512]{1,0:T(8,128)(2,1)S(1)}, bf16[144,512]{1,0:T(8,128)(2,...) custom-call(bf16[32,2048]{1,0:T(8,128)(2,1)} %states_hbm.1, f32[1,2048]{1,0:T(1,128)} %bitcast.4, ...), custom_call_target="tpu_custom_call" | custom-call | tf_op jit(solution)/shard_map/pallas_call | solution.py:29
  2.0 3.0 %collective-permute-start = (bf16[304,512]{1,0:T(8,128)(2,1)S(1)}, bf16[304,512]{1,0:T(8,128)(2,1)S(1)}, u32[]{:S(2)}, u32[]{:S(2)}) collective-permute-start(bf16[304,512]{1,0:T(8,128)(2,1)S(1)} %get-tuple-element.16), channel_id=1, source_target_pairs={{0,1},{1,0},{2,3},{3,2},{4,5},{5,4},{6,7},{7,6},{8,9},{9,8},{10,11... | collective-permute-start | bytes 933896 | tf_op jit(solution)/shard_map/ppermute | solution.py:21
  5.0 1.6 %collective-permute-start.3 = (bf16[64,1024]{1,0:T(8,128)(2,1)S(1)}, bf16[64,1024]{1,0:T(8,128)(2,1)S(1)}, u32[]{:S(2)}, u32[]{:S(2)}) collective-permute-start(bf16[64,1024]{1,0:T(8,128)(2,1)S(1)} %get-tuple-element.18), channel_id=1, source_target_pairs={{0,2},{1,3},{2,0},{3,1},{4,6},{5,7},{6,4},{7,5},{8,10},{9,11},{10,... | collective-permute-start | bytes 393224 | tf_op jit(solution)/shard_map/ppermute | solution.py:21
  6.6 2.5 %collective-permute-start.1 = (bf16[32,1024]{1,0:T(8,128)(2,1)S(1)}, bf16[32,1024]{1,0:T(8,128)(2,1)S(1)}, u32[]{:S(2)}, u32[]{:S(2)}) collective-permute-start(bf16[32,1024]{1,0:T(8,128)(2,1)S(1)} %get-tuple-element.17.refs_3_), channel_id=1, source_target_pairs={{0,6},{1,7},{2,4},{3,5},{4,2},{5,3},{6,0},{7,1},{8,14},{9,15},{10,... | collective-permute-start | bytes 196616 | tf_op jit(solution)/shard_map/ppermute | solution.py:21
  9.1 0.1 collective-permute-start.2
  9.2 5.0 %collective-permute-done.1.refs_0_ = bf16[32,1024]{1,0:T(8,128)(2,1)S(1)} collective-permute-done((bf16[32,1024]{1,0:T(8,128)(2,1)S(1)}, bf16[32,1024]{1,0:T(8,128)(2,1)S(1)}, u32[]{:S(2)}, u32[]{:S(2)}) %collective-permute-start.1) | collective-permute-done | bytes 65568 | tf_op jit(solution)/shard_map/ppermute | solution.py:21
  14.2 1.3 %collective-permute-done.2.refs_1_ = bf16[32,1024]{1,0:T(8,128)(2,1)S(1)} collective-permute-done((bf16[32,1024]{1,0:T(8,128)(2,1)S(1)}, bf16[32,1024]{1,0:T(8,128)(2,1)S(1)}, u32[]{:S(2)}, u32[]{:S(2)}) %collective-permute-start.2) | collective-permute-done | bytes 65568 | tf_op jit(solution)/shard_map/ppermute | solution.py:21
  15.5 0.0 collective-permute-done.3.refs_2_.refs_5_
  15.5 0.0 collective-permute-done.after_ref.second_ref.refs_7_
  15.6 0.6 %collective-permute-start.5 = (bf16[128,1024]{1,0:T(8,128)(2,1)S(1)}, bf16[128,1024]{1,0:T(8,128)(2,1)S(1)}, u32[]{:S(2)}, u32[]{:S(2)}) collective-permute-start(bf16[128,1024]{1,0:T(8,128)(2,1)S(1)} %shard_map.78.after_ref.near_ref), channel_id=1, source_target_pairs={{0,1},{1,0},{2,3},{3,2},{4,5},{5,4},{6,7},{7,6},{8,9},{9,8},{10,11... | collective-permute-start | bytes 786440 | tf_op jit(solution)/shard_map/ppermute | solution.py:21
  16.2 0.0 copy-start
  16.2 0.0 copy-start.1
  16.2 0.1 collective-permute-start.4
  16.3 0.1 collective-permute-start.7
  16.4 5.6 %collective-permute-done.5.far_ref.refs_1_ = bf16[128,1024]{1,0:T(8,128)(2,1)S(1)} collective-permute-done((bf16[128,1024]{1,0:T(8,128)(2,1)S(1)}, bf16[128,1024]{1,0:T(8,128)(2,1)S(1)}, u32[]{:S(2)}, u32[]{:S(2)}) %collective-permute-start.5) | collective-permute-done | bytes 262176 | tf_op jit(solution)/shard_map/ppermute | solution.py:21
  22.0 0.0 collective-permute-start.6
  22.0 0.5 collective-permute-start.11
  22.6 0.0 collective-permute-done.7.near2_ref
  22.6 0.0 copy-done
  22.6 0.0 copy-done.1
  22.6 0.8 %shard_map.80 = (bf16[192,128]{1,0:T(8,128)(2,1)S(1)}, f32[192,128]{1,0:T(8,128)S(1)}, f32[192,128]{1,0:T(8,128)S(1)}) custom-call(bf16[128,1024]{1,0:T(8,128)(2,1)S(1)} %shard_map.78.after_ref.near_ref, bf16[128,1024]{1,0:T(8,128)(2,1)S(1)} %collective-permute-done.7.near2_ref, bf16[128,1024]{1,0:T(8,128)(2,1)S(1)} %collective-permute-done.5.far_ref.refs_1_, ...), custom_call_target="tpu_custom_call" | custom-call | tf_op jit(solution)/shard_map/pallas_call | solution.py:29
  23.3 1.0 %collective-permute-done.4.after_ref.refs_6_ = bf16[352,512]{1,0:T(8,128)(2,1)S(1)} collective-permute-done((bf16[352,512]{1,0:T(8,128)(2,1)S(1)}, bf16[352,512]{1,0:T(8,128)(2,1)S(1)}, u32[]{:S(2)}, u32[]{:S(2)}) %collective-permute-start.4) | collective-permute-done | bytes 360480 | tf_op jit(solution)/shard_map/ppermute | solution.py:21
  24.3 0.0 collective-permute-done.6.far2_ref
  24.3 0.4 shard_map.81.refs_0_
  24.7 1.3 %collective-permute-start.10 = (bf16[192,256]{1,0:T(8,128)(2,1)S(1)}, bf16[192,256]{1,0:T(8,128)(2,1)S(1)}, u32[]{:S(2)}, u32[]{:S(2)}) collective-permute-start(bf16[192,256]{1,0:T(8,128)(2,1)S(1)} %shard_map.81.refs_0_), channel_id=1, source_target_pairs={{0,3},{1,2},{2,1},{3,0},{4,7},{5,6},{6,5},{7,4},{8,11},{9,10},{10,... | collective-permute-start | bytes 294920 | tf_op jit(solution)/shard_map/ppermute | solution.py:21
  26.0 0.8 %collective-permute-start.8 = (bf16[192,256]{1,0:T(8,128)(2,1)S(1)}, bf16[192,256]{1,0:T(8,128)(2,1)S(1)}, u32[]{:S(2)}, u32[]{:S(2)}) collective-permute-start(bf16[192,256]{1,0:T(8,128)(2,1)S(1)} %shard_map.81.refs_0_), channel_id=1, source_target_pairs={{0,1},{1,0},{2,3},{3,2},{4,5},{5,4},{6,7},{7,6},{8,9},{9,8},{10,11... | collective-permute-start | bytes 294920 | tf_op jit(solution)/shard_map/ppermute | solution.py:21
  26.8 1.5 %collective-permute-start.9 = (bf16[192,256]{1,0:T(8,128)(2,1)S(1)}, bf16[192,256]{1,0:T(8,128)(2,1)S(1)}, u32[]{:S(2)}, u32[]{:S(2)}) collective-permute-start(bf16[192,256]{1,0:T(8,128)(2,1)S(1)} %shard_map.81.refs_0_), channel_id=1, source_target_pairs={{0,2},{1,3},{2,0},{3,1},{4,6},{5,7},{6,4},{7,5},{8,10},{9,11},{10,... | collective-permute-start | bytes 294920 | tf_op jit(solution)/shard_map/ppermute | solution.py:21
  28.3 0.0 collective-permute-done.11.refs_8_
  28.3 2.6 %collective-permute-done.10.refs_3_ = bf16[192,256]{1,0:T(8,128)(2,1)S(1)} collective-permute-done((bf16[192,256]{1,0:T(8,128)(2,1)S(1)}, bf16[192,256]{1,0:T(8,128)(2,1)S(1)}, u32[]{:S(2)}, u32[]{:S(2)}) %collective-permute-start.10) | collective-permute-done | bytes 98336 | tf_op jit(solution)/shard_map/ppermute | solution.py:21
  30.9 0.9 %collective-permute-done.8.refs_1_ = bf16[192,256]{1,0:T(8,128)(2,1)S(1)} collective-permute-done((bf16[192,256]{1,0:T(8,128)(2,1)S(1)}, bf16[192,256]{1,0:T(8,128)(2,1)S(1)}, u32[]{:S(2)}, u32[]{:S(2)}) %collective-permute-start.8) | collective-permute-done | bytes 98336 | tf_op jit(solution)/shard_map/ppermute | solution.py:21
  31.8 0.0 collective-permute-done.9.refs_2_
  31.8 1.5 %shard_map.83 = (bf16[64,512]{1,0:T(8,128)(2,1)S(1)}, bf16[64,512]{1,0:T(8,128)(2,1)S(1)}, bf16[64,512]{1,0:T(8,128)(2,1)S(1)}, bf16[64,512]{1,0:T(8,128)(2,1)S(1)}, bf16[512,128]{1,0:T(8,128)(2,1)}) custom-call(bf16[192,256]{1,0:T(8,128)(2,1)S(1)} %shard_map.81.refs_0_, bf16[192,256]{1,0:T(8,128)(2,1)S(1)} %collective-permute-done.8.refs_1_, ...), custom_call_target="tpu_custom_call" | custom-call | tf_op jit(solution)/shard_map/pallas_call | solution.py:29
  33.3 4.8 %all-to-all-start = ((bf16[32,16,128]{2,1,0:T(8,128)(2,1)}), bf16[32,16,128]{2,1,0:T(8,128)(2,1)S(1)}, u32[]{:S(2)}, u32[]{:S(2)}) async-start(bf16[32,16,128]{2,1,0:T(8,128)(2,1)} %bitcast.1), calls=%async_computation | async-start | bytes 262144 | tf_op jit(solution)/shard_map/all_to_all | solution.py:356
  38.1 1.8 %collective-permute-start.12 = (bf16[64,512]{1,0:T(8,128)(2,1)S(1)}, bf16[64,512]{1,0:T(8,128)(2,1)S(1)}, u32[]{:S(2)}, u32[]{:S(2)}) collective-permute-start(bf16[64,512]{1,0:T(8,128)(2,1)S(1)} %get-tuple-element.26), channel_id=1, source_target_pairs={{0,1},{1,0},{2,3},{3,2},{4,5},{5,4},{6,7},{7,6},{8,9},{9,8},{10,11... | collective-permute-start | bytes 196616 | tf_op jit(solution)/shard_map/ppermute | solution.py:21
  39.9 1.5 %collective-permute-start.13 = (bf16[64,512]{1,0:T(8,128)(2,1)S(1)}, bf16[64,512]{1,0:T(8,128)(2,1)S(1)}, u32[]{:S(2)}, u32[]{:S(2)}) collective-permute-start(bf16[64,512]{1,0:T(8,128)(2,1)S(1)} %get-tuple-element.27), channel_id=1, source_target_pairs={{0,2},{1,3},{2,0},{3,1},{4,6},{5,7},{6,4},{7,5},{8,10},{9,11},{10,... | collective-permute-start | bytes 196616 | tf_op jit(solution)/shard_map/ppermute | solution.py:21
  41.4 0.3 collective-permute-start.14
  41.6 4.2 %all-to-all-done = bf16[32,16,128]{2,1,0:T(8,128)(2,1)S(1)} async-done(((bf16[32,16,128]{2,1,0:T(8,128)(2,1)}), bf16[32,16,128]{2,1,0:T(8,128)(2,1)S(1)}, u32[]{:S(2)}, u32[]{:S(2)}) %all-to-all-start) | async-done | bytes 131104 | tf_op jit(solution)/shard_map/all_to_all | solution.py:356
  45.8 0.8 %shard_map.85 = f32[32,1,128]{2,1,0:T(1,128)} custom-call(bf16[8,4,16,128]{3,2,1,0:T(8,128)(2,1)S(1)} %bitcast.3), custom_call_target="tpu_custom_call" | custom-call | tf_op jit(solution)/shard_map/pallas_call | solution.py:29
  46.6 2.6 %all-to-all-start.1 = ((f32[32,1,128]{2,1,0:T(1,128)}), f32[32,1,128]{2,1,0:T(1,128)S(1)}, u32[]{:S(2)}, u32[]{:S(2)}) async-start(f32[32,1,128]{2,1,0:T(1,128)} %shard_map.85), calls=%async_computation.1 | async-start | bytes 32768 | tf_op jit(solution)/shard_map/all_to_all | solution.py:367
  49.2 0.0 collective-permute-done.12.refs_1_
  49.2 0.0 collective-permute-done.13.refs_2_
  49.2 0.0 collective-permute-done.14.refs_3_
  49.2 0.7 %shard_map.84 = bf16[64,2048]{1,0:T(8,128)(2,1)} custom-call(bf16[64,512]{1,0:T(8,128)(2,1)S(1)} %get-tuple-element.25.refs_0_, bf16[64,512]{1,0:T(8,128)(2,1)S(1)} %collective-permute-done.12.refs_1_, bf16[64,512]{1,0:T(8,128)(2,1)S(1)} %collective-permute-done.13.refs_2_, bf16[64,512]{1,0:T(8,128)(2,1)S(1)} %collective-permute-done.14.refs_3_), custom_call_target="tpu_custom_call" | custom-call | tf_op jit(solution)/shard_map/pallas_call | solution.py:29
  49.9 6.3 %all-to-all-done.1.tables_ref = f32[32,1,128]{2,1,0:T(1,128)S(1)} async-done(((f32[32,1,128]{2,1,0:T(1,128)}), f32[32,1,128]{2,1,0:T(1,128)S(1)}, u32[]{:S(2)}, u32[]{:S(2)}) %all-to-all-start.1) | async-done | bytes 16416 | tf_op jit(solution)/shard_map/all_to_all | solution.py:367
  56.3 0.8 %shard_map.86 = f32[8,8]{1,0:T(8,128)} custom-call(f32[32,1,128]{2,1,0:T(1,128)S(1)} %all-to-all-done.1.tables_ref), custom_call_target="tpu_custom_call" | custom-call | tf_op jit(solution)/shard_map/pallas_call | solution.py:29
  (3 shorter events, 0.1 us)
Async XLA Ops:
  2.0 13.5 %collective-permute-start = (bf16[304,512]{1,0:T(8,128)(2,1)S(1)}, bf16[304,512]{1,0:T(8,128)(2,1)S(1)}, u32[]{:S(2)}, u32[]{:S(2)}) collective-permute-start(bf16[304,512]{1,0:T(8,128)(2,1)S(1)} %get-tuple-element.16), channel_id=1, source_target_pairs={{0,1},{1,0},{2,3},{3,2},{4,5},{5,4},{6,7},{7,6},{8,9},{9,8},{10,11... | collective-permute-start | bytes 933896 | tf_op jit(solution)/shard_map/ppermute | solution.py:21
  5.0 10.5 %collective-permute-start.3 = (bf16[64,1024]{1,0:T(8,128)(2,1)S(1)}, bf16[64,1024]{1,0:T(8,128)(2,1)S(1)}, u32[]{:S(2)}, u32[]{:S(2)}) collective-permute-start(bf16[64,1024]{1,0:T(8,128)(2,1)S(1)} %get-tuple-element.18), channel_id=1, source_target_pairs={{0,2},{1,3},{2,0},{3,1},{4,6},{5,7},{6,4},{7,5},{8,10},{9,11},{10,... | collective-permute-start | bytes 393224 | tf_op jit(solution)/shard_map/ppermute | solution.py:21
  6.6 7.6 %collective-permute-start.1 = (bf16[32,1024]{1,0:T(8,128)(2,1)S(1)}, bf16[32,1024]{1,0:T(8,128)(2,1)S(1)}, u32[]{:S(2)}, u32[]{:S(2)}) collective-permute-start(bf16[32,1024]{1,0:T(8,128)(2,1)S(1)} %get-tuple-element.17.refs_3_), channel_id=1, source_target_pairs={{0,6},{1,7},{2,4},{3,5},{4,2},{5,3},{6,0},{7,1},{8,14},{9,15},{10,... | collective-permute-start | bytes 196616 | tf_op jit(solution)/shard_map/ppermute | solution.py:21
  9.1 6.5 %collective-permute-start.2 = (bf16[32,1024]{1,0:T(8,128)(2,1)S(1)}, bf16[32,1024]{1,0:T(8,128)(2,1)S(1)}, u32[]{:S(2)}, u32[]{:S(2)}) collective-permute-start(bf16[32,1024]{1,0:T(8,128)(2,1)S(1)} %get-tuple-element.17.refs_3_), channel_id=1, source_target_pairs={{0,4},{1,5},{2,6},{3,7},{4,0},{5,1},{6,2},{7,3},{8,12},{9,13},{10,... | collective-permute-start | bytes 196616 | tf_op jit(solution)/shard_map/ppermute | solution.py:21
  15.6 6.4 %collective-permute-start.5 = (bf16[128,1024]{1,0:T(8,128)(2,1)S(1)}, bf16[128,1024]{1,0:T(8,128)(2,1)S(1)}, u32[]{:S(2)}, u32[]{:S(2)}) collective-permute-start(bf16[128,1024]{1,0:T(8,128)(2,1)S(1)} %shard_map.78.after_ref.near_ref), channel_id=1, source_target_pairs={{0,1},{1,0},{2,3},{3,2},{4,5},{5,4},{6,7},{7,6},{8,9},{9,8},{10,11... | collective-permute-start | bytes 786440 | tf_op jit(solution)/shard_map/ppermute | solution.py:21
  16.2 6.4 %copy-start = (bf16[192,2048]{1,0:T(8,128)(2,1)S(1)}, bf16[192,2048]{1,0:T(8,128)(2,1)}, u32[]{:S(2)}) copy-start(bf16[192,2048]{1,0:T(8,128)(2,1)} %gate_ref.3) | copy-start | bytes 2359300
  16.2 6.4 %copy-start.1 = (bf16[192,2048]{1,0:T(8,128)(2,1)S(1)}, bf16[192,2048]{1,0:T(8,128)(2,1)}, u32[]{:S(2)}) copy-start(bf16[192,2048]{1,0:T(8,128)(2,1)} %up_ref.3) | copy-start | bytes 2359300
  16.2 8.1 %collective-permute-start.4 = (bf16[352,512]{1,0:T(8,128)(2,1)S(1)}, bf16[352,512]{1,0:T(8,128)(2,1)S(1)}, u32[]{:S(2)}, u32[]{:S(2)}) collective-permute-start(bf16[352,512]{1,0:T(8,128)(2,1)S(1)} %shard_map.79), channel_id=1, source_target_pairs={{0,2},{1,3},{2,0},{3,1},{4,6},{5,7},{6,4},{7,5},{8,10},{9,11},{10,... | collective-permute-start | bytes 1081352 | tf_op jit(solution)/shard_map/ppermute | solution.py:21
  16.3 6.3 %collective-permute-start.7 = (bf16[128,1024]{1,0:T(8,128)(2,1)S(1)}, bf16[128,1024]{1,0:T(8,128)(2,1)S(1)}, u32[]{:S(2)}, u32[]{:S(2)}) collective-permute-start(bf16[128,1024]{1,0:T(8,128)(2,1)S(1)} %shard_map.78.after_ref.near_ref), channel_id=1, source_target_pairs={{0,8},{8,0},{16,24},{24,16},{1,9},{9,1},{17,25},{25,17},{2,10},{10... | collective-permute-start | bytes 786440 | tf_op jit(solution)/shard_map/ppermute | solution.py:21
  22.0 2.3 %collective-permute-start.6 = (bf16[128,1024]{1,0:T(8,128)(2,1)S(1)}, bf16[128,1024]{1,0:T(8,128)(2,1)S(1)}, u32[]{:S(2)}, u32[]{:S(2)}) collective-permute-start(bf16[128,1024]{1,0:T(8,128)(2,1)S(1)} %collective-permute-done.5.far_ref.refs_1_), channel_id=1, source_target_pairs={{0,8},{8,0},{16,24},{24,16},{1,9},{9,1},{17,25},{25,17},{2,10},{10... | collective-permute-start | bytes 786440 | tf_op jit(solution)/shard_map/ppermute | solution.py:21
  22.0 6.2 %collective-permute-start.11 = (bf16[112,512]{1,0:T(8,128)(2,1)S(1)}, bf16[112,512]{1,0:T(8,128)(2,1)S(1)}, u32[]{:S(2)}, u32[]{:S(2)}) collective-permute-start(bf16[112,512]{1,0:T(8,128)(2,1)S(1)} %shard_map.82), channel_id=1, source_target_pairs={{0,1},{1,0},{2,3},{3,2},{4,5},{5,4},{6,7},{7,6},{8,9},{9,8},{10,11... | collective-permute-start | bytes 344072 | tf_op jit(solution)/shard_map/ppermute | solution.py:21
  24.7 6.2 %collective-permute-start.10 = (bf16[192,256]{1,0:T(8,128)(2,1)S(1)}, bf16[192,256]{1,0:T(8,128)(2,1)S(1)}, u32[]{:S(2)}, u32[]{:S(2)}) collective-permute-start(bf16[192,256]{1,0:T(8,128)(2,1)S(1)} %shard_map.81.refs_0_), channel_id=1, source_target_pairs={{0,3},{1,2},{2,1},{3,0},{4,7},{5,6},{6,5},{7,4},{8,11},{9,10},{10,... | collective-permute-start | bytes 294920 | tf_op jit(solution)/shard_map/ppermute | solution.py:21
  26.0 5.8 %collective-permute-start.8 = (bf16[192,256]{1,0:T(8,128)(2,1)S(1)}, bf16[192,256]{1,0:T(8,128)(2,1)S(1)}, u32[]{:S(2)}, u32[]{:S(2)}) collective-permute-start(bf16[192,256]{1,0:T(8,128)(2,1)S(1)} %shard_map.81.refs_0_), channel_id=1, source_target_pairs={{0,1},{1,0},{2,3},{3,2},{4,5},{5,4},{6,7},{7,6},{8,9},{9,8},{10,11... | collective-permute-start | bytes 294920 | tf_op jit(solution)/shard_map/ppermute | solution.py:21
  26.8 5.0 %collective-permute-start.9 = (bf16[192,256]{1,0:T(8,128)(2,1)S(1)}, bf16[192,256]{1,0:T(8,128)(2,1)S(1)}, u32[]{:S(2)}, u32[]{:S(2)}) collective-permute-start(bf16[192,256]{1,0:T(8,128)(2,1)S(1)} %shard_map.81.refs_0_), channel_id=1, source_target_pairs={{0,2},{1,3},{2,0},{3,1},{4,6},{5,7},{6,4},{7,5},{8,10},{9,11},{10,... | collective-permute-start | bytes 294920 | tf_op jit(solution)/shard_map/ppermute | solution.py:21
  33.3 12.6 %all-to-all-start = ((bf16[32,16,128]{2,1,0:T(8,128)(2,1)}), bf16[32,16,128]{2,1,0:T(8,128)(2,1)S(1)}, u32[]{:S(2)}, u32[]{:S(2)}) async-start(bf16[32,16,128]{2,1,0:T(8,128)(2,1)} %bitcast.1), calls=%async_computation | async-start | bytes 262144 | tf_op jit(solution)/shard_map/all_to_all | solution.py:356
  38.1 11.1 %collective-permute-start.12 = (bf16[64,512]{1,0:T(8,128)(2,1)S(1)}, bf16[64,512]{1,0:T(8,128)(2,1)S(1)}, u32[]{:S(2)}, u32[]{:S(2)}) collective-permute-start(bf16[64,512]{1,0:T(8,128)(2,1)S(1)} %get-tuple-element.26), channel_id=1, source_target_pairs={{0,1},{1,0},{2,3},{3,2},{4,5},{5,4},{6,7},{7,6},{8,9},{9,8},{10,11... | collective-permute-start | bytes 196616 | tf_op jit(solution)/shard_map/ppermute | solution.py:21
  39.9 9.2 %collective-permute-start.13 = (bf16[64,512]{1,0:T(8,128)(2,1)S(1)}, bf16[64,512]{1,0:T(8,128)(2,1)S(1)}, u32[]{:S(2)}, u32[]{:S(2)}) collective-permute-start(bf16[64,512]{1,0:T(8,128)(2,1)S(1)} %get-tuple-element.27), channel_id=1, source_target_pairs={{0,2},{1,3},{2,0},{3,1},{4,6},{5,7},{6,4},{7,5},{8,10},{9,11},{10,... | collective-permute-start | bytes 196616 | tf_op jit(solution)/shard_map/ppermute | solution.py:21
  41.4 7.8 %collective-permute-start.14 = (bf16[64,512]{1,0:T(8,128)(2,1)S(1)}, bf16[64,512]{1,0:T(8,128)(2,1)S(1)}, u32[]{:S(2)}, u32[]{:S(2)}) collective-permute-start(bf16[64,512]{1,0:T(8,128)(2,1)S(1)} %get-tuple-element.28), channel_id=1, source_target_pairs={{0,3},{1,2},{2,1},{3,0},{4,7},{5,6},{6,5},{7,4},{8,11},{9,10},{10,... | collective-permute-start | bytes 196616 | tf_op jit(solution)/shard_map/ppermute | solution.py:21
  46.6 9.7 %all-to-all-start.1 = ((f32[32,1,128]{2,1,0:T(1,128)}), f32[32,1,128]{2,1,0:T(1,128)S(1)}, u32[]{:S(2)}, u32[]{:S(2)}) async-start(f32[32,1,128]{2,1,0:T(1,128)} %shard_map.85), calls=%async_computation.1 | async-start | bytes 32768 | tf_op jit(solution)/shard_map/all_to_all | solution.py:367

commit v21 on v20

--- a/solution.py
+++ b/solution.py
@@ -284,7 +284,7 @@
     part, token_part = model // HOLDERS, tokens // HOLDERS
 
     count = depth + TILE
-    beside, first_x = depth // 6 // TILE * TILE, depth // 2 // TILE * TILE
+    beside, first_x = depth // 4 // TILE * TILE, depth // 2 // TILE * TILE
     own, with_z, down_own, down_z, down_early, down_late = call(
         first_kernel,
         [jax.ShapeDtypeStruct((n, model // 2), bf16) for n in (rows, rows + beside)]

time: 57.3 us -> 56.4 us (0.984)
  starting transfers between devices: 22.9 us -> 21.8 us
    all_to_all x1, starting transfers between devices: 4.8 us -> 3.48 us  [shards(): lax.all_to_all(centered, ('grp', 'tok'), split_axis=0, concat_axis=0, til...]
  transfers between devices with their start and end apart: 17 -> 17, of which waited for: 8 -> 9; matrix products, arithmetic and copies ran while one was open for 0% -> 0% of each run, Pallas kernels for 5% -> 5%
where the time goes in v21:
time: 56.4 us; the launch traced here: 56.1 us
  waiting for transfers between devices  27.3 us (48%)
  starting transfers between devices  21.8 us (39%)
  Pallas kernels  6.33 us (11%)
  between operations  0.76 us (1%)
    ppermute x15, waiting for transfers between devices, swapped(): lax.ppermute(array, axis, [(i, i ^ mask) for i in range(lax.axis_size(axi...  16.7 us
    ppermute x15, starting transfers between devices, swapped(): lax.ppermute(array, axis, [(i, i ^ mask) for i in range(lax.axis_size(axi...  15.8 us
    all_to_all x1, waiting for transfers between devices, shards(): lax.all_to_all(tables, ('grp', 'tok'), split_axis=0, concat_axis=0, tiled...  6.33 us
    pallas_call x10, Pallas kernels, call(): pl.pallas_call(body, out_shape=outs, in_specs=in_specs, out_specs=jax.tre...  6.33 us
    all_to_all x1, waiting for transfers between devices, shards(): lax.all_to_all(centered, ('grp', 'tok'), split_axis=0, concat_axis=0, til...  4.19 us
    all_to_all x1, starting transfers between devices, shards(): lax.all_to_all(centered, ('grp', 'tok'), split_axis=0, concat_axis=0, til...  3.48 us
    all_to_all x1, starting transfers between devices, shards(): lax.all_to_all(tables, ('grp', 'tok'), split_axis=0, concat_axis=0, tiled...  2.55 us
  transfers between devices with their start and end apart: 17, of which 9 were waited for; matrix products, arithmetic and copies ran while one was open for 0% of the time, Pallas kernels for 5%

profile of v21, /device:TPU:0, one launch (start us, length us, event | category | flops | bytes accessed | tf_op | source)
XLA Modules:
  0.0 56.1 jit_solution(11588600503622034688)
XLA Ops:
  0.6 1.4 %shard_map.77 = (bf16[32,1024]{1,0:T(8,128)(2,1)S(1)}, bf16[80,1024]{1,0:T(8,128)(2,1)S(1)}, bf16[208,512]{1,0:T(8,128)(2,1)S(1)}, bf16[112,512]{1,0:T(8,128)(2,...) custom-call(bf16[32,2048]{1,0:T(8,128)(2,1)} %states_hbm.1, f32[1,2048]{1,0:T(1,128)} %bitcast.4, ...), custom_call_target="tpu_custom_call" | custom-call | tf_op jit(solution)/shard_map/pallas_call | solution.py:29
  2.0 3.0 %collective-permute-start = (bf16[304,512]{1,0:T(8,128)(2,1)S(1)}, bf16[304,512]{1,0:T(8,128)(2,1)S(1)}, u32[]{:S(2)}, u32[]{:S(2)}) collective-permute-start(bf16[304,512]{1,0:T(8,128)(2,1)S(1)} %get-tuple-element.16), channel_id=1, source_target_pairs={{0,1},{1,0},{2,3},{3,2},{4,5},{5,4},{6,7},{7,6},{8,9},{9,8},{10,11... | collective-permute-start | bytes 933896 | tf_op jit(solution)/shard_map/ppermute | solution.py:21
  5.0 1.6 %collective-permute-start.3 = (bf16[80,1024]{1,0:T(8,128)(2,1)S(1)}, bf16[80,1024]{1,0:T(8,128)(2,1)S(1)}, u32[]{:S(2)}, u32[]{:S(2)}) collective-permute-start(bf16[80,1024]{1,0:T(8,128)(2,1)S(1)} %get-tuple-element.18), channel_id=1, source_target_pairs={{0,2},{1,3},{2,0},{3,1},{4,6},{5,7},{6,4},{7,5},{8,10},{9,11},{10,... | collective-permute-start | bytes 491528 | tf_op jit(solution)/shard_map/ppermute | solution.py:21
  6.6 2.5 %collective-permute-start.1 = (bf16[32,1024]{1,0:T(8,128)(2,1)S(1)}, bf16[32,1024]{1,0:T(8,128)(2,1)S(1)}, u32[]{:S(2)}, u32[]{:S(2)}) collective-permute-start(bf16[32,1024]{1,0:T(8,128)(2,1)S(1)} %get-tuple-element.17.refs_3_), channel_id=1, source_target_pairs={{0,6},{1,7},{2,4},{3,5},{4,2},{5,3},{6,0},{7,1},{8,14},{9,15},{10,... | collective-permute-start | bytes 196616 | tf_op jit(solution)/shard_map/ppermute | solution.py:21
  9.1 0.1 collective-permute-start.2
  9.2 5.7 %collective-permute-done.1.refs_0_ = bf16[32,1024]{1,0:T(8,128)(2,1)S(1)} collective-permute-done((bf16[32,1024]{1,0:T(8,128)(2,1)S(1)}, bf16[32,1024]{1,0:T(8,128)(2,1)S(1)}, u32[]{:S(2)}, u32[]{:S(2)}) %collective-permute-start.1) | collective-permute-done | bytes 65568 | tf_op jit(solution)/shard_map/ppermute | solution.py:21
  14.9 1.0 %collective-permute-done.2.refs_1_ = bf16[32,1024]{1,0:T(8,128)(2,1)S(1)} collective-permute-done((bf16[32,1024]{1,0:T(8,128)(2,1)S(1)}, bf16[32,1024]{1,0:T(8,128)(2,1)S(1)}, u32[]{:S(2)}, u32[]{:S(2)}) %collective-permute-start.2) | collective-permute-done | bytes 65568 | tf_op jit(solution)/shard_map/ppermute | solution.py:21
  15.9 0.0 collective-permute-done.3.refs_2_.refs_5_
  15.9 0.0 collective-permute-done.after_ref.second_ref.refs_7_
  15.9 0.0 copy-start.1
  15.9 0.0 copy-start
  15.9 0.6 %collective-permute-start.5 = (bf16[128,1024]{1,0:T(8,128)(2,1)S(1)}, bf16[128,1024]{1,0:T(8,128)(2,1)S(1)}, u32[]{:S(2)}, u32[]{:S(2)}) collective-permute-start(bf16[128,1024]{1,0:T(8,128)(2,1)S(1)} %shard_map.78.after_ref.near_ref), channel_id=1, source_target_pairs={{0,1},{1,0},{2,3},{3,2},{4,5},{5,4},{6,7},{7,6},{8,9},{9,8},{10,11... | collective-permute-start | bytes 786440 | tf_op jit(solution)/shard_map/ppermute | solution.py:21
  16.6 0.3 collective-permute-start.4
  16.9 0.0 collective-permute-start.7
  16.9 5.5 %collective-permute-done.5.far_ref.refs_1_ = bf16[128,1024]{1,0:T(8,128)(2,1)S(1)} collective-permute-done((bf16[128,1024]{1,0:T(8,128)(2,1)S(1)}, bf16[128,1024]{1,0:T(8,128)(2,1)S(1)}, u32[]{:S(2)}, u32[]{:S(2)}) %collective-permute-start.5) | collective-permute-done | bytes 262176 | tf_op jit(solution)/shard_map/ppermute | solution.py:21
  22.4 0.0 collective-permute-start.6
  22.4 0.5 collective-permute-start.11
  22.9 0.0 collective-permute-done.7.near2_ref
  22.9 0.0 copy-done.1
  22.9 0.0 copy-done
  22.9 0.8 %shard_map.80 = (bf16[192,128]{1,0:T(8,128)(2,1)S(1)}, f32[192,128]{1,0:T(8,128)S(1)}, f32[192,128]{1,0:T(8,128)S(1)}) custom-call(bf16[128,1024]{1,0:T(8,128)(2,1)S(1)} %shard_map.78.after_ref.near_ref, bf16[128,1024]{1,0:T(8,128)(2,1)S(1)} %collective-permute-done.7.near2_ref, bf16[128,1024]{1,0:T(8,128)(2,1)S(1)} %collective-permute-done.5.far_ref.refs_1_, ...), custom_call_target="tpu_custom_call" | custom-call | tf_op jit(solution)/shard_map/pallas_call | solution.py:29
  23.7 0.0 collective-permute-done.4.after_ref.refs_6_
  23.7 0.2 collective-permute-done.6.far2_ref
  23.9 0.4 shard_map.81.refs_0_
  24.3 1.6 %collective-permute-start.10 = (bf16[192,256]{1,0:T(8,128)(2,1)S(1)}, bf16[192,256]{1,0:T(8,128)(2,1)S(1)}, u32[]{:S(2)}, u32[]{:S(2)}) collective-permute-start(bf16[192,256]{1,0:T(8,128)(2,1)S(1)} %shard_map.81.refs_0_), channel_id=1, source_target_pairs={{0,3},{1,2},{2,1},{3,0},{4,7},{5,6},{6,5},{7,4},{8,11},{9,10},{10,... | collective-permute-start | bytes 294920 | tf_op jit(solution)/shard_map/ppermute | solution.py:21
  25.9 0.5 collective-permute-start.8
  26.4 1.4 %collective-permute-start.9 = (bf16[192,256]{1,0:T(8,128)(2,1)S(1)}, bf16[192,256]{1,0:T(8,128)(2,1)S(1)}, u32[]{:S(2)}, u32[]{:S(2)}) collective-permute-start(bf16[192,256]{1,0:T(8,128)(2,1)S(1)} %shard_map.81.refs_0_), channel_id=1, source_target_pairs={{0,2},{1,3},{2,0},{3,1},{4,6},{5,7},{6,4},{7,5},{8,10},{9,11},{10,... | collective-permute-start | bytes 294920 | tf_op jit(solution)/shard_map/ppermute | solution.py:21
  27.9 0.1 collective-permute-done.11.refs_8_
  28.0 3.0 %collective-permute-done.10.refs_3_ = bf16[192,256]{1,0:T(8,128)(2,1)S(1)} collective-permute-done((bf16[192,256]{1,0:T(8,128)(2,1)S(1)}, bf16[192,256]{1,0:T(8,128)(2,1)S(1)}, u32[]{:S(2)}, u32[]{:S(2)}) %collective-permute-start.10) | collective-permute-done | bytes 98336 | tf_op jit(solution)/shard_map/ppermute | solution.py:21
  30.9 1.3 %collective-permute-done.8.refs_1_ = bf16[192,256]{1,0:T(8,128)(2,1)S(1)} collective-permute-done((bf16[192,256]{1,0:T(8,128)(2,1)S(1)}, bf16[192,256]{1,0:T(8,128)(2,1)S(1)}, u32[]{:S(2)}, u32[]{:S(2)}) %collective-permute-start.8) | collective-permute-done | bytes 98336 | tf_op jit(solution)/shard_map/ppermute | solution.py:21
  32.2 0.0 collective-permute-done.9.refs_2_
  32.2 1.5 %shard_map.83 = (bf16[64,512]{1,0:T(8,128)(2,1)S(1)}, bf16[64,512]{1,0:T(8,128)(2,1)S(1)}, bf16[64,512]{1,0:T(8,128)(2,1)S(1)}, bf16[64,512]{1,0:T(8,128)(2,1)S(1)}, bf16[512,128]{1,0:T(8,128)(2,1)}) custom-call(bf16[192,256]{1,0:T(8,128)(2,1)S(1)} %shard_map.81.refs_0_, bf16[192,256]{1,0:T(8,128)(2,1)S(1)} %collective-permute-done.8.refs_1_, ...), custom_call_target="tpu_custom_call" | custom-call | tf_op jit(solution)/shard_map/pallas_call | solution.py:29
  33.7 3.5 %all-to-all-start = ((bf16[32,16,128]{2,1,0:T(8,128)(2,1)}), bf16[32,16,128]{2,1,0:T(8,128)(2,1)S(1)}, u32[]{:S(2)}, u32[]{:S(2)}) async-start(bf16[32,16,128]{2,1,0:T(8,128)(2,1)} %bitcast.1), calls=%async_computation | async-start | bytes 262144 | tf_op jit(solution)/shard_map/all_to_all | solution.py:356
  37.2 1.8 %collective-permute-start.12 = (bf16[64,512]{1,0:T(8,128)(2,1)S(1)}, bf16[64,512]{1,0:T(8,128)(2,1)S(1)}, u32[]{:S(2)}, u32[]{:S(2)}) collective-permute-start(bf16[64,512]{1,0:T(8,128)(2,1)S(1)} %get-tuple-element.26), channel_id=1, source_target_pairs={{0,1},{1,0},{2,3},{3,2},{4,5},{5,4},{6,7},{7,6},{8,9},{9,8},{10,11... | collective-permute-start | bytes 196616 | tf_op jit(solution)/shard_map/ppermute | solution.py:21
  39.0 1.5 %collective-permute-start.13 = (bf16[64,512]{1,0:T(8,128)(2,1)S(1)}, bf16[64,512]{1,0:T(8,128)(2,1)S(1)}, u32[]{:S(2)}, u32[]{:S(2)}) collective-permute-start(bf16[64,512]{1,0:T(8,128)(2,1)S(1)} %get-tuple-element.27), channel_id=1, source_target_pairs={{0,2},{1,3},{2,0},{3,1},{4,6},{5,7},{6,4},{7,5},{8,10},{9,11},{10,... | collective-permute-start | bytes 196616 | tf_op jit(solution)/shard_map/ppermute | solution.py:21
  40.5 0.3 collective-permute-start.14
  40.7 4.2 %all-to-all-done = bf16[32,16,128]{2,1,0:T(8,128)(2,1)S(1)} async-done(((bf16[32,16,128]{2,1,0:T(8,128)(2,1)}), bf16[32,16,128]{2,1,0:T(8,128)(2,1)S(1)}, u32[]{:S(2)}, u32[]{:S(2)}) %all-to-all-start) | async-done | bytes 131104 | tf_op jit(solution)/shard_map/all_to_all | solution.py:356
  44.9 0.8 %shard_map.85 = f32[32,1,128]{2,1,0:T(1,128)} custom-call(bf16[8,4,16,128]{3,2,1,0:T(8,128)(2,1)S(1)} %bitcast.3), custom_call_target="tpu_custom_call" | custom-call | tf_op jit(solution)/shard_map/pallas_call | solution.py:29
  45.7 2.6 %all-to-all-start.1 = ((f32[32,1,128]{2,1,0:T(1,128)}), f32[32,1,128]{2,1,0:T(1,128)S(1)}, u32[]{:S(2)}, u32[]{:S(2)}) async-start(f32[32,1,128]{2,1,0:T(1,128)} %shard_map.85), calls=%async_computation.1 | async-start | bytes 32768 | tf_op jit(solution)/shard_map/all_to_all | solution.py:367
  48.2 0.0 collective-permute-done.12.refs_1_
  48.2 0.0 collective-permute-done.13.refs_2_
  48.2 0.0 collective-permute-done.14.refs_3_
  48.3 0.7 %shard_map.84 = bf16[64,2048]{1,0:T(8,128)(2,1)} custom-call(bf16[64,512]{1,0:T(8,128)(2,1)S(1)} %get-tuple-element.25.refs_0_, bf16[64,512]{1,0:T(8,128)(2,1)S(1)} %collective-permute-done.12.refs_1_, bf16[64,512]{1,0:T(8,128)(2,1)S(1)} %collective-permute-done.13.refs_2_, bf16[64,512]{1,0:T(8,128)(2,1)S(1)} %collective-permute-done.14.refs_3_), custom_call_target="tpu_custom_call" | custom-call | tf_op jit(solution)/shard_map/pallas_call | solution.py:29
  49.0 6.3 %all-to-all-done.1.tables_ref = f32[32,1,128]{2,1,0:T(1,128)S(1)} async-done(((f32[32,1,128]{2,1,0:T(1,128)}), f32[32,1,128]{2,1,0:T(1,128)S(1)}, u32[]{:S(2)}, u32[]{:S(2)}) %all-to-all-start.1) | async-done | bytes 16416 | tf_op jit(solution)/shard_map/all_to_all | solution.py:367
  55.3 0.8 %shard_map.86 = f32[8,8]{1,0:T(8,128)} custom-call(f32[32,1,128]{2,1,0:T(1,128)S(1)} %all-to-all-done.1.tables_ref), custom_call_target="tpu_custom_call" | custom-call | tf_op jit(solution)/shard_map/pallas_call | solution.py:29
  (3 shorter events, 0.1 us)
Async XLA Ops:
  2.0 13.9 %collective-permute-start = (bf16[304,512]{1,0:T(8,128)(2,1)S(1)}, bf16[304,512]{1,0:T(8,128)(2,1)S(1)}, u32[]{:S(2)}, u32[]{:S(2)}) collective-permute-start(bf16[304,512]{1,0:T(8,128)(2,1)S(1)} %get-tuple-element.16), channel_id=1, source_target_pairs={{0,1},{1,0},{2,3},{3,2},{4,5},{5,4},{6,7},{7,6},{8,9},{9,8},{10,11... | collective-permute-start | bytes 933896 | tf_op jit(solution)/shard_map/ppermute | solution.py:21
  5.0 10.9 %collective-permute-start.3 = (bf16[80,1024]{1,0:T(8,128)(2,1)S(1)}, bf16[80,1024]{1,0:T(8,128)(2,1)S(1)}, u32[]{:S(2)}, u32[]{:S(2)}) collective-permute-start(bf16[80,1024]{1,0:T(8,128)(2,1)S(1)} %get-tuple-element.18), channel_id=1, source_target_pairs={{0,2},{1,3},{2,0},{3,1},{4,6},{5,7},{6,4},{7,5},{8,10},{9,11},{10,... | collective-permute-start | bytes 491528 | tf_op jit(solution)/shard_map/ppermute | solution.py:21
  6.6 8.3 %collective-permute-start.1 = (bf16[32,1024]{1,0:T(8,128)(2,1)S(1)}, bf16[32,1024]{1,0:T(8,128)(2,1)S(1)}, u32[]{:S(2)}, u32[]{:S(2)}) collective-permute-start(bf16[32,1024]{1,0:T(8,128)(2,1)S(1)} %get-tuple-element.17.refs_3_), channel_id=1, source_target_pairs={{0,6},{1,7},{2,4},{3,5},{4,2},{5,3},{6,0},{7,1},{8,14},{9,15},{10,... | collective-permute-start | bytes 196616 | tf_op jit(solution)/shard_map/ppermute | solution.py:21
  9.1 6.8 %collective-permute-start.2 = (bf16[32,1024]{1,0:T(8,128)(2,1)S(1)}, bf16[32,1024]{1,0:T(8,128)(2,1)S(1)}, u32[]{:S(2)}, u32[]{:S(2)}) collective-permute-start(bf16[32,1024]{1,0:T(8,128)(2,1)S(1)} %get-tuple-element.17.refs_3_), channel_id=1, source_target_pairs={{0,4},{1,5},{2,6},{3,7},{4,0},{5,1},{6,2},{7,3},{8,12},{9,13},{10,... | collective-permute-start | bytes 196616 | tf_op jit(solution)/shard_map/ppermute | solution.py:21
  15.9 7.0 %copy-start.1 = (bf16[192,2048]{1,0:T(8,128)(2,1)S(1)}, bf16[192,2048]{1,0:T(8,128)(2,1)}, u32[]{:S(2)}) copy-start(bf16[192,2048]{1,0:T(8,128)(2,1)} %up_ref.3) | copy-start | bytes 2359300
  15.9 7.0 %copy-start = (bf16[192,2048]{1,0:T(8,128)(2,1)S(1)}, bf16[192,2048]{1,0:T(8,128)(2,1)}, u32[]{:S(2)}) copy-start(bf16[192,2048]{1,0:T(8,128)(2,1)} %gate_ref.3) | copy-start | bytes 2359300
  15.9 6.4 %collective-permute-start.5 = (bf16[128,1024]{1,0:T(8,128)(2,1)S(1)}, bf16[128,1024]{1,0:T(8,128)(2,1)S(1)}, u32[]{:S(2)}, u32[]{:S(2)}) collective-permute-start(bf16[128,1024]{1,0:T(8,128)(2,1)S(1)} %shard_map.78.after_ref.near_ref), channel_id=1, source_target_pairs={{0,1},{1,0},{2,3},{3,2},{4,5},{5,4},{6,7},{7,6},{8,9},{9,8},{10,11... | collective-permute-start | bytes 786440 | tf_op jit(solution)/shard_map/ppermute | solution.py:21
  16.6 7.1 %collective-permute-start.4 = (bf16[320,512]{1,0:T(8,128)(2,1)S(1)}, bf16[320,512]{1,0:T(8,128)(2,1)S(1)}, u32[]{:S(2)}, u32[]{:S(2)}) collective-permute-start(bf16[320,512]{1,0:T(8,128)(2,1)S(1)} %shard_map.79), channel_id=1, source_target_pairs={{0,2},{1,3},{2,0},{3,1},{4,6},{5,7},{6,4},{7,5},{8,10},{9,11},{10,... | collective-permute-start | bytes 983048 | tf_op jit(solution)/shard_map/ppermute | solution.py:21
  16.9 6.0 %collective-permute-start.7 = (bf16[128,1024]{1,0:T(8,128)(2,1)S(1)}, bf16[128,1024]{1,0:T(8,128)(2,1)S(1)}, u32[]{:S(2)}, u32[]{:S(2)}) collective-permute-start(bf16[128,1024]{1,0:T(8,128)(2,1)S(1)} %shard_map.78.after_ref.near_ref), channel_id=1, source_target_pairs={{0,8},{8,0},{16,24},{24,16},{1,9},{9,1},{17,25},{25,17},{2,10},{10... | collective-permute-start | bytes 786440 | tf_op jit(solution)/shard_map/ppermute | solution.py:21
  22.4 1.5 %collective-permute-start.6 = (bf16[128,1024]{1,0:T(8,128)(2,1)S(1)}, bf16[128,1024]{1,0:T(8,128)(2,1)S(1)}, u32[]{:S(2)}, u32[]{:S(2)}) collective-permute-start(bf16[128,1024]{1,0:T(8,128)(2,1)S(1)} %collective-permute-done.5.far_ref.refs_1_), channel_id=1, source_target_pairs={{0,8},{8,0},{16,24},{24,16},{1,9},{9,1},{17,25},{25,17},{2,10},{10... | collective-permute-start | bytes 786440 | tf_op jit(solution)/shard_map/ppermute | solution.py:21
  22.4 5.6 %collective-permute-start.11 = (bf16[112,512]{1,0:T(8,128)(2,1)S(1)}, bf16[112,512]{1,0:T(8,128)(2,1)S(1)}, u32[]{:S(2)}, u32[]{:S(2)}) collective-permute-start(bf16[112,512]{1,0:T(8,128)(2,1)S(1)} %shard_map.82), channel_id=1, source_target_pairs={{0,1},{1,0},{2,3},{3,2},{4,5},{5,4},{6,7},{7,6},{8,9},{9,8},{10,11... | collective-permute-start | bytes 344072 | tf_op jit(solution)/shard_map/ppermute | solution.py:21
  24.3 6.6 %collective-permute-start.10 = (bf16[192,256]{1,0:T(8,128)(2,1)S(1)}, bf16[192,256]{1,0:T(8,128)(2,1)S(1)}, u32[]{:S(2)}, u32[]{:S(2)}) collective-permute-start(bf16[192,256]{1,0:T(8,128)(2,1)S(1)} %shard_map.81.refs_0_), channel_id=1, source_target_pairs={{0,3},{1,2},{2,1},{3,0},{4,7},{5,6},{6,5},{7,4},{8,11},{9,10},{10,... | collective-permute-start | bytes 294920 | tf_op jit(solution)/shard_map/ppermute | solution.py:21
  25.9 6.3 %collective-permute-start.8 = (bf16[192,256]{1,0:T(8,128)(2,1)S(1)}, bf16[192,256]{1,0:T(8,128)(2,1)S(1)}, u32[]{:S(2)}, u32[]{:S(2)}) collective-permute-start(bf16[192,256]{1,0:T(8,128)(2,1)S(1)} %shard_map.81.refs_0_), channel_id=1, source_target_pairs={{0,1},{1,0},{2,3},{3,2},{4,5},{5,4},{6,7},{7,6},{8,9},{9,8},{10,11... | collective-permute-start | bytes 294920 | tf_op jit(solution)/shard_map/ppermute | solution.py:21
  26.4 5.8 %collective-permute-start.9 = (bf16[192,256]{1,0:T(8,128)(2,1)S(1)}, bf16[192,256]{1,0:T(8,128)(2,1)S(1)}, u32[]{:S(2)}, u32[]{:S(2)}) collective-permute-start(bf16[192,256]{1,0:T(8,128)(2,1)S(1)} %shard_map.81.refs_0_), channel_id=1, source_target_pairs={{0,2},{1,3},{2,0},{3,1},{4,6},{5,7},{6,4},{7,5},{8,10},{9,11},{10,... | collective-permute-start | bytes 294920 | tf_op jit(solution)/shard_map/ppermute | solution.py:21
  33.7 11.2 %all-to-all-start = ((bf16[32,16,128]{2,1,0:T(8,128)(2,1)}), bf16[32,16,128]{2,1,0:T(8,128)(2,1)S(1)}, u32[]{:S(2)}, u32[]{:S(2)}) async-start(bf16[32,16,128]{2,1,0:T(8,128)(2,1)} %bitcast.1), calls=%async_computation | async-start | bytes 262144 | tf_op jit(solution)/shard_map/all_to_all | solution.py:356
  37.2 11.1 %collective-permute-start.12 = (bf16[64,512]{1,0:T(8,128)(2,1)S(1)}, bf16[64,512]{1,0:T(8,128)(2,1)S(1)}, u32[]{:S(2)}, u32[]{:S(2)}) collective-permute-start(bf16[64,512]{1,0:T(8,128)(2,1)S(1)} %get-tuple-element.26), channel_id=1, source_target_pairs={{0,1},{1,0},{2,3},{3,2},{4,5},{5,4},{6,7},{7,6},{8,9},{9,8},{10,11... | collective-permute-start | bytes 196616 | tf_op jit(solution)/shard_map/ppermute | solution.py:21
  39.0 9.2 %collective-permute-start.13 = (bf16[64,512]{1,0:T(8,128)(2,1)S(1)}, bf16[64,512]{1,0:T(8,128)(2,1)S(1)}, u32[]{:S(2)}, u32[]{:S(2)}) collective-permute-start(bf16[64,512]{1,0:T(8,128)(2,1)S(1)} %get-tuple-element.27), channel_id=1, source_target_pairs={{0,2},{1,3},{2,0},{3,1},{4,6},{5,7},{6,4},{7,5},{8,10},{9,11},{10,... | collective-permute-start | bytes 196616 | tf_op jit(solution)/shard_map/ppermute | solution.py:21
  40.5 7.8 %collective-permute-start.14 = (bf16[64,512]{1,0:T(8,128)(2,1)S(1)}, bf16[64,512]{1,0:T(8,128)(2,1)S(1)}, u32[]{:S(2)}, u32[]{:S(2)}) collective-permute-start(bf16[64,512]{1,0:T(8,128)(2,1)S(1)} %get-tuple-element.28), channel_id=1, source_target_pairs={{0,3},{1,2},{2,1},{3,0},{4,7},{5,6},{6,5},{7,4},{8,11},{9,10},{10,... | collective-permute-start | bytes 196616 | tf_op jit(solution)/shard_map/ppermute | solution.py:21
  45.7 9.7 %all-to-all-start.1 = ((f32[32,1,128]{2,1,0:T(1,128)}), f32[32,1,128]{2,1,0:T(1,128)S(1)}, u32[]{:S(2)}, u32[]{:S(2)}) async-start(f32[32,1,128]{2,1,0:T(1,128)} %shard_map.85), calls=%async_computation.1 | async-start | bytes 32768 | tf_op jit(solution)/shard_map/all_to_all | solution.py:367

commit v22 on v21

--- a/solution.py
+++ b/solution.py
@@ -6,6 +6,7 @@
 from jax.sharding import PartitionSpec as P
 
 HOLDERS = 4
+ORDER = (0, 2, 3, 1)
 LANES = 128
 TILE = 16
 BIG = 24 * 1024 * 1024
@@ -185,7 +186,8 @@
         jnp.int32, (part, part), 1
     )
     output = None
-    for m, (hidden_ref, down) in enumerate(zip(hidden_refs, downs)):
+    for m, hidden_ref in zip(ORDER, hidden_refs):
+        down = downs[m]
         product = dot_f32(hidden_ref[...], down[:depth], (((0,), (0,)), ((), ())))
         output = product if output is None else output + product
         terms = down[depth:, :part].astype(f32)
@@ -336,7 +338,7 @@
         [ANY] + [VMEM] * 6,
         (down_z, swapped(far, "grp", 1), gate_weight, up_weight, near_hidden, gate_part, up_part),
     )
-    hiddens = [swapped(hidden, "tok", m) if m else hidden for m in range(HOLDERS)]
+    hiddens = [swapped(hidden, "tok", m) if m else hidden for m in ORDER]
     entries = tokens * tokens // LANES
     *blocks, centered = call(
         features_kernel,

time: 56.4 us -> 57.1 us (1.012)
  transfers between devices with their start and end apart: 17 -> 17, of which waited for: 9 -> 10; matrix products, arithmetic and copies ran while one was open for 0% -> 0% of each run, Pallas kernels for 5% -> 5%
where the time goes in v22:
time: 57.1 us; the launch traced here: 56.9 us
  waiting for transfers between devices  27.5 us (48%)
  starting transfers between devices  22.3 us (39%)
  Pallas kernels  6.33 us (11%)
  between operations  0.76 us (1%)
    ppermute x15, waiting for transfers between devices, swapped(): lax.ppermute(array, axis, [(i, i ^ mask) for i in range(lax.axis_size(axi...  17 us
    ppermute x15, starting transfers between devices, swapped(): lax.ppermute(array, axis, [(i, i ^ mask) for i in range(lax.axis_size(axi...  15.8 us
    all_to_all x1, waiting for transfers between devices, shards(): lax.all_to_all(tables, ('grp', 'tok'), split_axis=0, concat_axis=0, tiled...  6.33 us
    pallas_call x10, Pallas kernels, call(): pl.pallas_call(body, out_shape=outs, in_specs=in_specs, out_specs=jax.tre...  6.33 us
    all_to_all x1, waiting for transfers between devices, shards(): lax.all_to_all(centered, ('grp', 'tok'), split_axis=0, concat_axis=0, til...  4.19 us
    all_to_all x1, starting transfers between devices, shards(): lax.all_to_all(centered, ('grp', 'tok'), split_axis=0, concat_axis=0, til...  3.99 us
    all_to_all x1, starting transfers between devices, shards(): lax.all_to_all(tables, ('grp', 'tok'), split_axis=0, concat_axis=0, tiled...  2.55 us
  transfers between devices with their start and end apart: 17, of which 10 were waited for; matrix products, arithmetic and copies ran while one was open for 0% of the time, Pallas kernels for 5%

profile of v22, /device:TPU:0, one launch (start us, length us, event | category | flops | bytes accessed | tf_op | source)
XLA Modules:
  0.0 56.9 jit_solution(1146093177992191963)
XLA Ops:
  0.6 1.4 %shard_map.77 = (bf16[32,1024]{1,0:T(8,128)(2,1)S(1)}, bf16[80,1024]{1,0:T(8,128)(2,1)S(1)}, bf16[208,512]{1,0:T(8,128)(2,1)S(1)}, bf16[112,512]{1,0:T(8,128)(2,...) custom-call(bf16[32,2048]{1,0:T(8,128)(2,1)} %states_hbm.1, f32[1,2048]{1,0:T(1,128)} %bitcast.4, ...), custom_call_target="tpu_custom_call" | custom-call | tf_op jit(solution)/shard_map/pallas_call | solution.py:30
  2.0 3.0 %collective-permute-start = (bf16[304,512]{1,0:T(8,128)(2,1)S(1)}, bf16[304,512]{1,0:T(8,128)(2,1)S(1)}, u32[]{:S(2)}, u32[]{:S(2)}) collective-permute-start(bf16[304,512]{1,0:T(8,128)(2,1)S(1)} %get-tuple-element.16), channel_id=1, source_target_pairs={{0,1},{1,0},{2,3},{3,2},{4,5},{5,4},{6,7},{7,6},{8,9},{9,8},{10,11... | collective-permute-start | bytes 933896 | tf_op jit(solution)/shard_map/ppermute | solution.py:22
  5.0 1.6 %collective-permute-start.3 = (bf16[80,1024]{1,0:T(8,128)(2,1)S(1)}, bf16[80,1024]{1,0:T(8,128)(2,1)S(1)}, u32[]{:S(2)}, u32[]{:S(2)}) collective-permute-start(bf16[80,1024]{1,0:T(8,128)(2,1)S(1)} %get-tuple-element.18), channel_id=1, source_target_pairs={{0,2},{1,3},{2,0},{3,1},{4,6},{5,7},{6,4},{7,5},{8,10},{9,11},{10,... | collective-permute-start | bytes 491528 | tf_op jit(solution)/shard_map/ppermute | solution.py:22
  6.6 2.5 %collective-permute-start.1 = (bf16[32,1024]{1,0:T(8,128)(2,1)S(1)}, bf16[32,1024]{1,0:T(8,128)(2,1)S(1)}, u32[]{:S(2)}, u32[]{:S(2)}) collective-permute-start(bf16[32,1024]{1,0:T(8,128)(2,1)S(1)} %get-tuple-element.17.refs_3_), channel_id=1, source_target_pairs={{0,6},{1,7},{2,4},{3,5},{4,2},{5,3},{6,0},{7,1},{8,14},{9,15},{10,... | collective-permute-start | bytes 196616 | tf_op jit(solution)/shard_map/ppermute | solution.py:22
  9.1 0.1 collective-permute-start.2
  9.2 5.7 %collective-permute-done.1.refs_0_ = bf16[32,1024]{1,0:T(8,128)(2,1)S(1)} collective-permute-done((bf16[32,1024]{1,0:T(8,128)(2,1)S(1)}, bf16[32,1024]{1,0:T(8,128)(2,1)S(1)}, u32[]{:S(2)}, u32[]{:S(2)}) %collective-permute-start.1) | collective-permute-done | bytes 65568 | tf_op jit(solution)/shard_map/ppermute | solution.py:22
  14.9 1.0 %collective-permute-done.2.refs_1_ = bf16[32,1024]{1,0:T(8,128)(2,1)S(1)} collective-permute-done((bf16[32,1024]{1,0:T(8,128)(2,1)S(1)}, bf16[32,1024]{1,0:T(8,128)(2,1)S(1)}, u32[]{:S(2)}, u32[]{:S(2)}) %collective-permute-start.2) | collective-permute-done | bytes 65568 | tf_op jit(solution)/shard_map/ppermute | solution.py:22
  15.9 0.0 collective-permute-done.3.refs_2_.refs_5_
  15.9 0.0 collective-permute-done.after_ref.second_ref.refs_7_
  15.9 0.0 copy-start.1
  15.9 0.0 copy-start
  15.9 0.6 %collective-permute-start.5 = (bf16[128,1024]{1,0:T(8,128)(2,1)S(1)}, bf16[128,1024]{1,0:T(8,128)(2,1)S(1)}, u32[]{:S(2)}, u32[]{:S(2)}) collective-permute-start(bf16[128,1024]{1,0:T(8,128)(2,1)S(1)} %shard_map.78.after_ref.near_ref), channel_id=1, source_target_pairs={{0,1},{1,0},{2,3},{3,2},{4,5},{5,4},{6,7},{7,6},{8,9},{9,8},{10,11... | collective-permute-start | bytes 786440 | tf_op jit(solution)/shard_map/ppermute | solution.py:22
  16.6 0.3 collective-permute-start.4
  16.9 0.0 collective-permute-start.7
  16.9 5.5 %collective-permute-done.5.far_ref.refs_1_ = bf16[128,1024]{1,0:T(8,128)(2,1)S(1)} collective-permute-done((bf16[128,1024]{1,0:T(8,128)(2,1)S(1)}, bf16[128,1024]{1,0:T(8,128)(2,1)S(1)}, u32[]{:S(2)}, u32[]{:S(2)}) %collective-permute-start.5) | collective-permute-done | bytes 262176 | tf_op jit(solution)/shard_map/ppermute | solution.py:22
  22.4 0.0 collective-permute-start.6
  22.4 0.5 collective-permute-start.11
  22.9 0.0 collective-permute-done.7.near2_ref
  22.9 0.0 copy-done.1
  22.9 0.0 copy-done
  22.9 0.8 %shard_map.80 = (bf16[192,128]{1,0:T(8,128)(2,1)S(1)}, f32[192,128]{1,0:T(8,128)S(1)}, f32[192,128]{1,0:T(8,128)S(1)}) custom-call(bf16[128,1024]{1,0:T(8,128)(2,1)S(1)} %shard_map.78.after_ref.near_ref, bf16[128,1024]{1,0:T(8,128)(2,1)S(1)} %collective-permute-done.7.near2_ref, bf16[128,1024]{1,0:T(8,128)(2,1)S(1)} %collective-permute-done.5.far_ref.refs_1_, ...), custom_call_target="tpu_custom_call" | custom-call | tf_op jit(solution)/shard_map/pallas_call | solution.py:30
  23.7 0.0 collective-permute-done.4.after_ref.refs_6_
  23.7 0.2 collective-permute-done.6.far2_ref
  23.9 0.4 shard_map.81.refs_0_
  24.3 1.4 %collective-permute-start.10 = (bf16[192,256]{1,0:T(8,128)(2,1)S(1)}, bf16[192,256]{1,0:T(8,128)(2,1)S(1)}, u32[]{:S(2)}, u32[]{:S(2)}) collective-permute-start(bf16[192,256]{1,0:T(8,128)(2,1)S(1)} %shard_map.81.refs_0_), channel_id=1, source_target_pairs={{0,1},{1,0},{2,3},{3,2},{4,5},{5,4},{6,7},{7,6},{8,9},{9,8},{10,11... | collective-permute-start | bytes 294920 | tf_op jit(solution)/shard_map/ppermute | solution.py:22
  25.7 0.8 %collective-permute-start.8 = (bf16[192,256]{1,0:T(8,128)(2,1)S(1)}, bf16[192,256]{1,0:T(8,128)(2,1)S(1)}, u32[]{:S(2)}, u32[]{:S(2)}) collective-permute-start(bf16[192,256]{1,0:T(8,128)(2,1)S(1)} %shard_map.81.refs_0_), channel_id=1, source_target_pairs={{0,2},{1,3},{2,0},{3,1},{4,6},{5,7},{6,4},{7,5},{8,10},{9,11},{10,... | collective-permute-start | bytes 294920 | tf_op jit(solution)/shard_map/ppermute | solution.py:22
  26.4 1.4 %collective-permute-start.9 = (bf16[192,256]{1,0:T(8,128)(2,1)S(1)}, bf16[192,256]{1,0:T(8,128)(2,1)S(1)}, u32[]{:S(2)}, u32[]{:S(2)}) collective-permute-start(bf16[192,256]{1,0:T(8,128)(2,1)S(1)} %shard_map.81.refs_0_), channel_id=1, source_target_pairs={{0,3},{1,2},{2,1},{3,0},{4,7},{5,6},{6,5},{7,4},{8,11},{9,10},{10,... | collective-permute-start | bytes 294920 | tf_op jit(solution)/shard_map/ppermute | solution.py:22
  27.9 0.5 collective-permute-done.11.refs_8_
  28.3 2.5 %collective-permute-done.10.refs_3_ = bf16[192,256]{1,0:T(8,128)(2,1)S(1)} collective-permute-done((bf16[192,256]{1,0:T(8,128)(2,1)S(1)}, bf16[192,256]{1,0:T(8,128)(2,1)S(1)}, u32[]{:S(2)}, u32[]{:S(2)}) %collective-permute-start.10) | collective-permute-done | bytes 98336 | tf_op jit(solution)/shard_map/ppermute | solution.py:22
  30.9 0.5 collective-permute-done.8.refs_1_
  31.3 1.2 %collective-permute-done.9.refs_2_ = bf16[192,256]{1,0:T(8,128)(2,1)S(1)} collective-permute-done((bf16[192,256]{1,0:T(8,128)(2,1)S(1)}, bf16[192,256]{1,0:T(8,128)(2,1)S(1)}, u32[]{:S(2)}, u32[]{:S(2)}) %collective-permute-start.9) | collective-permute-done | bytes 98336 | tf_op jit(solution)/shard_map/ppermute | solution.py:22
  32.5 1.5 %shard_map.83 = (bf16[64,512]{1,0:T(8,128)(2,1)S(1)}, bf16[64,512]{1,0:T(8,128)(2,1)S(1)}, bf16[64,512]{1,0:T(8,128)(2,1)S(1)}, bf16[64,512]{1,0:T(8,128)(2,1)S(1)}, bf16[512,128]{1,0:T(8,128)(2,1)}) custom-call(bf16[192,256]{1,0:T(8,128)(2,1)S(1)} %shard_map.81.refs_0_, bf16[192,256]{1,0:T(8,128)(2,1)S(1)} %collective-permute-done.8.refs_1_, ...), custom_call_target="tpu_custom_call" | custom-call | tf_op jit(solution)/shard_map/pallas_call | solution.py:30
  34.0 4.0 %all-to-all-start = ((bf16[32,16,128]{2,1,0:T(8,128)(2,1)}), bf16[32,16,128]{2,1,0:T(8,128)(2,1)S(1)}, u32[]{:S(2)}, u32[]{:S(2)}) async-start(bf16[32,16,128]{2,1,0:T(8,128)(2,1)} %bitcast.1), calls=%async_computation | async-start | bytes 262144 | tf_op jit(solution)/shard_map/all_to_all | solution.py:358
  37.9 1.8 %collective-permute-start.12 = (bf16[64,512]{1,0:T(8,128)(2,1)S(1)}, bf16[64,512]{1,0:T(8,128)(2,1)S(1)}, u32[]{:S(2)}, u32[]{:S(2)}) collective-permute-start(bf16[64,512]{1,0:T(8,128)(2,1)S(1)} %get-tuple-element.26), channel_id=1, source_target_pairs={{0,1},{1,0},{2,3},{3,2},{4,5},{5,4},{6,7},{7,6},{8,9},{9,8},{10,11... | collective-permute-start | bytes 196616 | tf_op jit(solution)/shard_map/ppermute | solution.py:22
  39.8 1.5 %collective-permute-start.13 = (bf16[64,512]{1,0:T(8,128)(2,1)S(1)}, bf16[64,512]{1,0:T(8,128)(2,1)S(1)}, u32[]{:S(2)}, u32[]{:S(2)}) collective-permute-start(bf16[64,512]{1,0:T(8,128)(2,1)S(1)} %get-tuple-element.27), channel_id=1, source_target_pairs={{0,2},{1,3},{2,0},{3,1},{4,6},{5,7},{6,4},{7,5},{8,10},{9,11},{10,... | collective-permute-start | bytes 196616 | tf_op jit(solution)/shard_map/ppermute | solution.py:22
  41.2 0.3 collective-permute-start.14
  41.5 4.2 %all-to-all-done = bf16[32,16,128]{2,1,0:T(8,128)(2,1)S(1)} async-done(((bf16[32,16,128]{2,1,0:T(8,128)(2,1)}), bf16[32,16,128]{2,1,0:T(8,128)(2,1)S(1)}, u32[]{:S(2)}, u32[]{:S(2)}) %all-to-all-start) | async-done | bytes 131104 | tf_op jit(solution)/shard_map/all_to_all | solution.py:358
  45.7 0.8 %shard_map.85 = f32[32,1,128]{2,1,0:T(1,128)} custom-call(bf16[8,4,16,128]{3,2,1,0:T(8,128)(2,1)S(1)} %bitcast.3), custom_call_target="tpu_custom_call" | custom-call | tf_op jit(solution)/shard_map/pallas_call | solution.py:30
  46.5 2.6 %all-to-all-start.1 = ((f32[32,1,128]{2,1,0:T(1,128)}), f32[32,1,128]{2,1,0:T(1,128)S(1)}, u32[]{:S(2)}, u32[]{:S(2)}) async-start(f32[32,1,128]{2,1,0:T(1,128)} %shard_map.85), calls=%async_computation.1 | async-start | bytes 32768 | tf_op jit(solution)/shard_map/all_to_all | solution.py:369
  49.0 0.0 collective-permute-done.12.refs_1_
  49.0 0.0 collective-permute-done.13.refs_2_
  49.0 0.0 collective-permute-done.14.refs_3_
  49.0 0.7 %shard_map.84 = bf16[64,2048]{1,0:T(8,128)(2,1)} custom-call(bf16[64,512]{1,0:T(8,128)(2,1)S(1)} %get-tuple-element.25.refs_0_, bf16[64,512]{1,0:T(8,128)(2,1)S(1)} %collective-permute-done.12.refs_1_, bf16[64,512]{1,0:T(8,128)(2,1)S(1)} %collective-permute-done.13.refs_2_, bf16[64,512]{1,0:T(8,128)(2,1)S(1)} %collective-permute-done.14.refs_3_), custom_call_target="tpu_custom_call" | custom-call | tf_op jit(solution)/shard_map/pallas_call | solution.py:30
  49.8 6.3 %all-to-all-done.1.tables_ref = f32[32,1,128]{2,1,0:T(1,128)S(1)} async-done(((f32[32,1,128]{2,1,0:T(1,128)}), f32[32,1,128]{2,1,0:T(1,128)S(1)}, u32[]{:S(2)}, u32[]{:S(2)}) %all-to-all-start.1) | async-done | bytes 16416 | tf_op jit(solution)/shard_map/all_to_all | solution.py:369
  56.1 0.8 %shard_map.86 = f32[8,8]{1,0:T(8,128)} custom-call(f32[32,1,128]{2,1,0:T(1,128)S(1)} %all-to-all-done.1.tables_ref), custom_call_target="tpu_custom_call" | custom-call | tf_op jit(solution)/shard_map/pallas_call | solution.py:30
  (3 shorter events, 0.1 us)
Async XLA Ops:
  2.0 13.9 %collective-permute-start = (bf16[304,512]{1,0:T(8,128)(2,1)S(1)}, bf16[304,512]{1,0:T(8,128)(2,1)S(1)}, u32[]{:S(2)}, u32[]{:S(2)}) collective-permute-start(bf16[304,512]{1,0:T(8,128)(2,1)S(1)} %get-tuple-element.16), channel_id=1, source_target_pairs={{0,1},{1,0},{2,3},{3,2},{4,5},{5,4},{6,7},{7,6},{8,9},{9,8},{10,11... | collective-permute-start | bytes 933896 | tf_op jit(solution)/shard_map/ppermute | solution.py:22
  5.0 10.9 %collective-permute-start.3 = (bf16[80,1024]{1,0:T(8,128)(2,1)S(1)}, bf16[80,1024]{1,0:T(8,128)(2,1)S(1)}, u32[]{:S(2)}, u32[]{:S(2)}) collective-permute-start(bf16[80,1024]{1,0:T(8,128)(2,1)S(1)} %get-tuple-element.18), channel_id=1, source_target_pairs={{0,2},{1,3},{2,0},{3,1},{4,6},{5,7},{6,4},{7,5},{8,10},{9,11},{10,... | collective-permute-start | bytes 491528 | tf_op jit(solution)/shard_map/ppermute | solution.py:22
  6.6 8.3 %collective-permute-start.1 = (bf16[32,1024]{1,0:T(8,128)(2,1)S(1)}, bf16[32,1024]{1,0:T(8,128)(2,1)S(1)}, u32[]{:S(2)}, u32[]{:S(2)}) collective-permute-start(bf16[32,1024]{1,0:T(8,128)(2,1)S(1)} %get-tuple-element.17.refs_3_), channel_id=1, source_target_pairs={{0,6},{1,7},{2,4},{3,5},{4,2},{5,3},{6,0},{7,1},{8,14},{9,15},{10,... | collective-permute-start | bytes 196616 | tf_op jit(solution)/shard_map/ppermute | solution.py:22
  9.1 6.8 %collective-permute-start.2 = (bf16[32,1024]{1,0:T(8,128)(2,1)S(1)}, bf16[32,1024]{1,0:T(8,128)(2,1)S(1)}, u32[]{:S(2)}, u32[]{:S(2)}) collective-permute-start(bf16[32,1024]{1,0:T(8,128)(2,1)S(1)} %get-tuple-element.17.refs_3_), channel_id=1, source_target_pairs={{0,4},{1,5},{2,6},{3,7},{4,0},{5,1},{6,2},{7,3},{8,12},{9,13},{10,... | collective-permute-start | bytes 196616 | tf_op jit(solution)/shard_map/ppermute | solution.py:22
  15.9 7.0 %copy-start.1 = (bf16[192,2048]{1,0:T(8,128)(2,1)S(1)}, bf16[192,2048]{1,0:T(8,128)(2,1)}, u32[]{:S(2)}) copy-start(bf16[192,2048]{1,0:T(8,128)(2,1)} %up_ref.3) | copy-start | bytes 2359300
  15.9 7.0 %copy-start = (bf16[192,2048]{1,0:T(8,128)(2,1)S(1)}, bf16[192,2048]{1,0:T(8,128)(2,1)}, u32[]{:S(2)}) copy-start(bf16[192,2048]{1,0:T(8,128)(2,1)} %gate_ref.3) | copy-start | bytes 2359300
  15.9 6.4 %collective-permute-start.5 = (bf16[128,1024]{1,0:T(8,128)(2,1)S(1)}, bf16[128,1024]{1,0:T(8,128)(2,1)S(1)}, u32[]{:S(2)}, u32[]{:S(2)}) collective-permute-start(bf16[128,1024]{1,0:T(8,128)(2,1)S(1)} %shard_map.78.after_ref.near_ref), channel_id=1, source_target_pairs={{0,1},{1,0},{2,3},{3,2},{4,5},{5,4},{6,7},{7,6},{8,9},{9,8},{10,11... | collective-permute-start | bytes 786440 | tf_op jit(solution)/shard_map/ppermute | solution.py:22
  16.6 7.1 %collective-permute-start.4 = (bf16[320,512]{1,0:T(8,128)(2,1)S(1)}, bf16[320,512]{1,0:T(8,128)(2,1)S(1)}, u32[]{:S(2)}, u32[]{:S(2)}) collective-permute-start(bf16[320,512]{1,0:T(8,128)(2,1)S(1)} %shard_map.79), channel_id=1, source_target_pairs={{0,2},{1,3},{2,0},{3,1},{4,6},{5,7},{6,4},{7,5},{8,10},{9,11},{10,... | collective-permute-start | bytes 983048 | tf_op jit(solution)/shard_map/ppermute | solution.py:22
  16.9 6.0 %collective-permute-start.7 = (bf16[128,1024]{1,0:T(8,128)(2,1)S(1)}, bf16[128,1024]{1,0:T(8,128)(2,1)S(1)}, u32[]{:S(2)}, u32[]{:S(2)}) collective-permute-start(bf16[128,1024]{1,0:T(8,128)(2,1)S(1)} %shard_map.78.after_ref.near_ref), channel_id=1, source_target_pairs={{0,8},{8,0},{16,24},{24,16},{1,9},{9,1},{17,25},{25,17},{2,10},{10... | collective-permute-start | bytes 786440 | tf_op jit(solution)/shard_map/ppermute | solution.py:22
  22.4 1.5 %collective-permute-start.6 = (bf16[128,1024]{1,0:T(8,128)(2,1)S(1)}, bf16[128,1024]{1,0:T(8,128)(2,1)S(1)}, u32[]{:S(2)}, u32[]{:S(2)}) collective-permute-start(bf16[128,1024]{1,0:T(8,128)(2,1)S(1)} %collective-permute-done.5.far_ref.refs_1_), channel_id=1, source_target_pairs={{0,8},{8,0},{16,24},{24,16},{1,9},{9,1},{17,25},{25,17},{2,10},{10... | collective-permute-start | bytes 786440 | tf_op jit(solution)/shard_map/ppermute | solution.py:22
  22.4 5.9 %collective-permute-start.11 = (bf16[112,512]{1,0:T(8,128)(2,1)S(1)}, bf16[112,512]{1,0:T(8,128)(2,1)S(1)}, u32[]{:S(2)}, u32[]{:S(2)}) collective-permute-start(bf16[112,512]{1,0:T(8,128)(2,1)S(1)} %shard_map.82), channel_id=1, source_target_pairs={{0,1},{1,0},{2,3},{3,2},{4,5},{5,4},{6,7},{7,6},{8,9},{9,8},{10,11... | collective-permute-start | bytes 344072 | tf_op jit(solution)/shard_map/ppermute | solution.py:22
  24.3 6.6 %collective-permute-start.10 = (bf16[192,256]{1,0:T(8,128)(2,1)S(1)}, bf16[192,256]{1,0:T(8,128)(2,1)S(1)}, u32[]{:S(2)}, u32[]{:S(2)}) collective-permute-start(bf16[192,256]{1,0:T(8,128)(2,1)S(1)} %shard_map.81.refs_0_), channel_id=1, source_target_pairs={{0,1},{1,0},{2,3},{3,2},{4,5},{5,4},{6,7},{7,6},{8,9},{9,8},{10,11... | collective-permute-start | bytes 294920 | tf_op jit(solution)/shard_map/ppermute | solution.py:22
  25.7 5.7 %collective-permute-start.8 = (bf16[192,256]{1,0:T(8,128)(2,1)S(1)}, bf16[192,256]{1,0:T(8,128)(2,1)S(1)}, u32[]{:S(2)}, u32[]{:S(2)}) collective-permute-start(bf16[192,256]{1,0:T(8,128)(2,1)S(1)} %shard_map.81.refs_0_), channel_id=1, source_target_pairs={{0,2},{1,3},{2,0},{3,1},{4,6},{5,7},{6,4},{7,5},{8,10},{9,11},{10,... | collective-permute-start | bytes 294920 | tf_op jit(solution)/shard_map/ppermute | solution.py:22
  26.4 6.0 %collective-permute-start.9 = (bf16[192,256]{1,0:T(8,128)(2,1)S(1)}, bf16[192,256]{1,0:T(8,128)(2,1)S(1)}, u32[]{:S(2)}, u32[]{:S(2)}) collective-permute-start(bf16[192,256]{1,0:T(8,128)(2,1)S(1)} %shard_map.81.refs_0_), channel_id=1, source_target_pairs={{0,3},{1,2},{2,1},{3,0},{4,7},{5,6},{6,5},{7,4},{8,11},{9,10},{10,... | collective-permute-start | bytes 294920 | tf_op jit(solution)/shard_map/ppermute | solution.py:22
  34.0 11.7 %all-to-all-start = ((bf16[32,16,128]{2,1,0:T(8,128)(2,1)}), bf16[32,16,128]{2,1,0:T(8,128)(2,1)S(1)}, u32[]{:S(2)}, u32[]{:S(2)}) async-start(bf16[32,16,128]{2,1,0:T(8,128)(2,1)} %bitcast.1), calls=%async_computation | async-start | bytes 262144 | tf_op jit(solution)/shard_map/all_to_all | solution.py:358
  37.9 11.1 %collective-permute-start.12 = (bf16[64,512]{1,0:T(8,128)(2,1)S(1)}, bf16[64,512]{1,0:T(8,128)(2,1)S(1)}, u32[]{:S(2)}, u32[]{:S(2)}) collective-permute-start(bf16[64,512]{1,0:T(8,128)(2,1)S(1)} %get-tuple-element.26), channel_id=1, source_target_pairs={{0,1},{1,0},{2,3},{3,2},{4,5},{5,4},{6,7},{7,6},{8,9},{9,8},{10,11... | collective-permute-start | bytes 196616 | tf_op jit(solution)/shard_map/ppermute | solution.py:22
  39.8 9.2 %collective-permute-start.13 = (bf16[64,512]{1,0:T(8,128)(2,1)S(1)}, bf16[64,512]{1,0:T(8,128)(2,1)S(1)}, u32[]{:S(2)}, u32[]{:S(2)}) collective-permute-start(bf16[64,512]{1,0:T(8,128)(2,1)S(1)} %get-tuple-element.27), channel_id=1, source_target_pairs={{0,2},{1,3},{2,0},{3,1},{4,6},{5,7},{6,4},{7,5},{8,10},{9,11},{10,... | collective-permute-start | bytes 196616 | tf_op jit(solution)/shard_map/ppermute | solution.py:22
  41.2 7.8 %collective-permute-start.14 = (bf16[64,512]{1,0:T(8,128)(2,1)S(1)}, bf16[64,512]{1,0:T(8,128)(2,1)S(1)}, u32[]{:S(2)}, u32[]{:S(2)}) collective-permute-start(bf16[64,512]{1,0:T(8,128)(2,1)S(1)} %get-tuple-element.28), channel_id=1, source_target_pairs={{0,3},{1,2},{2,1},{3,0},{4,7},{5,6},{6,5},{7,4},{8,11},{9,10},{10,... | collective-permute-start | bytes 196616 | tf_op jit(solution)/shard_map/ppermute | solution.py:22
  46.5 9.7 %all-to-all-start.1 = ((f32[32,1,128]{2,1,0:T(1,128)}), f32[32,1,128]{2,1,0:T(1,128)S(1)}, u32[]{:S(2)}, u32[]{:S(2)}) async-start(f32[32,1,128]{2,1,0:T(1,128)} %shard_map.85), calls=%async_computation.1 | async-start | bytes 32768 | tf_op jit(solution)/shard_map/all_to_all | solution.py:369

commit v23 on v22

--- a/solution.py
+++ b/solution.py
@@ -6,7 +6,7 @@
 from jax.sharding import PartitionSpec as P
 
 HOLDERS = 4
-ORDER = (0, 2, 3, 1)
+ORDER = (0, 2, 1, 3)
 LANES = 128
 TILE = 16
 BIG = 24 * 1024 * 1024

time: 57.1 us -> 56.9 us (level)
  no operation moved by 1% of the time
where the time goes in v23:
time: 56.9 us; the launch traced here: 56.6 us
  waiting for transfers between devices  27.3 us (48%)
  starting transfers between devices  22.2 us (39%)
  Pallas kernels  6.33 us (11%)
  between operations  0.76 us (1%)
    ppermute x15, waiting for transfers between devices, swapped(): lax.ppermute(array, axis, [(i, i ^ mask) for i in range(lax.axis_size(axi...  16.8 us
    ppermute x15, starting transfers between devices, swapped(): lax.ppermute(array, axis, [(i, i ^ mask) for i in range(lax.axis_size(axi...  15.8 us
    all_to_all x1, waiting for transfers between devices, shards(): lax.all_to_all(tables, ('grp', 'tok'), split_axis=0, concat_axis=0, tiled...  6.33 us
    pallas_call x10, Pallas kernels, call(): pl.pallas_call(body, out_shape=outs, in_specs=in_specs, out_specs=jax.tre...  6.33 us
    all_to_all x1, waiting for transfers between devices, shards(): lax.all_to_all(centered, ('grp', 'tok'), split_axis=0, concat_axis=0, til...  4.19 us
    all_to_all x1, starting transfers between devices, shards(): lax.all_to_all(centered, ('grp', 'tok'), split_axis=0, concat_axis=0, til...  3.93 us
    all_to_all x1, starting transfers between devices, shards(): lax.all_to_all(tables, ('grp', 'tok'), split_axis=0, concat_axis=0, tiled...  2.55 us
  transfers between devices with their start and end apart: 17, of which 10 were waited for; matrix products, arithmetic and copies ran while one was open for 0% of the time, Pallas kernels for 5%

profile of v23, /device:TPU:0, one launch (start us, length us, event | category | flops | bytes accessed | tf_op | source)
XLA Modules:
  0.0 56.6 jit_solution(16374181294958542842)
XLA Ops:
  0.6 1.4 %shard_map.77 = (bf16[32,1024]{1,0:T(8,128)(2,1)S(1)}, bf16[80,1024]{1,0:T(8,128)(2,1)S(1)}, bf16[208,512]{1,0:T(8,128)(2,1)S(1)}, bf16[112,512]{1,0:T(8,128)(2,...) custom-call(bf16[32,2048]{1,0:T(8,128)(2,1)} %states_hbm.1, f32[1,2048]{1,0:T(1,128)} %bitcast.4, ...), custom_call_target="tpu_custom_call" | custom-call | tf_op jit(solution)/shard_map/pallas_call | solution.py:30
  2.0 3.0 %collective-permute-start = (bf16[304,512]{1,0:T(8,128)(2,1)S(1)}, bf16[304,512]{1,0:T(8,128)(2,1)S(1)}, u32[]{:S(2)}, u32[]{:S(2)}) collective-permute-start(bf16[304,512]{1,0:T(8,128)(2,1)S(1)} %get-tuple-element.16), channel_id=1, source_target_pairs={{0,1},{1,0},{2,3},{3,2},{4,5},{5,4},{6,7},{7,6},{8,9},{9,8},{10,11... | collective-permute-start | bytes 933896 | tf_op jit(solution)/shard_map/ppermute | solution.py:22
  5.0 1.6 %collective-permute-start.3 = (bf16[80,1024]{1,0:T(8,128)(2,1)S(1)}, bf16[80,1024]{1,0:T(8,128)(2,1)S(1)}, u32[]{:S(2)}, u32[]{:S(2)}) collective-permute-start(bf16[80,1024]{1,0:T(8,128)(2,1)S(1)} %get-tuple-element.18), channel_id=1, source_target_pairs={{0,2},{1,3},{2,0},{3,1},{4,6},{5,7},{6,4},{7,5},{8,10},{9,11},{10,... | collective-permute-start | bytes 491528 | tf_op jit(solution)/shard_map/ppermute | solution.py:22
  6.6 2.5 %collective-permute-start.1 = (bf16[32,1024]{1,0:T(8,128)(2,1)S(1)}, bf16[32,1024]{1,0:T(8,128)(2,1)S(1)}, u32[]{:S(2)}, u32[]{:S(2)}) collective-permute-start(bf16[32,1024]{1,0:T(8,128)(2,1)S(1)} %get-tuple-element.17.refs_3_), channel_id=1, source_target_pairs={{0,6},{1,7},{2,4},{3,5},{4,2},{5,3},{6,0},{7,1},{8,14},{9,15},{10,... | collective-permute-start | bytes 196616 | tf_op jit(solution)/shard_map/ppermute | solution.py:22
  9.1 0.1 collective-permute-start.2
  9.2 5.7 %collective-permute-done.1.refs_0_ = bf16[32,1024]{1,0:T(8,128)(2,1)S(1)} collective-permute-done((bf16[32,1024]{1,0:T(8,128)(2,1)S(1)}, bf16[32,1024]{1,0:T(8,128)(2,1)S(1)}, u32[]{:S(2)}, u32[]{:S(2)}) %collective-permute-start.1) | collective-permute-done | bytes 65568 | tf_op jit(solution)/shard_map/ppermute | solution.py:22
  14.9 1.0 %collective-permute-done.2.refs_1_ = bf16[32,1024]{1,0:T(8,128)(2,1)S(1)} collective-permute-done((bf16[32,1024]{1,0:T(8,128)(2,1)S(1)}, bf16[32,1024]{1,0:T(8,128)(2,1)S(1)}, u32[]{:S(2)}, u32[]{:S(2)}) %collective-permute-start.2) | collective-permute-done | bytes 65568 | tf_op jit(solution)/shard_map/ppermute | solution.py:22
  15.9 0.0 collective-permute-done.3.refs_2_.refs_5_
  15.9 0.0 collective-permute-done.after_ref.second_ref.refs_7_
  15.9 0.0 copy-start.1
  15.9 0.0 copy-start
  15.9 0.6 %collective-permute-start.5 = (bf16[128,1024]{1,0:T(8,128)(2,1)S(1)}, bf16[128,1024]{1,0:T(8,128)(2,1)S(1)}, u32[]{:S(2)}, u32[]{:S(2)}) collective-permute-start(bf16[128,1024]{1,0:T(8,128)(2,1)S(1)} %shard_map.78.after_ref.near_ref), channel_id=1, source_target_pairs={{0,1},{1,0},{2,3},{3,2},{4,5},{5,4},{6,7},{7,6},{8,9},{9,8},{10,11... | collective-permute-start | bytes 786440 | tf_op jit(solution)/shard_map/ppermute | solution.py:22
  16.6 0.3 collective-permute-start.4
  16.9 0.0 collective-permute-start.7
  16.9 5.5 %collective-permute-done.5.far_ref.refs_1_ = bf16[128,1024]{1,0:T(8,128)(2,1)S(1)} collective-permute-done((bf16[128,1024]{1,0:T(8,128)(2,1)S(1)}, bf16[128,1024]{1,0:T(8,128)(2,1)S(1)}, u32[]{:S(2)}, u32[]{:S(2)}) %collective-permute-start.5) | collective-permute-done | bytes 262176 | tf_op jit(solution)/shard_map/ppermute | solution.py:22
  22.4 0.0 collective-permute-start.6
  22.4 0.5 collective-permute-start.11
  22.9 0.0 collective-permute-done.7.near2_ref
  22.9 0.0 copy-done.1
  22.9 0.0 copy-done
  22.9 0.8 %shard_map.80 = (bf16[192,128]{1,0:T(8,128)(2,1)S(1)}, f32[192,128]{1,0:T(8,128)S(1)}, f32[192,128]{1,0:T(8,128)S(1)}) custom-call(bf16[128,1024]{1,0:T(8,128)(2,1)S(1)} %shard_map.78.after_ref.near_ref, bf16[128,1024]{1,0:T(8,128)(2,1)S(1)} %collective-permute-done.7.near2_ref, bf16[128,1024]{1,0:T(8,128)(2,1)S(1)} %collective-permute-done.5.far_ref.refs_1_, ...), custom_call_target="tpu_custom_call" | custom-call | tf_op jit(solution)/shard_map/pallas_call | solution.py:30
  23.7 0.0 collective-permute-done.4.after_ref.refs_6_
  23.7 0.2 collective-permute-done.6.far2_ref
  23.9 0.4 shard_map.81.refs_0_
  24.3 1.6 %collective-permute-start.10 = (bf16[192,256]{1,0:T(8,128)(2,1)S(1)}, bf16[192,256]{1,0:T(8,128)(2,1)S(1)}, u32[]{:S(2)}, u32[]{:S(2)}) collective-permute-start(bf16[192,256]{1,0:T(8,128)(2,1)S(1)} %shard_map.81.refs_0_), channel_id=1, source_target_pairs={{0,3},{1,2},{2,1},{3,0},{4,7},{5,6},{6,5},{7,4},{8,11},{9,10},{10,... | collective-permute-start | bytes 294920 | tf_op jit(solution)/shard_map/ppermute | solution.py:22
  25.9 1.2 %collective-permute-start.8 = (bf16[192,256]{1,0:T(8,128)(2,1)S(1)}, bf16[192,256]{1,0:T(8,128)(2,1)S(1)}, u32[]{:S(2)}, u32[]{:S(2)}) collective-permute-start(bf16[192,256]{1,0:T(8,128)(2,1)S(1)} %shard_map.81.refs_0_), channel_id=1, source_target_pairs={{0,2},{1,3},{2,0},{3,1},{4,6},{5,7},{6,4},{7,5},{8,10},{9,11},{10,... | collective-permute-start | bytes 294920 | tf_op jit(solution)/shard_map/ppermute | solution.py:22
  27.1 0.7 %collective-permute-start.9 = (bf16[192,256]{1,0:T(8,128)(2,1)S(1)}, bf16[192,256]{1,0:T(8,128)(2,1)S(1)}, u32[]{:S(2)}, u32[]{:S(2)}) collective-permute-start(bf16[192,256]{1,0:T(8,128)(2,1)S(1)} %shard_map.81.refs_0_), channel_id=1, source_target_pairs={{0,1},{1,0},{2,3},{3,2},{4,5},{5,4},{6,7},{7,6},{8,9},{9,8},{10,11... | collective-permute-start | bytes 294920 | tf_op jit(solution)/shard_map/ppermute | solution.py:22
  27.9 0.1 collective-permute-done.11.refs_8_
  28.0 3.0 %collective-permute-done.10.refs_3_ = bf16[192,256]{1,0:T(8,128)(2,1)S(1)} collective-permute-done((bf16[192,256]{1,0:T(8,128)(2,1)S(1)}, bf16[192,256]{1,0:T(8,128)(2,1)S(1)}, u32[]{:S(2)}, u32[]{:S(2)}) %collective-permute-start.10) | collective-permute-done | bytes 98336 | tf_op jit(solution)/shard_map/ppermute | solution.py:22
  30.9 1.2 %collective-permute-done.8.refs_1_ = bf16[192,256]{1,0:T(8,128)(2,1)S(1)} collective-permute-done((bf16[192,256]{1,0:T(8,128)(2,1)S(1)}, bf16[192,256]{1,0:T(8,128)(2,1)S(1)}, u32[]{:S(2)}, u32[]{:S(2)}) %collective-permute-start.8) | collective-permute-done | bytes 98336 | tf_op jit(solution)/shard_map/ppermute | solution.py:22
  32.1 0.1 collective-permute-done.9.refs_2_
  32.3 1.5 %shard_map.83 = (bf16[64,512]{1,0:T(8,128)(2,1)S(1)}, bf16[64,512]{1,0:T(8,128)(2,1)S(1)}, bf16[64,512]{1,0:T(8,128)(2,1)S(1)}, bf16[64,512]{1,0:T(8,128)(2,1)S(1)}, bf16[512,128]{1,0:T(8,128)(2,1)}) custom-call(bf16[192,256]{1,0:T(8,128)(2,1)S(1)} %shard_map.81.refs_0_, bf16[192,256]{1,0:T(8,128)(2,1)S(1)} %collective-permute-done.8.refs_1_, ...), custom_call_target="tpu_custom_call" | custom-call | tf_op jit(solution)/shard_map/pallas_call | solution.py:30
  33.7 3.9 %all-to-all-start = ((bf16[32,16,128]{2,1,0:T(8,128)(2,1)}), bf16[32,16,128]{2,1,0:T(8,128)(2,1)S(1)}, u32[]{:S(2)}, u32[]{:S(2)}) async-start(bf16[32,16,128]{2,1,0:T(8,128)(2,1)} %bitcast.1), calls=%async_computation | async-start | bytes 262144 | tf_op jit(solution)/shard_map/all_to_all | solution.py:358
  37.7 1.8 %collective-permute-start.12 = (bf16[64,512]{1,0:T(8,128)(2,1)S(1)}, bf16[64,512]{1,0:T(8,128)(2,1)S(1)}, u32[]{:S(2)}, u32[]{:S(2)}) collective-permute-start(bf16[64,512]{1,0:T(8,128)(2,1)S(1)} %get-tuple-element.26), channel_id=1, source_target_pairs={{0,1},{1,0},{2,3},{3,2},{4,5},{5,4},{6,7},{7,6},{8,9},{9,8},{10,11... | collective-permute-start | bytes 196616 | tf_op jit(solution)/shard_map/ppermute | solution.py:22
  39.5 1.5 %collective-permute-start.13 = (bf16[64,512]{1,0:T(8,128)(2,1)S(1)}, bf16[64,512]{1,0:T(8,128)(2,1)S(1)}, u32[]{:S(2)}, u32[]{:S(2)}) collective-permute-start(bf16[64,512]{1,0:T(8,128)(2,1)S(1)} %get-tuple-element.27), channel_id=1, source_target_pairs={{0,2},{1,3},{2,0},{3,1},{4,6},{5,7},{6,4},{7,5},{8,10},{9,11},{10,... | collective-permute-start | bytes 196616 | tf_op jit(solution)/shard_map/ppermute | solution.py:22
  41.0 0.3 collective-permute-start.14
  41.2 4.2 %all-to-all-done = bf16[32,16,128]{2,1,0:T(8,128)(2,1)S(1)} async-done(((bf16[32,16,128]{2,1,0:T(8,128)(2,1)}), bf16[32,16,128]{2,1,0:T(8,128)(2,1)S(1)}, u32[]{:S(2)}, u32[]{:S(2)}) %all-to-all-start) | async-done | bytes 131104 | tf_op jit(solution)/shard_map/all_to_all | solution.py:358
  45.4 0.8 %shard_map.85 = f32[32,1,128]{2,1,0:T(1,128)} custom-call(bf16[8,4,16,128]{3,2,1,0:T(8,128)(2,1)S(1)} %bitcast.3), custom_call_target="tpu_custom_call" | custom-call | tf_op jit(solution)/shard_map/pallas_call | solution.py:30
  46.2 2.6 %all-to-all-start.1 = ((f32[32,1,128]{2,1,0:T(1,128)}), f32[32,1,128]{2,1,0:T(1,128)S(1)}, u32[]{:S(2)}, u32[]{:S(2)}) async-start(f32[32,1,128]{2,1,0:T(1,128)} %shard_map.85), calls=%async_computation.1 | async-start | bytes 32768 | tf_op jit(solution)/shard_map/all_to_all | solution.py:369
  48.7 0.0 collective-permute-done.12.refs_1_
  48.7 0.0 collective-permute-done.13.refs_2_
  48.8 0.0 collective-permute-done.14.refs_3_
  48.8 0.7 %shard_map.84 = bf16[64,2048]{1,0:T(8,128)(2,1)} custom-call(bf16[64,512]{1,0:T(8,128)(2,1)S(1)} %get-tuple-element.25.refs_0_, bf16[64,512]{1,0:T(8,128)(2,1)S(1)} %collective-permute-done.12.refs_1_, bf16[64,512]{1,0:T(8,128)(2,1)S(1)} %collective-permute-done.13.refs_2_, bf16[64,512]{1,0:T(8,128)(2,1)S(1)} %collective-permute-done.14.refs_3_), custom_call_target="tpu_custom_call" | custom-call | tf_op jit(solution)/shard_map/pallas_call | solution.py:30
  49.5 6.3 %all-to-all-done.1.tables_ref = f32[32,1,128]{2,1,0:T(1,128)S(1)} async-done(((f32[32,1,128]{2,1,0:T(1,128)}), f32[32,1,128]{2,1,0:T(1,128)S(1)}, u32[]{:S(2)}, u32[]{:S(2)}) %all-to-all-start.1) | async-done | bytes 16416 | tf_op jit(solution)/shard_map/all_to_all | solution.py:369
  55.8 0.8 %shard_map.86 = f32[8,8]{1,0:T(8,128)} custom-call(f32[32,1,128]{2,1,0:T(1,128)S(1)} %all-to-all-done.1.tables_ref), custom_call_target="tpu_custom_call" | custom-call | tf_op jit(solution)/shard_map/pallas_call | solution.py:30
  (3 shorter events, 0.1 us)
Async XLA Ops:
  2.0 13.9 %collective-permute-start = (bf16[304,512]{1,0:T(8,128)(2,1)S(1)}, bf16[304,512]{1,0:T(8,128)(2,1)S(1)}, u32[]{:S(2)}, u32[]{:S(2)}) collective-permute-start(bf16[304,512]{1,0:T(8,128)(2,1)S(1)} %get-tuple-element.16), channel_id=1, source_target_pairs={{0,1},{1,0},{2,3},{3,2},{4,5},{5,4},{6,7},{7,6},{8,9},{9,8},{10,11... | collective-permute-start | bytes 933896 | tf_op jit(solution)/shard_map/ppermute | solution.py:22
  5.0 10.9 %collective-permute-start.3 = (bf16[80,1024]{1,0:T(8,128)(2,1)S(1)}, bf16[80,1024]{1,0:T(8,128)(2,1)S(1)}, u32[]{:S(2)}, u32[]{:S(2)}) collective-permute-start(bf16[80,1024]{1,0:T(8,128)(2,1)S(1)} %get-tuple-element.18), channel_id=1, source_target_pairs={{0,2},{1,3},{2,0},{3,1},{4,6},{5,7},{6,4},{7,5},{8,10},{9,11},{10,... | collective-permute-start | bytes 491528 | tf_op jit(solution)/shard_map/ppermute | solution.py:22
  6.6 8.3 %collective-permute-start.1 = (bf16[32,1024]{1,0:T(8,128)(2,1)S(1)}, bf16[32,1024]{1,0:T(8,128)(2,1)S(1)}, u32[]{:S(2)}, u32[]{:S(2)}) collective-permute-start(bf16[32,1024]{1,0:T(8,128)(2,1)S(1)} %get-tuple-element.17.refs_3_), channel_id=1, source_target_pairs={{0,6},{1,7},{2,4},{3,5},{4,2},{5,3},{6,0},{7,1},{8,14},{9,15},{10,... | collective-permute-start | bytes 196616 | tf_op jit(solution)/shard_map/ppermute | solution.py:22
  9.1 6.8 %collective-permute-start.2 = (bf16[32,1024]{1,0:T(8,128)(2,1)S(1)}, bf16[32,1024]{1,0:T(8,128)(2,1)S(1)}, u32[]{:S(2)}, u32[]{:S(2)}) collective-permute-start(bf16[32,1024]{1,0:T(8,128)(2,1)S(1)} %get-tuple-element.17.refs_3_), channel_id=1, source_target_pairs={{0,4},{1,5},{2,6},{3,7},{4,0},{5,1},{6,2},{7,3},{8,12},{9,13},{10,... | collective-permute-start | bytes 196616 | tf_op jit(solution)/shard_map/ppermute | solution.py:22
  15.9 7.0 %copy-start.1 = (bf16[192,2048]{1,0:T(8,128)(2,1)S(1)}, bf16[192,2048]{1,0:T(8,128)(2,1)}, u32[]{:S(2)}) copy-start(bf16[192,2048]{1,0:T(8,128)(2,1)} %up_ref.3) | copy-start | bytes 2359300
  15.9 7.0 %copy-start = (bf16[192,2048]{1,0:T(8,128)(2,1)S(1)}, bf16[192,2048]{1,0:T(8,128)(2,1)}, u32[]{:S(2)}) copy-start(bf16[192,2048]{1,0:T(8,128)(2,1)} %gate_ref.3) | copy-start | bytes 2359300
  15.9 6.4 %collective-permute-start.5 = (bf16[128,1024]{1,0:T(8,128)(2,1)S(1)}, bf16[128,1024]{1,0:T(8,128)(2,1)S(1)}, u32[]{:S(2)}, u32[]{:S(2)}) collective-permute-start(bf16[128,1024]{1,0:T(8,128)(2,1)S(1)} %shard_map.78.after_ref.near_ref), channel_id=1, source_target_pairs={{0,1},{1,0},{2,3},{3,2},{4,5},{5,4},{6,7},{7,6},{8,9},{9,8},{10,11... | collective-permute-start | bytes 786440 | tf_op jit(solution)/shard_map/ppermute | solution.py:22
  16.6 7.1 %collective-permute-start.4 = (bf16[320,512]{1,0:T(8,128)(2,1)S(1)}, bf16[320,512]{1,0:T(8,128)(2,1)S(1)}, u32[]{:S(2)}, u32[]{:S(2)}) collective-permute-start(bf16[320,512]{1,0:T(8,128)(2,1)S(1)} %shard_map.79), channel_id=1, source_target_pairs={{0,2},{1,3},{2,0},{3,1},{4,6},{5,7},{6,4},{7,5},{8,10},{9,11},{10,... | collective-permute-start | bytes 983048 | tf_op jit(solution)/shard_map/ppermute | solution.py:22
  16.9 6.0 %collective-permute-start.7 = (bf16[128,1024]{1,0:T(8,128)(2,1)S(1)}, bf16[128,1024]{1,0:T(8,128)(2,1)S(1)}, u32[]{:S(2)}, u32[]{:S(2)}) collective-permute-start(bf16[128,1024]{1,0:T(8,128)(2,1)S(1)} %shard_map.78.after_ref.near_ref), channel_id=1, source_target_pairs={{0,8},{8,0},{16,24},{24,16},{1,9},{9,1},{17,25},{25,17},{2,10},{10... | collective-permute-start | bytes 786440 | tf_op jit(solution)/shard_map/ppermute | solution.py:22
  22.4 1.5 %collective-permute-start.6 = (bf16[128,1024]{1,0:T(8,128)(2,1)S(1)}, bf16[128,1024]{1,0:T(8,128)(2,1)S(1)}, u32[]{:S(2)}, u32[]{:S(2)}) collective-permute-start(bf16[128,1024]{1,0:T(8,128)(2,1)S(1)} %collective-permute-done.5.far_ref.refs_1_), channel_id=1, source_target_pairs={{0,8},{8,0},{16,24},{24,16},{1,9},{9,1},{17,25},{25,17},{2,10},{10... | collective-permute-start | bytes 786440 | tf_op jit(solution)/shard_map/ppermute | solution.py:22
  22.4 5.6 %collective-permute-start.11 = (bf16[112,512]{1,0:T(8,128)(2,1)S(1)}, bf16[112,512]{1,0:T(8,128)(2,1)S(1)}, u32[]{:S(2)}, u32[]{:S(2)}) collective-permute-start(bf16[112,512]{1,0:T(8,128)(2,1)S(1)} %shard_map.82), channel_id=1, source_target_pairs={{0,1},{1,0},{2,3},{3,2},{4,5},{5,4},{6,7},{7,6},{8,9},{9,8},{10,11... | collective-permute-start | bytes 344072 | tf_op jit(solution)/shard_map/ppermute | solution.py:22
  24.3 6.6 %collective-permute-start.10 = (bf16[192,256]{1,0:T(8,128)(2,1)S(1)}, bf16[192,256]{1,0:T(8,128)(2,1)S(1)}, u32[]{:S(2)}, u32[]{:S(2)}) collective-permute-start(bf16[192,256]{1,0:T(8,128)(2,1)S(1)} %shard_map.81.refs_0_), channel_id=1, source_target_pairs={{0,3},{1,2},{2,1},{3,0},{4,7},{5,6},{6,5},{7,4},{8,11},{9,10},{10,... | collective-permute-start | bytes 294920 | tf_op jit(solution)/shard_map/ppermute | solution.py:22
  25.9 6.3 %collective-permute-start.8 = (bf16[192,256]{1,0:T(8,128)(2,1)S(1)}, bf16[192,256]{1,0:T(8,128)(2,1)S(1)}, u32[]{:S(2)}, u32[]{:S(2)}) collective-permute-start(bf16[192,256]{1,0:T(8,128)(2,1)S(1)} %shard_map.81.refs_0_), channel_id=1, source_target_pairs={{0,2},{1,3},{2,0},{3,1},{4,6},{5,7},{6,4},{7,5},{8,10},{9,11},{10,... | collective-permute-start | bytes 294920 | tf_op jit(solution)/shard_map/ppermute | solution.py:22
  27.1 5.1 %collective-permute-start.9 = (bf16[192,256]{1,0:T(8,128)(2,1)S(1)}, bf16[192,256]{1,0:T(8,128)(2,1)S(1)}, u32[]{:S(2)}, u32[]{:S(2)}) collective-permute-start(bf16[192,256]{1,0:T(8,128)(2,1)S(1)} %shard_map.81.refs_0_), channel_id=1, source_target_pairs={{0,1},{1,0},{2,3},{3,2},{4,5},{5,4},{6,7},{7,6},{8,9},{9,8},{10,11... | collective-permute-start | bytes 294920 | tf_op jit(solution)/shard_map/ppermute | solution.py:22
  33.7 11.7 %all-to-all-start = ((bf16[32,16,128]{2,1,0:T(8,128)(2,1)}), bf16[32,16,128]{2,1,0:T(8,128)(2,1)S(1)}, u32[]{:S(2)}, u32[]{:S(2)}) async-start(bf16[32,16,128]{2,1,0:T(8,128)(2,1)} %bitcast.1), calls=%async_computation | async-start | bytes 262144 | tf_op jit(solution)/shard_map/all_to_all | solution.py:358
  37.7 11.1 %collective-permute-start.12 = (bf16[64,512]{1,0:T(8,128)(2,1)S(1)}, bf16[64,512]{1,0:T(8,128)(2,1)S(1)}, u32[]{:S(2)}, u32[]{:S(2)}) collective-permute-start(bf16[64,512]{1,0:T(8,128)(2,1)S(1)} %get-tuple-element.26), channel_id=1, source_target_pairs={{0,1},{1,0},{2,3},{3,2},{4,5},{5,4},{6,7},{7,6},{8,9},{9,8},{10,11... | collective-permute-start | bytes 196616 | tf_op jit(solution)/shard_map/ppermute | solution.py:22
  39.5 9.2 %collective-permute-start.13 = (bf16[64,512]{1,0:T(8,128)(2,1)S(1)}, bf16[64,512]{1,0:T(8,128)(2,1)S(1)}, u32[]{:S(2)}, u32[]{:S(2)}) collective-permute-start(bf16[64,512]{1,0:T(8,128)(2,1)S(1)} %get-tuple-element.27), channel_id=1, source_target_pairs={{0,2},{1,3},{2,0},{3,1},{4,6},{5,7},{6,4},{7,5},{8,10},{9,11},{10,... | collective-permute-start | bytes 196616 | tf_op jit(solution)/shard_map/ppermute | solution.py:22
  41.0 7.8 %collective-permute-start.14 = (bf16[64,512]{1,0:T(8,128)(2,1)S(1)}, bf16[64,512]{1,0:T(8,128)(2,1)S(1)}, u32[]{:S(2)}, u32[]{:S(2)}) collective-permute-start(bf16[64,512]{1,0:T(8,128)(2,1)S(1)} %get-tuple-element.28), channel_id=1, source_target_pairs={{0,3},{1,2},{2,1},{3,0},{4,7},{5,6},{6,5},{7,4},{8,11},{9,10},{10,... | collective-permute-start | bytes 196616 | tf_op jit(solution)/shard_map/ppermute | solution.py:22
  46.2 9.7 %all-to-all-start.1 = ((f32[32,1,128]{2,1,0:T(1,128)}), f32[32,1,128]{2,1,0:T(1,128)S(1)}, u32[]{:S(2)}, u32[]{:S(2)}) async-start(f32[32,1,128]{2,1,0:T(1,128)} %shard_map.85), calls=%async_computation.1 | async-start | bytes 32768 | tf_op jit(solution)/shard_map/all_to_all | solution.py:369

commit v24 on v21

--- a/solution.py
+++ b/solution.py
@@ -50,16 +50,15 @@
 
 
 def first_kernel(states_hbm, gain_hbm, down_hbm, route_hbm, out_ref, *refs):
-    with_z_ref, kept_ref, z_ref, early_ref, late_ref = refs[:5]
-    states_ref, gain_ref, route_ref, sems = refs[5:]
-    depth, width = down_hbm.shape[0], kept_ref.shape[1]
+    with_z_ref, z_ref, early_ref, late_ref = refs[:4]
+    states_ref, gain_ref, route_ref, sems = refs[4:]
+    depth, width = down_hbm.shape[0], early_ref.shape[1]
     rows, count = states_ref.shape[0], depth + TILE
     beside, first_x = with_z_ref.shape[0] - rows, early_ref.shape[0] - count
     left, right = with_z_ref.at[pl.ds(rows, beside), pl.ds(0, width)], with_z_ref.at[
         pl.ds(rows, beside), pl.ds(width, width)
     ]
     blocks = (
-        (0, 0, depth, kept_ref.at[pl.ds(0, depth)]),
         (2, 0, beside, left),
         (2, beside, beside, right),
         (2, 2 * beside, depth - 2 * beside, z_ref.at[pl.ds(0, depth - 2 * beside)]),
@@ -94,7 +93,6 @@
     terms = jnp.where(row == 0, high, jnp.where(row == 1, middle, jnp.where(row == 2, low, 0.0)))
     terms = jnp.concatenate([terms, jnp.zeros((TILE, width - part), f32)], 1)
     for ref, top in (
-        (kept_ref, depth),
         (z_ref, depth - 2 * beside),
         (early_ref, depth),
         (late_ref, depth - first_x),
@@ -163,19 +161,21 @@
 
 
 def features_kernel(*refs):
-    hidden_refs, (kept_ref, with_z_ref, z_ref, early_ref, late_ref) = refs[:HOLDERS], refs[HOLDERS:][:5]
-    block_refs, shares_hbm = refs[HOLDERS + 5 : 2 * HOLDERS + 5], refs[2 * HOLDERS + 5]
-    route_ref, features_ref, whole_ref, shares_ref, sem = refs[2 * HOLDERS + 6 :]
+    hidden_refs = refs[:HOLDERS]
+    down_ref, own_route_ref, with_z_ref, z_ref, early_ref, late_ref = refs[HOLDERS:][:6]
+    block_refs, shares_hbm = refs[HOLDERS + 6 : 2 * HOLDERS + 6], refs[2 * HOLDERS + 6]
+    route_ref, features_ref, whole_ref, shares_ref, sems = refs[2 * HOLDERS + 7 :]
     depth, tokens = hidden_refs[0].shape
     part, members = tokens // HOLDERS, lax.axis_size("tok")
     rows = tokens // members
-    count, width = kept_ref.shape
+    count, width = depth + TILE, early_ref.shape[1]
     beside = (2 * count - z_ref.shape[0]) // 2
     x_block = jnp.concatenate([early_ref[count:], late_ref[...]])
     z_block = jnp.concatenate(
         [with_z_ref[rows:, :width], with_z_ref[rows:, width:], z_ref[: count - 2 * beside]]
     )
-    downs = (kept_ref[...], x_block, z_block, z_ref[count - 2 * beside :])
+    own_block = down_ref[:, columns_of(holder(), width)]
+    downs = (own_block, x_block, z_block, z_ref[count - 2 * beside :])
 
     def place(m, piece):
         z = (holder() ^ m) * (members // HOLDERS // 2) + piece // 2
@@ -188,8 +188,11 @@
     for m, (hidden_ref, down) in enumerate(zip(hidden_refs, downs)):
         product = dot_f32(hidden_ref[...], down[:depth], (((0,), (0,)), ((), ())))
         output = product if output is None else output + product
-        terms = down[depth:, :part].astype(f32)
-        route = jnp.sum(terms[:HOLDERS], axis=0, keepdims=True)
+        if m:
+            terms = down[depth:, :part].astype(f32)
+            route = jnp.sum(terms[:HOLDERS], axis=0, keepdims=True)
+        else:
+            route = own_route_ref[...]
         column = jnp.sum(jnp.where(eye, route, 0.0), axis=1, keepdims=True)
         column = jnp.broadcast_to(column, (part, LANES))
         for piece in range(part // rows):
@@ -200,21 +203,28 @@
     mean = jnp.sum(wide, axis=0, keepdims=True) / tokens
     column = jnp.sum(wide * mean, axis=1, keepdims=True)
     row = jnp.transpose(jnp.broadcast_to(column, (tokens, LANES)))[:1]
-    gram = dot_f32(features, features, TRANSPOSED)
-    whole_ref[...] = (gram - column - row + jnp.sum(mean * mean)).astype(bf16)
-    at = 0
-    for i in range(tokens // TILE):
-        for j in range(tokens // LANES):
-            shares_ref[at * TILE : (at + 1) * TILE] = whole_ref[
-                i * TILE : (i + 1) * TILE, j * LANES : (j + 1) * LANES
-            ]
-            at += 1
-    copy = pltpu.make_async_copy(shares_ref, shares_hbm, sem)
-    copy.start()
+    square = jnp.sum(mean * mean)
+    copies = []
+    half, size = tokens // 2, shares_ref.shape[0] // 2
+    for side in range(2):
+        top = side * half
+        gram = dot_f32(features[top : top + half], features, TRANSPOSED)
+        whole_ref[...] = (gram - column[top : top + half] - row + square).astype(bf16)
+        at = side * size
+        for i in range(half // TILE):
+            for j in range(tokens // LANES):
+                shares_ref[at : at + TILE] = whole_ref[
+                    i * TILE : (i + 1) * TILE, j * LANES : (j + 1) * LANES
+                ]
+                at += TILE
+        there = pl.ds(side * size, size)
+        copies.append(pltpu.make_async_copy(shares_ref.at[there], shares_hbm.at[there], sems.at[side]))
+        copies[-1].start()
     for m, block_ref in enumerate(block_refs):
         for piece in range(part // rows):
             block_ref[piece * rows : (piece + 1) * rows] = features_ref[place(m, piece)]
-    copy.wait()
+    for copy in copies:
+        copy.wait()
 
 
 def place_kernel(*refs):
@@ -285,12 +295,12 @@
 
     count = depth + TILE
     beside, first_x = depth // 4 // TILE * TILE, depth // 2 // TILE * TILE
-    own, with_z, down_own, down_z, down_early, down_late = call(
+    own, with_z, down_z, down_early, down_late = call(
         first_kernel,
         [jax.ShapeDtypeStruct((n, model // 2), bf16) for n in (rows, rows + beside)]
         + [
             jax.ShapeDtypeStruct((n, part), bf16)
-            for n in (count, count - 2 * beside, count + first_x, count - first_x)
+            for n in (count - 2 * beside, count + first_x, count - first_x)
         ],
         [HBM] * 4,
         [
@@ -342,15 +352,15 @@
         features_kernel,
         [jax.ShapeDtypeStruct((token_part, part), bf16)] * HOLDERS
         + [jax.ShapeDtypeStruct((entries, LANES), bf16)],
-        [VMEM] * (HOLDERS + 5),
-        (*hiddens, down_own, with_z, down_z, down_early, down_late),
+        [VMEM] * (HOLDERS + 6),
+        (*hiddens, down_weight, route_weight, with_z, down_z, down_early, down_late),
         out_specs=[VMEM] * HOLDERS + [HBM],
         scratch=[
             pltpu.VMEM((tokens, LANES), f32),
             pltpu.VMEM((tokens, part), bf16),
-            pltpu.VMEM((tokens, tokens), bf16),
+            pltpu.VMEM((tokens // 2, tokens), bf16),
             pltpu.VMEM((entries, LANES), bf16),
-            pltpu.SemaphoreType.DMA,
+            pltpu.SemaphoreType.DMA((2,)),
         ],
     )
     arrived = lax.all_to_all(centered, ("grp", "tok"), split_axis=0, concat_axis=0, tiled=True)

time: 56.4 us -> 56.3 us (level)
  no operation moved by 1% of the time
where the time goes in v24:
time: 56.3 us; the launch traced here: 56.1 us
  waiting for transfers between devices  27.3 us (48%)
  starting transfers between devices  21.8 us (39%)
  Pallas kernels  6.25 us (11%)
  between operations  0.76 us (1%)
    ppermute x15, waiting for transfers between devices, swapped(): lax.ppermute(array, axis, [(i, i ^ mask) for i in range(lax.axis_size(axi...  16.7 us
    ppermute x15, starting transfers between devices, swapped(): lax.ppermute(array, axis, [(i, i ^ mask) for i in range(lax.axis_size(axi...  15.8 us
    all_to_all x1, waiting for transfers between devices, shards(): lax.all_to_all(tables, ('grp', 'tok'), split_axis=0, concat_axis=0, tiled...  6.33 us
    pallas_call x10, Pallas kernels, call(): pl.pallas_call(body, out_shape=outs, in_specs=in_specs, out_specs=jax.tre...  6.25 us
    all_to_all x1, waiting for transfers between devices, shards(): lax.all_to_all(centered, ('grp', 'tok'), split_axis=0, concat_axis=0, til...  4.19 us
    all_to_all x1, starting transfers between devices, shards(): lax.all_to_all(centered, ('grp', 'tok'), split_axis=0, concat_axis=0, til...  3.48 us
    all_to_all x1, starting transfers between devices, shards(): lax.all_to_all(tables, ('grp', 'tok'), split_axis=0, concat_axis=0, tiled...  2.57 us
  transfers between devices with their start and end apart: 17, of which 9 were waited for; matrix products, arithmetic and copies ran while one was open for 0% of the time, Pallas kernels for 5%

profile of v24, /device:TPU:0, one launch (start us, length us, event | category | flops | bytes accessed | tf_op | source)
XLA Modules:
  0.0 56.1 jit_solution(2173569172907171099)
XLA Ops:
  0.6 1.3 %shard_map.77 = (bf16[32,1024]{1,0:T(8,128)(2,1)S(1)}, bf16[80,1024]{1,0:T(8,128)(2,1)S(1)}, bf16[112,512]{1,0:T(8,128)(2,1)S(1)}, bf16[304,512]{1,0:T(8,128)(2,1)S(1)}, bf16[112,512]{1,0:T(8,128)(2,1)S(1)}) custom-call(bf16[32,2048]{1,0:T(8,128)(2,1)} %states_hbm.1, f32[1,2048]{1,0:T(1,128)} %bitcast.4, bf16[192,2048]{1,0:T(8,128)(2,1)} %refs_4_.1, ...), custom_call_target="tpu_custom_call" | custom-call | tf_op jit(solution)/shard_map/pallas_call | solution.py:29
  1.9 3.0 %collective-permute-start = (bf16[304,512]{1,0:T(8,128)(2,1)S(1)}, bf16[304,512]{1,0:T(8,128)(2,1)S(1)}, u32[]{:S(2)}, u32[]{:S(2)}) collective-permute-start(bf16[304,512]{1,0:T(8,128)(2,1)S(1)} %get-tuple-element.15), channel_id=1, source_target_pairs={{0,1},{1,0},{2,3},{3,2},{4,5},{5,4},{6,7},{7,6},{8,9},{9,8},{10,11... | collective-permute-start | bytes 933896 | tf_op jit(solution)/shard_map/ppermute | solution.py:21
  5.0 1.6 %collective-permute-start.3 = (bf16[80,1024]{1,0:T(8,128)(2,1)S(1)}, bf16[80,1024]{1,0:T(8,128)(2,1)S(1)}, u32[]{:S(2)}, u32[]{:S(2)}) collective-permute-start(bf16[80,1024]{1,0:T(8,128)(2,1)S(1)} %get-tuple-element.17), channel_id=1, source_target_pairs={{0,2},{1,3},{2,0},{3,1},{4,6},{5,7},{6,4},{7,5},{8,10},{9,11},{10,... | collective-permute-start | bytes 491528 | tf_op jit(solution)/shard_map/ppermute | solution.py:21
  6.5 2.5 %collective-permute-start.1 = (bf16[32,1024]{1,0:T(8,128)(2,1)S(1)}, bf16[32,1024]{1,0:T(8,128)(2,1)S(1)}, u32[]{:S(2)}, u32[]{:S(2)}) collective-permute-start(bf16[32,1024]{1,0:T(8,128)(2,1)S(1)} %get-tuple-element.16.refs_3_), channel_id=1, source_target_pairs={{0,6},{1,7},{2,4},{3,5},{4,2},{5,3},{6,0},{7,1},{8,14},{9,15},{10,... | collective-permute-start | bytes 196616 | tf_op jit(solution)/shard_map/ppermute | solution.py:21
  9.0 0.1 collective-permute-start.2
  9.1 5.7 %collective-permute-done.1.refs_0_ = bf16[32,1024]{1,0:T(8,128)(2,1)S(1)} collective-permute-done((bf16[32,1024]{1,0:T(8,128)(2,1)S(1)}, bf16[32,1024]{1,0:T(8,128)(2,1)S(1)}, u32[]{:S(2)}, u32[]{:S(2)}) %collective-permute-start.1) | collective-permute-done | bytes 65568 | tf_op jit(solution)/shard_map/ppermute | solution.py:21
  14.8 1.0 %collective-permute-done.2.refs_1_ = bf16[32,1024]{1,0:T(8,128)(2,1)S(1)} collective-permute-done((bf16[32,1024]{1,0:T(8,128)(2,1)S(1)}, bf16[32,1024]{1,0:T(8,128)(2,1)S(1)}, u32[]{:S(2)}, u32[]{:S(2)}) %collective-permute-start.2) | collective-permute-done | bytes 65568 | tf_op jit(solution)/shard_map/ppermute | solution.py:21
  15.8 0.0 collective-permute-done.3.refs_2_.refs_6_
  15.8 0.0 collective-permute-done.after_ref.second_ref.refs_8_
  15.8 0.0 copy-start.1
  15.9 0.0 copy-start
  15.9 0.6 %collective-permute-start.5 = (bf16[128,1024]{1,0:T(8,128)(2,1)S(1)}, bf16[128,1024]{1,0:T(8,128)(2,1)S(1)}, u32[]{:S(2)}, u32[]{:S(2)}) collective-permute-start(bf16[128,1024]{1,0:T(8,128)(2,1)S(1)} %shard_map.78.after_ref.near_ref), channel_id=1, source_target_pairs={{0,1},{1,0},{2,3},{3,2},{4,5},{5,4},{6,7},{7,6},{8,9},{9,8},{10,11... | collective-permute-start | bytes 786440 | tf_op jit(solution)/shard_map/ppermute | solution.py:21
  16.5 0.3 collective-permute-start.4
  16.9 0.0 collective-permute-start.7
  16.9 5.5 %collective-permute-done.5.far_ref.refs_1_ = bf16[128,1024]{1,0:T(8,128)(2,1)S(1)} collective-permute-done((bf16[128,1024]{1,0:T(8,128)(2,1)S(1)}, bf16[128,1024]{1,0:T(8,128)(2,1)S(1)}, u32[]{:S(2)}, u32[]{:S(2)}) %collective-permute-start.5) | collective-permute-done | bytes 262176 | tf_op jit(solution)/shard_map/ppermute | solution.py:21
  22.3 0.0 collective-permute-start.6
  22.3 0.5 collective-permute-start.11
  22.9 0.0 collective-permute-done.7.near2_ref
  22.9 0.0 copy-done.1
  22.9 0.0 copy-done
  22.9 0.8 %shard_map.80 = (bf16[192,128]{1,0:T(8,128)(2,1)S(1)}, f32[192,128]{1,0:T(8,128)S(1)}, f32[192,128]{1,0:T(8,128)S(1)}) custom-call(bf16[128,1024]{1,0:T(8,128)(2,1)S(1)} %shard_map.78.after_ref.near_ref, bf16[128,1024]{1,0:T(8,128)(2,1)S(1)} %collective-permute-done.7.near2_ref, bf16[128,1024]{1,0:T(8,128)(2,1)S(1)} %collective-permute-done.5.far_ref.refs_1_, ...), custom_call_target="tpu_custom_call" | custom-call | tf_op jit(solution)/shard_map/pallas_call | solution.py:29
  23.7 0.0 collective-permute-done.4.after_ref.refs_7_
  23.7 0.2 collective-permute-done.6.far2_ref
  23.9 0.0 copy-start.2
  23.9 0.0 copy-start.3
  23.9 0.4 shard_map.81.refs_0_
  24.2 1.6 %collective-permute-start.10 = (bf16[192,256]{1,0:T(8,128)(2,1)S(1)}, bf16[192,256]{1,0:T(8,128)(2,1)S(1)}, u32[]{:S(2)}, u32[]{:S(2)}) collective-permute-start(bf16[192,256]{1,0:T(8,128)(2,1)S(1)} %shard_map.81.refs_0_), channel_id=1, source_target_pairs={{0,3},{1,2},{2,1},{3,0},{4,7},{5,6},{6,5},{7,4},{8,11},{9,10},{10,... | collective-permute-start | bytes 294920 | tf_op jit(solution)/shard_map/ppermute | solution.py:21
  25.8 0.5 collective-permute-start.8
  26.4 1.4 %collective-permute-start.9 = (bf16[192,256]{1,0:T(8,128)(2,1)S(1)}, bf16[192,256]{1,0:T(8,128)(2,1)S(1)}, u32[]{:S(2)}, u32[]{:S(2)}) collective-permute-start(bf16[192,256]{1,0:T(8,128)(2,1)S(1)} %shard_map.81.refs_0_), channel_id=1, source_target_pairs={{0,2},{1,3},{2,0},{3,1},{4,6},{5,7},{6,4},{7,5},{8,10},{9,11},{10,... | collective-permute-start | bytes 294920 | tf_op jit(solution)/shard_map/ppermute | solution.py:21
  27.8 0.1 collective-permute-done.11.refs_9_
  27.9 3.0 %collective-permute-done.10.refs_3_ = bf16[192,256]{1,0:T(8,128)(2,1)S(1)} collective-permute-done((bf16[192,256]{1,0:T(8,128)(2,1)S(1)}, bf16[192,256]{1,0:T(8,128)(2,1)S(1)}, u32[]{:S(2)}, u32[]{:S(2)}) %collective-permute-start.10) | collective-permute-done | bytes 98336 | tf_op jit(solution)/shard_map/ppermute | solution.py:21
  30.8 1.3 %collective-permute-done.8.refs_1_ = bf16[192,256]{1,0:T(8,128)(2,1)S(1)} collective-permute-done((bf16[192,256]{1,0:T(8,128)(2,1)S(1)}, bf16[192,256]{1,0:T(8,128)(2,1)S(1)}, u32[]{:S(2)}, u32[]{:S(2)}) %collective-permute-start.8) | collective-permute-done | bytes 98336 | tf_op jit(solution)/shard_map/ppermute | solution.py:21
  32.1 0.0 collective-permute-done.9.refs_2_
  32.2 0.0 copy-done.2
  32.2 0.0 copy-done.3
  32.2 1.4 %shard_map.83 = (bf16[64,512]{1,0:T(8,128)(2,1)S(1)}, bf16[64,512]{1,0:T(8,128)(2,1)S(1)}, bf16[64,512]{1,0:T(8,128)(2,1)S(1)}, bf16[64,512]{1,0:T(8,128)(2,1)S(1)}, bf16[512,128]{1,0:T(8,128)(2,1)}) custom-call(bf16[192,256]{1,0:T(8,128)(2,1)S(1)} %shard_map.81.refs_0_, bf16[192,256]{1,0:T(8,128)(2,1)S(1)} %collective-permute-done.8.refs_1_, ...), custom_call_target="tpu_custom_call" | custom-call | tf_op jit(solution)/shard_map/pallas_call | solution.py:29
  33.6 3.5 %all-to-all-start = ((bf16[32,16,128]{2,1,0:T(8,128)(2,1)}), bf16[32,16,128]{2,1,0:T(8,128)(2,1)S(1)}, u32[]{:S(2)}, u32[]{:S(2)}) async-start(bf16[32,16,128]{2,1,0:T(8,128)(2,1)} %bitcast.1), calls=%async_computation | async-start | bytes 262144 | tf_op jit(solution)/shard_map/all_to_all | solution.py:366
  37.1 1.8 %collective-permute-start.12 = (bf16[64,512]{1,0:T(8,128)(2,1)S(1)}, bf16[64,512]{1,0:T(8,128)(2,1)S(1)}, u32[]{:S(2)}, u32[]{:S(2)}) collective-permute-start(bf16[64,512]{1,0:T(8,128)(2,1)S(1)} %get-tuple-element.24), channel_id=1, source_target_pairs={{0,1},{1,0},{2,3},{3,2},{4,5},{5,4},{6,7},{7,6},{8,9},{9,8},{10,11... | collective-permute-start | bytes 196616 | tf_op jit(solution)/shard_map/ppermute | solution.py:21
  38.9 1.5 %collective-permute-start.13 = (bf16[64,512]{1,0:T(8,128)(2,1)S(1)}, bf16[64,512]{1,0:T(8,128)(2,1)S(1)}, u32[]{:S(2)}, u32[]{:S(2)}) collective-permute-start(bf16[64,512]{1,0:T(8,128)(2,1)S(1)} %get-tuple-element.25), channel_id=1, source_target_pairs={{0,2},{1,3},{2,0},{3,1},{4,6},{5,7},{6,4},{7,5},{8,10},{9,11},{10,... | collective-permute-start | bytes 196616 | tf_op jit(solution)/shard_map/ppermute | solution.py:21
  40.4 0.3 collective-permute-start.14
  40.7 4.2 %all-to-all-done = bf16[32,16,128]{2,1,0:T(8,128)(2,1)S(1)} async-done(((bf16[32,16,128]{2,1,0:T(8,128)(2,1)}), bf16[32,16,128]{2,1,0:T(8,128)(2,1)S(1)}, u32[]{:S(2)}, u32[]{:S(2)}) %all-to-all-start) | async-done | bytes 131104 | tf_op jit(solution)/shard_map/all_to_all | solution.py:366
  44.8 0.8 %shard_map.85 = f32[32,1,128]{2,1,0:T(1,128)} custom-call(bf16[8,4,16,128]{3,2,1,0:T(8,128)(2,1)S(1)} %bitcast.3), custom_call_target="tpu_custom_call" | custom-call | tf_op jit(solution)/shard_map/pallas_call | solution.py:29
  45.6 2.6 %all-to-all-start.1 = ((f32[32,1,128]{2,1,0:T(1,128)}), f32[32,1,128]{2,1,0:T(1,128)S(1)}, u32[]{:S(2)}, u32[]{:S(2)}) async-start(f32[32,1,128]{2,1,0:T(1,128)} %shard_map.85), calls=%async_computation.1 | async-start | bytes 32768 | tf_op jit(solution)/shard_map/all_to_all | solution.py:377
  48.2 0.0 collective-permute-done.12.refs_1_
  48.2 0.0 collective-permute-done.13.refs_2_
  48.2 0.0 collective-permute-done.14.refs_3_
  48.2 0.7 %shard_map.84 = bf16[64,2048]{1,0:T(8,128)(2,1)} custom-call(bf16[64,512]{1,0:T(8,128)(2,1)S(1)} %get-tuple-element.23.refs_0_, bf16[64,512]{1,0:T(8,128)(2,1)S(1)} %collective-permute-done.12.refs_1_, bf16[64,512]{1,0:T(8,128)(2,1)S(1)} %collective-permute-done.13.refs_2_, bf16[64,512]{1,0:T(8,128)(2,1)S(1)} %collective-permute-done.14.refs_3_), custom_call_target="tpu_custom_call" | custom-call | tf_op jit(solution)/shard_map/pallas_call | solution.py:29
  49.0 6.3 %all-to-all-done.1.tables_ref = f32[32,1,128]{2,1,0:T(1,128)S(1)} async-done(((f32[32,1,128]{2,1,0:T(1,128)}), f32[32,1,128]{2,1,0:T(1,128)S(1)}, u32[]{:S(2)}, u32[]{:S(2)}) %all-to-all-start.1) | async-done | bytes 16416 | tf_op jit(solution)/shard_map/all_to_all | solution.py:377
  55.3 0.8 %shard_map.86 = f32[8,8]{1,0:T(8,128)} custom-call(f32[32,1,128]{2,1,0:T(1,128)S(1)} %all-to-all-done.1.tables_ref), custom_call_target="tpu_custom_call" | custom-call | tf_op jit(solution)/shard_map/pallas_call | solution.py:29
  (3 shorter events, 0.1 us)
Async XLA Ops:
  1.9 13.9 %collective-permute-start = (bf16[304,512]{1,0:T(8,128)(2,1)S(1)}, bf16[304,512]{1,0:T(8,128)(2,1)S(1)}, u32[]{:S(2)}, u32[]{:S(2)}) collective-permute-start(bf16[304,512]{1,0:T(8,128)(2,1)S(1)} %get-tuple-element.15), channel_id=1, source_target_pairs={{0,1},{1,0},{2,3},{3,2},{4,5},{5,4},{6,7},{7,6},{8,9},{9,8},{10,11... | collective-permute-start | bytes 933896 | tf_op jit(solution)/shard_map/ppermute | solution.py:21
  5.0 10.9 %collective-permute-start.3 = (bf16[80,1024]{1,0:T(8,128)(2,1)S(1)}, bf16[80,1024]{1,0:T(8,128)(2,1)S(1)}, u32[]{:S(2)}, u32[]{:S(2)}) collective-permute-start(bf16[80,1024]{1,0:T(8,128)(2,1)S(1)} %get-tuple-element.17), channel_id=1, source_target_pairs={{0,2},{1,3},{2,0},{3,1},{4,6},{5,7},{6,4},{7,5},{8,10},{9,11},{10,... | collective-permute-start | bytes 491528 | tf_op jit(solution)/shard_map/ppermute | solution.py:21
  6.5 8.3 %collective-permute-start.1 = (bf16[32,1024]{1,0:T(8,128)(2,1)S(1)}, bf16[32,1024]{1,0:T(8,128)(2,1)S(1)}, u32[]{:S(2)}, u32[]{:S(2)}) collective-permute-start(bf16[32,1024]{1,0:T(8,128)(2,1)S(1)} %get-tuple-element.16.refs_3_), channel_id=1, source_target_pairs={{0,6},{1,7},{2,4},{3,5},{4,2},{5,3},{6,0},{7,1},{8,14},{9,15},{10,... | collective-permute-start | bytes 196616 | tf_op jit(solution)/shard_map/ppermute | solution.py:21
  9.0 6.8 %collective-permute-start.2 = (bf16[32,1024]{1,0:T(8,128)(2,1)S(1)}, bf16[32,1024]{1,0:T(8,128)(2,1)S(1)}, u32[]{:S(2)}, u32[]{:S(2)}) collective-permute-start(bf16[32,1024]{1,0:T(8,128)(2,1)S(1)} %get-tuple-element.16.refs_3_), channel_id=1, source_target_pairs={{0,4},{1,5},{2,6},{3,7},{4,0},{5,1},{6,2},{7,3},{8,12},{9,13},{10,... | collective-permute-start | bytes 196616 | tf_op jit(solution)/shard_map/ppermute | solution.py:21
  15.8 7.0 %copy-start.1 = (bf16[192,2048]{1,0:T(8,128)(2,1)S(1)}, bf16[192,2048]{1,0:T(8,128)(2,1)}, u32[]{:S(2)}) copy-start(bf16[192,2048]{1,0:T(8,128)(2,1)} %up_ref.3) | copy-start | bytes 2359300
  15.9 7.0 %copy-start = (bf16[192,2048]{1,0:T(8,128)(2,1)S(1)}, bf16[192,2048]{1,0:T(8,128)(2,1)}, u32[]{:S(2)}) copy-start(bf16[192,2048]{1,0:T(8,128)(2,1)} %gate_ref.3) | copy-start | bytes 2359300
  15.9 6.4 %collective-permute-start.5 = (bf16[128,1024]{1,0:T(8,128)(2,1)S(1)}, bf16[128,1024]{1,0:T(8,128)(2,1)S(1)}, u32[]{:S(2)}, u32[]{:S(2)}) collective-permute-start(bf16[128,1024]{1,0:T(8,128)(2,1)S(1)} %shard_map.78.after_ref.near_ref), channel_id=1, source_target_pairs={{0,1},{1,0},{2,3},{3,2},{4,5},{5,4},{6,7},{7,6},{8,9},{9,8},{10,11... | collective-permute-start | bytes 786440 | tf_op jit(solution)/shard_map/ppermute | solution.py:21
  16.5 7.1 %collective-permute-start.4 = (bf16[320,512]{1,0:T(8,128)(2,1)S(1)}, bf16[320,512]{1,0:T(8,128)(2,1)S(1)}, u32[]{:S(2)}, u32[]{:S(2)}) collective-permute-start(bf16[320,512]{1,0:T(8,128)(2,1)S(1)} %shard_map.79), channel_id=1, source_target_pairs={{0,2},{1,3},{2,0},{3,1},{4,6},{5,7},{6,4},{7,5},{8,10},{9,11},{10,... | collective-permute-start | bytes 983048 | tf_op jit(solution)/shard_map/ppermute | solution.py:21
  16.9 6.0 %collective-permute-start.7 = (bf16[128,1024]{1,0:T(8,128)(2,1)S(1)}, bf16[128,1024]{1,0:T(8,128)(2,1)S(1)}, u32[]{:S(2)}, u32[]{:S(2)}) collective-permute-start(bf16[128,1024]{1,0:T(8,128)(2,1)S(1)} %shard_map.78.after_ref.near_ref), channel_id=1, source_target_pairs={{0,8},{8,0},{16,24},{24,16},{1,9},{9,1},{17,25},{25,17},{2,10},{10... | collective-permute-start | bytes 786440 | tf_op jit(solution)/shard_map/ppermute | solution.py:21
  22.3 1.5 %collective-permute-start.6 = (bf16[128,1024]{1,0:T(8,128)(2,1)S(1)}, bf16[128,1024]{1,0:T(8,128)(2,1)S(1)}, u32[]{:S(2)}, u32[]{:S(2)}) collective-permute-start(bf16[128,1024]{1,0:T(8,128)(2,1)S(1)} %collective-permute-done.5.far_ref.refs_1_), channel_id=1, source_target_pairs={{0,8},{8,0},{16,24},{24,16},{1,9},{9,1},{17,25},{25,17},{2,10},{10... | collective-permute-start | bytes 786440 | tf_op jit(solution)/shard_map/ppermute | solution.py:21
  22.3 5.6 %collective-permute-start.11 = (bf16[112,512]{1,0:T(8,128)(2,1)S(1)}, bf16[112,512]{1,0:T(8,128)(2,1)S(1)}, u32[]{:S(2)}, u32[]{:S(2)}) collective-permute-start(bf16[112,512]{1,0:T(8,128)(2,1)S(1)} %shard_map.82), channel_id=1, source_target_pairs={{0,1},{1,0},{2,3},{3,2},{4,5},{5,4},{6,7},{7,6},{8,9},{9,8},{10,11... | collective-permute-start | bytes 344072 | tf_op jit(solution)/shard_map/ppermute | solution.py:21
  23.9 8.3 %copy-start.2 = (bf16[192,2048]{1,0:T(8,128)(2,1)S(1)}, bf16[192,2048]{1,0:T(8,128)(2,1)}, u32[]{:S(2)}) copy-start(bf16[192,2048]{1,0:T(8,128)(2,1)} %refs_4_.1) | copy-start | bytes 2359300
  23.9 8.3 %copy-start.3 = (f32[1,64]{1,0:T(1,128)S(1)}, f32[1,64]{1,0:T(1,128)}, u32[]{:S(2)}) copy-start(f32[1,64]{1,0:T(1,128)} %refs_5_.1) | copy-start | bytes 772
  24.2 6.6 %collective-permute-start.10 = (bf16[192,256]{1,0:T(8,128)(2,1)S(1)}, bf16[192,256]{1,0:T(8,128)(2,1)S(1)}, u32[]{:S(2)}, u32[]{:S(2)}) collective-permute-start(bf16[192,256]{1,0:T(8,128)(2,1)S(1)} %shard_map.81.refs_0_), channel_id=1, source_target_pairs={{0,3},{1,2},{2,1},{3,0},{4,7},{5,6},{6,5},{7,4},{8,11},{9,10},{10,... | collective-permute-start | bytes 294920 | tf_op jit(solution)/shard_map/ppermute | solution.py:21
  25.8 6.3 %collective-permute-start.8 = (bf16[192,256]{1,0:T(8,128)(2,1)S(1)}, bf16[192,256]{1,0:T(8,128)(2,1)S(1)}, u32[]{:S(2)}, u32[]{:S(2)}) collective-permute-start(bf16[192,256]{1,0:T(8,128)(2,1)S(1)} %shard_map.81.refs_0_), channel_id=1, source_target_pairs={{0,1},{1,0},{2,3},{3,2},{4,5},{5,4},{6,7},{7,6},{8,9},{9,8},{10,11... | collective-permute-start | bytes 294920 | tf_op jit(solution)/shard_map/ppermute | solution.py:21
  26.4 5.8 %collective-permute-start.9 = (bf16[192,256]{1,0:T(8,128)(2,1)S(1)}, bf16[192,256]{1,0:T(8,128)(2,1)S(1)}, u32[]{:S(2)}, u32[]{:S(2)}) collective-permute-start(bf16[192,256]{1,0:T(8,128)(2,1)S(1)} %shard_map.81.refs_0_), channel_id=1, source_target_pairs={{0,2},{1,3},{2,0},{3,1},{4,6},{5,7},{6,4},{7,5},{8,10},{9,11},{10,... | collective-permute-start | bytes 294920 | tf_op jit(solution)/shard_map/ppermute | solution.py:21
  33.6 11.2 %all-to-all-start = ((bf16[32,16,128]{2,1,0:T(8,128)(2,1)}), bf16[32,16,128]{2,1,0:T(8,128)(2,1)S(1)}, u32[]{:S(2)}, u32[]{:S(2)}) async-start(bf16[32,16,128]{2,1,0:T(8,128)(2,1)} %bitcast.1), calls=%async_computation | async-start | bytes 262144 | tf_op jit(solution)/shard_map/all_to_all | solution.py:366
  37.1 11.1 %collective-permute-start.12 = (bf16[64,512]{1,0:T(8,128)(2,1)S(1)}, bf16[64,512]{1,0:T(8,128)(2,1)S(1)}, u32[]{:S(2)}, u32[]{:S(2)}) collective-permute-start(bf16[64,512]{1,0:T(8,128)(2,1)S(1)} %get-tuple-element.24), channel_id=1, source_target_pairs={{0,1},{1,0},{2,3},{3,2},{4,5},{5,4},{6,7},{7,6},{8,9},{9,8},{10,11... | collective-permute-start | bytes 196616 | tf_op jit(solution)/shard_map/ppermute | solution.py:21
  38.9 9.3 %collective-permute-start.13 = (bf16[64,512]{1,0:T(8,128)(2,1)S(1)}, bf16[64,512]{1,0:T(8,128)(2,1)S(1)}, u32[]{:S(2)}, u32[]{:S(2)}) collective-permute-start(bf16[64,512]{1,0:T(8,128)(2,1)S(1)} %get-tuple-element.25), channel_id=1, source_target_pairs={{0,2},{1,3},{2,0},{3,1},{4,6},{5,7},{6,4},{7,5},{8,10},{9,11},{10,... | collective-permute-start | bytes 196616 | tf_op jit(solution)/shard_map/ppermute | solution.py:21
  40.4 7.8 %collective-permute-start.14 = (bf16[64,512]{1,0:T(8,128)(2,1)S(1)}, bf16[64,512]{1,0:T(8,128)(2,1)S(1)}, u32[]{:S(2)}, u32[]{:S(2)}) collective-permute-start(bf16[64,512]{1,0:T(8,128)(2,1)S(1)} %get-tuple-element.26), channel_id=1, source_target_pairs={{0,3},{1,2},{2,1},{3,0},{4,7},{5,6},{6,5},{7,4},{8,11},{9,10},{10,... | collective-permute-start | bytes 196616 | tf_op jit(solution)/shard_map/ppermute | solution.py:21
  45.6 9.7 %all-to-all-start.1 = ((f32[32,1,128]{2,1,0:T(1,128)}), f32[32,1,128]{2,1,0:T(1,128)S(1)}, u32[]{:S(2)}, u32[]{:S(2)}) async-start(f32[32,1,128]{2,1,0:T(1,128)} %shard_map.85), calls=%async_computation.1 | async-start | bytes 32768 | tf_op jit(solution)/shard_map/all_to_all | solution.py:377

commit v25 on v21

--- a/solution.py
+++ b/solution.py
@@ -284,7 +284,7 @@
     part, token_part = model // HOLDERS, tokens // HOLDERS
 
     count = depth + TILE
-    beside, first_x = depth // 4 // TILE * TILE, depth // 2 // TILE * TILE
+    beside, first_x = depth // 4 // TILE * TILE, depth // 3 // TILE * TILE
     own, with_z, down_own, down_z, down_early, down_late = call(
         first_kernel,
         [jax.ShapeDtypeStruct((n, model // 2), bf16) for n in (rows, rows + beside)]

time: 56.4 us -> 56.7 us (level)
  waiting for transfers between devices: 27.3 us -> 27.9 us
    ppermute x15, waiting for transfers between devices: 16.7 us -> 17.4 us  [swapped(): lax.ppermute(array, axis, [(i, i ^ mask) for i in range(lax.axis_size(axi...]
  transfers between devices with their start and end apart: 17 -> 17, of which waited for: 9 -> 8; matrix products, arithmetic and copies ran while one was open for 0% -> 0% of each run, Pallas kernels for 5% -> 5%
where the time goes in v25:
time: 56.7 us; the launch traced here: 56.5 us
  waiting for transfers between devices  27.9 us (49%)
  starting transfers between devices  21.5 us (38%)
  Pallas kernels  6.32 us (11%)
  between operations  0.75 us (1%)
    ppermute x15, waiting for transfers between devices, swapped(): lax.ppermute(array, axis, [(i, i ^ mask) for i in range(lax.axis_size(axi...  17.4 us
    ppermute x15, starting transfers between devices, swapped(): lax.ppermute(array, axis, [(i, i ^ mask) for i in range(lax.axis_size(axi...  15.8 us
    all_to_all x1, waiting for transfers between devices, shards(): lax.all_to_all(tables, ('grp', 'tok'), split_axis=0, concat_axis=0, tiled...  6.33 us
    pallas_call x10, Pallas kernels, call(): pl.pallas_call(body, out_shape=outs, in_specs=in_specs, out_specs=jax.tre...  6.32 us
    all_to_all x1, waiting for transfers between devices, shards(): lax.all_to_all(centered, ('grp', 'tok'), split_axis=0, concat_axis=0, til...  4.19 us
    all_to_all x1, starting transfers between devices, shards(): lax.all_to_all(centered, ('grp', 'tok'), split_axis=0, concat_axis=0, til...  3.15 us
    all_to_all x1, starting transfers between devices, shards(): lax.all_to_all(tables, ('grp', 'tok'), split_axis=0, concat_axis=0, tiled...  2.55 us
  transfers between devices with their start and end apart: 17, of which 8 were waited for; matrix products, arithmetic and copies ran while one was open for 0% of the time, Pallas kernels for 5%

profile of v25, /device:TPU:0, one launch (start us, length us, event | category | flops | bytes accessed | tf_op | source)
XLA Modules:
  0.0 56.5 jit_solution(8189813449675406368)
XLA Ops:
  0.6 1.4 %shard_map.77 = (bf16[32,1024]{1,0:T(8,128)(2,1)S(1)}, bf16[80,1024]{1,0:T(8,128)(2,1)S(1)}, bf16[208,512]{1,0:T(8,128)(2,1)S(1)}, bf16[112,512]{1,0:T(8,128)(2,...) custom-call(bf16[32,2048]{1,0:T(8,128)(2,1)} %states_hbm.1, f32[1,2048]{1,0:T(1,128)} %bitcast.4, ...), custom_call_target="tpu_custom_call" | custom-call | tf_op jit(solution)/shard_map/pallas_call | solution.py:29
  2.0 3.0 %collective-permute-start = (bf16[272,512]{1,0:T(8,128)(2,1)S(1)}, bf16[272,512]{1,0:T(8,128)(2,1)S(1)}, u32[]{:S(2)}, u32[]{:S(2)}) collective-permute-start(bf16[272,512]{1,0:T(8,128)(2,1)S(1)} %get-tuple-element.16), channel_id=1, source_target_pairs={{0,1},{1,0},{2,3},{3,2},{4,5},{5,4},{6,7},{7,6},{8,9},{9,8},{10,11... | collective-permute-start | bytes 835592 | tf_op jit(solution)/shard_map/ppermute | solution.py:21
  5.0 1.6 %collective-permute-start.3 = (bf16[80,1024]{1,0:T(8,128)(2,1)S(1)}, bf16[80,1024]{1,0:T(8,128)(2,1)S(1)}, u32[]{:S(2)}, u32[]{:S(2)}) collective-permute-start(bf16[80,1024]{1,0:T(8,128)(2,1)S(1)} %get-tuple-element.18), channel_id=1, source_target_pairs={{0,2},{1,3},{2,0},{3,1},{4,6},{5,7},{6,4},{7,5},{8,10},{9,11},{10,... | collective-permute-start | bytes 491528 | tf_op jit(solution)/shard_map/ppermute | solution.py:21
  6.6 2.5 %collective-permute-start.1 = (bf16[32,1024]{1,0:T(8,128)(2,1)S(1)}, bf16[32,1024]{1,0:T(8,128)(2,1)S(1)}, u32[]{:S(2)}, u32[]{:S(2)}) collective-permute-start(bf16[32,1024]{1,0:T(8,128)(2,1)S(1)} %get-tuple-element.17.refs_3_), channel_id=1, source_target_pairs={{0,6},{1,7},{2,4},{3,5},{4,2},{5,3},{6,0},{7,1},{8,14},{9,15},{10,... | collective-permute-start | bytes 196616 | tf_op jit(solution)/shard_map/ppermute | solution.py:21
  9.1 0.1 collective-permute-start.2
  9.2 5.7 %collective-permute-done.1.refs_0_ = bf16[32,1024]{1,0:T(8,128)(2,1)S(1)} collective-permute-done((bf16[32,1024]{1,0:T(8,128)(2,1)S(1)}, bf16[32,1024]{1,0:T(8,128)(2,1)S(1)}, u32[]{:S(2)}, u32[]{:S(2)}) %collective-permute-start.1) | collective-permute-done | bytes 65568 | tf_op jit(solution)/shard_map/ppermute | solution.py:21
  14.9 1.0 %collective-permute-done.2.refs_1_ = bf16[32,1024]{1,0:T(8,128)(2,1)S(1)} collective-permute-done((bf16[32,1024]{1,0:T(8,128)(2,1)S(1)}, bf16[32,1024]{1,0:T(8,128)(2,1)S(1)}, u32[]{:S(2)}, u32[]{:S(2)}) %collective-permute-start.2) | collective-permute-done | bytes 65568 | tf_op jit(solution)/shard_map/ppermute | solution.py:21
  15.9 0.0 collective-permute-done.3.refs_2_.refs_5_
  15.9 0.0 collective-permute-done.after_ref.second_ref.refs_7_
  15.9 0.0 copy-start.1
  15.9 0.0 copy-start
  16.0 0.6 %collective-permute-start.5 = (bf16[128,1024]{1,0:T(8,128)(2,1)S(1)}, bf16[128,1024]{1,0:T(8,128)(2,1)S(1)}, u32[]{:S(2)}, u32[]{:S(2)}) collective-permute-start(bf16[128,1024]{1,0:T(8,128)(2,1)S(1)} %shard_map.78.after_ref.near_ref), channel_id=1, source_target_pairs={{0,1},{1,0},{2,3},{3,2},{4,5},{5,4},{6,7},{7,6},{8,9},{9,8},{10,11... | collective-permute-start | bytes 786440 | tf_op jit(solution)/shard_map/ppermute | solution.py:21
  16.6 0.3 collective-permute-start.4
  16.9 0.0 collective-permute-start.7
  16.9 5.5 %collective-permute-done.5.far_ref.refs_1_ = bf16[128,1024]{1,0:T(8,128)(2,1)S(1)} collective-permute-done((bf16[128,1024]{1,0:T(8,128)(2,1)S(1)}, bf16[128,1024]{1,0:T(8,128)(2,1)S(1)}, u32[]{:S(2)}, u32[]{:S(2)}) %collective-permute-start.5) | collective-permute-done | bytes 262176 | tf_op jit(solution)/shard_map/ppermute | solution.py:21
  22.4 0.0 collective-permute-start.6
  22.4 0.5 collective-permute-start.11
  22.9 0.0 collective-permute-done.7.near2_ref
  22.9 0.0 copy-done.1
  22.9 0.0 copy-done
  22.9 0.8 %shard_map.80 = (bf16[192,128]{1,0:T(8,128)(2,1)S(1)}, f32[192,128]{1,0:T(8,128)S(1)}, f32[192,128]{1,0:T(8,128)S(1)}) custom-call(bf16[128,1024]{1,0:T(8,128)(2,1)S(1)} %shard_map.78.after_ref.near_ref, bf16[128,1024]{1,0:T(8,128)(2,1)S(1)} %collective-permute-done.7.near2_ref, bf16[128,1024]{1,0:T(8,128)(2,1)S(1)} %collective-permute-done.5.far_ref.refs_1_, ...), custom_call_target="tpu_custom_call" | custom-call | tf_op jit(solution)/shard_map/pallas_call | solution.py:29
  23.7 0.0 collective-permute-done.4.after_ref.refs_6_
  23.7 0.2 collective-permute-done.6.far2_ref
  23.9 0.4 shard_map.81.refs_0_
  24.3 1.6 %collective-permute-start.10 = (bf16[192,256]{1,0:T(8,128)(2,1)S(1)}, bf16[192,256]{1,0:T(8,128)(2,1)S(1)}, u32[]{:S(2)}, u32[]{:S(2)}) collective-permute-start(bf16[192,256]{1,0:T(8,128)(2,1)S(1)} %shard_map.81.refs_0_), channel_id=1, source_target_pairs={{0,3},{1,2},{2,1},{3,0},{4,7},{5,6},{6,5},{7,4},{8,11},{9,10},{10,... | collective-permute-start | bytes 294920 | tf_op jit(solution)/shard_map/ppermute | solution.py:21
  25.9 0.5 collective-permute-start.8
  26.4 1.4 %collective-permute-start.9 = (bf16[192,256]{1,0:T(8,128)(2,1)S(1)}, bf16[192,256]{1,0:T(8,128)(2,1)S(1)}, u32[]{:S(2)}, u32[]{:S(2)}) collective-permute-start(bf16[192,256]{1,0:T(8,128)(2,1)S(1)} %shard_map.81.refs_0_), channel_id=1, source_target_pairs={{0,2},{1,3},{2,0},{3,1},{4,6},{5,7},{6,4},{7,5},{8,10},{9,11},{10,... | collective-permute-start | bytes 294920 | tf_op jit(solution)/shard_map/ppermute | solution.py:21
  27.9 3.3 %collective-permute-done.11.refs_8_ = bf16[144,512]{1,0:T(8,128)(2,1)S(1)} collective-permute-done((bf16[144,512]{1,0:T(8,128)(2,1)S(1)}, bf16[144,512]{1,0:T(8,128)(2,1)S(1)}, u32[]{:S(2)}, u32[]{:S(2)}) %collective-permute-start.11) | collective-permute-done | bytes 147488 | tf_op jit(solution)/shard_map/ppermute | solution.py:21
  31.1 0.0 collective-permute-done.10.refs_3_
  31.1 1.7 %collective-permute-done.8.refs_1_ = bf16[192,256]{1,0:T(8,128)(2,1)S(1)} collective-permute-done((bf16[192,256]{1,0:T(8,128)(2,1)S(1)}, bf16[192,256]{1,0:T(8,128)(2,1)S(1)}, u32[]{:S(2)}, u32[]{:S(2)}) %collective-permute-start.8) | collective-permute-done | bytes 98336 | tf_op jit(solution)/shard_map/ppermute | solution.py:21
  32.9 0.0 collective-permute-done.9.refs_2_
  32.9 1.5 %shard_map.83 = (bf16[64,512]{1,0:T(8,128)(2,1)S(1)}, bf16[64,512]{1,0:T(8,128)(2,1)S(1)}, bf16[64,512]{1,0:T(8,128)(2,1)S(1)}, bf16[64,512]{1,0:T(8,128)(2,1)S(1)}, bf16[512,128]{1,0:T(8,128)(2,1)}) custom-call(bf16[192,256]{1,0:T(8,128)(2,1)S(1)} %shard_map.81.refs_0_, bf16[192,256]{1,0:T(8,128)(2,1)S(1)} %collective-permute-done.8.refs_1_, ...), custom_call_target="tpu_custom_call" | custom-call | tf_op jit(solution)/shard_map/pallas_call | solution.py:29
  34.3 3.1 %all-to-all-start = ((bf16[32,16,128]{2,1,0:T(8,128)(2,1)}), bf16[32,16,128]{2,1,0:T(8,128)(2,1)S(1)}, u32[]{:S(2)}, u32[]{:S(2)}) async-start(bf16[32,16,128]{2,1,0:T(8,128)(2,1)} %bitcast.1), calls=%async_computation | async-start | bytes 262144 | tf_op jit(solution)/shard_map/all_to_all | solution.py:356
  37.5 1.8 %collective-permute-start.12 = (bf16[64,512]{1,0:T(8,128)(2,1)S(1)}, bf16[64,512]{1,0:T(8,128)(2,1)S(1)}, u32[]{:S(2)}, u32[]{:S(2)}) collective-permute-start(bf16[64,512]{1,0:T(8,128)(2,1)S(1)} %get-tuple-element.26), channel_id=1, source_target_pairs={{0,1},{1,0},{2,3},{3,2},{4,5},{5,4},{6,7},{7,6},{8,9},{9,8},{10,11... | collective-permute-start | bytes 196616 | tf_op jit(solution)/shard_map/ppermute | solution.py:21
  39.3 1.5 %collective-permute-start.13 = (bf16[64,512]{1,0:T(8,128)(2,1)S(1)}, bf16[64,512]{1,0:T(8,128)(2,1)S(1)}, u32[]{:S(2)}, u32[]{:S(2)}) collective-permute-start(bf16[64,512]{1,0:T(8,128)(2,1)S(1)} %get-tuple-element.27), channel_id=1, source_target_pairs={{0,2},{1,3},{2,0},{3,1},{4,6},{5,7},{6,4},{7,5},{8,10},{9,11},{10,... | collective-permute-start | bytes 196616 | tf_op jit(solution)/shard_map/ppermute | solution.py:21
  40.8 0.3 collective-permute-start.14
  41.1 4.2 %all-to-all-done = bf16[32,16,128]{2,1,0:T(8,128)(2,1)S(1)} async-done(((bf16[32,16,128]{2,1,0:T(8,128)(2,1)}), bf16[32,16,128]{2,1,0:T(8,128)(2,1)S(1)}, u32[]{:S(2)}, u32[]{:S(2)}) %all-to-all-start) | async-done | bytes 131104 | tf_op jit(solution)/shard_map/all_to_all | solution.py:356
  45.2 0.8 %shard_map.85 = f32[32,1,128]{2,1,0:T(1,128)} custom-call(bf16[8,4,16,128]{3,2,1,0:T(8,128)(2,1)S(1)} %bitcast.3), custom_call_target="tpu_custom_call" | custom-call | tf_op jit(solution)/shard_map/pallas_call | solution.py:29
  46.0 2.6 %all-to-all-start.1 = ((f32[32,1,128]{2,1,0:T(1,128)}), f32[32,1,128]{2,1,0:T(1,128)S(1)}, u32[]{:S(2)}, u32[]{:S(2)}) async-start(f32[32,1,128]{2,1,0:T(1,128)} %shard_map.85), calls=%async_computation.1 | async-start | bytes 32768 | tf_op jit(solution)/shard_map/all_to_all | solution.py:367
  48.6 0.0 collective-permute-done.12.refs_1_
  48.6 0.0 collective-permute-done.13.refs_2_
  48.6 0.0 collective-permute-done.14.refs_3_
  48.6 0.7 %shard_map.84 = bf16[64,2048]{1,0:T(8,128)(2,1)} custom-call(bf16[64,512]{1,0:T(8,128)(2,1)S(1)} %get-tuple-element.25.refs_0_, bf16[64,512]{1,0:T(8,128)(2,1)S(1)} %collective-permute-done.12.refs_1_, bf16[64,512]{1,0:T(8,128)(2,1)S(1)} %collective-permute-done.13.refs_2_, bf16[64,512]{1,0:T(8,128)(2,1)S(1)} %collective-permute-done.14.refs_3_), custom_call_target="tpu_custom_call" | custom-call | tf_op jit(solution)/shard_map/pallas_call | solution.py:29
  49.3 6.3 %all-to-all-done.1.tables_ref = f32[32,1,128]{2,1,0:T(1,128)S(1)} async-done(((f32[32,1,128]{2,1,0:T(1,128)}), f32[32,1,128]{2,1,0:T(1,128)S(1)}, u32[]{:S(2)}, u32[]{:S(2)}) %all-to-all-start.1) | async-done | bytes 16416 | tf_op jit(solution)/shard_map/all_to_all | solution.py:367
  55.7 0.8 %shard_map.86 = f32[8,8]{1,0:T(8,128)} custom-call(f32[32,1,128]{2,1,0:T(1,128)S(1)} %all-to-all-done.1.tables_ref), custom_call_target="tpu_custom_call" | custom-call | tf_op jit(solution)/shard_map/pallas_call | solution.py:29
  (3 shorter events, 0.1 us)
Async XLA Ops:
  2.0 13.9 %collective-permute-start = (bf16[272,512]{1,0:T(8,128)(2,1)S(1)}, bf16[272,512]{1,0:T(8,128)(2,1)S(1)}, u32[]{:S(2)}, u32[]{:S(2)}) collective-permute-start(bf16[272,512]{1,0:T(8,128)(2,1)S(1)} %get-tuple-element.16), channel_id=1, source_target_pairs={{0,1},{1,0},{2,3},{3,2},{4,5},{5,4},{6,7},{7,6},{8,9},{9,8},{10,11... | collective-permute-start | bytes 835592 | tf_op jit(solution)/shard_map/ppermute | solution.py:21
  5.0 10.9 %collective-permute-start.3 = (bf16[80,1024]{1,0:T(8,128)(2,1)S(1)}, bf16[80,1024]{1,0:T(8,128)(2,1)S(1)}, u32[]{:S(2)}, u32[]{:S(2)}) collective-permute-start(bf16[80,1024]{1,0:T(8,128)(2,1)S(1)} %get-tuple-element.18), channel_id=1, source_target_pairs={{0,2},{1,3},{2,0},{3,1},{4,6},{5,7},{6,4},{7,5},{8,10},{9,11},{10,... | collective-permute-start | bytes 491528 | tf_op jit(solution)/shard_map/ppermute | solution.py:21
  6.6 8.3 %collective-permute-start.1 = (bf16[32,1024]{1,0:T(8,128)(2,1)S(1)}, bf16[32,1024]{1,0:T(8,128)(2,1)S(1)}, u32[]{:S(2)}, u32[]{:S(2)}) collective-permute-start(bf16[32,1024]{1,0:T(8,128)(2,1)S(1)} %get-tuple-element.17.refs_3_), channel_id=1, source_target_pairs={{0,6},{1,7},{2,4},{3,5},{4,2},{5,3},{6,0},{7,1},{8,14},{9,15},{10,... | collective-permute-start | bytes 196616 | tf_op jit(solution)/shard_map/ppermute | solution.py:21
  9.1 6.8 %collective-permute-start.2 = (bf16[32,1024]{1,0:T(8,128)(2,1)S(1)}, bf16[32,1024]{1,0:T(8,128)(2,1)S(1)}, u32[]{:S(2)}, u32[]{:S(2)}) collective-permute-start(bf16[32,1024]{1,0:T(8,128)(2,1)S(1)} %get-tuple-element.17.refs_3_), channel_id=1, source_target_pairs={{0,4},{1,5},{2,6},{3,7},{4,0},{5,1},{6,2},{7,3},{8,12},{9,13},{10,... | collective-permute-start | bytes 196616 | tf_op jit(solution)/shard_map/ppermute | solution.py:21
  15.9 7.0 %copy-start.1 = (bf16[192,2048]{1,0:T(8,128)(2,1)S(1)}, bf16[192,2048]{1,0:T(8,128)(2,1)}, u32[]{:S(2)}) copy-start(bf16[192,2048]{1,0:T(8,128)(2,1)} %up_ref.3) | copy-start | bytes 2359300
  15.9 7.0 %copy-start = (bf16[192,2048]{1,0:T(8,128)(2,1)S(1)}, bf16[192,2048]{1,0:T(8,128)(2,1)}, u32[]{:S(2)}) copy-start(bf16[192,2048]{1,0:T(8,128)(2,1)} %gate_ref.3) | copy-start | bytes 2359300
  16.0 6.4 %collective-permute-start.5 = (bf16[128,1024]{1,0:T(8,128)(2,1)S(1)}, bf16[128,1024]{1,0:T(8,128)(2,1)S(1)}, u32[]{:S(2)}, u32[]{:S(2)}) collective-permute-start(bf16[128,1024]{1,0:T(8,128)(2,1)S(1)} %shard_map.78.after_ref.near_ref), channel_id=1, source_target_pairs={{0,1},{1,0},{2,3},{3,2},{4,5},{5,4},{6,7},{7,6},{8,9},{9,8},{10,11... | collective-permute-start | bytes 786440 | tf_op jit(solution)/shard_map/ppermute | solution.py:21
  16.6 7.1 %collective-permute-start.4 = (bf16[320,512]{1,0:T(8,128)(2,1)S(1)}, bf16[320,512]{1,0:T(8,128)(2,1)S(1)}, u32[]{:S(2)}, u32[]{:S(2)}) collective-permute-start(bf16[320,512]{1,0:T(8,128)(2,1)S(1)} %shard_map.79), channel_id=1, source_target_pairs={{0,2},{1,3},{2,0},{3,1},{4,6},{5,7},{6,4},{7,5},{8,10},{9,11},{10,... | collective-permute-start | bytes 983048 | tf_op jit(solution)/shard_map/ppermute | solution.py:21
  16.9 6.0 %collective-permute-start.7 = (bf16[128,1024]{1,0:T(8,128)(2,1)S(1)}, bf16[128,1024]{1,0:T(8,128)(2,1)S(1)}, u32[]{:S(2)}, u32[]{:S(2)}) collective-permute-start(bf16[128,1024]{1,0:T(8,128)(2,1)S(1)} %shard_map.78.after_ref.near_ref), channel_id=1, source_target_pairs={{0,8},{8,0},{16,24},{24,16},{1,9},{9,1},{17,25},{25,17},{2,10},{10... | collective-permute-start | bytes 786440 | tf_op jit(solution)/shard_map/ppermute | solution.py:21
  22.4 1.5 %collective-permute-start.6 = (bf16[128,1024]{1,0:T(8,128)(2,1)S(1)}, bf16[128,1024]{1,0:T(8,128)(2,1)S(1)}, u32[]{:S(2)}, u32[]{:S(2)}) collective-permute-start(bf16[128,1024]{1,0:T(8,128)(2,1)S(1)} %collective-permute-done.5.far_ref.refs_1_), channel_id=1, source_target_pairs={{0,8},{8,0},{16,24},{24,16},{1,9},{9,1},{17,25},{25,17},{2,10},{10... | collective-permute-start | bytes 786440 | tf_op jit(solution)/shard_map/ppermute | solution.py:21
  22.4 8.8 %collective-permute-start.11 = (bf16[144,512]{1,0:T(8,128)(2,1)S(1)}, bf16[144,512]{1,0:T(8,128)(2,1)S(1)}, u32[]{:S(2)}, u32[]{:S(2)}) collective-permute-start(bf16[144,512]{1,0:T(8,128)(2,1)S(1)} %shard_map.82), channel_id=1, source_target_pairs={{0,1},{1,0},{2,3},{3,2},{4,5},{5,4},{6,7},{7,6},{8,9},{9,8},{10,11... | collective-permute-start | bytes 442376 | tf_op jit(solution)/shard_map/ppermute | solution.py:21
  24.3 6.9 %collective-permute-start.10 = (bf16[192,256]{1,0:T(8,128)(2,1)S(1)}, bf16[192,256]{1,0:T(8,128)(2,1)S(1)}, u32[]{:S(2)}, u32[]{:S(2)}) collective-permute-start(bf16[192,256]{1,0:T(8,128)(2,1)S(1)} %shard_map.81.refs_0_), channel_id=1, source_target_pairs={{0,3},{1,2},{2,1},{3,0},{4,7},{5,6},{6,5},{7,4},{8,11},{9,10},{10,... | collective-permute-start | bytes 294920 | tf_op jit(solution)/shard_map/ppermute | solution.py:21
  25.9 7.0 %collective-permute-start.8 = (bf16[192,256]{1,0:T(8,128)(2,1)S(1)}, bf16[192,256]{1,0:T(8,128)(2,1)S(1)}, u32[]{:S(2)}, u32[]{:S(2)}) collective-permute-start(bf16[192,256]{1,0:T(8,128)(2,1)S(1)} %shard_map.81.refs_0_), channel_id=1, source_target_pairs={{0,1},{1,0},{2,3},{3,2},{4,5},{5,4},{6,7},{7,6},{8,9},{9,8},{10,11... | collective-permute-start | bytes 294920 | tf_op jit(solution)/shard_map/ppermute | solution.py:21
  26.4 6.5 %collective-permute-start.9 = (bf16[192,256]{1,0:T(8,128)(2,1)S(1)}, bf16[192,256]{1,0:T(8,128)(2,1)S(1)}, u32[]{:S(2)}, u32[]{:S(2)}) collective-permute-start(bf16[192,256]{1,0:T(8,128)(2,1)S(1)} %shard_map.81.refs_0_), channel_id=1, source_target_pairs={{0,2},{1,3},{2,0},{3,1},{4,6},{5,7},{6,4},{7,5},{8,10},{9,11},{10,... | collective-permute-start | bytes 294920 | tf_op jit(solution)/shard_map/ppermute | solution.py:21
  34.3 10.9 %all-to-all-start = ((bf16[32,16,128]{2,1,0:T(8,128)(2,1)}), bf16[32,16,128]{2,1,0:T(8,128)(2,1)S(1)}, u32[]{:S(2)}, u32[]{:S(2)}) async-start(bf16[32,16,128]{2,1,0:T(8,128)(2,1)} %bitcast.1), calls=%async_computation | async-start | bytes 262144 | tf_op jit(solution)/shard_map/all_to_all | solution.py:356
  37.5 11.1 %collective-permute-start.12 = (bf16[64,512]{1,0:T(8,128)(2,1)S(1)}, bf16[64,512]{1,0:T(8,128)(2,1)S(1)}, u32[]{:S(2)}, u32[]{:S(2)}) collective-permute-start(bf16[64,512]{1,0:T(8,128)(2,1)S(1)} %get-tuple-element.26), channel_id=1, source_target_pairs={{0,1},{1,0},{2,3},{3,2},{4,5},{5,4},{6,7},{7,6},{8,9},{9,8},{10,11... | collective-permute-start | bytes 196616 | tf_op jit(solution)/shard_map/ppermute | solution.py:21
  39.3 9.2 %collective-permute-start.13 = (bf16[64,512]{1,0:T(8,128)(2,1)S(1)}, bf16[64,512]{1,0:T(8,128)(2,1)S(1)}, u32[]{:S(2)}, u32[]{:S(2)}) collective-permute-start(bf16[64,512]{1,0:T(8,128)(2,1)S(1)} %get-tuple-element.27), channel_id=1, source_target_pairs={{0,2},{1,3},{2,0},{3,1},{4,6},{5,7},{6,4},{7,5},{8,10},{9,11},{10,... | collective-permute-start | bytes 196616 | tf_op jit(solution)/shard_map/ppermute | solution.py:21
  40.8 7.8 %collective-permute-start.14 = (bf16[64,512]{1,0:T(8,128)(2,1)S(1)}, bf16[64,512]{1,0:T(8,128)(2,1)S(1)}, u32[]{:S(2)}, u32[]{:S(2)}) collective-permute-start(bf16[64,512]{1,0:T(8,128)(2,1)S(1)} %get-tuple-element.28), channel_id=1, source_target_pairs={{0,3},{1,2},{2,1},{3,0},{4,7},{5,6},{6,5},{7,4},{8,11},{9,10},{10,... | collective-permute-start | bytes 196616 | tf_op jit(solution)/shard_map/ppermute | solution.py:21
  46.0 9.7 %all-to-all-start.1 = ((f32[32,1,128]{2,1,0:T(1,128)}), f32[32,1,128]{2,1,0:T(1,128)S(1)}, u32[]{:S(2)}, u32[]{:S(2)}) async-start(f32[32,1,128]{2,1,0:T(1,128)} %shard_map.85), calls=%async_computation.1 | async-start | bytes 32768 | tf_op jit(solution)/shard_map/all_to_all | solution.py:367

commit v26 on v23

--- a/solution.py
+++ b/solution.py
@@ -286,7 +286,7 @@
     part, token_part = model // HOLDERS, tokens // HOLDERS
 
     count = depth + TILE
-    beside, first_x = depth // 4 // TILE * TILE, depth // 2 // TILE * TILE
+    beside, first_x = depth // 4 // TILE * TILE, depth // 3 // TILE * TILE
     own, with_z, down_own, down_z, down_early, down_late = call(
         first_kernel,
         [jax.ShapeDtypeStruct((n, model // 2), bf16) for n in (rows, rows + beside)]

time: 56.9 us -> 56.9 us (level)
  starting transfers between devices: 22.2 us -> 21.6 us
  waiting for transfers between devices: 27.3 us -> 27.9 us
    ppermute x15, waiting for transfers between devices: 16.8 us -> 17.4 us  [swapped(): lax.ppermute(array, axis, [(i, i ^ mask) for i in range(lax.axis_size(axi...]
    all_to_all x1, starting transfers between devices: 3.93 us -> 3.32 us  [shards(): lax.all_to_all(centered, ('grp', 'tok'), split_axis=0, concat_axis=0, til...]
  transfers between devices with their start and end apart: 17 -> 17, of which waited for: 10 -> 9; matrix products, arithmetic and copies ran while one was open for 0% -> 0% of each run, Pallas kernels for 5% -> 5%
where the time goes in v26:
time: 56.9 us; the launch traced here: 56.6 us
  waiting for transfers between devices  27.9 us (49%)
  starting transfers between devices  21.6 us (38%)
  Pallas kernels  6.31 us (11%)
  between operations  0.75 us (1%)
    ppermute x15, waiting for transfers between devices, swapped(): lax.ppermute(array, axis, [(i, i ^ mask) for i in range(lax.axis_size(axi...  17.4 us
    ppermute x15, starting transfers between devices, swapped(): lax.ppermute(array, axis, [(i, i ^ mask) for i in range(lax.axis_size(axi...  15.8 us
    all_to_all x1, waiting for transfers between devices, shards(): lax.all_to_all(tables, ('grp', 'tok'), split_axis=0, concat_axis=0, tiled...  6.33 us
    pallas_call x10, Pallas kernels, call(): pl.pallas_call(body, out_shape=outs, in_specs=in_specs, out_specs=jax.tre...  6.31 us
    all_to_all x1, waiting for transfers between devices, shards(): lax.all_to_all(centered, ('grp', 'tok'), split_axis=0, concat_axis=0, til...  4.19 us
    all_to_all x1, starting transfers between devices, shards(): lax.all_to_all(centered, ('grp', 'tok'), split_axis=0, concat_axis=0, til...  3.32 us
    all_to_all x1, starting transfers between devices, shards(): lax.all_to_all(tables, ('grp', 'tok'), split_axis=0, concat_axis=0, tiled...  2.55 us
  transfers between devices with their start and end apart: 17, of which 9 were waited for; matrix products, arithmetic and copies ran while one was open for 0% of the time, Pallas kernels for 5%

profile of v26, /device:TPU:0, one launch (start us, length us, event | category | flops | bytes accessed | tf_op | source)
XLA Modules:
  0.0 56.6 jit_solution(14010246384941748638)
XLA Ops:
  0.6 1.4 %shard_map.77 = (bf16[32,1024]{1,0:T(8,128)(2,1)S(1)}, bf16[80,1024]{1,0:T(8,128)(2,1)S(1)}, bf16[208,512]{1,0:T(8,128)(2,1)S(1)}, bf16[112,512]{1,0:T(8,128)(2,...) custom-call(bf16[32,2048]{1,0:T(8,128)(2,1)} %states_hbm.1, f32[1,2048]{1,0:T(1,128)} %bitcast.4, ...), custom_call_target="tpu_custom_call" | custom-call | tf_op jit(solution)/shard_map/pallas_call | solution.py:30
  2.0 3.0 %collective-permute-start = (bf16[272,512]{1,0:T(8,128)(2,1)S(1)}, bf16[272,512]{1,0:T(8,128)(2,1)S(1)}, u32[]{:S(2)}, u32[]{:S(2)}) collective-permute-start(bf16[272,512]{1,0:T(8,128)(2,1)S(1)} %get-tuple-element.16), channel_id=1, source_target_pairs={{0,1},{1,0},{2,3},{3,2},{4,5},{5,4},{6,7},{7,6},{8,9},{9,8},{10,11... | collective-permute-start | bytes 835592 | tf_op jit(solution)/shard_map/ppermute | solution.py:22
  5.0 1.6 %collective-permute-start.3 = (bf16[80,1024]{1,0:T(8,128)(2,1)S(1)}, bf16[80,1024]{1,0:T(8,128)(2,1)S(1)}, u32[]{:S(2)}, u32[]{:S(2)}) collective-permute-start(bf16[80,1024]{1,0:T(8,128)(2,1)S(1)} %get-tuple-element.18), channel_id=1, source_target_pairs={{0,2},{1,3},{2,0},{3,1},{4,6},{5,7},{6,4},{7,5},{8,10},{9,11},{10,... | collective-permute-start | bytes 491528 | tf_op jit(solution)/shard_map/ppermute | solution.py:22
  6.6 2.5 %collective-permute-start.1 = (bf16[32,1024]{1,0:T(8,128)(2,1)S(1)}, bf16[32,1024]{1,0:T(8,128)(2,1)S(1)}, u32[]{:S(2)}, u32[]{:S(2)}) collective-permute-start(bf16[32,1024]{1,0:T(8,128)(2,1)S(1)} %get-tuple-element.17.refs_3_), channel_id=1, source_target_pairs={{0,6},{1,7},{2,4},{3,5},{4,2},{5,3},{6,0},{7,1},{8,14},{9,15},{10,... | collective-permute-start | bytes 196616 | tf_op jit(solution)/shard_map/ppermute | solution.py:22
  9.1 0.1 collective-permute-start.2
  9.2 5.7 %collective-permute-done.1.refs_0_ = bf16[32,1024]{1,0:T(8,128)(2,1)S(1)} collective-permute-done((bf16[32,1024]{1,0:T(8,128)(2,1)S(1)}, bf16[32,1024]{1,0:T(8,128)(2,1)S(1)}, u32[]{:S(2)}, u32[]{:S(2)}) %collective-permute-start.1) | collective-permute-done | bytes 65568 | tf_op jit(solution)/shard_map/ppermute | solution.py:22
  14.9 1.0 %collective-permute-done.2.refs_1_ = bf16[32,1024]{1,0:T(8,128)(2,1)S(1)} collective-permute-done((bf16[32,1024]{1,0:T(8,128)(2,1)S(1)}, bf16[32,1024]{1,0:T(8,128)(2,1)S(1)}, u32[]{:S(2)}, u32[]{:S(2)}) %collective-permute-start.2) | collective-permute-done | bytes 65568 | tf_op jit(solution)/shard_map/ppermute | solution.py:22
  15.9 0.0 collective-permute-done.3.refs_2_.refs_5_
  15.9 0.0 collective-permute-done.after_ref.second_ref.refs_7_
  15.9 0.0 copy-start.1
  15.9 0.0 copy-start
  16.0 0.6 %collective-permute-start.5 = (bf16[128,1024]{1,0:T(8,128)(2,1)S(1)}, bf16[128,1024]{1,0:T(8,128)(2,1)S(1)}, u32[]{:S(2)}, u32[]{:S(2)}) collective-permute-start(bf16[128,1024]{1,0:T(8,128)(2,1)S(1)} %shard_map.78.after_ref.near_ref), channel_id=1, source_target_pairs={{0,1},{1,0},{2,3},{3,2},{4,5},{5,4},{6,7},{7,6},{8,9},{9,8},{10,11... | collective-permute-start | bytes 786440 | tf_op jit(solution)/shard_map/ppermute | solution.py:22
  16.6 0.3 collective-permute-start.4
  16.9 0.0 collective-permute-start.7
  16.9 5.5 %collective-permute-done.5.far_ref.refs_1_ = bf16[128,1024]{1,0:T(8,128)(2,1)S(1)} collective-permute-done((bf16[128,1024]{1,0:T(8,128)(2,1)S(1)}, bf16[128,1024]{1,0:T(8,128)(2,1)S(1)}, u32[]{:S(2)}, u32[]{:S(2)}) %collective-permute-start.5) | collective-permute-done | bytes 262176 | tf_op jit(solution)/shard_map/ppermute | solution.py:22
  22.4 0.0 collective-permute-start.6
  22.4 0.5 collective-permute-start.11
  22.9 0.0 collective-permute-done.7.near2_ref
  22.9 0.0 copy-done.1
  22.9 0.0 copy-done
  22.9 0.8 %shard_map.80 = (bf16[192,128]{1,0:T(8,128)(2,1)S(1)}, f32[192,128]{1,0:T(8,128)S(1)}, f32[192,128]{1,0:T(8,128)S(1)}) custom-call(bf16[128,1024]{1,0:T(8,128)(2,1)S(1)} %shard_map.78.after_ref.near_ref, bf16[128,1024]{1,0:T(8,128)(2,1)S(1)} %collective-permute-done.7.near2_ref, bf16[128,1024]{1,0:T(8,128)(2,1)S(1)} %collective-permute-done.5.far_ref.refs_1_, ...), custom_call_target="tpu_custom_call" | custom-call | tf_op jit(solution)/shard_map/pallas_call | solution.py:30
  23.7 0.0 collective-permute-done.4.after_ref.refs_6_
  23.7 0.2 collective-permute-done.6.far2_ref
  23.9 0.4 shard_map.81.refs_0_
  24.3 1.6 %collective-permute-start.10 = (bf16[192,256]{1,0:T(8,128)(2,1)S(1)}, bf16[192,256]{1,0:T(8,128)(2,1)S(1)}, u32[]{:S(2)}, u32[]{:S(2)}) collective-permute-start(bf16[192,256]{1,0:T(8,128)(2,1)S(1)} %shard_map.81.refs_0_), channel_id=1, source_target_pairs={{0,3},{1,2},{2,1},{3,0},{4,7},{5,6},{6,5},{7,4},{8,11},{9,10},{10,... | collective-permute-start | bytes 294920 | tf_op jit(solution)/shard_map/ppermute | solution.py:22
  25.9 1.2 %collective-permute-start.8 = (bf16[192,256]{1,0:T(8,128)(2,1)S(1)}, bf16[192,256]{1,0:T(8,128)(2,1)S(1)}, u32[]{:S(2)}, u32[]{:S(2)}) collective-permute-start(bf16[192,256]{1,0:T(8,128)(2,1)S(1)} %shard_map.81.refs_0_), channel_id=1, source_target_pairs={{0,2},{1,3},{2,0},{3,1},{4,6},{5,7},{6,4},{7,5},{8,10},{9,11},{10,... | collective-permute-start | bytes 294920 | tf_op jit(solution)/shard_map/ppermute | solution.py:22
  27.1 0.7 %collective-permute-start.9 = (bf16[192,256]{1,0:T(8,128)(2,1)S(1)}, bf16[192,256]{1,0:T(8,128)(2,1)S(1)}, u32[]{:S(2)}, u32[]{:S(2)}) collective-permute-start(bf16[192,256]{1,0:T(8,128)(2,1)S(1)} %shard_map.81.refs_0_), channel_id=1, source_target_pairs={{0,1},{1,0},{2,3},{3,2},{4,5},{5,4},{6,7},{7,6},{8,9},{9,8},{10,11... | collective-permute-start | bytes 294920 | tf_op jit(solution)/shard_map/ppermute | solution.py:22
  27.9 3.3 %collective-permute-done.11.refs_8_ = bf16[144,512]{1,0:T(8,128)(2,1)S(1)} collective-permute-done((bf16[144,512]{1,0:T(8,128)(2,1)S(1)}, bf16[144,512]{1,0:T(8,128)(2,1)S(1)}, u32[]{:S(2)}, u32[]{:S(2)}) %collective-permute-start.11) | collective-permute-done | bytes 147488 | tf_op jit(solution)/shard_map/ppermute | solution.py:22
  31.1 0.0 collective-permute-done.10.refs_3_
  31.1 1.0 %collective-permute-done.8.refs_1_ = bf16[192,256]{1,0:T(8,128)(2,1)S(1)} collective-permute-done((bf16[192,256]{1,0:T(8,128)(2,1)S(1)}, bf16[192,256]{1,0:T(8,128)(2,1)S(1)}, u32[]{:S(2)}, u32[]{:S(2)}) %collective-permute-start.8) | collective-permute-done | bytes 98336 | tf_op jit(solution)/shard_map/ppermute | solution.py:22
  32.1 0.7 %collective-permute-done.9.refs_2_ = bf16[192,256]{1,0:T(8,128)(2,1)S(1)} collective-permute-done((bf16[192,256]{1,0:T(8,128)(2,1)S(1)}, bf16[192,256]{1,0:T(8,128)(2,1)S(1)}, u32[]{:S(2)}, u32[]{:S(2)}) %collective-permute-start.9) | collective-permute-done | bytes 98336 | tf_op jit(solution)/shard_map/ppermute | solution.py:22
  32.9 1.5 %shard_map.83 = (bf16[64,512]{1,0:T(8,128)(2,1)S(1)}, bf16[64,512]{1,0:T(8,128)(2,1)S(1)}, bf16[64,512]{1,0:T(8,128)(2,1)S(1)}, bf16[64,512]{1,0:T(8,128)(2,1)S(1)}, bf16[512,128]{1,0:T(8,128)(2,1)}) custom-call(bf16[192,256]{1,0:T(8,128)(2,1)S(1)} %shard_map.81.refs_0_, bf16[192,256]{1,0:T(8,128)(2,1)S(1)} %collective-permute-done.8.refs_1_, ...), custom_call_target="tpu_custom_call" | custom-call | tf_op jit(solution)/shard_map/pallas_call | solution.py:30
  34.3 3.3 %all-to-all-start = ((bf16[32,16,128]{2,1,0:T(8,128)(2,1)}), bf16[32,16,128]{2,1,0:T(8,128)(2,1)S(1)}, u32[]{:S(2)}, u32[]{:S(2)}) async-start(bf16[32,16,128]{2,1,0:T(8,128)(2,1)} %bitcast.1), calls=%async_computation | async-start | bytes 262144 | tf_op jit(solution)/shard_map/all_to_all | solution.py:358
  37.7 1.8 %collective-permute-start.12 = (bf16[64,512]{1,0:T(8,128)(2,1)S(1)}, bf16[64,512]{1,0:T(8,128)(2,1)S(1)}, u32[]{:S(2)}, u32[]{:S(2)}) collective-permute-start(bf16[64,512]{1,0:T(8,128)(2,1)S(1)} %get-tuple-element.26), channel_id=1, source_target_pairs={{0,1},{1,0},{2,3},{3,2},{4,5},{5,4},{6,7},{7,6},{8,9},{9,8},{10,11... | collective-permute-start | bytes 196616 | tf_op jit(solution)/shard_map/ppermute | solution.py:22
  39.5 1.5 %collective-permute-start.13 = (bf16[64,512]{1,0:T(8,128)(2,1)S(1)}, bf16[64,512]{1,0:T(8,128)(2,1)S(1)}, u32[]{:S(2)}, u32[]{:S(2)}) collective-permute-start(bf16[64,512]{1,0:T(8,128)(2,1)S(1)} %get-tuple-element.27), channel_id=1, source_target_pairs={{0,2},{1,3},{2,0},{3,1},{4,6},{5,7},{6,4},{7,5},{8,10},{9,11},{10,... | collective-permute-start | bytes 196616 | tf_op jit(solution)/shard_map/ppermute | solution.py:22
  41.0 0.3 collective-permute-start.14
  41.2 4.2 %all-to-all-done = bf16[32,16,128]{2,1,0:T(8,128)(2,1)S(1)} async-done(((bf16[32,16,128]{2,1,0:T(8,128)(2,1)}), bf16[32,16,128]{2,1,0:T(8,128)(2,1)S(1)}, u32[]{:S(2)}, u32[]{:S(2)}) %all-to-all-start) | async-done | bytes 131104 | tf_op jit(solution)/shard_map/all_to_all | solution.py:358
  45.4 0.8 %shard_map.85 = f32[32,1,128]{2,1,0:T(1,128)} custom-call(bf16[8,4,16,128]{3,2,1,0:T(8,128)(2,1)S(1)} %bitcast.3), custom_call_target="tpu_custom_call" | custom-call | tf_op jit(solution)/shard_map/pallas_call | solution.py:30
  46.2 2.6 %all-to-all-start.1 = ((f32[32,1,128]{2,1,0:T(1,128)}), f32[32,1,128]{2,1,0:T(1,128)S(1)}, u32[]{:S(2)}, u32[]{:S(2)}) async-start(f32[32,1,128]{2,1,0:T(1,128)} %shard_map.85), calls=%async_computation.1 | async-start | bytes 32768 | tf_op jit(solution)/shard_map/all_to_all | solution.py:369
  48.7 0.0 collective-permute-done.12.refs_1_
  48.7 0.0 collective-permute-done.13.refs_2_
  48.8 0.0 collective-permute-done.14.refs_3_
  48.8 0.7 %shard_map.84 = bf16[64,2048]{1,0:T(8,128)(2,1)} custom-call(bf16[64,512]{1,0:T(8,128)(2,1)S(1)} %get-tuple-element.25.refs_0_, bf16[64,512]{1,0:T(8,128)(2,1)S(1)} %collective-permute-done.12.refs_1_, bf16[64,512]{1,0:T(8,128)(2,1)S(1)} %collective-permute-done.13.refs_2_, bf16[64,512]{1,0:T(8,128)(2,1)S(1)} %collective-permute-done.14.refs_3_), custom_call_target="tpu_custom_call" | custom-call | tf_op jit(solution)/shard_map/pallas_call | solution.py:30
  49.5 6.3 %all-to-all-done.1.tables_ref = f32[32,1,128]{2,1,0:T(1,128)S(1)} async-done(((f32[32,1,128]{2,1,0:T(1,128)}), f32[32,1,128]{2,1,0:T(1,128)S(1)}, u32[]{:S(2)}, u32[]{:S(2)}) %all-to-all-start.1) | async-done | bytes 16416 | tf_op jit(solution)/shard_map/all_to_all | solution.py:369
  55.8 0.8 %shard_map.86 = f32[8,8]{1,0:T(8,128)} custom-call(f32[32,1,128]{2,1,0:T(1,128)S(1)} %all-to-all-done.1.tables_ref), custom_call_target="tpu_custom_call" | custom-call | tf_op jit(solution)/shard_map/pallas_call | solution.py:30
  (3 shorter events, 0.1 us)
Async XLA Ops:
  2.0 13.9 %collective-permute-start = (bf16[272,512]{1,0:T(8,128)(2,1)S(1)}, bf16[272,512]{1,0:T(8,128)(2,1)S(1)}, u32[]{:S(2)}, u32[]{:S(2)}) collective-permute-start(bf16[272,512]{1,0:T(8,128)(2,1)S(1)} %get-tuple-element.16), channel_id=1, source_target_pairs={{0,1},{1,0},{2,3},{3,2},{4,5},{5,4},{6,7},{7,6},{8,9},{9,8},{10,11... | collective-permute-start | bytes 835592 | tf_op jit(solution)/shard_map/ppermute | solution.py:22
  5.0 10.9 %collective-permute-start.3 = (bf16[80,1024]{1,0:T(8,128)(2,1)S(1)}, bf16[80,1024]{1,0:T(8,128)(2,1)S(1)}, u32[]{:S(2)}, u32[]{:S(2)}) collective-permute-start(bf16[80,1024]{1,0:T(8,128)(2,1)S(1)} %get-tuple-element.18), channel_id=1, source_target_pairs={{0,2},{1,3},{2,0},{3,1},{4,6},{5,7},{6,4},{7,5},{8,10},{9,11},{10,... | collective-permute-start | bytes 491528 | tf_op jit(solution)/shard_map/ppermute | solution.py:22
  6.6 8.3 %collective-permute-start.1 = (bf16[32,1024]{1,0:T(8,128)(2,1)S(1)}, bf16[32,1024]{1,0:T(8,128)(2,1)S(1)}, u32[]{:S(2)}, u32[]{:S(2)}) collective-permute-start(bf16[32,1024]{1,0:T(8,128)(2,1)S(1)} %get-tuple-element.17.refs_3_), channel_id=1, source_target_pairs={{0,6},{1,7},{2,4},{3,5},{4,2},{5,3},{6,0},{7,1},{8,14},{9,15},{10,... | collective-permute-start | bytes 196616 | tf_op jit(solution)/shard_map/ppermute | solution.py:22
  9.1 6.8 %collective-permute-start.2 = (bf16[32,1024]{1,0:T(8,128)(2,1)S(1)}, bf16[32,1024]{1,0:T(8,128)(2,1)S(1)}, u32[]{:S(2)}, u32[]{:S(2)}) collective-permute-start(bf16[32,1024]{1,0:T(8,128)(2,1)S(1)} %get-tuple-element.17.refs_3_), channel_id=1, source_target_pairs={{0,4},{1,5},{2,6},{3,7},{4,0},{5,1},{6,2},{7,3},{8,12},{9,13},{10,... | collective-permute-start | bytes 196616 | tf_op jit(solution)/shard_map/ppermute | solution.py:22
  15.9 7.0 %copy-start.1 = (bf16[192,2048]{1,0:T(8,128)(2,1)S(1)}, bf16[192,2048]{1,0:T(8,128)(2,1)}, u32[]{:S(2)}) copy-start(bf16[192,2048]{1,0:T(8,128)(2,1)} %up_ref.3) | copy-start | bytes 2359300
  15.9 7.0 %copy-start = (bf16[192,2048]{1,0:T(8,128)(2,1)S(1)}, bf16[192,2048]{1,0:T(8,128)(2,1)}, u32[]{:S(2)}) copy-start(bf16[192,2048]{1,0:T(8,128)(2,1)} %gate_ref.3) | copy-start | bytes 2359300
  16.0 6.4 %collective-permute-start.5 = (bf16[128,1024]{1,0:T(8,128)(2,1)S(1)}, bf16[128,1024]{1,0:T(8,128)(2,1)S(1)}, u32[]{:S(2)}, u32[]{:S(2)}) collective-permute-start(bf16[128,1024]{1,0:T(8,128)(2,1)S(1)} %shard_map.78.after_ref.near_ref), channel_id=1, source_target_pairs={{0,1},{1,0},{2,3},{3,2},{4,5},{5,4},{6,7},{7,6},{8,9},{9,8},{10,11... | collective-permute-start | bytes 786440 | tf_op jit(solution)/shard_map/ppermute | solution.py:22
  16.6 7.1 %collective-permute-start.4 = (bf16[320,512]{1,0:T(8,128)(2,1)S(1)}, bf16[320,512]{1,0:T(8,128)(2,1)S(1)}, u32[]{:S(2)}, u32[]{:S(2)}) collective-permute-start(bf16[320,512]{1,0:T(8,128)(2,1)S(1)} %shard_map.79), channel_id=1, source_target_pairs={{0,2},{1,3},{2,0},{3,1},{4,6},{5,7},{6,4},{7,5},{8,10},{9,11},{10,... | collective-permute-start | bytes 983048 | tf_op jit(solution)/shard_map/ppermute | solution.py:22
  16.9 6.0 %collective-permute-start.7 = (bf16[128,1024]{1,0:T(8,128)(2,1)S(1)}, bf16[128,1024]{1,0:T(8,128)(2,1)S(1)}, u32[]{:S(2)}, u32[]{:S(2)}) collective-permute-start(bf16[128,1024]{1,0:T(8,128)(2,1)S(1)} %shard_map.78.after_ref.near_ref), channel_id=1, source_target_pairs={{0,8},{8,0},{16,24},{24,16},{1,9},{9,1},{17,25},{25,17},{2,10},{10... | collective-permute-start | bytes 786440 | tf_op jit(solution)/shard_map/ppermute | solution.py:22
  22.4 1.5 %collective-permute-start.6 = (bf16[128,1024]{1,0:T(8,128)(2,1)S(1)}, bf16[128,1024]{1,0:T(8,128)(2,1)S(1)}, u32[]{:S(2)}, u32[]{:S(2)}) collective-permute-start(bf16[128,1024]{1,0:T(8,128)(2,1)S(1)} %collective-permute-done.5.far_ref.refs_1_), channel_id=1, source_target_pairs={{0,8},{8,0},{16,24},{24,16},{1,9},{9,1},{17,25},{25,17},{2,10},{10... | collective-permute-start | bytes 786440 | tf_op jit(solution)/shard_map/ppermute | solution.py:22
  22.4 8.8 %collective-permute-start.11 = (bf16[144,512]{1,0:T(8,128)(2,1)S(1)}, bf16[144,512]{1,0:T(8,128)(2,1)S(1)}, u32[]{:S(2)}, u32[]{:S(2)}) collective-permute-start(bf16[144,512]{1,0:T(8,128)(2,1)S(1)} %shard_map.82), channel_id=1, source_target_pairs={{0,1},{1,0},{2,3},{3,2},{4,5},{5,4},{6,7},{7,6},{8,9},{9,8},{10,11... | collective-permute-start | bytes 442376 | tf_op jit(solution)/shard_map/ppermute | solution.py:22
  24.3 6.9 %collective-permute-start.10 = (bf16[192,256]{1,0:T(8,128)(2,1)S(1)}, bf16[192,256]{1,0:T(8,128)(2,1)S(1)}, u32[]{:S(2)}, u32[]{:S(2)}) collective-permute-start(bf16[192,256]{1,0:T(8,128)(2,1)S(1)} %shard_map.81.refs_0_), channel_id=1, source_target_pairs={{0,3},{1,2},{2,1},{3,0},{4,7},{5,6},{6,5},{7,4},{8,11},{9,10},{10,... | collective-permute-start | bytes 294920 | tf_op jit(solution)/shard_map/ppermute | solution.py:22
  25.9 6.2 %collective-permute-start.8 = (bf16[192,256]{1,0:T(8,128)(2,1)S(1)}, bf16[192,256]{1,0:T(8,128)(2,1)S(1)}, u32[]{:S(2)}, u32[]{:S(2)}) collective-permute-start(bf16[192,256]{1,0:T(8,128)(2,1)S(1)} %shard_map.81.refs_0_), channel_id=1, source_target_pairs={{0,2},{1,3},{2,0},{3,1},{4,6},{5,7},{6,4},{7,5},{8,10},{9,11},{10,... | collective-permute-start | bytes 294920 | tf_op jit(solution)/shard_map/ppermute | solution.py:22
  27.1 5.7 %collective-permute-start.9 = (bf16[192,256]{1,0:T(8,128)(2,1)S(1)}, bf16[192,256]{1,0:T(8,128)(2,1)S(1)}, u32[]{:S(2)}, u32[]{:S(2)}) collective-permute-start(bf16[192,256]{1,0:T(8,128)(2,1)S(1)} %shard_map.81.refs_0_), channel_id=1, source_target_pairs={{0,1},{1,0},{2,3},{3,2},{4,5},{5,4},{6,7},{7,6},{8,9},{9,8},{10,11... | collective-permute-start | bytes 294920 | tf_op jit(solution)/shard_map/ppermute | solution.py:22
  34.3 11.1 %all-to-all-start = ((bf16[32,16,128]{2,1,0:T(8,128)(2,1)}), bf16[32,16,128]{2,1,0:T(8,128)(2,1)S(1)}, u32[]{:S(2)}, u32[]{:S(2)}) async-start(bf16[32,16,128]{2,1,0:T(8,128)(2,1)} %bitcast.1), calls=%async_computation | async-start | bytes 262144 | tf_op jit(solution)/shard_map/all_to_all | solution.py:358
  37.7 11.1 %collective-permute-start.12 = (bf16[64,512]{1,0:T(8,128)(2,1)S(1)}, bf16[64,512]{1,0:T(8,128)(2,1)S(1)}, u32[]{:S(2)}, u32[]{:S(2)}) collective-permute-start(bf16[64,512]{1,0:T(8,128)(2,1)S(1)} %get-tuple-element.26), channel_id=1, source_target_pairs={{0,1},{1,0},{2,3},{3,2},{4,5},{5,4},{6,7},{7,6},{8,9},{9,8},{10,11... | collective-permute-start | bytes 196616 | tf_op jit(solution)/shard_map/ppermute | solution.py:22
  39.5 9.2 %collective-permute-start.13 = (bf16[64,512]{1,0:T(8,128)(2,1)S(1)}, bf16[64,512]{1,0:T(8,128)(2,1)S(1)}, u32[]{:S(2)}, u32[]{:S(2)}) collective-permute-start(bf16[64,512]{1,0:T(8,128)(2,1)S(1)} %get-tuple-element.27), channel_id=1, source_target_pairs={{0,2},{1,3},{2,0},{3,1},{4,6},{5,7},{6,4},{7,5},{8,10},{9,11},{10,... | collective-permute-start | bytes 196616 | tf_op jit(solution)/shard_map/ppermute | solution.py:22
  41.0 7.8 %collective-permute-start.14 = (bf16[64,512]{1,0:T(8,128)(2,1)S(1)}, bf16[64,512]{1,0:T(8,128)(2,1)S(1)}, u32[]{:S(2)}, u32[]{:S(2)}) collective-permute-start(bf16[64,512]{1,0:T(8,128)(2,1)S(1)} %get-tuple-element.28), channel_id=1, source_target_pairs={{0,3},{1,2},{2,1},{3,0},{4,7},{5,6},{6,5},{7,4},{8,11},{9,10},{10,... | collective-permute-start | bytes 196616 | tf_op jit(solution)/shard_map/ppermute | solution.py:22
  46.2 9.7 %all-to-all-start.1 = ((f32[32,1,128]{2,1,0:T(1,128)}), f32[32,1,128]{2,1,0:T(1,128)S(1)}, u32[]{:S(2)}, u32[]{:S(2)}) async-start(f32[32,1,128]{2,1,0:T(1,128)} %shard_map.85), calls=%async_computation.1 | async-start | bytes 32768 | tf_op jit(solution)/shard_map/all_to_all | solution.py:369
